TPU v7x, 32 devices: a whole 2x2x4 slice. The times are simulated.
32 devices in a mesh: parts: 2 (over y), graph: 4 (over z), feat: 2 (over x), rep: 2 (over core).
Axes of the slice: x: 2, y: 2, z: 4, core: 2. Of those that a mesh axis runs over, the one named last changes fastest.
Arguments:
- features: bfloat16 [64, 256, 128], P(('parts', 'graph'), 'feat'), parts along dimension 0, may hold values from -6 to 6
- weight: bfloat16 [256, 256], replicated, may hold values from -0.375 to 0.375
- cotangent: bfloat16 [64, 256, 128], P(('parts', 'graph'), 'feat'), parts along dimension 0, may hold values from -6 to 6
- tiles: bfloat16 [2048, 128, 128], P(('parts', 'graph', 'rep')), parts along dimension 0
- tile_row: int32 [2048], P(('parts', 'graph', 'rep')), parts along dimension 0, may hold values from 0 to 7, as said below
- tile_col: int32 [2048], P(('parts', 'graph', 'rep')), parts along dimension 0, may hold values from 0 to 31, as said below
- tile_count: int32 [16], P(('parts', 'graph', 'rep')), parts along dimension 0, may hold values from 64 to 128, as said below
Outputs:
- activated: bfloat16 [64, 256, 128], P(('parts', 'graph'), 'feat'), parts along dimension 0
- input_grad: bfloat16 [64, 256, 128], P(('parts', 'graph'), 'feat'), parts along dimension 0
- weight_grad: float32 [512, 256], P('parts', 'feat'), parts along dimension 0
There are 2 independent parts, one for each index of `parts`. A program takes and returns all parts, laid end to end along the dimension named above; an argument that names none is the same for every part. Nothing has to cross between parts.
Inputs may be any that keep to these rules, and one draw needn't show every extreme that they name: `tile_row`: within the blocks of the list's graph index. Within each list tile_col never falls; the entries at and after tile_count repeat the last live column; the live entries of one list name at most 2 distinct blocks of any one graph index's blocks, and exactly 2 from every graph index in at least one list. `tile_count`: one list is full in every draw.
All inputs are finite; a program needn't handle non-finite values.
Results may differ from a plain program's by a relative error of at most 0.0067.
Values may be sent and summed in bfloat16 or wider, within the bound.
No kernel may reach another device: no remote copies, remote signals or barrier semaphores. Data moves between devices by JAX's collectives and lax.ppermute only.
A program may use at most 128 MiB of HBM per device.

v0:
```python
import functools

import jax
import jax.numpy as jnp
from jax import lax
from jax.experimental import pallas as pl
from jax.experimental.pallas import tpu as pltpu
from jax.sharding import PartitionSpec as P

CAP = 2
GROUP = 8
CHUNK = 16
TAIL = 16
VMEM_LIMIT = 40 * 2 ** 20
VMEM_MOST = 50 * 2 ** 20

NT = (((1,), (1,)), ((), ()))
TN = (((0,), (0,)), ((), ()))
F32 = jnp.float32
BF16 = jnp.bfloat16


def vmem():
    return pl.BlockSpec(memory_space=pltpu.VMEM)


def smem():
    return pl.BlockSpec(memory_space=pltpu.SMEM)


def hbm():
    return pl.BlockSpec(memory_space=pltpu.HBM)


def shape(dims, dtype):
    return jax.ShapeDtypeStruct(tuple(dims), dtype)


def dot(a, b, dims=None):
    if dims is None:
        return jnp.dot(a, b, preferred_element_type=F32)
    return lax.dot_general(a, b, dims, preferred_element_type=F32)


def call(kernel, name, outs, in_specs, scratch=(), flops=0, moved=2 ** 18, limit=VMEM_LIMIT, **kwargs):
    return pl.pallas_call(
        kernel,
        out_shape=outs,
        in_specs=in_specs,
        scratch_shapes=list(scratch),
        compiler_params=pltpu.CompilerParams(vmem_limit_bytes=limit),
        cost_estimate=pl.CostEstimate(flops=flops, bytes_accessed=moved, transcendentals=0),
        name=name,
        **kwargs,
    )


def lanes(x3):
    return jnp.concatenate([x3[b] for b in range(x3.shape[0])], axis=1)


def wanted_of(col, count, peer, blocks_dev):
    lane = lax.broadcasted_iota(jnp.int32, col.shape, 1)
    local = col - peer * blocks_dev
    inside = (lane < count) & (local >= 0) & (local < blocks_dev)
    low = jnp.min(jnp.where(inside, local, blocks_dev - 1), axis=1, keepdims=True)
    high = jnp.max(jnp.where(inside, local, 0), axis=1, keepdims=True)
    return low, high


def put_mirror(out_ref, sums, low, high):
    columns, both = sums.shape
    out_ref[:columns, :] = sums.astype(BF16)
    lane = lax.broadcasted_iota(jnp.int32, (TAIL, both), 1)
    out_ref[columns:, :] = jnp.where(lane < both // CAP, low, high).astype(F32).astype(BF16)


def mirror_outs(peers, near, m_ref, col_ref, count_ref, blocks_dev, mir, mirror_refs, self_ref, ids_ref):
    me = lax.axis_index("graph")
    width = near.shape[1] // blocks_dev
    both = CAP * width
    slots = peers * CAP
    if slots <= GROUP:
        mir[...] = dot(near, m_ref[...])
    else:
        part = GROUP * width

        @pl.loop(0, slots // GROUP)
        def _(i):
            where = pl.ds(pl.multiple_of(i * part, part), part)
            mir[:, where] = dot(near, m_ref[:, where])

    count = count_ref[0]
    col = col_ref[...]
    self_ref[...] = mir[:, :both]
    low, high = wanted_of(col, count, me, blocks_dev)
    lane = lax.broadcasted_iota(jnp.int32, col.shape, 1)
    ids_ref[...] = jnp.where(lane == 0, low, high)
    for k in range(1, peers):
        low, high = wanted_of(col, count, lax.rem(me + k, peers), blocks_dev)
        put_mirror(mirror_refs[k - 1], mir[:, k * both : (k + 1) * both], low, high)


def operator_kernel(peers, blocks_dev, slots_here, groups, fused, *refs):
    row_ref, col_ref, count_ref, tiles_ref = refs[:4]
    refs = refs[4:]
    if fused:
        lanes_ref, near_ref = refs[:2]
        m_ref = refs[2]
        mirror_refs, self_ref, ids_ref = refs[3 : 2 + peers], refs[2 + peers], refs[3 + peers]
        tiles, acc, sems, mir = refs[4 + peers :]
    else:
        m_ref, tiles, acc, sems = refs
    step = pl.program_id(0)
    per, width = tiles.shape[0], tiles.shape[1]
    chunks = per // CHUNK
    spare = slots_here * blocks_dev

    def chunk_copy(c):
        part = pl.ds(c * CHUNK, CHUNK)
        return pltpu.make_async_copy(tiles_ref.at[part], tiles.at[part], sems.at[c])

    @pl.when(step == 0)
    def _():
        for c in range(chunks):
            chunk_copy(c).start()

    me = lax.axis_index("graph")
    count = count_ref[0]
    acc[...] = jnp.zeros_like(acc)

    def add_chunk(c, carry):
        last_peer, first_col = carry

        @pl.when(step == 0)
        def _():
            chunk_copy(c).wait()

        for u in range(CHUNK):
            t = c * CHUNK + u
            col = col_ref[t]
            peer = col // blocks_dev
            first_col = jnp.where(peer == last_peer, first_col, col)
            last_peer = peer
            ahead_by = lax.rem(peer - me + peers, peers)
            slot = ahead_by * CAP + (col != first_col).astype(jnp.int32) - step * slots_here
            here = t < count
            if groups > 1:
                here = here & (slot >= 0) & (slot < slots_here)
            place = jnp.where(here, slot * blocks_dev + row_ref[t], spare)
            acc[place] = acc[place] + tiles[t].astype(F32)
        return (last_peer, first_col)

    lax.fori_loop(0, chunks, add_chunk, (jnp.int32(-1), jnp.int32(-1)))
    for s in range(slots_here):
        for r in range(blocks_dev):
            m_ref[r * width : (r + 1) * width, s * width : (s + 1) * width] = acc[
                s * blocks_dev + r
            ].astype(BF16)
    if fused:
        mirror_outs(
            peers, lanes(near_ref), m_ref, lanes_ref, count_ref, blocks_dev, mir, mirror_refs, self_ref, ids_ref
        )


def mirror_kernel(peers, blocks_dev, *refs):
    lanes_ref, count_ref, near_ref, m_ref = refs[:4]
    refs = refs[4:]
    mirror_outs(
        peers,
        lanes(near_ref),
        m_ref,
        lanes_ref,
        count_ref,
        blocks_dev,
        refs[peers + 1],
        refs[: peers - 1],
        refs[peers - 1],
        refs[peers],
    )


def list_operator(features, tiles, tile_row, tile_col, tile_count, peers):
    blocks_dev, columns, width = features.shape
    per = tiles.shape[0]
    slots = peers * CAP
    slots_here = min(slots, GROUP)
    groups = slots // slots_here
    fused = groups == 1
    m_shape = shape((blocks_dev * width, slots * width), BF16)
    m_spec = pl.BlockSpec((blocks_dev * width, slots_here * width), lambda i: (0, i))
    outs = [shape((columns + TAIL, CAP * width), BF16)] * (peers - 1) + [
        shape((columns, CAP * width), F32),
        shape((1, per), jnp.int32),
    ]
    mir = pltpu.VMEM((columns, slots * width), F32)
    scratch = [
        pltpu.VMEM((per, width, width), BF16),
        pltpu.VMEM((slots_here * blocks_dev + 1, width, width), F32),
        pltpu.SemaphoreType.DMA((per // CHUNK,)),
    ]
    col_lanes = tile_col.reshape(1, per)
    kernel = functools.partial(operator_kernel, peers, blocks_dev, slots_here, groups, fused)
    ins = [smem(), smem(), smem(), hbm()]
    if fused:
        made = call(
            kernel,
            "operator",
            [m_shape] + outs,
            ins + [vmem(), vmem()],
            scratch + [mir],
            flops=2 ** 28,
            moved=2 ** 24,
            limit=VMEM_MOST,
            grid=(1,),
            out_specs=[m_spec] + [vmem()] * (peers + 1),
        )(tile_row, tile_col, tile_count, tiles, col_lanes, features)
        operator, made = made[0], made[1:]
    else:
        operator = call(
            kernel, "operator", m_shape, ins, scratch, moved=2 ** 24, grid=(groups,), out_specs=m_spec
        )(tile_row, tile_col, tile_count, tiles)
        made = call(
            functools.partial(mirror_kernel, peers, blocks_dev),
            "mirrored",
            outs,
            [vmem(), smem(), vmem(), vmem()],
            [mir],
            flops=2 ** 28,
        )(col_lanes, tile_count, features, operator)
    return operator, list(made[: peers - 1]), made[peers - 1], made[peers]


def far_kernel(came_ref, x3, out_ref, ids_ref):
    _, columns, width = x3.shape
    lane = lax.broadcasted_iota(jnp.int32, ids_ref.shape, 1)
    ids = jnp.zeros(ids_ref.shape, jnp.int32)
    for s in range(CAP):
        tail = came_ref[columns:, s * width : (s + 1) * width].astype(F32)
        block = jnp.max(tail).astype(jnp.int32)
        ids = jnp.where(lane == s, block, ids)
        out_ref[:, s * width : (s + 1) * width] = x3[block]
    ids_ref[...] = ids


def far_of(came, values):
    _, columns, width = values.shape
    return call(
        far_kernel,
        "far_blocks",
        [shape((columns, CAP * width), BF16), shape((1, width), jnp.int32)],
        [vmem(), vmem()],
    )(came, values)


def own_rows(far, m_ref, firsts, width):
    both = CAP * width
    if len(firsts) <= GROUP:
        total = None
        for i, k in enumerate(firsts):
            add = dot(far[:, i * both : (i + 1) * both], m_ref[:, k * both : (k + 1) * both], NT)
            total = add if total is None else total + add
        return total
    first = firsts[0]

    def add_peer(i, total):
        here = pl.ds(pl.multiple_of(i * both, both), both)
        there = pl.ds(pl.multiple_of((i + first) * both, both), both)
        return total + dot(far[:, here], m_ref[:, there], NT)

    return lax.fori_loop(0, len(firsts), add_peer, jnp.zeros((far.shape[0], m_ref.shape[0]), F32))


def rows_kernel(peers, firsts, at, split, *refs):
    ids_refs, refs = refs[:peers], refs[peers:]
    came_refs, refs = refs[: peers - 1], refs[peers - 1 :]
    far_refs, refs = refs[: len(firsts)], refs[len(firsts) :]
    x3, m_ref, self_ref, refs = refs[0], refs[1], refs[2], refs[3:]
    outs, far, acc = refs[:-2], refs[-2], refs[-1]
    blocks_dev, columns, width = x3.shape
    both = CAP * width
    for s in range(CAP):
        far[:, s * width : (s + 1) * width] = x3[ids_refs[0][0, s]]
    for i in range(len(firsts)):
        far[:, (i + 1) * both : (i + 2) * both] = far_refs[i][:, at : at + both]
    own = own_rows(far, m_ref, [0] + firsts, width)
    for b in range(blocks_dev):
        acc[b] = own[:, b * width : (b + 1) * width]
    for s in range(CAP):
        block = ids_refs[0][0, s]
        acc[block] = acc[block] + self_ref[:, s * width : (s + 1) * width]
    for k in range(1, peers):
        for s in range(CAP):
            block = ids_refs[k][0, s]
            acc[block] = acc[block] + came_refs[k - 1][:columns, s * width : (s + 1) * width].astype(F32)
    if split:
        give_ref, keep_ref = outs
        half = lax.axis_index("rep")
        share = give_ref.shape[0]
        give_ref[...] = acc[pl.ds((1 - half) * share, share)].astype(BF16)
        keep_ref[...] = acc[pl.ds(half * share, share)]
    else:
        outs[0][...] = acc[...].astype(BF16)


def rows_of(values, operator, ids, came, fars, at, own_mirror, peers, reps, split):
    blocks_dev, columns, width = values.shape
    firsts = list(range(1, peers))
    share = (blocks_dev // reps, columns, width)
    if split:
        outs = [shape(share, BF16), shape(share, F32)]
    else:
        outs = [shape(values.shape, BF16)]
    return call(
        functools.partial(rows_kernel, peers, firsts, at, split),
        "rows",
        outs,
        [smem()] * peers + [vmem()] * (2 * (peers - 1) + 3),
        [
            pltpu.VMEM((columns, peers * CAP * width), BF16),
            pltpu.VMEM((blocks_dev, columns, width), F32),
        ],
        flops=2 ** 28,
        moved=2 ** 21,
    )(*ids, *came, *fars, values, operator, own_mirror)


def add_kernel(keep_ref, came_ref, out_ref):
    out_ref[...] = (keep_ref[...] + came_ref[...].astype(F32)).astype(BF16)


def add_up(keep, came):
    return call(add_kernel, "add_up", shape(came.shape, BF16), [vmem(), vmem()])(keep, came)


def dense_kernel(feats, *refs):
    sums, cots, refs = refs[:feats], refs[feats : 2 * feats], refs[2 * feats :]
    w_ref, act_ref, give_ref, spread_ref, keep_ref, wide, wide_cot, pre_scr, grad, term = refs
    share, columns, width = act_ref.shape
    me = lax.axis_index("feat")
    half = lax.axis_index("rep")
    rows = [pl.ds(pl.multiple_of(lax.rem(me + q, feats) * columns, columns), columns) for q in range(feats)]
    for q in range(feats):
        for b in range(share):
            wide[rows[q], b * width : (b + 1) * width] = sums[q][b]
            wide_cot[rows[q], b * width : (b + 1) * width] = cots[q][half * share + b]
    pre = dot(w_ref[...], wide[...], TN)
    pre_scr[...] = pre
    sig = jax.nn.sigmoid(pre)
    factor = wide_cot[...].astype(F32) * sig * (1.0 + pre * (1.0 - sig))
    grad[...] = factor.astype(BF16)
    spread = dot(w_ref[rows[0], :], grad[...]).astype(BF16)
    term[...] = dot(grad[rows[0], :], wide[...], NT)
    part = keep_ref.shape[1]
    give_ref[:, : share * width] = spread
    give_ref[:, share * width :] = term[:, pl.ds(pl.multiple_of((1 - half) * part, part), part)].astype(BF16)
    keep_ref[...] = term[:, pl.ds(pl.multiple_of(half * part, part), part)]
    for b in range(share):
        spread_ref[b] = spread[:, b * width : (b + 1) * width]
    own = pre_scr[rows[0], :]
    act = (own * jax.nn.sigmoid(own)).astype(BF16)
    for b in range(share):
        act_ref[b] = act[:, b * width : (b + 1) * width]


def dense(sums, cots, weight, feats, reps):
    share, columns, width = sums[0].shape
    features = weight.shape[0]
    part = features // reps
    return call(
        functools.partial(dense_kernel, feats),
        "dense",
        [
            shape((share, columns, width), BF16),
            shape((columns, share * width + part), BF16),
            shape((share, columns, width), BF16),
            shape((columns, part), F32),
        ],
        [vmem()] * (2 * feats + 1),
        [
            pltpu.VMEM((features, share * width), BF16),
            pltpu.VMEM((features, share * width), BF16),
            pltpu.VMEM((features, share * width), F32),
            pltpu.VMEM((features, share * width), BF16),
            pltpu.VMEM((columns, features), F32),
        ],
        flops=2 ** 28,
        moved=2 ** 20,
    )(*sums, *cots, weight)


def send_kernel(peers, *refs):
    ids_refs, refs = refs[:peers], refs[peers:]
    mine_ref, came_ref, keep_ref, m_ref, refs = refs[0], refs[1], refs[2], refs[3], refs[4:]
    x3, refs = refs[0], refs[1:]
    send_refs, refs = refs[: peers - 1], refs[peers - 1 :]
    self_ref, term_ref, mir = refs
    blocks_dev, columns, width = x3.shape
    share = mine_ref.shape[0]
    both = CAP * width
    half = lax.axis_index("rep")
    x3[pl.ds(half * share, share)] = mine_ref[...]
    for b in range(share):
        x3[(1 - half) * share + b] = came_ref[:, b * width : (b + 1) * width]
    term = (keep_ref[...] + came_ref[:, share * width :].astype(F32)).astype(BF16)
    term_ref[...] = term
    near = lanes(x3)
    slots = peers * CAP
    if slots <= GROUP:
        mir[...] = dot(near, m_ref[...])
    else:
        part = GROUP * width

        @pl.loop(0, slots // GROUP)
        def _(i):
            where = pl.ds(pl.multiple_of(i * part, part), part)
            mir[:, where] = dot(near, m_ref[:, where])

    self_ref[...] = mir[:, :both]
    for k in range(1, peers):
        out = send_refs[k - 1]
        out[:, :both] = mir[:, k * both : (k + 1) * both].astype(BF16)
        for s in range(CAP):
            at = (CAP + s) * width
            out[:, at : at + width] = x3[ids_refs[peers - k][0, s]]
        out[:, 2 * both :] = term


def sends_of(mine, came, keep, operator, ids, peers, reps):
    share, columns, width = mine.shape
    slots = peers * CAP
    return call(
        functools.partial(send_kernel, peers),
        "sends",
        [shape((share * reps, columns, width), BF16)]
        + [shape((columns, 2 * CAP * width + keep.shape[1]), BF16)] * (peers - 1)
        + [shape((columns, CAP * width), F32), shape(keep.shape, BF16)],
        [smem()] * peers + [vmem()] * 4,
        [pltpu.VMEM((columns, slots * width), F32)],
        flops=2 ** 28,
        moved=2 ** 21,
    )(*ids, mine, came, keep, operator)


def terms_kernel(peers, at, *refs):
    out_ref, terms = refs[peers], refs[peers + 1]
    me = lax.axis_index("graph")
    terms[0] = refs[0][...].astype(F32)
    for k in range(1, peers):
        terms[k] = refs[k][:, at:].astype(F32)
    total = terms[lax.rem(me, peers)]
    for p in range(1, peers):
        total = total + terms[lax.rem(me - p + peers, peers)]
    out_ref[...] = total


def sum_terms(terms, at):
    peers = len(terms)
    return call(
        functools.partial(terms_kernel, peers, at),
        "terms",
        shape(terms[0].shape, F32),
        [vmem()] * peers,
        [pltpu.VMEM((peers,) + terms[0].shape, F32)],
    )(*terms)


def join_kernel(mine_ref, came_ref, out_ref):
    half = lax.axis_index("rep")
    share = mine_ref.shape[0]
    out_ref[pl.ds(half * share, share)] = mine_ref[...]
    out_ref[pl.ds((1 - half) * share, share)] = came_ref[...]


def join(mine, came):
    out = shape((2 * mine.shape[0],) + mine.shape[1:], BF16)
    return call(join_kernel, "join", out, [vmem(), vmem()])(mine, came)


def finish_kernel(mine_ref, other_ref, share_ref, other_share_ref, grad_ref, weight_ref):
    half = lax.axis_index("rep")
    share = share_ref.shape[1]
    grad_ref[...] = (mine_ref[...].astype(F32) + other_ref[...].astype(F32)).astype(BF16)
    weight_ref[pl.ds(pl.multiple_of(half * share, share), share), :] = share_ref[...].T
    weight_ref[pl.ds(pl.multiple_of((1 - half) * share, share), share), :] = other_share_ref[...].T


def finish(mine, other, share, other_share):
    columns, width = share.shape
    return call(
        finish_kernel,
        "finish",
        [shape(mine.shape, BF16), shape((2 * width, columns), F32)],
        [vmem()] * 4,
    )(mine, other, share, other_share)


def ahead(value, axis, size, k):
    return lax.ppermute(value, axis, [(i, (i + k) % size) for i in range(size)])


def after(value, first):
    return lax.optimization_barrier((value, first))[0]


def shifts(peers):
    return sorted(range(1, peers), key=lambda k: (abs(2 * k - peers), k))


def local(features, weight, cotangent, tiles, tile_row, tile_col, tile_count):
    peers = lax.axis_size("graph")
    feats = lax.axis_size("feat")
    reps = lax.axis_size("rep")
    order = shifts(peers)

    operator, mirrors, own_mirror, own_ids = list_operator(
        features, tiles, tile_row, tile_col, tile_count, peers
    )
    came, ids, fars = [None] * peers, [own_ids] + [None] * (peers - 1), [None] * peers
    for k in order:
        came[k] = ahead(mirrors[k - 1], "graph", peers, k)
    for k in order:
        packed, ids[peers - k] = far_of(came[peers - k], features)
        fars[peers - k] = ahead(packed, "graph", peers, k)
    cots = [cotangent]
    if feats > 1:
        held = after(cotangent, mirrors[0])
        cots += [ahead(held, "feat", feats, feats - q) for q in range(1, feats)]
        cots, fars = lax.optimization_barrier((cots, fars))
    give, keep = rows_of(features, operator, ids, came[1:], fars[1:], 0, own_mirror, peers, reps, True)

    mine = add_up(keep, ahead(give, "rep", reps, 1))
    sums = [mine] + [ahead(mine, "feat", feats, feats - q) for q in range(1, feats)]
    act, give, spread, keep = dense(sums, cots, weight, feats, reps)
    outs = sends_of(spread, ahead(give, "rep", reps, 1), keep, operator, ids, peers, reps)
    values, sends, own_mirror, term = outs[0], outs[1:peers], outs[peers], outs[peers + 1]

    came, fars = [None] * peers, [None] * peers
    for k in order:
        came[k] = ahead(sends[k - 1], "graph", peers, k)
        fars[peers - k] = came[k]
    activated = join(act, ahead(act, "rep", reps, 1))
    (part,) = rows_of(
        values, operator, ids, came[1:], fars[1:], CAP * values.shape[2], own_mirror, peers, reps, False
    )
    share = sum_terms([term] + came[1:], 2 * CAP * values.shape[2])
    input_grad, weight_grad = finish(
        part, ahead(part, "rep", reps, 1), share, ahead(share, "rep", reps, 1)
    )
    return (activated, input_grad, weight_grad)


def solution(mesh):
    placed = (
        P(("parts", "graph"), "feat", None),
        P(),
        P(("parts", "graph"), "feat", None),
        P(("parts", "graph", "rep"), None, None),
        P(("parts", "graph", "rep")),
        P(("parts", "graph", "rep")),
        P(("parts", "graph", "rep")),
    )
    return jax.shard_map(
        local,
        mesh=mesh,
        in_specs=placed,
        out_specs=(
            P(("parts", "graph"), "feat", None),
            P(("parts", "graph"), "feat", None),
            P("parts", "feat"),
        ),
        check_vma=False,
    )
```

profile of v0, /device:TPU:9, one launch (start us, length us, event | category | flops | bytes accessed | tf_op | source)
XLA Modules:
  0.0 61.5 jit_solution(12598849665236162634)
XLA Ops:
  1.3 0.9 %copy-done = bf16[8,128,128]{2,1,0:T(8,128)(2,1)S(1)} copy-done((bf16[8,128,128]{2,1,0:T(8,128)(2,1)S(1)}, bf16[8,128,128]{2,1,0:T(8,128)(2,1)}, u32[]{:S(2)}) %copy-start) | copy-done | bytes 262168
  3.5 3.8 %operator.1 = (bf16[1024,1024]{1,0:T(8,128)(2,1)S(1)}, bf16[144,256]{1,0:T(8,128)(2,1)S(1)}, bf16[144,256]{1,0:T(8,128)(2,1)S(1)}, bf16[144,256]{1,0:T(8,128)(2,...) custom-call(s32[128]{0:T(128)S(1)} %copy-done.2, s32[128]{0:T(128)S(1)} %copy-done.1, s32[1]{0:T(128)S(6)} %copy.10.refs_2_, ...), custom_call_target="tpu_custom_call" | custom-call | flops 268435456 | bytes 16777216 | tf_op jit(solution)/shard_map/operator/pallas_call | solution.py:206
  7.4 1.3 %collective-permute-start.3 = (bf16[8,128,128]{2,1,0:T(8,128)(2,1)S(1)}, bf16[8,128,128]{2,1,0:T(8,128)(2,1)S(1)}, u32[]{:S(2)}, u32[]{:S(2)}) collective-permute-start(bf16[8,128,128]{2,1,0:T(8,128)(2,1)S(1)} %copy-done.3), channel_id=1, source_target_pairs={{0,2},{2,0},{1,3},{3,1},{4,6},{6,4},{5,7},{7,5},{8,10},{10,8},{9,1... | collective-permute-start | bytes 786440 | tf_op jit(solution)/shard_map/ppermute | solution.py:499
  8.6 1.3 %collective-permute-start = (bf16[144,256]{1,0:T(8,128)(2,1)S(1)}, bf16[144,256]{1,0:T(8,128)(2,1)S(1)}, u32[]{:S(2)}, u32[]{:S(2)}) collective-permute-start(bf16[144,256]{1,0:T(8,128)(2,1)S(1)} %get-tuple-element.36), channel_id=1, source_target_pairs={{0,4},{4,8},{8,12},{12,0},{1,5},{5,9},{9,13},{13,1},{2,6},{6,10},{... | collective-permute-start | bytes 221192 | tf_op jit(solution)/shard_map/ppermute | solution.py:499
  9.9 1.0 %collective-permute-start.1 = (bf16[144,256]{1,0:T(8,128)(2,1)S(1)}, bf16[144,256]{1,0:T(8,128)(2,1)S(1)}, u32[]{:S(2)}, u32[]{:S(2)}) collective-permute-start(bf16[144,256]{1,0:T(8,128)(2,1)S(1)} %get-tuple-element.38), channel_id=1, source_target_pairs={{0,8},{4,12},{8,0},{12,4},{1,9},{5,13},{9,1},{13,5},{2,10},{6,14},... | collective-permute-start | bytes 221192 | tf_op jit(solution)/shard_map/ppermute | solution.py:499
  11.0 1.5 %collective-permute-start.2 = (bf16[144,256]{1,0:T(8,128)(2,1)S(1)}, bf16[144,256]{1,0:T(8,128)(2,1)S(1)}, u32[]{:S(2)}, u32[]{:S(2)}) collective-permute-start(bf16[144,256]{1,0:T(8,128)(2,1)S(1)} %get-tuple-element.40), channel_id=1, source_target_pairs={{0,12},{4,0},{8,4},{12,8},{1,13},{5,1},{9,5},{13,9},{2,14},{6,2},{... | collective-permute-start | bytes 221192 | tf_op jit(solution)/shard_map/ppermute | solution.py:499
  12.6 1.5 %collective-permute-start.4 = (bf16[128,256]{1,0:T(8,128)(2,1)S(1)}, bf16[128,256]{1,0:T(8,128)(2,1)S(1)}, u32[]{:S(2)}, u32[]{:S(2)}) collective-permute-start(bf16[128,256]{1,0:T(8,128)(2,1)S(1)} %get-tuple-element.43), channel_id=1, source_target_pairs={{0,12},{4,0},{8,4},{12,8},{1,13},{5,1},{9,5},{13,9},{2,14},{6,2},{... | collective-permute-start | bytes 196616 | tf_op jit(solution)/shard_map/ppermute | solution.py:499
  14.1 0.8 %collective-permute-done.1.came_ref.refs_5_ = bf16[144,256]{1,0:T(8,128)(2,1)S(1)} collective-permute-done((bf16[144,256]{1,0:T(8,128)(2,1)S(1)}, bf16[144,256]{1,0:T(8,128)(2,1)S(1)}, u32[]{:S(2)}, u32[]{:S(2)}) %collective-permute-start.1) | collective-permute-done | bytes 73760 | tf_op jit(solution)/shard_map/ppermute | solution.py:499
  15.8 2.0 %collective-permute-done.2.came_ref.refs_6_ = bf16[144,256]{1,0:T(8,128)(2,1)S(1)} collective-permute-done((bf16[144,256]{1,0:T(8,128)(2,1)S(1)}, bf16[144,256]{1,0:T(8,128)(2,1)S(1)}, u32[]{:S(2)}, u32[]{:S(2)}) %collective-permute-start.2) | collective-permute-done | bytes 73760 | tf_op jit(solution)/shard_map/ppermute | solution.py:499
  18.3 1.6 %collective-permute-done.4.refs_7_ = bf16[128,256]{1,0:T(8,128)(2,1)S(1)} collective-permute-done((bf16[128,256]{1,0:T(8,128)(2,1)S(1)}, bf16[128,256]{1,0:T(8,128)(2,1)S(1)}, u32[]{:S(2)}, u32[]{:S(2)}) %collective-permute-start.4) | collective-permute-done | bytes 65568 | tf_op jit(solution)/shard_map/ppermute | solution.py:499
  19.9 1.6 %collective-permute-done.6.refs_9_ = bf16[128,256]{1,0:T(8,128)(2,1)S(1)} collective-permute-done((bf16[128,256]{1,0:T(8,128)(2,1)S(1)}, bf16[128,256]{1,0:T(8,128)(2,1)S(1)}, u32[]{:S(2)}, u32[]{:S(2)}) %collective-permute-start.6) | collective-permute-done | bytes 65568 | tf_op jit(solution)/shard_map/ppermute | solution.py:499
  21.5 1.5 %rows.2 = (bf16[4,128,128]{2,1,0:T(8,128)(2,1)S(1)}, f32[4,128,128]{2,1,0:T(8,128)S(1)}) custom-call(s32[1,128]{1,0:T(1,128)S(1)} %get-tuple-element.35.refs_0_, s32[1,128]{1,0:T(1,128)S(1)} %get-tuple-element.37.refs_1_, s32[1,128]{1,0:T(1,128)S(1)} %get-tuple-element.39.refs_2_, s32[1,128]{1,0:T(1,128)S(1)} %get-tuple-element.41.refs_3_, ...), custom_call_target="tpu_custom_call" | custom-call | flops 268435456 | bytes 2097152 | tf_op jit(solution)/shard_map/rows/pallas_call | solution.py:314
  23.0 6.6 %collective-permute-start.7 = (bf16[4,128,128]{2,1,0:T(8,128)(2,1)S(1)}, bf16[4,128,128]{2,1,0:T(8,128)(2,1)S(1)}, u32[]{:S(2)}, u32[]{:S(2)}) collective-permute-start(bf16[4,128,128]{2,1,0:T(8,128)(2,1)S(1)} %get-tuple-element.52), channel_id=1, source_target_pairs={{0,1},{1,0},{2,3},{3,2},{4,5},{5,4},{6,7},{7,6},{8,9},{9,8},{10,11... | collective-permute-start | bytes 393224 | tf_op jit(solution)/shard_map/ppermute | solution.py:499
  29.6 1.0 %collective-permute-done.7.came_ref = bf16[4,128,128]{2,1,0:T(8,128)(2,1)S(1)} collective-permute-done((bf16[4,128,128]{2,1,0:T(8,128)(2,1)S(1)}, bf16[4,128,128]{2,1,0:T(8,128)(2,1)S(1)}, u32[]{:S(2)}, u32[]{:S(2)}) %collective-permute-start.7) | collective-permute-done | bytes 131104 | tf_op jit(solution)/shard_map/ppermute | solution.py:499
  31.0 4.5 %collective-permute-done.8.refs_1_ = bf16[4,128,128]{2,1,0:T(8,128)(2,1)S(1)} collective-permute-done((bf16[4,128,128]{2,1,0:T(8,128)(2,1)S(1)}, bf16[4,128,128]{2,1,0:T(8,128)(2,1)S(1)}, u32[]{:S(2)}, u32[]{:S(2)}) %collective-permute-start.8) | collective-permute-done | bytes 131104 | tf_op jit(solution)/shard_map/ppermute | solution.py:499
  36.2 1.2 %collective-permute-start.10 = (bf16[128,640]{1,0:T(8,128)(2,1)S(1)}, bf16[128,640]{1,0:T(8,128)(2,1)S(1)}, u32[]{:S(2)}, u32[]{:S(2)}) collective-permute-start(bf16[128,640]{1,0:T(8,128)(2,1)S(1)} %get-tuple-element.57), channel_id=1, source_target_pairs={{0,1},{1,0},{2,3},{3,2},{4,5},{5,4},{6,7},{7,6},{8,9},{9,8},{10,11... | collective-permute-start | bytes 491528 | tf_op jit(solution)/shard_map/ppermute | solution.py:499
  37.4 1.0 %collective-permute-done.10.refs_5_ = bf16[128,640]{1,0:T(8,128)(2,1)S(1)} collective-permute-done((bf16[128,640]{1,0:T(8,128)(2,1)S(1)}, bf16[128,640]{1,0:T(8,128)(2,1)S(1)}, u32[]{:S(2)}, u32[]{:S(2)}) %collective-permute-start.10) | collective-permute-done | bytes 163872 | tf_op jit(solution)/shard_map/ppermute | solution.py:499
  38.4 1.1 %sends.1 = (bf16[8,128,128]{2,1,0:T(8,128)(2,1)S(1)}, bf16[128,640]{1,0:T(8,128)(2,1)S(1)}, bf16[128,640]{1,0:T(8,128)(2,1)S(1)}, bf16[128,640]{1,0:T(8,128)(2,1...) custom-call(s32[1,128]{1,0:T(1,128)S(1)} %get-tuple-element.35.refs_0_, ...), custom_call_target="tpu_custom_call" | custom-call | flops 268435456 | bytes 2097152 | tf_op jit(solution)/shard_map/sends/pallas_call | solution.py:432
  39.8 1.5 %collective-permute-start.12 = (bf16[128,640]{1,0:T(8,128)(2,1)S(1)}, bf16[128,640]{1,0:T(8,128)(2,1)S(1)}, u32[]{:S(2)}, u32[]{:S(2)}) collective-permute-start(bf16[128,640]{1,0:T(8,128)(2,1)S(1)} %get-tuple-element.60), channel_id=1, source_target_pairs={{0,8},{4,12},{8,0},{12,4},{1,9},{5,13},{9,1},{13,5},{2,10},{6,14},... | collective-permute-start | bytes 491528 | tf_op jit(solution)/shard_map/ppermute | solution.py:499
  41.5 3.5 %collective-permute-done.11.refs_4_.refs_9_.refs_1_ = bf16[128,640]{1,0:T(8,128)(2,1)S(1)} collective-permute-done((bf16[128,640]{1,0:T(8,128)(2,1)S(1)}, bf16[128,640]{1,0:T(8,128)(2,1)S(1)}, u32[]{:S(2)}, u32[]{:S(2)}) %collective-permute-start.11) | collective-permute-done | bytes 163872 | tf_op jit(solution)/shard_map/ppermute | solution.py:499
  45.0 8.6 %collective-permute-done.12.refs_5_.refs_8_.refs_2_ = bf16[128,640]{1,0:T(8,128)(2,1)S(1)} collective-permute-done((bf16[128,640]{1,0:T(8,128)(2,1)S(1)}, bf16[128,640]{1,0:T(8,128)(2,1)S(1)}, u32[]{:S(2)}, u32[]{:S(2)}) %collective-permute-start.12) | collective-permute-done | bytes 163872 | tf_op jit(solution)/shard_map/ppermute | solution.py:499
  53.5 3.0 %collective-permute-done.13.refs_6_.refs_7_.refs_3_ = bf16[128,640]{1,0:T(8,128)(2,1)S(1)} collective-permute-done((bf16[128,640]{1,0:T(8,128)(2,1)S(1)}, bf16[128,640]{1,0:T(8,128)(2,1)S(1)}, u32[]{:S(2)}, u32[]{:S(2)}) %collective-permute-start.13) | collective-permute-done | bytes 163872 | tf_op jit(solution)/shard_map/ppermute | solution.py:499
  56.5 1.5 %rows.3.mine_ref = bf16[8,128,128]{2,1,0:T(8,128)(2,1)S(1)} custom-call(s32[1,128]{1,0:T(1,128)S(1)} %get-tuple-element.35.refs_0_, s32[1,128]{1,0:T(1,128)S(1)} %get-tuple-element.37.refs_1_, s32[1,128]{1,0:T(1,128)S(1)} %get-tuple-element.39.refs_2_, s32[1,128]{1,0:T(1,128)S(1)} %get-tuple-element.41.refs_3_, ...), custom_call_target="tpu_custom_call" | custom-call | flops 268435456 | bytes 2097152 | tf_op jit(solution)/shard_map/rows/pallas_call | solution.py:314
  60.6 0.9 %finish.1 = (bf16[8,128,128]{2,1,0:T(8,128)(2,1)}, f32[256,128]{1,0:T(8,128)}) custom-call(bf16[8,128,128]{2,1,0:T(8,128)(2,1)S(1)} %rows.3.mine_ref, bf16[8,128,128]{2,1,0:T(8,128)(2,1)S(1)} %collective-permute-done.14.other_ref, f32[128,128]{1,0:T(8,128)S(1)} %terms.1.share_ref, f32[128,128]{1,0:T(8,128)S(1)} %collective-permute-done.15.other_share_ref), custom_call_target="tpu_custom_call" | custom-call | bytes 262144 | tf_op jit(solution)/shard_map/finish/pallas_call | solution.py:490
  (30 shorter events, 6.9 us)
Async XLA Ops:
  1.3 1.0 %copy-start = (bf16[8,128,128]{2,1,0:T(8,128)(2,1)S(1)}, bf16[8,128,128]{2,1,0:T(8,128)(2,1)}, u32[]{:S(2)}) copy-start(bf16[8,128,128]{2,1,0:T(8,128)(2,1)} %refs_10_.1) | copy-start | bytes 786436
  2.2 0.7 %copy-start.1 = (s32[128]{0:T(128)S(1)}, s32[128]{0:T(128)}, u32[]{:S(2)}) copy-start(s32[128]{0:T(128)} %refs_1_.1) | copy-start | bytes 1540
  2.9 0.7 %copy-start.2 = (s32[128]{0:T(128)S(1)}, s32[128]{0:T(128)}, u32[]{:S(2)}) copy-start(s32[128]{0:T(128)} %refs_0_.1) | copy-start | bytes 1540
  3.5 3.8 %copy-start.3 = (bf16[8,128,128]{2,1,0:T(8,128)(2,1)S(1)}, bf16[8,128,128]{2,1,0:T(8,128)(2,1)}, u32[]{:S(2)}) copy-start(bf16[8,128,128]{2,1,0:T(8,128)(2,1)} %refs_2_.1) | copy-start | bytes 786436
  3.5 31.9 %copy-start.4 = (bf16[256,256]{1,0:T(8,128)(2,1)S(1)}, bf16[256,256]{1,0:T(8,128)(2,1)}, u32[]{:S(2)}) copy-start(bf16[256,256]{1,0:T(8,128)(2,1)} %refs_4_.1) | copy-start | bytes 393220
  7.4 14.2 %collective-permute-start.3 = (bf16[8,128,128]{2,1,0:T(8,128)(2,1)S(1)}, bf16[8,128,128]{2,1,0:T(8,128)(2,1)S(1)}, u32[]{:S(2)}, u32[]{:S(2)}) collective-permute-start(bf16[8,128,128]{2,1,0:T(8,128)(2,1)S(1)} %copy-done.3), channel_id=1, source_target_pairs={{0,2},{2,0},{1,3},{3,1},{4,6},{6,4},{5,7},{7,5},{8,10},{10,8},{9,1... | collective-permute-start | bytes 786440 | tf_op jit(solution)/shard_map/ppermute | solution.py:499
  8.6 3.8 %collective-permute-start = (bf16[144,256]{1,0:T(8,128)(2,1)S(1)}, bf16[144,256]{1,0:T(8,128)(2,1)S(1)}, u32[]{:S(2)}, u32[]{:S(2)}) collective-permute-start(bf16[144,256]{1,0:T(8,128)(2,1)S(1)} %get-tuple-element.36), channel_id=1, source_target_pairs={{0,4},{4,8},{8,12},{12,0},{1,5},{5,9},{9,13},{13,1},{2,6},{6,10},{... | collective-permute-start | bytes 221192 | tf_op jit(solution)/shard_map/ppermute | solution.py:499
  9.9 5.0 %collective-permute-start.1 = (bf16[144,256]{1,0:T(8,128)(2,1)S(1)}, bf16[144,256]{1,0:T(8,128)(2,1)S(1)}, u32[]{:S(2)}, u32[]{:S(2)}) collective-permute-start(bf16[144,256]{1,0:T(8,128)(2,1)S(1)} %get-tuple-element.38), channel_id=1, source_target_pairs={{0,8},{4,12},{8,0},{12,4},{1,9},{5,13},{9,1},{13,5},{2,10},{6,14},... | collective-permute-start | bytes 221192 | tf_op jit(solution)/shard_map/ppermute | solution.py:499
  11.0 6.8 %collective-permute-start.2 = (bf16[144,256]{1,0:T(8,128)(2,1)S(1)}, bf16[144,256]{1,0:T(8,128)(2,1)S(1)}, u32[]{:S(2)}, u32[]{:S(2)}) collective-permute-start(bf16[144,256]{1,0:T(8,128)(2,1)S(1)} %get-tuple-element.40), channel_id=1, source_target_pairs={{0,12},{4,0},{8,4},{12,8},{1,13},{5,1},{9,5},{13,9},{2,14},{6,2},{... | collective-permute-start | bytes 221192 | tf_op jit(solution)/shard_map/ppermute | solution.py:499
  12.6 7.3 %collective-permute-start.4 = (bf16[128,256]{1,0:T(8,128)(2,1)S(1)}, bf16[128,256]{1,0:T(8,128)(2,1)S(1)}, u32[]{:S(2)}, u32[]{:S(2)}) collective-permute-start(bf16[128,256]{1,0:T(8,128)(2,1)S(1)} %get-tuple-element.43), channel_id=1, source_target_pairs={{0,12},{4,0},{8,4},{12,8},{1,13},{5,1},{9,5},{13,9},{2,14},{6,2},{... | collective-permute-start | bytes 196616 | tf_op jit(solution)/shard_map/ppermute | solution.py:499
  15.1 4.8 %collective-permute-start.5 = (bf16[128,256]{1,0:T(8,128)(2,1)S(1)}, bf16[128,256]{1,0:T(8,128)(2,1)S(1)}, u32[]{:S(2)}, u32[]{:S(2)}) collective-permute-start(bf16[128,256]{1,0:T(8,128)(2,1)S(1)} %get-tuple-element.44), channel_id=1, source_target_pairs={{0,8},{4,12},{8,0},{12,4},{1,9},{5,13},{9,1},{13,5},{2,10},{6,14},... | collective-permute-start | bytes 196616 | tf_op jit(solution)/shard_map/ppermute | solution.py:499
  17.9 3.6 %collective-permute-start.6 = (bf16[128,256]{1,0:T(8,128)(2,1)S(1)}, bf16[128,256]{1,0:T(8,128)(2,1)S(1)}, u32[]{:S(2)}, u32[]{:S(2)}) collective-permute-start(bf16[128,256]{1,0:T(8,128)(2,1)S(1)} %get-tuple-element.45), channel_id=1, source_target_pairs={{0,4},{4,8},{8,12},{12,0},{1,5},{5,9},{9,13},{13,1},{2,6},{6,10},{... | collective-permute-start | bytes 196616 | tf_op jit(solution)/shard_map/ppermute | solution.py:499
  23.0 7.6 %collective-permute-start.7 = (bf16[4,128,128]{2,1,0:T(8,128)(2,1)S(1)}, bf16[4,128,128]{2,1,0:T(8,128)(2,1)S(1)}, u32[]{:S(2)}, u32[]{:S(2)}) collective-permute-start(bf16[4,128,128]{2,1,0:T(8,128)(2,1)S(1)} %get-tuple-element.52), channel_id=1, source_target_pairs={{0,1},{1,0},{2,3},{3,2},{4,5},{5,4},{6,7},{7,6},{8,9},{9,8},{10,11... | collective-permute-start | bytes 393224 | tf_op jit(solution)/shard_map/ppermute | solution.py:499
  30.7 4.8 %collective-permute-start.8 = (bf16[4,128,128]{2,1,0:T(8,128)(2,1)S(1)}, bf16[4,128,128]{2,1,0:T(8,128)(2,1)S(1)}, u32[]{:S(2)}, u32[]{:S(2)}) collective-permute-start(bf16[4,128,128]{2,1,0:T(8,128)(2,1)S(1)} %add_up.1.refs_0_), channel_id=1, source_target_pairs={{0,2},{2,0},{1,3},{3,1},{4,6},{6,4},{5,7},{7,5},{8,10},{10,8},{9,1... | collective-permute-start | bytes 393224 | tf_op jit(solution)/shard_map/ppermute | solution.py:499
  36.2 2.3 %collective-permute-start.10 = (bf16[128,640]{1,0:T(8,128)(2,1)S(1)}, bf16[128,640]{1,0:T(8,128)(2,1)S(1)}, u32[]{:S(2)}, u32[]{:S(2)}) collective-permute-start(bf16[128,640]{1,0:T(8,128)(2,1)S(1)} %get-tuple-element.57), channel_id=1, source_target_pairs={{0,1},{1,0},{2,3},{3,2},{4,5},{5,4},{6,7},{7,6},{8,9},{9,8},{10,11... | collective-permute-start | bytes 491528 | tf_op jit(solution)/shard_map/ppermute | solution.py:499
  39.5 5.5 %collective-permute-start.11 = (bf16[128,640]{1,0:T(8,128)(2,1)S(1)}, bf16[128,640]{1,0:T(8,128)(2,1)S(1)}, u32[]{:S(2)}, u32[]{:S(2)}) collective-permute-start(bf16[128,640]{1,0:T(8,128)(2,1)S(1)} %get-tuple-element.59), channel_id=1, source_target_pairs={{0,4},{4,8},{8,12},{12,0},{1,5},{5,9},{9,13},{13,1},{2,6},{6,10},{... | collective-permute-start | bytes 491528 | tf_op jit(solution)/shard_map/ppermute | solution.py:499
  39.8 13.7 %collective-permute-start.12 = (bf16[128,640]{1,0:T(8,128)(2,1)S(1)}, bf16[128,640]{1,0:T(8,128)(2,1)S(1)}, u32[]{:S(2)}, u32[]{:S(2)}) collective-permute-start(bf16[128,640]{1,0:T(8,128)(2,1)S(1)} %get-tuple-element.60), channel_id=1, source_target_pairs={{0,8},{4,12},{8,0},{12,4},{1,9},{5,13},{9,1},{13,5},{2,10},{6,14},... | collective-permute-start | bytes 491528 | tf_op jit(solution)/shard_map/ppermute | solution.py:499
  41.3 15.2 %collective-permute-start.13 = (bf16[128,640]{1,0:T(8,128)(2,1)S(1)}, bf16[128,640]{1,0:T(8,128)(2,1)S(1)}, u32[]{:S(2)}, u32[]{:S(2)}) collective-permute-start(bf16[128,640]{1,0:T(8,128)(2,1)S(1)} %get-tuple-element.61), channel_id=1, source_target_pairs={{0,12},{4,0},{8,4},{12,8},{1,13},{5,1},{9,5},{13,9},{2,14},{6,2},{... | collective-permute-start | bytes 491528 | tf_op jit(solution)/shard_map/ppermute | solution.py:499
  58.0 2.6 %collective-permute-start.14 = (bf16[8,128,128]{2,1,0:T(8,128)(2,1)S(1)}, bf16[8,128,128]{2,1,0:T(8,128)(2,1)S(1)}, u32[]{:S(2)}, u32[]{:S(2)}) collective-permute-start(bf16[8,128,128]{2,1,0:T(8,128)(2,1)S(1)} %rows.3.mine_ref), channel_id=1, source_target_pairs={{0,1},{1,0},{2,3},{3,2},{4,5},{5,4},{6,7},{7,6},{8,9},{9,8},{10,11... | collective-permute-start | bytes 786440 | tf_op jit(solution)/shard_map/ppermute | solution.py:499
  58.6 1.3 %collective-permute-start.9 = (bf16[4,128,128]{2,1,0:T(8,128)(2,1)S(1)}, bf16[4,128,128]{2,1,0:T(8,128)(2,1)S(1)}, u32[]{:S(2)}, u32[]{:S(2)}) collective-permute-start(bf16[4,128,128]{2,1,0:T(8,128)(2,1)S(1)} %get-tuple-element.55.mine_ref), channel_id=1, source_target_pairs={{0,1},{1,0},{2,3},{3,2},{4,5},{5,4},{6,7},{7,6},{8,9},{9,8},{10,11... | collective-permute-start | bytes 393224 | tf_op jit(solution)/shard_map/ppermute | solution.py:499
  58.7 2.0 %collective-permute-start.15 = (f32[128,128]{1,0:T(8,128)S(1)}, f32[128,128]{1,0:T(8,128)S(1)}, u32[]{:S(2)}, u32[]{:S(2)}) collective-permute-start(f32[128,128]{1,0:T(8,128)S(1)} %terms.1.share_ref), channel_id=1, source_target_pairs={{0,1},{1,0},{2,3},{3,2},{4,5},{5,4},{6,7},{7,6},{8,9},{9,8},{10,11... | collective-permute-start | bytes 196616 | tf_op jit(solution)/shard_map/ppermute | solution.py:499
where the time goes:
time: 61.7 us; the launch traced here: 61.5 us
  waiting for transfers between devices  28.4 us (46%)
  starting transfers between devices  19 us (31%)
  Pallas kernels  10.6 us (17%)
  local copies, waits for them, and re-layouts  2.26 us (4%)
  between operations  1.38 us (2%)
    ppermute x16, waiting for transfers between devices, ahead(): return lax.ppermute(value, axis, [(i, (i + k) % size) for i in range(size)])  28.4 us
    ppermute x16, starting transfers between devices, ahead(): return lax.ppermute(value, axis, [(i, (i + k) % size) for i in range(size)])  19 us
    pallas_call x1, Pallas kernels, list_operator(): call(kernel, 'operator', [m_shape] + outs, ins + [vmem(), vmem()], scratc...  3.8 us
    pallas_call x2, Pallas kernels, rows_of(): call(functools.partial(rows_kernel, peers, firsts, at, split), 'rows', ou...  2.93 us
    unnamed x10, local copies, waits for them, and re-layouts  2.26 us
  transfers between devices with their start and end apart: 16, of which 11 were waited for; matrix products, arithmetic and copies ran while one was open for 0% of the time, Pallas kernels for 2%

commit v1 on v0

v1 whole, which is shorter than its diff:
```python
import functools

import jax
import jax.numpy as jnp
from jax import lax
from jax.experimental import pallas as pl
from jax.experimental.pallas import tpu as pltpu
from jax.sharding import PartitionSpec as P

CAP = 2
GROUP = 8
CHUNK = 16
SIDES = 2
VMEM_LIMIT = 40 * 2 ** 20
VMEM_MOST = 50 * 2 ** 20

NT = (((1,), (1,)), ((), ()))
TN = (((0,), (0,)), ((), ()))
F32 = jnp.float32
BF16 = jnp.bfloat16


def vmem():
    return pl.BlockSpec(memory_space=pltpu.VMEM)


def smem():
    return pl.BlockSpec(memory_space=pltpu.SMEM)


def hbm():
    return pl.BlockSpec(memory_space=pltpu.HBM)


def shape(dims, dtype):
    return jax.ShapeDtypeStruct(tuple(dims), dtype)


def dot(a, b, dims=None):
    if dims is None:
        return jnp.dot(a, b, preferred_element_type=F32)
    return lax.dot_general(a, b, dims, preferred_element_type=F32)


def call(kernel, name, outs, in_specs, scratch=(), flops=0, moved=2 ** 18, limit=VMEM_LIMIT, **kwargs):
    return pl.pallas_call(
        kernel,
        out_shape=outs,
        in_specs=in_specs,
        scratch_shapes=list(scratch),
        compiler_params=pltpu.CompilerParams(vmem_limit_bytes=limit),
        cost_estimate=pl.CostEstimate(flops=flops, bytes_accessed=moved, transcendentals=0),
        name=name,
        **kwargs,
    )


def lanes(x3):
    return jnp.concatenate([x3[b] for b in range(x3.shape[0])], axis=1)


def request_kernel(peers, blocks_dev, count_ref, row_ref, col_ref, place_ref, *ask_refs):
    me = lax.axis_index("graph")
    col = col_ref[...]
    lane = lax.broadcasted_iota(jnp.int32, col.shape, 1)
    live = lane < count_ref[0]
    place = jnp.full(col.shape, peers * CAP * blocks_dev, jnp.int32)
    for k in range(peers):
        local = col - lax.rem(me + k, peers) * blocks_dev
        inside = live & (local >= 0) & (local < blocks_dev)
        low = jnp.min(jnp.where(inside, local, blocks_dev - 1), axis=1, keepdims=True)
        high = jnp.max(jnp.where(inside, local, 0), axis=1, keepdims=True)
        ask_refs[k][...] = jnp.where(lane == 0, low, high)
        slot = k * CAP + (local != low).astype(jnp.int32)
        place = jnp.where(inside, slot * blocks_dev + row_ref[...], place)
    place_ref[...] = place


def request(tile_row, tile_col, tile_count, peers, blocks_dev):
    per = tile_col.shape[0]
    outs = call(
        functools.partial(request_kernel, peers, blocks_dev),
        "request",
        [shape((1, per), jnp.int32)] * (peers + 1),
        [smem(), vmem(), vmem()],
        limit=VMEM_MOST,
    )(tile_count, tile_row.reshape(1, per), tile_col.reshape(1, per))
    return outs[0], list(outs[1:])


def operator_kernel(blocks_dev, slots_here, groups, place_ref, tiles_ref, m_ref, tiles, acc, sems):
    step = pl.program_id(0)
    per, width = tiles.shape[0], tiles.shape[1]
    chunks = per // CHUNK
    spare = slots_here * blocks_dev

    def chunk_copy(c):
        part = pl.ds(c * CHUNK, CHUNK)
        return pltpu.make_async_copy(tiles_ref.at[part], tiles.at[part], sems.at[c])

    @pl.when(step == 0)
    def _():
        for c in range(chunks):
            chunk_copy(c).start()

    acc[...] = jnp.zeros_like(acc)

    def add_chunk(c, carry):
        @pl.when(step == 0)
        def _():
            chunk_copy(c).wait()

        for u in range(CHUNK):
            t = c * CHUNK + u
            place = place_ref[0, t]
            if groups > 1:
                place = place - step * spare
                place = jnp.where((place >= 0) & (place < spare), place, spare)
            side = u % SIDES
            acc[side, place] = acc[side, place] + tiles[t].astype(F32)
        return carry

    lax.fori_loop(0, chunks, add_chunk, 0)
    for s in range(slots_here):
        for r in range(blocks_dev):
            total = acc[0, s * blocks_dev + r]
            for side in range(1, SIDES):
                total = total + acc[side, s * blocks_dev + r]
            m_ref[r * width : (r + 1) * width, s * width : (s + 1) * width] = total.astype(BF16)


def list_operator(tiles, place, peers, blocks_dev):
    per, width = tiles.shape[0], tiles.shape[1]
    slots = peers * CAP
    slots_here = min(slots, GROUP)
    groups = slots // slots_here
    return call(
        functools.partial(operator_kernel, blocks_dev, slots_here, groups),
        "operator",
        shape((blocks_dev * width, slots * width), BF16),
        [smem(), hbm()],
        [
            pltpu.VMEM((per, width, width), BF16),
            pltpu.VMEM((SIDES, slots_here * blocks_dev + 1, width, width), F32),
            pltpu.SemaphoreType.DMA((per // CHUNK,)),
        ],
        moved=2 ** 24,
        limit=VMEM_MOST,
        grid=(groups,),
        out_specs=pl.BlockSpec((blocks_dev * width, slots_here * width), lambda i: (0, i)),
    )(place, tiles)


def fill_sends(peers, x3, m_ref, ids_refs, mir, send_refs, self_ref, extra):
    blocks_dev, _, width = x3.shape
    slots = peers * CAP
    both = CAP * width
    near = lanes(x3)
    if slots <= GROUP:
        mir[...] = dot(near, m_ref[...])
    else:
        part = GROUP * width

        @pl.loop(0, slots // GROUP)
        def _(i):
            where = pl.ds(pl.multiple_of(i * part, part), part)
            mir[:, where] = dot(near, m_ref[:, where])

    self_ref[...] = mir[:, :both]
    for k in range(1, peers):
        out = send_refs[k - 1]
        out[:, :both] = mir[:, k * both : (k + 1) * both].astype(BF16)
        for s in range(CAP):
            at = (CAP + s) * width
            out[:, at : at + width] = x3[ids_refs[peers - k][0, s]]
        if extra is not None:
            out[:, 2 * both :] = extra


def first_sends_kernel(peers, *refs):
    ids_refs, refs = refs[:peers], refs[peers:]
    x3, cot, m_ref, refs = refs[0], refs[1], refs[2], refs[3:]
    cot_ref, mir = refs[peers:]
    share = cot_ref.shape[0]
    cot_ref[...] = cot[pl.ds(lax.axis_index("rep") * share, share)]
    fill_sends(peers, x3, m_ref, ids_refs, mir, refs[: peers - 1], refs[peers - 1], None)


def first_sends(values, cotangent, operator, ids, peers, reps):
    blocks_dev, columns, width = values.shape
    outs = call(
        functools.partial(first_sends_kernel, peers),
        "first_sends",
        [shape((columns, 2 * CAP * width), BF16)] * (peers - 1)
        + [shape((columns, CAP * width), F32), shape((blocks_dev // reps, columns, width), BF16)],
        [smem()] * peers + [vmem()] * 3,
        [pltpu.VMEM((columns, peers * CAP * width), F32)],
        flops=2 ** 28,
        moved=2 ** 21,
    )(*ids, values, cotangent, operator)
    return outs[: peers - 1], outs[peers - 1], outs[peers]


def add_blocks(acc, ids_ref, sums):
    width = acc.shape[2]
    for s in range(CAP):
        block = ids_ref[0, s]
        acc[block] = acc[block] + sums[:, s * width : (s + 1) * width].astype(F32)


def rows_kernel(peers, k, first, last, *refs):
    at = 0
    if first:
        own_ids, x3, self_ref = refs[:3]
        at = 3
    else:
        before = refs[0]
        at = 1
    ids_ref, came_ref, m_ref = refs[at : at + 3]
    outs = refs[at + 3 :]
    acc = outs[-1] if last else outs[0]
    blocks_dev, columns, width = acc.shape
    both = CAP * width
    there = (peers - k) * both
    own = dot(came_ref[:, both : 2 * both], m_ref[:, there : there + both], NT)
    if first:
        far = jnp.concatenate([x3[own_ids[0, s]] for s in range(CAP)], axis=1)
        own = own + dot(far, m_ref[:, :both], NT)
    for b in range(blocks_dev):
        add = own[:, b * width : (b + 1) * width]
        acc[b] = add if first else before[b] + add
    if first:
        add_blocks(acc, own_ids, self_ref)
    add_blocks(acc, ids_ref, came_ref[:, :both])
    if last == "split":
        give_ref, keep_ref = outs[:2]
        half = lax.axis_index("rep")
        share = give_ref.shape[0]
        give_ref[...] = acc[pl.ds((1 - half) * share, share)].astype(BF16)
        keep_ref[...] = acc[pl.ds(half * share, share)]
    elif last:
        outs[0][...] = acc[...].astype(BF16)


def rows_of(values, operator, ids, came, own_mirror, order, peers, reps, how):
    blocks_dev, columns, width = values.shape
    acc = None
    for k in order:
        first, last = k == order[0], how if k == order[-1] else ""
        if last == "split":
            share = (blocks_dev // reps, columns, width)
            outs = [shape(share, BF16), shape(share, F32)]
        else:
            outs = [shape(values.shape, BF16 if last else F32)]
        head = [ids[0], values, own_mirror] if first else [acc]
        specs = [smem(), vmem(), vmem()] if first else [vmem()]
        made = call(
            functools.partial(rows_kernel, peers, k, first, last),
            "rows",
            outs,
            specs + [smem(), vmem(), vmem()],
            [pltpu.VMEM(values.shape, F32)] if last else [],
            flops=2 ** 27,
            moved=2 ** 20,
            input_output_aliases={} if first or last else {0: 0},
        )(*head, ids[k], came[k], operator)
        acc = made[0]
    return made


def add_kernel(keep_ref, came_ref, out_ref):
    out_ref[...] = (keep_ref[...] + came_ref[...].astype(F32)).astype(BF16)


def add_up(keep, came):
    return call(add_kernel, "add_up", shape(came.shape, BF16), [vmem(), vmem()])(keep, came)


def dense_kernel(feats, *refs):
    sums, cots, refs = refs[:feats], refs[feats : 2 * feats], refs[2 * feats :]
    w_ref, act_ref, give_ref, spread_ref, keep_ref, wide, wide_cot, pre_scr, grad, term = refs
    share, columns, width = act_ref.shape
    me = lax.axis_index("feat")
    half = lax.axis_index("rep")
    rows = [pl.ds(pl.multiple_of(lax.rem(me + q, feats) * columns, columns), columns) for q in range(feats)]
    for q in range(feats):
        for b in range(share):
            wide[rows[q], b * width : (b + 1) * width] = sums[q][b]
            wide_cot[rows[q], b * width : (b + 1) * width] = cots[q][b]
    pre = dot(w_ref[...], wide[...], TN)
    pre_scr[...] = pre
    sig = jax.nn.sigmoid(pre)
    factor = wide_cot[...].astype(F32) * sig * (1.0 + pre * (1.0 - sig))
    grad[...] = factor.astype(BF16)
    spread = dot(w_ref[rows[0], :], grad[...]).astype(BF16)
    term[...] = dot(grad[rows[0], :], wide[...], NT)
    part = keep_ref.shape[1]
    wide_share = share * width
    give_ref[:, :wide_share] = spread
    give_ref[:, 2 * wide_share :] = term[:, pl.ds(pl.multiple_of((1 - half) * part, part), part)].astype(BF16)
    keep_ref[...] = term[:, pl.ds(pl.multiple_of(half * part, part), part)]
    for b in range(share):
        spread_ref[b] = spread[:, b * width : (b + 1) * width]
    own = pre_scr[rows[0], :]
    act = (own * jax.nn.sigmoid(own)).astype(BF16)
    give_ref[:, wide_share : 2 * wide_share] = act
    for b in range(share):
        act_ref[b] = act[:, b * width : (b + 1) * width]


def dense(sums, cots, weight, feats, reps):
    share, columns, width = sums[0].shape
    features = weight.shape[0]
    part = features // reps
    return call(
        functools.partial(dense_kernel, feats),
        "dense",
        [
            shape((share, columns, width), BF16),
            shape((columns, 2 * share * width + part), BF16),
            shape((share, columns, width), BF16),
            shape((columns, part), F32),
        ],
        [vmem()] * (2 * feats + 1),
        [
            pltpu.VMEM((features, share * width), BF16),
            pltpu.VMEM((features, share * width), BF16),
            pltpu.VMEM((features, share * width), F32),
            pltpu.VMEM((features, share * width), BF16),
            pltpu.VMEM((columns, features), F32),
        ],
        flops=2 ** 28,
        moved=2 ** 20,
    )(*sums, *cots, weight)


def send_kernel(peers, *refs):
    ids_refs, refs = refs[:peers], refs[peers:]
    mine_ref, act_ref, came_ref, keep_ref, m_ref, refs = refs[0], refs[1], refs[2], refs[3], refs[4], refs[5:]
    x3, joined, refs = refs[0], refs[1], refs[2:]
    send_refs, refs = refs[: peers - 1], refs[peers - 1 :]
    self_ref, term_ref, mir = refs
    share, _, width = mine_ref.shape
    wide_share = share * width
    half = lax.axis_index("rep")
    x3[pl.ds(half * share, share)] = mine_ref[...]
    joined[pl.ds(half * share, share)] = act_ref[...]
    for b in range(share):
        x3[(1 - half) * share + b] = came_ref[:, b * width : (b + 1) * width]
        joined[(1 - half) * share + b] = came_ref[:, wide_share + b * width : wide_share + (b + 1) * width]
    term = (keep_ref[...] + came_ref[:, 2 * wide_share :].astype(F32)).astype(BF16)
    term_ref[...] = term
    fill_sends(peers, x3, m_ref, ids_refs, mir, send_refs, self_ref, term)


def sends_of(mine, act, came, keep, operator, ids, peers, reps):
    share, columns, width = mine.shape
    whole = shape((share * reps, columns, width), BF16)
    return call(
        functools.partial(send_kernel, peers),
        "sends",
        [whole, whole]
        + [shape((columns, 2 * CAP * width + keep.shape[1]), BF16)] * (peers - 1)
        + [shape((columns, CAP * width), F32), shape(keep.shape, BF16)],
        [smem()] * peers + [vmem()] * 5,
        [pltpu.VMEM((columns, peers * CAP * width), F32)],
        flops=2 ** 28,
        moved=2 ** 21,
    )(*ids, mine, act, came, keep, operator)


def terms_kernel(peers, at, *refs):
    out_ref, terms = refs[peers], refs[peers + 1]
    me = lax.axis_index("graph")
    terms[0] = refs[0][...].astype(F32)
    for k in range(1, peers):
        terms[k] = refs[k][:, at:].astype(F32)
    total = terms[lax.rem(me, peers)]
    for p in range(1, peers):
        total = total + terms[lax.rem(me - p + peers, peers)]
    out_ref[...] = total


def sum_terms(terms, at):
    peers = len(terms)
    return call(
        functools.partial(terms_kernel, peers, at),
        "terms",
        shape(terms[0].shape, F32),
        [vmem()] * peers,
        [pltpu.VMEM((peers,) + terms[0].shape, F32)],
    )(*terms)


def finish_kernel(mine_ref, other_ref, share_ref, other_share_ref, grad_ref, weight_ref):
    half = lax.axis_index("rep")
    share = share_ref.shape[1]
    grad_ref[...] = (mine_ref[...].astype(F32) + other_ref[...].astype(F32)).astype(BF16)
    weight_ref[pl.ds(pl.multiple_of(half * share, share), share), :] = share_ref[...].T
    weight_ref[pl.ds(pl.multiple_of((1 - half) * share, share), share), :] = other_share_ref[...].T


def finish(mine, other, share, other_share):
    columns, width = share.shape
    return call(
        finish_kernel,
        "finish",
        [shape(mine.shape, BF16), shape((2 * width, columns), F32)],
        [vmem()] * 4,
    )(mine, other, share, other_share)


def ahead(value, axis, size, k):
    return lax.ppermute(value, axis, [(i, (i + k) % size) for i in range(size)])


def after(value, first):
    return lax.optimization_barrier((value, first))[0]


def shifts(peers):
    return sorted(range(1, peers), key=lambda k: (abs(2 * k - peers), k))


def local(features, weight, cotangent, tiles, tile_row, tile_col, tile_count):
    blocks_dev = features.shape[0]
    peers = lax.axis_size("graph")
    feats = lax.axis_size("feat")
    reps = lax.axis_size("rep")
    order = shifts(peers)

    place, wanted = request(tile_row, tile_col, tile_count, peers, blocks_dev)
    ids = [wanted[0]] + [ahead(wanted[k], "graph", peers, k) for k in range(1, peers)]
    place, ids = lax.optimization_barrier((place, ids))
    operator = list_operator(tiles, place, peers, blocks_dev)
    sends, own_mirror, own_cot = first_sends(features, cotangent, operator, ids, peers, reps)
    came = [None] * peers
    for k in order:
        came[k] = ahead(sends[k - 1], "graph", peers, k)
    cots = [own_cot]
    if feats > 1:
        held = after(own_cot, came[order[0]])
        cots += [ahead(held, "feat", feats, feats - q) for q in range(1, feats)]
    give, keep = rows_of(features, operator, ids, came, own_mirror, order, peers, reps, "split")

    given, cots = lax.optimization_barrier((ahead(give, "rep", reps, 1), cots))
    mine = add_up(keep, given)
    sums = [mine] + [ahead(mine, "feat", feats, feats - q) for q in range(1, feats)]
    act, give, spread, keep = dense(sums, cots, weight, feats, reps)
    outs = sends_of(spread, act, ahead(give, "rep", reps, 1), keep, operator, ids, peers, reps)
    values, activated, sends, own_mirror, term = outs[0], outs[1], outs[2 : peers + 1], outs[peers + 1], outs[peers + 2]

    came = [None] * peers
    for k in order:
        came[k] = ahead(sends[k - 1], "graph", peers, k)
    (part,) = rows_of(values, operator, ids, came, own_mirror, order, peers, reps, "whole")
    share = sum_terms([term] + came[1:], 2 * CAP * values.shape[2])
    input_grad, weight_grad = finish(
        part, ahead(part, "rep", reps, 1), share, ahead(share, "rep", reps, 1)
    )
    return (activated, input_grad, weight_grad)


def solution(mesh):
    placed = (
        P(("parts", "graph"), "feat", None),
        P(),
        P(("parts", "graph"), "feat", None),
        P(("parts", "graph", "rep"), None, None),
        P(("parts", "graph", "rep")),
        P(("parts", "graph", "rep")),
        P(("parts", "graph", "rep")),
    )
    return jax.shard_map(
        local,
        mesh=mesh,
        in_specs=placed,
        out_specs=(
            P(("parts", "graph"), "feat", None),
            P(("parts", "graph"), "feat", None),
            P("parts", "feat"),
        ),
        check_vma=False,
    )
```

time: 61.7 us -> 63 us (1.021)
  the two profiles are of different devices: /device:TPU:9 before, /device:TPU:0 now
where the time goes in v1:
time: 63 us; the launch traced here: 62.8 us
  waiting for transfers between devices  26.8 us (43%)
  starting transfers between devices  19.5 us (31%)
  Pallas kernels  13.7 us (22%)
  between operations  1.52 us (2%)
  local copies, waits for them, and re-layouts  1.32 us (2%)
    ppermute x15, waiting for transfers between devices, ahead(): return lax.ppermute(value, axis, [(i, (i + k) % size) for i in range(size)])  26.8 us
    ppermute x15, starting transfers between devices, ahead(): return lax.ppermute(value, axis, [(i, (i + k) % size) for i in range(size)])  19.5 us
    pallas_call x6, Pallas kernels, rows_of(): call(functools.partial(rows_kernel, peers, k, first, last), 'rows', outs,...  5.63 us
    pallas_call x1, Pallas kernels, list_operator(): call(functools.partial(operator_kernel, blocks_dev, slots_here, groups),...  3.56 us
    pallas_call x1, Pallas kernels, sends_of(): call(functools.partial(send_kernel, peers), 'sends', [whole, whole] + [sh...  1.65 us
    unnamed x10, local copies, waits for them, and re-layouts  1.32 us
  transfers between devices with their start and end apart: 15, of which 9 were waited for; matrix products, arithmetic and copies ran while one was open for 0% of the time, Pallas kernels for 8%

profile of v1, /device:TPU:0, one launch (start us, length us, event | category | flops | bytes accessed | tf_op | source)
XLA Modules:
  0.0 62.8 jit_solution(4202772054025879487)
XLA Ops:
  2.8 3.1 %collective-permute-start = (s32[1,128]{1,0:T(1,128)S(1)}, s32[1,128]{1,0:T(1,128)S(1)}, u32[]{:S(2)}, u32[]{:S(2)}) collective-permute-start(s32[1,128]{1,0:T(1,128)S(1)} %get-tuple-element.39), channel_id=1, source_target_pairs={{0,4},{4,8},{8,12},{12,0},{1,5},{5,9},{9,13},{13,1},{2,6},{6,10},{... | collective-permute-start | bytes 1544 | tf_op jit(solution)/shard_map/ppermute | solution.py:414
  5.9 2.6 %collective-permute-start.1 = (s32[1,128]{1,0:T(1,128)S(1)}, s32[1,128]{1,0:T(1,128)S(1)}, u32[]{:S(2)}, u32[]{:S(2)}) collective-permute-start(s32[1,128]{1,0:T(1,128)S(1)} %get-tuple-element.40), channel_id=1, source_target_pairs={{0,8},{4,12},{8,0},{12,4},{1,9},{5,13},{9,1},{13,5},{2,10},{6,14},... | collective-permute-start | bytes 1544 | tf_op jit(solution)/shard_map/ppermute | solution.py:414
  8.5 1.3 %collective-permute-start.2 = (s32[1,128]{1,0:T(1,128)S(1)}, s32[1,128]{1,0:T(1,128)S(1)}, u32[]{:S(2)}, u32[]{:S(2)}) collective-permute-start(s32[1,128]{1,0:T(1,128)S(1)} %get-tuple-element.41), channel_id=1, source_target_pairs={{0,12},{4,0},{8,4},{12,8},{1,13},{5,1},{9,5},{13,9},{2,14},{6,2},{... | collective-permute-start | bytes 1544 | tf_op jit(solution)/shard_map/ppermute | solution.py:414
  10.4 1.7 %collective-permute-done.2.refs_3_.refs_1_ = s32[1,128]{1,0:T(1,128)S(1)} collective-permute-done((s32[1,128]{1,0:T(1,128)S(1)}, s32[1,128]{1,0:T(1,128)S(1)}, u32[]{:S(2)}, u32[]{:S(2)}) %collective-permute-start.2) | collective-permute-done | bytes 544 | tf_op jit(solution)/shard_map/ppermute | solution.py:414
  12.0 3.6 %operator.1.refs_6_.refs_5_.refs_3_.refs_8_ = bf16[1024,1024]{1,0:T(8,128)(2,1)S(1)} custom-call(s32[1,128]{1,0:T(1,128)S(1)} %get-tuple-element.46.place_ref, bf16[128,128,128]{2,1,0:T(8,128)(2,1)} %tiles_ref.1), custom_call_target="tpu_custom_call" | custom-call | bytes 16777216 | tf_op jit(solution)/shard_map/operator/pallas_call | solution.py:137
  15.6 1.0 %first_sends.1 = (bf16[128,512]{1,0:T(8,128)(2,1)S(1)}, bf16[128,512]{1,0:T(8,128)(2,1)S(1)}, bf16[128,512]{1,0:T(8,128)(2,1)S(1)}, f32[128,256]{1,0:T(8,128)S(1)}, bf16[4,128,128]{2,1,0:T(8,128)(2,1)S(1)}) custom-call(s32[1,128]{1,0:T(1,128)S(1)} %get-tuple-element.42.refs_0_, s32[1,128]{1,0:T(1,128)S(1)} %collective-permute-done.refs_1_, ...), custom_call_target="tpu_custom_call" | custom-call | flops 268435456 | bytes 2097152 | tf_op jit(solution)/shard_map/first_sends/pallas_call | solution.py:191
  16.7 1.0 %collective-permute-start.3 = (bf16[128,512]{1,0:T(8,128)(2,1)S(1)}, bf16[128,512]{1,0:T(8,128)(2,1)S(1)}, u32[]{:S(2)}, u32[]{:S(2)}) collective-permute-start(bf16[128,512]{1,0:T(8,128)(2,1)S(1)} %get-tuple-element.48), channel_id=1, source_target_pairs={{0,8},{4,12},{8,0},{12,4},{1,9},{5,13},{9,1},{13,5},{2,10},{6,14},... | collective-permute-start | bytes 393224 | tf_op jit(solution)/shard_map/ppermute | solution.py:414
  17.6 2.8 %collective-permute-start.4 = (bf16[128,512]{1,0:T(8,128)(2,1)S(1)}, bf16[128,512]{1,0:T(8,128)(2,1)S(1)}, u32[]{:S(2)}, u32[]{:S(2)}) collective-permute-start(bf16[128,512]{1,0:T(8,128)(2,1)S(1)} %get-tuple-element.49), channel_id=1, source_target_pairs={{0,4},{4,8},{8,12},{12,0},{1,5},{5,9},{9,13},{13,1},{2,6},{6,10},{... | collective-permute-start | bytes 393224 | tf_op jit(solution)/shard_map/ppermute | solution.py:414
  20.4 1.0 %collective-permute-start.5 = (bf16[128,512]{1,0:T(8,128)(2,1)S(1)}, bf16[128,512]{1,0:T(8,128)(2,1)S(1)}, u32[]{:S(2)}, u32[]{:S(2)}) collective-permute-start(bf16[128,512]{1,0:T(8,128)(2,1)S(1)} %get-tuple-element.50), channel_id=1, source_target_pairs={{0,12},{4,0},{8,4},{12,8},{1,13},{5,1},{9,5},{13,9},{2,14},{6,2},{... | collective-permute-start | bytes 393224 | tf_op jit(solution)/shard_map/ppermute | solution.py:414
  21.4 6.0 %collective-permute-done.3.refs_4_ = bf16[128,512]{1,0:T(8,128)(2,1)S(1)} collective-permute-done((bf16[128,512]{1,0:T(8,128)(2,1)S(1)}, bf16[128,512]{1,0:T(8,128)(2,1)S(1)}, u32[]{:S(2)}, u32[]{:S(2)}) %collective-permute-start.3) | collective-permute-done | bytes 131104 | tf_op jit(solution)/shard_map/ppermute | solution.py:414
  27.4 1.5 %collective-permute-start.7 = (bf16[4,128,128]{2,1,0:T(8,128)(2,1)S(1)}, bf16[4,128,128]{2,1,0:T(8,128)(2,1)S(1)}, u32[]{:S(2)}, u32[]{:S(2)}) collective-permute-start(bf16[4,128,128]{2,1,0:T(8,128)(2,1)S(1)} %get-tuple-element.56.refs_2_), channel_id=1, source_target_pairs={{0,2},{2,0},{1,3},{3,1},{4,6},{6,4},{5,7},{7,5},{8,10},{10,8},{9,1... | collective-permute-start | bytes 393224 | tf_op jit(solution)/shard_map/ppermute | solution.py:414
  28.9 1.0 %rows.6.refs_0_ = f32[8,128,128]{2,1,0:T(8,128)S(1)} custom-call(s32[1,128]{1,0:T(1,128)S(1)} %get-tuple-element.42.refs_0_, bf16[8,128,128]{2,1,0:T(8,128)(2,1)S(1)} %copy-done, f32[128,256]{1,0:T(8,128)S(1)} %get-tuple-element.47.refs_2_, s32[1,128]{1,0:T(1,128)S(1)} %collective-permute-done.1.refs_2_.refs_3_, ...), custom_call_target="tpu_custom_call" | custom-call | flops 134217728 | bytes 1048576 | tf_op jit(solution)/shard_map/rows/pallas_call | solution.py:257
  30.9 0.9 %rows.8 = (bf16[4,128,128]{2,1,0:T(8,128)(2,1)S(1)}, f32[4,128,128]{2,1,0:T(8,128)S(1)}) custom-call(f32[8,128,128]{2,1,0:T(8,128)S(1)} %rows.7.refs_0_, s32[1,128]{1,0:T(1,128)S(1)} %collective-permute-done.2.refs_3_.refs_1_, bf16[128,512]{1,0:T(8,128)(2,1)S(1)} %collective-permute-done.5.refs_2_, bf16[1024,1024]{1,0:T(8,128)(2,1)S(1)} %operator.1.refs_6_.refs_5_.refs_3_.refs_8_), custom_call_target="tpu_custom_call" | custom-call | flops 134217728 | bytes 1048576 | tf_op jit(solution)/shard_map/rows/pallas_call | solution.py:257
  34.0 4.9 %collective-permute-done.8.refs_1_ = bf16[4,128,128]{2,1,0:T(8,128)(2,1)S(1)} collective-permute-done((bf16[4,128,128]{2,1,0:T(8,128)(2,1)S(1)}, bf16[4,128,128]{2,1,0:T(8,128)(2,1)S(1)}, u32[]{:S(2)}, u32[]{:S(2)}) %collective-permute-start.8) | collective-permute-done | bytes 131104 | tf_op jit(solution)/shard_map/ppermute | solution.py:414
  39.6 1.6 %collective-permute-done.9.refs_6_ = bf16[128,1152]{1,0:T(8,128)(2,1)S(1)} collective-permute-done((bf16[128,1152]{1,0:T(8,128)(2,1)S(1)}, bf16[128,1152]{1,0:T(8,128)(2,1)S(1)}, u32[]{:S(2)}, u32[]{:S(2)}) %collective-permute-start.9) | collective-permute-done | bytes 294944 | tf_op jit(solution)/shard_map/ppermute | solution.py:414
  41.2 1.6 %sends.1 = (bf16[8,128,128]{2,1,0:T(8,128)(2,1)S(1)}, bf16[8,128,128]{2,1,0:T(8,128)(2,1)}, bf16[128,640]{1,0:T(8,128)(2,1)S(1)}, bf16[128,640]{1,0:T(8,128)(2,1...) custom-call(s32[1,128]{1,0:T(1,128)S(1)} %get-tuple-element.42.refs_0_, ...), custom_call_target="tpu_custom_call" | custom-call | flops 268435456 | bytes 2097152 | tf_op jit(solution)/shard_map/sends/pallas_call | solution.py:359
  43.7 2.6 %collective-permute-start.11 = (bf16[128,640]{1,0:T(8,128)(2,1)S(1)}, bf16[128,640]{1,0:T(8,128)(2,1)S(1)}, u32[]{:S(2)}, u32[]{:S(2)}) collective-permute-start(bf16[128,640]{1,0:T(8,128)(2,1)S(1)} %get-tuple-element.66), channel_id=1, source_target_pairs={{0,4},{4,8},{8,12},{12,0},{1,5},{5,9},{9,13},{13,1},{2,6},{6,10},{... | collective-permute-start | bytes 491528 | tf_op jit(solution)/shard_map/ppermute | solution.py:414
  46.3 1.2 %collective-permute-start.12 = (bf16[128,640]{1,0:T(8,128)(2,1)S(1)}, bf16[128,640]{1,0:T(8,128)(2,1)S(1)}, u32[]{:S(2)}, u32[]{:S(2)}) collective-permute-start(bf16[128,640]{1,0:T(8,128)(2,1)S(1)} %get-tuple-element.67), channel_id=1, source_target_pairs={{0,12},{4,0},{8,4},{12,8},{1,13},{5,1},{9,5},{13,9},{2,14},{6,2},{... | collective-permute-start | bytes 491528 | tf_op jit(solution)/shard_map/ppermute | solution.py:414
  47.5 9.9 %collective-permute-done.10.refs_4_.refs_2_ = bf16[128,640]{1,0:T(8,128)(2,1)S(1)} collective-permute-done((bf16[128,640]{1,0:T(8,128)(2,1)S(1)}, bf16[128,640]{1,0:T(8,128)(2,1)S(1)}, u32[]{:S(2)}, u32[]{:S(2)}) %collective-permute-start.10) | collective-permute-done | bytes 163872 | tf_op jit(solution)/shard_map/ppermute | solution.py:414
  57.4 1.0 %rows.9.refs_0_ = f32[8,128,128]{2,1,0:T(8,128)S(1)} custom-call(s32[1,128]{1,0:T(1,128)S(1)} %get-tuple-element.42.refs_0_, bf16[8,128,128]{2,1,0:T(8,128)(2,1)S(1)} %get-tuple-element.63.refs_1_, f32[128,256]{1,0:T(8,128)S(1)} %get-tuple-element.64.refs_2_, s32[1,128]{1,0:T(1,128)S(1)} %collective-permute-done.1.refs_2_.refs_3_, ...), custom_call_target="tpu_custom_call" | custom-call | flops 134217728 | bytes 1048576 | tf_op jit(solution)/shard_map/rows/pallas_call | solution.py:257
  58.4 0.9 %rows.10.refs_0_ = f32[8,128,128]{2,1,0:T(8,128)S(1)} custom-call(f32[8,128,128]{2,1,0:T(8,128)S(1)} %rows.9.refs_0_, s32[1,128]{1,0:T(1,128)S(1)} %collective-permute-done.refs_1_, bf16[128,640]{1,0:T(8,128)(2,1)S(1)} %collective-permute-done.11.refs_2_.refs_1_, ...), custom_call_target="tpu_custom_call", output_to_operand_aliasing={{}: (0, {})} | custom-call | flops 134217728 | bytes 1048576 | tf_op jit(solution)/shard_map/rows/pallas_call | solution.py:257
  59.3 0.9 %rows.11.mine_ref = bf16[8,128,128]{2,1,0:T(8,128)(2,1)S(1)} custom-call(f32[8,128,128]{2,1,0:T(8,128)S(1)} %rows.10.refs_0_, s32[1,128]{1,0:T(1,128)S(1)} %collective-permute-done.2.refs_3_.refs_1_, bf16[128,640]{1,0:T(8,128)(2,1)S(1)} %collective-permute-done.12.refs_2_.refs_3_, bf16[1024,1024]{1,0:T(8,128)(2,1)S(1)} %operator.1.refs_6_.refs_5_.refs_3_.refs_8_), custom_call_target="tpu_custom_call" | custom-call | flops 134217728 | bytes 1048576 | tf_op jit(solution)/shard_map/rows/pallas_call | solution.py:257
  60.9 1.0 %collective-permute-done.14.other_share_ref = f32[128,128]{1,0:T(8,128)S(1)} collective-permute-done((f32[128,128]{1,0:T(8,128)S(1)}, f32[128,128]{1,0:T(8,128)S(1)}, u32[]{:S(2)}, u32[]{:S(2)}) %collective-permute-start.14) | collective-permute-done | bytes 65568 | tf_op jit(solution)/shard_map/ppermute | solution.py:414
  61.9 0.9 %finish.1 = (bf16[8,128,128]{2,1,0:T(8,128)(2,1)}, f32[256,128]{1,0:T(8,128)}) custom-call(bf16[8,128,128]{2,1,0:T(8,128)(2,1)S(1)} %rows.11.mine_ref, bf16[8,128,128]{2,1,0:T(8,128)(2,1)S(1)} %collective-permute-done.13.other_ref, f32[128,128]{1,0:T(8,128)S(1)} %terms.1.share_ref, f32[128,128]{1,0:T(8,128)S(1)} %collective-permute-done.14.other_share_ref), custom_call_target="tpu_custom_call" | custom-call | bytes 262144 | tf_op jit(solution)/shard_map/finish/pallas_call | solution.py:405
  (30 shorter events, 7.3 us)
Async XLA Ops:
  0.6 15.0 %copy-start = (bf16[8,128,128]{2,1,0:T(8,128)(2,1)S(1)}, bf16[8,128,128]{2,1,0:T(8,128)(2,1)}, u32[]{:S(2)}) copy-start(bf16[8,128,128]{2,1,0:T(8,128)(2,1)} %refs_1_.1) | copy-start | bytes 786436
  0.6 15.0 %copy-start.1 = (bf16[8,128,128]{2,1,0:T(8,128)(2,1)S(1)}, bf16[8,128,128]{2,1,0:T(8,128)(2,1)}, u32[]{:S(2)}) copy-start(bf16[8,128,128]{2,1,0:T(8,128)(2,1)} %refs_5_.1) | copy-start | bytes 786436
  1.4 0.7 %copy-start.3 = (s32[128]{0:T(128)S(1)}, s32[128]{0:T(128)}, u32[]{:S(2)}) copy-start(s32[128]{0:T(128)} %param.11) | copy-start | bytes 1540
  2.0 0.7 %copy-start.4 = (s32[128]{0:T(128)S(1)}, s32[128]{0:T(128)}, u32[]{:S(2)}) copy-start(s32[128]{0:T(128)} %param.12) | copy-start | bytes 1540
  2.8 7.0 %collective-permute-start = (s32[1,128]{1,0:T(1,128)S(1)}, s32[1,128]{1,0:T(1,128)S(1)}, u32[]{:S(2)}, u32[]{:S(2)}) collective-permute-start(s32[1,128]{1,0:T(1,128)S(1)} %get-tuple-element.39), channel_id=1, source_target_pairs={{0,4},{4,8},{8,12},{12,0},{1,5},{5,9},{9,13},{13,1},{2,6},{6,10},{... | collective-permute-start | bytes 1544 | tf_op jit(solution)/shard_map/ppermute | solution.py:414
  5.9 4.4 %collective-permute-start.1 = (s32[1,128]{1,0:T(1,128)S(1)}, s32[1,128]{1,0:T(1,128)S(1)}, u32[]{:S(2)}, u32[]{:S(2)}) collective-permute-start(s32[1,128]{1,0:T(1,128)S(1)} %get-tuple-element.40), channel_id=1, source_target_pairs={{0,8},{4,12},{8,0},{12,4},{1,9},{5,13},{9,1},{13,5},{2,10},{6,14},... | collective-permute-start | bytes 1544 | tf_op jit(solution)/shard_map/ppermute | solution.py:414
  8.5 3.5 %collective-permute-start.2 = (s32[1,128]{1,0:T(1,128)S(1)}, s32[1,128]{1,0:T(1,128)S(1)}, u32[]{:S(2)}, u32[]{:S(2)}) collective-permute-start(s32[1,128]{1,0:T(1,128)S(1)} %get-tuple-element.41), channel_id=1, source_target_pairs={{0,12},{4,0},{8,4},{12,8},{1,13},{5,1},{9,5},{13,9},{2,14},{6,2},{... | collective-permute-start | bytes 1544 | tf_op jit(solution)/shard_map/ppermute | solution.py:414
  16.7 10.8 %collective-permute-start.3 = (bf16[128,512]{1,0:T(8,128)(2,1)S(1)}, bf16[128,512]{1,0:T(8,128)(2,1)S(1)}, u32[]{:S(2)}, u32[]{:S(2)}) collective-permute-start(bf16[128,512]{1,0:T(8,128)(2,1)S(1)} %get-tuple-element.48), channel_id=1, source_target_pairs={{0,8},{4,12},{8,0},{12,4},{1,9},{5,13},{9,1},{13,5},{2,10},{6,14},... | collective-permute-start | bytes 393224 | tf_op jit(solution)/shard_map/ppermute | solution.py:414
  17.6 12.4 %collective-permute-start.4 = (bf16[128,512]{1,0:T(8,128)(2,1)S(1)}, bf16[128,512]{1,0:T(8,128)(2,1)S(1)}, u32[]{:S(2)}, u32[]{:S(2)}) collective-permute-start(bf16[128,512]{1,0:T(8,128)(2,1)S(1)} %get-tuple-element.49), channel_id=1, source_target_pairs={{0,4},{4,8},{8,12},{12,0},{1,5},{5,9},{9,13},{13,1},{2,6},{6,10},{... | collective-permute-start | bytes 393224 | tf_op jit(solution)/shard_map/ppermute | solution.py:414
  20.4 10.4 %collective-permute-start.5 = (bf16[128,512]{1,0:T(8,128)(2,1)S(1)}, bf16[128,512]{1,0:T(8,128)(2,1)S(1)}, u32[]{:S(2)}, u32[]{:S(2)}) collective-permute-start(bf16[128,512]{1,0:T(8,128)(2,1)S(1)} %get-tuple-element.50), channel_id=1, source_target_pairs={{0,12},{4,0},{8,4},{12,8},{1,13},{5,1},{9,5},{13,9},{2,14},{6,2},{... | collective-permute-start | bytes 393224 | tf_op jit(solution)/shard_map/ppermute | solution.py:414
  27.4 5.0 %collective-permute-start.7 = (bf16[4,128,128]{2,1,0:T(8,128)(2,1)S(1)}, bf16[4,128,128]{2,1,0:T(8,128)(2,1)S(1)}, u32[]{:S(2)}, u32[]{:S(2)}) collective-permute-start(bf16[4,128,128]{2,1,0:T(8,128)(2,1)S(1)} %get-tuple-element.56.refs_2_), channel_id=1, source_target_pairs={{0,2},{2,0},{1,3},{3,1},{4,6},{6,4},{5,7},{7,5},{8,10},{10,8},{9,1... | collective-permute-start | bytes 393224 | tf_op jit(solution)/shard_map/ppermute | solution.py:414
  28.9 9.9 %copy-start.2 = (bf16[256,256]{1,0:T(8,128)(2,1)S(1)}, bf16[256,256]{1,0:T(8,128)(2,1)}, u32[]{:S(2)}) copy-start(bf16[256,256]{1,0:T(8,128)(2,1)} %refs_4_.3) | copy-start | bytes 393220
  31.8 1.4 %collective-permute-start.6 = (bf16[4,128,128]{2,1,0:T(8,128)(2,1)S(1)}, bf16[4,128,128]{2,1,0:T(8,128)(2,1)S(1)}, u32[]{:S(2)}, u32[]{:S(2)}) collective-permute-start(bf16[4,128,128]{2,1,0:T(8,128)(2,1)S(1)} %get-tuple-element.52), channel_id=1, source_target_pairs={{0,1},{1,0},{2,3},{3,2},{4,5},{5,4},{6,7},{7,6},{8,9},{9,8},{10,11... | collective-permute-start | bytes 393224 | tf_op jit(solution)/shard_map/ppermute | solution.py:414
  33.2 5.6 %collective-permute-start.8 = (bf16[4,128,128]{2,1,0:T(8,128)(2,1)S(1)}, bf16[4,128,128]{2,1,0:T(8,128)(2,1)S(1)}, u32[]{:S(2)}, u32[]{:S(2)}) collective-permute-start(bf16[4,128,128]{2,1,0:T(8,128)(2,1)S(1)} %add_up.1.refs_0_), channel_id=1, source_target_pairs={{0,2},{2,0},{1,3},{3,1},{4,6},{6,4},{5,7},{7,5},{8,10},{10,8},{9,1... | collective-permute-start | bytes 393224 | tf_op jit(solution)/shard_map/ppermute | solution.py:414
  39.6 1.6 %collective-permute-start.9 = (bf16[128,1152]{1,0:T(8,128)(2,1)S(1)}, bf16[128,1152]{1,0:T(8,128)(2,1)S(1)}, u32[]{:S(2)}, u32[]{:S(2)}) collective-permute-start(bf16[128,1152]{1,0:T(8,128)(2,1)S(1)} %get-tuple-element.60), channel_id=1, source_target_pairs={{0,1},{1,0},{2,3},{3,2},{4,5},{5,4},{6,7},{7,6},{8,9},{9,8},{10,11... | collective-permute-start | bytes 884744 | tf_op jit(solution)/shard_map/ppermute | solution.py:414
  42.8 14.5 %collective-permute-start.10 = (bf16[128,640]{1,0:T(8,128)(2,1)S(1)}, bf16[128,640]{1,0:T(8,128)(2,1)S(1)}, u32[]{:S(2)}, u32[]{:S(2)}) collective-permute-start(bf16[128,640]{1,0:T(8,128)(2,1)S(1)} %get-tuple-element.65), channel_id=1, source_target_pairs={{0,8},{4,12},{8,0},{12,4},{1,9},{5,13},{9,1},{13,5},{2,10},{6,14},... | collective-permute-start | bytes 491528 | tf_op jit(solution)/shard_map/ppermute | solution.py:414
  43.7 14.8 %collective-permute-start.11 = (bf16[128,640]{1,0:T(8,128)(2,1)S(1)}, bf16[128,640]{1,0:T(8,128)(2,1)S(1)}, u32[]{:S(2)}, u32[]{:S(2)}) collective-permute-start(bf16[128,640]{1,0:T(8,128)(2,1)S(1)} %get-tuple-element.66), channel_id=1, source_target_pairs={{0,4},{4,8},{8,12},{12,0},{1,5},{5,9},{9,13},{13,1},{2,6},{6,10},{... | collective-permute-start | bytes 491528 | tf_op jit(solution)/shard_map/ppermute | solution.py:414
  46.3 13.1 %collective-permute-start.12 = (bf16[128,640]{1,0:T(8,128)(2,1)S(1)}, bf16[128,640]{1,0:T(8,128)(2,1)S(1)}, u32[]{:S(2)}, u32[]{:S(2)}) collective-permute-start(bf16[128,640]{1,0:T(8,128)(2,1)S(1)} %get-tuple-element.67), channel_id=1, source_target_pairs={{0,12},{4,0},{8,4},{12,8},{1,13},{5,1},{9,5},{13,9},{2,14},{6,2},{... | collective-permute-start | bytes 491528 | tf_op jit(solution)/shard_map/ppermute | solution.py:414
  60.2 1.7 %collective-permute-start.13 = (bf16[8,128,128]{2,1,0:T(8,128)(2,1)S(1)}, bf16[8,128,128]{2,1,0:T(8,128)(2,1)S(1)}, u32[]{:S(2)}, u32[]{:S(2)}) collective-permute-start(bf16[8,128,128]{2,1,0:T(8,128)(2,1)S(1)} %rows.11.mine_ref), channel_id=1, source_target_pairs={{0,1},{1,0},{2,3},{3,2},{4,5},{5,4},{6,7},{7,6},{8,9},{9,8},{10,11... | collective-permute-start | bytes 786440 | tf_op jit(solution)/shard_map/ppermute | solution.py:414
  60.4 1.6 %collective-permute-start.14 = (f32[128,128]{1,0:T(8,128)S(1)}, f32[128,128]{1,0:T(8,128)S(1)}, u32[]{:S(2)}, u32[]{:S(2)}) collective-permute-start(f32[128,128]{1,0:T(8,128)S(1)} %terms.1.share_ref), channel_id=1, source_target_pairs={{0,1},{1,0},{2,3},{3,2},{4,5},{5,4},{6,7},{7,6},{8,9},{9,8},{10,11... | collective-permute-start | bytes 196616 | tf_op jit(solution)/shard_map/ppermute | solution.py:414

commit v2 on v1

v2 whole, which is shorter than its diff:
```python
import functools

import jax
import jax.numpy as jnp
from jax import lax
from jax.experimental import pallas as pl
from jax.experimental.pallas import tpu as pltpu
from jax.sharding import PartitionSpec as P

CAP = 2
GROUP = 8
CHUNK = 16
SIDES = 2
TAIL = 16
VMEM_LIMIT = 40 * 2 ** 20
VMEM_MOST = 50 * 2 ** 20
VMEM_ALL = 58 * 2 ** 20

NT = (((1,), (1,)), ((), ()))
TN = (((0,), (0,)), ((), ()))
F32 = jnp.float32
BF16 = jnp.bfloat16


def vmem():
    return pl.BlockSpec(memory_space=pltpu.VMEM)


def smem():
    return pl.BlockSpec(memory_space=pltpu.SMEM)


def hbm():
    return pl.BlockSpec(memory_space=pltpu.HBM)


def shape(dims, dtype):
    return jax.ShapeDtypeStruct(tuple(dims), dtype)


def dot(a, b, dims=None):
    if dims is None:
        return jnp.dot(a, b, preferred_element_type=F32)
    return lax.dot_general(a, b, dims, preferred_element_type=F32)


def call(kernel, name, outs, in_specs, scratch=(), flops=0, moved=2 ** 18, limit=VMEM_LIMIT, **kwargs):
    return pl.pallas_call(
        kernel,
        out_shape=outs,
        in_specs=in_specs,
        scratch_shapes=list(scratch),
        compiler_params=pltpu.CompilerParams(vmem_limit_bytes=limit),
        cost_estimate=pl.CostEstimate(flops=flops, bytes_accessed=moved, transcendentals=0),
        name=name,
        **kwargs,
    )


def lanes(x3):
    return jnp.concatenate([x3[b] for b in range(x3.shape[0])], axis=1)


def prepare_kernel(peers, count_ref, row_ref, col_ref, x3, cot, place_ref, half_ref, cot_ref, *ask_refs):
    blocks_dev = x3.shape[0]
    share = half_ref.shape[0]
    mine = pl.ds(lax.axis_index("rep") * share, share)
    half_ref[...] = x3[mine]
    cot_ref[...] = cot[mine]
    me = lax.axis_index("graph")
    col = col_ref[...]
    lane = lax.broadcasted_iota(jnp.int32, col.shape, 1)
    live = lane < count_ref[0]
    place = jnp.full(col.shape, peers * CAP * blocks_dev, jnp.int32)
    for k in range(peers):
        local = col - jnp.bitwise_xor(me, k) * blocks_dev
        inside = live & (local >= 0) & (local < blocks_dev)
        low = jnp.min(jnp.where(inside, local, blocks_dev - 1), axis=1, keepdims=True)
        high = jnp.max(jnp.where(inside, local, 0), axis=1, keepdims=True)
        ask_refs[k][...] = jnp.where(lane == 0, low, high)
        slot = k * CAP + (local != low).astype(jnp.int32)
        place = jnp.where(inside, slot * blocks_dev + row_ref[...], place)
    place_ref[...] = place


def prepare(features, cotangent, tile_row, tile_col, tile_count, peers, reps):
    per = tile_col.shape[0]
    blocks_dev, columns, width = features.shape
    share = shape((blocks_dev // reps, columns, width), BF16)
    outs = call(
        functools.partial(prepare_kernel, peers),
        "prepare",
        [shape((1, per), jnp.int32), share, share] + [shape((1, per), jnp.int32)] * peers,
        [smem()] + [vmem()] * 4,
        limit=VMEM_ALL,
    )(tile_count, tile_row.reshape(1, per), tile_col.reshape(1, per), features, cotangent)
    return outs[0], outs[1], outs[2], list(outs[3:])


def pick(ids_ref, lane):
    ids = ids_ref[...].astype(F32)
    at = lax.broadcasted_iota(jnp.int32, ids.shape, 1)
    return jnp.max(jnp.where(at == lane, ids, 0.0)).astype(jnp.int32)


def operator_kernel(blocks_dev, slots_here, groups, place_in, tiles_ref, m_ref, tiles, acc, place_ref, sems, sem):
    step = pl.program_id(0)
    per, width = tiles.shape[0], tiles.shape[1]
    chunks = per // CHUNK
    spare = slots_here * blocks_dev

    def chunk_copy(c):
        part = pl.ds(c * CHUNK, CHUNK)
        return pltpu.make_async_copy(tiles_ref.at[part], tiles.at[part], sems.at[c])

    @pl.when(step == 0)
    def _():
        placed = pltpu.make_async_copy(place_in, place_ref, sem)
        placed.start()
        for c in range(chunks):
            chunk_copy(c).start()
        placed.wait()

    acc[...] = jnp.zeros_like(acc)

    def add_chunk(c, carry):
        @pl.when(step == 0)
        def _():
            chunk_copy(c).wait()

        for u in range(CHUNK):
            t = c * CHUNK + u
            place = place_ref[0, t]
            if groups > 1:
                place = place - step * spare
                place = jnp.where((place >= 0) & (place < spare), place, spare)
            side = u % SIDES
            acc[side, place] = acc[side, place] + tiles[t].astype(F32)
        return carry

    lax.fori_loop(0, chunks, add_chunk, 0)
    for s in range(slots_here):
        for r in range(blocks_dev):
            total = acc[0, s * blocks_dev + r]
            for side in range(1, SIDES):
                total = total + acc[side, s * blocks_dev + r]
            m_ref[r * width : (r + 1) * width, s * width : (s + 1) * width] = total.astype(BF16)


def list_operator(tiles, place, peers, blocks_dev):
    per, width = tiles.shape[0], tiles.shape[1]
    slots = peers * CAP
    slots_here = min(slots, GROUP)
    groups = slots // slots_here
    return call(
        functools.partial(operator_kernel, blocks_dev, slots_here, groups),
        "operator",
        shape((blocks_dev * width, slots * width), BF16),
        [pl.BlockSpec(memory_space=pl.ANY), hbm()],
        [
            pltpu.VMEM((per, width, width), BF16),
            pltpu.VMEM((SIDES, slots_here * blocks_dev + 1, width, width), F32),
            pltpu.SMEM((1, per), jnp.int32),
            pltpu.SemaphoreType.DMA((per // CHUNK,)),
            pltpu.SemaphoreType.DMA,
        ],
        moved=2 ** 24,
        limit=VMEM_MOST,
        grid=(groups,),
        out_specs=pl.BlockSpec((blocks_dev * width, slots_here * width), lambda i: (0, i)),
    )(place, tiles)


def mirrored(near, m_ref, mir, slots, width):
    if slots <= GROUP:
        mir[...] = dot(near, m_ref[...])
    else:
        part = GROUP * width

        @pl.loop(0, slots // GROUP)
        def _(i):
            where = pl.ds(pl.multiple_of(i * part, part), part)
            mir[:, where] = dot(near, m_ref[:, where])


def first_sends_kernel(peers, *refs):
    ask_refs, refs = refs[: peers - 1], refs[peers - 1 :]
    x3, m_ref, refs = refs[0], refs[1], refs[2:]
    send_refs, self_ref, mir = refs[: peers - 1], refs[peers - 1], refs[peers]
    _, columns, width = x3.shape
    both = CAP * width
    mirrored(lanes(x3), m_ref, mir, peers * CAP, width)
    self_ref[...] = mir[:, :both]
    lane = lax.broadcasted_iota(jnp.int32, (TAIL, both), 1)
    for k in range(1, peers):
        out = send_refs[k - 1]
        out[:columns, :] = mir[:, k * both : (k + 1) * both].astype(BF16)
        low, high = ask_refs[k - 1][:, :1], ask_refs[k - 1][:, 1:2]
        out[columns:, :] = jnp.where(lane < width, low, high).astype(F32).astype(BF16)


def first_sends(values, operator, asks, peers):
    _, columns, width = values.shape
    outs = call(
        functools.partial(first_sends_kernel, peers),
        "first_sends",
        [shape((columns + TAIL, CAP * width), BF16)] * (peers - 1) + [shape((columns, CAP * width), F32)],
        [vmem()] * (peers + 1),
        [pltpu.VMEM((columns, peers * CAP * width), F32)],
        flops=2 ** 28,
        moved=2 ** 21,
    )(*asks, values, operator)
    return [None] + list(outs[: peers - 1]), outs[peers - 1]


def add_sums(acc, block, sums):
    acc[block] = acc[block] + sums.astype(F32)


def own_rows(far, m_ref, k):
    both = far.shape[1]
    return dot(far, m_ref[:, k * both : (k + 1) * both], NT)


def put_rows(acc, own, before=None):
    blocks_dev, _, width = acc.shape
    for b in range(blocks_dev):
        add = own[:, b * width : (b + 1) * width]
        acc[b] = add if before is None else before[b] + add


def split_rows(acc, give_ref, keep_ref):
    half = lax.axis_index("rep")
    share = give_ref.shape[0]
    give_ref[...] = acc[pl.ds((1 - half) * share, share)].astype(BF16)
    keep_ref[...] = acc[pl.ds(half * share, share)]


def self_rows(x3, m_ref, ask_ref):
    far = jnp.concatenate([x3[pick(ask_ref, s)] for s in range(CAP)], axis=1)
    return own_rows(far, m_ref, 0)


def far_of(block, mine_ref, other_ref, ask_ref, at=0):
    half = lax.axis_index("rep")
    share = block.shape[0] // 2
    block[pl.ds(half * share, share)] = mine_ref[at * share : (at + 1) * share]
    block[pl.ds((1 - half) * share, share)] = other_ref[at * share : (at + 1) * share]
    return jnp.concatenate([block[pick(ask_ref, s)] for s in range(CAP)], axis=1)


def first_rows_kernel(peers, *refs):
    ask_ref, refs = refs[0], refs[1:]
    came_refs, refs = refs[: peers - 1], refs[peers - 1 :]
    x3, m_ref, self_ref, acc, ids_refs = refs[0], refs[1], refs[2], refs[3], refs[4:]
    _, columns, width = x3.shape
    put_rows(acc, self_rows(x3, m_ref, ask_ref))
    for s in range(CAP):
        add_sums(acc, pick(ask_ref, s), self_ref[:, s * width : (s + 1) * width])
    lane = lax.broadcasted_iota(jnp.int32, ids_refs[0].shape, 1)
    for k in range(1, peers):
        came = came_refs[k - 1]
        ids = jnp.zeros(lane.shape, jnp.int32)
        for s in range(CAP):
            here = slice(s * width, (s + 1) * width)
            asked = jnp.max(came[columns:, here].astype(F32)).astype(jnp.int32)
            ids = jnp.where(lane == s, asked, ids)
            add_sums(acc, asked, came[:columns, here])
        ids_refs[k - 1][...] = ids


def first_rows(values, operator, ask, came, own_mirror, peers):
    _, columns, width = values.shape
    outs = call(
        functools.partial(first_rows_kernel, peers),
        "first_rows",
        [shape(values.shape, F32)] + [shape((1, width), jnp.int32)] * (peers - 1),
        [vmem()] * (peers + 3),
        flops=2 ** 27,
        moved=2 ** 20,
    )(ask, *came[1:], values, operator, own_mirror)
    return outs[0], [None] + list(outs[1:])


def stack_kernel(*refs):
    share = refs[0].shape[0]
    for i, ref in enumerate(refs[:-1]):
        refs[-1][i * share : (i + 1) * share] = ref[...]


def stack(pieces):
    share, columns, width = pieces[0].shape
    out = shape((len(pieces) * share, columns, width), BF16)
    return call(stack_kernel, "stack", out, [vmem()] * len(pieces))(*pieces)


def far_rows_kernel(peers, *refs):
    ask_refs, refs = refs[: peers - 1], refs[peers - 1 :]
    before, mine_ref, other_ref, m_ref, give_ref, keep_ref, acc, block, far = refs
    both = CAP * acc.shape[2]
    for k in range(1, peers):
        far[:, k * both : (k + 1) * both] = far_of(block, mine_ref, other_ref, ask_refs[k - 1], k - 1)
    if peers * CAP <= GROUP:
        own = dot(far[:, both:], m_ref[:, both:], NT)
    else:

        def add_peer(k, total):
            here = pl.ds(pl.multiple_of(k * both, both), both)
            return total + dot(far[:, here], m_ref[:, here], NT)

        own = lax.fori_loop(1, peers, add_peer, jnp.zeros((acc.shape[1], m_ref.shape[0]), F32))
    put_rows(acc, own, before)
    split_rows(acc, give_ref, keep_ref)


def far_rows(before, asks, mine, other, operator, peers, reps):
    blocks_dev, columns, width = before.shape
    share = (blocks_dev // reps, columns, width)
    return call(
        functools.partial(far_rows_kernel, peers),
        "far_rows",
        [shape(share, BF16), shape(share, F32)],
        [vmem()] * (peers + 3),
        [
            pltpu.VMEM(before.shape, F32),
            pltpu.VMEM(before.shape, BF16),
            pltpu.VMEM((columns, peers * CAP * width), BF16),
        ],
        flops=2 ** 28,
        moved=2 ** 21,
    )(*asks[1:], before, mine, other, operator)


def late_rows_kernel(ks, first, last, *refs):
    if first:
        ask_ref, x3, self_ref = refs[:3]
    else:
        before = refs[0]
    refs = refs[3 if first else 1 :]
    ids_refs, refs = refs[: len(ks)], refs[len(ks) :]
    came_refs, refs = refs[: len(ks)], refs[len(ks) :]
    m_ref, out_ref = refs[:2]
    acc = refs[2] if last else out_ref
    width = acc.shape[2]
    both = CAP * width
    own = self_rows(x3, m_ref, ask_ref) if first else None
    for i, k in enumerate(ks):
        add = own_rows(came_refs[i][:, both : 2 * both], m_ref, k)
        own = add if own is None else own + add
    put_rows(acc, own, None if first else before)
    if first:
        for s in range(CAP):
            add_sums(acc, pick(ask_ref, s), self_ref[:, s * width : (s + 1) * width])
    for i in range(len(ks)):
        for s in range(CAP):
            add_sums(acc, pick(ids_refs[i], s), came_refs[i][:, s * width : (s + 1) * width])
    if last:
        out_ref[...] = acc[...].astype(BF16)


def late_rows(head, ids, came, ks, operator, first, last):
    values = head[1] if first else head[0]
    return call(
        functools.partial(late_rows_kernel, ks, first, last),
        "late_rows",
        shape(values.shape, BF16 if last else F32),
        [vmem()] * (len(head) + 2 * len(ks) + 1),
        [pltpu.VMEM(values.shape, F32)] if last else [],
        flops=2 ** 27,
        moved=2 ** 20,
    )(*head, *[ids[k] for k in ks], *[came[k] for k in ks], operator)


def add_kernel(keep_ref, came_ref, out_ref):
    out_ref[...] = (keep_ref[...] + came_ref[...].astype(F32)).astype(BF16)


def add_up(keep, came):
    return call(add_kernel, "add_up", shape(came.shape, BF16), [vmem(), vmem()])(keep, came)


def dense_kernel(feats, *refs):
    sums, cots, refs = refs[:feats], refs[feats : 2 * feats], refs[2 * feats :]
    w_ref, act_ref, give_ref, spread_ref, keep_ref, wide, wide_cot, pre_scr, grad, term = refs
    share, columns, width = act_ref.shape
    me = lax.axis_index("feat")
    half = lax.axis_index("rep")
    rows = [pl.ds(pl.multiple_of(lax.rem(me + q, feats) * columns, columns), columns) for q in range(feats)]
    for q in range(feats):
        for b in range(share):
            wide[rows[q], b * width : (b + 1) * width] = sums[q][b]
            wide_cot[rows[q], b * width : (b + 1) * width] = cots[q][b]
    pre = dot(w_ref[...], wide[...], TN)
    pre_scr[...] = pre
    sig = jax.nn.sigmoid(pre)
    factor = wide_cot[...].astype(F32) * sig * (1.0 + pre * (1.0 - sig))
    grad[...] = factor.astype(BF16)
    spread = dot(w_ref[rows[0], :], grad[...]).astype(BF16)
    term[...] = dot(grad[rows[0], :], wide[...], NT)
    part = keep_ref.shape[1]
    wide_share = share * width
    give_ref[:, :wide_share] = spread
    give_ref[:, 2 * wide_share :] = term[:, pl.ds(pl.multiple_of((1 - half) * part, part), part)].astype(BF16)
    keep_ref[...] = term[:, pl.ds(pl.multiple_of(half * part, part), part)]
    for b in range(share):
        spread_ref[b] = spread[:, b * width : (b + 1) * width]
    own = pre_scr[rows[0], :]
    act = (own * jax.nn.sigmoid(own)).astype(BF16)
    give_ref[:, wide_share : 2 * wide_share] = act
    for b in range(share):
        act_ref[b] = act[:, b * width : (b + 1) * width]


def dense(sums, cots, weight, feats, reps):
    share, columns, width = sums[0].shape
    features = weight.shape[0]
    part = features // reps
    return call(
        functools.partial(dense_kernel, feats),
        "dense",
        [
            shape((share, columns, width), BF16),
            shape((columns, 2 * share * width + part), BF16),
            shape((share, columns, width), BF16),
            shape((columns, part), F32),
        ],
        [vmem()] * (2 * feats + 1),
        [
            pltpu.VMEM((features, share * width), BF16),
            pltpu.VMEM((features, share * width), BF16),
            pltpu.VMEM((features, share * width), F32),
            pltpu.VMEM((features, share * width), BF16),
            pltpu.VMEM((columns, features), F32),
        ],
        flops=2 ** 28,
        moved=2 ** 20,
    )(*sums, *cots, weight)


def send_kernel(peers, *refs):
    ids_refs, refs = refs[: peers - 1], refs[peers - 1 :]
    mine_ref, came_ref, keep_ref, m_ref, refs = refs[0], refs[1], refs[2], refs[3], refs[4:]
    x3, refs = refs[0], refs[1:]
    send_refs, refs = refs[: peers - 1], refs[peers - 1 :]
    self_ref, term_ref, mir = refs
    share, _, width = mine_ref.shape
    both = CAP * width
    half = lax.axis_index("rep")
    x3[pl.ds(half * share, share)] = mine_ref[...]
    for b in range(share):
        x3[(1 - half) * share + b] = came_ref[:, b * width : (b + 1) * width]
    term = (keep_ref[...] + came_ref[:, 2 * share * width :].astype(F32)).astype(BF16)
    term_ref[...] = term
    mirrored(lanes(x3), m_ref, mir, peers * CAP, width)
    self_ref[...] = mir[:, :both]
    for k in range(1, peers):
        out = send_refs[k - 1]
        out[:, :both] = mir[:, k * both : (k + 1) * both].astype(BF16)
        for s in range(CAP):
            at = (CAP + s) * width
            out[:, at : at + width] = x3[pick(ids_refs[k - 1], s)]
    send_refs[0][:, 2 * both :] = term


def sends_of(mine, came, keep, operator, ids, peers, reps):
    share, columns, width = mine.shape
    chunk = 2 * CAP * width
    outs = call(
        functools.partial(send_kernel, peers),
        "sends",
        [shape((share * reps, columns, width), BF16), shape((columns, chunk + keep.shape[1]), BF16)]
        + [shape((columns, chunk), BF16)] * (peers - 2)
        + [shape((columns, CAP * width), F32), shape(keep.shape, BF16)],
        [vmem()] * (peers + 3),
        [pltpu.VMEM((columns, peers * CAP * width), F32)],
        flops=2 ** 28,
        moved=2 ** 21,
    )(*ids[1:], mine, came, keep, operator)
    return outs[0], [None] + list(outs[1:peers]), outs[peers], outs[peers + 1]


def pair_kernel(at, mine_ref, came_ref, out_ref):
    total = mine_ref[...].astype(F32) + came_ref[:, at:].astype(F32)
    out_ref[...] = total.astype(out_ref.dtype)


def pair_sum(mine, came, at, dtype):
    return call(functools.partial(pair_kernel, at), "pair_sum", shape(mine.shape, dtype), [vmem(), vmem()])(
        mine, came
    )


def finish_kernel(mine_ref, other_ref, share_ref, other_share_ref, act_ref, came_ref, grad_ref, weight_ref, out_ref):
    half = lax.axis_index("rep")
    share = share_ref.shape[1]
    grad_ref[...] = (mine_ref[...].astype(F32) + other_ref[...].astype(F32)).astype(BF16)
    weight_ref[pl.ds(pl.multiple_of(half * share, share), share), :] = share_ref[...].T
    weight_ref[pl.ds(pl.multiple_of((1 - half) * share, share), share), :] = other_share_ref[...].T
    blocks, _, width = act_ref.shape
    out_ref[pl.ds(half * blocks, blocks)] = act_ref[...]
    for b in range(blocks):
        at = (blocks + b) * width
        out_ref[(1 - half) * blocks + b] = came_ref[:, at : at + width]


def finish(mine, other, share, other_share, act, came):
    columns, width = share.shape
    return call(
        finish_kernel,
        "finish",
        [shape(mine.shape, BF16), shape((2 * width, columns), F32), shape(mine.shape, BF16)],
        [vmem()] * 6,
    )(mine, other, share, other_share, act, came)


def ahead(value, axis, size, k):
    return lax.ppermute(value, axis, [(i, (i + k) % size) for i in range(size)])


def across(value, peers, k):
    return lax.ppermute(value, "graph", [(i, i ^ k) for i in range(peers)])


def after(value, first):
    return lax.optimization_barrier((value, first))[0]


def local(features, weight, cotangent, tiles, tile_row, tile_col, tile_count):
    blocks_dev, _, width = features.shape
    peers = lax.axis_size("graph")
    feats = lax.axis_size("feat")
    reps = lax.axis_size("rep")
    far_first = sorted(range(1, peers), key=lambda k: (-(k & (peers // 2)), k))

    place, half, own_cot, asks = prepare(features, cotangent, tile_row, tile_col, tile_count, peers, reps)
    operator = list_operator(tiles, place, peers, blocks_dev)
    sends, own_mirror = first_sends(features, operator, asks[1:], peers)
    pieces, held = {0: half}, [0]
    bit = peers // 2
    while bit:
        for k in held:
            piece = after(pieces[k], sends[1]) if k else half
            pieces[k ^ bit] = across(piece, peers, bit)
        held = held + [k ^ bit for k in held]
        bit //= 2
    came = [None] * peers
    for k in far_first:
        came[k] = across(sends[k], peers, k)
    cots = [own_cot]
    if feats > 1:
        waited = after(own_cot, pieces[peers // 2])
        cots += [ahead(waited, "feat", feats, feats - q) for q in range(1, feats)]
    arrived = [pieces[k] for k in range(1, peers)]
    arrived, came, cots = lax.optimization_barrier((arrived, came, cots))
    stacked = stack(arrived)
    swapped = ahead(stacked, "rep", reps, 1)
    acc, ids = first_rows(features, operator, asks[0], came, own_mirror, peers)
    give, keep = far_rows(acc, asks, stacked, swapped, operator, peers, reps)

    mine = add_up(keep, ahead(give, "rep", reps, 1))
    sums = [mine] + [ahead(mine, "feat", feats, feats - q) for q in range(1, feats)]
    act, give, spread, keep = dense(sums, cots, weight, feats, reps)
    shared = ahead(give, "rep", reps, 1)
    values, sends, own_mirror, term = sends_of(spread, shared, keep, operator, ids, peers, reps)

    came = [None] * peers
    for k in far_first:
        came[k] = across(sends[k], peers, k)
    total = pair_sum(term, came[1], 2 * CAP * width, F32 if peers == 2 else BF16)
    bit = 2
    while bit < peers:
        total = pair_sum(total, across(total, peers, bit), 0, F32 if 2 * bit == peers else BF16)
        bit *= 2
    ends = [peers // 2]
    acc = late_rows([asks[0], values, own_mirror], ids, came, [k for k in range(1, peers) if k not in ends], operator, True, False)
    acc, total = lax.optimization_barrier((acc, total))
    part = late_rows([acc], ids, came, ends, operator, False, True)
    input_grad, weight_grad, activated = finish(
        part, ahead(part, "rep", reps, 1), total, ahead(total, "rep", reps, 1), act, shared
    )
    return (activated, input_grad, weight_grad)


def solution(mesh):
    placed = (
        P(("parts", "graph"), "feat", None),
        P(),
        P(("parts", "graph"), "feat", None),
        P(("parts", "graph", "rep"), None, None),
        P(("parts", "graph", "rep")),
        P(("parts", "graph", "rep")),
        P(("parts", "graph", "rep")),
    )
    return jax.shard_map(
        local,
        mesh=mesh,
        in_specs=placed,
        out_specs=(
            P(("parts", "graph"), "feat", None),
            P(("parts", "graph"), "feat", None),
            P("parts", "feat"),
        ),
        check_vma=False,
    )
```

time: 63 us -> 58.6 us (0.930)
  Pallas kernels: 13.7 us -> 9.89 us
  starting transfers between devices: 19.5 us -> 22.7 us
  waiting for transfers between devices: 26.8 us -> 23.6 us
  local copies, waits for them, and re-layouts: 1.32 us -> 0.69 us
    ppermute x0 -> x10, starting transfers between devices: none -> 19.6 us  [across(): return lax.ppermute(value, 'graph', [(i, i ^ k) for i in range(peers)])]
    ppermute x15 -> x7, waiting for transfers between devices: 26.8 us -> 10.1 us  [ahead(): return lax.ppermute(value, axis, [(i, (i + k) % size) for i in range(size)])]
    ppermute x15 -> x7, starting transfers between devices: 19.5 us -> 3.16 us  [ahead(): return lax.ppermute(value, axis, [(i, (i + k) % size) for i in range(size)])]
    ppermute x0 -> x10, waiting for transfers between devices: none -> 13.5 us  [across(): return lax.ppermute(value, 'graph', [(i, i ^ k) for i in range(peers)])]
    pallas_call x9, Pallas kernels: 7.49 us -> 4.66 us  [the longest x1 1.86 us: prepare(): call(functools.partial(prepare_kernel, peers), 'prepare', [shape((1, per)...]
    unnamed x10 -> x18, local copies, waits for them, and re-layouts: 1.32 us -> 0.69 us
  transfers between devices with their start and end apart: 15 -> 17, of which waited for: 9 -> 10; matrix products, arithmetic and copies ran while one was open for 0% -> 0% of each run, Pallas kernels for 8% -> 8%
where the time goes in v2:
time: 58.6 us; the launch traced here: 58.4 us
  waiting for transfers between devices  23.6 us (40%)
  starting transfers between devices  22.7 us (39%)
  Pallas kernels  9.89 us (17%)
  between operations  1.52 us (3%)
  local copies, waits for them, and re-layouts  0.69 us (1%)
    ppermute x10, starting transfers between devices, across(): return lax.ppermute(value, 'graph', [(i, i ^ k) for i in range(peers)])  19.6 us
    ppermute x10, waiting for transfers between devices, across(): return lax.ppermute(value, 'graph', [(i, i ^ k) for i in range(peers)])  13.5 us
    ppermute x7, waiting for transfers between devices, ahead(): return lax.ppermute(value, axis, [(i, (i + k) % size) for i in range(size)])  10.1 us
    ppermute x7, starting transfers between devices, ahead(): return lax.ppermute(value, axis, [(i, (i + k) % size) for i in range(size)])  3.16 us
    pallas_call x1, Pallas kernels, list_operator(): call(functools.partial(operator_kernel, blocks_dev, slots_here, groups),...  3.07 us
    pallas_call x1, Pallas kernels, prepare(): call(functools.partial(prepare_kernel, peers), 'prepare', [shape((1, per)...  1.86 us
  transfers between devices with their start and end apart: 17, of which 10 were waited for; matrix products, arithmetic and copies ran while one was open for 0% of the time, Pallas kernels for 8%

profile of v2, /device:TPU:0, one launch (start us, length us, event | category | flops | bytes accessed | tf_op | source)
XLA Modules:
  0.0 58.4 jit_solution(15955599170360410533)
XLA Ops:
  1.3 1.9 %prepare.1 = (s32[1,128]{1,0:T(1,128)}, bf16[4,128,128]{2,1,0:T(8,128)(2,1)}, bf16[4,128,128]{2,1,0:T(8,128)(2,1)}, s32[1,128]{1,0:T(1,128)}, s32[1,128]{1,0:T(1...) custom-call(s32[1]{0:T(128)S(6)} %copy.10.count_ref, s32[1,128]{1,0:T(1,128)} %bitcast.2, s32[1,128]{1,0:T(1,128)} %bitcast.3, ...), custom_call_target="tpu_custom_call" | custom-call | bytes 262144 | tf_op jit(solution)/shard_map/prepare/pallas_call | solution.py:90
  3.2 4.1 %collective-permute-start.1 = (bf16[4,128,128]{2,1,0:T(8,128)(2,1)}, bf16[4,128,128]{2,1,0:T(8,128)(2,1)S(1)}, u32[]{:S(2)}, u32[]{:S(2)}) collective-permute-start(bf16[4,128,128]{2,1,0:T(8,128)(2,1)} %get-tuple-element.46), channel_id=1, source_target_pairs={{0,8},{4,12},{8,0},{12,4},{1,9},{5,13},{9,1},{13,5},{2,10},{6,14},... | collective-permute-start | bytes 393224 | tf_op jit(solution)/shard_map/ppermute | solution.py:521
  8.0 3.1 %operator.1.refs_4_.refs_5_.refs_6_.refs_7_.refs_3_ = bf16[1024,1024]{1,0:T(8,128)(2,1)S(1)} custom-call(s32[1,128]{1,0:T(1,128)S(1)} %copy-done.5, bf16[128,128,128]{2,1,0:T(8,128)(2,1)} %tiles_ref.1), custom_call_target="tpu_custom_call" | custom-call | bytes 16777216 | tf_op jit(solution)/shard_map/operator/pallas_call | solution.py:155
  11.7 1.9 %collective-permute-start = (bf16[4,128,128]{2,1,0:T(8,128)(2,1)S(1)}, bf16[4,128,128]{2,1,0:T(8,128)(2,1)S(1)}, u32[]{:S(2)}, u32[]{:S(2)}) collective-permute-start(bf16[4,128,128]{2,1,0:T(8,128)(2,1)S(1)} %copy-done.8), channel_id=1, source_target_pairs={{0,4},{4,0},{8,12},{12,8},{1,5},{5,1},{9,13},{13,9},{2,6},{6,2},{1... | collective-permute-start | bytes 393224 | tf_op jit(solution)/shard_map/ppermute | solution.py:521
  13.8 1.5 %collective-permute-start.6 = (bf16[4,128,128]{2,1,0:T(8,128)(2,1)S(1)}, bf16[4,128,128]{2,1,0:T(8,128)(2,1)S(1)}, u32[]{:S(2)}, u32[]{:S(2)}) collective-permute-start(bf16[4,128,128]{2,1,0:T(8,128)(2,1)S(1)} %copy-done.7), channel_id=1, source_target_pairs={{0,2},{2,0},{1,3},{3,1},{4,6},{6,4},{5,7},{7,5},{8,10},{10,8},{9,1... | collective-permute-start | bytes 393224 | tf_op jit(solution)/shard_map/ppermute | solution.py:517
  15.4 2.2 %collective-permute-start.2 = (bf16[4,128,128]{2,1,0:T(8,128)(2,1)S(1)}, bf16[4,128,128]{2,1,0:T(8,128)(2,1)S(1)}, u32[]{:S(2)}, u32[]{:S(2)}) collective-permute-start(bf16[4,128,128]{2,1,0:T(8,128)(2,1)S(1)} %collective-permute-done.1.refs_1_), channel_id=1, source_target_pairs={{0,4},{4,0},{8,12},{12,8},{1,5},{5,1},{9,13},{13,9},{2,6},{6,2},{1... | collective-permute-start | bytes 393224 | tf_op jit(solution)/shard_map/ppermute | solution.py:521
  17.6 3.0 %collective-permute-start.5 = (bf16[144,256]{1,0:T(8,128)(2,1)S(1)}, bf16[144,256]{1,0:T(8,128)(2,1)S(1)}, u32[]{:S(2)}, u32[]{:S(2)}) collective-permute-start(bf16[144,256]{1,0:T(8,128)(2,1)S(1)} %get-tuple-element.54), channel_id=1, source_target_pairs={{0,12},{4,8},{8,4},{12,0},{1,13},{5,9},{9,5},{13,1},{2,14},{6,10},... | collective-permute-start | bytes 221192 | tf_op jit(solution)/shard_map/ppermute | solution.py:521
  20.6 1.1 %collective-permute-start.3 = (bf16[144,256]{1,0:T(8,128)(2,1)S(1)}, bf16[144,256]{1,0:T(8,128)(2,1)S(1)}, u32[]{:S(2)}, u32[]{:S(2)}) collective-permute-start(bf16[144,256]{1,0:T(8,128)(2,1)S(1)} %get-tuple-element.51), channel_id=1, source_target_pairs={{0,4},{4,0},{8,12},{12,8},{1,5},{5,1},{9,13},{13,9},{2,6},{6,2},{1... | collective-permute-start | bytes 221192 | tf_op jit(solution)/shard_map/ppermute | solution.py:521
  21.8 4.4 %collective-permute-done.5.refs_3_ = bf16[144,256]{1,0:T(8,128)(2,1)S(1)} collective-permute-done((bf16[144,256]{1,0:T(8,128)(2,1)S(1)}, bf16[144,256]{1,0:T(8,128)(2,1)S(1)}, u32[]{:S(2)}, u32[]{:S(2)}) %collective-permute-start.5) | collective-permute-done | bytes 73760 | tf_op jit(solution)/shard_map/ppermute | solution.py:521
  26.7 1.3 %collective-permute-done.7.refs_5_ = bf16[12,128,128]{2,1,0:T(8,128)(2,1)S(1)} collective-permute-done((bf16[12,128,128]{2,1,0:T(8,128)(2,1)S(1)}, bf16[12,128,128]{2,1,0:T(8,128)(2,1)S(1)}, u32[]{:S(2)}, u32[]{:S(2)}) %collective-permute-start.7) | collective-permute-done | bytes 393248 | tf_op jit(solution)/shard_map/ppermute | solution.py:517
  28.0 0.8 %far_rows.1 = (bf16[4,128,128]{2,1,0:T(8,128)(2,1)S(1)}, f32[4,128,128]{2,1,0:T(8,128)S(1)}) custom-call(s32[1,128]{1,0:T(1,128)S(1)} %copy-done.2, s32[1,128]{1,0:T(1,128)S(1)} %copy-done.3, s32[1,128]{1,0:T(1,128)S(1)} %copy-done.4, f32[8,128,128]{2,1,0:T(8,128)S(1)} %get-tuple-element.64.refs_3_, bf16[12,128,128]{2,1,0:T(8,128)(2,1)S(1)} %stack.1.refs_4_, ...), custom_call_target="tpu_custom_call" | custom-call | flops 268435456 | bytes 2097152 | tf_op jit(solution)/shard_map/far_rows/pallas_call | solution.py:319
  29.0 1.2 %collective-permute-done.8.came_ref = bf16[4,128,128]{2,1,0:T(8,128)(2,1)S(1)} collective-permute-done((bf16[4,128,128]{2,1,0:T(8,128)(2,1)S(1)}, bf16[4,128,128]{2,1,0:T(8,128)(2,1)S(1)}, u32[]{:S(2)}, u32[]{:S(2)}) %collective-permute-start.8) | collective-permute-done | bytes 131104 | tf_op jit(solution)/shard_map/ppermute | solution.py:517
  30.2 0.7 %collective-permute-start.9 = (bf16[4,128,128]{2,1,0:T(8,128)(2,1)S(1)}, bf16[4,128,128]{2,1,0:T(8,128)(2,1)S(1)}, u32[]{:S(2)}, u32[]{:S(2)}) collective-permute-start(bf16[4,128,128]{2,1,0:T(8,128)(2,1)S(1)} %add_up.1.refs_0_), channel_id=1, source_target_pairs={{0,2},{2,0},{1,3},{3,1},{4,6},{6,4},{5,7},{7,5},{8,10},{10,8},{9,1... | collective-permute-start | bytes 393224 | tf_op jit(solution)/shard_map/ppermute | solution.py:517
  30.9 4.9 %collective-permute-done.9.refs_1_ = bf16[4,128,128]{2,1,0:T(8,128)(2,1)S(1)} collective-permute-done((bf16[4,128,128]{2,1,0:T(8,128)(2,1)S(1)}, bf16[4,128,128]{2,1,0:T(8,128)(2,1)S(1)}, u32[]{:S(2)}, u32[]{:S(2)}) %collective-permute-start.9) | collective-permute-done | bytes 131104 | tf_op jit(solution)/shard_map/ppermute | solution.py:517
  35.8 0.7 %dense.1 = (bf16[4,128,128]{2,1,0:T(8,128)(2,1)S(1)}, bf16[128,1152]{1,0:T(8,128)(2,1)S(1)}, bf16[4,128,128]{2,1,0:T(8,128)(2,1)S(1)}, f32[128,128]{1,0:T(8,128)S(1)}) custom-call(bf16[4,128,128]{2,1,0:T(8,128)(2,1)S(1)} %add_up.1.refs_0_, bf16[4,128,128]{2,1,0:T(8,128)(2,1)S(1)} %collective-permute-done.9.refs_1_, bf16[4,128,128]{2,1,0:T(8,128)(2,1)S(1)} %copy-done.7, ...), custom_call_target="tpu_custom_call" | custom-call | flops 268435456 | bytes 1048576 | tf_op jit(solution)/shard_map/dense/pallas_call | solution.py:418
  36.6 1.6 %collective-permute-done.10.refs_4_.came_ref = bf16[128,1152]{1,0:T(8,128)(2,1)S(1)} collective-permute-done((bf16[128,1152]{1,0:T(8,128)(2,1)S(1)}, bf16[128,1152]{1,0:T(8,128)(2,1)S(1)}, u32[]{:S(2)}, u32[]{:S(2)}) %collective-permute-start.10) | collective-permute-done | bytes 294944 | tf_op jit(solution)/shard_map/ppermute | solution.py:517
  38.8 2.8 %collective-permute-start.12 = (bf16[128,512]{1,0:T(8,128)(2,1)S(1)}, bf16[128,512]{1,0:T(8,128)(2,1)S(1)}, u32[]{:S(2)}, u32[]{:S(2)}) collective-permute-start(bf16[128,512]{1,0:T(8,128)(2,1)S(1)} %get-tuple-element.78), channel_id=1, source_target_pairs={{0,12},{4,8},{8,4},{12,0},{1,13},{5,9},{9,5},{13,1},{2,14},{6,10},... | collective-permute-start | bytes 393224 | tf_op jit(solution)/shard_map/ppermute | solution.py:521
  42.2 2.8 %collective-permute-done.11.refs_5_.came_ref = bf16[128,640]{1,0:T(8,128)(2,1)S(1)} collective-permute-done((bf16[128,640]{1,0:T(8,128)(2,1)S(1)}, bf16[128,640]{1,0:T(8,128)(2,1)S(1)}, u32[]{:S(2)}, u32[]{:S(2)}) %collective-permute-start.11) | collective-permute-done | bytes 163872 | tf_op jit(solution)/shard_map/ppermute | solution.py:521
  45.1 3.6 %collective-permute-start.13 = (bf16[128,128]{1,0:T(8,128)(2,1)S(1)}, bf16[128,128]{1,0:T(8,128)(2,1)S(1)}, u32[]{:S(2)}, u32[]{:S(2)}) collective-permute-start(bf16[128,128]{1,0:T(8,128)(2,1)S(1)} %pair_sum.2.mine_ref), channel_id=1, source_target_pairs={{0,8},{4,12},{8,0},{12,4},{1,9},{5,13},{9,1},{13,5},{2,10},{6,14},... | collective-permute-start | bytes 98312 | tf_op jit(solution)/shard_map/ppermute | solution.py:521
  48.7 0.8 %collective-permute-done.12.refs_6_ = bf16[128,512]{1,0:T(8,128)(2,1)S(1)} collective-permute-done((bf16[128,512]{1,0:T(8,128)(2,1)S(1)}, bf16[128,512]{1,0:T(8,128)(2,1)S(1)}, u32[]{:S(2)}, u32[]{:S(2)}) %collective-permute-start.12) | collective-permute-done | bytes 131104 | tf_op jit(solution)/shard_map/ppermute | solution.py:521
  49.4 0.7 %late_rows.2.refs_0_ = f32[8,128,128]{2,1,0:T(8,128)S(1)} custom-call(s32[1,128]{1,0:T(1,128)S(1)} %copy-done.1, bf16[8,128,128]{2,1,0:T(8,128)(2,1)S(1)} %get-tuple-element.75.refs_1_, f32[128,256]{1,0:T(8,128)S(1)} %get-tuple-element.76.refs_2_, s32[1,128]{1,0:T(1,128)S(1)} %get-tuple-element.61.refs_0_.refs_3_, ...), custom_call_target="tpu_custom_call" | custom-call | flops 134217728 | bytes 1048576 | tf_op jit(solution)/shard_map/late_rows/pallas_call | solution.py:363
  50.2 5.2 %collective-permute-done.13.came_ref = bf16[128,128]{1,0:T(8,128)(2,1)S(1)} collective-permute-done((bf16[128,128]{1,0:T(8,128)(2,1)S(1)}, bf16[128,128]{1,0:T(8,128)(2,1)S(1)}, u32[]{:S(2)}, u32[]{:S(2)}) %collective-permute-start.13) | collective-permute-done | bytes 32800 | tf_op jit(solution)/shard_map/ppermute | solution.py:521
  56.3 1.1 %collective-permute-done.16.other_share_ref = f32[128,128]{1,0:T(8,128)S(1)} collective-permute-done((f32[128,128]{1,0:T(8,128)S(1)}, f32[128,128]{1,0:T(8,128)S(1)}, u32[]{:S(2)}, u32[]{:S(2)}) %collective-permute-start.16) | collective-permute-done | bytes 65568 | tf_op jit(solution)/shard_map/ppermute | solution.py:517
  57.4 1.0 %finish.1 = (bf16[8,128,128]{2,1,0:T(8,128)(2,1)}, f32[256,128]{1,0:T(8,128)}, bf16[8,128,128]{2,1,0:T(8,128)(2,1)}) custom-call(bf16[8,128,128]{2,1,0:T(8,128)(2,1)S(1)} %late_rows.3.mine_ref, bf16[8,128,128]{2,1,0:T(8,128)(2,1)S(1)} %collective-permute-done.15.other_ref, f32[128,128]{1,0:T(8,128)S(1)} %pair_sum.3.share_ref, ...), custom_call_target="tpu_custom_call" | custom-call | bytes 262144 | tf_op jit(solution)/shard_map/finish/pallas_call | solution.py:508
  (42 shorter events, 4.5 us)
Async XLA Ops:
  0.6 10.4 %copy-start = (bf16[8,128,128]{2,1,0:T(8,128)(2,1)S(1)}, bf16[8,128,128]{2,1,0:T(8,128)(2,1)}, u32[]{:S(2)}) copy-start(bf16[8,128,128]{2,1,0:T(8,128)(2,1)} %refs_4_.2) | copy-start | bytes 786436
  3.2 7.9 %copy-start.2 = (s32[1,128]{1,0:T(1,128)S(1)}, s32[1,128]{1,0:T(1,128)}, u32[]{:S(2)}) copy-start(s32[1,128]{1,0:T(1,128)} %get-tuple-element.47.refs_0_) | copy-start | bytes 1540
  3.2 7.9 %copy-start.3 = (s32[1,128]{1,0:T(1,128)S(1)}, s32[1,128]{1,0:T(1,128)}, u32[]{:S(2)}) copy-start(s32[1,128]{1,0:T(1,128)} %get-tuple-element.48.refs_1_) | copy-start | bytes 1540
  3.2 7.9 %copy-start.4 = (s32[1,128]{1,0:T(1,128)S(1)}, s32[1,128]{1,0:T(1,128)}, u32[]{:S(2)}) copy-start(s32[1,128]{1,0:T(1,128)} %get-tuple-element.49.refs_2_) | copy-start | bytes 1540
  3.2 10.6 %collective-permute-start.1 = (bf16[4,128,128]{2,1,0:T(8,128)(2,1)}, bf16[4,128,128]{2,1,0:T(8,128)(2,1)S(1)}, u32[]{:S(2)}, u32[]{:S(2)}) collective-permute-start(bf16[4,128,128]{2,1,0:T(8,128)(2,1)} %get-tuple-element.46), channel_id=1, source_target_pairs={{0,8},{4,12},{8,0},{12,4},{1,9},{5,13},{9,1},{13,5},{2,10},{6,14},... | collective-permute-start | bytes 393224 | tf_op jit(solution)/shard_map/ppermute | solution.py:521
  8.0 5.9 %copy-start.7 = (bf16[4,128,128]{2,1,0:T(8,128)(2,1)S(1)}, bf16[4,128,128]{2,1,0:T(8,128)(2,1)}, u32[]{:S(2)}) copy-start(bf16[4,128,128]{2,1,0:T(8,128)(2,1)} %get-tuple-element.70.refs_2_) | copy-start | bytes 393220
  8.0 18.3 %copy-start.1 = (s32[1,128]{1,0:T(1,128)S(1)}, s32[1,128]{1,0:T(1,128)}, u32[]{:S(2)}) copy-start(s32[1,128]{1,0:T(1,128)} %get-tuple-element.45.refs_0_) | copy-start | bytes 1540
  11.6 24.3 %copy-start.6 = (bf16[256,256]{1,0:T(8,128)(2,1)S(1)}, bf16[256,256]{1,0:T(8,128)(2,1)}, u32[]{:S(2)}) copy-start(bf16[256,256]{1,0:T(8,128)(2,1)} %refs_4_.3) | copy-start | bytes 393220
  11.6 9.1 %collective-permute-start.4 = (bf16[144,256]{1,0:T(8,128)(2,1)S(1)}, bf16[144,256]{1,0:T(8,128)(2,1)S(1)}, u32[]{:S(2)}, u32[]{:S(2)}) collective-permute-start(bf16[144,256]{1,0:T(8,128)(2,1)S(1)} %get-tuple-element.53), channel_id=1, source_target_pairs={{0,8},{4,12},{8,0},{12,4},{1,9},{5,13},{9,1},{13,5},{2,10},{6,14},... | collective-permute-start | bytes 221192 | tf_op jit(solution)/shard_map/ppermute | solution.py:521
  11.7 14.5 %collective-permute-start = (bf16[4,128,128]{2,1,0:T(8,128)(2,1)S(1)}, bf16[4,128,128]{2,1,0:T(8,128)(2,1)S(1)}, u32[]{:S(2)}, u32[]{:S(2)}) collective-permute-start(bf16[4,128,128]{2,1,0:T(8,128)(2,1)S(1)} %copy-done.8), channel_id=1, source_target_pairs={{0,4},{4,0},{8,12},{12,8},{1,5},{5,1},{9,13},{13,9},{2,6},{6,2},{1... | collective-permute-start | bytes 393224 | tf_op jit(solution)/shard_map/ppermute | solution.py:521
  13.8 12.3 %collective-permute-start.6 = (bf16[4,128,128]{2,1,0:T(8,128)(2,1)S(1)}, bf16[4,128,128]{2,1,0:T(8,128)(2,1)S(1)}, u32[]{:S(2)}, u32[]{:S(2)}) collective-permute-start(bf16[4,128,128]{2,1,0:T(8,128)(2,1)S(1)} %copy-done.7), channel_id=1, source_target_pairs={{0,2},{2,0},{1,3},{3,1},{4,6},{6,4},{5,7},{7,5},{8,10},{10,8},{9,1... | collective-permute-start | bytes 393224 | tf_op jit(solution)/shard_map/ppermute | solution.py:517
  15.4 10.8 %collective-permute-start.2 = (bf16[4,128,128]{2,1,0:T(8,128)(2,1)S(1)}, bf16[4,128,128]{2,1,0:T(8,128)(2,1)S(1)}, u32[]{:S(2)}, u32[]{:S(2)}) collective-permute-start(bf16[4,128,128]{2,1,0:T(8,128)(2,1)S(1)} %collective-permute-done.1.refs_1_), channel_id=1, source_target_pairs={{0,4},{4,0},{8,12},{12,8},{1,5},{5,1},{9,13},{13,9},{2,6},{6,2},{1... | collective-permute-start | bytes 393224 | tf_op jit(solution)/shard_map/ppermute | solution.py:521
  17.6 8.5 %collective-permute-start.5 = (bf16[144,256]{1,0:T(8,128)(2,1)S(1)}, bf16[144,256]{1,0:T(8,128)(2,1)S(1)}, u32[]{:S(2)}, u32[]{:S(2)}) collective-permute-start(bf16[144,256]{1,0:T(8,128)(2,1)S(1)} %get-tuple-element.54), channel_id=1, source_target_pairs={{0,12},{4,8},{8,4},{12,0},{1,13},{5,9},{9,5},{13,1},{2,14},{6,10},... | collective-permute-start | bytes 221192 | tf_op jit(solution)/shard_map/ppermute | solution.py:521
  20.6 5.5 %collective-permute-start.3 = (bf16[144,256]{1,0:T(8,128)(2,1)S(1)}, bf16[144,256]{1,0:T(8,128)(2,1)S(1)}, u32[]{:S(2)}, u32[]{:S(2)}) collective-permute-start(bf16[144,256]{1,0:T(8,128)(2,1)S(1)} %get-tuple-element.51), channel_id=1, source_target_pairs={{0,4},{4,0},{8,12},{12,8},{1,5},{5,1},{9,13},{13,9},{2,6},{6,2},{1... | collective-permute-start | bytes 221192 | tf_op jit(solution)/shard_map/ppermute | solution.py:521
  26.2 1.8 %collective-permute-start.7 = (bf16[12,128,128]{2,1,0:T(8,128)(2,1)S(1)}, bf16[12,128,128]{2,1,0:T(8,128)(2,1)S(1)}, u32[]{:S(2)}, u32[]{:S(2)}) collective-permute-start(bf16[12,128,128]{2,1,0:T(8,128)(2,1)S(1)} %stack.1.refs_4_), channel_id=1, source_target_pairs={{0,1},{1,0},{2,3},{3,2},{4,5},{5,4},{6,7},{7,6},{8,9},{9,8},{10,11... | collective-permute-start | bytes 1179656 | tf_op jit(solution)/shard_map/ppermute | solution.py:517
  28.8 1.4 %collective-permute-start.8 = (bf16[4,128,128]{2,1,0:T(8,128)(2,1)S(1)}, bf16[4,128,128]{2,1,0:T(8,128)(2,1)S(1)}, u32[]{:S(2)}, u32[]{:S(2)}) collective-permute-start(bf16[4,128,128]{2,1,0:T(8,128)(2,1)S(1)} %get-tuple-element.69), channel_id=1, source_target_pairs={{0,1},{1,0},{2,3},{3,2},{4,5},{5,4},{6,7},{7,6},{8,9},{9,8},{10,11... | collective-permute-start | bytes 393224 | tf_op jit(solution)/shard_map/ppermute | solution.py:517
  30.2 5.6 %collective-permute-start.9 = (bf16[4,128,128]{2,1,0:T(8,128)(2,1)S(1)}, bf16[4,128,128]{2,1,0:T(8,128)(2,1)S(1)}, u32[]{:S(2)}, u32[]{:S(2)}) collective-permute-start(bf16[4,128,128]{2,1,0:T(8,128)(2,1)S(1)} %add_up.1.refs_0_), channel_id=1, source_target_pairs={{0,2},{2,0},{1,3},{3,1},{4,6},{6,4},{5,7},{7,5},{8,10},{10,8},{9,1... | collective-permute-start | bytes 393224 | tf_op jit(solution)/shard_map/ppermute | solution.py:517
  36.5 1.6 %collective-permute-start.10 = (bf16[128,1152]{1,0:T(8,128)(2,1)S(1)}, bf16[128,1152]{1,0:T(8,128)(2,1)S(1)}, u32[]{:S(2)}, u32[]{:S(2)}) collective-permute-start(bf16[128,1152]{1,0:T(8,128)(2,1)S(1)} %get-tuple-element.73), channel_id=1, source_target_pairs={{0,1},{1,0},{2,3},{3,2},{4,5},{5,4},{6,7},{7,6},{8,9},{9,8},{10,11... | collective-permute-start | bytes 884744 | tf_op jit(solution)/shard_map/ppermute | solution.py:517
  38.7 6.4 %collective-permute-start.11 = (bf16[128,640]{1,0:T(8,128)(2,1)S(1)}, bf16[128,640]{1,0:T(8,128)(2,1)S(1)}, u32[]{:S(2)}, u32[]{:S(2)}) collective-permute-start(bf16[128,640]{1,0:T(8,128)(2,1)S(1)} %get-tuple-element.77), channel_id=1, source_target_pairs={{0,4},{4,0},{8,12},{12,8},{1,5},{5,1},{9,13},{13,9},{2,6},{6,2},{1... | collective-permute-start | bytes 491528 | tf_op jit(solution)/shard_map/ppermute | solution.py:521
  38.8 10.7 %collective-permute-start.12 = (bf16[128,512]{1,0:T(8,128)(2,1)S(1)}, bf16[128,512]{1,0:T(8,128)(2,1)S(1)}, u32[]{:S(2)}, u32[]{:S(2)}) collective-permute-start(bf16[128,512]{1,0:T(8,128)(2,1)S(1)} %get-tuple-element.78), channel_id=1, source_target_pairs={{0,12},{4,8},{8,4},{12,0},{1,13},{5,9},{9,5},{13,1},{2,14},{6,10},... | collective-permute-start | bytes 393224 | tf_op jit(solution)/shard_map/ppermute | solution.py:521
  41.5 13.8 %collective-permute-start.14 = (bf16[128,512]{1,0:T(8,128)(2,1)S(1)}, bf16[128,512]{1,0:T(8,128)(2,1)S(1)}, u32[]{:S(2)}, u32[]{:S(2)}) collective-permute-start(bf16[128,512]{1,0:T(8,128)(2,1)S(1)} %get-tuple-element.81), channel_id=1, source_target_pairs={{0,8},{4,12},{8,0},{12,4},{1,9},{5,13},{9,1},{13,5},{2,10},{6,14},... | collective-permute-start | bytes 393224 | tf_op jit(solution)/shard_map/ppermute | solution.py:521
  45.1 10.3 %collective-permute-start.13 = (bf16[128,128]{1,0:T(8,128)(2,1)S(1)}, bf16[128,128]{1,0:T(8,128)(2,1)S(1)}, u32[]{:S(2)}, u32[]{:S(2)}) collective-permute-start(bf16[128,128]{1,0:T(8,128)(2,1)S(1)} %pair_sum.2.mine_ref), channel_id=1, source_target_pairs={{0,8},{4,12},{8,0},{12,4},{1,9},{5,13},{9,1},{13,5},{2,10},{6,14},... | collective-permute-start | bytes 98312 | tf_op jit(solution)/shard_map/ppermute | solution.py:521
  55.7 1.7 %collective-permute-start.15 = (bf16[8,128,128]{2,1,0:T(8,128)(2,1)S(1)}, bf16[8,128,128]{2,1,0:T(8,128)(2,1)S(1)}, u32[]{:S(2)}, u32[]{:S(2)}) collective-permute-start(bf16[8,128,128]{2,1,0:T(8,128)(2,1)S(1)} %late_rows.3.mine_ref), channel_id=1, source_target_pairs={{0,1},{1,0},{2,3},{3,2},{4,5},{5,4},{6,7},{7,6},{8,9},{9,8},{10,11... | collective-permute-start | bytes 786440 | tf_op jit(solution)/shard_map/ppermute | solution.py:517
  55.8 1.6 %collective-permute-start.16 = (f32[128,128]{1,0:T(8,128)S(1)}, f32[128,128]{1,0:T(8,128)S(1)}, u32[]{:S(2)}, u32[]{:S(2)}) collective-permute-start(f32[128,128]{1,0:T(8,128)S(1)} %pair_sum.3.share_ref), channel_id=1, source_target_pairs={{0,1},{1,0},{2,3},{3,2},{4,5},{5,4},{6,7},{7,6},{8,9},{9,8},{10,11... | collective-permute-start | bytes 196616 | tf_op jit(solution)/shard_map/ppermute | solution.py:517
  (2 other events, 4.3 us)

commit v3 on v2

--- a/solution.py
+++ b/solution.py
@@ -61,16 +61,31 @@
     return jnp.concatenate([x3[b] for b in range(x3.shape[0])], axis=1)
 
 
-def prepare_kernel(peers, count_ref, row_ref, col_ref, x3, cot, place_ref, half_ref, cot_ref, *ask_refs):
-    blocks_dev = x3.shape[0]
+def half_kernel(x3, half_ref, sem):
     share = half_ref.shape[0]
-    mine = pl.ds(lax.axis_index("rep") * share, share)
-    half_ref[...] = x3[mine]
-    cot_ref[...] = cot[mine]
+    copy = pltpu.make_async_copy(x3.at[pl.ds(lax.axis_index("rep") * share, share)], half_ref, sem)
+    copy.start()
+    copy.wait()
+
+
+def half_of(values, reps):
+    blocks_dev, columns, width = values.shape
+    anywhere = pl.BlockSpec(memory_space=pl.ANY)
+    return call(
+        half_kernel,
+        "half",
+        shape((blocks_dev // reps, columns, width), BF16),
+        [anywhere],
+        [pltpu.SemaphoreType.DMA],
+        limit=VMEM_ALL,
+        out_specs=anywhere,
+    )(values)
+
+
+def places(peers, blocks_dev, count, row, col, ask_refs):
     me = lax.axis_index("graph")
-    col = col_ref[...]
     lane = lax.broadcasted_iota(jnp.int32, col.shape, 1)
-    live = lane < count_ref[0]
+    live = lane < count
     place = jnp.full(col.shape, peers * CAP * blocks_dev, jnp.int32)
     for k in range(peers):
         local = col - jnp.bitwise_xor(me, k) * blocks_dev
@@ -79,22 +94,8 @@
         high = jnp.max(jnp.where(inside, local, 0), axis=1, keepdims=True)
         ask_refs[k][...] = jnp.where(lane == 0, low, high)
         slot = k * CAP + (local != low).astype(jnp.int32)
-        place = jnp.where(inside, slot * blocks_dev + row_ref[...], place)
-    place_ref[...] = place
-
-
-def prepare(features, cotangent, tile_row, tile_col, tile_count, peers, reps):
-    per = tile_col.shape[0]
-    blocks_dev, columns, width = features.shape
-    share = shape((blocks_dev // reps, columns, width), BF16)
-    outs = call(
-        functools.partial(prepare_kernel, peers),
-        "prepare",
-        [shape((1, per), jnp.int32), share, share] + [shape((1, per), jnp.int32)] * peers,
-        [smem()] + [vmem()] * 4,
-        limit=VMEM_ALL,
-    )(tile_count, tile_row.reshape(1, per), tile_col.reshape(1, per), features, cotangent)
-    return outs[0], outs[1], outs[2], list(outs[3:])
+        place = jnp.where(inside, slot * blocks_dev + row, place)
+    return place
 
 
 def pick(ids_ref, lane):
@@ -103,7 +104,10 @@
     return jnp.max(jnp.where(at == lane, ids, 0.0)).astype(jnp.int32)
 
 
-def operator_kernel(blocks_dev, slots_here, groups, place_in, tiles_ref, m_ref, tiles, acc, place_ref, sems, sem):
+def operator_kernel(peers, blocks_dev, slots_here, groups, *refs):
+    count_ref, row_ref, col_ref, tiles_ref, m_ref = refs[:5]
+    ask_refs, refs = refs[5 : 5 + peers], refs[5 + peers :]
+    tiles, acc, place_lanes, place_ref, sems, sem = refs
     step = pl.program_id(0)
     per, width = tiles.shape[0], tiles.shape[1]
     chunks = per // CHUNK
@@ -115,10 +119,11 @@
 
     @pl.when(step == 0)
     def _():
-        placed = pltpu.make_async_copy(place_in, place_ref, sem)
-        placed.start()
         for c in range(chunks):
             chunk_copy(c).start()
+        place_lanes[...] = places(peers, blocks_dev, count_ref[...], row_ref[...], col_ref[...], ask_refs)
+        placed = pltpu.make_async_copy(place_lanes, place_ref, sem)
+        placed.start()
         placed.wait()
 
     acc[...] = jnp.zeros_like(acc)
@@ -147,19 +152,20 @@
             m_ref[r * width : (r + 1) * width, s * width : (s + 1) * width] = total.astype(BF16)
 
 
-def list_operator(tiles, place, peers, blocks_dev):
+def list_operator(tiles, tile_row, tile_col, tile_count, peers, blocks_dev):
     per, width = tiles.shape[0], tiles.shape[1]
     slots = peers * CAP
     slots_here = min(slots, GROUP)
     groups = slots // slots_here
-    return call(
-        functools.partial(operator_kernel, blocks_dev, slots_here, groups),
+    outs = call(
+        functools.partial(operator_kernel, peers, blocks_dev, slots_here, groups),
         "operator",
-        shape((blocks_dev * width, slots * width), BF16),
-        [pl.BlockSpec(memory_space=pl.ANY), hbm()],
+        [shape((blocks_dev * width, slots * width), BF16)] + [shape((1, per), jnp.int32)] * peers,
+        [vmem(), vmem(), vmem(), hbm()],
         [
             pltpu.VMEM((per, width, width), BF16),
             pltpu.VMEM((SIDES, slots_here * blocks_dev + 1, width, width), F32),
+            pltpu.VMEM((1, per), jnp.int32),
             pltpu.SMEM((1, per), jnp.int32),
             pltpu.SemaphoreType.DMA((per // CHUNK,)),
             pltpu.SemaphoreType.DMA,
@@ -167,8 +173,9 @@
         moved=2 ** 24,
         limit=VMEM_MOST,
         grid=(groups,),
-        out_specs=pl.BlockSpec((blocks_dev * width, slots_here * width), lambda i: (0, i)),
-    )(place, tiles)
+        out_specs=[pl.BlockSpec((blocks_dev * width, slots_here * width), lambda i: (0, i))] + [vmem()] * peers,
+    )(tile_count.reshape(1, 1), tile_row.reshape(1, per), tile_col.reshape(1, per), tiles)
+    return outs[0], list(outs[1:])
 
 
 def mirrored(near, m_ref, mir, slots, width):
@@ -283,14 +290,30 @@
 
 
 def stack_kernel(*refs):
-    share = refs[0].shape[0]
-    for i, ref in enumerate(refs[:-1]):
-        refs[-1][i * share : (i + 1) * share] = ref[...]
+    at = 0
+    for ref in refs[:-1]:
+        share = ref.shape[0]
+        refs[-1][at : at + share] = ref[...]
+        at += share
+
+
+def halves_kernel(in_ref, low_ref, high_ref):
+    share = low_ref.shape[0]
+    low_ref[...] = in_ref[:share]
+    high_ref[...] = in_ref[share:]
+
+
+def halves(parts):
+    if len(parts) > 1:
+        return parts
+    share, columns, width = parts[0].shape
+    part = shape((share // 2, columns, width), BF16)
+    return list(call(halves_kernel, "halves", [part, part], [vmem()])(*parts))
 
 
 def stack(pieces):
-    share, columns, width = pieces[0].shape
-    out = shape((len(pieces) * share, columns, width), BF16)
+    _, columns, width = pieces[0].shape
+    out = shape((sum(piece.shape[0] for piece in pieces), columns, width), BF16)
     return call(stack_kernel, "stack", out, [vmem()] * len(pieces))(*pieces)
 
 
@@ -532,32 +555,36 @@
     reps = lax.axis_size("rep")
     far_first = sorted(range(1, peers), key=lambda k: (-(k & (peers // 2)), k))
 
-    place, half, own_cot, asks = prepare(features, cotangent, tile_row, tile_col, tile_count, peers, reps)
-    operator = list_operator(tiles, place, peers, blocks_dev)
+    half = half_of(features, reps)
+    operator, asks = list_operator(tiles, tile_row, tile_col, tile_count, peers, blocks_dev)
     sends, own_mirror = first_sends(features, operator, asks[1:], peers)
-    pieces, held = {0: half}, [0]
+    pieces, held = {0: [half]}, [0]
     bit = peers // 2
     while bit:
         for k in held:
-            piece = after(pieces[k], sends[1]) if k else half
-            pieces[k ^ bit] = across(piece, peers, bit)
+            parts = pieces[k]
+            if k:
+                parts = after(halves(after(parts, sends[1])), pieces.get(1, half))
+            pieces[k ^ bit] = [across(part, peers, bit) for part in parts]
         held = held + [k ^ bit for k in held]
         bit //= 2
     came = [None] * peers
     for k in far_first:
         came[k] = across(sends[k], peers, k)
-    cots = [own_cot]
+    arrived = [pieces[k] for k in range(1, peers)]
+    ordered, arrived = lax.optimization_barrier(([came[k] for k in far_first], arrived))
+    came = [None] + [ordered[far_first.index(k)] for k in range(1, peers)]
+    stacked = stack([part for parts in arrived for part in parts])
+    swapped = ahead(stacked, "rep", reps, 1)
+    cots = [half_of(cotangent, reps)]
     if feats > 1:
-        waited = after(own_cot, pieces[peers // 2])
+        waited = after(cots[0], stacked)
         cots += [ahead(waited, "feat", feats, feats - q) for q in range(1, feats)]
-    arrived = [pieces[k] for k in range(1, peers)]
-    arrived, came, cots = lax.optimization_barrier((arrived, came, cots))
-    stacked = stack(arrived)
-    swapped = ahead(stacked, "rep", reps, 1)
     acc, ids = first_rows(features, operator, asks[0], came, own_mirror, peers)
     give, keep = far_rows(acc, asks, stacked, swapped, operator, peers, reps)
 
-    mine = add_up(keep, ahead(give, "rep", reps, 1))
+    given, cots = lax.optimization_barrier((ahead(give, "rep", reps, 1), cots))
+    mine = add_up(keep, given)
     sums = [mine] + [ahead(mine, "feat", feats, feats - q) for q in range(1, feats)]
     act, give, spread, keep = dense(sums, cots, weight, feats, reps)
     shared = ahead(give, "rep", reps, 1)
@@ -571,10 +598,8 @@
     while bit < peers:
         total = pair_sum(total, across(total, peers, bit), 0, F32 if 2 * bit == peers else BF16)
         bit *= 2
-    ends = [peers // 2]
-    acc = late_rows([asks[0], values, own_mirror], ids, came, [k for k in range(1, peers) if k not in ends], operator, True, False)
-    acc, total = lax.optimization_barrier((acc, total))
-    part = late_rows([acc], ids, came, ends, operator, False, True)
+    came, total = lax.optimization_barrier((came, total))
+    part = late_rows([asks[0], values, own_mirror], ids, came, far_first, operator, True, True)
     input_grad, weight_grad, activated = finish(
         part, ahead(part, "rep", reps, 1), total, ahead(total, "rep", reps, 1), act, shared
     )

time: 58.6 us -> 67.7 us (1.16)
  Pallas kernels: 9.89 us -> 18.1 us
  waiting for transfers between devices: 23.6 us -> 26.7 us
  starting transfers between devices: 22.7 us -> 19.9 us
    pallas_call x2 -> x4, Pallas kernels: 4.93 us -> 13.3 us  [the longest x2 10.2 us: half_of(): call(half_kernel, 'half', shape((blocks_dev // reps, columns, width), BF1...]
    ppermute x10 -> x11, waiting for transfers between devices: 13.5 us -> 17.3 us  [across(): return lax.ppermute(value, 'graph', [(i, i ^ k) for i in range(peers)])]
    ppermute x10 -> x11, starting transfers between devices: 19.6 us -> 15.8 us  [across(): return lax.ppermute(value, 'graph', [(i, i ^ k) for i in range(peers)])]
    ppermute x7, starting transfers between devices: 3.16 us -> 4.09 us  [ahead(): return lax.ppermute(value, axis, [(i, (i + k) % size) for i in range(size)])]
  transfers between devices with their start and end apart: 17 -> 18, of which waited for: 10 -> 10; matrix products, arithmetic and copies ran while one was open for 0% -> 0% of each run, Pallas kernels for 8% -> 15%
where the time goes in v3:
time: 67.7 us; the launch traced here: 67.6 us
  waiting for transfers between devices  26.7 us (39%)
  starting transfers between devices  19.9 us (29%)
  Pallas kernels  18.1 us (27%)
  between operations  1.48 us (2%)
  local copies, waits for them, and re-layouts  1.32 us (2%)
    ppermute x11, waiting for transfers between devices, across(): return lax.ppermute(value, 'graph', [(i, i ^ k) for i in range(peers)])  17.3 us
    ppermute x11, starting transfers between devices, across(): return lax.ppermute(value, 'graph', [(i, i ^ k) for i in range(peers)])  15.8 us
    pallas_call x2, Pallas kernels, half_of(): call(half_kernel, 'half', shape((blocks_dev // reps, columns, width), BF1...  10.2 us
    ppermute x7, waiting for transfers between devices, ahead(): return lax.ppermute(value, axis, [(i, (i + k) % size) for i in range(size)])  9.43 us
    ppermute x7, starting transfers between devices, ahead(): return lax.ppermute(value, axis, [(i, (i + k) % size) for i in range(size)])  4.09 us
    pallas_call x1, Pallas kernels, list_operator(): call(functools.partial(operator_kernel, peers, blocks_dev, slots_here, gr...  3.14 us
  transfers between devices with their start and end apart: 18, of which 10 were waited for; matrix products, arithmetic and copies ran while one was open for 0% of the time, Pallas kernels for 15%

profile of v3, /device:TPU:0, one launch (start us, length us, event | category | flops | bytes accessed | tf_op | source)
XLA Modules:
  0.0 67.6 jit_solution(17053201424998856136)
XLA Ops:
  0.6 5.1 %half.2 = bf16[4,128,128]{2,1,0:T(8,128)(2,1)} custom-call(bf16[8,128,128]{2,1,0:T(8,128)(2,1)} %refs_4_.2), custom_call_target="tpu_custom_call" | custom-call | bytes 262144 | tf_op jit(solution)/shard_map/half/pallas_call | solution.py:74
  5.7 4.1 %collective-permute-start.4 = (bf16[4,128,128]{2,1,0:T(8,128)(2,1)}, bf16[4,128,128]{2,1,0:T(8,128)(2,1)S(1)}, u32[]{:S(2)}, u32[]{:S(2)}) collective-permute-start(bf16[4,128,128]{2,1,0:T(8,128)(2,1)} %half.2), channel_id=1, source_target_pairs={{0,8},{4,12},{8,0},{12,4},{1,9},{5,13},{9,1},{13,5},{2,10},{6,14},... | collective-permute-start | bytes 393224 | tf_op jit(solution)/shard_map/ppermute | solution.py:544
  9.8 1.6 %collective-permute-start.3 = (bf16[4,128,128]{2,1,0:T(8,128)(2,1)}, bf16[4,128,128]{2,1,0:T(8,128)(2,1)S(1)}, u32[]{:S(2)}, u32[]{:S(2)}) collective-permute-start(bf16[4,128,128]{2,1,0:T(8,128)(2,1)} %half.2), channel_id=1, source_target_pairs={{0,4},{4,0},{8,12},{12,8},{1,5},{5,1},{9,13},{13,9},{2,6},{6,2},{1... | collective-permute-start | bytes 393224 | tf_op jit(solution)/shard_map/ppermute | solution.py:544
  13.4 3.1 %operator.1 = (bf16[1024,1024]{1,0:T(8,128)(2,1)S(1)}, s32[1,128]{1,0:T(1,128)S(1)}, s32[1,128]{1,0:T(1,128)S(1)}, s32[1,128]{1,0:T(1,128)S(1)}, s32[1,128]{1,0:T(1,128)S(1)}) custom-call(s32[1,1]{1,0:T(1,128)} %bitcast.3.refs_0_, s32[1,128]{1,0:T(1,128)S(1)} %bitcast.4, s32[1,128]{1,0:T(1,128)S(1)} %bitcast.5, bf16[128,128,128]{2,1,0:T(8,128)(2,1)} %refs_3_.2), custom_call_target="tpu_custom_call" | custom-call | bytes 16777216 | tf_op jit(solution)/shard_map/operator/pallas_call | solution.py:160
  17.4 2.5 %collective-permute-start.1 = (bf16[144,256]{1,0:T(8,128)(2,1)S(1)}, bf16[144,256]{1,0:T(8,128)(2,1)S(1)}, u32[]{:S(2)}, u32[]{:S(2)}) collective-permute-start(bf16[144,256]{1,0:T(8,128)(2,1)S(1)} %get-tuple-element.57), channel_id=1, source_target_pairs={{0,12},{4,8},{8,4},{12,0},{1,13},{5,9},{9,5},{13,1},{2,14},{6,10},... | collective-permute-start | bytes 221192 | tf_op jit(solution)/shard_map/ppermute | solution.py:544
  20.6 1.4 %collective-permute-start.5 = (bf16[2,128,128]{2,1,0:T(8,128)(2,1)S(1)}, bf16[2,128,128]{2,1,0:T(8,128)(2,1)S(1)}, u32[]{:S(2)}, u32[]{:S(2)}) collective-permute-start(bf16[2,128,128]{2,1,0:T(8,128)(2,1)S(1)} %get-tuple-element.62), channel_id=1, source_target_pairs={{0,4},{4,0},{8,12},{12,8},{1,5},{5,1},{9,13},{13,9},{2,6},{6,2},{1... | collective-permute-start | bytes 196616 | tf_op jit(solution)/shard_map/ppermute | solution.py:544
  22.7 2.1 %collective-permute-done.refs_2_ = bf16[144,256]{1,0:T(8,128)(2,1)S(1)} collective-permute-done((bf16[144,256]{1,0:T(8,128)(2,1)S(1)}, bf16[144,256]{1,0:T(8,128)(2,1)S(1)}, u32[]{:S(2)}, u32[]{:S(2)}) %collective-permute-start) | collective-permute-done | bytes 73760 | tf_op jit(solution)/shard_map/ppermute | solution.py:544
  24.8 1.4 %collective-permute-done.2.refs_1_ = bf16[144,256]{1,0:T(8,128)(2,1)S(1)} collective-permute-done((bf16[144,256]{1,0:T(8,128)(2,1)S(1)}, bf16[144,256]{1,0:T(8,128)(2,1)S(1)}, u32[]{:S(2)}, u32[]{:S(2)}) %collective-permute-start.2) | collective-permute-done | bytes 73760 | tf_op jit(solution)/shard_map/ppermute | solution.py:544
  26.2 1.2 %collective-permute-done.5.refs_2_ = bf16[2,128,128]{2,1,0:T(8,128)(2,1)S(1)} collective-permute-done((bf16[2,128,128]{2,1,0:T(8,128)(2,1)S(1)}, bf16[2,128,128]{2,1,0:T(8,128)(2,1)S(1)}, u32[]{:S(2)}, u32[]{:S(2)}) %collective-permute-start.5) | collective-permute-done | bytes 65568 | tf_op jit(solution)/shard_map/ppermute | solution.py:544
  27.4 0.7 %collective-permute-done.6.refs_3_ = bf16[2,128,128]{2,1,0:T(8,128)(2,1)S(1)} collective-permute-done((bf16[2,128,128]{2,1,0:T(8,128)(2,1)S(1)}, bf16[2,128,128]{2,1,0:T(8,128)(2,1)S(1)}, u32[]{:S(2)}, u32[]{:S(2)}) %collective-permute-start.6) | collective-permute-done | bytes 65568 | tf_op jit(solution)/shard_map/ppermute | solution.py:544
  28.2 5.1 %half.3.refs_2_ = bf16[4,128,128]{2,1,0:T(8,128)(2,1)} custom-call(bf16[8,128,128]{2,1,0:T(8,128)(2,1)} %x3.3), custom_call_target="tpu_custom_call" | custom-call | bytes 262144 | tf_op jit(solution)/shard_map/half/pallas_call | solution.py:74
  33.3 1.6 %collective-permute-start.9 = (bf16[4,128,128]{2,1,0:T(8,128)(2,1)}, bf16[4,128,128]{2,1,0:T(8,128)(2,1)S(1)}, u32[]{:S(2)}, u32[]{:S(2)}) collective-permute-start(bf16[4,128,128]{2,1,0:T(8,128)(2,1)} %half.3.refs_2_), channel_id=1, source_target_pairs={{0,2},{2,0},{1,3},{3,1},{4,6},{6,4},{5,7},{7,5},{8,10},{10,8},{9,1... | collective-permute-start | bytes 393224 | tf_op jit(solution)/shard_map/ppermute | solution.py:540
  35.3 0.8 %far_rows.1 = (bf16[4,128,128]{2,1,0:T(8,128)(2,1)S(1)}, f32[4,128,128]{2,1,0:T(8,128)S(1)}) custom-call(s32[1,128]{1,0:T(1,128)S(1)} %get-tuple-element.52.refs_0_, s32[1,128]{1,0:T(1,128)S(1)} %get-tuple-element.53.refs_1_, s32[1,128]{1,0:T(1,128)S(1)} %get-tuple-element.54.refs_2_, f32[8,128,128]{2,1,0:T(8,128)S(1)} %get-tuple-element.71.refs_3_, ...), custom_call_target="tpu_custom_call" | custom-call | flops 268435456 | bytes 2097152 | tf_op jit(solution)/shard_map/far_rows/pallas_call | solution.py:342
  36.3 3.1 %collective-permute-done.9.refs_3_ = bf16[4,128,128]{2,1,0:T(8,128)(2,1)S(1)} collective-permute-done((bf16[4,128,128]{2,1,0:T(8,128)(2,1)}, bf16[4,128,128]{2,1,0:T(8,128)(2,1)S(1)}, u32[]{:S(2)}, u32[]{:S(2)}) %collective-permute-start.9) | collective-permute-done | bytes 131104 | tf_op jit(solution)/shard_map/ppermute | solution.py:540
  39.5 1.6 %collective-permute-start.10 = (bf16[4,128,128]{2,1,0:T(8,128)(2,1)S(1)}, bf16[4,128,128]{2,1,0:T(8,128)(2,1)S(1)}, u32[]{:S(2)}, u32[]{:S(2)}) collective-permute-start(bf16[4,128,128]{2,1,0:T(8,128)(2,1)S(1)} %add_up.1.refs_0_), channel_id=1, source_target_pairs={{0,2},{2,0},{1,3},{3,1},{4,6},{6,4},{5,7},{7,5},{8,10},{10,8},{9,1... | collective-permute-start | bytes 393224 | tf_op jit(solution)/shard_map/ppermute | solution.py:540
  41.0 3.6 %collective-permute-done.10.refs_1_ = bf16[4,128,128]{2,1,0:T(8,128)(2,1)S(1)} collective-permute-done((bf16[4,128,128]{2,1,0:T(8,128)(2,1)S(1)}, bf16[4,128,128]{2,1,0:T(8,128)(2,1)S(1)}, u32[]{:S(2)}, u32[]{:S(2)}) %collective-permute-start.10) | collective-permute-done | bytes 131104 | tf_op jit(solution)/shard_map/ppermute | solution.py:540
  45.5 1.6 %collective-permute-done.11.refs_4_.came_ref = bf16[128,1152]{1,0:T(8,128)(2,1)S(1)} collective-permute-done((bf16[128,1152]{1,0:T(8,128)(2,1)S(1)}, bf16[128,1152]{1,0:T(8,128)(2,1)S(1)}, u32[]{:S(2)}, u32[]{:S(2)}) %collective-permute-start.11) | collective-permute-done | bytes 294944 | tf_op jit(solution)/shard_map/ppermute | solution.py:540
  47.6 1.2 %collective-permute-start.13 = (bf16[128,512]{1,0:T(8,128)(2,1)S(1)}, bf16[128,512]{1,0:T(8,128)(2,1)S(1)}, u32[]{:S(2)}, u32[]{:S(2)}) collective-permute-start(bf16[128,512]{1,0:T(8,128)(2,1)S(1)} %get-tuple-element.88), channel_id=1, source_target_pairs={{0,8},{4,12},{8,0},{12,4},{1,9},{5,13},{9,1},{13,5},{2,10},{6,14},... | collective-permute-start | bytes 393224 | tf_op jit(solution)/shard_map/ppermute | solution.py:544
  48.8 3.2 %collective-permute-start.14 = (bf16[128,512]{1,0:T(8,128)(2,1)S(1)}, bf16[128,512]{1,0:T(8,128)(2,1)S(1)}, u32[]{:S(2)}, u32[]{:S(2)}) collective-permute-start(bf16[128,512]{1,0:T(8,128)(2,1)S(1)} %get-tuple-element.89), channel_id=1, source_target_pairs={{0,12},{4,8},{8,4},{12,0},{1,13},{5,9},{9,5},{13,1},{2,14},{6,10},... | collective-permute-start | bytes 393224 | tf_op jit(solution)/shard_map/ppermute | solution.py:544
  52.0 4.3 %collective-permute-done.12.came_ref.refs_8_ = bf16[128,640]{1,0:T(8,128)(2,1)S(1)} collective-permute-done((bf16[128,640]{1,0:T(8,128)(2,1)S(1)}, bf16[128,640]{1,0:T(8,128)(2,1)S(1)}, u32[]{:S(2)}, u32[]{:S(2)}) %collective-permute-start.12) | collective-permute-done | bytes 163872 | tf_op jit(solution)/shard_map/ppermute | solution.py:544
  56.4 7.6 %collective-permute-done.15.came_ref = bf16[128,128]{1,0:T(8,128)(2,1)S(1)} collective-permute-done((bf16[128,128]{1,0:T(8,128)(2,1)S(1)}, bf16[128,128]{1,0:T(8,128)(2,1)S(1)}, u32[]{:S(2)}, u32[]{:S(2)}) %collective-permute-start.15) | collective-permute-done | bytes 32800 | tf_op jit(solution)/shard_map/ppermute | solution.py:544
  64.0 0.9 %late_rows.1.mine_ref = bf16[8,128,128]{2,1,0:T(8,128)(2,1)S(1)} custom-call(s32[1,128]{1,0:T(1,128)S(1)} %get-tuple-element.51.refs_0_, bf16[8,128,128]{2,1,0:T(8,128)(2,1)S(1)} %get-tuple-element.85.refs_1_, f32[128,256]{1,0:T(8,128)S(1)} %get-tuple-element.86.refs_2_, s32[1,128]{1,0:T(1,128)S(1)} %get-tuple-element.69.refs_1_.refs_3_, ...), custom_call_target="tpu_custom_call" | custom-call | flops 134217728 | bytes 1048576 | tf_op jit(solution)/shard_map/late_rows/pallas_call | solution.py:386
  65.5 1.1 %collective-permute-done.17.other_share_ref = f32[128,128]{1,0:T(8,128)S(1)} collective-permute-done((f32[128,128]{1,0:T(8,128)S(1)}, f32[128,128]{1,0:T(8,128)S(1)}, u32[]{:S(2)}, u32[]{:S(2)}) %collective-permute-start.17) | collective-permute-done | bytes 65568 | tf_op jit(solution)/shard_map/ppermute | solution.py:540
  66.6 1.0 %finish.1 = (bf16[8,128,128]{2,1,0:T(8,128)(2,1)}, f32[256,128]{1,0:T(8,128)}, bf16[8,128,128]{2,1,0:T(8,128)(2,1)}) custom-call(bf16[8,128,128]{2,1,0:T(8,128)(2,1)S(1)} %late_rows.1.mine_ref, bf16[8,128,128]{2,1,0:T(8,128)(2,1)S(1)} %collective-permute-done.16.other_ref, f32[128,128]{1,0:T(8,128)S(1)} %pair_sum.3.share_ref, ...), custom_call_target="tpu_custom_call" | custom-call | bytes 262144 | tf_op jit(solution)/shard_map/finish/pallas_call | solution.py:531
  (37 shorter events, 6.4 us)
Async XLA Ops:
  0.6 15.9 %copy-start = (bf16[8,128,128]{2,1,0:T(8,128)(2,1)S(1)}, bf16[8,128,128]{2,1,0:T(8,128)(2,1)}, u32[]{:S(2)}) copy-start(bf16[8,128,128]{2,1,0:T(8,128)(2,1)} %refs_4_.2) | copy-start | bytes 786436
  5.7 14.9 %collective-permute-start.4 = (bf16[4,128,128]{2,1,0:T(8,128)(2,1)}, bf16[4,128,128]{2,1,0:T(8,128)(2,1)S(1)}, u32[]{:S(2)}, u32[]{:S(2)}) collective-permute-start(bf16[4,128,128]{2,1,0:T(8,128)(2,1)} %half.2), channel_id=1, source_target_pairs={{0,8},{4,12},{8,0},{12,4},{1,9},{5,13},{9,1},{13,5},{2,10},{6,14},... | collective-permute-start | bytes 393224 | tf_op jit(solution)/shard_map/ppermute | solution.py:544
  9.8 10.8 %collective-permute-start.3 = (bf16[4,128,128]{2,1,0:T(8,128)(2,1)}, bf16[4,128,128]{2,1,0:T(8,128)(2,1)S(1)}, u32[]{:S(2)}, u32[]{:S(2)}) collective-permute-start(bf16[4,128,128]{2,1,0:T(8,128)(2,1)} %half.2), channel_id=1, source_target_pairs={{0,4},{4,0},{8,12},{12,8},{1,5},{5,1},{9,13},{13,9},{2,6},{6,2},{1... | collective-permute-start | bytes 393224 | tf_op jit(solution)/shard_map/ppermute | solution.py:544
  12.1 0.7 copy-start.2
  12.7 0.7 copy-start.3
  17.0 27.7 %copy-start.4 = (bf16[256,256]{1,0:T(8,128)(2,1)S(1)}, bf16[256,256]{1,0:T(8,128)(2,1)}, u32[]{:S(2)}) copy-start(bf16[256,256]{1,0:T(8,128)(2,1)} %refs_4_.3) | copy-start | bytes 393220
  17.0 7.8 %collective-permute-start = (bf16[144,256]{1,0:T(8,128)(2,1)S(1)}, bf16[144,256]{1,0:T(8,128)(2,1)S(1)}, u32[]{:S(2)}, u32[]{:S(2)}) collective-permute-start(bf16[144,256]{1,0:T(8,128)(2,1)S(1)} %get-tuple-element.56), channel_id=1, source_target_pairs={{0,8},{4,12},{8,0},{12,4},{1,9},{5,13},{9,1},{13,5},{2,10},{6,14},... | collective-permute-start | bytes 221192 | tf_op jit(solution)/shard_map/ppermute | solution.py:544
  17.4 7.4 %collective-permute-start.1 = (bf16[144,256]{1,0:T(8,128)(2,1)S(1)}, bf16[144,256]{1,0:T(8,128)(2,1)S(1)}, u32[]{:S(2)}, u32[]{:S(2)}) collective-permute-start(bf16[144,256]{1,0:T(8,128)(2,1)S(1)} %get-tuple-element.57), channel_id=1, source_target_pairs={{0,12},{4,8},{8,4},{12,0},{1,13},{5,9},{9,5},{13,1},{2,14},{6,10},... | collective-permute-start | bytes 221192 | tf_op jit(solution)/shard_map/ppermute | solution.py:544
  19.9 6.3 %collective-permute-start.2 = (bf16[144,256]{1,0:T(8,128)(2,1)S(1)}, bf16[144,256]{1,0:T(8,128)(2,1)S(1)}, u32[]{:S(2)}, u32[]{:S(2)}) collective-permute-start(bf16[144,256]{1,0:T(8,128)(2,1)S(1)} %get-tuple-element.58), channel_id=1, source_target_pairs={{0,4},{4,0},{8,12},{12,8},{1,5},{5,1},{9,13},{13,9},{2,6},{6,2},{1... | collective-permute-start | bytes 221192 | tf_op jit(solution)/shard_map/ppermute | solution.py:544
  20.6 6.8 %collective-permute-start.5 = (bf16[2,128,128]{2,1,0:T(8,128)(2,1)S(1)}, bf16[2,128,128]{2,1,0:T(8,128)(2,1)S(1)}, u32[]{:S(2)}, u32[]{:S(2)}) collective-permute-start(bf16[2,128,128]{2,1,0:T(8,128)(2,1)S(1)} %get-tuple-element.62), channel_id=1, source_target_pairs={{0,4},{4,0},{8,12},{12,8},{1,5},{5,1},{9,13},{13,9},{2,6},{6,2},{1... | collective-permute-start | bytes 196616 | tf_op jit(solution)/shard_map/ppermute | solution.py:544
  22.0 6.0 %collective-permute-start.6 = (bf16[2,128,128]{2,1,0:T(8,128)(2,1)S(1)}, bf16[2,128,128]{2,1,0:T(8,128)(2,1)S(1)}, u32[]{:S(2)}, u32[]{:S(2)}) collective-permute-start(bf16[2,128,128]{2,1,0:T(8,128)(2,1)S(1)} %get-tuple-element.63), channel_id=1, source_target_pairs={{0,4},{4,0},{8,12},{12,8},{1,5},{5,1},{9,13},{13,9},{2,6},{6,2},{1... | collective-permute-start | bytes 196616 | tf_op jit(solution)/shard_map/ppermute | solution.py:544
  28.1 7.2 %collective-permute-start.7 = (bf16[12,128,128]{2,1,0:T(8,128)(2,1)S(1)}, bf16[12,128,128]{2,1,0:T(8,128)(2,1)S(1)}, u32[]{:S(2)}, u32[]{:S(2)}) collective-permute-start(bf16[12,128,128]{2,1,0:T(8,128)(2,1)S(1)} %stack.1.refs_4_), channel_id=1, source_target_pairs={{0,1},{1,0},{2,3},{3,2},{4,5},{5,4},{6,7},{7,6},{8,9},{9,8},{10,11... | collective-permute-start | bytes 1179656 | tf_op jit(solution)/shard_map/ppermute | solution.py:540
  33.3 11.4 %copy-start.1 = (bf16[4,128,128]{2,1,0:T(8,128)(2,1)S(1)}, bf16[4,128,128]{2,1,0:T(8,128)(2,1)}, u32[]{:S(2)}) copy-start(bf16[4,128,128]{2,1,0:T(8,128)(2,1)} %half.3.refs_2_) | copy-start | bytes 393220
  33.3 6.2 %collective-permute-start.9 = (bf16[4,128,128]{2,1,0:T(8,128)(2,1)}, bf16[4,128,128]{2,1,0:T(8,128)(2,1)S(1)}, u32[]{:S(2)}, u32[]{:S(2)}) collective-permute-start(bf16[4,128,128]{2,1,0:T(8,128)(2,1)} %half.3.refs_2_), channel_id=1, source_target_pairs={{0,2},{2,0},{1,3},{3,1},{4,6},{6,4},{5,7},{7,5},{8,10},{10,8},{9,1... | collective-permute-start | bytes 393224 | tf_op jit(solution)/shard_map/ppermute | solution.py:540
  36.1 3.4 %collective-permute-start.8 = (bf16[4,128,128]{2,1,0:T(8,128)(2,1)S(1)}, bf16[4,128,128]{2,1,0:T(8,128)(2,1)S(1)}, u32[]{:S(2)}, u32[]{:S(2)}) collective-permute-start(bf16[4,128,128]{2,1,0:T(8,128)(2,1)S(1)} %get-tuple-element.77), channel_id=1, source_target_pairs={{0,1},{1,0},{2,3},{3,2},{4,5},{5,4},{6,7},{7,6},{8,9},{9,8},{10,11... | collective-permute-start | bytes 393224 | tf_op jit(solution)/shard_map/ppermute | solution.py:540
  39.5 5.2 %collective-permute-start.10 = (bf16[4,128,128]{2,1,0:T(8,128)(2,1)S(1)}, bf16[4,128,128]{2,1,0:T(8,128)(2,1)S(1)}, u32[]{:S(2)}, u32[]{:S(2)}) collective-permute-start(bf16[4,128,128]{2,1,0:T(8,128)(2,1)S(1)} %add_up.1.refs_0_), channel_id=1, source_target_pairs={{0,2},{2,0},{1,3},{3,1},{4,6},{6,4},{5,7},{7,5},{8,10},{10,8},{9,1... | collective-permute-start | bytes 393224 | tf_op jit(solution)/shard_map/ppermute | solution.py:540
  45.4 1.6 %collective-permute-start.11 = (bf16[128,1152]{1,0:T(8,128)(2,1)S(1)}, bf16[128,1152]{1,0:T(8,128)(2,1)S(1)}, u32[]{:S(2)}, u32[]{:S(2)}) collective-permute-start(bf16[128,1152]{1,0:T(8,128)(2,1)S(1)} %get-tuple-element.83), channel_id=1, source_target_pairs={{0,1},{1,0},{2,3},{3,2},{4,5},{5,4},{6,7},{7,6},{8,9},{9,8},{10,11... | collective-permute-start | bytes 884744 | tf_op jit(solution)/shard_map/ppermute | solution.py:540
  47.5 8.8 %collective-permute-start.12 = (bf16[128,640]{1,0:T(8,128)(2,1)S(1)}, bf16[128,640]{1,0:T(8,128)(2,1)S(1)}, u32[]{:S(2)}, u32[]{:S(2)}) collective-permute-start(bf16[128,640]{1,0:T(8,128)(2,1)S(1)} %get-tuple-element.87), channel_id=1, source_target_pairs={{0,4},{4,0},{8,12},{12,8},{1,5},{5,1},{9,13},{13,9},{2,6},{6,2},{1... | collective-permute-start | bytes 491528 | tf_op jit(solution)/shard_map/ppermute | solution.py:544
  47.6 16.4 %collective-permute-start.13 = (bf16[128,512]{1,0:T(8,128)(2,1)S(1)}, bf16[128,512]{1,0:T(8,128)(2,1)S(1)}, u32[]{:S(2)}, u32[]{:S(2)}) collective-permute-start(bf16[128,512]{1,0:T(8,128)(2,1)S(1)} %get-tuple-element.88), channel_id=1, source_target_pairs={{0,8},{4,12},{8,0},{12,4},{1,9},{5,13},{9,1},{13,5},{2,10},{6,14},... | collective-permute-start | bytes 393224 | tf_op jit(solution)/shard_map/ppermute | solution.py:544
  48.8 15.2 %collective-permute-start.14 = (bf16[128,512]{1,0:T(8,128)(2,1)S(1)}, bf16[128,512]{1,0:T(8,128)(2,1)S(1)}, u32[]{:S(2)}, u32[]{:S(2)}) collective-permute-start(bf16[128,512]{1,0:T(8,128)(2,1)S(1)} %get-tuple-element.89), channel_id=1, source_target_pairs={{0,12},{4,8},{8,4},{12,0},{1,13},{5,9},{9,5},{13,1},{2,14},{6,10},... | collective-permute-start | bytes 393224 | tf_op jit(solution)/shard_map/ppermute | solution.py:544
  56.3 7.6 %collective-permute-start.15 = (bf16[128,128]{1,0:T(8,128)(2,1)S(1)}, bf16[128,128]{1,0:T(8,128)(2,1)S(1)}, u32[]{:S(2)}, u32[]{:S(2)}) collective-permute-start(bf16[128,128]{1,0:T(8,128)(2,1)S(1)} %pair_sum.2.mine_ref), channel_id=1, source_target_pairs={{0,8},{4,12},{8,0},{12,4},{1,9},{5,13},{9,1},{13,5},{2,10},{6,14},... | collective-permute-start | bytes 98312 | tf_op jit(solution)/shard_map/ppermute | solution.py:544
  64.9 1.7 %collective-permute-start.16 = (bf16[8,128,128]{2,1,0:T(8,128)(2,1)S(1)}, bf16[8,128,128]{2,1,0:T(8,128)(2,1)S(1)}, u32[]{:S(2)}, u32[]{:S(2)}) collective-permute-start(bf16[8,128,128]{2,1,0:T(8,128)(2,1)S(1)} %late_rows.1.mine_ref), channel_id=1, source_target_pairs={{0,1},{1,0},{2,3},{3,2},{4,5},{5,4},{6,7},{7,6},{8,9},{9,8},{10,11... | collective-permute-start | bytes 786440 | tf_op jit(solution)/shard_map/ppermute | solution.py:540
  65.0 1.6 %collective-permute-start.17 = (f32[128,128]{1,0:T(8,128)S(1)}, f32[128,128]{1,0:T(8,128)S(1)}, u32[]{:S(2)}, u32[]{:S(2)}) collective-permute-start(f32[128,128]{1,0:T(8,128)S(1)} %pair_sum.3.share_ref), channel_id=1, source_target_pairs={{0,1},{1,0},{2,3},{3,2},{4,5},{5,4},{6,7},{7,6},{8,9},{9,8},{10,11... | collective-permute-start | bytes 196616 | tf_op jit(solution)/shard_map/ppermute | solution.py:540

commit v4 on v3

--- a/solution.py
+++ b/solution.py
@@ -59,27 +59,6 @@
 
 def lanes(x3):
     return jnp.concatenate([x3[b] for b in range(x3.shape[0])], axis=1)
-
-
-def half_kernel(x3, half_ref, sem):
-    share = half_ref.shape[0]
-    copy = pltpu.make_async_copy(x3.at[pl.ds(lax.axis_index("rep") * share, share)], half_ref, sem)
-    copy.start()
-    copy.wait()
-
-
-def half_of(values, reps):
-    blocks_dev, columns, width = values.shape
-    anywhere = pl.BlockSpec(memory_space=pl.ANY)
-    return call(
-        half_kernel,
-        "half",
-        shape((blocks_dev // reps, columns, width), BF16),
-        [anywhere],
-        [pltpu.SemaphoreType.DMA],
-        limit=VMEM_ALL,
-        out_specs=anywhere,
-    )(values)
 
 
 def places(peers, blocks_dev, count, row, col, ask_refs):
@@ -98,16 +77,33 @@
     return place
 
 
+def prepare_kernel(peers, count_ref, row_ref, col_ref, x3, half_ref, place_ref, *ask_refs):
+    share = half_ref.shape[0]
+    half_ref[...] = x3[pl.ds(lax.axis_index("rep") * share, share)]
+    count = jnp.broadcast_to(count_ref[...], (1, 1))
+    place_ref[...] = places(peers, x3.shape[0], count, row_ref[...], col_ref[...], ask_refs)
+
+
+def prepare(features, tile_row, tile_col, tile_count, peers, reps):
+    per = tile_col.shape[0]
+    blocks_dev, columns, width = features.shape
+    outs = call(
+        functools.partial(prepare_kernel, peers),
+        "prepare",
+        [shape((blocks_dev // reps, columns, width), BF16)] + [shape((1, per), jnp.int32)] * (peers + 1),
+        [vmem()] * 4,
+        limit=VMEM_ALL,
+    )(tile_count, tile_row.reshape(1, per), tile_col.reshape(1, per), features)
+    return outs[0], outs[1], list(outs[2:])
+
+
 def pick(ids_ref, lane):
     ids = ids_ref[...].astype(F32)
     at = lax.broadcasted_iota(jnp.int32, ids.shape, 1)
     return jnp.max(jnp.where(at == lane, ids, 0.0)).astype(jnp.int32)
 
 
-def operator_kernel(peers, blocks_dev, slots_here, groups, *refs):
-    count_ref, row_ref, col_ref, tiles_ref, m_ref = refs[:5]
-    ask_refs, refs = refs[5 : 5 + peers], refs[5 + peers :]
-    tiles, acc, place_lanes, place_ref, sems, sem = refs
+def operator_kernel(blocks_dev, slots_here, groups, place_in, tiles_ref, m_ref, tiles, acc, place_ref, sems, sem):
     step = pl.program_id(0)
     per, width = tiles.shape[0], tiles.shape[1]
     chunks = per // CHUNK
@@ -119,11 +115,10 @@
 
     @pl.when(step == 0)
     def _():
+        placed = pltpu.make_async_copy(place_in, place_ref, sem)
+        placed.start()
         for c in range(chunks):
             chunk_copy(c).start()
-        place_lanes[...] = places(peers, blocks_dev, count_ref[...], row_ref[...], col_ref[...], ask_refs)
-        placed = pltpu.make_async_copy(place_lanes, place_ref, sem)
-        placed.start()
         placed.wait()
 
     acc[...] = jnp.zeros_like(acc)
@@ -152,20 +147,19 @@
             m_ref[r * width : (r + 1) * width, s * width : (s + 1) * width] = total.astype(BF16)
 
 
-def list_operator(tiles, tile_row, tile_col, tile_count, peers, blocks_dev):
+def list_operator(tiles, place, peers, blocks_dev):
     per, width = tiles.shape[0], tiles.shape[1]
     slots = peers * CAP
     slots_here = min(slots, GROUP)
     groups = slots // slots_here
-    outs = call(
-        functools.partial(operator_kernel, peers, blocks_dev, slots_here, groups),
+    return call(
+        functools.partial(operator_kernel, blocks_dev, slots_here, groups),
         "operator",
-        [shape((blocks_dev * width, slots * width), BF16)] + [shape((1, per), jnp.int32)] * peers,
-        [vmem(), vmem(), vmem(), hbm()],
+        shape((blocks_dev * width, slots * width), BF16),
+        [pl.BlockSpec(memory_space=pl.ANY), hbm()],
         [
             pltpu.VMEM((per, width, width), BF16),
             pltpu.VMEM((SIDES, slots_here * blocks_dev + 1, width, width), F32),
-            pltpu.VMEM((1, per), jnp.int32),
             pltpu.SMEM((1, per), jnp.int32),
             pltpu.SemaphoreType.DMA((per // CHUNK,)),
             pltpu.SemaphoreType.DMA,
@@ -173,9 +167,8 @@
         moved=2 ** 24,
         limit=VMEM_MOST,
         grid=(groups,),
-        out_specs=[pl.BlockSpec((blocks_dev * width, slots_here * width), lambda i: (0, i))] + [vmem()] * peers,
-    )(tile_count.reshape(1, 1), tile_row.reshape(1, per), tile_col.reshape(1, per), tiles)
-    return outs[0], list(outs[1:])
+        out_specs=pl.BlockSpec((blocks_dev * width, slots_here * width), lambda i: (0, i)),
+    )(place, tiles)
 
 
 def mirrored(near, m_ref, mir, slots, width):
@@ -192,10 +185,12 @@
 
 def first_sends_kernel(peers, *refs):
     ask_refs, refs = refs[: peers - 1], refs[peers - 1 :]
-    x3, m_ref, refs = refs[0], refs[1], refs[2:]
-    send_refs, self_ref, mir = refs[: peers - 1], refs[peers - 1], refs[peers]
+    x3, cot, m_ref, refs = refs[0], refs[1], refs[2], refs[3:]
+    send_refs, self_ref, cot_ref, mir = refs[: peers - 1], refs[peers - 1], refs[peers], refs[peers + 1]
     _, columns, width = x3.shape
+    share = cot_ref.shape[0]
     both = CAP * width
+    half = lax.axis_index("rep")
     mirrored(lanes(x3), m_ref, mir, peers * CAP, width)
     self_ref[...] = mir[:, :both]
     lane = lax.broadcasted_iota(jnp.int32, (TAIL, both), 1)
@@ -204,20 +199,23 @@
         out[:columns, :] = mir[:, k * both : (k + 1) * both].astype(BF16)
         low, high = ask_refs[k - 1][:, :1], ask_refs[k - 1][:, 1:2]
         out[columns:, :] = jnp.where(lane < width, low, high).astype(F32).astype(BF16)
-
-
-def first_sends(values, operator, asks, peers):
-    _, columns, width = values.shape
+    cot_ref[...] = cot[pl.ds(half * share, share)]
+
+
+def first_sends(values, cotangent, operator, asks, peers, reps):
+    blocks_dev, columns, width = values.shape
+    share = blocks_dev // reps
     outs = call(
         functools.partial(first_sends_kernel, peers),
         "first_sends",
-        [shape((columns + TAIL, CAP * width), BF16)] * (peers - 1) + [shape((columns, CAP * width), F32)],
-        [vmem()] * (peers + 1),
+        [shape((columns + TAIL, CAP * width), BF16)] * (peers - 1)
+        + [shape((columns, CAP * width), F32), shape((share, columns, width), BF16)],
+        [vmem()] * (peers + 2),
         [pltpu.VMEM((columns, peers * CAP * width), F32)],
         flops=2 ** 28,
         moved=2 ** 21,
-    )(*asks, values, operator)
-    return [None] + list(outs[: peers - 1]), outs[peers - 1]
+    )(*asks, values, cotangent, operator)
+    return [None] + list(outs[: peers - 1]), outs[peers - 1], outs[peers]
 
 
 def add_sums(acc, block, sums):
@@ -482,7 +480,6 @@
         for s in range(CAP):
             at = (CAP + s) * width
             out[:, at : at + width] = x3[pick(ids_refs[k - 1], s)]
-    send_refs[0][:, 2 * both :] = term
 
 
 def sends_of(mine, came, keep, operator, ids, peers, reps):
@@ -491,8 +488,8 @@
     outs = call(
         functools.partial(send_kernel, peers),
         "sends",
-        [shape((share * reps, columns, width), BF16), shape((columns, chunk + keep.shape[1]), BF16)]
-        + [shape((columns, chunk), BF16)] * (peers - 2)
+        [shape((share * reps, columns, width), BF16)]
+        + [shape((columns, chunk), BF16)] * (peers - 1)
         + [shape((columns, CAP * width), F32), shape(keep.shape, BF16)],
         [vmem()] * (peers + 3),
         [pltpu.VMEM((columns, peers * CAP * width), F32)],
@@ -502,15 +499,12 @@
     return outs[0], [None] + list(outs[1:peers]), outs[peers], outs[peers + 1]
 
 
-def pair_kernel(at, mine_ref, came_ref, out_ref):
-    total = mine_ref[...].astype(F32) + came_ref[:, at:].astype(F32)
-    out_ref[...] = total.astype(out_ref.dtype)
-
-
-def pair_sum(mine, came, at, dtype):
-    return call(functools.partial(pair_kernel, at), "pair_sum", shape(mine.shape, dtype), [vmem(), vmem()])(
-        mine, came
-    )
+def pair_kernel(mine_ref, came_ref, out_ref):
+    out_ref[...] = (mine_ref[...].astype(F32) + came_ref[...].astype(F32)).astype(out_ref.dtype)
+
+
+def pair_sum(mine, came, dtype):
+    return call(pair_kernel, "pair_sum", shape(mine.shape, dtype), [vmem(), vmem()])(mine, came)
 
 
 def finish_kernel(mine_ref, other_ref, share_ref, other_share_ref, act_ref, came_ref, grad_ref, weight_ref, out_ref):
@@ -555,9 +549,9 @@
     reps = lax.axis_size("rep")
     far_first = sorted(range(1, peers), key=lambda k: (-(k & (peers // 2)), k))
 
-    half = half_of(features, reps)
-    operator, asks = list_operator(tiles, tile_row, tile_col, tile_count, peers, blocks_dev)
-    sends, own_mirror = first_sends(features, operator, asks[1:], peers)
+    half, place, asks = prepare(features, tile_row, tile_col, tile_count, peers, reps)
+    operator = list_operator(tiles, place, peers, blocks_dev)
+    sends, own_mirror, own_cot = first_sends(features, cotangent, operator, asks[1:], peers, reps)
     pieces, held = {0: [half]}, [0]
     bit = peers // 2
     while bit:
@@ -571,14 +565,14 @@
     came = [None] * peers
     for k in far_first:
         came[k] = across(sends[k], peers, k)
-    arrived = [pieces[k] for k in range(1, peers)]
+    arrived = [part for k in range(1, peers) for part in pieces[k]]
     ordered, arrived = lax.optimization_barrier(([came[k] for k in far_first], arrived))
     came = [None] + [ordered[far_first.index(k)] for k in range(1, peers)]
-    stacked = stack([part for parts in arrived for part in parts])
+    stacked = stack(arrived)
     swapped = ahead(stacked, "rep", reps, 1)
-    cots = [half_of(cotangent, reps)]
+    cots = [own_cot]
     if feats > 1:
-        waited = after(cots[0], stacked)
+        waited = after(own_cot, stacked)
         cots += [ahead(waited, "feat", feats, feats - q) for q in range(1, feats)]
     acc, ids = first_rows(features, operator, asks[0], came, own_mirror, peers)
     give, keep = far_rows(acc, asks, stacked, swapped, operator, peers, reps)
@@ -593,12 +587,12 @@
     came = [None] * peers
     for k in far_first:
         came[k] = across(sends[k], peers, k)
-    total = pair_sum(term, came[1], 2 * CAP * width, F32 if peers == 2 else BF16)
-    bit = 2
+    total, bit = term, 1
     while bit < peers:
-        total = pair_sum(total, across(total, peers, bit), 0, F32 if 2 * bit == peers else BF16)
+        total = pair_sum(total, across(total, peers, bit), F32 if 2 * bit == peers else BF16)
         bit *= 2
-    came, total = lax.optimization_barrier((came, total))
+    ordered, total = lax.optimization_barrier(([came[k] for k in far_first], total))
+    came = [None] + [ordered[far_first.index(k)] for k in range(1, peers)]
     part = late_rows([asks[0], values, own_mirror], ids, came, far_first, operator, True, True)
     input_grad, weight_grad, activated = finish(
         part, ahead(part, "rep", reps, 1), total, ahead(total, "rep", reps, 1), act, shared

time: 67.7 us -> 60.2 us (0.89)
  Pallas kernels: 18.1 us -> 9.69 us
  waiting for transfers between devices: 26.7 us -> 28.4 us
    pallas_call x5 -> x4, Pallas kernels: 13.3 us -> 4.88 us  [the longest x1 3.04 us: list_operator(): call(functools.partial(operator_kernel, blocks_dev, slots_here, groups),...]
    ppermute x11 -> x12, waiting for transfers between devices: 17.3 us -> 19.3 us  [across(): return lax.ppermute(value, 'graph', [(i, i ^ k) for i in range(peers)])]
    ppermute x11 -> x12, starting transfers between devices: 15.8 us -> 15.7 us  [across(): return lax.ppermute(value, 'graph', [(i, i ^ k) for i in range(peers)])]
  transfers between devices with their start and end apart: 18 -> 19, of which waited for: 10 -> 10; matrix products, arithmetic and copies ran while one was open for 0% -> 0% of each run, Pallas kernels for 15% -> 8%
where the time goes in v4:
time: 60.2 us; the launch traced here: 60.1 us
  waiting for transfers between devices  28.4 us (47%)
  starting transfers between devices  19.8 us (33%)
  Pallas kernels  9.69 us (16%)
  between operations  1.54 us (3%)
  local copies, waits for them, and re-layouts  0.68 us (1%)
    ppermute x12, waiting for transfers between devices, across(): return lax.ppermute(value, 'graph', [(i, i ^ k) for i in range(peers)])  19.3 us
    ppermute x12, starting transfers between devices, across(): return lax.ppermute(value, 'graph', [(i, i ^ k) for i in range(peers)])  15.7 us
    ppermute x7, waiting for transfers between devices, ahead(): return lax.ppermute(value, axis, [(i, (i + k) % size) for i in range(size)])  9.14 us
    ppermute x7, starting transfers between devices, ahead(): return lax.ppermute(value, axis, [(i, (i + k) % size) for i in range(size)])  4.06 us
    pallas_call x1, Pallas kernels, list_operator(): call(functools.partial(operator_kernel, blocks_dev, slots_here, groups),...  3.04 us
    pallas_call x1, Pallas kernels, prepare(): call(functools.partial(prepare_kernel, peers), 'prepare', [shape((blocks_...  1.81 us
  transfers between devices with their start and end apart: 19, of which 10 were waited for; matrix products, arithmetic and copies ran while one was open for 0% of the time, Pallas kernels for 8%

profile of v4, /device:TPU:0, one launch (start us, length us, event | category | flops | bytes accessed | tf_op | source)
XLA Modules:
  0.0 60.1 jit_solution(12443215340068530043)
XLA Ops:
  1.4 1.8 %prepare.1 = (bf16[4,128,128]{2,1,0:T(8,128)(2,1)}, s32[1,128]{1,0:T(1,128)}, s32[1,128]{1,0:T(1,128)}, s32[1,128]{1,0:T(1,128)}, s32[1,128]{1,0:T(1,128)}, /*index=5*/s32[1,128]{1,0:T(1,128)}) custom-call(s32[1]{0:T(128)S(6)} %copy.10.count_ref, s32[1,128]{1,0:T(1,128)} %bitcast.2, s32[1,128]{1,0:T(1,128)} %bitcast.3, bf16[8,128,128]{2,1,0:T(8,128)(2,1)} %refs_4_.4), custom_call_target="tpu_custom_call" | custom-call | bytes 262144 | tf_op jit(solution)/shard_map/prepare/pallas_call | solution.py:90
  3.2 4.1 %collective-permute-start.4 = (bf16[4,128,128]{2,1,0:T(8,128)(2,1)}, bf16[4,128,128]{2,1,0:T(8,128)(2,1)S(1)}, u32[]{:S(2)}, u32[]{:S(2)}) collective-permute-start(bf16[4,128,128]{2,1,0:T(8,128)(2,1)} %get-tuple-element.61), channel_id=1, source_target_pairs={{0,8},{4,12},{8,0},{12,4},{1,9},{5,13},{9,1},{13,5},{2,10},{6,14},... | collective-permute-start | bytes 393224 | tf_op jit(solution)/shard_map/ppermute | solution.py:538
  7.3 1.6 %collective-permute-start.3 = (bf16[4,128,128]{2,1,0:T(8,128)(2,1)}, bf16[4,128,128]{2,1,0:T(8,128)(2,1)S(1)}, u32[]{:S(2)}, u32[]{:S(2)}) collective-permute-start(bf16[4,128,128]{2,1,0:T(8,128)(2,1)} %get-tuple-element.61), channel_id=1, source_target_pairs={{0,4},{4,0},{8,12},{12,8},{1,5},{5,1},{9,13},{13,9},{2,6},{6,2},{1... | collective-permute-start | bytes 393224 | tf_op jit(solution)/shard_map/ppermute | solution.py:538
  9.5 3.0 %operator.1.refs_5_.refs_6_.refs_9_ = bf16[1024,1024]{1,0:T(8,128)(2,1)S(1)} custom-call(s32[1,128]{1,0:T(1,128)S(1)} %copy-done.6, bf16[128,128,128]{2,1,0:T(8,128)(2,1)} %tiles_ref.1), custom_call_target="tpu_custom_call" | custom-call | bytes 16777216 | tf_op jit(solution)/shard_map/operator/pallas_call | solution.py:155
  13.5 2.5 %collective-permute-start.1 = (bf16[144,256]{1,0:T(8,128)(2,1)S(1)}, bf16[144,256]{1,0:T(8,128)(2,1)S(1)}, u32[]{:S(2)}, u32[]{:S(2)}) collective-permute-start(bf16[144,256]{1,0:T(8,128)(2,1)S(1)} %get-tuple-element.59), channel_id=1, source_target_pairs={{0,12},{4,8},{8,4},{12,0},{1,13},{5,9},{9,5},{13,1},{2,14},{6,10},... | collective-permute-start | bytes 221192 | tf_op jit(solution)/shard_map/ppermute | solution.py:538
  16.7 1.4 %collective-permute-start.5 = (bf16[2,128,128]{2,1,0:T(8,128)(2,1)S(1)}, bf16[2,128,128]{2,1,0:T(8,128)(2,1)S(1)}, u32[]{:S(2)}, u32[]{:S(2)}) collective-permute-start(bf16[2,128,128]{2,1,0:T(8,128)(2,1)S(1)} %get-tuple-element.65), channel_id=1, source_target_pairs={{0,4},{4,0},{8,12},{12,8},{1,5},{5,1},{9,13},{13,9},{2,6},{6,2},{1... | collective-permute-start | bytes 196616 | tf_op jit(solution)/shard_map/ppermute | solution.py:538
  18.8 2.1 %collective-permute-done.refs_2_ = bf16[144,256]{1,0:T(8,128)(2,1)S(1)} collective-permute-done((bf16[144,256]{1,0:T(8,128)(2,1)S(1)}, bf16[144,256]{1,0:T(8,128)(2,1)S(1)}, u32[]{:S(2)}, u32[]{:S(2)}) %collective-permute-start) | collective-permute-done | bytes 73760 | tf_op jit(solution)/shard_map/ppermute | solution.py:538
  20.9 1.4 %collective-permute-done.2.refs_1_ = bf16[144,256]{1,0:T(8,128)(2,1)S(1)} collective-permute-done((bf16[144,256]{1,0:T(8,128)(2,1)S(1)}, bf16[144,256]{1,0:T(8,128)(2,1)S(1)}, u32[]{:S(2)}, u32[]{:S(2)}) %collective-permute-start.2) | collective-permute-done | bytes 73760 | tf_op jit(solution)/shard_map/ppermute | solution.py:538
  22.2 1.2 %collective-permute-done.5.refs_2_ = bf16[2,128,128]{2,1,0:T(8,128)(2,1)S(1)} collective-permute-done((bf16[2,128,128]{2,1,0:T(8,128)(2,1)S(1)}, bf16[2,128,128]{2,1,0:T(8,128)(2,1)S(1)}, u32[]{:S(2)}, u32[]{:S(2)}) %collective-permute-start.5) | collective-permute-done | bytes 65568 | tf_op jit(solution)/shard_map/ppermute | solution.py:538
  23.5 0.7 %collective-permute-done.6.refs_3_ = bf16[2,128,128]{2,1,0:T(8,128)(2,1)S(1)} collective-permute-done((bf16[2,128,128]{2,1,0:T(8,128)(2,1)S(1)}, bf16[2,128,128]{2,1,0:T(8,128)(2,1)S(1)}, u32[]{:S(2)}, u32[]{:S(2)}) %collective-permute-start.6) | collective-permute-done | bytes 65568 | tf_op jit(solution)/shard_map/ppermute | solution.py:538
  24.3 1.6 %collective-permute-start.9 = (bf16[4,128,128]{2,1,0:T(8,128)(2,1)S(1)}, bf16[4,128,128]{2,1,0:T(8,128)(2,1)S(1)}, u32[]{:S(2)}, u32[]{:S(2)}) collective-permute-start(bf16[4,128,128]{2,1,0:T(8,128)(2,1)S(1)} %get-tuple-element.84.refs_2_), channel_id=1, source_target_pairs={{0,2},{2,0},{1,3},{3,1},{4,6},{6,4},{5,7},{7,5},{8,10},{10,8},{9,1... | collective-permute-start | bytes 393224 | tf_op jit(solution)/shard_map/ppermute | solution.py:534
  26.3 0.8 %far_rows.1 = (bf16[4,128,128]{2,1,0:T(8,128)(2,1)S(1)}, f32[4,128,128]{2,1,0:T(8,128)S(1)}) custom-call(s32[1,128]{1,0:T(1,128)S(1)} %copy-done.3, s32[1,128]{1,0:T(1,128)S(1)} %copy-done.4, s32[1,128]{1,0:T(1,128)S(1)} %copy-done.5, f32[8,128,128]{2,1,0:T(8,128)S(1)} %get-tuple-element.74.refs_3_, bf16[12,128,128]{2,1,0:T(8,128)(2,1)S(1)} %stack.1.refs_4_, ...), custom_call_target="tpu_custom_call" | custom-call | flops 268435456 | bytes 2097152 | tf_op jit(solution)/shard_map/far_rows/pallas_call | solution.py:340
  27.3 2.9 %collective-permute-done.9.refs_3_ = bf16[4,128,128]{2,1,0:T(8,128)(2,1)S(1)} collective-permute-done((bf16[4,128,128]{2,1,0:T(8,128)(2,1)S(1)}, bf16[4,128,128]{2,1,0:T(8,128)(2,1)S(1)}, u32[]{:S(2)}, u32[]{:S(2)}) %collective-permute-start.9) | collective-permute-done | bytes 131104 | tf_op jit(solution)/shard_map/ppermute | solution.py:534
  30.2 1.6 %collective-permute-start.10 = (bf16[4,128,128]{2,1,0:T(8,128)(2,1)S(1)}, bf16[4,128,128]{2,1,0:T(8,128)(2,1)S(1)}, u32[]{:S(2)}, u32[]{:S(2)}) collective-permute-start(bf16[4,128,128]{2,1,0:T(8,128)(2,1)S(1)} %add_up.1.refs_0_), channel_id=1, source_target_pairs={{0,2},{2,0},{1,3},{3,1},{4,6},{6,4},{5,7},{7,5},{8,10},{10,8},{9,1... | collective-permute-start | bytes 393224 | tf_op jit(solution)/shard_map/ppermute | solution.py:534
  31.8 3.6 %collective-permute-done.10.refs_1_ = bf16[4,128,128]{2,1,0:T(8,128)(2,1)S(1)} collective-permute-done((bf16[4,128,128]{2,1,0:T(8,128)(2,1)S(1)}, bf16[4,128,128]{2,1,0:T(8,128)(2,1)S(1)}, u32[]{:S(2)}, u32[]{:S(2)}) %collective-permute-start.10) | collective-permute-done | bytes 131104 | tf_op jit(solution)/shard_map/ppermute | solution.py:534
  35.3 0.7 %dense.1 = (bf16[4,128,128]{2,1,0:T(8,128)(2,1)S(1)}, bf16[128,1152]{1,0:T(8,128)(2,1)S(1)}, bf16[4,128,128]{2,1,0:T(8,128)(2,1)S(1)}, f32[128,128]{1,0:T(8,128)S(1)}) custom-call(bf16[4,128,128]{2,1,0:T(8,128)(2,1)S(1)} %add_up.1.refs_0_, bf16[4,128,128]{2,1,0:T(8,128)(2,1)S(1)} %collective-permute-done.10.refs_1_, ...), custom_call_target="tpu_custom_call" | custom-call | flops 268435456 | bytes 1048576 | tf_op jit(solution)/shard_map/dense/pallas_call | solution.py:439
  36.1 1.6 %collective-permute-done.11.refs_4_.came_ref = bf16[128,1152]{1,0:T(8,128)(2,1)S(1)} collective-permute-done((bf16[128,1152]{1,0:T(8,128)(2,1)S(1)}, bf16[128,1152]{1,0:T(8,128)(2,1)S(1)}, u32[]{:S(2)}, u32[]{:S(2)}) %collective-permute-start.11) | collective-permute-done | bytes 294944 | tf_op jit(solution)/shard_map/ppermute | solution.py:534
  38.3 2.0 %collective-permute-start.13 = (bf16[128,512]{1,0:T(8,128)(2,1)S(1)}, bf16[128,512]{1,0:T(8,128)(2,1)S(1)}, u32[]{:S(2)}, u32[]{:S(2)}) collective-permute-start(bf16[128,512]{1,0:T(8,128)(2,1)S(1)} %get-tuple-element.92), channel_id=1, source_target_pairs={{0,12},{4,8},{8,4},{12,0},{1,13},{5,9},{9,5},{13,1},{2,14},{6,10},... | collective-permute-start | bytes 393224 | tf_op jit(solution)/shard_map/ppermute | solution.py:538
  40.3 1.4 %collective-permute-start.14 = (bf16[128,512]{1,0:T(8,128)(2,1)S(1)}, bf16[128,512]{1,0:T(8,128)(2,1)S(1)}, u32[]{:S(2)}, u32[]{:S(2)}) collective-permute-start(bf16[128,512]{1,0:T(8,128)(2,1)S(1)} %get-tuple-element.93), channel_id=1, source_target_pairs={{0,4},{4,0},{8,12},{12,8},{1,5},{5,1},{9,13},{13,9},{2,6},{6,2},{1... | collective-permute-start | bytes 393224 | tf_op jit(solution)/shard_map/ppermute | solution.py:538
  42.3 9.2 %collective-permute-done.15.came_ref = bf16[128,128]{1,0:T(8,128)(2,1)S(1)} collective-permute-done((bf16[128,128]{1,0:T(8,128)(2,1)S(1)}, bf16[128,128]{1,0:T(8,128)(2,1)S(1)}, u32[]{:S(2)}, u32[]{:S(2)}) %collective-permute-start.15) | collective-permute-done | bytes 32800 | tf_op jit(solution)/shard_map/ppermute | solution.py:538
  51.8 4.7 %collective-permute-done.16.came_ref = bf16[128,128]{1,0:T(8,128)(2,1)S(1)} collective-permute-done((bf16[128,128]{1,0:T(8,128)(2,1)S(1)}, bf16[128,128]{1,0:T(8,128)(2,1)S(1)}, u32[]{:S(2)}, u32[]{:S(2)}) %collective-permute-start.16) | collective-permute-done | bytes 32800 | tf_op jit(solution)/shard_map/ppermute | solution.py:538
  56.5 0.9 %late_rows.1.mine_ref = bf16[8,128,128]{2,1,0:T(8,128)(2,1)S(1)} custom-call(s32[1,128]{1,0:T(1,128)S(1)} %copy-done.2, bf16[8,128,128]{2,1,0:T(8,128)(2,1)S(1)} %get-tuple-element.89.refs_1_, f32[128,256]{1,0:T(8,128)S(1)} %get-tuple-element.90.refs_2_, s32[1,128]{1,0:T(1,128)S(1)} %get-tuple-element.72.refs_1_.refs_3_, ...), custom_call_target="tpu_custom_call" | custom-call | flops 134217728 | bytes 1048576 | tf_op jit(solution)/shard_map/late_rows/pallas_call | solution.py:384
  58.0 1.1 %collective-permute-done.18.other_share_ref = f32[128,128]{1,0:T(8,128)S(1)} collective-permute-done((f32[128,128]{1,0:T(8,128)S(1)}, f32[128,128]{1,0:T(8,128)S(1)}, u32[]{:S(2)}, u32[]{:S(2)}) %collective-permute-start.18) | collective-permute-done | bytes 65568 | tf_op jit(solution)/shard_map/ppermute | solution.py:534
  59.1 1.0 %finish.1 = (bf16[8,128,128]{2,1,0:T(8,128)(2,1)}, f32[256,128]{1,0:T(8,128)}, bf16[8,128,128]{2,1,0:T(8,128)(2,1)}) custom-call(bf16[8,128,128]{2,1,0:T(8,128)(2,1)S(1)} %late_rows.1.mine_ref, bf16[8,128,128]{2,1,0:T(8,128)(2,1)S(1)} %collective-permute-done.17.other_ref, f32[128,128]{1,0:T(8,128)S(1)} %pair_sum.3.share_ref, ...), custom_call_target="tpu_custom_call" | custom-call | bytes 262144 | tf_op jit(solution)/shard_map/finish/pallas_call | solution.py:525
  (44 shorter events, 5.8 us)
Async XLA Ops:
  0.6 11.9 %copy-start = (bf16[8,128,128]{2,1,0:T(8,128)(2,1)S(1)}, bf16[8,128,128]{2,1,0:T(8,128)(2,1)}, u32[]{:S(2)}) copy-start(bf16[8,128,128]{2,1,0:T(8,128)(2,1)} %refs_4_.4) | copy-start | bytes 786436
  0.6 11.9 %copy-start.1 = (bf16[8,128,128]{2,1,0:T(8,128)(2,1)S(1)}, bf16[8,128,128]{2,1,0:T(8,128)(2,1)}, u32[]{:S(2)}) copy-start(bf16[8,128,128]{2,1,0:T(8,128)(2,1)} %refs_4_.3) | copy-start | bytes 786436
  3.2 9.4 %copy-start.5 = (s32[1,128]{1,0:T(1,128)S(1)}, s32[1,128]{1,0:T(1,128)}, u32[]{:S(2)}) copy-start(s32[1,128]{1,0:T(1,128)} %get-tuple-element.56.refs_2_) | copy-start | bytes 1540
  3.2 13.5 %collective-permute-start.4 = (bf16[4,128,128]{2,1,0:T(8,128)(2,1)}, bf16[4,128,128]{2,1,0:T(8,128)(2,1)S(1)}, u32[]{:S(2)}, u32[]{:S(2)}) collective-permute-start(bf16[4,128,128]{2,1,0:T(8,128)(2,1)} %get-tuple-element.61), channel_id=1, source_target_pairs={{0,8},{4,12},{8,0},{12,4},{1,9},{5,13},{9,1},{13,5},{2,10},{6,14},... | collective-permute-start | bytes 393224 | tf_op jit(solution)/shard_map/ppermute | solution.py:538
  7.3 9.4 %collective-permute-start.3 = (bf16[4,128,128]{2,1,0:T(8,128)(2,1)}, bf16[4,128,128]{2,1,0:T(8,128)(2,1)S(1)}, u32[]{:S(2)}, u32[]{:S(2)}) collective-permute-start(bf16[4,128,128]{2,1,0:T(8,128)(2,1)} %get-tuple-element.61), channel_id=1, source_target_pairs={{0,4},{4,0},{8,12},{12,8},{1,5},{5,1},{9,13},{13,9},{2,6},{6,2},{1... | collective-permute-start | bytes 393224 | tf_op jit(solution)/shard_map/ppermute | solution.py:538
  9.5 16.3 %copy-start.2 = (s32[1,128]{1,0:T(1,128)S(1)}, s32[1,128]{1,0:T(1,128)}, u32[]{:S(2)}) copy-start(s32[1,128]{1,0:T(1,128)} %get-tuple-element.53.refs_0_) | copy-start | bytes 1540
  13.1 22.2 %copy-start.7 = (bf16[256,256]{1,0:T(8,128)(2,1)S(1)}, bf16[256,256]{1,0:T(8,128)(2,1)}, u32[]{:S(2)}) copy-start(bf16[256,256]{1,0:T(8,128)(2,1)} %refs_4_.5) | copy-start | bytes 393220
  13.1 7.7 %collective-permute-start = (bf16[144,256]{1,0:T(8,128)(2,1)S(1)}, bf16[144,256]{1,0:T(8,128)(2,1)S(1)}, u32[]{:S(2)}, u32[]{:S(2)}) collective-permute-start(bf16[144,256]{1,0:T(8,128)(2,1)S(1)} %get-tuple-element.58), channel_id=1, source_target_pairs={{0,8},{4,12},{8,0},{12,4},{1,9},{5,13},{9,1},{13,5},{2,10},{6,14},... | collective-permute-start | bytes 221192 | tf_op jit(solution)/shard_map/ppermute | solution.py:538
  13.5 7.4 %collective-permute-start.1 = (bf16[144,256]{1,0:T(8,128)(2,1)S(1)}, bf16[144,256]{1,0:T(8,128)(2,1)S(1)}, u32[]{:S(2)}, u32[]{:S(2)}) collective-permute-start(bf16[144,256]{1,0:T(8,128)(2,1)S(1)} %get-tuple-element.59), channel_id=1, source_target_pairs={{0,12},{4,8},{8,4},{12,0},{1,13},{5,9},{9,5},{13,1},{2,14},{6,10},... | collective-permute-start | bytes 221192 | tf_op jit(solution)/shard_map/ppermute | solution.py:538
  16.0 6.3 %collective-permute-start.2 = (bf16[144,256]{1,0:T(8,128)(2,1)S(1)}, bf16[144,256]{1,0:T(8,128)(2,1)S(1)}, u32[]{:S(2)}, u32[]{:S(2)}) collective-permute-start(bf16[144,256]{1,0:T(8,128)(2,1)S(1)} %get-tuple-element.60), channel_id=1, source_target_pairs={{0,4},{4,0},{8,12},{12,8},{1,5},{5,1},{9,13},{13,9},{2,6},{6,2},{1... | collective-permute-start | bytes 221192 | tf_op jit(solution)/shard_map/ppermute | solution.py:538
  16.7 6.8 %collective-permute-start.5 = (bf16[2,128,128]{2,1,0:T(8,128)(2,1)S(1)}, bf16[2,128,128]{2,1,0:T(8,128)(2,1)S(1)}, u32[]{:S(2)}, u32[]{:S(2)}) collective-permute-start(bf16[2,128,128]{2,1,0:T(8,128)(2,1)S(1)} %get-tuple-element.65), channel_id=1, source_target_pairs={{0,4},{4,0},{8,12},{12,8},{1,5},{5,1},{9,13},{13,9},{2,6},{6,2},{1... | collective-permute-start | bytes 196616 | tf_op jit(solution)/shard_map/ppermute | solution.py:538
  18.1 6.1 %collective-permute-start.6 = (bf16[2,128,128]{2,1,0:T(8,128)(2,1)S(1)}, bf16[2,128,128]{2,1,0:T(8,128)(2,1)S(1)}, u32[]{:S(2)}, u32[]{:S(2)}) collective-permute-start(bf16[2,128,128]{2,1,0:T(8,128)(2,1)S(1)} %get-tuple-element.66), channel_id=1, source_target_pairs={{0,4},{4,0},{8,12},{12,8},{1,5},{5,1},{9,13},{13,9},{2,6},{6,2},{1... | collective-permute-start | bytes 196616 | tf_op jit(solution)/shard_map/ppermute | solution.py:538
  24.2 2.1 %collective-permute-start.7 = (bf16[12,128,128]{2,1,0:T(8,128)(2,1)S(1)}, bf16[12,128,128]{2,1,0:T(8,128)(2,1)S(1)}, u32[]{:S(2)}, u32[]{:S(2)}) collective-permute-start(bf16[12,128,128]{2,1,0:T(8,128)(2,1)S(1)} %stack.1.refs_4_), channel_id=1, source_target_pairs={{0,1},{1,0},{2,3},{3,2},{4,5},{5,4},{6,7},{7,6},{8,9},{9,8},{10,11... | collective-permute-start | bytes 1179656 | tf_op jit(solution)/shard_map/ppermute | solution.py:534
  24.3 5.9 %collective-permute-start.9 = (bf16[4,128,128]{2,1,0:T(8,128)(2,1)S(1)}, bf16[4,128,128]{2,1,0:T(8,128)(2,1)S(1)}, u32[]{:S(2)}, u32[]{:S(2)}) collective-permute-start(bf16[4,128,128]{2,1,0:T(8,128)(2,1)S(1)} %get-tuple-element.84.refs_2_), channel_id=1, source_target_pairs={{0,2},{2,0},{1,3},{3,1},{4,6},{6,4},{5,7},{7,5},{8,10},{10,8},{9,1... | collective-permute-start | bytes 393224 | tf_op jit(solution)/shard_map/ppermute | solution.py:534
  27.1 3.1 %collective-permute-start.8 = (bf16[4,128,128]{2,1,0:T(8,128)(2,1)S(1)}, bf16[4,128,128]{2,1,0:T(8,128)(2,1)S(1)}, u32[]{:S(2)}, u32[]{:S(2)}) collective-permute-start(bf16[4,128,128]{2,1,0:T(8,128)(2,1)S(1)} %get-tuple-element.80), channel_id=1, source_target_pairs={{0,1},{1,0},{2,3},{3,2},{4,5},{5,4},{6,7},{7,6},{8,9},{9,8},{10,11... | collective-permute-start | bytes 393224 | tf_op jit(solution)/shard_map/ppermute | solution.py:534
  30.2 5.1 %collective-permute-start.10 = (bf16[4,128,128]{2,1,0:T(8,128)(2,1)S(1)}, bf16[4,128,128]{2,1,0:T(8,128)(2,1)S(1)}, u32[]{:S(2)}, u32[]{:S(2)}) collective-permute-start(bf16[4,128,128]{2,1,0:T(8,128)(2,1)S(1)} %add_up.1.refs_0_), channel_id=1, source_target_pairs={{0,2},{2,0},{1,3},{3,1},{4,6},{6,4},{5,7},{7,5},{8,10},{10,8},{9,1... | collective-permute-start | bytes 393224 | tf_op jit(solution)/shard_map/ppermute | solution.py:534
  36.0 1.6 %collective-permute-start.11 = (bf16[128,1152]{1,0:T(8,128)(2,1)S(1)}, bf16[128,1152]{1,0:T(8,128)(2,1)S(1)}, u32[]{:S(2)}, u32[]{:S(2)}) collective-permute-start(bf16[128,1152]{1,0:T(8,128)(2,1)S(1)} %get-tuple-element.87), channel_id=1, source_target_pairs={{0,1},{1,0},{2,3},{3,2},{4,5},{5,4},{6,7},{7,6},{8,9},{9,8},{10,11... | collective-permute-start | bytes 884744 | tf_op jit(solution)/shard_map/ppermute | solution.py:534
  38.2 18.3 %collective-permute-start.12 = (bf16[128,512]{1,0:T(8,128)(2,1)S(1)}, bf16[128,512]{1,0:T(8,128)(2,1)S(1)}, u32[]{:S(2)}, u32[]{:S(2)}) collective-permute-start(bf16[128,512]{1,0:T(8,128)(2,1)S(1)} %get-tuple-element.91), channel_id=1, source_target_pairs={{0,8},{4,12},{8,0},{12,4},{1,9},{5,13},{9,1},{13,5},{2,10},{6,14},... | collective-permute-start | bytes 393224 | tf_op jit(solution)/shard_map/ppermute | solution.py:538
  38.3 18.2 %collective-permute-start.13 = (bf16[128,512]{1,0:T(8,128)(2,1)S(1)}, bf16[128,512]{1,0:T(8,128)(2,1)S(1)}, u32[]{:S(2)}, u32[]{:S(2)}) collective-permute-start(bf16[128,512]{1,0:T(8,128)(2,1)S(1)} %get-tuple-element.92), channel_id=1, source_target_pairs={{0,12},{4,8},{8,4},{12,0},{1,13},{5,9},{9,5},{13,1},{2,14},{6,10},... | collective-permute-start | bytes 393224 | tf_op jit(solution)/shard_map/ppermute | solution.py:538
  40.3 16.2 %collective-permute-start.14 = (bf16[128,512]{1,0:T(8,128)(2,1)S(1)}, bf16[128,512]{1,0:T(8,128)(2,1)S(1)}, u32[]{:S(2)}, u32[]{:S(2)}) collective-permute-start(bf16[128,512]{1,0:T(8,128)(2,1)S(1)} %get-tuple-element.93), channel_id=1, source_target_pairs={{0,4},{4,0},{8,12},{12,8},{1,5},{5,1},{9,13},{13,9},{2,6},{6,2},{1... | collective-permute-start | bytes 393224 | tf_op jit(solution)/shard_map/ppermute | solution.py:538
  41.7 9.8 %collective-permute-start.15 = (bf16[128,128]{1,0:T(8,128)(2,1)S(1)}, bf16[128,128]{1,0:T(8,128)(2,1)S(1)}, u32[]{:S(2)}, u32[]{:S(2)}) collective-permute-start(bf16[128,128]{1,0:T(8,128)(2,1)S(1)} %get-tuple-element.94.mine_ref), channel_id=1, source_target_pairs={{0,4},{4,0},{8,12},{12,8},{1,5},{5,1},{9,13},{13,9},{2,6},{6,2},{1... | collective-permute-start | bytes 98312 | tf_op jit(solution)/shard_map/ppermute | solution.py:538
  51.6 4.9 %collective-permute-start.16 = (bf16[128,128]{1,0:T(8,128)(2,1)S(1)}, bf16[128,128]{1,0:T(8,128)(2,1)S(1)}, u32[]{:S(2)}, u32[]{:S(2)}) collective-permute-start(bf16[128,128]{1,0:T(8,128)(2,1)S(1)} %pair_sum.2.mine_ref), channel_id=1, source_target_pairs={{0,8},{4,12},{8,0},{12,4},{1,9},{5,13},{9,1},{13,5},{2,10},{6,14},... | collective-permute-start | bytes 98312 | tf_op jit(solution)/shard_map/ppermute | solution.py:538
  57.4 1.7 %collective-permute-start.17 = (bf16[8,128,128]{2,1,0:T(8,128)(2,1)S(1)}, bf16[8,128,128]{2,1,0:T(8,128)(2,1)S(1)}, u32[]{:S(2)}, u32[]{:S(2)}) collective-permute-start(bf16[8,128,128]{2,1,0:T(8,128)(2,1)S(1)} %late_rows.1.mine_ref), channel_id=1, source_target_pairs={{0,1},{1,0},{2,3},{3,2},{4,5},{5,4},{6,7},{7,6},{8,9},{9,8},{10,11... | collective-permute-start | bytes 786440 | tf_op jit(solution)/shard_map/ppermute | solution.py:534
  57.5 1.6 %collective-permute-start.18 = (f32[128,128]{1,0:T(8,128)S(1)}, f32[128,128]{1,0:T(8,128)S(1)}, u32[]{:S(2)}, u32[]{:S(2)}) collective-permute-start(f32[128,128]{1,0:T(8,128)S(1)} %pair_sum.3.share_ref), channel_id=1, source_target_pairs={{0,1},{1,0},{2,3},{3,2},{4,5},{5,4},{6,7},{7,6},{8,9},{9,8},{10,11... | collective-permute-start | bytes 196616 | tf_op jit(solution)/shard_map/ppermute | solution.py:534
  (3 other events, 19.5 us)

commit v5 on v4

--- a/solution.py
+++ b/solution.py
@@ -480,6 +480,7 @@
         for s in range(CAP):
             at = (CAP + s) * width
             out[:, at : at + width] = x3[pick(ids_refs[k - 1], s)]
+    send_refs[peers // 2 - 1][:, 2 * both :] = term
 
 
 def sends_of(mine, came, keep, operator, ids, peers, reps):
@@ -489,7 +490,7 @@
         functools.partial(send_kernel, peers),
         "sends",
         [shape((share * reps, columns, width), BF16)]
-        + [shape((columns, chunk), BF16)] * (peers - 1)
+        + [shape((columns, chunk + (keep.shape[1] if 2 * k == peers else 0)), BF16) for k in range(1, peers)]
         + [shape((columns, CAP * width), F32), shape(keep.shape, BF16)],
         [vmem()] * (peers + 3),
         [pltpu.VMEM((columns, peers * CAP * width), F32)],
@@ -499,12 +500,13 @@
     return outs[0], [None] + list(outs[1:peers]), outs[peers], outs[peers + 1]
 
 
-def pair_kernel(mine_ref, came_ref, out_ref):
-    out_ref[...] = (mine_ref[...].astype(F32) + came_ref[...].astype(F32)).astype(out_ref.dtype)
-
-
-def pair_sum(mine, came, dtype):
-    return call(pair_kernel, "pair_sum", shape(mine.shape, dtype), [vmem(), vmem()])(mine, came)
+def pair_kernel(at, mine_ref, came_ref, out_ref):
+    out_ref[...] = (mine_ref[...].astype(F32) + came_ref[:, at:].astype(F32)).astype(out_ref.dtype)
+
+
+def pair_sum(mine, came, at, dtype):
+    kernel = functools.partial(pair_kernel, at)
+    return call(kernel, "pair_sum", shape(mine.shape, dtype), [vmem(), vmem()])(mine, came)
 
 
 def finish_kernel(mine_ref, other_ref, share_ref, other_share_ref, act_ref, came_ref, grad_ref, weight_ref, out_ref):
@@ -577,8 +579,7 @@
     acc, ids = first_rows(features, operator, asks[0], came, own_mirror, peers)
     give, keep = far_rows(acc, asks, stacked, swapped, operator, peers, reps)
 
-    given, cots = lax.optimization_barrier((ahead(give, "rep", reps, 1), cots))
-    mine = add_up(keep, given)
+    mine = add_up(keep, ahead(give, "rep", reps, 1))
     sums = [mine] + [ahead(mine, "feat", feats, feats - q) for q in range(1, feats)]
     act, give, spread, keep = dense(sums, cots, weight, feats, reps)
     shared = ahead(give, "rep", reps, 1)
@@ -587,13 +588,16 @@
     came = [None] * peers
     for k in far_first:
         came[k] = across(sends[k], peers, k)
-    total, bit = term, 1
-    while bit < peers:
-        total = pair_sum(total, across(total, peers, bit), F32 if 2 * bit == peers else BF16)
-        bit *= 2
-    ordered, total = lax.optimization_barrier(([came[k] for k in far_first], total))
-    came = [None] + [ordered[far_first.index(k)] for k in range(1, peers)]
-    part = late_rows([asks[0], values, own_mirror], ids, came, far_first, operator, True, True)
+    middle = peers // 2
+    total = pair_sum(term, came[middle], 2 * CAP * width, F32 if middle == 1 else BF16)
+    bit = middle // 2
+    while bit:
+        total = pair_sum(total, across(total, peers, bit), 0, F32 if bit == 1 else BF16)
+        bit //= 2
+    late = far_first[-2]
+    acc = late_rows([asks[0], values, own_mirror], ids, came, [k for k in far_first if k != late], operator, True, False)
+    acc, total = lax.optimization_barrier((acc, total))
+    part = late_rows([acc], ids, came, [late], operator, False, True)
     input_grad, weight_grad, activated = finish(
         part, ahead(part, "rep", reps, 1), total, ahead(total, "rep", reps, 1), act, shared
     )

time: 60.2 us -> 58.4 us (0.970)
  waiting for transfers between devices: 28.4 us -> 26.6 us
    ppermute x12 -> x11, waiting for transfers between devices: 19.3 us -> 16.9 us  [across(): return lax.ppermute(value, 'graph', [(i, i ^ k) for i in range(peers)])]
    ppermute x7, waiting for transfers between devices: 9.14 us -> 9.75 us  [ahead(): return lax.ppermute(value, axis, [(i, (i + k) % size) for i in range(size)])]
    ppermute x12 -> x11, starting transfers between devices: 15.7 us -> 15.8 us  [across(): return lax.ppermute(value, 'graph', [(i, i ^ k) for i in range(peers)])]
  transfers between devices with their start and end apart: 19 -> 18, of which waited for: 10 -> 11; matrix products, arithmetic and copies ran while one was open for 0% -> 0% of each run, Pallas kernels for 8% -> 8%
where the time goes in v5:
time: 58.4 us; the launch traced here: 58.2 us
  waiting for transfers between devices  26.6 us (46%)
  starting transfers between devices  19.5 us (33%)
  Pallas kernels  9.82 us (17%)
  between operations  1.55 us (3%)
  local copies, waits for them, and re-layouts  0.68 us (1%)
    ppermute x11, waiting for transfers between devices, across(): return lax.ppermute(value, 'graph', [(i, i ^ k) for i in range(peers)])  16.9 us
    ppermute x11, starting transfers between devices, across(): return lax.ppermute(value, 'graph', [(i, i ^ k) for i in range(peers)])  15.8 us
    ppermute x7, waiting for transfers between devices, ahead(): return lax.ppermute(value, axis, [(i, (i + k) % size) for i in range(size)])  9.75 us
    ppermute x7, starting transfers between devices, ahead(): return lax.ppermute(value, axis, [(i, (i + k) % size) for i in range(size)])  3.68 us
    pallas_call x1, Pallas kernels, list_operator(): call(functools.partial(operator_kernel, blocks_dev, slots_here, groups),...  3.04 us
    pallas_call x1, Pallas kernels, prepare(): call(functools.partial(prepare_kernel, peers), 'prepare', [shape((blocks_...  1.81 us
  transfers between devices with their start and end apart: 18, of which 11 were waited for; matrix products, arithmetic and copies ran while one was open for 0% of the time, Pallas kernels for 8%

profile of v5, /device:TPU:0, one launch (start us, length us, event | category | flops | bytes accessed | tf_op | source)
XLA Modules:
  0.0 58.2 jit_solution(4842890716983459586)
XLA Ops:
  1.4 1.8 %prepare.1 = (bf16[4,128,128]{2,1,0:T(8,128)(2,1)}, s32[1,128]{1,0:T(1,128)}, s32[1,128]{1,0:T(1,128)}, s32[1,128]{1,0:T(1,128)}, s32[1,128]{1,0:T(1,128)}, /*index=5*/s32[1,128]{1,0:T(1,128)}) custom-call(s32[1]{0:T(128)S(6)} %copy.10.count_ref, s32[1,128]{1,0:T(1,128)} %bitcast.2, s32[1,128]{1,0:T(1,128)} %bitcast.3, bf16[8,128,128]{2,1,0:T(8,128)(2,1)} %refs_4_.4), custom_call_target="tpu_custom_call" | custom-call | bytes 262144 | tf_op jit(solution)/shard_map/prepare/pallas_call | solution.py:90
  3.2 4.1 %collective-permute-start.4 = (bf16[4,128,128]{2,1,0:T(8,128)(2,1)}, bf16[4,128,128]{2,1,0:T(8,128)(2,1)S(1)}, u32[]{:S(2)}, u32[]{:S(2)}) collective-permute-start(bf16[4,128,128]{2,1,0:T(8,128)(2,1)} %get-tuple-element.56), channel_id=1, source_target_pairs={{0,8},{4,12},{8,0},{12,4},{1,9},{5,13},{9,1},{13,5},{2,10},{6,14},... | collective-permute-start | bytes 393224 | tf_op jit(solution)/shard_map/ppermute | solution.py:540
  7.3 1.6 %collective-permute-start.3 = (bf16[4,128,128]{2,1,0:T(8,128)(2,1)}, bf16[4,128,128]{2,1,0:T(8,128)(2,1)S(1)}, u32[]{:S(2)}, u32[]{:S(2)}) collective-permute-start(bf16[4,128,128]{2,1,0:T(8,128)(2,1)} %get-tuple-element.56), channel_id=1, source_target_pairs={{0,4},{4,0},{8,12},{12,8},{1,5},{5,1},{9,13},{13,9},{2,6},{6,2},{1... | collective-permute-start | bytes 393224 | tf_op jit(solution)/shard_map/ppermute | solution.py:540
  9.5 3.0 %operator.1.refs_5_.refs_6_.refs_7_.refs_3_ = bf16[1024,1024]{1,0:T(8,128)(2,1)S(1)} custom-call(s32[1,128]{1,0:T(1,128)S(1)} %copy-done.6, bf16[128,128,128]{2,1,0:T(8,128)(2,1)} %tiles_ref.1), custom_call_target="tpu_custom_call" | custom-call | bytes 16777216 | tf_op jit(solution)/shard_map/operator/pallas_call | solution.py:155
  13.5 2.5 %collective-permute-start.1 = (bf16[144,256]{1,0:T(8,128)(2,1)S(1)}, bf16[144,256]{1,0:T(8,128)(2,1)S(1)}, u32[]{:S(2)}, u32[]{:S(2)}) collective-permute-start(bf16[144,256]{1,0:T(8,128)(2,1)S(1)} %get-tuple-element.54), channel_id=1, source_target_pairs={{0,12},{4,8},{8,4},{12,0},{1,13},{5,9},{9,5},{13,1},{2,14},{6,10},... | collective-permute-start | bytes 221192 | tf_op jit(solution)/shard_map/ppermute | solution.py:540
  16.7 1.4 %collective-permute-start.5 = (bf16[2,128,128]{2,1,0:T(8,128)(2,1)S(1)}, bf16[2,128,128]{2,1,0:T(8,128)(2,1)S(1)}, u32[]{:S(2)}, u32[]{:S(2)}) collective-permute-start(bf16[2,128,128]{2,1,0:T(8,128)(2,1)S(1)} %get-tuple-element.60), channel_id=1, source_target_pairs={{0,4},{4,0},{8,12},{12,8},{1,5},{5,1},{9,13},{13,9},{2,6},{6,2},{1... | collective-permute-start | bytes 196616 | tf_op jit(solution)/shard_map/ppermute | solution.py:540
  18.8 2.1 %collective-permute-done.refs_2_ = bf16[144,256]{1,0:T(8,128)(2,1)S(1)} collective-permute-done((bf16[144,256]{1,0:T(8,128)(2,1)S(1)}, bf16[144,256]{1,0:T(8,128)(2,1)S(1)}, u32[]{:S(2)}, u32[]{:S(2)}) %collective-permute-start) | collective-permute-done | bytes 73760 | tf_op jit(solution)/shard_map/ppermute | solution.py:540
  20.9 1.4 %collective-permute-done.2.refs_1_ = bf16[144,256]{1,0:T(8,128)(2,1)S(1)} collective-permute-done((bf16[144,256]{1,0:T(8,128)(2,1)S(1)}, bf16[144,256]{1,0:T(8,128)(2,1)S(1)}, u32[]{:S(2)}, u32[]{:S(2)}) %collective-permute-start.2) | collective-permute-done | bytes 73760 | tf_op jit(solution)/shard_map/ppermute | solution.py:540
  22.2 1.2 %collective-permute-done.5.refs_2_ = bf16[2,128,128]{2,1,0:T(8,128)(2,1)S(1)} collective-permute-done((bf16[2,128,128]{2,1,0:T(8,128)(2,1)S(1)}, bf16[2,128,128]{2,1,0:T(8,128)(2,1)S(1)}, u32[]{:S(2)}, u32[]{:S(2)}) %collective-permute-start.5) | collective-permute-done | bytes 65568 | tf_op jit(solution)/shard_map/ppermute | solution.py:540
  23.5 0.7 %collective-permute-done.6.refs_3_ = bf16[2,128,128]{2,1,0:T(8,128)(2,1)S(1)} collective-permute-done((bf16[2,128,128]{2,1,0:T(8,128)(2,1)S(1)}, bf16[2,128,128]{2,1,0:T(8,128)(2,1)S(1)}, u32[]{:S(2)}, u32[]{:S(2)}) %collective-permute-start.6) | collective-permute-done | bytes 65568 | tf_op jit(solution)/shard_map/ppermute | solution.py:540
  24.7 1.3 %collective-permute-done.7.refs_5_ = bf16[12,128,128]{2,1,0:T(8,128)(2,1)S(1)} collective-permute-done((bf16[12,128,128]{2,1,0:T(8,128)(2,1)S(1)}, bf16[12,128,128]{2,1,0:T(8,128)(2,1)S(1)}, u32[]{:S(2)}, u32[]{:S(2)}) %collective-permute-start.7) | collective-permute-done | bytes 393248 | tf_op jit(solution)/shard_map/ppermute | solution.py:536
  26.0 0.8 %far_rows.1 = (bf16[4,128,128]{2,1,0:T(8,128)(2,1)S(1)}, f32[4,128,128]{2,1,0:T(8,128)S(1)}) custom-call(s32[1,128]{1,0:T(1,128)S(1)} %copy-done.3, s32[1,128]{1,0:T(1,128)S(1)} %copy-done.4, s32[1,128]{1,0:T(1,128)S(1)} %copy-done.5, f32[8,128,128]{2,1,0:T(8,128)S(1)} %get-tuple-element.69.refs_3_, bf16[12,128,128]{2,1,0:T(8,128)(2,1)S(1)} %stack.1.refs_4_, ...), custom_call_target="tpu_custom_call" | custom-call | flops 268435456 | bytes 2097152 | tf_op jit(solution)/shard_map/far_rows/pallas_call | solution.py:340
  27.0 1.5 %collective-permute-start.10 = (bf16[4,128,128]{2,1,0:T(8,128)(2,1)S(1)}, bf16[4,128,128]{2,1,0:T(8,128)(2,1)S(1)}, u32[]{:S(2)}, u32[]{:S(2)}) collective-permute-start(bf16[4,128,128]{2,1,0:T(8,128)(2,1)S(1)} %get-tuple-element.77.refs_2_), channel_id=1, source_target_pairs={{0,2},{2,0},{1,3},{3,1},{4,6},{6,4},{5,7},{7,5},{8,10},{10,8},{9,1... | collective-permute-start | bytes 393224 | tf_op jit(solution)/shard_map/ppermute | solution.py:536
  28.5 1.3 %collective-permute-start.9 = (bf16[4,128,128]{2,1,0:T(8,128)(2,1)S(1)}, bf16[4,128,128]{2,1,0:T(8,128)(2,1)S(1)}, u32[]{:S(2)}, u32[]{:S(2)}) collective-permute-start(bf16[4,128,128]{2,1,0:T(8,128)(2,1)S(1)} %add_up.1.refs_0_), channel_id=1, source_target_pairs={{0,2},{2,0},{1,3},{3,1},{4,6},{6,4},{5,7},{7,5},{8,10},{10,8},{9,1... | collective-permute-start | bytes 393224 | tf_op jit(solution)/shard_map/ppermute | solution.py:536
  29.8 3.5 %collective-permute-done.10.refs_3_ = bf16[4,128,128]{2,1,0:T(8,128)(2,1)S(1)} collective-permute-done((bf16[4,128,128]{2,1,0:T(8,128)(2,1)S(1)}, bf16[4,128,128]{2,1,0:T(8,128)(2,1)S(1)}, u32[]{:S(2)}, u32[]{:S(2)}) %collective-permute-start.10) | collective-permute-done | bytes 131104 | tf_op jit(solution)/shard_map/ppermute | solution.py:536
  33.3 2.2 %collective-permute-done.9.refs_1_ = bf16[4,128,128]{2,1,0:T(8,128)(2,1)S(1)} collective-permute-done((bf16[4,128,128]{2,1,0:T(8,128)(2,1)S(1)}, bf16[4,128,128]{2,1,0:T(8,128)(2,1)S(1)}, u32[]{:S(2)}, u32[]{:S(2)}) %collective-permute-start.9) | collective-permute-done | bytes 131104 | tf_op jit(solution)/shard_map/ppermute | solution.py:536
  36.3 1.6 %collective-permute-done.11.refs_4_.came_ref = bf16[128,1152]{1,0:T(8,128)(2,1)S(1)} collective-permute-done((bf16[128,1152]{1,0:T(8,128)(2,1)S(1)}, bf16[128,1152]{1,0:T(8,128)(2,1)S(1)}, u32[]{:S(2)}, u32[]{:S(2)}) %collective-permute-start.11) | collective-permute-done | bytes 294944 | tf_op jit(solution)/shard_map/ppermute | solution.py:536
  38.5 2.0 %collective-permute-start.13 = (bf16[128,512]{1,0:T(8,128)(2,1)S(1)}, bf16[128,512]{1,0:T(8,128)(2,1)S(1)}, u32[]{:S(2)}, u32[]{:S(2)}) collective-permute-start(bf16[128,512]{1,0:T(8,128)(2,1)S(1)} %get-tuple-element.84), channel_id=1, source_target_pairs={{0,4},{4,0},{8,12},{12,8},{1,5},{5,1},{9,13},{13,9},{2,6},{6,2},{1... | collective-permute-start | bytes 393224 | tf_op jit(solution)/shard_map/ppermute | solution.py:540
  40.5 2.3 %collective-permute-start.15 = (bf16[128,512]{1,0:T(8,128)(2,1)S(1)}, bf16[128,512]{1,0:T(8,128)(2,1)S(1)}, u32[]{:S(2)}, u32[]{:S(2)}) collective-permute-start(bf16[128,512]{1,0:T(8,128)(2,1)S(1)} %get-tuple-element.87), channel_id=1, source_target_pairs={{0,12},{4,8},{8,4},{12,0},{1,13},{5,9},{9,5},{13,1},{2,14},{6,10},... | collective-permute-start | bytes 393224 | tf_op jit(solution)/shard_map/ppermute | solution.py:540
  42.8 8.3 %collective-permute-done.12.refs_5_.came_ref = bf16[128,640]{1,0:T(8,128)(2,1)S(1)} collective-permute-done((bf16[128,640]{1,0:T(8,128)(2,1)S(1)}, bf16[128,640]{1,0:T(8,128)(2,1)S(1)}, u32[]{:S(2)}, u32[]{:S(2)}) %collective-permute-start.12) | collective-permute-done | bytes 163872 | tf_op jit(solution)/shard_map/ppermute | solution.py:540
  51.2 0.7 %late_rows.2.refs_0_ = f32[8,128,128]{2,1,0:T(8,128)S(1)} custom-call(s32[1,128]{1,0:T(1,128)S(1)} %copy-done.2, bf16[8,128,128]{2,1,0:T(8,128)(2,1)S(1)} %get-tuple-element.81.refs_1_, f32[128,256]{1,0:T(8,128)S(1)} %get-tuple-element.82.refs_2_, s32[1,128]{1,0:T(1,128)S(1)} %get-tuple-element.67.refs_1_.refs_3_, ...), custom_call_target="tpu_custom_call" | custom-call | flops 134217728 | bytes 1048576 | tf_op jit(solution)/shard_map/late_rows/pallas_call | solution.py:384
  52.0 3.2 %collective-permute-done.14.came_ref = bf16[128,128]{1,0:T(8,128)(2,1)S(1)} collective-permute-done((bf16[128,128]{1,0:T(8,128)(2,1)S(1)}, bf16[128,128]{1,0:T(8,128)(2,1)S(1)}, u32[]{:S(2)}, u32[]{:S(2)}) %collective-permute-start.14) | collective-permute-done | bytes 32800 | tf_op jit(solution)/shard_map/ppermute | solution.py:540
  56.1 1.1 %collective-permute-done.17.other_share_ref = f32[128,128]{1,0:T(8,128)S(1)} collective-permute-done((f32[128,128]{1,0:T(8,128)S(1)}, f32[128,128]{1,0:T(8,128)S(1)}, u32[]{:S(2)}, u32[]{:S(2)}) %collective-permute-start.17) | collective-permute-done | bytes 65568 | tf_op jit(solution)/shard_map/ppermute | solution.py:536
  57.2 1.0 %finish.1 = (bf16[8,128,128]{2,1,0:T(8,128)(2,1)}, f32[256,128]{1,0:T(8,128)}, bf16[8,128,128]{2,1,0:T(8,128)(2,1)}) custom-call(bf16[8,128,128]{2,1,0:T(8,128)(2,1)S(1)} %late_rows.3.mine_ref, bf16[8,128,128]{2,1,0:T(8,128)(2,1)S(1)} %collective-permute-done.16.other_ref, f32[128,128]{1,0:T(8,128)S(1)} %pair_sum.3.share_ref, ...), custom_call_target="tpu_custom_call" | custom-call | bytes 262144 | tf_op jit(solution)/shard_map/finish/pallas_call | solution.py:527
  (43 shorter events, 6.1 us)
Async XLA Ops:
  0.6 11.9 %copy-start = (bf16[8,128,128]{2,1,0:T(8,128)(2,1)S(1)}, bf16[8,128,128]{2,1,0:T(8,128)(2,1)}, u32[]{:S(2)}) copy-start(bf16[8,128,128]{2,1,0:T(8,128)(2,1)} %refs_4_.4) | copy-start | bytes 786436
  0.6 11.9 %copy-start.1 = (bf16[8,128,128]{2,1,0:T(8,128)(2,1)S(1)}, bf16[8,128,128]{2,1,0:T(8,128)(2,1)}, u32[]{:S(2)}) copy-start(bf16[8,128,128]{2,1,0:T(8,128)(2,1)} %refs_4_.3) | copy-start | bytes 786436
  3.2 9.4 %copy-start.4 = (s32[1,128]{1,0:T(1,128)S(1)}, s32[1,128]{1,0:T(1,128)}, u32[]{:S(2)}) copy-start(s32[1,128]{1,0:T(1,128)} %get-tuple-element.50.refs_1_) | copy-start | bytes 1540
  3.2 9.4 %copy-start.5 = (s32[1,128]{1,0:T(1,128)S(1)}, s32[1,128]{1,0:T(1,128)}, u32[]{:S(2)}) copy-start(s32[1,128]{1,0:T(1,128)} %get-tuple-element.51.refs_2_) | copy-start | bytes 1540
  3.2 13.5 %collective-permute-start.4 = (bf16[4,128,128]{2,1,0:T(8,128)(2,1)}, bf16[4,128,128]{2,1,0:T(8,128)(2,1)S(1)}, u32[]{:S(2)}, u32[]{:S(2)}) collective-permute-start(bf16[4,128,128]{2,1,0:T(8,128)(2,1)} %get-tuple-element.56), channel_id=1, source_target_pairs={{0,8},{4,12},{8,0},{12,4},{1,9},{5,13},{9,1},{13,5},{2,10},{6,14},... | collective-permute-start | bytes 393224 | tf_op jit(solution)/shard_map/ppermute | solution.py:540
  7.3 9.4 %collective-permute-start.3 = (bf16[4,128,128]{2,1,0:T(8,128)(2,1)}, bf16[4,128,128]{2,1,0:T(8,128)(2,1)S(1)}, u32[]{:S(2)}, u32[]{:S(2)}) collective-permute-start(bf16[4,128,128]{2,1,0:T(8,128)(2,1)} %get-tuple-element.56), channel_id=1, source_target_pairs={{0,4},{4,0},{8,12},{12,8},{1,5},{5,1},{9,13},{13,9},{2,6},{6,2},{1... | collective-permute-start | bytes 393224 | tf_op jit(solution)/shard_map/ppermute | solution.py:540
  9.5 14.7 %copy-start.2 = (s32[1,128]{1,0:T(1,128)S(1)}, s32[1,128]{1,0:T(1,128)}, u32[]{:S(2)}) copy-start(s32[1,128]{1,0:T(1,128)} %get-tuple-element.48.refs_0_) | copy-start | bytes 1540
  13.1 22.5 %copy-start.7 = (bf16[256,256]{1,0:T(8,128)(2,1)S(1)}, bf16[256,256]{1,0:T(8,128)(2,1)}, u32[]{:S(2)}) copy-start(bf16[256,256]{1,0:T(8,128)(2,1)} %refs_4_.5) | copy-start | bytes 393220
  13.1 7.7 %collective-permute-start = (bf16[144,256]{1,0:T(8,128)(2,1)S(1)}, bf16[144,256]{1,0:T(8,128)(2,1)S(1)}, u32[]{:S(2)}, u32[]{:S(2)}) collective-permute-start(bf16[144,256]{1,0:T(8,128)(2,1)S(1)} %get-tuple-element.53), channel_id=1, source_target_pairs={{0,8},{4,12},{8,0},{12,4},{1,9},{5,13},{9,1},{13,5},{2,10},{6,14},... | collective-permute-start | bytes 221192 | tf_op jit(solution)/shard_map/ppermute | solution.py:540
  13.5 7.4 %collective-permute-start.1 = (bf16[144,256]{1,0:T(8,128)(2,1)S(1)}, bf16[144,256]{1,0:T(8,128)(2,1)S(1)}, u32[]{:S(2)}, u32[]{:S(2)}) collective-permute-start(bf16[144,256]{1,0:T(8,128)(2,1)S(1)} %get-tuple-element.54), channel_id=1, source_target_pairs={{0,12},{4,8},{8,4},{12,0},{1,13},{5,9},{9,5},{13,1},{2,14},{6,10},... | collective-permute-start | bytes 221192 | tf_op jit(solution)/shard_map/ppermute | solution.py:540
  16.0 6.3 %collective-permute-start.2 = (bf16[144,256]{1,0:T(8,128)(2,1)S(1)}, bf16[144,256]{1,0:T(8,128)(2,1)S(1)}, u32[]{:S(2)}, u32[]{:S(2)}) collective-permute-start(bf16[144,256]{1,0:T(8,128)(2,1)S(1)} %get-tuple-element.55), channel_id=1, source_target_pairs={{0,4},{4,0},{8,12},{12,8},{1,5},{5,1},{9,13},{13,9},{2,6},{6,2},{1... | collective-permute-start | bytes 221192 | tf_op jit(solution)/shard_map/ppermute | solution.py:540
  16.7 6.8 %collective-permute-start.5 = (bf16[2,128,128]{2,1,0:T(8,128)(2,1)S(1)}, bf16[2,128,128]{2,1,0:T(8,128)(2,1)S(1)}, u32[]{:S(2)}, u32[]{:S(2)}) collective-permute-start(bf16[2,128,128]{2,1,0:T(8,128)(2,1)S(1)} %get-tuple-element.60), channel_id=1, source_target_pairs={{0,4},{4,0},{8,12},{12,8},{1,5},{5,1},{9,13},{13,9},{2,6},{6,2},{1... | collective-permute-start | bytes 196616 | tf_op jit(solution)/shard_map/ppermute | solution.py:540
  18.1 6.1 %collective-permute-start.6 = (bf16[2,128,128]{2,1,0:T(8,128)(2,1)S(1)}, bf16[2,128,128]{2,1,0:T(8,128)(2,1)S(1)}, u32[]{:S(2)}, u32[]{:S(2)}) collective-permute-start(bf16[2,128,128]{2,1,0:T(8,128)(2,1)S(1)} %get-tuple-element.61), channel_id=1, source_target_pairs={{0,4},{4,0},{8,12},{12,8},{1,5},{5,1},{9,13},{13,9},{2,6},{6,2},{1... | collective-permute-start | bytes 196616 | tf_op jit(solution)/shard_map/ppermute | solution.py:540
  24.2 1.8 %collective-permute-start.7 = (bf16[12,128,128]{2,1,0:T(8,128)(2,1)S(1)}, bf16[12,128,128]{2,1,0:T(8,128)(2,1)S(1)}, u32[]{:S(2)}, u32[]{:S(2)}) collective-permute-start(bf16[12,128,128]{2,1,0:T(8,128)(2,1)S(1)} %stack.1.refs_4_), channel_id=1, source_target_pairs={{0,1},{1,0},{2,3},{3,2},{4,5},{5,4},{6,7},{7,6},{8,9},{9,8},{10,11... | collective-permute-start | bytes 1179656 | tf_op jit(solution)/shard_map/ppermute | solution.py:536
  26.8 1.7 %collective-permute-start.8 = (bf16[4,128,128]{2,1,0:T(8,128)(2,1)S(1)}, bf16[4,128,128]{2,1,0:T(8,128)(2,1)S(1)}, u32[]{:S(2)}, u32[]{:S(2)}) collective-permute-start(bf16[4,128,128]{2,1,0:T(8,128)(2,1)S(1)} %get-tuple-element.75), channel_id=1, source_target_pairs={{0,1},{1,0},{2,3},{3,2},{4,5},{5,4},{6,7},{7,6},{8,9},{9,8},{10,11... | collective-permute-start | bytes 393224 | tf_op jit(solution)/shard_map/ppermute | solution.py:536
  27.0 6.3 %collective-permute-start.10 = (bf16[4,128,128]{2,1,0:T(8,128)(2,1)S(1)}, bf16[4,128,128]{2,1,0:T(8,128)(2,1)S(1)}, u32[]{:S(2)}, u32[]{:S(2)}) collective-permute-start(bf16[4,128,128]{2,1,0:T(8,128)(2,1)S(1)} %get-tuple-element.77.refs_2_), channel_id=1, source_target_pairs={{0,2},{2,0},{1,3},{3,1},{4,6},{6,4},{5,7},{7,5},{8,10},{10,8},{9,1... | collective-permute-start | bytes 393224 | tf_op jit(solution)/shard_map/ppermute | solution.py:536
  28.5 7.0 %collective-permute-start.9 = (bf16[4,128,128]{2,1,0:T(8,128)(2,1)S(1)}, bf16[4,128,128]{2,1,0:T(8,128)(2,1)S(1)}, u32[]{:S(2)}, u32[]{:S(2)}) collective-permute-start(bf16[4,128,128]{2,1,0:T(8,128)(2,1)S(1)} %add_up.1.refs_0_), channel_id=1, source_target_pairs={{0,2},{2,0},{1,3},{3,1},{4,6},{6,4},{5,7},{7,5},{8,10},{10,8},{9,1... | collective-permute-start | bytes 393224 | tf_op jit(solution)/shard_map/ppermute | solution.py:536
  36.3 1.6 %collective-permute-start.11 = (bf16[128,1152]{1,0:T(8,128)(2,1)S(1)}, bf16[128,1152]{1,0:T(8,128)(2,1)S(1)}, u32[]{:S(2)}, u32[]{:S(2)}) collective-permute-start(bf16[128,1152]{1,0:T(8,128)(2,1)S(1)} %get-tuple-element.79), channel_id=1, source_target_pairs={{0,1},{1,0},{2,3},{3,2},{4,5},{5,4},{6,7},{7,6},{8,9},{9,8},{10,11... | collective-permute-start | bytes 884744 | tf_op jit(solution)/shard_map/ppermute | solution.py:536
  38.4 12.8 %collective-permute-start.12 = (bf16[128,640]{1,0:T(8,128)(2,1)S(1)}, bf16[128,640]{1,0:T(8,128)(2,1)S(1)}, u32[]{:S(2)}, u32[]{:S(2)}) collective-permute-start(bf16[128,640]{1,0:T(8,128)(2,1)S(1)} %get-tuple-element.83), channel_id=1, source_target_pairs={{0,8},{4,12},{8,0},{12,4},{1,9},{5,13},{9,1},{13,5},{2,10},{6,14},... | collective-permute-start | bytes 491528 | tf_op jit(solution)/shard_map/ppermute | solution.py:540
  38.5 12.7 %collective-permute-start.13 = (bf16[128,512]{1,0:T(8,128)(2,1)S(1)}, bf16[128,512]{1,0:T(8,128)(2,1)S(1)}, u32[]{:S(2)}, u32[]{:S(2)}) collective-permute-start(bf16[128,512]{1,0:T(8,128)(2,1)S(1)} %get-tuple-element.84), channel_id=1, source_target_pairs={{0,4},{4,0},{8,12},{12,8},{1,5},{5,1},{9,13},{13,9},{2,6},{6,2},{1... | collective-permute-start | bytes 393224 | tf_op jit(solution)/shard_map/ppermute | solution.py:540
  40.5 14.6 %collective-permute-start.15 = (bf16[128,512]{1,0:T(8,128)(2,1)S(1)}, bf16[128,512]{1,0:T(8,128)(2,1)S(1)}, u32[]{:S(2)}, u32[]{:S(2)}) collective-permute-start(bf16[128,512]{1,0:T(8,128)(2,1)S(1)} %get-tuple-element.87), channel_id=1, source_target_pairs={{0,12},{4,8},{8,4},{12,0},{1,13},{5,9},{9,5},{13,1},{2,14},{6,10},... | collective-permute-start | bytes 393224 | tf_op jit(solution)/shard_map/ppermute | solution.py:540
  51.2 4.0 %collective-permute-start.14 = (bf16[128,128]{1,0:T(8,128)(2,1)S(1)}, bf16[128,128]{1,0:T(8,128)(2,1)S(1)}, u32[]{:S(2)}, u32[]{:S(2)}) collective-permute-start(bf16[128,128]{1,0:T(8,128)(2,1)S(1)} %pair_sum.2.mine_ref), channel_id=1, source_target_pairs={{0,4},{4,0},{8,12},{12,8},{1,5},{5,1},{9,13},{13,9},{2,6},{6,2},{1... | collective-permute-start | bytes 98312 | tf_op jit(solution)/shard_map/ppermute | solution.py:540
  55.5 1.7 %collective-permute-start.16 = (bf16[8,128,128]{2,1,0:T(8,128)(2,1)S(1)}, bf16[8,128,128]{2,1,0:T(8,128)(2,1)S(1)}, u32[]{:S(2)}, u32[]{:S(2)}) collective-permute-start(bf16[8,128,128]{2,1,0:T(8,128)(2,1)S(1)} %late_rows.3.mine_ref), channel_id=1, source_target_pairs={{0,1},{1,0},{2,3},{3,2},{4,5},{5,4},{6,7},{7,6},{8,9},{9,8},{10,11... | collective-permute-start | bytes 786440 | tf_op jit(solution)/shard_map/ppermute | solution.py:536
  55.6 1.6 %collective-permute-start.17 = (f32[128,128]{1,0:T(8,128)S(1)}, f32[128,128]{1,0:T(8,128)S(1)}, u32[]{:S(2)}, u32[]{:S(2)}) collective-permute-start(f32[128,128]{1,0:T(8,128)S(1)} %pair_sum.3.share_ref), channel_id=1, source_target_pairs={{0,1},{1,0},{2,3},{3,2},{4,5},{5,4},{6,7},{7,6},{8,9},{9,8},{10,11... | collective-permute-start | bytes 196616 | tf_op jit(solution)/shard_map/ppermute | solution.py:536
  (2 other events, 10.1 us)

commit v6 on v4

--- a/solution.py
+++ b/solution.py
@@ -198,7 +198,11 @@
         out = send_refs[k - 1]
         out[:columns, :] = mir[:, k * both : (k + 1) * both].astype(BF16)
         low, high = ask_refs[k - 1][:, :1], ask_refs[k - 1][:, 1:2]
-        out[columns:, :] = jnp.where(lane < width, low, high).astype(F32).astype(BF16)
+        out[columns : columns + TAIL, :] = jnp.where(lane < width, low, high).astype(F32).astype(BF16)
+    for b in range(share):
+        top = columns + TAIL + b // CAP * columns
+        left = b % CAP * width
+        send_refs[0][top : top + columns, left : left + width] = x3[half * share + b]
     cot_ref[...] = cot[pl.ds(half * share, share)]
 
 
@@ -208,7 +212,8 @@
     outs = call(
         functools.partial(first_sends_kernel, peers),
         "first_sends",
-        [shape((columns + TAIL, CAP * width), BF16)] * (peers - 1)
+        [shape((columns + TAIL + share // CAP * columns, CAP * width), BF16)]
+        + [shape((columns + TAIL, CAP * width), BF16)] * (peers - 2)
         + [shape((columns, CAP * width), F32), shape((share, columns, width), BF16)],
         [vmem()] * (peers + 2),
         [pltpu.VMEM((columns, peers * CAP * width), F32)],
@@ -268,7 +273,7 @@
         ids = jnp.zeros(lane.shape, jnp.int32)
         for s in range(CAP):
             here = slice(s * width, (s + 1) * width)
-            asked = jnp.max(came[columns:, here].astype(F32)).astype(jnp.int32)
+            asked = jnp.max(came[columns : columns + TAIL, here].astype(F32)).astype(jnp.int32)
             ids = jnp.where(lane == s, asked, ids)
             add_sums(acc, asked, came[:columns, here])
         ids_refs[k - 1][...] = ids
@@ -287,11 +292,17 @@
     return outs[0], [None] + list(outs[1:])
 
 
-def stack_kernel(*refs):
-    at = 0
+def stack_kernel(below_ref, *refs):
+    out_ref = refs[-1]
+    _, columns, width = out_ref.shape
+    at = (below_ref.shape[0] - TAIL) // columns * CAP - CAP
+    for b in range(at):
+        top = columns + TAIL + b // CAP * columns
+        left = b % CAP * width
+        out_ref[b] = below_ref[top : top + columns, left : left + width]
     for ref in refs[:-1]:
         share = ref.shape[0]
-        refs[-1][at : at + share] = ref[...]
+        out_ref[at : at + share] = ref[...]
         at += share
 
 
@@ -309,10 +320,11 @@
     return list(call(halves_kernel, "halves", [part, part], [vmem()])(*parts))
 
 
-def stack(pieces):
+def stack(below, pieces):
     _, columns, width = pieces[0].shape
-    out = shape((sum(piece.shape[0] for piece in pieces), columns, width), BF16)
-    return call(stack_kernel, "stack", out, [vmem()] * len(pieces))(*pieces)
+    count = (below.shape[0] - TAIL) // columns * CAP - CAP + sum(piece.shape[0] for piece in pieces)
+    out = shape((count, columns, width), BF16)
+    return call(stack_kernel, "stack", out, [vmem()] * (len(pieces) + 1))(below, *pieces)
 
 
 def far_rows_kernel(peers, *refs):
@@ -400,9 +412,26 @@
     return call(add_kernel, "add_up", shape(came.shape, BF16), [vmem(), vmem()])(keep, came)
 
 
+def widen_kernel(feats, *refs):
+    out_ref = refs[feats]
+    share, columns, width = refs[0].shape
+    me = lax.axis_index("feat")
+    for q in range(feats):
+        rows = pl.ds(pl.multiple_of(lax.rem(me + q, feats) * columns, columns), columns)
+        for b in range(share):
+            out_ref[rows, b * width : (b + 1) * width] = refs[q][b]
+
+
+def widen(parts):
+    share, columns, width = parts[0].shape
+    out = shape((len(parts) * columns, share * width), BF16)
+    kernel = functools.partial(widen_kernel, len(parts))
+    return call(kernel, "widen", out, [vmem()] * len(parts))(*parts)
+
+
 def dense_kernel(feats, *refs):
-    sums, cots, refs = refs[:feats], refs[feats : 2 * feats], refs[2 * feats :]
-    w_ref, act_ref, give_ref, spread_ref, keep_ref, wide, wide_cot, pre_scr, grad, term = refs
+    sums, wide_cot, refs = refs[:feats], refs[feats], refs[feats + 1 :]
+    w_ref, act_ref, give_ref, spread_ref, keep_ref, wide, pre_scr, grad, term = refs
     share, columns, width = act_ref.shape
     me = lax.axis_index("feat")
     half = lax.axis_index("rep")
@@ -410,7 +439,6 @@
     for q in range(feats):
         for b in range(share):
             wide[rows[q], b * width : (b + 1) * width] = sums[q][b]
-            wide_cot[rows[q], b * width : (b + 1) * width] = cots[q][b]
     pre = dot(w_ref[...], wide[...], TN)
     pre_scr[...] = pre
     sig = jax.nn.sigmoid(pre)
@@ -432,7 +460,7 @@
         act_ref[b] = act[:, b * width : (b + 1) * width]
 
 
-def dense(sums, cots, weight, feats, reps):
+def dense(sums, cot, weight, feats, reps):
     share, columns, width = sums[0].shape
     features = weight.shape[0]
     part = features // reps
@@ -445,9 +473,8 @@
             shape((share, columns, width), BF16),
             shape((columns, part), F32),
         ],
-        [vmem()] * (2 * feats + 1),
+        [vmem()] * (feats + 2),
         [
-            pltpu.VMEM((features, share * width), BF16),
             pltpu.VMEM((features, share * width), BF16),
             pltpu.VMEM((features, share * width), F32),
             pltpu.VMEM((features, share * width), BF16),
@@ -455,7 +482,7 @@
         ],
         flops=2 ** 28,
         moved=2 ** 20,
-    )(*sums, *cots, weight)
+    )(*sums, cot, weight)
 
 
 def send_kernel(peers, *refs):
@@ -480,6 +507,7 @@
         for s in range(CAP):
             at = (CAP + s) * width
             out[:, at : at + width] = x3[pick(ids_refs[k - 1], s)]
+        out[:, 2 * both :] = term
 
 
 def sends_of(mine, came, keep, operator, ids, peers, reps):
@@ -489,7 +517,7 @@
         functools.partial(send_kernel, peers),
         "sends",
         [shape((share * reps, columns, width), BF16)]
-        + [shape((columns, chunk), BF16)] * (peers - 1)
+        + [shape((columns, chunk + keep.shape[1]), BF16)] * (peers - 1)
         + [shape((columns, CAP * width), F32), shape(keep.shape, BF16)],
         [vmem()] * (peers + 3),
         [pltpu.VMEM((columns, peers * CAP * width), F32)],
@@ -499,12 +527,27 @@
     return outs[0], [None] + list(outs[1:peers]), outs[peers], outs[peers + 1]
 
 
-def pair_kernel(mine_ref, came_ref, out_ref):
-    out_ref[...] = (mine_ref[...].astype(F32) + came_ref[...].astype(F32)).astype(out_ref.dtype)
-
-
-def pair_sum(mine, came, dtype):
-    return call(pair_kernel, "pair_sum", shape(mine.shape, dtype), [vmem(), vmem()])(mine, came)
+def terms_kernel(peers, at, *refs):
+    out_ref, terms = refs[peers], refs[peers + 1]
+    me = lax.axis_index("graph")
+    terms[0] = refs[0][...].astype(F32)
+    for k in range(1, peers):
+        terms[k] = refs[k][:, at:].astype(F32)
+    total = terms[me]
+    for p in range(1, peers):
+        total = total + terms[jnp.bitwise_xor(me, p)]
+    out_ref[...] = total
+
+
+def sum_terms(term, came, at):
+    peers = len(came)
+    return call(
+        functools.partial(terms_kernel, peers, at),
+        "terms",
+        shape(term.shape, F32),
+        [vmem()] * peers,
+        [pltpu.VMEM((peers,) + term.shape, F32)],
+    )(term, *came[1:])
 
 
 def finish_kernel(mine_ref, other_ref, share_ref, other_share_ref, act_ref, came_ref, grad_ref, weight_ref, out_ref):
@@ -556,19 +599,20 @@
     bit = peers // 2
     while bit:
         for k in held:
-            parts = pieces[k]
-            if k:
-                parts = after(halves(after(parts, sends[1])), pieces.get(1, half))
+            if k ^ bit == 1:
+                continue
+            parts = halves(after(pieces[k], sends[1])) if k else pieces[k]
             pieces[k ^ bit] = [across(part, peers, bit) for part in parts]
         held = held + [k ^ bit for k in held]
         bit //= 2
     came = [None] * peers
     for k in far_first:
-        came[k] = across(sends[k], peers, k)
-    arrived = [part for k in range(1, peers) for part in pieces[k]]
+        send = after(sends[k], pieces[peers // 2]) if k == peers - 1 else sends[k]
+        came[k] = across(send, peers, k)
+    arrived = [part for k in range(2, peers) for part in pieces[k]]
     ordered, arrived = lax.optimization_barrier(([came[k] for k in far_first], arrived))
     came = [None] + [ordered[far_first.index(k)] for k in range(1, peers)]
-    stacked = stack(arrived)
+    stacked = stack(came[1], arrived)
     swapped = ahead(stacked, "rep", reps, 1)
     cots = [own_cot]
     if feats > 1:
@@ -577,23 +621,20 @@
     acc, ids = first_rows(features, operator, asks[0], came, own_mirror, peers)
     give, keep = far_rows(acc, asks, stacked, swapped, operator, peers, reps)
 
-    given, cots = lax.optimization_barrier((ahead(give, "rep", reps, 1), cots))
-    mine = add_up(keep, given)
+    mine = add_up(keep, ahead(give, "rep", reps, 1))
+    cot = widen(cots)
     sums = [mine] + [ahead(mine, "feat", feats, feats - q) for q in range(1, feats)]
-    act, give, spread, keep = dense(sums, cots, weight, feats, reps)
+    act, give, spread, keep = dense(sums, cot, weight, feats, reps)
     shared = ahead(give, "rep", reps, 1)
     values, sends, own_mirror, term = sends_of(spread, shared, keep, operator, ids, peers, reps)
 
     came = [None] * peers
     for k in far_first:
         came[k] = across(sends[k], peers, k)
-    total, bit = term, 1
-    while bit < peers:
-        total = pair_sum(total, across(total, peers, bit), F32 if 2 * bit == peers else BF16)
-        bit *= 2
-    ordered, total = lax.optimization_barrier(([came[k] for k in far_first], total))
+    ordered = lax.optimization_barrier([came[k] for k in far_first])
     came = [None] + [ordered[far_first.index(k)] for k in range(1, peers)]
     part = late_rows([asks[0], values, own_mirror], ids, came, far_first, operator, True, True)
+    total = sum_terms(term, came, 2 * CAP * width)
     input_grad, weight_grad, activated = finish(
         part, ahead(part, "rep", reps, 1), total, ahead(total, "rep", reps, 1), act, shared
     )

time: 60.2 us -> 58 us (0.963)
  waiting for transfers between devices: 28.4 us -> 25.8 us
    ppermute x12 -> x9, waiting for transfers between devices: 19.3 us -> 16.3 us  [across(): return lax.ppermute(value, 'graph', [(i, i ^ k) for i in range(peers)])]
    ppermute x12 -> x9, starting transfers between devices: 15.7 us -> 16.1 us  [across(): return lax.ppermute(value, 'graph', [(i, i ^ k) for i in range(peers)])]
  transfers between devices with their start and end apart: 19 -> 16, of which waited for: 10 -> 11; matrix products, arithmetic and copies ran while one was open for 0% -> 0% of each run, Pallas kernels for 8% -> 7%
where the time goes in v6:
time: 58 us; the launch traced here: 57.6 us
  waiting for transfers between devices  25.8 us (44%)
  starting transfers between devices  19.9 us (34%)
  Pallas kernels  9.75 us (17%)
  between operations  1.52 us (3%)
  local copies, waits for them, and re-layouts  0.68 us (1%)
    ppermute x9, waiting for transfers between devices, across(): return lax.ppermute(value, 'graph', [(i, i ^ k) for i in range(peers)])  16.3 us
    ppermute x9, starting transfers between devices, across(): return lax.ppermute(value, 'graph', [(i, i ^ k) for i in range(peers)])  16.1 us
    ppermute x7, waiting for transfers between devices, ahead(): return lax.ppermute(value, axis, [(i, (i + k) % size) for i in range(size)])  9.55 us
    ppermute x7, starting transfers between devices, ahead(): return lax.ppermute(value, axis, [(i, (i + k) % size) for i in range(size)])  3.79 us
    pallas_call x1, Pallas kernels, list_operator(): call(functools.partial(operator_kernel, blocks_dev, slots_here, groups),...  3.04 us
    pallas_call x1, Pallas kernels, prepare(): call(functools.partial(prepare_kernel, peers), 'prepare', [shape((blocks_...  1.82 us
  transfers between devices with their start and end apart: 16, of which 11 were waited for; matrix products, arithmetic and copies ran while one was open for 0% of the time, Pallas kernels for 7%

profile of v6, /device:TPU:0, one launch (start us, length us, event | category | flops | bytes accessed | tf_op | source)
XLA Modules:
  0.0 57.6 jit_solution(9162962467324146300)
XLA Ops:
  1.4 1.8 %prepare.1 = (bf16[4,128,128]{2,1,0:T(8,128)(2,1)}, s32[1,128]{1,0:T(1,128)}, s32[1,128]{1,0:T(1,128)}, s32[1,128]{1,0:T(1,128)}, s32[1,128]{1,0:T(1,128)}, /*index=5*/s32[1,128]{1,0:T(1,128)}) custom-call(s32[1]{0:T(128)S(6)} %copy.10.count_ref, s32[1,128]{1,0:T(1,128)} %bitcast.2, s32[1,128]{1,0:T(1,128)} %bitcast.3, bf16[8,128,128]{2,1,0:T(8,128)(2,1)} %refs_4_.3), custom_call_target="tpu_custom_call" | custom-call | bytes 262144 | tf_op jit(solution)/shard_map/prepare/pallas_call | solution.py:90
  3.2 4.1 %collective-permute-start.1 = (bf16[4,128,128]{2,1,0:T(8,128)(2,1)}, bf16[4,128,128]{2,1,0:T(8,128)(2,1)S(1)}, u32[]{:S(2)}, u32[]{:S(2)}) collective-permute-start(bf16[4,128,128]{2,1,0:T(8,128)(2,1)} %get-tuple-element.54), channel_id=1, source_target_pairs={{0,8},{4,12},{8,0},{12,4},{1,9},{5,13},{9,1},{13,5},{2,10},{6,14},... | collective-permute-start | bytes 393224 | tf_op jit(solution)/shard_map/ppermute | solution.py:581
  7.3 0.7 %copy-done.6 = s32[1,128]{1,0:T(1,128)S(1)} copy-done((s32[1,128]{1,0:T(1,128)S(1)}, s32[1,128]{1,0:T(1,128)}, u32[]{:S(2)}) %copy-start.6) | copy-done | bytes 536
  7.9 3.0 %operator.1.refs_5_.refs_6_.refs_9_ = bf16[1024,1024]{1,0:T(8,128)(2,1)S(1)} custom-call(s32[1,128]{1,0:T(1,128)S(1)} %copy-done.6, bf16[128,128,128]{2,1,0:T(8,128)(2,1)} %tiles_ref.1), custom_call_target="tpu_custom_call" | custom-call | bytes 16777216 | tf_op jit(solution)/shard_map/operator/pallas_call | solution.py:155
  11.5 1.6 %collective-permute-start.3 = (bf16[400,256]{1,0:T(8,128)(2,1)S(1)}, bf16[400,256]{1,0:T(8,128)(2,1)S(1)}, u32[]{:S(2)}, u32[]{:S(2)}) collective-permute-start(bf16[400,256]{1,0:T(8,128)(2,1)S(1)} %get-tuple-element.56), channel_id=1, source_target_pairs={{0,4},{4,0},{8,12},{12,8},{1,5},{5,1},{9,13},{13,9},{2,6},{6,2},{1... | collective-permute-start | bytes 614408 | tf_op jit(solution)/shard_map/ppermute | solution.py:581
  13.8 3.7 %collective-permute-start.2 = (bf16[144,256]{1,0:T(8,128)(2,1)S(1)}, bf16[144,256]{1,0:T(8,128)(2,1)S(1)}, u32[]{:S(2)}, u32[]{:S(2)}) collective-permute-start(bf16[144,256]{1,0:T(8,128)(2,1)S(1)} %get-tuple-element.55), channel_id=1, source_target_pairs={{0,12},{4,8},{8,4},{12,0},{1,13},{5,9},{9,5},{13,1},{2,14},{6,10},... | collective-permute-start | bytes 221192 | tf_op jit(solution)/shard_map/ppermute | solution.py:581
  17.6 2.0 %collective-permute-start.5 = (bf16[2,128,128]{2,1,0:T(8,128)(2,1)S(1)}, bf16[2,128,128]{2,1,0:T(8,128)(2,1)S(1)}, u32[]{:S(2)}, u32[]{:S(2)}) collective-permute-start(bf16[2,128,128]{2,1,0:T(8,128)(2,1)S(1)} %get-tuple-element.59), channel_id=1, source_target_pairs={{0,4},{4,0},{8,12},{12,8},{1,5},{5,1},{9,13},{13,9},{2,6},{6,2},{1... | collective-permute-start | bytes 196616 | tf_op jit(solution)/shard_map/ppermute | solution.py:581
  19.6 1.1 %collective-permute-done.refs_2_ = bf16[144,256]{1,0:T(8,128)(2,1)S(1)} collective-permute-done((bf16[144,256]{1,0:T(8,128)(2,1)S(1)}, bf16[144,256]{1,0:T(8,128)(2,1)S(1)}, u32[]{:S(2)}, u32[]{:S(2)}) %collective-permute-start) | collective-permute-done | bytes 73760 | tf_op jit(solution)/shard_map/ppermute | solution.py:581
  20.8 2.3 %collective-permute-done.4.refs_1_ = bf16[2,128,128]{2,1,0:T(8,128)(2,1)S(1)} collective-permute-done((bf16[2,128,128]{2,1,0:T(8,128)(2,1)S(1)}, bf16[2,128,128]{2,1,0:T(8,128)(2,1)S(1)}, u32[]{:S(2)}, u32[]{:S(2)}) %collective-permute-start.4) | collective-permute-done | bytes 65568 | tf_op jit(solution)/shard_map/ppermute | solution.py:581
  23.1 1.1 %collective-permute-done.5.refs_2_ = bf16[2,128,128]{2,1,0:T(8,128)(2,1)S(1)} collective-permute-done((bf16[2,128,128]{2,1,0:T(8,128)(2,1)S(1)}, bf16[2,128,128]{2,1,0:T(8,128)(2,1)S(1)}, u32[]{:S(2)}, u32[]{:S(2)}) %collective-permute-start.5) | collective-permute-done | bytes 65568 | tf_op jit(solution)/shard_map/ppermute | solution.py:581
  24.7 1.3 %collective-permute-done.6.refs_5_ = bf16[12,128,128]{2,1,0:T(8,128)(2,1)S(1)} collective-permute-done((bf16[12,128,128]{2,1,0:T(8,128)(2,1)S(1)}, bf16[12,128,128]{2,1,0:T(8,128)(2,1)S(1)}, u32[]{:S(2)}, u32[]{:S(2)}) %collective-permute-start.6) | collective-permute-done | bytes 393248 | tf_op jit(solution)/shard_map/ppermute | solution.py:577
  26.0 0.8 %far_rows.1 = (bf16[4,128,128]{2,1,0:T(8,128)(2,1)S(1)}, f32[4,128,128]{2,1,0:T(8,128)S(1)}) custom-call(s32[1,128]{1,0:T(1,128)S(1)} %copy-done.3, s32[1,128]{1,0:T(1,128)S(1)} %copy-done.4, s32[1,128]{1,0:T(1,128)S(1)} %copy-done.5, f32[8,128,128]{2,1,0:T(8,128)S(1)} %get-tuple-element.67.refs_3_, bf16[12,128,128]{2,1,0:T(8,128)(2,1)S(1)} %stack.1.refs_4_, ...), custom_call_target="tpu_custom_call" | custom-call | flops 268435456 | bytes 2097152 | tf_op jit(solution)/shard_map/far_rows/pallas_call | solution.py:352
  27.0 1.6 %collective-permute-start.9 = (bf16[4,128,128]{2,1,0:T(8,128)(2,1)S(1)}, bf16[4,128,128]{2,1,0:T(8,128)(2,1)S(1)}, u32[]{:S(2)}, u32[]{:S(2)}) collective-permute-start(bf16[4,128,128]{2,1,0:T(8,128)(2,1)S(1)} %get-tuple-element.74.refs_0_), channel_id=1, source_target_pairs={{0,2},{2,0},{1,3},{3,1},{4,6},{6,4},{5,7},{7,5},{8,10},{10,8},{9,1... | collective-permute-start | bytes 393224 | tf_op jit(solution)/shard_map/ppermute | solution.py:577
  28.6 1.3 %collective-permute-start.8 = (bf16[4,128,128]{2,1,0:T(8,128)(2,1)S(1)}, bf16[4,128,128]{2,1,0:T(8,128)(2,1)S(1)}, u32[]{:S(2)}, u32[]{:S(2)}) collective-permute-start(bf16[4,128,128]{2,1,0:T(8,128)(2,1)S(1)} %add_up.1.refs_0_), channel_id=1, source_target_pairs={{0,2},{2,0},{1,3},{3,1},{4,6},{6,4},{5,7},{7,5},{8,10},{10,8},{9,1... | collective-permute-start | bytes 393224 | tf_op jit(solution)/shard_map/ppermute | solution.py:577
  29.9 3.5 %collective-permute-done.9.refs_1_ = bf16[4,128,128]{2,1,0:T(8,128)(2,1)S(1)} collective-permute-done((bf16[4,128,128]{2,1,0:T(8,128)(2,1)S(1)}, bf16[4,128,128]{2,1,0:T(8,128)(2,1)S(1)}, u32[]{:S(2)}, u32[]{:S(2)}) %collective-permute-start.9) | collective-permute-done | bytes 131104 | tf_op jit(solution)/shard_map/ppermute | solution.py:577
  33.4 2.2 %collective-permute-done.8.refs_1_ = bf16[4,128,128]{2,1,0:T(8,128)(2,1)S(1)} collective-permute-done((bf16[4,128,128]{2,1,0:T(8,128)(2,1)S(1)}, bf16[4,128,128]{2,1,0:T(8,128)(2,1)S(1)}, u32[]{:S(2)}, u32[]{:S(2)}) %collective-permute-start.8) | collective-permute-done | bytes 131104 | tf_op jit(solution)/shard_map/ppermute | solution.py:577
  35.6 0.7 %dense.1 = (bf16[4,128,128]{2,1,0:T(8,128)(2,1)S(1)}, bf16[128,1152]{1,0:T(8,128)(2,1)S(1)}, bf16[4,128,128]{2,1,0:T(8,128)(2,1)S(1)}, f32[128,128]{1,0:T(8,128)S(1)}) custom-call(bf16[4,128,128]{2,1,0:T(8,128)(2,1)S(1)} %add_up.1.refs_0_, bf16[4,128,128]{2,1,0:T(8,128)(2,1)S(1)} %collective-permute-done.8.refs_1_, bf16[256,512]{1,0:T(8,128)(2,1)S(1)} %widen.1.refs_2_, ...), custom_call_target="tpu_custom_call" | custom-call | flops 268435456 | bytes 1048576 | tf_op jit(solution)/shard_map/dense/pallas_call | solution.py:467
  36.4 1.6 %collective-permute-done.10.refs_4_.came_ref = bf16[128,1152]{1,0:T(8,128)(2,1)S(1)} collective-permute-done((bf16[128,1152]{1,0:T(8,128)(2,1)S(1)}, bf16[128,1152]{1,0:T(8,128)(2,1)S(1)}, u32[]{:S(2)}, u32[]{:S(2)}) %collective-permute-start.10) | collective-permute-done | bytes 294944 | tf_op jit(solution)/shard_map/ppermute | solution.py:577
  38.4 1.7 %collective-permute-start.11 = (bf16[128,640]{1,0:T(8,128)(2,1)S(1)}, bf16[128,640]{1,0:T(8,128)(2,1)S(1)}, u32[]{:S(2)}, u32[]{:S(2)}) collective-permute-start(bf16[128,640]{1,0:T(8,128)(2,1)S(1)} %get-tuple-element.80), channel_id=1, source_target_pairs={{0,8},{4,12},{8,0},{12,4},{1,9},{5,13},{9,1},{13,5},{2,10},{6,14},... | collective-permute-start | bytes 491528 | tf_op jit(solution)/shard_map/ppermute | solution.py:581
  40.1 2.3 %collective-permute-start.12 = (bf16[128,640]{1,0:T(8,128)(2,1)S(1)}, bf16[128,640]{1,0:T(8,128)(2,1)S(1)}, u32[]{:S(2)}, u32[]{:S(2)}) collective-permute-start(bf16[128,640]{1,0:T(8,128)(2,1)S(1)} %get-tuple-element.81), channel_id=1, source_target_pairs={{0,12},{4,8},{8,4},{12,0},{1,13},{5,9},{9,5},{13,1},{2,14},{6,10},... | collective-permute-start | bytes 491528 | tf_op jit(solution)/shard_map/ppermute | solution.py:581
  42.6 10.9 %collective-permute-done.11.refs_6_.refs_2_ = bf16[128,640]{1,0:T(8,128)(2,1)S(1)} collective-permute-done((bf16[128,640]{1,0:T(8,128)(2,1)S(1)}, bf16[128,640]{1,0:T(8,128)(2,1)S(1)}, u32[]{:S(2)}, u32[]{:S(2)}) %collective-permute-start.11) | collective-permute-done | bytes 163872 | tf_op jit(solution)/shard_map/ppermute | solution.py:581
  54.0 0.9 %late_rows.1.mine_ref = bf16[8,128,128]{2,1,0:T(8,128)(2,1)S(1)} custom-call(s32[1,128]{1,0:T(1,128)S(1)} %copy-done.2, bf16[8,128,128]{2,1,0:T(8,128)(2,1)S(1)} %get-tuple-element.78.refs_1_, f32[128,256]{1,0:T(8,128)S(1)} %get-tuple-element.79.refs_2_, s32[1,128]{1,0:T(1,128)S(1)} %get-tuple-element.65.refs_1_.refs_3_, ...), custom_call_target="tpu_custom_call" | custom-call | flops 134217728 | bytes 1048576 | tf_op jit(solution)/shard_map/late_rows/pallas_call | solution.py:396
  55.6 1.0 %collective-permute-done.15.other_share_ref = f32[128,128]{1,0:T(8,128)S(1)} collective-permute-done((f32[128,128]{1,0:T(8,128)S(1)}, f32[128,128]{1,0:T(8,128)S(1)}, u32[]{:S(2)}, u32[]{:S(2)}) %collective-permute-start.15) | collective-permute-done | bytes 65568 | tf_op jit(solution)/shard_map/ppermute | solution.py:577
  56.6 1.0 %finish.1 = (bf16[8,128,128]{2,1,0:T(8,128)(2,1)}, f32[256,128]{1,0:T(8,128)}, bf16[8,128,128]{2,1,0:T(8,128)(2,1)}) custom-call(bf16[8,128,128]{2,1,0:T(8,128)(2,1)S(1)} %late_rows.1.mine_ref, bf16[8,128,128]{2,1,0:T(8,128)(2,1)S(1)} %collective-permute-done.14.other_ref, f32[128,128]{1,0:T(8,128)S(1)} %terms.1.share_ref, ...), custom_call_target="tpu_custom_call" | custom-call | bytes 262144 | tf_op jit(solution)/shard_map/finish/pallas_call | solution.py:568
  (38 shorter events, 4.0 us)
Async XLA Ops:
  0.6 10.4 %copy-start = (bf16[8,128,128]{2,1,0:T(8,128)(2,1)S(1)}, bf16[8,128,128]{2,1,0:T(8,128)(2,1)}, u32[]{:S(2)}) copy-start(bf16[8,128,128]{2,1,0:T(8,128)(2,1)} %refs_4_.3) | copy-start | bytes 786436
  0.6 10.4 %copy-start.1 = (bf16[8,128,128]{2,1,0:T(8,128)(2,1)S(1)}, bf16[8,128,128]{2,1,0:T(8,128)(2,1)}, u32[]{:S(2)}) copy-start(bf16[8,128,128]{2,1,0:T(8,128)(2,1)} %refs_4_.2) | copy-start | bytes 786436
  3.2 7.8 %copy-start.3 = (s32[1,128]{1,0:T(1,128)S(1)}, s32[1,128]{1,0:T(1,128)}, u32[]{:S(2)}) copy-start(s32[1,128]{1,0:T(1,128)} %get-tuple-element.48.refs_0_) | copy-start | bytes 1540
  3.2 7.9 %copy-start.4 = (s32[1,128]{1,0:T(1,128)S(1)}, s32[1,128]{1,0:T(1,128)}, u32[]{:S(2)}) copy-start(s32[1,128]{1,0:T(1,128)} %get-tuple-element.49.refs_1_) | copy-start | bytes 1540
  3.2 7.9 %copy-start.5 = (s32[1,128]{1,0:T(1,128)S(1)}, s32[1,128]{1,0:T(1,128)}, u32[]{:S(2)}) copy-start(s32[1,128]{1,0:T(1,128)} %get-tuple-element.50.refs_2_) | copy-start | bytes 1540
  3.2 10.6 %collective-permute-start.1 = (bf16[4,128,128]{2,1,0:T(8,128)(2,1)}, bf16[4,128,128]{2,1,0:T(8,128)(2,1)S(1)}, u32[]{:S(2)}, u32[]{:S(2)}) collective-permute-start(bf16[4,128,128]{2,1,0:T(8,128)(2,1)} %get-tuple-element.54), channel_id=1, source_target_pairs={{0,8},{4,12},{8,0},{12,4},{1,9},{5,13},{9,1},{13,5},{2,10},{6,14},... | collective-permute-start | bytes 393224 | tf_op jit(solution)/shard_map/ppermute | solution.py:581
  7.3 0.7 %copy-start.6 = (s32[1,128]{1,0:T(1,128)S(1)}, s32[1,128]{1,0:T(1,128)}, u32[]{:S(2)}) copy-start(s32[1,128]{1,0:T(1,128)} %get-tuple-element.51.place_in) | copy-start | bytes 1540
  7.9 16.4 %copy-start.2 = (s32[1,128]{1,0:T(1,128)S(1)}, s32[1,128]{1,0:T(1,128)}, u32[]{:S(2)}) copy-start(s32[1,128]{1,0:T(1,128)} %get-tuple-element.47.refs_0_) | copy-start | bytes 1540
  11.5 24.1 %copy-start.7 = (bf16[256,256]{1,0:T(8,128)(2,1)S(1)}, bf16[256,256]{1,0:T(8,128)(2,1)}, u32[]{:S(2)}) copy-start(bf16[256,256]{1,0:T(8,128)(2,1)} %refs_3_.3) | copy-start | bytes 393220
  11.5 12.6 %collective-permute-start.3 = (bf16[400,256]{1,0:T(8,128)(2,1)S(1)}, bf16[400,256]{1,0:T(8,128)(2,1)S(1)}, u32[]{:S(2)}, u32[]{:S(2)}) collective-permute-start(bf16[400,256]{1,0:T(8,128)(2,1)S(1)} %get-tuple-element.56), channel_id=1, source_target_pairs={{0,4},{4,0},{8,12},{12,8},{1,5},{5,1},{9,13},{13,9},{2,6},{6,2},{1... | collective-permute-start | bytes 614408 | tf_op jit(solution)/shard_map/ppermute | solution.py:581
  13.2 7.6 %collective-permute-start = (bf16[144,256]{1,0:T(8,128)(2,1)S(1)}, bf16[144,256]{1,0:T(8,128)(2,1)S(1)}, u32[]{:S(2)}, u32[]{:S(2)}) collective-permute-start(bf16[144,256]{1,0:T(8,128)(2,1)S(1)} %get-tuple-element.52), channel_id=1, source_target_pairs={{0,8},{4,12},{8,0},{12,4},{1,9},{5,13},{9,1},{13,5},{2,10},{6,14},... | collective-permute-start | bytes 221192 | tf_op jit(solution)/shard_map/ppermute | solution.py:581
  13.8 10.4 %collective-permute-start.2 = (bf16[144,256]{1,0:T(8,128)(2,1)S(1)}, bf16[144,256]{1,0:T(8,128)(2,1)S(1)}, u32[]{:S(2)}, u32[]{:S(2)}) collective-permute-start(bf16[144,256]{1,0:T(8,128)(2,1)S(1)} %get-tuple-element.55), channel_id=1, source_target_pairs={{0,12},{4,8},{8,4},{12,0},{1,13},{5,9},{9,5},{13,1},{2,14},{6,10},... | collective-permute-start | bytes 221192 | tf_op jit(solution)/shard_map/ppermute | solution.py:581
  17.5 5.5 %collective-permute-start.4 = (bf16[2,128,128]{2,1,0:T(8,128)(2,1)S(1)}, bf16[2,128,128]{2,1,0:T(8,128)(2,1)S(1)}, u32[]{:S(2)}, u32[]{:S(2)}) collective-permute-start(bf16[2,128,128]{2,1,0:T(8,128)(2,1)S(1)} %get-tuple-element.58), channel_id=1, source_target_pairs={{0,4},{4,0},{8,12},{12,8},{1,5},{5,1},{9,13},{13,9},{2,6},{6,2},{1... | collective-permute-start | bytes 196616 | tf_op jit(solution)/shard_map/ppermute | solution.py:581
  17.6 6.5 %collective-permute-start.5 = (bf16[2,128,128]{2,1,0:T(8,128)(2,1)S(1)}, bf16[2,128,128]{2,1,0:T(8,128)(2,1)S(1)}, u32[]{:S(2)}, u32[]{:S(2)}) collective-permute-start(bf16[2,128,128]{2,1,0:T(8,128)(2,1)S(1)} %get-tuple-element.59), channel_id=1, source_target_pairs={{0,4},{4,0},{8,12},{12,8},{1,5},{5,1},{9,13},{13,9},{2,6},{6,2},{1... | collective-permute-start | bytes 196616 | tf_op jit(solution)/shard_map/ppermute | solution.py:581
  24.2 1.8 %collective-permute-start.6 = (bf16[12,128,128]{2,1,0:T(8,128)(2,1)S(1)}, bf16[12,128,128]{2,1,0:T(8,128)(2,1)S(1)}, u32[]{:S(2)}, u32[]{:S(2)}) collective-permute-start(bf16[12,128,128]{2,1,0:T(8,128)(2,1)S(1)} %stack.1.refs_4_), channel_id=1, source_target_pairs={{0,1},{1,0},{2,3},{3,2},{4,5},{5,4},{6,7},{7,6},{8,9},{9,8},{10,11... | collective-permute-start | bytes 1179656 | tf_op jit(solution)/shard_map/ppermute | solution.py:577
  26.8 1.8 %collective-permute-start.7 = (bf16[4,128,128]{2,1,0:T(8,128)(2,1)S(1)}, bf16[4,128,128]{2,1,0:T(8,128)(2,1)S(1)}, u32[]{:S(2)}, u32[]{:S(2)}) collective-permute-start(bf16[4,128,128]{2,1,0:T(8,128)(2,1)S(1)} %get-tuple-element.72), channel_id=1, source_target_pairs={{0,1},{1,0},{2,3},{3,2},{4,5},{5,4},{6,7},{7,6},{8,9},{9,8},{10,11... | collective-permute-start | bytes 393224 | tf_op jit(solution)/shard_map/ppermute | solution.py:577
  27.0 6.3 %collective-permute-start.9 = (bf16[4,128,128]{2,1,0:T(8,128)(2,1)S(1)}, bf16[4,128,128]{2,1,0:T(8,128)(2,1)S(1)}, u32[]{:S(2)}, u32[]{:S(2)}) collective-permute-start(bf16[4,128,128]{2,1,0:T(8,128)(2,1)S(1)} %get-tuple-element.74.refs_0_), channel_id=1, source_target_pairs={{0,2},{2,0},{1,3},{3,1},{4,6},{6,4},{5,7},{7,5},{8,10},{10,8},{9,1... | collective-permute-start | bytes 393224 | tf_op jit(solution)/shard_map/ppermute | solution.py:577
  28.6 7.0 %collective-permute-start.8 = (bf16[4,128,128]{2,1,0:T(8,128)(2,1)S(1)}, bf16[4,128,128]{2,1,0:T(8,128)(2,1)S(1)}, u32[]{:S(2)}, u32[]{:S(2)}) collective-permute-start(bf16[4,128,128]{2,1,0:T(8,128)(2,1)S(1)} %add_up.1.refs_0_), channel_id=1, source_target_pairs={{0,2},{2,0},{1,3},{3,1},{4,6},{6,4},{5,7},{7,5},{8,10},{10,8},{9,1... | collective-permute-start | bytes 393224 | tf_op jit(solution)/shard_map/ppermute | solution.py:577
  36.3 1.6 %collective-permute-start.10 = (bf16[128,1152]{1,0:T(8,128)(2,1)S(1)}, bf16[128,1152]{1,0:T(8,128)(2,1)S(1)}, u32[]{:S(2)}, u32[]{:S(2)}) collective-permute-start(bf16[128,1152]{1,0:T(8,128)(2,1)S(1)} %get-tuple-element.76), channel_id=1, source_target_pairs={{0,1},{1,0},{2,3},{3,2},{4,5},{5,4},{6,7},{7,6},{8,9},{9,8},{10,11... | collective-permute-start | bytes 884744 | tf_op jit(solution)/shard_map/ppermute | solution.py:577
  38.4 15.1 %collective-permute-start.11 = (bf16[128,640]{1,0:T(8,128)(2,1)S(1)}, bf16[128,640]{1,0:T(8,128)(2,1)S(1)}, u32[]{:S(2)}, u32[]{:S(2)}) collective-permute-start(bf16[128,640]{1,0:T(8,128)(2,1)S(1)} %get-tuple-element.80), channel_id=1, source_target_pairs={{0,8},{4,12},{8,0},{12,4},{1,9},{5,13},{9,1},{13,5},{2,10},{6,14},... | collective-permute-start | bytes 491528 | tf_op jit(solution)/shard_map/ppermute | solution.py:581
  40.1 13.4 %collective-permute-start.12 = (bf16[128,640]{1,0:T(8,128)(2,1)S(1)}, bf16[128,640]{1,0:T(8,128)(2,1)S(1)}, u32[]{:S(2)}, u32[]{:S(2)}) collective-permute-start(bf16[128,640]{1,0:T(8,128)(2,1)S(1)} %get-tuple-element.81), channel_id=1, source_target_pairs={{0,12},{4,8},{8,4},{12,0},{1,13},{5,9},{9,5},{13,1},{2,14},{6,10},... | collective-permute-start | bytes 491528 | tf_op jit(solution)/shard_map/ppermute | solution.py:581
  42.4 11.7 %collective-permute-start.13 = (bf16[128,640]{1,0:T(8,128)(2,1)S(1)}, bf16[128,640]{1,0:T(8,128)(2,1)S(1)}, u32[]{:S(2)}, u32[]{:S(2)}) collective-permute-start(bf16[128,640]{1,0:T(8,128)(2,1)S(1)} %get-tuple-element.82), channel_id=1, source_target_pairs={{0,4},{4,0},{8,12},{12,8},{1,5},{5,1},{9,13},{13,9},{2,6},{6,2},{1... | collective-permute-start | bytes 491528 | tf_op jit(solution)/shard_map/ppermute | solution.py:581
  54.9 1.7 %collective-permute-start.14 = (bf16[8,128,128]{2,1,0:T(8,128)(2,1)S(1)}, bf16[8,128,128]{2,1,0:T(8,128)(2,1)S(1)}, u32[]{:S(2)}, u32[]{:S(2)}) collective-permute-start(bf16[8,128,128]{2,1,0:T(8,128)(2,1)S(1)} %late_rows.1.mine_ref), channel_id=1, source_target_pairs={{0,1},{1,0},{2,3},{3,2},{4,5},{5,4},{6,7},{7,6},{8,9},{9,8},{10,11... | collective-permute-start | bytes 786440 | tf_op jit(solution)/shard_map/ppermute | solution.py:577
  55.1 1.6 %collective-permute-start.15 = (f32[128,128]{1,0:T(8,128)S(1)}, f32[128,128]{1,0:T(8,128)S(1)}, u32[]{:S(2)}, u32[]{:S(2)}) collective-permute-start(f32[128,128]{1,0:T(8,128)S(1)} %terms.1.share_ref), channel_id=1, source_target_pairs={{0,1},{1,0},{2,3},{3,2},{4,5},{5,4},{6,7},{7,6},{8,9},{9,8},{10,11... | collective-permute-start | bytes 196616 | tf_op jit(solution)/shard_map/ppermute | solution.py:577

commit v7 on v6

--- a/solution.py
+++ b/solution.py
@@ -306,18 +306,19 @@
         at += share
 
 
-def halves_kernel(in_ref, low_ref, high_ref):
+def cut_kernel(in_ref, low_ref, high_ref):
     share = low_ref.shape[0]
     low_ref[...] = in_ref[:share]
     high_ref[...] = in_ref[share:]
 
 
-def halves(parts):
+def cut(parts):
     if len(parts) > 1:
         return parts
     share, columns, width = parts[0].shape
-    part = shape((share // 2, columns, width), BF16)
-    return list(call(halves_kernel, "halves", [part, part], [vmem()])(*parts))
+    low = share - share // 4
+    outs = [shape((low, columns, width), BF16), shape((share - low, columns, width), BF16)]
+    return list(call(cut_kernel, "cut", outs, [vmem()])(*parts))
 
 
 def stack(below, pieces):
@@ -431,10 +432,9 @@
 
 def dense_kernel(feats, *refs):
     sums, wide_cot, refs = refs[:feats], refs[feats], refs[feats + 1 :]
-    w_ref, act_ref, give_ref, spread_ref, keep_ref, wide, pre_scr, grad, term = refs
+    w_ref, act_ref, give_ref, spread_ref, term_ref, wide, pre_scr, grad = refs
     share, columns, width = act_ref.shape
     me = lax.axis_index("feat")
-    half = lax.axis_index("rep")
     rows = [pl.ds(pl.multiple_of(lax.rem(me + q, feats) * columns, columns), columns) for q in range(feats)]
     for q in range(feats):
         for b in range(share):
@@ -445,40 +445,35 @@
     factor = wide_cot[...].astype(F32) * sig * (1.0 + pre * (1.0 - sig))
     grad[...] = factor.astype(BF16)
     spread = dot(w_ref[rows[0], :], grad[...]).astype(BF16)
-    term[...] = dot(grad[rows[0], :], wide[...], NT)
-    part = keep_ref.shape[1]
+    term_ref[...] = dot(grad[rows[0], :], wide[...], NT).astype(BF16)
     wide_share = share * width
     give_ref[:, :wide_share] = spread
-    give_ref[:, 2 * wide_share :] = term[:, pl.ds(pl.multiple_of((1 - half) * part, part), part)].astype(BF16)
-    keep_ref[...] = term[:, pl.ds(pl.multiple_of(half * part, part), part)]
     for b in range(share):
         spread_ref[b] = spread[:, b * width : (b + 1) * width]
     own = pre_scr[rows[0], :]
     act = (own * jax.nn.sigmoid(own)).astype(BF16)
-    give_ref[:, wide_share : 2 * wide_share] = act
+    give_ref[:, wide_share:] = act
     for b in range(share):
         act_ref[b] = act[:, b * width : (b + 1) * width]
 
 
-def dense(sums, cot, weight, feats, reps):
+def dense(sums, cot, weight, feats):
     share, columns, width = sums[0].shape
     features = weight.shape[0]
-    part = features // reps
     return call(
         functools.partial(dense_kernel, feats),
         "dense",
         [
             shape((share, columns, width), BF16),
-            shape((columns, 2 * share * width + part), BF16),
+            shape((columns, 2 * share * width), BF16),
             shape((share, columns, width), BF16),
-            shape((columns, part), F32),
+            shape((columns, features), BF16),
         ],
         [vmem()] * (feats + 2),
         [
             pltpu.VMEM((features, share * width), BF16),
             pltpu.VMEM((features, share * width), F32),
             pltpu.VMEM((features, share * width), BF16),
-            pltpu.VMEM((columns, features), F32),
         ],
         flops=2 ** 28,
         moved=2 ** 20,
@@ -487,18 +482,16 @@
 
 def send_kernel(peers, *refs):
     ids_refs, refs = refs[: peers - 1], refs[peers - 1 :]
-    mine_ref, came_ref, keep_ref, m_ref, refs = refs[0], refs[1], refs[2], refs[3], refs[4:]
+    mine_ref, came_ref, m_ref, refs = refs[0], refs[1], refs[2], refs[3:]
     x3, refs = refs[0], refs[1:]
     send_refs, refs = refs[: peers - 1], refs[peers - 1 :]
-    self_ref, term_ref, mir = refs
+    self_ref, mir = refs
     share, _, width = mine_ref.shape
     both = CAP * width
     half = lax.axis_index("rep")
     x3[pl.ds(half * share, share)] = mine_ref[...]
     for b in range(share):
         x3[(1 - half) * share + b] = came_ref[:, b * width : (b + 1) * width]
-    term = (keep_ref[...] + came_ref[:, 2 * share * width :].astype(F32)).astype(BF16)
-    term_ref[...] = term
     mirrored(lanes(x3), m_ref, mir, peers * CAP, width)
     self_ref[...] = mir[:, :both]
     for k in range(1, peers):
@@ -507,47 +500,61 @@
         for s in range(CAP):
             at = (CAP + s) * width
             out[:, at : at + width] = x3[pick(ids_refs[k - 1], s)]
-        out[:, 2 * both :] = term
-
-
-def sends_of(mine, came, keep, operator, ids, peers, reps):
+
+
+def sends_of(mine, came, operator, ids, peers, reps):
     share, columns, width = mine.shape
     chunk = 2 * CAP * width
     outs = call(
         functools.partial(send_kernel, peers),
         "sends",
         [shape((share * reps, columns, width), BF16)]
-        + [shape((columns, chunk + keep.shape[1]), BF16)] * (peers - 1)
-        + [shape((columns, CAP * width), F32), shape(keep.shape, BF16)],
-        [vmem()] * (peers + 3),
+        + [shape((columns, chunk), BF16)] * (peers - 1)
+        + [shape((columns, CAP * width), F32)],
+        [vmem()] * (peers + 2),
         [pltpu.VMEM((columns, peers * CAP * width), F32)],
         flops=2 ** 28,
         moved=2 ** 21,
-    )(*ids[1:], mine, came, keep, operator)
-    return outs[0], [None] + list(outs[1:peers]), outs[peers], outs[peers + 1]
-
-
-def terms_kernel(peers, at, *refs):
-    out_ref, terms = refs[peers], refs[peers + 1]
-    me = lax.axis_index("graph")
-    terms[0] = refs[0][...].astype(F32)
-    for k in range(1, peers):
-        terms[k] = refs[k][:, at:].astype(F32)
-    total = terms[me]
-    for p in range(1, peers):
-        total = total + terms[jnp.bitwise_xor(me, p)]
-    out_ref[...] = total
-
-
-def sum_terms(term, came, at):
-    peers = len(came)
+    )(*ids[1:], mine, came, operator)
+    return outs[0], [None] + list(outs[1:peers]), outs[peers]
+
+
+def pair_kernel(mine_ref, came_ref, out_ref):
+    out_ref[...] = (mine_ref[...].astype(F32) + came_ref[...].astype(F32)).astype(out_ref.dtype)
+
+
+def pair_sum(mine, came, dtype):
+    return call(pair_kernel, "pair_sum", shape(mine.shape, dtype), [vmem(), vmem()])(mine, came)
+
+
+def split_kernel(mine_ref, came_ref, give_ref, keep_ref, total):
+    half = lax.axis_index("rep")
+    part = keep_ref.shape[1]
+    total[...] = mine_ref[...].astype(F32) + came_ref[...].astype(F32)
+    give_ref[...] = total[:, pl.ds(pl.multiple_of((1 - half) * part, part), part)].astype(BF16)
+    keep_ref[...] = total[:, pl.ds(pl.multiple_of(half * part, part), part)]
+
+
+def split_sum(mine, came, reps):
+    columns, features = mine.shape
+    part = (columns, features // reps)
     return call(
-        functools.partial(terms_kernel, peers, at),
-        "terms",
-        shape(term.shape, F32),
-        [vmem()] * peers,
-        [pltpu.VMEM((peers,) + term.shape, F32)],
-    )(term, *came[1:])
+        split_kernel,
+        "split_sum",
+        [shape(part, BF16), shape(part, F32)],
+        [vmem(), vmem()],
+        [pltpu.VMEM(mine.shape, F32)],
+    )(mine, came)
+
+
+def total_term(term, peers, reps):
+    bit = peers // 2
+    give, total = split_sum(term, across(term, peers, bit), reps)
+    total = pair_sum(total, ahead(give, "rep", reps, 1), F32 if bit == 1 else BF16)
+    while bit > 1:
+        bit //= 2
+        total = pair_sum(total, across(total, peers, bit), F32 if bit == 1 else BF16)
+    return total
 
 
 def finish_kernel(mine_ref, other_ref, share_ref, other_share_ref, act_ref, came_ref, grad_ref, weight_ref, out_ref):
@@ -595,46 +602,48 @@
     half, place, asks = prepare(features, tile_row, tile_col, tile_count, peers, reps)
     operator = list_operator(tiles, place, peers, blocks_dev)
     sends, own_mirror, own_cot = first_sends(features, cotangent, operator, asks[1:], peers, reps)
+    middle = peers // 2
+    came = [None] * peers
+    came[middle] = across(sends[middle], peers, middle)
     pieces, held = {0: [half]}, [0]
-    bit = peers // 2
+    bit = middle
     while bit:
         for k in held:
             if k ^ bit == 1:
                 continue
-            parts = halves(after(pieces[k], sends[1])) if k else pieces[k]
+            parts = pieces[k]
+            if k:
+                parts = cut(after(parts, sends[1]))
+                parts[-1] = after(parts[-1], came[middle])
             pieces[k ^ bit] = [across(part, peers, bit) for part in parts]
         held = held + [k ^ bit for k in held]
         bit //= 2
-    came = [None] * peers
-    for k in far_first:
-        send = after(sends[k], pieces[peers // 2]) if k == peers - 1 else sends[k]
+    for k in far_first[1:]:
+        send = after(sends[k], pieces[middle]) if k == peers - 1 else sends[k]
         came[k] = across(send, peers, k)
+    cots = [own_cot] + [ahead(own_cot, "feat", feats, feats - q) for q in range(1, feats)]
     arrived = [part for k in range(2, peers) for part in pieces[k]]
-    ordered, arrived = lax.optimization_barrier(([came[k] for k in far_first], arrived))
+    ordered, arrived, cots = lax.optimization_barrier(([came[k] for k in far_first], arrived, cots))
     came = [None] + [ordered[far_first.index(k)] for k in range(1, peers)]
     stacked = stack(came[1], arrived)
     swapped = ahead(stacked, "rep", reps, 1)
-    cots = [own_cot]
-    if feats > 1:
-        waited = after(own_cot, stacked)
-        cots += [ahead(waited, "feat", feats, feats - q) for q in range(1, feats)]
     acc, ids = first_rows(features, operator, asks[0], came, own_mirror, peers)
     give, keep = far_rows(acc, asks, stacked, swapped, operator, peers, reps)
 
     mine = add_up(keep, ahead(give, "rep", reps, 1))
     cot = widen(cots)
     sums = [mine] + [ahead(mine, "feat", feats, feats - q) for q in range(1, feats)]
-    act, give, spread, keep = dense(sums, cot, weight, feats, reps)
+    act, give, spread, term = dense(sums, cot, weight, feats)
+    total = total_term(term, peers, reps)
     shared = ahead(give, "rep", reps, 1)
-    values, sends, own_mirror, term = sends_of(spread, shared, keep, operator, ids, peers, reps)
+    values, sends, own_mirror = sends_of(spread, shared, operator, ids, peers, reps)
 
     came = [None] * peers
     for k in far_first:
         came[k] = across(sends[k], peers, k)
-    ordered = lax.optimization_barrier([came[k] for k in far_first])
+    ordered, total = lax.optimization_barrier(([came[k] for k in far_first], total))
     came = [None] + [ordered[far_first.index(k)] for k in range(1, peers)]
     part = late_rows([asks[0], values, own_mirror], ids, came, far_first, operator, True, True)
-    total = sum_terms(term, came, 2 * CAP * width)
     input_grad, weight_grad, activated = finish(
         part, ahead(part, "rep", reps, 1), total, ahead(total, "rep", reps, 1), act, shared
     )

time: 58 us -> 56.9 us (0.981)
  starting transfers between devices: 19.9 us -> 18.3 us
  waiting for transfers between devices: 25.8 us -> 26.4 us
    ppermute x7 -> x8, starting transfers between devices: 3.79 us -> 2.55 us  [ahead(): return lax.ppermute(value, axis, [(i, (i + k) % size) for i in range(size)])]
    ppermute x7 -> x8, waiting for transfers between devices: 9.55 us -> 10.3 us  [ahead(): return lax.ppermute(value, axis, [(i, (i + k) % size) for i in range(size)])]
    ppermute x9 -> x11, starting transfers between devices: 16.1 us -> 15.7 us  [across(): return lax.ppermute(value, 'graph', [(i, i ^ k) for i in range(peers)])]
    ppermute x9 -> x11, waiting for transfers between devices: 16.3 us -> 16.2 us  [across(): return lax.ppermute(value, 'graph', [(i, i ^ k) for i in range(peers)])]
  transfers between devices with their start and end apart: 16 -> 19, of which waited for: 11 -> 9; matrix products, arithmetic and copies ran while one was open for 0% -> 0% of each run, Pallas kernels for 7% -> 8%
where the time goes in v7:
time: 56.9 us; the launch traced here: 56.7 us
  waiting for transfers between devices  26.4 us (46%)
  starting transfers between devices  18.3 us (32%)
  Pallas kernels  9.73 us (17%)
  between operations  1.57 us (3%)
  local copies, waits for them, and re-layouts  0.68 us (1%)
    ppermute x11, waiting for transfers between devices, across(): return lax.ppermute(value, 'graph', [(i, i ^ k) for i in range(peers)])  16.2 us
    ppermute x11, starting transfers between devices, across(): return lax.ppermute(value, 'graph', [(i, i ^ k) for i in range(peers)])  15.7 us
    ppermute x8, waiting for transfers between devices, ahead(): return lax.ppermute(value, axis, [(i, (i + k) % size) for i in range(size)])  10.3 us
    pallas_call x1, Pallas kernels, list_operator(): call(functools.partial(operator_kernel, blocks_dev, slots_here, groups),...  3.04 us
    ppermute x8, starting transfers between devices, ahead(): return lax.ppermute(value, axis, [(i, (i + k) % size) for i in range(size)])  2.55 us
    pallas_call x1, Pallas kernels, prepare(): call(functools.partial(prepare_kernel, peers), 'prepare', [shape((blocks_...  1.82 us
  transfers between devices with their start and end apart: 19, of which 9 were waited for; matrix products, arithmetic and copies ran while one was open for 0% of the time, Pallas kernels for 8%

profile of v7, /device:TPU:0, one launch (start us, length us, event | category | flops | bytes accessed | tf_op | source)
XLA Modules:
  0.0 56.7 jit_solution(3759869677019685632)
XLA Ops:
  1.4 1.8 %prepare.1 = (bf16[4,128,128]{2,1,0:T(8,128)(2,1)}, s32[1,128]{1,0:T(1,128)}, s32[1,128]{1,0:T(1,128)}, s32[1,128]{1,0:T(1,128)}, s32[1,128]{1,0:T(1,128)}, /*index=5*/s32[1,128]{1,0:T(1,128)}) custom-call(s32[1]{0:T(128)S(6)} %copy.10.count_ref, s32[1,128]{1,0:T(1,128)} %bitcast.2, s32[1,128]{1,0:T(1,128)} %bitcast.3, bf16[8,128,128]{2,1,0:T(8,128)(2,1)} %refs_4_.3), custom_call_target="tpu_custom_call" | custom-call | bytes 262144 | tf_op jit(solution)/shard_map/prepare/pallas_call | solution.py:90
  3.2 4.1 %collective-permute-start.1 = (bf16[4,128,128]{2,1,0:T(8,128)(2,1)}, bf16[4,128,128]{2,1,0:T(8,128)(2,1)S(1)}, u32[]{:S(2)}, u32[]{:S(2)}) collective-permute-start(bf16[4,128,128]{2,1,0:T(8,128)(2,1)} %get-tuple-element.58), channel_id=1, source_target_pairs={{0,8},{4,12},{8,0},{12,4},{1,9},{5,13},{9,1},{13,5},{2,10},{6,14},... | collective-permute-start | bytes 393224 | tf_op jit(solution)/shard_map/ppermute | solution.py:588
  7.3 0.7 %copy-done.6 = s32[1,128]{1,0:T(1,128)S(1)} copy-done((s32[1,128]{1,0:T(1,128)S(1)}, s32[1,128]{1,0:T(1,128)}, u32[]{:S(2)}) %copy-start.6) | copy-done | bytes 536
  7.9 3.0 %operator.1.refs_5_.refs_6_.refs_9_ = bf16[1024,1024]{1,0:T(8,128)(2,1)S(1)} custom-call(s32[1,128]{1,0:T(1,128)S(1)} %copy-done.6, bf16[128,128,128]{2,1,0:T(8,128)(2,1)} %tiles_ref.1), custom_call_target="tpu_custom_call" | custom-call | bytes 16777216 | tf_op jit(solution)/shard_map/operator/pallas_call | solution.py:155
  11.5 1.6 %collective-permute-start.3 = (bf16[400,256]{1,0:T(8,128)(2,1)S(1)}, bf16[400,256]{1,0:T(8,128)(2,1)S(1)}, u32[]{:S(2)}, u32[]{:S(2)}) collective-permute-start(bf16[400,256]{1,0:T(8,128)(2,1)S(1)} %get-tuple-element.60), channel_id=1, source_target_pairs={{0,4},{4,0},{8,12},{12,8},{1,5},{5,1},{9,13},{13,9},{2,6},{6,2},{1... | collective-permute-start | bytes 614408 | tf_op jit(solution)/shard_map/ppermute | solution.py:588
  13.2 1.5 %collective-permute-start.6 = (bf16[4,128,128]{2,1,0:T(8,128)(2,1)S(1)}, bf16[4,128,128]{2,1,0:T(8,128)(2,1)S(1)}, u32[]{:S(2)}, u32[]{:S(2)}) collective-permute-start(bf16[4,128,128]{2,1,0:T(8,128)(2,1)S(1)} %get-tuple-element.79.refs_0_), channel_id=1, source_target_pairs={{0,2},{2,0},{1,3},{3,1},{4,6},{6,4},{5,7},{7,5},{8,10},{10,8},{9,1... | collective-permute-start | bytes 393224 | tf_op jit(solution)/shard_map/ppermute | solution.py:584
  15.0 0.5 collective-permute-start.4
  15.5 3.6 %collective-permute-start.2 = (bf16[144,256]{1,0:T(8,128)(2,1)S(1)}, bf16[144,256]{1,0:T(8,128)(2,1)S(1)}, u32[]{:S(2)}, u32[]{:S(2)}) collective-permute-start(bf16[144,256]{1,0:T(8,128)(2,1)S(1)} %get-tuple-element.59), channel_id=1, source_target_pairs={{0,12},{4,8},{8,4},{12,0},{1,13},{5,9},{9,5},{13,1},{2,14},{6,10},... | collective-permute-start | bytes 221192 | tf_op jit(solution)/shard_map/ppermute | solution.py:588
  19.1 2.8 %collective-permute-done.refs_2_ = bf16[144,256]{1,0:T(8,128)(2,1)S(1)} collective-permute-done((bf16[144,256]{1,0:T(8,128)(2,1)S(1)}, bf16[144,256]{1,0:T(8,128)(2,1)S(1)}, u32[]{:S(2)}, u32[]{:S(2)}) %collective-permute-start) | collective-permute-done | bytes 73760 | tf_op jit(solution)/shard_map/ppermute | solution.py:588
  21.9 3.9 %collective-permute-done.5.refs_2_ = bf16[1,128,128]{2,1,0:T(8,128)(2,1)S(1)} collective-permute-done((bf16[1,128,128]{2,1,0:T(8,128)(2,1)S(1)}, bf16[1,128,128]{2,1,0:T(8,128)(2,1)S(1)}, u32[]{:S(2)}, u32[]{:S(2)}) %collective-permute-start.5) | collective-permute-done | bytes 32800 | tf_op jit(solution)/shard_map/ppermute | solution.py:588
  26.4 1.3 %collective-permute-done.7.refs_5_ = bf16[12,128,128]{2,1,0:T(8,128)(2,1)S(1)} collective-permute-done((bf16[12,128,128]{2,1,0:T(8,128)(2,1)S(1)}, bf16[12,128,128]{2,1,0:T(8,128)(2,1)S(1)}, u32[]{:S(2)}, u32[]{:S(2)}) %collective-permute-start.7) | collective-permute-done | bytes 393248 | tf_op jit(solution)/shard_map/ppermute | solution.py:584
  27.7 0.8 %far_rows.1 = (bf16[4,128,128]{2,1,0:T(8,128)(2,1)S(1)}, f32[4,128,128]{2,1,0:T(8,128)S(1)}) custom-call(s32[1,128]{1,0:T(1,128)S(1)} %copy-done.3, s32[1,128]{1,0:T(1,128)S(1)} %copy-done.4, s32[1,128]{1,0:T(1,128)S(1)} %copy-done.5, f32[8,128,128]{2,1,0:T(8,128)S(1)} %get-tuple-element.73.refs_3_, bf16[12,128,128]{2,1,0:T(8,128)(2,1)S(1)} %stack.1.refs_4_, ...), custom_call_target="tpu_custom_call" | custom-call | flops 268435456 | bytes 2097152 | tf_op jit(solution)/shard_map/far_rows/pallas_call | solution.py:353
  28.7 1.2 %collective-permute-done.8.came_ref = bf16[4,128,128]{2,1,0:T(8,128)(2,1)S(1)} collective-permute-done((bf16[4,128,128]{2,1,0:T(8,128)(2,1)S(1)}, bf16[4,128,128]{2,1,0:T(8,128)(2,1)S(1)}, u32[]{:S(2)}, u32[]{:S(2)}) %collective-permute-start.8) | collective-permute-done | bytes 131104 | tf_op jit(solution)/shard_map/ppermute | solution.py:584
  30.1 5.5 %collective-permute-done.9.refs_1_ = bf16[4,128,128]{2,1,0:T(8,128)(2,1)S(1)} collective-permute-done((bf16[4,128,128]{2,1,0:T(8,128)(2,1)S(1)}, bf16[4,128,128]{2,1,0:T(8,128)(2,1)S(1)}, u32[]{:S(2)}, u32[]{:S(2)}) %collective-permute-start.9) | collective-permute-done | bytes 131104 | tf_op jit(solution)/shard_map/ppermute | solution.py:584
  35.6 0.7 %dense.1 = (bf16[4,128,128]{2,1,0:T(8,128)(2,1)S(1)}, bf16[128,1024]{1,0:T(8,128)(2,1)S(1)}, bf16[4,128,128]{2,1,0:T(8,128)(2,1)S(1)}, bf16[128,256]{1,0:T(8,128)(2,1)S(1)}) custom-call(bf16[4,128,128]{2,1,0:T(8,128)(2,1)S(1)} %add_up.1.refs_0_, bf16[4,128,128]{2,1,0:T(8,128)(2,1)S(1)} %collective-permute-done.9.refs_1_, bf16[256,512]{1,0:T(8,128)(2,1)S(1)} %widen.1.refs_2_, ...), custom_call_target="tpu_custom_call" | custom-call | flops 268435456 | bytes 1048576 | tf_op jit(solution)/shard_map/dense/pallas_call | solution.py:463
  36.3 1.8 %collective-permute-start.14 = (bf16[128,256]{1,0:T(8,128)(2,1)S(1)}, bf16[128,256]{1,0:T(8,128)(2,1)S(1)}, u32[]{:S(2)}, u32[]{:S(2)}) collective-permute-start(bf16[128,256]{1,0:T(8,128)(2,1)S(1)} %get-tuple-element.88.mine_ref), channel_id=1, source_target_pairs={{0,8},{4,12},{8,0},{12,4},{1,9},{5,13},{9,1},{13,5},{2,10},{6,14},... | collective-permute-start | bytes 196616 | tf_op jit(solution)/shard_map/ppermute | solution.py:588
  38.6 1.5 %collective-permute-start.11 = (bf16[128,512]{1,0:T(8,128)(2,1)S(1)}, bf16[128,512]{1,0:T(8,128)(2,1)S(1)}, u32[]{:S(2)}, u32[]{:S(2)}) collective-permute-start(bf16[128,512]{1,0:T(8,128)(2,1)S(1)} %get-tuple-element.85), channel_id=1, source_target_pairs={{0,8},{4,12},{8,0},{12,4},{1,9},{5,13},{9,1},{13,5},{2,10},{6,14},... | collective-permute-start | bytes 393224 | tf_op jit(solution)/shard_map/ppermute | solution.py:588
  40.1 1.6 %collective-permute-start.12 = (bf16[128,512]{1,0:T(8,128)(2,1)S(1)}, bf16[128,512]{1,0:T(8,128)(2,1)S(1)}, u32[]{:S(2)}, u32[]{:S(2)}) collective-permute-start(bf16[128,512]{1,0:T(8,128)(2,1)S(1)} %get-tuple-element.86), channel_id=1, source_target_pairs={{0,12},{4,8},{8,4},{12,0},{1,13},{5,9},{9,5},{13,1},{2,14},{6,10},... | collective-permute-start | bytes 393224 | tf_op jit(solution)/shard_map/ppermute | solution.py:588
  42.2 5.5 %collective-permute-done.14.came_ref = bf16[128,256]{1,0:T(8,128)(2,1)S(1)} collective-permute-done((bf16[128,256]{1,0:T(8,128)(2,1)S(1)}, bf16[128,256]{1,0:T(8,128)(2,1)S(1)}, u32[]{:S(2)}, u32[]{:S(2)}) %collective-permute-start.14) | collective-permute-done | bytes 65568 | tf_op jit(solution)/shard_map/ppermute | solution.py:588
  47.8 1.2 %collective-permute-done.15.came_ref = bf16[128,128]{1,0:T(8,128)(2,1)S(1)} collective-permute-done((bf16[128,128]{1,0:T(8,128)(2,1)S(1)}, bf16[128,128]{1,0:T(8,128)(2,1)S(1)}, u32[]{:S(2)}, u32[]{:S(2)}) %collective-permute-start.15) | collective-permute-done | bytes 32800 | tf_op jit(solution)/shard_map/ppermute | solution.py:584
  49.2 3.9 %collective-permute-done.16.came_ref = bf16[128,128]{1,0:T(8,128)(2,1)S(1)} collective-permute-done((bf16[128,128]{1,0:T(8,128)(2,1)S(1)}, bf16[128,128]{1,0:T(8,128)(2,1)S(1)}, u32[]{:S(2)}, u32[]{:S(2)}) %collective-permute-start.16) | collective-permute-done | bytes 32800 | tf_op jit(solution)/shard_map/ppermute | solution.py:588
  53.1 0.9 %late_rows.1.mine_ref = bf16[8,128,128]{2,1,0:T(8,128)(2,1)S(1)} custom-call(s32[1,128]{1,0:T(1,128)S(1)} %copy-done.2, bf16[8,128,128]{2,1,0:T(8,128)(2,1)S(1)} %get-tuple-element.83.refs_1_, f32[128,256]{1,0:T(8,128)S(1)} %get-tuple-element.84.refs_2_, s32[1,128]{1,0:T(1,128)S(1)} %get-tuple-element.71.refs_1_.refs_3_, ...), custom_call_target="tpu_custom_call" | custom-call | flops 134217728 | bytes 1048576 | tf_op jit(solution)/shard_map/late_rows/pallas_call | solution.py:397
  54.6 1.1 %collective-permute-done.18.other_share_ref = f32[128,128]{1,0:T(8,128)S(1)} collective-permute-done((f32[128,128]{1,0:T(8,128)S(1)}, f32[128,128]{1,0:T(8,128)S(1)}, u32[]{:S(2)}, u32[]{:S(2)}) %collective-permute-start.18) | collective-permute-done | bytes 65568 | tf_op jit(solution)/shard_map/ppermute | solution.py:584
  55.7 1.0 %finish.1 = (bf16[8,128,128]{2,1,0:T(8,128)(2,1)}, f32[256,128]{1,0:T(8,128)}, bf16[8,128,128]{2,1,0:T(8,128)(2,1)}) custom-call(bf16[8,128,128]{2,1,0:T(8,128)(2,1)S(1)} %late_rows.1.mine_ref, bf16[8,128,128]{2,1,0:T(8,128)(2,1)S(1)} %collective-permute-done.17.other_ref, f32[128,128]{1,0:T(8,128)S(1)} %pair_sum.3.share_ref, ...), custom_call_target="tpu_custom_call" | custom-call | bytes 262144 | tf_op jit(solution)/shard_map/finish/pallas_call | solution.py:575
  (46 shorter events, 3.6 us)
Async XLA Ops:
  0.6 10.4 %copy-start = (bf16[8,128,128]{2,1,0:T(8,128)(2,1)S(1)}, bf16[8,128,128]{2,1,0:T(8,128)(2,1)}, u32[]{:S(2)}) copy-start(bf16[8,128,128]{2,1,0:T(8,128)(2,1)} %refs_4_.3) | copy-start | bytes 786436
  0.6 10.4 %copy-start.1 = (bf16[8,128,128]{2,1,0:T(8,128)(2,1)S(1)}, bf16[8,128,128]{2,1,0:T(8,128)(2,1)}, u32[]{:S(2)}) copy-start(bf16[8,128,128]{2,1,0:T(8,128)(2,1)} %refs_4_.2) | copy-start | bytes 786436
  3.2 7.9 %copy-start.5 = (s32[1,128]{1,0:T(1,128)S(1)}, s32[1,128]{1,0:T(1,128)}, u32[]{:S(2)}) copy-start(s32[1,128]{1,0:T(1,128)} %get-tuple-element.54.refs_2_) | copy-start | bytes 1540
  3.2 11.8 %collective-permute-start.1 = (bf16[4,128,128]{2,1,0:T(8,128)(2,1)}, bf16[4,128,128]{2,1,0:T(8,128)(2,1)S(1)}, u32[]{:S(2)}, u32[]{:S(2)}) collective-permute-start(bf16[4,128,128]{2,1,0:T(8,128)(2,1)} %get-tuple-element.58), channel_id=1, source_target_pairs={{0,8},{4,12},{8,0},{12,4},{1,9},{5,13},{9,1},{13,5},{2,10},{6,14},... | collective-permute-start | bytes 393224 | tf_op jit(solution)/shard_map/ppermute | solution.py:588
  7.9 18.0 %copy-start.2 = (s32[1,128]{1,0:T(1,128)S(1)}, s32[1,128]{1,0:T(1,128)}, u32[]{:S(2)}) copy-start(s32[1,128]{1,0:T(1,128)} %get-tuple-element.51.refs_0_) | copy-start | bytes 1540
  11.5 24.0 %copy-start.7 = (bf16[256,256]{1,0:T(8,128)(2,1)S(1)}, bf16[256,256]{1,0:T(8,128)(2,1)}, u32[]{:S(2)}) copy-start(bf16[256,256]{1,0:T(8,128)(2,1)} %refs_3_.3) | copy-start | bytes 393220
  11.5 14.3 %collective-permute-start.3 = (bf16[400,256]{1,0:T(8,128)(2,1)S(1)}, bf16[400,256]{1,0:T(8,128)(2,1)S(1)}, u32[]{:S(2)}, u32[]{:S(2)}) collective-permute-start(bf16[400,256]{1,0:T(8,128)(2,1)S(1)} %get-tuple-element.60), channel_id=1, source_target_pairs={{0,4},{4,0},{8,12},{12,8},{1,5},{5,1},{9,13},{13,9},{2,6},{6,2},{1... | collective-permute-start | bytes 614408 | tf_op jit(solution)/shard_map/ppermute | solution.py:588
  13.2 8.8 %collective-permute-start.6 = (bf16[4,128,128]{2,1,0:T(8,128)(2,1)S(1)}, bf16[4,128,128]{2,1,0:T(8,128)(2,1)S(1)}, u32[]{:S(2)}, u32[]{:S(2)}) collective-permute-start(bf16[4,128,128]{2,1,0:T(8,128)(2,1)S(1)} %get-tuple-element.79.refs_0_), channel_id=1, source_target_pairs={{0,2},{2,0},{1,3},{3,1},{4,6},{6,4},{5,7},{7,5},{8,10},{10,8},{9,1... | collective-permute-start | bytes 393224 | tf_op jit(solution)/shard_map/ppermute | solution.py:584
  14.7 7.3 %collective-permute-start = (bf16[144,256]{1,0:T(8,128)(2,1)S(1)}, bf16[144,256]{1,0:T(8,128)(2,1)S(1)}, u32[]{:S(2)}, u32[]{:S(2)}) collective-permute-start(bf16[144,256]{1,0:T(8,128)(2,1)S(1)} %get-tuple-element.56), channel_id=1, source_target_pairs={{0,8},{4,12},{8,0},{12,4},{1,9},{5,13},{9,1},{13,5},{2,10},{6,14},... | collective-permute-start | bytes 221192 | tf_op jit(solution)/shard_map/ppermute | solution.py:588
  15.0 10.8 %collective-permute-start.4 = (bf16[3,128,128]{2,1,0:T(8,128)(2,1)S(1)}, bf16[3,128,128]{2,1,0:T(8,128)(2,1)S(1)}, u32[]{:S(2)}, u32[]{:S(2)}) collective-permute-start(bf16[3,128,128]{2,1,0:T(8,128)(2,1)S(1)} %get-tuple-element.62), channel_id=1, source_target_pairs={{0,4},{4,0},{8,12},{12,8},{1,5},{5,1},{9,13},{13,9},{2,6},{6,2},{1... | collective-permute-start | bytes 294920 | tf_op jit(solution)/shard_map/ppermute | solution.py:588
  15.5 10.3 %collective-permute-start.2 = (bf16[144,256]{1,0:T(8,128)(2,1)S(1)}, bf16[144,256]{1,0:T(8,128)(2,1)S(1)}, u32[]{:S(2)}, u32[]{:S(2)}) collective-permute-start(bf16[144,256]{1,0:T(8,128)(2,1)S(1)} %get-tuple-element.59), channel_id=1, source_target_pairs={{0,12},{4,8},{8,4},{12,0},{1,13},{5,9},{9,5},{13,1},{2,14},{6,10},... | collective-permute-start | bytes 221192 | tf_op jit(solution)/shard_map/ppermute | solution.py:588
  21.9 3.9 %collective-permute-start.5 = (bf16[1,128,128]{2,1,0:T(8,128)(2,1)S(1)}, bf16[1,128,128]{2,1,0:T(8,128)(2,1)S(1)}, u32[]{:S(2)}, u32[]{:S(2)}) collective-permute-start(bf16[1,128,128]{2,1,0:T(8,128)(2,1)S(1)} %get-tuple-element.64), channel_id=1, source_target_pairs={{0,4},{4,0},{8,12},{12,8},{1,5},{5,1},{9,13},{13,9},{2,6},{6,2},{1... | collective-permute-start | bytes 98312 | tf_op jit(solution)/shard_map/ppermute | solution.py:588
  25.9 1.8 %collective-permute-start.7 = (bf16[12,128,128]{2,1,0:T(8,128)(2,1)S(1)}, bf16[12,128,128]{2,1,0:T(8,128)(2,1)S(1)}, u32[]{:S(2)}, u32[]{:S(2)}) collective-permute-start(bf16[12,128,128]{2,1,0:T(8,128)(2,1)S(1)} %stack.1.refs_4_), channel_id=1, source_target_pairs={{0,1},{1,0},{2,3},{3,2},{4,5},{5,4},{6,7},{7,6},{8,9},{9,8},{10,11... | collective-permute-start | bytes 1179656 | tf_op jit(solution)/shard_map/ppermute | solution.py:584
  28.5 1.4 %collective-permute-start.8 = (bf16[4,128,128]{2,1,0:T(8,128)(2,1)S(1)}, bf16[4,128,128]{2,1,0:T(8,128)(2,1)S(1)}, u32[]{:S(2)}, u32[]{:S(2)}) collective-permute-start(bf16[4,128,128]{2,1,0:T(8,128)(2,1)S(1)} %get-tuple-element.78), channel_id=1, source_target_pairs={{0,1},{1,0},{2,3},{3,2},{4,5},{5,4},{6,7},{7,6},{8,9},{9,8},{10,11... | collective-permute-start | bytes 393224 | tf_op jit(solution)/shard_map/ppermute | solution.py:584
  29.9 5.6 %collective-permute-start.9 = (bf16[4,128,128]{2,1,0:T(8,128)(2,1)S(1)}, bf16[4,128,128]{2,1,0:T(8,128)(2,1)S(1)}, u32[]{:S(2)}, u32[]{:S(2)}) collective-permute-start(bf16[4,128,128]{2,1,0:T(8,128)(2,1)S(1)} %add_up.1.refs_0_), channel_id=1, source_target_pairs={{0,2},{2,0},{1,3},{3,1},{4,6},{6,4},{5,7},{7,5},{8,10},{10,8},{9,1... | collective-permute-start | bytes 393224 | tf_op jit(solution)/shard_map/ppermute | solution.py:584
  36.2 1.9 %collective-permute-start.10 = (bf16[128,1024]{1,0:T(8,128)(2,1)S(1)}, bf16[128,1024]{1,0:T(8,128)(2,1)S(1)}, u32[]{:S(2)}, u32[]{:S(2)}) collective-permute-start(bf16[128,1024]{1,0:T(8,128)(2,1)S(1)} %get-tuple-element.82), channel_id=1, source_target_pairs={{0,1},{1,0},{2,3},{3,2},{4,5},{5,4},{6,7},{7,6},{8,9},{9,8},{10,11... | collective-permute-start | bytes 786440 | tf_op jit(solution)/shard_map/ppermute | solution.py:584
  36.3 11.4 %collective-permute-start.14 = (bf16[128,256]{1,0:T(8,128)(2,1)S(1)}, bf16[128,256]{1,0:T(8,128)(2,1)S(1)}, u32[]{:S(2)}, u32[]{:S(2)}) collective-permute-start(bf16[128,256]{1,0:T(8,128)(2,1)S(1)} %get-tuple-element.88.mine_ref), channel_id=1, source_target_pairs={{0,8},{4,12},{8,0},{12,4},{1,9},{5,13},{9,1},{13,5},{2,10},{6,14},... | collective-permute-start | bytes 196616 | tf_op jit(solution)/shard_map/ppermute | solution.py:588
  38.6 14.5 %collective-permute-start.11 = (bf16[128,512]{1,0:T(8,128)(2,1)S(1)}, bf16[128,512]{1,0:T(8,128)(2,1)S(1)}, u32[]{:S(2)}, u32[]{:S(2)}) collective-permute-start(bf16[128,512]{1,0:T(8,128)(2,1)S(1)} %get-tuple-element.85), channel_id=1, source_target_pairs={{0,8},{4,12},{8,0},{12,4},{1,9},{5,13},{9,1},{13,5},{2,10},{6,14},... | collective-permute-start | bytes 393224 | tf_op jit(solution)/shard_map/ppermute | solution.py:588
  40.1 12.9 %collective-permute-start.12 = (bf16[128,512]{1,0:T(8,128)(2,1)S(1)}, bf16[128,512]{1,0:T(8,128)(2,1)S(1)}, u32[]{:S(2)}, u32[]{:S(2)}) collective-permute-start(bf16[128,512]{1,0:T(8,128)(2,1)S(1)} %get-tuple-element.86), channel_id=1, source_target_pairs={{0,12},{4,8},{8,4},{12,0},{1,13},{5,9},{9,5},{13,1},{2,14},{6,10},... | collective-permute-start | bytes 393224 | tf_op jit(solution)/shard_map/ppermute | solution.py:588
  41.7 11.4 %collective-permute-start.13 = (bf16[128,512]{1,0:T(8,128)(2,1)S(1)}, bf16[128,512]{1,0:T(8,128)(2,1)S(1)}, u32[]{:S(2)}, u32[]{:S(2)}) collective-permute-start(bf16[128,512]{1,0:T(8,128)(2,1)S(1)} %get-tuple-element.87), channel_id=1, source_target_pairs={{0,4},{4,0},{8,12},{12,8},{1,5},{5,1},{9,13},{13,9},{2,6},{6,2},{1... | collective-permute-start | bytes 393224 | tf_op jit(solution)/shard_map/ppermute | solution.py:588
  47.7 1.3 %collective-permute-start.15 = (bf16[128,128]{1,0:T(8,128)(2,1)S(1)}, bf16[128,128]{1,0:T(8,128)(2,1)S(1)}, u32[]{:S(2)}, u32[]{:S(2)}) collective-permute-start(bf16[128,128]{1,0:T(8,128)(2,1)S(1)} %get-tuple-element.90), channel_id=1, source_target_pairs={{0,1},{1,0},{2,3},{3,2},{4,5},{5,4},{6,7},{7,6},{8,9},{9,8},{10,11... | collective-permute-start | bytes 98312 | tf_op jit(solution)/shard_map/ppermute | solution.py:584
  49.0 4.0 %collective-permute-start.16 = (bf16[128,128]{1,0:T(8,128)(2,1)S(1)}, bf16[128,128]{1,0:T(8,128)(2,1)S(1)}, u32[]{:S(2)}, u32[]{:S(2)}) collective-permute-start(bf16[128,128]{1,0:T(8,128)(2,1)S(1)} %pair_sum.2.mine_ref), channel_id=1, source_target_pairs={{0,4},{4,0},{8,12},{12,8},{1,5},{5,1},{9,13},{13,9},{2,6},{6,2},{1... | collective-permute-start | bytes 98312 | tf_op jit(solution)/shard_map/ppermute | solution.py:588
  54.0 1.7 %collective-permute-start.17 = (bf16[8,128,128]{2,1,0:T(8,128)(2,1)S(1)}, bf16[8,128,128]{2,1,0:T(8,128)(2,1)S(1)}, u32[]{:S(2)}, u32[]{:S(2)}) collective-permute-start(bf16[8,128,128]{2,1,0:T(8,128)(2,1)S(1)} %late_rows.1.mine_ref), channel_id=1, source_target_pairs={{0,1},{1,0},{2,3},{3,2},{4,5},{5,4},{6,7},{7,6},{8,9},{9,8},{10,11... | collective-permute-start | bytes 786440 | tf_op jit(solution)/shard_map/ppermute | solution.py:584
  54.1 1.6 %collective-permute-start.18 = (f32[128,128]{1,0:T(8,128)S(1)}, f32[128,128]{1,0:T(8,128)S(1)}, u32[]{:S(2)}, u32[]{:S(2)}) collective-permute-start(f32[128,128]{1,0:T(8,128)S(1)} %pair_sum.3.share_ref), channel_id=1, source_target_pairs={{0,1},{1,0},{2,3},{3,2},{4,5},{5,4},{6,7},{7,6},{8,9},{9,8},{10,11... | collective-permute-start | bytes 196616 | tf_op jit(solution)/shard_map/ppermute | solution.py:584
  (3 other events, 16.4 us)

commit v8 on v7

--- a/solution.py
+++ b/solution.py
@@ -186,41 +186,63 @@
 def first_sends_kernel(peers, *refs):
     ask_refs, refs = refs[: peers - 1], refs[peers - 1 :]
     x3, cot, m_ref, refs = refs[0], refs[1], refs[2], refs[3:]
-    send_refs, self_ref, cot_ref, mir = refs[: peers - 1], refs[peers - 1], refs[peers], refs[peers + 1]
+    middle = peers // 2
+    far_ref, near_refs, refs = refs[0], refs[1:middle], refs[middle:]
+    self_ref, cot_ref, mir = refs
     _, columns, width = x3.shape
     share = cot_ref.shape[0]
     both = CAP * width
-    half = lax.axis_index("rep")
     mirrored(lanes(x3), m_ref, mir, peers * CAP, width)
     self_ref[...] = mir[:, :both]
     lane = lax.broadcasted_iota(jnp.int32, (TAIL, both), 1)
     for k in range(1, peers):
-        out = send_refs[k - 1]
-        out[:columns, :] = mir[:, k * both : (k + 1) * both].astype(BF16)
+        out, left = (near_refs[k - 1], 0) if k < middle else (far_ref, (k - middle) * both)
+        out[:columns, left : left + both] = mir[:, k * both : (k + 1) * both].astype(BF16)
         low, high = ask_refs[k - 1][:, :1], ask_refs[k - 1][:, 1:2]
-        out[columns : columns + TAIL, :] = jnp.where(lane < width, low, high).astype(F32).astype(BF16)
-    for b in range(share):
-        top = columns + TAIL + b // CAP * columns
-        left = b % CAP * width
-        send_refs[0][top : top + columns, left : left + width] = x3[half * share + b]
-    cot_ref[...] = cot[pl.ds(half * share, share)]
+        out[columns:, left : left + both] = jnp.where(lane < width, low, high).astype(F32).astype(BF16)
+    cot_ref[...] = cot[pl.ds(lax.axis_index("rep") * share, share)]
 
 
 def first_sends(values, cotangent, operator, asks, peers, reps):
     blocks_dev, columns, width = values.shape
-    share = blocks_dev // reps
+    middle = peers // 2
     outs = call(
         functools.partial(first_sends_kernel, peers),
         "first_sends",
-        [shape((columns + TAIL + share // CAP * columns, CAP * width), BF16)]
-        + [shape((columns + TAIL, CAP * width), BF16)] * (peers - 2)
-        + [shape((columns, CAP * width), F32), shape((share, columns, width), BF16)],
+        [shape((columns + TAIL, middle * CAP * width), BF16)]
+        + [shape((columns + TAIL, CAP * width), BF16)] * (middle - 1)
+        + [shape((columns, CAP * width), F32), shape((blocks_dev // reps, columns, width), BF16)],
         [vmem()] * (peers + 2),
         [pltpu.VMEM((columns, peers * CAP * width), F32)],
         flops=2 ** 28,
         moved=2 ** 21,
     )(*asks, values, cotangent, operator)
-    return [None] + list(outs[: peers - 1]), outs[peers - 1], outs[peers]
+    return outs[0], [None] + list(outs[1:middle]), outs[middle], outs[middle + 1]
+
+
+def below_kernel(sums_ref, half_ref, out_ref):
+    top = sums_ref.shape[0]
+    share, columns, width = half_ref.shape
+    out_ref[:top, :] = sums_ref[...]
+    for b in range(share):
+        row, left = top + b // CAP * columns, b % CAP * width
+        out_ref[row : row + columns, left : left + width] = half_ref[b]
+
+
+def below(sums, half):
+    share, columns, width = half.shape
+    out = shape((sums.shape[0] + share // CAP * columns, sums.shape[1]), BF16)
+    return call(below_kernel, "below", out, [vmem(), vmem()])(sums, half)
+
+
+def pass_kernel(j, came_ref, out_ref):
+    both = out_ref.shape[1]
+    out_ref[...] = came_ref[:, j * both : (j + 1) * both]
+
+
+def pass_on(came, j, middle):
+    out = shape((came.shape[0], came.shape[1] // middle), BF16)
+    return call(functools.partial(pass_kernel, j), "pass_on", out, [vmem()])(came)
 
 
 def add_sums(acc, block, sums):
@@ -292,40 +314,23 @@
     return outs[0], [None] + list(outs[1:])
 
 
-def stack_kernel(below_ref, *refs):
+def stack_kernel(middle, *refs):
     out_ref = refs[-1]
-    _, columns, width = out_ref.shape
-    at = (below_ref.shape[0] - TAIL) // columns * CAP - CAP
-    for b in range(at):
-        top = columns + TAIL + b // CAP * columns
-        left = b % CAP * width
-        out_ref[b] = below_ref[top : top + columns, left : left + width]
-    for ref in refs[:-1]:
-        share = ref.shape[0]
-        out_ref[at : at + share] = ref[...]
-        at += share
-
-
-def cut_kernel(in_ref, low_ref, high_ref):
-    share = low_ref.shape[0]
-    low_ref[...] = in_ref[:share]
-    high_ref[...] = in_ref[share:]
-
-
-def cut(parts):
-    if len(parts) > 1:
-        return parts
-    share, columns, width = parts[0].shape
-    low = share - share // 4
-    outs = [shape((low, columns, width), BF16), shape((share - low, columns, width), BF16)]
-    return list(call(cut_kernel, "cut", outs, [vmem()])(*parts))
-
-
-def stack(below, pieces):
-    _, columns, width = pieces[0].shape
-    count = (below.shape[0] - TAIL) // columns * CAP - CAP + sum(piece.shape[0] for piece in pieces)
-    out = shape((count, columns, width), BF16)
-    return call(stack_kernel, "stack", out, [vmem()] * (len(pieces) + 1))(below, *pieces)
+    share, columns, width = refs[0].shape
+    for k in range(1, middle + 1):
+        out_ref[(k - 1) * share : k * share] = refs[k - 1][...]
+    for k in range(middle + 1, 2 * middle):
+        ref = refs[k - 1]
+        for b in range(share):
+            row, left = columns + TAIL + b // CAP * columns, b % CAP * width
+            out_ref[(k - 1) * share + b] = ref[row : row + columns, left : left + width]
+
+
+def stack(pieces, chunks):
+    share, columns, width = pieces[0].shape
+    out = shape(((len(pieces) + len(chunks)) * share, columns, width), BF16)
+    kernel = functools.partial(stack_kernel, len(pieces))
+    return call(kernel, "stack", out, [vmem()] * (len(pieces) + len(chunks)))(*pieces, *chunks)
 
 
 def far_rows_kernel(peers, *refs):
@@ -601,31 +606,20 @@
 
     half, place, asks = prepare(features, tile_row, tile_col, tile_count, peers, reps)
     operator = list_operator(tiles, place, peers, blocks_dev)
-    sends, own_mirror, own_cot = first_sends(features, cotangent, operator, asks[1:], peers, reps)
+    far, near, own_mirror, own_cot = first_sends(features, cotangent, operator, asks[1:], peers, reps)
     middle = peers // 2
-    came = [None] * peers
-    came[middle] = across(sends[middle], peers, middle)
-    pieces, held = {0: [half]}, [0]
-    bit = middle
-    while bit:
-        for k in held:
-            if k ^ bit == 1:
-                continue
-            parts = pieces[k]
-            if k:
-                parts = cut(after(parts, sends[1]))
-                parts[-1] = after(parts[-1], came[middle])
-            pieces[k ^ bit] = [across(part, peers, bit) for part in parts]
-        held = held + [k ^ bit for k in held]
-        bit //= 2
-    for k in far_first[1:]:
-        send = after(sends[k], pieces[middle]) if k == peers - 1 else sends[k]
-        came[k] = across(send, peers, k)
+    pieces = [across(half, peers, j) for j in range(1, middle)]
+    crossed = across(half, peers, middle)
+    sums = across(far, peers, middle)
+    chunks = []
+    for j in range(1, middle):
+        chunk, pieces[j - 1] = lax.optimization_barrier((below(near[j], crossed), pieces[j - 1]))
+        chunks.append(across(chunk, peers, j))
+    passed = [across(pass_on(sums, j, middle), peers, j) for j in range(1, middle)]
     cots = [own_cot] + [ahead(own_cot, "feat", feats, feats - q) for q in range(1, feats)]
-    arrived = [part for k in range(2, peers) for part in pieces[k]]
-    ordered, arrived, cots = lax.optimization_barrier(([came[k] for k in far_first], arrived, cots))
-    came = [None] + [ordered[far_first.index(k)] for k in range(1, peers)]
-    stacked = stack(came[1], arrived)
+    chunks, passed, cots = lax.optimization_barrier((chunks, passed, cots))
+    came = [None] + chunks + [sums] + passed
+    stacked = stack(pieces + [crossed], chunks)
     swapped = ahead(stacked, "rep", reps, 1)
     acc, ids = first_rows(features, operator, asks[0], came, own_mirror, peers)
     give, keep = far_rows(acc, asks, stacked, swapped, operator, peers, reps)

time: 56.9 us -> 57.6 us (1.012)
  waiting for transfers between devices: 26.4 us -> 28.4 us
  starting transfers between devices: 18.3 us -> 17.1 us
    ppermute x11 -> x10, starting transfers between devices: 15.7 us -> 13 us  [across(): return lax.ppermute(value, 'graph', [(i, i ^ k) for i in range(peers)])]
    ppermute x11 -> x10, waiting for transfers between devices: 16.2 us -> 18.3 us  [across(): return lax.ppermute(value, 'graph', [(i, i ^ k) for i in range(peers)])]
    ppermute x8, starting transfers between devices: 2.55 us -> 4.05 us  [ahead(): return lax.ppermute(value, axis, [(i, (i + k) % size) for i in range(size)])]
  transfers between devices with their start and end apart: 19 -> 18, of which waited for: 9 -> 12; matrix products, arithmetic and copies ran while one was open for 0% -> 0% of each run, Pallas kernels for 8% -> 8%
where the time goes in v8:
time: 57.6 us; the launch traced here: 57.4 us
  waiting for transfers between devices  28.4 us (49%)
  starting transfers between devices  17.1 us (30%)
  Pallas kernels  9.75 us (17%)
  between operations  1.55 us (3%)
  local copies, waits for them, and re-layouts  0.68 us (1%)
    ppermute x10, waiting for transfers between devices, across(): return lax.ppermute(value, 'graph', [(i, i ^ k) for i in range(peers)])  18.3 us
    ppermute x10, starting transfers between devices, across(): return lax.ppermute(value, 'graph', [(i, i ^ k) for i in range(peers)])  13 us
    ppermute x8, waiting for transfers between devices, ahead(): return lax.ppermute(value, axis, [(i, (i + k) % size) for i in range(size)])  10 us
    ppermute x8, starting transfers between devices, ahead(): return lax.ppermute(value, axis, [(i, (i + k) % size) for i in range(size)])  4.05 us
    pallas_call x1, Pallas kernels, list_operator(): call(functools.partial(operator_kernel, blocks_dev, slots_here, groups),...  3.04 us
    pallas_call x1, Pallas kernels, prepare(): call(functools.partial(prepare_kernel, peers), 'prepare', [shape((blocks_...  1.81 us
  transfers between devices with their start and end apart: 18, of which 12 were waited for; matrix products, arithmetic and copies ran while one was open for 0% of the time, Pallas kernels for 8%

profile of v8, /device:TPU:0, one launch (start us, length us, event | category | flops | bytes accessed | tf_op | source)
XLA Modules:
  0.0 57.4 jit_solution(9722629595438175042)
XLA Ops:
  1.4 1.8 %prepare.1 = (bf16[4,128,128]{2,1,0:T(8,128)(2,1)}, s32[1,128]{1,0:T(1,128)}, s32[1,128]{1,0:T(1,128)}, s32[1,128]{1,0:T(1,128)}, s32[1,128]{1,0:T(1,128)}, /*index=5*/s32[1,128]{1,0:T(1,128)}) custom-call(s32[1]{0:T(128)S(6)} %copy.10.count_ref, s32[1,128]{1,0:T(1,128)} %bitcast.2, s32[1,128]{1,0:T(1,128)} %bitcast.3, bf16[8,128,128]{2,1,0:T(8,128)(2,1)} %refs_4_.3), custom_call_target="tpu_custom_call" | custom-call | bytes 262144 | tf_op jit(solution)/shard_map/prepare/pallas_call | solution.py:90
  3.2 4.1 %collective-permute-start = (bf16[4,128,128]{2,1,0:T(8,128)(2,1)}, bf16[4,128,128]{2,1,0:T(8,128)(2,1)S(1)}, u32[]{:S(2)}, u32[]{:S(2)}) collective-permute-start(bf16[4,128,128]{2,1,0:T(8,128)(2,1)} %get-tuple-element.49), channel_id=1, source_target_pairs={{0,8},{4,12},{8,0},{12,4},{1,9},{5,13},{9,1},{13,5},{2,10},{6,14},... | collective-permute-start | bytes 393224 | tf_op jit(solution)/shard_map/ppermute | solution.py:593
  7.3 1.6 %collective-permute-start.1 = (bf16[4,128,128]{2,1,0:T(8,128)(2,1)}, bf16[4,128,128]{2,1,0:T(8,128)(2,1)S(1)}, u32[]{:S(2)}, u32[]{:S(2)}) collective-permute-start(bf16[4,128,128]{2,1,0:T(8,128)(2,1)} %get-tuple-element.49), channel_id=1, source_target_pairs={{0,4},{4,0},{8,12},{12,8},{1,5},{5,1},{9,13},{13,9},{2,6},{6,2},{1... | collective-permute-start | bytes 393224 | tf_op jit(solution)/shard_map/ppermute | solution.py:593
  8.9 0.7 %copy-done.6 = s32[1,128]{1,0:T(1,128)S(1)} copy-done((s32[1,128]{1,0:T(1,128)S(1)}, s32[1,128]{1,0:T(1,128)}, u32[]{:S(2)}) %copy-start.6) | copy-done | bytes 536
  9.5 3.0 %operator.1.refs_5_.refs_6_.refs_9_ = bf16[1024,1024]{1,0:T(8,128)(2,1)S(1)} custom-call(s32[1,128]{1,0:T(1,128)S(1)} %copy-done.6, bf16[128,128,128]{2,1,0:T(8,128)(2,1)} %tiles_ref.1), custom_call_target="tpu_custom_call" | custom-call | bytes 16777216 | tf_op jit(solution)/shard_map/operator/pallas_call | solution.py:155
  14.1 1.5 %collective-permute-start.2 = (bf16[400,256]{1,0:T(8,128)(2,1)S(1)}, bf16[400,256]{1,0:T(8,128)(2,1)S(1)}, u32[]{:S(2)}, u32[]{:S(2)}) collective-permute-start(bf16[400,256]{1,0:T(8,128)(2,1)S(1)} %below.1), channel_id=1, source_target_pairs={{0,4},{4,0},{8,12},{12,8},{1,5},{5,1},{9,13},{13,9},{2,6},{6,2},{1... | collective-permute-start | bytes 614408 | tf_op jit(solution)/shard_map/ppermute | solution.py:593
  15.6 1.5 %collective-permute-start.5 = (bf16[4,128,128]{2,1,0:T(8,128)(2,1)S(1)}, bf16[4,128,128]{2,1,0:T(8,128)(2,1)S(1)}, u32[]{:S(2)}, u32[]{:S(2)}) collective-permute-start(bf16[4,128,128]{2,1,0:T(8,128)(2,1)S(1)} %get-tuple-element.63.refs_0_), channel_id=1, source_target_pairs={{0,2},{2,0},{1,3},{3,1},{4,6},{6,4},{5,7},{7,5},{8,10},{10,8},{9,1... | collective-permute-start | bytes 393224 | tf_op jit(solution)/shard_map/ppermute | solution.py:589
  17.1 5.0 %collective-permute-done.3.came_ref.refs_2_ = bf16[144,512]{1,0:T(8,128)(2,1)S(1)} collective-permute-done((bf16[144,512]{1,0:T(8,128)(2,1)S(1)}, bf16[144,512]{1,0:T(8,128)(2,1)S(1)}, u32[]{:S(2)}, u32[]{:S(2)}) %collective-permute-start.3) | collective-permute-done | bytes 147488 | tf_op jit(solution)/shard_map/ppermute | solution.py:593
  22.2 4.3 %collective-permute-done.4.refs_3_ = bf16[144,256]{1,0:T(8,128)(2,1)S(1)} collective-permute-done((bf16[144,256]{1,0:T(8,128)(2,1)S(1)}, bf16[144,256]{1,0:T(8,128)(2,1)S(1)}, u32[]{:S(2)}, u32[]{:S(2)}) %collective-permute-start.4) | collective-permute-done | bytes 73760 | tf_op jit(solution)/shard_map/ppermute | solution.py:593
  27.1 1.3 %collective-permute-done.6.refs_5_ = bf16[12,128,128]{2,1,0:T(8,128)(2,1)S(1)} collective-permute-done((bf16[12,128,128]{2,1,0:T(8,128)(2,1)S(1)}, bf16[12,128,128]{2,1,0:T(8,128)(2,1)S(1)}, u32[]{:S(2)}, u32[]{:S(2)}) %collective-permute-start.6) | collective-permute-done | bytes 393248 | tf_op jit(solution)/shard_map/ppermute | solution.py:589
  28.4 0.8 %far_rows.1 = (bf16[4,128,128]{2,1,0:T(8,128)(2,1)S(1)}, f32[4,128,128]{2,1,0:T(8,128)S(1)}) custom-call(s32[1,128]{1,0:T(1,128)S(1)} %copy-done.3, s32[1,128]{1,0:T(1,128)S(1)} %copy-done.4, s32[1,128]{1,0:T(1,128)S(1)} %copy-done.5, f32[8,128,128]{2,1,0:T(8,128)S(1)} %get-tuple-element.59.refs_3_, bf16[12,128,128]{2,1,0:T(8,128)(2,1)S(1)} %stack.1.refs_4_, ...), custom_call_target="tpu_custom_call" | custom-call | flops 268435456 | bytes 2097152 | tf_op jit(solution)/shard_map/far_rows/pallas_call | solution.py:358
  29.4 1.2 %collective-permute-done.7.came_ref = bf16[4,128,128]{2,1,0:T(8,128)(2,1)S(1)} collective-permute-done((bf16[4,128,128]{2,1,0:T(8,128)(2,1)S(1)}, bf16[4,128,128]{2,1,0:T(8,128)(2,1)S(1)}, u32[]{:S(2)}, u32[]{:S(2)}) %collective-permute-start.7) | collective-permute-done | bytes 131104 | tf_op jit(solution)/shard_map/ppermute | solution.py:589
  30.6 1.6 %collective-permute-start.8 = (bf16[4,128,128]{2,1,0:T(8,128)(2,1)S(1)}, bf16[4,128,128]{2,1,0:T(8,128)(2,1)S(1)}, u32[]{:S(2)}, u32[]{:S(2)}) collective-permute-start(bf16[4,128,128]{2,1,0:T(8,128)(2,1)S(1)} %add_up.1.refs_0_), channel_id=1, source_target_pairs={{0,2},{2,0},{1,3},{3,1},{4,6},{6,4},{5,7},{7,5},{8,10},{10,8},{9,1... | collective-permute-start | bytes 393224 | tf_op jit(solution)/shard_map/ppermute | solution.py:589
  32.2 4.0 %collective-permute-done.8.refs_1_ = bf16[4,128,128]{2,1,0:T(8,128)(2,1)S(1)} collective-permute-done((bf16[4,128,128]{2,1,0:T(8,128)(2,1)S(1)}, bf16[4,128,128]{2,1,0:T(8,128)(2,1)S(1)}, u32[]{:S(2)}, u32[]{:S(2)}) %collective-permute-start.8) | collective-permute-done | bytes 131104 | tf_op jit(solution)/shard_map/ppermute | solution.py:589
  37.3 1.2 %collective-permute-done.9.refs_4_.came_ref = bf16[128,1024]{1,0:T(8,128)(2,1)S(1)} collective-permute-done((bf16[128,1024]{1,0:T(8,128)(2,1)S(1)}, bf16[128,1024]{1,0:T(8,128)(2,1)S(1)}, u32[]{:S(2)}, u32[]{:S(2)}) %collective-permute-start.9) | collective-permute-done | bytes 262176 | tf_op jit(solution)/shard_map/ppermute | solution.py:589
  39.0 1.5 %collective-permute-start.10 = (bf16[128,512]{1,0:T(8,128)(2,1)S(1)}, bf16[128,512]{1,0:T(8,128)(2,1)S(1)}, u32[]{:S(2)}, u32[]{:S(2)}) collective-permute-start(bf16[128,512]{1,0:T(8,128)(2,1)S(1)} %get-tuple-element.69), channel_id=1, source_target_pairs={{0,8},{4,12},{8,0},{12,4},{1,9},{5,13},{9,1},{13,5},{2,10},{6,14},... | collective-permute-start | bytes 393224 | tf_op jit(solution)/shard_map/ppermute | solution.py:593
  40.5 2.1 %collective-permute-start.11 = (bf16[128,512]{1,0:T(8,128)(2,1)S(1)}, bf16[128,512]{1,0:T(8,128)(2,1)S(1)}, u32[]{:S(2)}, u32[]{:S(2)}) collective-permute-start(bf16[128,512]{1,0:T(8,128)(2,1)S(1)} %get-tuple-element.70), channel_id=1, source_target_pairs={{0,12},{4,8},{8,4},{12,0},{1,13},{5,9},{9,5},{13,1},{2,14},{6,10},... | collective-permute-start | bytes 393224 | tf_op jit(solution)/shard_map/ppermute | solution.py:593
  42.7 0.7 %collective-permute-done.13.came_ref = bf16[128,256]{1,0:T(8,128)(2,1)S(1)} collective-permute-done((bf16[128,256]{1,0:T(8,128)(2,1)S(1)}, bf16[128,256]{1,0:T(8,128)(2,1)S(1)}, u32[]{:S(2)}, u32[]{:S(2)}) %collective-permute-start.13) | collective-permute-done | bytes 65568 | tf_op jit(solution)/shard_map/ppermute | solution.py:593
  43.4 1.2 %collective-permute-done.14.came_ref = bf16[128,128]{1,0:T(8,128)(2,1)S(1)} collective-permute-done((bf16[128,128]{1,0:T(8,128)(2,1)S(1)}, bf16[128,128]{1,0:T(8,128)(2,1)S(1)}, u32[]{:S(2)}, u32[]{:S(2)}) %collective-permute-start.14) | collective-permute-done | bytes 32800 | tf_op jit(solution)/shard_map/ppermute | solution.py:589
  44.6 1.4 %collective-permute-start.15 = (bf16[128,128]{1,0:T(8,128)(2,1)S(1)}, bf16[128,128]{1,0:T(8,128)(2,1)S(1)}, u32[]{:S(2)}, u32[]{:S(2)}) collective-permute-start(bf16[128,128]{1,0:T(8,128)(2,1)S(1)} %pair_sum.2.mine_ref), channel_id=1, source_target_pairs={{0,4},{4,0},{8,12},{12,8},{1,5},{5,1},{9,13},{13,9},{2,6},{6,2},{1... | collective-permute-start | bytes 98312 | tf_op jit(solution)/shard_map/ppermute | solution.py:593
  46.1 7.7 %collective-permute-done.15.came_ref = bf16[128,128]{1,0:T(8,128)(2,1)S(1)} collective-permute-done((bf16[128,128]{1,0:T(8,128)(2,1)S(1)}, bf16[128,128]{1,0:T(8,128)(2,1)S(1)}, u32[]{:S(2)}, u32[]{:S(2)}) %collective-permute-start.15) | collective-permute-done | bytes 32800 | tf_op jit(solution)/shard_map/ppermute | solution.py:593
  53.8 0.9 %late_rows.1.mine_ref = bf16[8,128,128]{2,1,0:T(8,128)(2,1)S(1)} custom-call(s32[1,128]{1,0:T(1,128)S(1)} %copy-done.2, bf16[8,128,128]{2,1,0:T(8,128)(2,1)S(1)} %get-tuple-element.67.refs_1_, f32[128,256]{1,0:T(8,128)S(1)} %get-tuple-element.68.refs_2_, s32[1,128]{1,0:T(1,128)S(1)} %get-tuple-element.57.refs_1_.refs_3_, ...), custom_call_target="tpu_custom_call" | custom-call | flops 134217728 | bytes 1048576 | tf_op jit(solution)/shard_map/late_rows/pallas_call | solution.py:402
  55.3 1.1 %collective-permute-done.17.other_share_ref = f32[128,128]{1,0:T(8,128)S(1)} collective-permute-done((f32[128,128]{1,0:T(8,128)S(1)}, f32[128,128]{1,0:T(8,128)S(1)}, u32[]{:S(2)}, u32[]{:S(2)}) %collective-permute-start.17) | collective-permute-done | bytes 65568 | tf_op jit(solution)/shard_map/ppermute | solution.py:589
  56.4 1.0 %finish.1 = (bf16[8,128,128]{2,1,0:T(8,128)(2,1)}, f32[256,128]{1,0:T(8,128)}, bf16[8,128,128]{2,1,0:T(8,128)(2,1)}) custom-call(bf16[8,128,128]{2,1,0:T(8,128)(2,1)S(1)} %late_rows.1.mine_ref, bf16[8,128,128]{2,1,0:T(8,128)(2,1)S(1)} %collective-permute-done.16.other_ref, f32[128,128]{1,0:T(8,128)S(1)} %pair_sum.3.share_ref, ...), custom_call_target="tpu_custom_call" | custom-call | bytes 262144 | tf_op jit(solution)/shard_map/finish/pallas_call | solution.py:580
  (45 shorter events, 4.5 us)
Async XLA Ops:
  0.6 11.9 %copy-start = (bf16[8,128,128]{2,1,0:T(8,128)(2,1)S(1)}, bf16[8,128,128]{2,1,0:T(8,128)(2,1)}, u32[]{:S(2)}) copy-start(bf16[8,128,128]{2,1,0:T(8,128)(2,1)} %refs_4_.3) | copy-start | bytes 786436
  0.6 11.9 %copy-start.1 = (bf16[8,128,128]{2,1,0:T(8,128)(2,1)S(1)}, bf16[8,128,128]{2,1,0:T(8,128)(2,1)}, u32[]{:S(2)}) copy-start(bf16[8,128,128]{2,1,0:T(8,128)(2,1)} %refs_4_.2) | copy-start | bytes 786436
  3.2 9.4 %copy-start.4 = (s32[1,128]{1,0:T(1,128)S(1)}, s32[1,128]{1,0:T(1,128)}, u32[]{:S(2)}) copy-start(s32[1,128]{1,0:T(1,128)} %get-tuple-element.45.refs_1_) | copy-start | bytes 1540
  3.2 9.4 %copy-start.5 = (s32[1,128]{1,0:T(1,128)S(1)}, s32[1,128]{1,0:T(1,128)}, u32[]{:S(2)}) copy-start(s32[1,128]{1,0:T(1,128)} %get-tuple-element.46.refs_2_) | copy-start | bytes 1540
  3.2 10.7 %collective-permute-start = (bf16[4,128,128]{2,1,0:T(8,128)(2,1)}, bf16[4,128,128]{2,1,0:T(8,128)(2,1)S(1)}, u32[]{:S(2)}, u32[]{:S(2)}) collective-permute-start(bf16[4,128,128]{2,1,0:T(8,128)(2,1)} %get-tuple-element.49), channel_id=1, source_target_pairs={{0,8},{4,12},{8,0},{12,4},{1,9},{5,13},{9,1},{13,5},{2,10},{6,14},... | collective-permute-start | bytes 393224 | tf_op jit(solution)/shard_map/ppermute | solution.py:593
  7.3 6.8 %collective-permute-start.1 = (bf16[4,128,128]{2,1,0:T(8,128)(2,1)}, bf16[4,128,128]{2,1,0:T(8,128)(2,1)S(1)}, u32[]{:S(2)}, u32[]{:S(2)}) collective-permute-start(bf16[4,128,128]{2,1,0:T(8,128)(2,1)} %get-tuple-element.49), channel_id=1, source_target_pairs={{0,4},{4,0},{8,12},{12,8},{1,5},{5,1},{9,13},{13,9},{2,6},{6,2},{1... | collective-permute-start | bytes 393224 | tf_op jit(solution)/shard_map/ppermute | solution.py:593
  9.5 17.2 %copy-start.2 = (s32[1,128]{1,0:T(1,128)S(1)}, s32[1,128]{1,0:T(1,128)}, u32[]{:S(2)}) copy-start(s32[1,128]{1,0:T(1,128)} %get-tuple-element.43.refs_0_) | copy-start | bytes 1540
  13.1 9.1 %collective-permute-start.3 = (bf16[144,512]{1,0:T(8,128)(2,1)S(1)}, bf16[144,512]{1,0:T(8,128)(2,1)S(1)}, u32[]{:S(2)}, u32[]{:S(2)}) collective-permute-start(bf16[144,512]{1,0:T(8,128)(2,1)S(1)} %get-tuple-element.51), channel_id=1, source_target_pairs={{0,8},{4,12},{8,0},{12,4},{1,9},{5,13},{9,1},{13,5},{2,10},{6,14},... | collective-permute-start | bytes 442376 | tf_op jit(solution)/shard_map/ppermute | solution.py:593
  14.1 12.4 %collective-permute-start.2 = (bf16[400,256]{1,0:T(8,128)(2,1)S(1)}, bf16[400,256]{1,0:T(8,128)(2,1)S(1)}, u32[]{:S(2)}, u32[]{:S(2)}) collective-permute-start(bf16[400,256]{1,0:T(8,128)(2,1)S(1)} %below.1), channel_id=1, source_target_pairs={{0,4},{4,0},{8,12},{12,8},{1,5},{5,1},{9,13},{13,9},{2,6},{6,2},{1... | collective-permute-start | bytes 614408 | tf_op jit(solution)/shard_map/ppermute | solution.py:593
  15.6 20.6 %copy-start.7 = (bf16[256,256]{1,0:T(8,128)(2,1)S(1)}, bf16[256,256]{1,0:T(8,128)(2,1)}, u32[]{:S(2)}) copy-start(bf16[256,256]{1,0:T(8,128)(2,1)} %refs_3_.3) | copy-start | bytes 393220
  15.6 6.6 %collective-permute-start.5 = (bf16[4,128,128]{2,1,0:T(8,128)(2,1)S(1)}, bf16[4,128,128]{2,1,0:T(8,128)(2,1)S(1)}, u32[]{:S(2)}, u32[]{:S(2)}) collective-permute-start(bf16[4,128,128]{2,1,0:T(8,128)(2,1)S(1)} %get-tuple-element.63.refs_0_), channel_id=1, source_target_pairs={{0,2},{2,0},{1,3},{3,1},{4,6},{6,4},{5,7},{7,5},{8,10},{10,8},{9,1... | collective-permute-start | bytes 393224 | tf_op jit(solution)/shard_map/ppermute | solution.py:589
  22.2 4.4 %collective-permute-start.4 = (bf16[144,256]{1,0:T(8,128)(2,1)S(1)}, bf16[144,256]{1,0:T(8,128)(2,1)S(1)}, u32[]{:S(2)}, u32[]{:S(2)}) collective-permute-start(bf16[144,256]{1,0:T(8,128)(2,1)S(1)} %pass_on.1), channel_id=1, source_target_pairs={{0,4},{4,0},{8,12},{12,8},{1,5},{5,1},{9,13},{13,9},{2,6},{6,2},{1... | collective-permute-start | bytes 221192 | tf_op jit(solution)/shard_map/ppermute | solution.py:593
  26.6 1.8 %collective-permute-start.6 = (bf16[12,128,128]{2,1,0:T(8,128)(2,1)S(1)}, bf16[12,128,128]{2,1,0:T(8,128)(2,1)S(1)}, u32[]{:S(2)}, u32[]{:S(2)}) collective-permute-start(bf16[12,128,128]{2,1,0:T(8,128)(2,1)S(1)} %stack.1.refs_4_), channel_id=1, source_target_pairs={{0,1},{1,0},{2,3},{3,2},{4,5},{5,4},{6,7},{7,6},{8,9},{9,8},{10,11... | collective-permute-start | bytes 1179656 | tf_op jit(solution)/shard_map/ppermute | solution.py:589
  29.2 1.4 %collective-permute-start.7 = (bf16[4,128,128]{2,1,0:T(8,128)(2,1)S(1)}, bf16[4,128,128]{2,1,0:T(8,128)(2,1)S(1)}, u32[]{:S(2)}, u32[]{:S(2)}) collective-permute-start(bf16[4,128,128]{2,1,0:T(8,128)(2,1)S(1)} %get-tuple-element.62), channel_id=1, source_target_pairs={{0,1},{1,0},{2,3},{3,2},{4,5},{5,4},{6,7},{7,6},{8,9},{9,8},{10,11... | collective-permute-start | bytes 393224 | tf_op jit(solution)/shard_map/ppermute | solution.py:589
  30.6 5.6 %collective-permute-start.8 = (bf16[4,128,128]{2,1,0:T(8,128)(2,1)S(1)}, bf16[4,128,128]{2,1,0:T(8,128)(2,1)S(1)}, u32[]{:S(2)}, u32[]{:S(2)}) collective-permute-start(bf16[4,128,128]{2,1,0:T(8,128)(2,1)S(1)} %add_up.1.refs_0_), channel_id=1, source_target_pairs={{0,2},{2,0},{1,3},{3,1},{4,6},{6,4},{5,7},{7,5},{8,10},{10,8},{9,1... | collective-permute-start | bytes 393224 | tf_op jit(solution)/shard_map/ppermute | solution.py:589
  36.9 1.6 %collective-permute-start.9 = (bf16[128,1024]{1,0:T(8,128)(2,1)S(1)}, bf16[128,1024]{1,0:T(8,128)(2,1)S(1)}, u32[]{:S(2)}, u32[]{:S(2)}) collective-permute-start(bf16[128,1024]{1,0:T(8,128)(2,1)S(1)} %get-tuple-element.66), channel_id=1, source_target_pairs={{0,1},{1,0},{2,3},{3,2},{4,5},{5,4},{6,7},{7,6},{8,9},{9,8},{10,11... | collective-permute-start | bytes 786440 | tf_op jit(solution)/shard_map/ppermute | solution.py:589
  37.0 6.3 %collective-permute-start.13 = (bf16[128,256]{1,0:T(8,128)(2,1)S(1)}, bf16[128,256]{1,0:T(8,128)(2,1)S(1)}, u32[]{:S(2)}, u32[]{:S(2)}) collective-permute-start(bf16[128,256]{1,0:T(8,128)(2,1)S(1)} %get-tuple-element.72.mine_ref), channel_id=1, source_target_pairs={{0,8},{4,12},{8,0},{12,4},{1,9},{5,13},{9,1},{13,5},{2,10},{6,14},... | collective-permute-start | bytes 196616 | tf_op jit(solution)/shard_map/ppermute | solution.py:593
  39.0 14.8 %collective-permute-start.10 = (bf16[128,512]{1,0:T(8,128)(2,1)S(1)}, bf16[128,512]{1,0:T(8,128)(2,1)S(1)}, u32[]{:S(2)}, u32[]{:S(2)}) collective-permute-start(bf16[128,512]{1,0:T(8,128)(2,1)S(1)} %get-tuple-element.69), channel_id=1, source_target_pairs={{0,8},{4,12},{8,0},{12,4},{1,9},{5,13},{9,1},{13,5},{2,10},{6,14},... | collective-permute-start | bytes 393224 | tf_op jit(solution)/shard_map/ppermute | solution.py:593
  40.5 13.3 %collective-permute-start.11 = (bf16[128,512]{1,0:T(8,128)(2,1)S(1)}, bf16[128,512]{1,0:T(8,128)(2,1)S(1)}, u32[]{:S(2)}, u32[]{:S(2)}) collective-permute-start(bf16[128,512]{1,0:T(8,128)(2,1)S(1)} %get-tuple-element.70), channel_id=1, source_target_pairs={{0,12},{4,8},{8,4},{12,0},{1,13},{5,9},{9,5},{13,1},{2,14},{6,10},... | collective-permute-start | bytes 393224 | tf_op jit(solution)/shard_map/ppermute | solution.py:593
  42.7 11.2 %collective-permute-start.12 = (bf16[128,512]{1,0:T(8,128)(2,1)S(1)}, bf16[128,512]{1,0:T(8,128)(2,1)S(1)}, u32[]{:S(2)}, u32[]{:S(2)}) collective-permute-start(bf16[128,512]{1,0:T(8,128)(2,1)S(1)} %get-tuple-element.71), channel_id=1, source_target_pairs={{0,4},{4,0},{8,12},{12,8},{1,5},{5,1},{9,13},{13,9},{2,6},{6,2},{1... | collective-permute-start | bytes 393224 | tf_op jit(solution)/shard_map/ppermute | solution.py:593
  43.4 1.3 %collective-permute-start.14 = (bf16[128,128]{1,0:T(8,128)(2,1)S(1)}, bf16[128,128]{1,0:T(8,128)(2,1)S(1)}, u32[]{:S(2)}, u32[]{:S(2)}) collective-permute-start(bf16[128,128]{1,0:T(8,128)(2,1)S(1)} %get-tuple-element.74), channel_id=1, source_target_pairs={{0,1},{1,0},{2,3},{3,2},{4,5},{5,4},{6,7},{7,6},{8,9},{9,8},{10,11... | collective-permute-start | bytes 98312 | tf_op jit(solution)/shard_map/ppermute | solution.py:589
  44.6 9.1 %collective-permute-start.15 = (bf16[128,128]{1,0:T(8,128)(2,1)S(1)}, bf16[128,128]{1,0:T(8,128)(2,1)S(1)}, u32[]{:S(2)}, u32[]{:S(2)}) collective-permute-start(bf16[128,128]{1,0:T(8,128)(2,1)S(1)} %pair_sum.2.mine_ref), channel_id=1, source_target_pairs={{0,4},{4,0},{8,12},{12,8},{1,5},{5,1},{9,13},{13,9},{2,6},{6,2},{1... | collective-permute-start | bytes 98312 | tf_op jit(solution)/shard_map/ppermute | solution.py:593
  54.7 1.7 %collective-permute-start.16 = (bf16[8,128,128]{2,1,0:T(8,128)(2,1)S(1)}, bf16[8,128,128]{2,1,0:T(8,128)(2,1)S(1)}, u32[]{:S(2)}, u32[]{:S(2)}) collective-permute-start(bf16[8,128,128]{2,1,0:T(8,128)(2,1)S(1)} %late_rows.1.mine_ref), channel_id=1, source_target_pairs={{0,1},{1,0},{2,3},{3,2},{4,5},{5,4},{6,7},{7,6},{8,9},{9,8},{10,11... | collective-permute-start | bytes 786440 | tf_op jit(solution)/shard_map/ppermute | solution.py:589
  54.8 1.6 %collective-permute-start.17 = (f32[128,128]{1,0:T(8,128)S(1)}, f32[128,128]{1,0:T(8,128)S(1)}, u32[]{:S(2)}, u32[]{:S(2)}) collective-permute-start(f32[128,128]{1,0:T(8,128)S(1)} %pair_sum.3.share_ref), channel_id=1, source_target_pairs={{0,1},{1,0},{2,3},{3,2},{4,5},{5,4},{6,7},{7,6},{8,9},{9,8},{10,11... | collective-permute-start | bytes 196616 | tf_op jit(solution)/shard_map/ppermute | solution.py:589
  (2 other events, 10.1 us)

commit v9 on v7

--- a/solution.py
+++ b/solution.py
@@ -119,9 +119,12 @@
         placed.start()
         for c in range(chunks):
             chunk_copy(c).start()
-        placed.wait()
 
     acc[...] = jnp.zeros_like(acc)
+
+    @pl.when(step == 0)
+    def _():
+        pltpu.make_async_copy(place_in, place_ref, sem).wait()
 
     def add_chunk(c, carry):
         @pl.when(step == 0)
@@ -185,12 +188,10 @@
 
 def first_sends_kernel(peers, *refs):
     ask_refs, refs = refs[: peers - 1], refs[peers - 1 :]
-    x3, cot, m_ref, refs = refs[0], refs[1], refs[2], refs[3:]
-    send_refs, self_ref, cot_ref, mir = refs[: peers - 1], refs[peers - 1], refs[peers], refs[peers + 1]
+    x3, m_ref, refs = refs[0], refs[1], refs[2:]
+    send_refs, self_ref, mir = refs[: peers - 1], refs[peers - 1], refs[peers]
     _, columns, width = x3.shape
-    share = cot_ref.shape[0]
     both = CAP * width
-    half = lax.axis_index("rep")
     mirrored(lanes(x3), m_ref, mir, peers * CAP, width)
     self_ref[...] = mir[:, :both]
     lane = lax.broadcasted_iota(jnp.int32, (TAIL, both), 1)
@@ -198,29 +199,22 @@
         out = send_refs[k - 1]
         out[:columns, :] = mir[:, k * both : (k + 1) * both].astype(BF16)
         low, high = ask_refs[k - 1][:, :1], ask_refs[k - 1][:, 1:2]
-        out[columns : columns + TAIL, :] = jnp.where(lane < width, low, high).astype(F32).astype(BF16)
-    for b in range(share):
-        top = columns + TAIL + b // CAP * columns
-        left = b % CAP * width
-        send_refs[0][top : top + columns, left : left + width] = x3[half * share + b]
-    cot_ref[...] = cot[pl.ds(half * share, share)]
-
-
-def first_sends(values, cotangent, operator, asks, peers, reps):
-    blocks_dev, columns, width = values.shape
-    share = blocks_dev // reps
+        out[columns:, :] = jnp.where(lane < width, low, high).astype(F32).astype(BF16)
+
+
+def first_sends(values, operator, asks, peers):
+    _, columns, width = values.shape
     outs = call(
         functools.partial(first_sends_kernel, peers),
         "first_sends",
-        [shape((columns + TAIL + share // CAP * columns, CAP * width), BF16)]
-        + [shape((columns + TAIL, CAP * width), BF16)] * (peers - 2)
-        + [shape((columns, CAP * width), F32), shape((share, columns, width), BF16)],
-        [vmem()] * (peers + 2),
+        [shape((columns + TAIL, CAP * width), BF16)] * (peers - 1)
+        + [shape((columns, CAP * width), F32)],
+        [vmem()] * (peers + 1),
         [pltpu.VMEM((columns, peers * CAP * width), F32)],
         flops=2 ** 28,
         moved=2 ** 21,
-    )(*asks, values, cotangent, operator)
-    return [None] + list(outs[: peers - 1]), outs[peers - 1], outs[peers]
+    )(*asks, values, operator)
+    return [None] + list(outs[: peers - 1]), outs[peers - 1]
 
 
 def add_sums(acc, block, sums):
@@ -292,40 +286,32 @@
     return outs[0], [None] + list(outs[1:])
 
 
-def stack_kernel(below_ref, *refs):
-    out_ref = refs[-1]
-    _, columns, width = out_ref.shape
-    at = (below_ref.shape[0] - TAIL) // columns * CAP - CAP
-    for b in range(at):
-        top = columns + TAIL + b // CAP * columns
-        left = b % CAP * width
-        out_ref[b] = below_ref[top : top + columns, left : left + width]
+def stack_kernel(*refs):
+    at = 0
     for ref in refs[:-1]:
         share = ref.shape[0]
-        out_ref[at : at + share] = ref[...]
+        refs[-1][at : at + share] = ref[...]
         at += share
 
 
-def cut_kernel(in_ref, low_ref, high_ref):
+def halves_kernel(in_ref, low_ref, high_ref):
     share = low_ref.shape[0]
     low_ref[...] = in_ref[:share]
     high_ref[...] = in_ref[share:]
 
 
-def cut(parts):
+def halves(parts):
     if len(parts) > 1:
         return parts
     share, columns, width = parts[0].shape
-    low = share - share // 4
-    outs = [shape((low, columns, width), BF16), shape((share - low, columns, width), BF16)]
-    return list(call(cut_kernel, "cut", outs, [vmem()])(*parts))
-
-
-def stack(below, pieces):
+    part = shape((share // 2, columns, width), BF16)
+    return list(call(halves_kernel, "halves", [part, part], [vmem()])(*parts))
+
+
+def stack(pieces):
     _, columns, width = pieces[0].shape
-    count = (below.shape[0] - TAIL) // columns * CAP - CAP + sum(piece.shape[0] for piece in pieces)
-    out = shape((count, columns, width), BF16)
-    return call(stack_kernel, "stack", out, [vmem()] * (len(pieces) + 1))(below, *pieces)
+    out = shape((sum(piece.shape[0] for piece in pieces), columns, width), BF16)
+    return call(stack_kernel, "stack", out, [vmem()] * len(pieces))(*pieces)
 
 
 def far_rows_kernel(peers, *refs):
@@ -415,17 +401,19 @@
 
 def widen_kernel(feats, *refs):
     out_ref = refs[feats]
-    share, columns, width = refs[0].shape
+    _, columns, width = refs[0].shape
+    share = out_ref.shape[1] // width
+    first = lax.axis_index("rep") * share
     me = lax.axis_index("feat")
     for q in range(feats):
         rows = pl.ds(pl.multiple_of(lax.rem(me + q, feats) * columns, columns), columns)
         for b in range(share):
-            out_ref[rows, b * width : (b + 1) * width] = refs[q][b]
-
-
-def widen(parts):
-    share, columns, width = parts[0].shape
-    out = shape((len(parts) * columns, share * width), BF16)
+            out_ref[rows, b * width : (b + 1) * width] = refs[q][first + b]
+
+
+def widen(parts, reps):
+    blocks_dev, columns, width = parts[0].shape
+    out = shape((len(parts) * columns, blocks_dev // reps * width), BF16)
     kernel = functools.partial(widen_kernel, len(parts))
     return call(kernel, "widen", out, [vmem()] * len(parts))(*parts)
 
@@ -601,37 +589,33 @@
 
     half, place, asks = prepare(features, tile_row, tile_col, tile_count, peers, reps)
     operator = list_operator(tiles, place, peers, blocks_dev)
-    sends, own_mirror, own_cot = first_sends(features, cotangent, operator, asks[1:], peers, reps)
-    middle = peers // 2
-    came = [None] * peers
-    came[middle] = across(sends[middle], peers, middle)
+    sends, own_mirror = first_sends(features, operator, asks[1:], peers)
+    cots = [cotangent] + [ahead(cotangent, "feat", feats, feats - q) for q in range(1, feats)]
     pieces, held = {0: [half]}, [0]
-    bit = middle
+    bit = peers // 2
     while bit:
         for k in held:
-            if k ^ bit == 1:
-                continue
             parts = pieces[k]
             if k:
-                parts = cut(after(parts, sends[1]))
-                parts[-1] = after(parts[-1], came[middle])
+                parts, cots, _ = lax.optimization_barrier(
+                    (halves(after(parts, sends[1])), cots, pieces.get(1, half))
+                )
             pieces[k ^ bit] = [across(part, peers, bit) for part in parts]
         held = held + [k ^ bit for k in held]
         bit //= 2
-    for k in far_first[1:]:
-        send = after(sends[k], pieces[middle]) if k == peers - 1 else sends[k]
-        came[k] = across(send, peers, k)
-    cots = [own_cot] + [ahead(own_cot, "feat", feats, feats - q) for q in range(1, feats)]
-    arrived = [part for k in range(2, peers) for part in pieces[k]]
-    ordered, arrived, cots = lax.optimization_barrier(([came[k] for k in far_first], arrived, cots))
+    came = [None] * peers
+    for k in far_first:
+        came[k] = across(sends[k], peers, k)
+    arrived = [part for k in range(1, peers) for part in pieces[k]]
+    ordered, arrived = lax.optimization_barrier(([came[k] for k in far_first], arrived))
     came = [None] + [ordered[far_first.index(k)] for k in range(1, peers)]
-    stacked = stack(came[1], arrived)
+    stacked = stack(arrived)
     swapped = ahead(stacked, "rep", reps, 1)
     acc, ids = first_rows(features, operator, asks[0], came, own_mirror, peers)
     give, keep = far_rows(acc, asks, stacked, swapped, operator, peers, reps)
 
     mine = add_up(keep, ahead(give, "rep", reps, 1))
-    cot = widen(cots)
+    cot = widen(cots, reps)
     sums = [mine] + [ahead(mine, "feat", feats, feats - q) for q in range(1, feats)]
     act, give, spread, term = dense(sums, cot, weight, feats)
     total = total_term(term, peers, reps)

time: 56.9 us -> 56.3 us (0.989)
  waiting for transfers between devices: 26.4 us -> 24.7 us
  starting transfers between devices: 18.3 us -> 19.6 us
    ppermute x11 -> x12, waiting for transfers between devices: 16.2 us -> 13.6 us  [across(): return lax.ppermute(value, 'graph', [(i, i ^ k) for i in range(peers)])]
    ppermute x8, starting transfers between devices: 2.55 us -> 4.59 us  [ahead(): return lax.ppermute(value, axis, [(i, (i + k) % size) for i in range(size)])]
    ppermute x8, waiting for transfers between devices: 10.3 us -> 11 us  [ahead(): return lax.ppermute(value, axis, [(i, (i + k) % size) for i in range(size)])]
    ppermute x11 -> x12, starting transfers between devices: 15.7 us -> 15 us  [across(): return lax.ppermute(value, 'graph', [(i, i ^ k) for i in range(peers)])]
  transfers between devices with their start and end apart: 19 -> 20, of which waited for: 9 -> 12; matrix products, arithmetic and copies ran while one was open for 0% -> 0% of each run, Pallas kernels for 8% -> 11%
where the time goes in v9:
time: 56.3 us; the launch traced here: 56.2 us
  waiting for transfers between devices  24.7 us (44%)
  starting transfers between devices  19.6 us (35%)
  Pallas kernels  9.7 us (17%)
  between operations  1.51 us (3%)
  local copies, waits for them, and re-layouts  0.69 us (1%)
    ppermute x12, starting transfers between devices, across(): return lax.ppermute(value, 'graph', [(i, i ^ k) for i in range(peers)])  15 us
    ppermute x12, waiting for transfers between devices, across(): return lax.ppermute(value, 'graph', [(i, i ^ k) for i in range(peers)])  13.6 us
    ppermute x8, waiting for transfers between devices, ahead(): return lax.ppermute(value, axis, [(i, (i + k) % size) for i in range(size)])  11 us
    ppermute x8, starting transfers between devices, ahead(): return lax.ppermute(value, axis, [(i, (i + k) % size) for i in range(size)])  4.59 us
    pallas_call x1, Pallas kernels, list_operator(): call(functools.partial(operator_kernel, blocks_dev, slots_here, groups),...  3.04 us
    pallas_call x1, Pallas kernels, prepare(): call(functools.partial(prepare_kernel, peers), 'prepare', [shape((blocks_...  1.81 us
  transfers between devices with their start and end apart: 20, of which 12 were waited for; matrix products, arithmetic and copies ran while one was open for 0% of the time, Pallas kernels for 11%

profile of v9, /device:TPU:0, one launch (start us, length us, event | category | flops | bytes accessed | tf_op | source)
XLA Modules:
  0.0 56.2 jit_solution(11448964881738841127)
XLA Ops:
  0.6 3.0 %collective-permute-start.5 = (bf16[8,128,128]{2,1,0:T(8,128)(2,1)}, bf16[8,128,128]{2,1,0:T(8,128)(2,1)S(1)}, u32[]{:S(2)}, u32[]{:S(2)}) collective-permute-start(bf16[8,128,128]{2,1,0:T(8,128)(2,1)} %refs_0_), channel_id=1, source_target_pairs={{0,2},{2,0},{1,3},{3,1},{4,6},{6,4},{5,7},{7,5},{8,10},{10,8},{9,1... | collective-permute-start | bytes 786440 | tf_op jit(solution)/shard_map/ppermute | solution.py:572
  4.3 1.8 %prepare.1 = (bf16[4,128,128]{2,1,0:T(8,128)(2,1)}, s32[1,128]{1,0:T(1,128)}, s32[1,128]{1,0:T(1,128)}, s32[1,128]{1,0:T(1,128)}, s32[1,128]{1,0:T(1,128)}, /*index=5*/s32[1,128]{1,0:T(1,128)}) custom-call(s32[1]{0:T(128)S(6)} %copy.10.count_ref, s32[1,128]{1,0:T(1,128)} %bitcast.2, s32[1,128]{1,0:T(1,128)} %bitcast.3, bf16[8,128,128]{2,1,0:T(8,128)(2,1)} %refs_4_.1), custom_call_target="tpu_custom_call" | custom-call | bytes 262144 | tf_op jit(solution)/shard_map/prepare/pallas_call | solution.py:90
  6.1 2.7 %collective-permute-start.4 = (bf16[4,128,128]{2,1,0:T(8,128)(2,1)}, bf16[4,128,128]{2,1,0:T(8,128)(2,1)S(1)}, u32[]{:S(2)}, u32[]{:S(2)}) collective-permute-start(bf16[4,128,128]{2,1,0:T(8,128)(2,1)} %get-tuple-element.59), channel_id=1, source_target_pairs={{0,8},{4,12},{8,0},{12,4},{1,9},{5,13},{9,1},{13,5},{2,10},{6,14},... | collective-permute-start | bytes 393224 | tf_op jit(solution)/shard_map/ppermute | solution.py:576
  8.8 1.6 %collective-permute-start.3 = (bf16[4,128,128]{2,1,0:T(8,128)(2,1)}, bf16[4,128,128]{2,1,0:T(8,128)(2,1)S(1)}, u32[]{:S(2)}, u32[]{:S(2)}) collective-permute-start(bf16[4,128,128]{2,1,0:T(8,128)(2,1)} %get-tuple-element.59), channel_id=1, source_target_pairs={{0,4},{4,0},{8,12},{12,8},{1,5},{5,1},{9,13},{13,9},{2,6},{6,2},{1... | collective-permute-start | bytes 393224 | tf_op jit(solution)/shard_map/ppermute | solution.py:576
  11.0 3.0 %operator.1.refs_4_.refs_5_.refs_6_.refs_9_ = bf16[1024,1024]{1,0:T(8,128)(2,1)S(1)} custom-call(s32[1,128]{1,0:T(1,128)S(1)} %copy-done.6, bf16[128,128,128]{2,1,0:T(8,128)(2,1)} %tiles_ref.1), custom_call_target="tpu_custom_call" | custom-call | bytes 16777216 | tf_op jit(solution)/shard_map/operator/pallas_call | solution.py:158
  15.0 2.5 %collective-permute-start.1 = (bf16[144,256]{1,0:T(8,128)(2,1)S(1)}, bf16[144,256]{1,0:T(8,128)(2,1)S(1)}, u32[]{:S(2)}, u32[]{:S(2)}) collective-permute-start(bf16[144,256]{1,0:T(8,128)(2,1)S(1)} %get-tuple-element.57), channel_id=1, source_target_pairs={{0,12},{4,8},{8,4},{12,0},{1,13},{5,9},{9,5},{13,1},{2,14},{6,10},... | collective-permute-start | bytes 221192 | tf_op jit(solution)/shard_map/ppermute | solution.py:576
  18.2 1.4 %collective-permute-start.6 = (bf16[2,128,128]{2,1,0:T(8,128)(2,1)S(1)}, bf16[2,128,128]{2,1,0:T(8,128)(2,1)S(1)}, u32[]{:S(2)}, u32[]{:S(2)}) collective-permute-start(bf16[2,128,128]{2,1,0:T(8,128)(2,1)S(1)} %get-tuple-element.63), channel_id=1, source_target_pairs={{0,4},{4,0},{8,12},{12,8},{1,5},{5,1},{9,13},{13,9},{2,6},{6,2},{1... | collective-permute-start | bytes 196616 | tf_op jit(solution)/shard_map/ppermute | solution.py:576
  20.3 2.0 %collective-permute-done.refs_2_ = bf16[144,256]{1,0:T(8,128)(2,1)S(1)} collective-permute-done((bf16[144,256]{1,0:T(8,128)(2,1)S(1)}, bf16[144,256]{1,0:T(8,128)(2,1)S(1)}, u32[]{:S(2)}, u32[]{:S(2)}) %collective-permute-start) | collective-permute-done | bytes 73760 | tf_op jit(solution)/shard_map/ppermute | solution.py:576
  22.3 1.2 %collective-permute-done.2.refs_1_ = bf16[144,256]{1,0:T(8,128)(2,1)S(1)} collective-permute-done((bf16[144,256]{1,0:T(8,128)(2,1)S(1)}, bf16[144,256]{1,0:T(8,128)(2,1)S(1)}, u32[]{:S(2)}, u32[]{:S(2)}) %collective-permute-start.2) | collective-permute-done | bytes 73760 | tf_op jit(solution)/shard_map/ppermute | solution.py:576
  23.5 1.2 %collective-permute-done.6.refs_2_ = bf16[2,128,128]{2,1,0:T(8,128)(2,1)S(1)} collective-permute-done((bf16[2,128,128]{2,1,0:T(8,128)(2,1)S(1)}, bf16[2,128,128]{2,1,0:T(8,128)(2,1)S(1)}, u32[]{:S(2)}, u32[]{:S(2)}) %collective-permute-start.6) | collective-permute-done | bytes 65568 | tf_op jit(solution)/shard_map/ppermute | solution.py:576
  25.9 1.3 %collective-permute-done.8.refs_5_ = bf16[12,128,128]{2,1,0:T(8,128)(2,1)S(1)} collective-permute-done((bf16[12,128,128]{2,1,0:T(8,128)(2,1)S(1)}, bf16[12,128,128]{2,1,0:T(8,128)(2,1)S(1)}, u32[]{:S(2)}, u32[]{:S(2)}) %collective-permute-start.8) | collective-permute-done | bytes 393248 | tf_op jit(solution)/shard_map/ppermute | solution.py:572
  27.2 0.8 %far_rows.1 = (bf16[4,128,128]{2,1,0:T(8,128)(2,1)S(1)}, f32[4,128,128]{2,1,0:T(8,128)S(1)}) custom-call(s32[1,128]{1,0:T(1,128)S(1)} %copy-done.3, s32[1,128]{1,0:T(1,128)S(1)} %copy-done.4, s32[1,128]{1,0:T(1,128)S(1)} %copy-done.5, f32[8,128,128]{2,1,0:T(8,128)S(1)} %get-tuple-element.72.refs_3_, bf16[12,128,128]{2,1,0:T(8,128)(2,1)S(1)} %stack.1.refs_4_, ...), custom_call_target="tpu_custom_call" | custom-call | flops 268435456 | bytes 2097152 | tf_op jit(solution)/shard_map/far_rows/pallas_call | solution.py:339
  28.2 1.2 %collective-permute-done.9.came_ref = bf16[4,128,128]{2,1,0:T(8,128)(2,1)S(1)} collective-permute-done((bf16[4,128,128]{2,1,0:T(8,128)(2,1)S(1)}, bf16[4,128,128]{2,1,0:T(8,128)(2,1)S(1)}, u32[]{:S(2)}, u32[]{:S(2)}) %collective-permute-start.9) | collective-permute-done | bytes 131104 | tf_op jit(solution)/shard_map/ppermute | solution.py:572
  30.1 5.0 %collective-permute-done.10.refs_1_ = bf16[4,128,128]{2,1,0:T(8,128)(2,1)S(1)} collective-permute-done((bf16[4,128,128]{2,1,0:T(8,128)(2,1)S(1)}, bf16[4,128,128]{2,1,0:T(8,128)(2,1)S(1)}, u32[]{:S(2)}, u32[]{:S(2)}) %collective-permute-start.10) | collective-permute-done | bytes 131104 | tf_op jit(solution)/shard_map/ppermute | solution.py:572
  36.0 1.3 %collective-permute-done.11.refs_4_.came_ref = bf16[128,1024]{1,0:T(8,128)(2,1)S(1)} collective-permute-done((bf16[128,1024]{1,0:T(8,128)(2,1)S(1)}, bf16[128,1024]{1,0:T(8,128)(2,1)S(1)}, u32[]{:S(2)}, u32[]{:S(2)}) %collective-permute-start.11) | collective-permute-done | bytes 262176 | tf_op jit(solution)/shard_map/ppermute | solution.py:572
  37.8 1.5 %collective-permute-start.12 = (bf16[128,512]{1,0:T(8,128)(2,1)S(1)}, bf16[128,512]{1,0:T(8,128)(2,1)S(1)}, u32[]{:S(2)}, u32[]{:S(2)}) collective-permute-start(bf16[128,512]{1,0:T(8,128)(2,1)S(1)} %get-tuple-element.85), channel_id=1, source_target_pairs={{0,8},{4,12},{8,0},{12,4},{1,9},{5,13},{9,1},{13,5},{2,10},{6,14},... | collective-permute-start | bytes 393224 | tf_op jit(solution)/shard_map/ppermute | solution.py:576
  39.3 2.0 %collective-permute-start.13 = (bf16[128,512]{1,0:T(8,128)(2,1)S(1)}, bf16[128,512]{1,0:T(8,128)(2,1)S(1)}, u32[]{:S(2)}, u32[]{:S(2)}) collective-permute-start(bf16[128,512]{1,0:T(8,128)(2,1)S(1)} %get-tuple-element.86), channel_id=1, source_target_pairs={{0,12},{4,8},{8,4},{12,0},{1,13},{5,9},{9,5},{13,1},{2,14},{6,10},... | collective-permute-start | bytes 393224 | tf_op jit(solution)/shard_map/ppermute | solution.py:576
  41.4 0.7 %collective-permute-done.15.came_ref = bf16[128,256]{1,0:T(8,128)(2,1)S(1)} collective-permute-done((bf16[128,256]{1,0:T(8,128)(2,1)S(1)}, bf16[128,256]{1,0:T(8,128)(2,1)S(1)}, u32[]{:S(2)}, u32[]{:S(2)}) %collective-permute-start.15) | collective-permute-done | bytes 65568 | tf_op jit(solution)/shard_map/ppermute | solution.py:576
  42.2 1.2 %collective-permute-done.16.came_ref = bf16[128,128]{1,0:T(8,128)(2,1)S(1)} collective-permute-done((bf16[128,128]{1,0:T(8,128)(2,1)S(1)}, bf16[128,128]{1,0:T(8,128)(2,1)S(1)}, u32[]{:S(2)}, u32[]{:S(2)}) %collective-permute-start.16) | collective-permute-done | bytes 32800 | tf_op jit(solution)/shard_map/ppermute | solution.py:572
  43.4 1.3 %collective-permute-start.17 = (bf16[128,128]{1,0:T(8,128)(2,1)S(1)}, bf16[128,128]{1,0:T(8,128)(2,1)S(1)}, u32[]{:S(2)}, u32[]{:S(2)}) collective-permute-start(bf16[128,128]{1,0:T(8,128)(2,1)S(1)} %pair_sum.2.mine_ref), channel_id=1, source_target_pairs={{0,4},{4,0},{8,12},{12,8},{1,5},{5,1},{9,13},{13,9},{2,6},{6,2},{1... | collective-permute-start | bytes 98312 | tf_op jit(solution)/shard_map/ppermute | solution.py:576
  44.7 7.8 %collective-permute-done.17.came_ref = bf16[128,128]{1,0:T(8,128)(2,1)S(1)} collective-permute-done((bf16[128,128]{1,0:T(8,128)(2,1)S(1)}, bf16[128,128]{1,0:T(8,128)(2,1)S(1)}, u32[]{:S(2)}, u32[]{:S(2)}) %collective-permute-start.17) | collective-permute-done | bytes 32800 | tf_op jit(solution)/shard_map/ppermute | solution.py:576
  52.6 0.9 %late_rows.1.mine_ref = bf16[8,128,128]{2,1,0:T(8,128)(2,1)S(1)} custom-call(s32[1,128]{1,0:T(1,128)S(1)} %copy-done.2, bf16[8,128,128]{2,1,0:T(8,128)(2,1)S(1)} %get-tuple-element.83.refs_1_, f32[128,256]{1,0:T(8,128)S(1)} %get-tuple-element.84.refs_2_, s32[1,128]{1,0:T(1,128)S(1)} %get-tuple-element.70.refs_1_.refs_3_, ...), custom_call_target="tpu_custom_call" | custom-call | flops 134217728 | bytes 1048576 | tf_op jit(solution)/shard_map/late_rows/pallas_call | solution.py:383
  54.1 1.1 %collective-permute-done.19.other_share_ref = f32[128,128]{1,0:T(8,128)S(1)} collective-permute-done((f32[128,128]{1,0:T(8,128)S(1)}, f32[128,128]{1,0:T(8,128)S(1)}, u32[]{:S(2)}, u32[]{:S(2)}) %collective-permute-start.19) | collective-permute-done | bytes 65568 | tf_op jit(solution)/shard_map/ppermute | solution.py:572
  55.2 1.0 %finish.1 = (bf16[8,128,128]{2,1,0:T(8,128)(2,1)}, f32[256,128]{1,0:T(8,128)}, bf16[8,128,128]{2,1,0:T(8,128)(2,1)}) custom-call(bf16[8,128,128]{2,1,0:T(8,128)(2,1)S(1)} %late_rows.1.mine_ref, bf16[8,128,128]{2,1,0:T(8,128)(2,1)S(1)} %collective-permute-done.18.other_ref, f32[128,128]{1,0:T(8,128)S(1)} %pair_sum.3.share_ref, ...), custom_call_target="tpu_custom_call" | custom-call | bytes 262144 | tf_op jit(solution)/shard_map/finish/pallas_call | solution.py:563
  (48 shorter events, 7.2 us)
Async XLA Ops:
  0.6 13.4 %copy-start = (bf16[8,128,128]{2,1,0:T(8,128)(2,1)S(1)}, bf16[8,128,128]{2,1,0:T(8,128)(2,1)}, u32[]{:S(2)}) copy-start(bf16[8,128,128]{2,1,0:T(8,128)(2,1)} %refs_4_.1) | copy-start | bytes 786436
  0.6 17.5 %collective-permute-start.5 = (bf16[8,128,128]{2,1,0:T(8,128)(2,1)}, bf16[8,128,128]{2,1,0:T(8,128)(2,1)S(1)}, u32[]{:S(2)}, u32[]{:S(2)}) collective-permute-start(bf16[8,128,128]{2,1,0:T(8,128)(2,1)} %refs_0_), channel_id=1, source_target_pairs={{0,2},{2,0},{1,3},{3,1},{4,6},{6,4},{5,7},{7,5},{8,10},{10,8},{9,1... | collective-permute-start | bytes 786440 | tf_op jit(solution)/shard_map/ppermute | solution.py:572
  6.1 11.4 %collective-permute-start.4 = (bf16[4,128,128]{2,1,0:T(8,128)(2,1)}, bf16[4,128,128]{2,1,0:T(8,128)(2,1)S(1)}, u32[]{:S(2)}, u32[]{:S(2)}) collective-permute-start(bf16[4,128,128]{2,1,0:T(8,128)(2,1)} %get-tuple-element.59), channel_id=1, source_target_pairs={{0,8},{4,12},{8,0},{12,4},{1,9},{5,13},{9,1},{13,5},{2,10},{6,14},... | collective-permute-start | bytes 393224 | tf_op jit(solution)/shard_map/ppermute | solution.py:576
  8.8 9.4 %collective-permute-start.3 = (bf16[4,128,128]{2,1,0:T(8,128)(2,1)}, bf16[4,128,128]{2,1,0:T(8,128)(2,1)S(1)}, u32[]{:S(2)}, u32[]{:S(2)}) collective-permute-start(bf16[4,128,128]{2,1,0:T(8,128)(2,1)} %get-tuple-element.59), channel_id=1, source_target_pairs={{0,4},{4,0},{8,12},{12,8},{1,5},{5,1},{9,13},{13,9},{2,6},{6,2},{1... | collective-permute-start | bytes 393224 | tf_op jit(solution)/shard_map/ppermute | solution.py:576
  11.0 14.5 %copy-start.2 = (s32[1,128]{1,0:T(1,128)S(1)}, s32[1,128]{1,0:T(1,128)}, u32[]{:S(2)}) copy-start(s32[1,128]{1,0:T(1,128)} %get-tuple-element.51.refs_0_) | copy-start | bytes 1540
  14.6 15.5 %copy-start.1 = (bf16[8,128,128]{2,1,0:T(8,128)(2,1)S(1)}, bf16[8,128,128]{2,1,0:T(8,128)(2,1)}, u32[]{:S(2)}) copy-start(bf16[8,128,128]{2,1,0:T(8,128)(2,1)} %refs_0_) | copy-start | bytes 786436
  14.6 20.5 %copy-start.7 = (bf16[256,256]{1,0:T(8,128)(2,1)S(1)}, bf16[256,256]{1,0:T(8,128)(2,1)}, u32[]{:S(2)}) copy-start(bf16[256,256]{1,0:T(8,128)(2,1)} %refs_3_.3) | copy-start | bytes 393220
  14.6 7.7 %collective-permute-start = (bf16[144,256]{1,0:T(8,128)(2,1)S(1)}, bf16[144,256]{1,0:T(8,128)(2,1)S(1)}, u32[]{:S(2)}, u32[]{:S(2)}) collective-permute-start(bf16[144,256]{1,0:T(8,128)(2,1)S(1)} %get-tuple-element.56), channel_id=1, source_target_pairs={{0,8},{4,12},{8,0},{12,4},{1,9},{5,13},{9,1},{13,5},{2,10},{6,14},... | collective-permute-start | bytes 221192 | tf_op jit(solution)/shard_map/ppermute | solution.py:576
  15.0 7.3 %collective-permute-start.1 = (bf16[144,256]{1,0:T(8,128)(2,1)S(1)}, bf16[144,256]{1,0:T(8,128)(2,1)S(1)}, u32[]{:S(2)}, u32[]{:S(2)}) collective-permute-start(bf16[144,256]{1,0:T(8,128)(2,1)S(1)} %get-tuple-element.57), channel_id=1, source_target_pairs={{0,12},{4,8},{8,4},{12,0},{1,13},{5,9},{9,5},{13,1},{2,14},{6,10},... | collective-permute-start | bytes 221192 | tf_op jit(solution)/shard_map/ppermute | solution.py:576
  17.5 6.0 %collective-permute-start.2 = (bf16[144,256]{1,0:T(8,128)(2,1)S(1)}, bf16[144,256]{1,0:T(8,128)(2,1)S(1)}, u32[]{:S(2)}, u32[]{:S(2)}) collective-permute-start(bf16[144,256]{1,0:T(8,128)(2,1)S(1)} %get-tuple-element.58), channel_id=1, source_target_pairs={{0,4},{4,0},{8,12},{12,8},{1,5},{5,1},{9,13},{13,9},{2,6},{6,2},{1... | collective-permute-start | bytes 221192 | tf_op jit(solution)/shard_map/ppermute | solution.py:576
  18.2 6.5 %collective-permute-start.6 = (bf16[2,128,128]{2,1,0:T(8,128)(2,1)S(1)}, bf16[2,128,128]{2,1,0:T(8,128)(2,1)S(1)}, u32[]{:S(2)}, u32[]{:S(2)}) collective-permute-start(bf16[2,128,128]{2,1,0:T(8,128)(2,1)S(1)} %get-tuple-element.63), channel_id=1, source_target_pairs={{0,4},{4,0},{8,12},{12,8},{1,5},{5,1},{9,13},{13,9},{2,6},{6,2},{1... | collective-permute-start | bytes 196616 | tf_op jit(solution)/shard_map/ppermute | solution.py:576
  19.6 5.8 %collective-permute-start.7 = (bf16[2,128,128]{2,1,0:T(8,128)(2,1)S(1)}, bf16[2,128,128]{2,1,0:T(8,128)(2,1)S(1)}, u32[]{:S(2)}, u32[]{:S(2)}) collective-permute-start(bf16[2,128,128]{2,1,0:T(8,128)(2,1)S(1)} %get-tuple-element.64), channel_id=1, source_target_pairs={{0,4},{4,0},{8,12},{12,8},{1,5},{5,1},{9,13},{13,9},{2,6},{6,2},{1... | collective-permute-start | bytes 196616 | tf_op jit(solution)/shard_map/ppermute | solution.py:576
  25.4 1.8 %collective-permute-start.8 = (bf16[12,128,128]{2,1,0:T(8,128)(2,1)S(1)}, bf16[12,128,128]{2,1,0:T(8,128)(2,1)S(1)}, u32[]{:S(2)}, u32[]{:S(2)}) collective-permute-start(bf16[12,128,128]{2,1,0:T(8,128)(2,1)S(1)} %stack.1.refs_4_), channel_id=1, source_target_pairs={{0,1},{1,0},{2,3},{3,2},{4,5},{5,4},{6,7},{7,6},{8,9},{9,8},{10,11... | collective-permute-start | bytes 1179656 | tf_op jit(solution)/shard_map/ppermute | solution.py:572
  28.0 1.4 %collective-permute-start.9 = (bf16[4,128,128]{2,1,0:T(8,128)(2,1)S(1)}, bf16[4,128,128]{2,1,0:T(8,128)(2,1)S(1)}, u32[]{:S(2)}, u32[]{:S(2)}) collective-permute-start(bf16[4,128,128]{2,1,0:T(8,128)(2,1)S(1)} %get-tuple-element.78), channel_id=1, source_target_pairs={{0,1},{1,0},{2,3},{3,2},{4,5},{5,4},{6,7},{7,6},{8,9},{9,8},{10,11... | collective-permute-start | bytes 393224 | tf_op jit(solution)/shard_map/ppermute | solution.py:572
  29.4 5.6 %collective-permute-start.10 = (bf16[4,128,128]{2,1,0:T(8,128)(2,1)S(1)}, bf16[4,128,128]{2,1,0:T(8,128)(2,1)S(1)}, u32[]{:S(2)}, u32[]{:S(2)}) collective-permute-start(bf16[4,128,128]{2,1,0:T(8,128)(2,1)S(1)} %add_up.1.refs_0_), channel_id=1, source_target_pairs={{0,2},{2,0},{1,3},{3,1},{4,6},{6,4},{5,7},{7,5},{8,10},{10,8},{9,1... | collective-permute-start | bytes 393224 | tf_op jit(solution)/shard_map/ppermute | solution.py:572
  35.7 1.6 %collective-permute-start.11 = (bf16[128,1024]{1,0:T(8,128)(2,1)S(1)}, bf16[128,1024]{1,0:T(8,128)(2,1)S(1)}, u32[]{:S(2)}, u32[]{:S(2)}) collective-permute-start(bf16[128,1024]{1,0:T(8,128)(2,1)S(1)} %get-tuple-element.82), channel_id=1, source_target_pairs={{0,1},{1,0},{2,3},{3,2},{4,5},{5,4},{6,7},{7,6},{8,9},{9,8},{10,11... | collective-permute-start | bytes 786440 | tf_op jit(solution)/shard_map/ppermute | solution.py:572
  35.8 6.3 %collective-permute-start.15 = (bf16[128,256]{1,0:T(8,128)(2,1)S(1)}, bf16[128,256]{1,0:T(8,128)(2,1)S(1)}, u32[]{:S(2)}, u32[]{:S(2)}) collective-permute-start(bf16[128,256]{1,0:T(8,128)(2,1)S(1)} %get-tuple-element.88.mine_ref), channel_id=1, source_target_pairs={{0,8},{4,12},{8,0},{12,4},{1,9},{5,13},{9,1},{13,5},{2,10},{6,14},... | collective-permute-start | bytes 196616 | tf_op jit(solution)/shard_map/ppermute | solution.py:576
  37.8 14.7 %collective-permute-start.12 = (bf16[128,512]{1,0:T(8,128)(2,1)S(1)}, bf16[128,512]{1,0:T(8,128)(2,1)S(1)}, u32[]{:S(2)}, u32[]{:S(2)}) collective-permute-start(bf16[128,512]{1,0:T(8,128)(2,1)S(1)} %get-tuple-element.85), channel_id=1, source_target_pairs={{0,8},{4,12},{8,0},{12,4},{1,9},{5,13},{9,1},{13,5},{2,10},{6,14},... | collective-permute-start | bytes 393224 | tf_op jit(solution)/shard_map/ppermute | solution.py:576
  39.3 13.2 %collective-permute-start.13 = (bf16[128,512]{1,0:T(8,128)(2,1)S(1)}, bf16[128,512]{1,0:T(8,128)(2,1)S(1)}, u32[]{:S(2)}, u32[]{:S(2)}) collective-permute-start(bf16[128,512]{1,0:T(8,128)(2,1)S(1)} %get-tuple-element.86), channel_id=1, source_target_pairs={{0,12},{4,8},{8,4},{12,0},{1,13},{5,9},{9,5},{13,1},{2,14},{6,10},... | collective-permute-start | bytes 393224 | tf_op jit(solution)/shard_map/ppermute | solution.py:576
  41.3 11.2 %collective-permute-start.14 = (bf16[128,512]{1,0:T(8,128)(2,1)S(1)}, bf16[128,512]{1,0:T(8,128)(2,1)S(1)}, u32[]{:S(2)}, u32[]{:S(2)}) collective-permute-start(bf16[128,512]{1,0:T(8,128)(2,1)S(1)} %get-tuple-element.87), channel_id=1, source_target_pairs={{0,4},{4,0},{8,12},{12,8},{1,5},{5,1},{9,13},{13,9},{2,6},{6,2},{1... | collective-permute-start | bytes 393224 | tf_op jit(solution)/shard_map/ppermute | solution.py:576
  42.1 1.3 %collective-permute-start.16 = (bf16[128,128]{1,0:T(8,128)(2,1)S(1)}, bf16[128,128]{1,0:T(8,128)(2,1)S(1)}, u32[]{:S(2)}, u32[]{:S(2)}) collective-permute-start(bf16[128,128]{1,0:T(8,128)(2,1)S(1)} %get-tuple-element.90), channel_id=1, source_target_pairs={{0,1},{1,0},{2,3},{3,2},{4,5},{5,4},{6,7},{7,6},{8,9},{9,8},{10,11... | collective-permute-start | bytes 98312 | tf_op jit(solution)/shard_map/ppermute | solution.py:572
  43.4 9.1 %collective-permute-start.17 = (bf16[128,128]{1,0:T(8,128)(2,1)S(1)}, bf16[128,128]{1,0:T(8,128)(2,1)S(1)}, u32[]{:S(2)}, u32[]{:S(2)}) collective-permute-start(bf16[128,128]{1,0:T(8,128)(2,1)S(1)} %pair_sum.2.mine_ref), channel_id=1, source_target_pairs={{0,4},{4,0},{8,12},{12,8},{1,5},{5,1},{9,13},{13,9},{2,6},{6,2},{1... | collective-permute-start | bytes 98312 | tf_op jit(solution)/shard_map/ppermute | solution.py:576
  53.5 1.7 %collective-permute-start.18 = (bf16[8,128,128]{2,1,0:T(8,128)(2,1)S(1)}, bf16[8,128,128]{2,1,0:T(8,128)(2,1)S(1)}, u32[]{:S(2)}, u32[]{:S(2)}) collective-permute-start(bf16[8,128,128]{2,1,0:T(8,128)(2,1)S(1)} %late_rows.1.mine_ref), channel_id=1, source_target_pairs={{0,1},{1,0},{2,3},{3,2},{4,5},{5,4},{6,7},{7,6},{8,9},{9,8},{10,11... | collective-permute-start | bytes 786440 | tf_op jit(solution)/shard_map/ppermute | solution.py:572
  53.6 1.6 %collective-permute-start.19 = (f32[128,128]{1,0:T(8,128)S(1)}, f32[128,128]{1,0:T(8,128)S(1)}, u32[]{:S(2)}, u32[]{:S(2)}) collective-permute-start(f32[128,128]{1,0:T(8,128)S(1)} %pair_sum.3.share_ref), channel_id=1, source_target_pairs={{0,1},{1,0},{2,3},{3,2},{4,5},{5,4},{6,7},{7,6},{8,9},{9,8},{10,11... | collective-permute-start | bytes 196616 | tf_op jit(solution)/shard_map/ppermute | solution.py:572
  (4 other events, 24.6 us)

commit v10 on v9

--- a/solution.py
+++ b/solution.py
@@ -11,6 +11,8 @@
 GROUP = 8
 CHUNK = 16
 SIDES = 2
+PLACE_ROWS = 8
+PLACE_BUFFER = 2 ** 22
 TAIL = 16
 VMEM_LIMIT = 40 * 2 ** 20
 VMEM_MOST = 50 * 2 ** 20
@@ -77,11 +79,16 @@
     return place
 
 
-def prepare_kernel(peers, count_ref, row_ref, col_ref, x3, half_ref, place_ref, *ask_refs):
+def prepare_kernel(peers, count_ref, row_ref, col_ref, x3, half_ref, place_out, *refs):
+    ask_refs, place_ref, sem = refs[:peers], refs[peers], refs[peers + 1]
     share = half_ref.shape[0]
     half_ref[...] = x3[pl.ds(lax.axis_index("rep") * share, share)]
     count = jnp.broadcast_to(count_ref[...], (1, 1))
-    place_ref[...] = places(peers, x3.shape[0], count, row_ref[...], col_ref[...], ask_refs)
+    place = places(peers, x3.shape[0], count, row_ref[...], col_ref[...], ask_refs)
+    place_ref[...] = jnp.broadcast_to(place, place_ref.shape)
+    copy = pltpu.make_async_copy(place_ref, place_out.at[pl.ds(0, PLACE_ROWS)], sem)
+    copy.start()
+    copy.wait()
 
 
 def prepare(features, tile_row, tile_col, tile_count, peers, reps):
@@ -90,8 +97,11 @@
     outs = call(
         functools.partial(prepare_kernel, peers),
         "prepare",
-        [shape((blocks_dev // reps, columns, width), BF16)] + [shape((1, per), jnp.int32)] * (peers + 1),
+        [shape((blocks_dev // reps, columns, width), BF16), shape((PLACE_BUFFER // (4 * per), per), jnp.int32)]
+        + [shape((1, per), jnp.int32)] * peers,
         [vmem()] * 4,
+        [pltpu.VMEM((PLACE_ROWS, per), jnp.int32), pltpu.SemaphoreType.DMA],
+        out_specs=[vmem(), hbm()] + [vmem()] * peers,
         limit=VMEM_ALL,
     )(tile_count, tile_row.reshape(1, per), tile_col.reshape(1, per), features)
     return outs[0], outs[1], list(outs[2:])
@@ -113,10 +123,12 @@
         part = pl.ds(c * CHUNK, CHUNK)
         return pltpu.make_async_copy(tiles_ref.at[part], tiles.at[part], sems.at[c])
 
+    def place_copy():
+        return pltpu.make_async_copy(place_in.at[pl.ds(0, PLACE_ROWS)], place_ref, sem)
+
     @pl.when(step == 0)
     def _():
-        placed = pltpu.make_async_copy(place_in, place_ref, sem)
-        placed.start()
+        place_copy().start()
         for c in range(chunks):
             chunk_copy(c).start()
 
@@ -124,7 +136,7 @@
 
     @pl.when(step == 0)
     def _():
-        pltpu.make_async_copy(place_in, place_ref, sem).wait()
+        place_copy().wait()
 
     def add_chunk(c, carry):
         @pl.when(step == 0)
@@ -159,11 +171,11 @@
         functools.partial(operator_kernel, blocks_dev, slots_here, groups),
         "operator",
         shape((blocks_dev * width, slots * width), BF16),
-        [pl.BlockSpec(memory_space=pl.ANY), hbm()],
+        [hbm(), hbm()],
         [
             pltpu.VMEM((per, width, width), BF16),
             pltpu.VMEM((SIDES, slots_here * blocks_dev + 1, width, width), F32),
-            pltpu.SMEM((1, per), jnp.int32),
+            pltpu.SMEM((PLACE_ROWS, per), jnp.int32),
             pltpu.SemaphoreType.DMA((per // CHUNK,)),
             pltpu.SemaphoreType.DMA,
         ],
@@ -231,13 +243,6 @@
     for b in range(blocks_dev):
         add = own[:, b * width : (b + 1) * width]
         acc[b] = add if before is None else before[b] + add
-
-
-def split_rows(acc, give_ref, keep_ref):
-    half = lax.axis_index("rep")
-    share = give_ref.shape[0]
-    give_ref[...] = acc[pl.ds((1 - half) * share, share)].astype(BF16)
-    keep_ref[...] = acc[pl.ds(half * share, share)]
 
 
 def self_rows(x3, m_ref, ask_ref):
@@ -314,41 +319,66 @@
     return call(stack_kernel, "stack", out, [vmem()] * len(pieces))(*pieces)
 
 
-def far_rows_kernel(peers, *refs):
-    ask_refs, refs = refs[: peers - 1], refs[peers - 1 :]
-    before, mine_ref, other_ref, m_ref, give_ref, keep_ref, acc, block, far = refs
-    both = CAP * acc.shape[2]
-    for k in range(1, peers):
-        far[:, k * both : (k + 1) * both] = far_of(block, mine_ref, other_ref, ask_refs[k - 1], k - 1)
-    if peers * CAP <= GROUP:
-        own = dot(far[:, both:], m_ref[:, both:], NT)
+def half_rows(before, far_ref, m_ref, first, share):
+    columns, width = before.shape[1:]
+    both = CAP * width
+    rows = pl.ds(pl.multiple_of(first * width, share * width), share * width)
+    if m_ref.shape[1] <= GROUP * width:
+        own = dot(far_ref[:, both:], m_ref[rows, both:], NT)
     else:
 
         def add_peer(k, total):
             here = pl.ds(pl.multiple_of(k * both, both), both)
-            return total + dot(far[:, here], m_ref[:, here], NT)
-
-        own = lax.fori_loop(1, peers, add_peer, jnp.zeros((acc.shape[1], m_ref.shape[0]), F32))
-    put_rows(acc, own, before)
-    split_rows(acc, give_ref, keep_ref)
-
-
-def far_rows(before, asks, mine, other, operator, peers, reps):
+            return total + dot(far_ref[:, here], m_ref[rows, here], NT)
+
+        zeros = jnp.zeros((columns, share * width), F32)
+        own = lax.fori_loop(1, m_ref.shape[1] // both, add_peer, zeros)
+    return [before[first + b] + own[:, b * width : (b + 1) * width] for b in range(share)]
+
+
+def give_rows_kernel(peers, *refs):
+    ask_refs, refs = refs[: peers - 1], refs[peers - 1 :]
+    before, mine_ref, other_ref, m_ref, give_ref, far_ref, block = refs
+    both = CAP * before.shape[2]
+    for k in range(1, peers):
+        far_ref[:, k * both : (k + 1) * both] = far_of(block, mine_ref, other_ref, ask_refs[k - 1], k - 1)
+    far_ref[:, :both] = jnp.zeros((far_ref.shape[0], both), BF16)
+    share = give_ref.shape[0]
+    rows = half_rows(before, far_ref, m_ref, (1 - lax.axis_index("rep")) * share, share)
+    for b in range(share):
+        give_ref[b] = rows[b].astype(BF16)
+
+
+def give_rows(before, asks, mine, other, operator, peers, reps):
     blocks_dev, columns, width = before.shape
-    share = (blocks_dev // reps, columns, width)
     return call(
-        functools.partial(far_rows_kernel, peers),
-        "far_rows",
-        [shape(share, BF16), shape(share, F32)],
+        functools.partial(give_rows_kernel, peers),
+        "give_rows",
+        [shape((blocks_dev // reps, columns, width), BF16), shape((columns, peers * CAP * width), BF16)],
         [vmem()] * (peers + 3),
-        [
-            pltpu.VMEM(before.shape, F32),
-            pltpu.VMEM(before.shape, BF16),
-            pltpu.VMEM((columns, peers * CAP * width), BF16),
-        ],
-        flops=2 ** 28,
-        moved=2 ** 21,
+        [pltpu.VMEM(before.shape, BF16)],
+        flops=2 ** 27,
+        moved=2 ** 20,
     )(*asks[1:], before, mine, other, operator)
+
+
+def keep_rows_kernel(before, far_ref, m_ref, keep_ref):
+    share = keep_ref.shape[0]
+    rows = half_rows(before, far_ref, m_ref, lax.axis_index("rep") * share, share)
+    for b in range(share):
+        keep_ref[b] = rows[b]
+
+
+def keep_rows(before, far, operator, reps):
+    blocks_dev, columns, width = before.shape
+    return call(
+        keep_rows_kernel,
+        "keep_rows",
+        shape((blocks_dev // reps, columns, width), F32),
+        [vmem()] * 3,
+        flops=2 ** 27,
+        moved=2 ** 20,
+    )(before, far, operator)
 
 
 def late_rows_kernel(ks, first, last, *refs):
@@ -515,57 +545,57 @@
     return call(pair_kernel, "pair_sum", shape(mine.shape, dtype), [vmem(), vmem()])(mine, came)
 
 
-def split_kernel(mine_ref, came_ref, give_ref, keep_ref, total):
+def split_kernel(mine_ref, came_ref, act_ref, shared_ref, give_ref, keep_ref, out_ref, total):
     half = lax.axis_index("rep")
+    blocks, _, width = act_ref.shape
+    out_ref[pl.ds(half * blocks, blocks)] = act_ref[...]
+    for b in range(blocks):
+        at = (blocks + b) * width
+        out_ref[(1 - half) * blocks + b] = shared_ref[:, at : at + width]
     part = keep_ref.shape[1]
     total[...] = mine_ref[...].astype(F32) + came_ref[...].astype(F32)
     give_ref[...] = total[:, pl.ds(pl.multiple_of((1 - half) * part, part), part)].astype(BF16)
     keep_ref[...] = total[:, pl.ds(pl.multiple_of(half * part, part), part)]
 
 
-def split_sum(mine, came, reps):
+def split_sum(mine, came, act, shared, reps):
     columns, features = mine.shape
     part = (columns, features // reps)
     return call(
         split_kernel,
         "split_sum",
-        [shape(part, BF16), shape(part, F32)],
-        [vmem(), vmem()],
+        [shape(part, BF16), shape(part, F32), shape((reps * act.shape[0],) + act.shape[1:], BF16)],
+        [vmem()] * 4,
         [pltpu.VMEM(mine.shape, F32)],
-    )(mine, came)
-
-
-def total_term(term, peers, reps):
+    )(mine, came, act, shared)
+
+
+def total_term(term, act, shared, peers, reps):
     bit = peers // 2
-    give, total = split_sum(term, across(term, peers, bit), reps)
+    give, total, activated = split_sum(term, across(term, peers, bit), act, shared, reps)
     total = pair_sum(total, ahead(give, "rep", reps, 1), F32 if bit == 1 else BF16)
     while bit > 1:
         bit //= 2
         total = pair_sum(total, across(total, peers, bit), F32 if bit == 1 else BF16)
-    return total
-
-
-def finish_kernel(mine_ref, other_ref, share_ref, other_share_ref, act_ref, came_ref, grad_ref, weight_ref, out_ref):
+    return total, activated
+
+
+def finish_kernel(mine_ref, other_ref, share_ref, other_share_ref, grad_ref, weight_ref):
     half = lax.axis_index("rep")
     share = share_ref.shape[1]
     grad_ref[...] = (mine_ref[...].astype(F32) + other_ref[...].astype(F32)).astype(BF16)
     weight_ref[pl.ds(pl.multiple_of(half * share, share), share), :] = share_ref[...].T
     weight_ref[pl.ds(pl.multiple_of((1 - half) * share, share), share), :] = other_share_ref[...].T
-    blocks, _, width = act_ref.shape
-    out_ref[pl.ds(half * blocks, blocks)] = act_ref[...]
-    for b in range(blocks):
-        at = (blocks + b) * width
-        out_ref[(1 - half) * blocks + b] = came_ref[:, at : at + width]
-
-
-def finish(mine, other, share, other_share, act, came):
+
+
+def finish(mine, other, share, other_share):
     columns, width = share.shape
     return call(
         finish_kernel,
         "finish",
-        [shape(mine.shape, BF16), shape((2 * width, columns), F32), shape(mine.shape, BF16)],
-        [vmem()] * 6,
-    )(mine, other, share, other_share, act, came)
+        [shape(mine.shape, BF16), shape((2 * width, columns), F32)],
+        [vmem()] * 4,
+    )(mine, other, share, other_share)
 
 
 def ahead(value, axis, size, k):
@@ -607,19 +637,21 @@
     for k in far_first:
         came[k] = across(sends[k], peers, k)
     arrived = [part for k in range(1, peers) for part in pieces[k]]
-    ordered, arrived = lax.optimization_barrier(([came[k] for k in far_first], arrived))
-    came = [None] + [ordered[far_first.index(k)] for k in range(1, peers)]
+    middle = peers // 2
+    came[middle:], arrived = lax.optimization_barrier((came[middle:], arrived))
+    came[1:middle], arrived = lax.optimization_barrier((came[1:middle], arrived))
     stacked = stack(arrived)
     swapped = ahead(stacked, "rep", reps, 1)
     acc, ids = first_rows(features, operator, asks[0], came, own_mirror, peers)
-    give, keep = far_rows(acc, asks, stacked, swapped, operator, peers, reps)
+    give, asked = give_rows(acc, asks, stacked, swapped, operator, peers, reps)
+    keep = keep_rows(acc, asked, operator, reps)
 
     mine = add_up(keep, ahead(give, "rep", reps, 1))
     cot = widen(cots, reps)
     sums = [mine] + [ahead(mine, "feat", feats, feats - q) for q in range(1, feats)]
     act, give, spread, term = dense(sums, cot, weight, feats)
-    total = total_term(term, peers, reps)
     shared = ahead(give, "rep", reps, 1)
+    total, activated = total_term(term, act, shared, peers, reps)
     values, sends, own_mirror = sends_of(spread, shared, operator, ids, peers, reps)
 
     came = [None] * peers
@@ -627,9 +659,10 @@
         came[k] = across(sends[k], peers, k)
     ordered, total = lax.optimization_barrier(([came[k] for k in far_first], total))
     came = [None] + [ordered[far_first.index(k)] for k in range(1, peers)]
-    part = late_rows([asks[0], values, own_mirror], ids, came, far_first, operator, True, True)
-    input_grad, weight_grad, activated = finish(
-        part, ahead(part, "rep", reps, 1), total, ahead(total, "rep", reps, 1), act, shared
+    acc = late_rows([asks[0], values, own_mirror], ids, came, [], operator, True, False)
+    part = late_rows([acc], ids, came, far_first, operator, False, True)
+    input_grad, weight_grad = finish(
+        part, ahead(part, "rep", reps, 1), total, ahead(total, "rep", reps, 1)
     )
     return (activated, input_grad, weight_grad)
 

time: 56.3 us -> 56.3 us (level)
  waiting for transfers between devices: 24.7 us -> 19.3 us
  starting transfers between devices: 19.6 us -> 24.1 us
  Pallas kernels: 9.7 us -> 11.3 us
  local copies, waits for them, and re-layouts: 0.69 us -> 0.03 us
    ppermute x12, starting transfers between devices: 15 us -> 19.6 us  [across(): return lax.ppermute(value, 'graph', [(i, i ^ k) for i in range(peers)])]
    ppermute x12, waiting for transfers between devices: 13.6 us -> 9.47 us  [across(): return lax.ppermute(value, 'graph', [(i, i ^ k) for i in range(peers)])]
    ppermute x8, waiting for transfers between devices: 11 us -> 9.79 us  [ahead(): return lax.ppermute(value, axis, [(i, (i + k) % size) for i in range(size)])]
    pallas_call x2 -> x3, Pallas kernels: 0.82 us -> 1.63 us  [the longest x1 0.74 us: split_sum(): call(split_kernel, 'split_sum', [shape(part, BF16), shape(part, F32), sha...]
    pallas_call x1, Pallas kernels: 1.81 us -> 2.49 us  [prepare(): call(functools.partial(prepare_kernel, peers), 'prepare', [shape((blocks_...]
    unnamed x16 -> x14, local copies, waits for them, and re-layouts: 0.69 us -> 0.03 us
  transfers between devices with their start and end apart: 20 -> 20, of which waited for: 12 -> 11; matrix products, arithmetic and copies ran while one was open for 0% -> 0% of each run, Pallas kernels for 11% -> 15%
where the time goes in v10:
time: 56.3 us; the launch traced here: 56.2 us
  starting transfers between devices  24.1 us (43%)
  waiting for transfers between devices  19.3 us (34%)
  Pallas kernels  11.3 us (20%)
  between operations  1.51 us (3%)
    ppermute x12, starting transfers between devices, across(): return lax.ppermute(value, 'graph', [(i, i ^ k) for i in range(peers)])  19.6 us
    ppermute x8, waiting for transfers between devices, ahead(): return lax.ppermute(value, axis, [(i, (i + k) % size) for i in range(size)])  9.79 us
    ppermute x12, waiting for transfers between devices, across(): return lax.ppermute(value, 'graph', [(i, i ^ k) for i in range(peers)])  9.47 us
    ppermute x8, starting transfers between devices, ahead(): return lax.ppermute(value, axis, [(i, (i + k) % size) for i in range(size)])  4.51 us
    pallas_call x1, Pallas kernels, list_operator(): call(functools.partial(operator_kernel, blocks_dev, slots_here, groups),...  3.07 us
    pallas_call x1, Pallas kernels, prepare(): call(functools.partial(prepare_kernel, peers), 'prepare', [shape((blocks_...  2.49 us
  transfers between devices with their start and end apart: 20, of which 11 were waited for; matrix products, arithmetic and copies ran while one was open for 0% of the time, Pallas kernels for 15%

profile of v10, /device:TPU:0, one launch (start us, length us, event | category | flops | bytes accessed | tf_op | source)
XLA Modules:
  0.0 56.2 jit_solution(3243972432946128231)
XLA Ops:
  0.6 3.0 %collective-permute-start.5 = (bf16[8,128,128]{2,1,0:T(8,128)(2,1)}, bf16[8,128,128]{2,1,0:T(8,128)(2,1)S(1)}, u32[]{:S(2)}, u32[]{:S(2)}) collective-permute-start(bf16[8,128,128]{2,1,0:T(8,128)(2,1)} %refs_0_), channel_id=1, source_target_pairs={{0,2},{2,0},{1,3},{3,1},{4,6},{6,4},{5,7},{7,5},{8,10},{10,8},{9,1... | collective-permute-start | bytes 786440 | tf_op jit(solution)/shard_map/ppermute | solution.py:602
  4.3 2.5 %prepare.1 = (bf16[4,128,128]{2,1,0:T(8,128)(2,1)}, s32[8192,128]{1,0:T(8,128)}, s32[1,128]{1,0:T(1,128)}, s32[1,128]{1,0:T(1,128)}, s32[1,128]{1,0:T(1,128)}, /*index=5*/s32[1,128]{1,0:T(1,128)}) custom-call(s32[1]{0:T(128)S(6)} %copy.10.count_ref, s32[1,128]{1,0:T(1,128)} %bitcast.2, s32[1,128]{1,0:T(1,128)} %bitcast.3, bf16[8,128,128]{2,1,0:T(8,128)(2,1)} %refs_4_.1), custom_call_target="tpu_custom_call" | custom-call | bytes 262144 | tf_op jit(solution)/shard_map/prepare/pallas_call | solution.py:97
  6.8 2.7 %collective-permute-start.4 = (bf16[4,128,128]{2,1,0:T(8,128)(2,1)}, bf16[4,128,128]{2,1,0:T(8,128)(2,1)S(1)}, u32[]{:S(2)}, u32[]{:S(2)}) collective-permute-start(bf16[4,128,128]{2,1,0:T(8,128)(2,1)} %get-tuple-element.63), channel_id=1, source_target_pairs={{0,8},{4,12},{8,0},{12,4},{1,9},{5,13},{9,1},{13,5},{2,10},{6,14},... | collective-permute-start | bytes 393224 | tf_op jit(solution)/shard_map/ppermute | solution.py:606
  9.4 1.6 %collective-permute-start.3 = (bf16[4,128,128]{2,1,0:T(8,128)(2,1)}, bf16[4,128,128]{2,1,0:T(8,128)(2,1)S(1)}, u32[]{:S(2)}, u32[]{:S(2)}) collective-permute-start(bf16[4,128,128]{2,1,0:T(8,128)(2,1)} %get-tuple-element.63), channel_id=1, source_target_pairs={{0,4},{4,0},{8,12},{12,8},{1,5},{5,1},{9,13},{13,9},{2,6},{6,2},{1... | collective-permute-start | bytes 393224 | tf_op jit(solution)/shard_map/ppermute | solution.py:606
  11.0 3.1 %operator.1.refs_4_.refs_5_.refs_6_.m_ref.refs_3_.refs_7_ = bf16[1024,1024]{1,0:T(8,128)(2,1)S(1)} custom-call(s32[8192,128]{1,0:T(8,128)} %get-tuple-element.59.place_in, bf16[128,128,128]{2,1,0:T(8,128)(2,1)} %tiles_ref.1), custom_call_target="tpu_custom_call" | custom-call | bytes 16777216 | tf_op jit(solution)/shard_map/operator/pallas_call | solution.py:170
  15.0 2.5 %collective-permute-start.2 = (bf16[144,256]{1,0:T(8,128)(2,1)S(1)}, bf16[144,256]{1,0:T(8,128)(2,1)S(1)}, u32[]{:S(2)}, u32[]{:S(2)}) collective-permute-start(bf16[144,256]{1,0:T(8,128)(2,1)S(1)} %get-tuple-element.62), channel_id=1, source_target_pairs={{0,12},{4,8},{8,4},{12,0},{1,13},{5,9},{9,5},{13,1},{2,14},{6,10},... | collective-permute-start | bytes 221192 | tf_op jit(solution)/shard_map/ppermute | solution.py:606
  17.5 0.7 %collective-permute-start = (bf16[144,256]{1,0:T(8,128)(2,1)S(1)}, bf16[144,256]{1,0:T(8,128)(2,1)S(1)}, u32[]{:S(2)}, u32[]{:S(2)}) collective-permute-start(bf16[144,256]{1,0:T(8,128)(2,1)S(1)} %get-tuple-element.60), channel_id=1, source_target_pairs={{0,4},{4,0},{8,12},{12,8},{1,5},{5,1},{9,13},{13,9},{2,6},{6,2},{1... | collective-permute-start | bytes 221192 | tf_op jit(solution)/shard_map/ppermute | solution.py:606
  18.2 1.4 %collective-permute-start.6 = (bf16[2,128,128]{2,1,0:T(8,128)(2,1)S(1)}, bf16[2,128,128]{2,1,0:T(8,128)(2,1)S(1)}, u32[]{:S(2)}, u32[]{:S(2)}) collective-permute-start(bf16[2,128,128]{2,1,0:T(8,128)(2,1)S(1)} %get-tuple-element.67), channel_id=1, source_target_pairs={{0,4},{4,0},{8,12},{12,8},{1,5},{5,1},{9,13},{13,9},{2,6},{6,2},{1... | collective-permute-start | bytes 196616 | tf_op jit(solution)/shard_map/ppermute | solution.py:606
  20.3 2.0 %collective-permute-done.1.refs_2_ = bf16[144,256]{1,0:T(8,128)(2,1)S(1)} collective-permute-done((bf16[144,256]{1,0:T(8,128)(2,1)S(1)}, bf16[144,256]{1,0:T(8,128)(2,1)S(1)}, u32[]{:S(2)}, u32[]{:S(2)}) %collective-permute-start.1) | collective-permute-done | bytes 73760 | tf_op jit(solution)/shard_map/ppermute | solution.py:606
  22.3 2.4 %collective-permute-done.6.refs_2_ = bf16[2,128,128]{2,1,0:T(8,128)(2,1)S(1)} collective-permute-done((bf16[2,128,128]{2,1,0:T(8,128)(2,1)S(1)}, bf16[2,128,128]{2,1,0:T(8,128)(2,1)S(1)}, u32[]{:S(2)}, u32[]{:S(2)}) %collective-permute-start.6) | collective-permute-done | bytes 65568 | tf_op jit(solution)/shard_map/ppermute | solution.py:606
  24.7 0.7 %collective-permute-done.7.refs_3_ = bf16[2,128,128]{2,1,0:T(8,128)(2,1)S(1)} collective-permute-done((bf16[2,128,128]{2,1,0:T(8,128)(2,1)S(1)}, bf16[2,128,128]{2,1,0:T(8,128)(2,1)S(1)}, u32[]{:S(2)}, u32[]{:S(2)}) %collective-permute-start.7) | collective-permute-done | bytes 65568 | tf_op jit(solution)/shard_map/ppermute | solution.py:606
  26.0 1.3 %collective-permute-done.8.refs_5_ = bf16[12,128,128]{2,1,0:T(8,128)(2,1)S(1)} collective-permute-done((bf16[12,128,128]{2,1,0:T(8,128)(2,1)S(1)}, bf16[12,128,128]{2,1,0:T(8,128)(2,1)S(1)}, u32[]{:S(2)}, u32[]{:S(2)}) %collective-permute-start.8) | collective-permute-done | bytes 393248 | tf_op jit(solution)/shard_map/ppermute | solution.py:602
  28.3 0.8 %collective-permute-done.9.came_ref = bf16[4,128,128]{2,1,0:T(8,128)(2,1)S(1)} collective-permute-done((bf16[4,128,128]{2,1,0:T(8,128)(2,1)S(1)}, bf16[4,128,128]{2,1,0:T(8,128)(2,1)S(1)}, u32[]{:S(2)}, u32[]{:S(2)}) %collective-permute-start.9) | collective-permute-done | bytes 131104 | tf_op jit(solution)/shard_map/ppermute | solution.py:602
  29.8 5.0 %collective-permute-done.10.refs_1_ = bf16[4,128,128]{2,1,0:T(8,128)(2,1)S(1)} collective-permute-done((bf16[4,128,128]{2,1,0:T(8,128)(2,1)S(1)}, bf16[4,128,128]{2,1,0:T(8,128)(2,1)S(1)}, u32[]{:S(2)}, u32[]{:S(2)}) %collective-permute-start.10) | collective-permute-done | bytes 131104 | tf_op jit(solution)/shard_map/ppermute | solution.py:602
  35.5 1.1 %collective-permute-start.11 = (bf16[128,256]{1,0:T(8,128)(2,1)S(1)}, bf16[128,256]{1,0:T(8,128)(2,1)S(1)}, u32[]{:S(2)}, u32[]{:S(2)}) collective-permute-start(bf16[128,256]{1,0:T(8,128)(2,1)S(1)} %get-tuple-element.86.mine_ref), channel_id=1, source_target_pairs={{0,8},{4,12},{8,0},{12,4},{1,9},{5,13},{9,1},{13,5},{2,10},{6,14},... | collective-permute-start | bytes 196616 | tf_op jit(solution)/shard_map/ppermute | solution.py:606
  37.5 1.5 %collective-permute-start.13 = (bf16[128,512]{1,0:T(8,128)(2,1)S(1)}, bf16[128,512]{1,0:T(8,128)(2,1)S(1)}, u32[]{:S(2)}, u32[]{:S(2)}) collective-permute-start(bf16[128,512]{1,0:T(8,128)(2,1)S(1)} %get-tuple-element.96), channel_id=1, source_target_pairs={{0,8},{4,12},{8,0},{12,4},{1,9},{5,13},{9,1},{13,5},{2,10},{6,14},... | collective-permute-start | bytes 393224 | tf_op jit(solution)/shard_map/ppermute | solution.py:606
  39.1 2.9 %collective-permute-start.14 = (bf16[128,512]{1,0:T(8,128)(2,1)S(1)}, bf16[128,512]{1,0:T(8,128)(2,1)S(1)}, u32[]{:S(2)}, u32[]{:S(2)}) collective-permute-start(bf16[128,512]{1,0:T(8,128)(2,1)S(1)} %get-tuple-element.97), channel_id=1, source_target_pairs={{0,12},{4,8},{8,4},{12,0},{1,13},{5,9},{9,5},{13,1},{2,14},{6,10},... | collective-permute-start | bytes 393224 | tf_op jit(solution)/shard_map/ppermute | solution.py:606
  42.7 0.7 %split_sum.1 = (bf16[128,128]{1,0:T(8,128)(2,1)S(1)}, f32[128,128]{1,0:T(8,128)S(1)}, bf16[8,128,128]{2,1,0:T(8,128)(2,1)}) custom-call(bf16[128,256]{1,0:T(8,128)(2,1)S(1)} %get-tuple-element.86.mine_ref, bf16[128,256]{1,0:T(8,128)(2,1)S(1)} %collective-permute-done.11.came_ref, bf16[4,128,128]{2,1,0:T(8,128)(2,1)S(1)} %get-tuple-element.87.act_ref, ...), custom_call_target="tpu_custom_call" | custom-call | bytes 262144 | tf_op jit(solution)/shard_map/split_sum/pallas_call | solution.py:564
  43.4 1.2 %collective-permute-done.16.came_ref = bf16[128,128]{1,0:T(8,128)(2,1)S(1)} collective-permute-done((bf16[128,128]{1,0:T(8,128)(2,1)S(1)}, bf16[128,128]{1,0:T(8,128)(2,1)S(1)}, u32[]{:S(2)}, u32[]{:S(2)}) %collective-permute-start.16) | collective-permute-done | bytes 32800 | tf_op jit(solution)/shard_map/ppermute | solution.py:602
  44.6 4.1 %collective-permute-start.17 = (bf16[128,128]{1,0:T(8,128)(2,1)S(1)}, bf16[128,128]{1,0:T(8,128)(2,1)S(1)}, u32[]{:S(2)}, u32[]{:S(2)}) collective-permute-start(bf16[128,128]{1,0:T(8,128)(2,1)S(1)} %pair_sum.2.mine_ref), channel_id=1, source_target_pairs={{0,4},{4,0},{8,12},{12,8},{1,5},{5,1},{9,13},{13,9},{2,6},{6,2},{1... | collective-permute-start | bytes 98312 | tf_op jit(solution)/shard_map/ppermute | solution.py:606
  49.1 3.7 %collective-permute-done.17.came_ref = bf16[128,128]{1,0:T(8,128)(2,1)S(1)} collective-permute-done((bf16[128,128]{1,0:T(8,128)(2,1)S(1)}, bf16[128,128]{1,0:T(8,128)(2,1)S(1)}, u32[]{:S(2)}, u32[]{:S(2)}) %collective-permute-start.17) | collective-permute-done | bytes 32800 | tf_op jit(solution)/shard_map/ppermute | solution.py:606
  52.9 0.7 %late_rows.3.mine_ref = bf16[8,128,128]{2,1,0:T(8,128)(2,1)S(1)} custom-call(f32[8,128,128]{2,1,0:T(8,128)S(1)} %late_rows.2.refs_0_, s32[1,128]{1,0:T(1,128)S(1)} %get-tuple-element.91.refs_1_, s32[1,128]{1,0:T(1,128)S(1)} %get-tuple-element.92.refs_2_, s32[1,128]{1,0:T(1,128)S(1)} %get-tuple-element.90.refs_0_.refs_3_, ...), custom_call_target="tpu_custom_call" | custom-call | flops 134217728 | bytes 1048576 | tf_op jit(solution)/shard_map/late_rows/pallas_call | solution.py:413
  54.2 1.1 %collective-permute-done.19.other_share_ref = f32[128,128]{1,0:T(8,128)S(1)} collective-permute-done((f32[128,128]{1,0:T(8,128)S(1)}, f32[128,128]{1,0:T(8,128)S(1)}, u32[]{:S(2)}, u32[]{:S(2)}) %collective-permute-start.19) | collective-permute-done | bytes 65568 | tf_op jit(solution)/shard_map/ppermute | solution.py:602
  55.3 0.9 %finish.1 = (bf16[8,128,128]{2,1,0:T(8,128)(2,1)}, f32[256,128]{1,0:T(8,128)}) custom-call(bf16[8,128,128]{2,1,0:T(8,128)(2,1)S(1)} %late_rows.3.mine_ref, bf16[8,128,128]{2,1,0:T(8,128)(2,1)S(1)} %collective-permute-done.18.other_ref, f32[128,128]{1,0:T(8,128)S(1)} %pair_sum.3.share_ref, f32[128,128]{1,0:T(8,128)S(1)} %collective-permute-done.19.other_share_ref), custom_call_target="tpu_custom_call" | custom-call | bytes 262144 | tf_op jit(solution)/shard_map/finish/pallas_call | solution.py:593
  (48 shorter events, 7.1 us)
Async XLA Ops:
  0.6 17.6 %collective-permute-start.5 = (bf16[8,128,128]{2,1,0:T(8,128)(2,1)}, bf16[8,128,128]{2,1,0:T(8,128)(2,1)S(1)}, u32[]{:S(2)}, u32[]{:S(2)}) collective-permute-start(bf16[8,128,128]{2,1,0:T(8,128)(2,1)} %refs_0_), channel_id=1, source_target_pairs={{0,2},{2,0},{1,3},{3,1},{4,6},{6,4},{5,7},{7,5},{8,10},{10,8},{9,1... | collective-permute-start | bytes 786440 | tf_op jit(solution)/shard_map/ppermute | solution.py:602
  6.8 10.7 %collective-permute-start.4 = (bf16[4,128,128]{2,1,0:T(8,128)(2,1)}, bf16[4,128,128]{2,1,0:T(8,128)(2,1)S(1)}, u32[]{:S(2)}, u32[]{:S(2)}) collective-permute-start(bf16[4,128,128]{2,1,0:T(8,128)(2,1)} %get-tuple-element.63), channel_id=1, source_target_pairs={{0,8},{4,12},{8,0},{12,4},{1,9},{5,13},{9,1},{13,5},{2,10},{6,14},... | collective-permute-start | bytes 393224 | tf_op jit(solution)/shard_map/ppermute | solution.py:606
  9.4 8.7 %collective-permute-start.3 = (bf16[4,128,128]{2,1,0:T(8,128)(2,1)}, bf16[4,128,128]{2,1,0:T(8,128)(2,1)S(1)}, u32[]{:S(2)}, u32[]{:S(2)}) collective-permute-start(bf16[4,128,128]{2,1,0:T(8,128)(2,1)} %get-tuple-element.63), channel_id=1, source_target_pairs={{0,4},{4,0},{8,12},{12,8},{1,5},{5,1},{9,13},{13,9},{2,6},{6,2},{1... | collective-permute-start | bytes 393224 | tf_op jit(solution)/shard_map/ppermute | solution.py:606
  11.0 3.1 %copy-start.5 = (s32[1,128]{1,0:T(1,128)S(1)}, s32[1,128]{1,0:T(1,128)}, u32[]{:S(2)}) copy-start(s32[1,128]{1,0:T(1,128)} %get-tuple-element.58.refs_2_) | copy-start | bytes 1540
  11.0 14.5 %copy-start.2 = (s32[1,128]{1,0:T(1,128)S(1)}, s32[1,128]{1,0:T(1,128)}, u32[]{:S(2)}) copy-start(s32[1,128]{1,0:T(1,128)} %get-tuple-element.55.refs_0_) | copy-start | bytes 1540
  14.6 7.7 %collective-permute-start.1 = (bf16[144,256]{1,0:T(8,128)(2,1)S(1)}, bf16[144,256]{1,0:T(8,128)(2,1)S(1)}, u32[]{:S(2)}, u32[]{:S(2)}) collective-permute-start(bf16[144,256]{1,0:T(8,128)(2,1)S(1)} %get-tuple-element.61), channel_id=1, source_target_pairs={{0,8},{4,12},{8,0},{12,4},{1,9},{5,13},{9,1},{13,5},{2,10},{6,14},... | collective-permute-start | bytes 221192 | tf_op jit(solution)/shard_map/ppermute | solution.py:606
  15.0 7.3 %collective-permute-start.2 = (bf16[144,256]{1,0:T(8,128)(2,1)S(1)}, bf16[144,256]{1,0:T(8,128)(2,1)S(1)}, u32[]{:S(2)}, u32[]{:S(2)}) collective-permute-start(bf16[144,256]{1,0:T(8,128)(2,1)S(1)} %get-tuple-element.62), channel_id=1, source_target_pairs={{0,12},{4,8},{8,4},{12,0},{1,13},{5,9},{9,5},{13,1},{2,14},{6,10},... | collective-permute-start | bytes 221192 | tf_op jit(solution)/shard_map/ppermute | solution.py:606
  17.5 7.9 %collective-permute-start = (bf16[144,256]{1,0:T(8,128)(2,1)S(1)}, bf16[144,256]{1,0:T(8,128)(2,1)S(1)}, u32[]{:S(2)}, u32[]{:S(2)}) collective-permute-start(bf16[144,256]{1,0:T(8,128)(2,1)S(1)} %get-tuple-element.60), channel_id=1, source_target_pairs={{0,4},{4,0},{8,12},{12,8},{1,5},{5,1},{9,13},{13,9},{2,6},{6,2},{1... | collective-permute-start | bytes 221192 | tf_op jit(solution)/shard_map/ppermute | solution.py:606
  18.2 6.5 %collective-permute-start.6 = (bf16[2,128,128]{2,1,0:T(8,128)(2,1)S(1)}, bf16[2,128,128]{2,1,0:T(8,128)(2,1)S(1)}, u32[]{:S(2)}, u32[]{:S(2)}) collective-permute-start(bf16[2,128,128]{2,1,0:T(8,128)(2,1)S(1)} %get-tuple-element.67), channel_id=1, source_target_pairs={{0,4},{4,0},{8,12},{12,8},{1,5},{5,1},{9,13},{13,9},{2,6},{6,2},{1... | collective-permute-start | bytes 196616 | tf_op jit(solution)/shard_map/ppermute | solution.py:606
  19.6 5.8 %collective-permute-start.7 = (bf16[2,128,128]{2,1,0:T(8,128)(2,1)S(1)}, bf16[2,128,128]{2,1,0:T(8,128)(2,1)S(1)}, u32[]{:S(2)}, u32[]{:S(2)}) collective-permute-start(bf16[2,128,128]{2,1,0:T(8,128)(2,1)S(1)} %get-tuple-element.68), channel_id=1, source_target_pairs={{0,4},{4,0},{8,12},{12,8},{1,5},{5,1},{9,13},{13,9},{2,6},{6,2},{1... | collective-permute-start | bytes 196616 | tf_op jit(solution)/shard_map/ppermute | solution.py:606
  25.4 1.8 %collective-permute-start.8 = (bf16[12,128,128]{2,1,0:T(8,128)(2,1)S(1)}, bf16[12,128,128]{2,1,0:T(8,128)(2,1)S(1)}, u32[]{:S(2)}, u32[]{:S(2)}) collective-permute-start(bf16[12,128,128]{2,1,0:T(8,128)(2,1)S(1)} %stack.1.refs_4_), channel_id=1, source_target_pairs={{0,1},{1,0},{2,3},{3,2},{4,5},{5,4},{6,7},{7,6},{8,9},{9,8},{10,11... | collective-permute-start | bytes 1179656 | tf_op jit(solution)/shard_map/ppermute | solution.py:602
  25.9 3.8 %copy-start.1 = (bf16[8,128,128]{2,1,0:T(8,128)(2,1)S(1)}, bf16[8,128,128]{2,1,0:T(8,128)(2,1)}, u32[]{:S(2)}) copy-start(bf16[8,128,128]{2,1,0:T(8,128)(2,1)} %refs_0_) | copy-start | bytes 786436
  26.0 8.8 %copy-start.6 = (bf16[256,256]{1,0:T(8,128)(2,1)S(1)}, bf16[256,256]{1,0:T(8,128)(2,1)}, u32[]{:S(2)}) copy-start(bf16[256,256]{1,0:T(8,128)(2,1)} %refs_3_.3) | copy-start | bytes 393220
  27.7 1.4 %collective-permute-start.9 = (bf16[4,128,128]{2,1,0:T(8,128)(2,1)S(1)}, bf16[4,128,128]{2,1,0:T(8,128)(2,1)S(1)}, u32[]{:S(2)}, u32[]{:S(2)}) collective-permute-start(bf16[4,128,128]{2,1,0:T(8,128)(2,1)S(1)} %get-tuple-element.83), channel_id=1, source_target_pairs={{0,1},{1,0},{2,3},{3,2},{4,5},{5,4},{6,7},{7,6},{8,9},{9,8},{10,11... | collective-permute-start | bytes 393224 | tf_op jit(solution)/shard_map/ppermute | solution.py:602
  29.2 5.6 %collective-permute-start.10 = (bf16[4,128,128]{2,1,0:T(8,128)(2,1)S(1)}, bf16[4,128,128]{2,1,0:T(8,128)(2,1)S(1)}, u32[]{:S(2)}, u32[]{:S(2)}) collective-permute-start(bf16[4,128,128]{2,1,0:T(8,128)(2,1)S(1)} %add_up.1.refs_0_), channel_id=1, source_target_pairs={{0,2},{2,0},{1,3},{3,1},{4,6},{6,4},{5,7},{7,5},{8,10},{10,8},{9,1... | collective-permute-start | bytes 393224 | tf_op jit(solution)/shard_map/ppermute | solution.py:602
  35.4 1.6 %collective-permute-start.12 = (bf16[128,1024]{1,0:T(8,128)(2,1)S(1)}, bf16[128,1024]{1,0:T(8,128)(2,1)S(1)}, u32[]{:S(2)}, u32[]{:S(2)}) collective-permute-start(bf16[128,1024]{1,0:T(8,128)(2,1)S(1)} %get-tuple-element.88), channel_id=1, source_target_pairs={{0,1},{1,0},{2,3},{3,2},{4,5},{5,4},{6,7},{7,6},{8,9},{9,8},{10,11... | collective-permute-start | bytes 786440 | tf_op jit(solution)/shard_map/ppermute | solution.py:602
  35.5 7.1 %collective-permute-start.11 = (bf16[128,256]{1,0:T(8,128)(2,1)S(1)}, bf16[128,256]{1,0:T(8,128)(2,1)S(1)}, u32[]{:S(2)}, u32[]{:S(2)}) collective-permute-start(bf16[128,256]{1,0:T(8,128)(2,1)S(1)} %get-tuple-element.86.mine_ref), channel_id=1, source_target_pairs={{0,8},{4,12},{8,0},{12,4},{1,9},{5,13},{9,1},{13,5},{2,10},{6,14},... | collective-permute-start | bytes 196616 | tf_op jit(solution)/shard_map/ppermute | solution.py:606
  37.5 15.3 %collective-permute-start.13 = (bf16[128,512]{1,0:T(8,128)(2,1)S(1)}, bf16[128,512]{1,0:T(8,128)(2,1)S(1)}, u32[]{:S(2)}, u32[]{:S(2)}) collective-permute-start(bf16[128,512]{1,0:T(8,128)(2,1)S(1)} %get-tuple-element.96), channel_id=1, source_target_pairs={{0,8},{4,12},{8,0},{12,4},{1,9},{5,13},{9,1},{13,5},{2,10},{6,14},... | collective-permute-start | bytes 393224 | tf_op jit(solution)/shard_map/ppermute | solution.py:606
  39.1 13.8 %collective-permute-start.14 = (bf16[128,512]{1,0:T(8,128)(2,1)S(1)}, bf16[128,512]{1,0:T(8,128)(2,1)S(1)}, u32[]{:S(2)}, u32[]{:S(2)}) collective-permute-start(bf16[128,512]{1,0:T(8,128)(2,1)S(1)} %get-tuple-element.97), channel_id=1, source_target_pairs={{0,12},{4,8},{8,4},{12,0},{1,13},{5,9},{9,5},{13,1},{2,14},{6,10},... | collective-permute-start | bytes 393224 | tf_op jit(solution)/shard_map/ppermute | solution.py:606
  42.0 10.9 %collective-permute-start.15 = (bf16[128,512]{1,0:T(8,128)(2,1)S(1)}, bf16[128,512]{1,0:T(8,128)(2,1)S(1)}, u32[]{:S(2)}, u32[]{:S(2)}) collective-permute-start(bf16[128,512]{1,0:T(8,128)(2,1)S(1)} %get-tuple-element.98), channel_id=1, source_target_pairs={{0,4},{4,0},{8,12},{12,8},{1,5},{5,1},{9,13},{13,9},{2,6},{6,2},{1... | collective-permute-start | bytes 393224 | tf_op jit(solution)/shard_map/ppermute | solution.py:606
  43.4 1.2 %collective-permute-start.16 = (bf16[128,128]{1,0:T(8,128)(2,1)S(1)}, bf16[128,128]{1,0:T(8,128)(2,1)S(1)}, u32[]{:S(2)}, u32[]{:S(2)}) collective-permute-start(bf16[128,128]{1,0:T(8,128)(2,1)S(1)} %get-tuple-element.100), channel_id=1, source_target_pairs={{0,1},{1,0},{2,3},{3,2},{4,5},{5,4},{6,7},{7,6},{8,9},{9,8},{10,11... | collective-permute-start | bytes 98312 | tf_op jit(solution)/shard_map/ppermute | solution.py:602
  44.6 8.2 %collective-permute-start.17 = (bf16[128,128]{1,0:T(8,128)(2,1)S(1)}, bf16[128,128]{1,0:T(8,128)(2,1)S(1)}, u32[]{:S(2)}, u32[]{:S(2)}) collective-permute-start(bf16[128,128]{1,0:T(8,128)(2,1)S(1)} %pair_sum.2.mine_ref), channel_id=1, source_target_pairs={{0,4},{4,0},{8,12},{12,8},{1,5},{5,1},{9,13},{13,9},{2,6},{6,2},{1... | collective-permute-start | bytes 98312 | tf_op jit(solution)/shard_map/ppermute | solution.py:606
  53.6 1.7 %collective-permute-start.18 = (bf16[8,128,128]{2,1,0:T(8,128)(2,1)S(1)}, bf16[8,128,128]{2,1,0:T(8,128)(2,1)S(1)}, u32[]{:S(2)}, u32[]{:S(2)}) collective-permute-start(bf16[8,128,128]{2,1,0:T(8,128)(2,1)S(1)} %late_rows.3.mine_ref), channel_id=1, source_target_pairs={{0,1},{1,0},{2,3},{3,2},{4,5},{5,4},{6,7},{7,6},{8,9},{9,8},{10,11... | collective-permute-start | bytes 786440 | tf_op jit(solution)/shard_map/ppermute | solution.py:602
  53.7 1.6 %collective-permute-start.19 = (f32[128,128]{1,0:T(8,128)S(1)}, f32[128,128]{1,0:T(8,128)S(1)}, u32[]{:S(2)}, u32[]{:S(2)}) collective-permute-start(f32[128,128]{1,0:T(8,128)S(1)} %pair_sum.3.share_ref), channel_id=1, source_target_pairs={{0,1},{1,0},{2,3},{3,2},{4,5},{5,4},{6,7},{7,6},{8,9},{9,8},{10,11... | collective-permute-start | bytes 196616 | tf_op jit(solution)/shard_map/ppermute | solution.py:602
  (3 other events, 9.3 us)

commit v11 on v10

--- a/solution.py
+++ b/solution.py
@@ -63,7 +63,7 @@
     return jnp.concatenate([x3[b] for b in range(x3.shape[0])], axis=1)
 
 
-def places(peers, blocks_dev, count, row, col, ask_refs):
+def places(peers, blocks_dev, count, row, col, table):
     me = lax.axis_index("graph")
     lane = lax.broadcasted_iota(jnp.int32, col.shape, 1)
     live = lane < count
@@ -73,38 +73,47 @@
         inside = live & (local >= 0) & (local < blocks_dev)
         low = jnp.min(jnp.where(inside, local, blocks_dev - 1), axis=1, keepdims=True)
         high = jnp.max(jnp.where(inside, local, 0), axis=1, keepdims=True)
-        ask_refs[k][...] = jnp.where(lane == 0, low, high)
+        table[PLACE_ROWS + k : PLACE_ROWS + k + 1, :] = jnp.where(lane == 0, low, high)
         slot = k * CAP + (local != low).astype(jnp.int32)
         place = jnp.where(inside, slot * blocks_dev + row, place)
-    return place
-
-
-def prepare_kernel(peers, count_ref, row_ref, col_ref, x3, half_ref, place_out, *refs):
-    ask_refs, place_ref, sem = refs[:peers], refs[peers], refs[peers + 1]
-    share = half_ref.shape[0]
-    half_ref[...] = x3[pl.ds(lax.axis_index("rep") * share, share)]
+    table[:PLACE_ROWS, :] = jnp.broadcast_to(place, (PLACE_ROWS, place.shape[1]))
+
+
+def table_rows(peers):
+    return PLACE_ROWS + -(-peers // 8) * 8
+
+
+def prepare_kernel(peers, count_ref, row_ref, col_ref, x3, half_out, table_out, table, half_sem, sem):
+    share = half_out.shape[0]
+    mine = pl.ds(lax.axis_index("rep") * share, share)
+    half_copy = pltpu.make_async_copy(x3.at[mine], half_out, half_sem)
+    half_copy.start()
     count = jnp.broadcast_to(count_ref[...], (1, 1))
-    place = places(peers, x3.shape[0], count, row_ref[...], col_ref[...], ask_refs)
-    place_ref[...] = jnp.broadcast_to(place, place_ref.shape)
-    copy = pltpu.make_async_copy(place_ref, place_out.at[pl.ds(0, PLACE_ROWS)], sem)
+    if table.shape[0] > PLACE_ROWS + peers:
+        table[...] = jnp.zeros(table.shape, jnp.int32)
+    places(peers, x3.shape[0], count, row_ref[...], col_ref[...], table)
+    copy = pltpu.make_async_copy(table, table_out.at[pl.ds(0, table.shape[0])], sem)
     copy.start()
+    half_copy.wait()
     copy.wait()
 
 
 def prepare(features, tile_row, tile_col, tile_count, peers, reps):
     per = tile_col.shape[0]
     blocks_dev, columns, width = features.shape
-    outs = call(
+    return call(
         functools.partial(prepare_kernel, peers),
         "prepare",
-        [shape((blocks_dev // reps, columns, width), BF16), shape((PLACE_BUFFER // (4 * per), per), jnp.int32)]
-        + [shape((1, per), jnp.int32)] * peers,
+        [shape((blocks_dev // reps, columns, width), BF16), shape((PLACE_BUFFER // (4 * per), per), jnp.int32)],
         [vmem()] * 4,
-        [pltpu.VMEM((PLACE_ROWS, per), jnp.int32), pltpu.SemaphoreType.DMA],
-        out_specs=[vmem(), hbm()] + [vmem()] * peers,
+        [
+            pltpu.VMEM((table_rows(peers), per), jnp.int32),
+            pltpu.SemaphoreType.DMA,
+            pltpu.SemaphoreType.DMA,
+        ],
         limit=VMEM_ALL,
+        out_specs=[hbm(), hbm()],
     )(tile_count, tile_row.reshape(1, per), tile_col.reshape(1, per), features)
-    return outs[0], outs[1], list(outs[2:])
 
 
 def pick(ids_ref, lane):
@@ -113,7 +122,8 @@
     return jnp.max(jnp.where(at == lane, ids, 0.0)).astype(jnp.int32)
 
 
-def operator_kernel(blocks_dev, slots_here, groups, place_in, tiles_ref, m_ref, tiles, acc, place_ref, sems, sem):
+def operator_kernel(blocks_dev, slots_here, groups, table_in, tiles_ref, m_ref, *refs):
+    asks, (tiles, acc, place_ref, table, sems, sem, table_sem) = refs[:-7], refs[-7:]
     step = pl.program_id(0)
     per, width = tiles.shape[0], tiles.shape[1]
     chunks = per // CHUNK
@@ -124,11 +134,15 @@
         return pltpu.make_async_copy(tiles_ref.at[part], tiles.at[part], sems.at[c])
 
     def place_copy():
-        return pltpu.make_async_copy(place_in.at[pl.ds(0, PLACE_ROWS)], place_ref, sem)
+        return pltpu.make_async_copy(table_in.at[pl.ds(0, PLACE_ROWS)], place_ref, sem)
+
+    def table_copy():
+        return pltpu.make_async_copy(table_in.at[pl.ds(0, table.shape[0])], table, table_sem)
 
     @pl.when(step == 0)
     def _():
         place_copy().start()
+        table_copy().start()
         for c in range(chunks):
             chunk_copy(c).start()
 
@@ -137,6 +151,9 @@
     @pl.when(step == 0)
     def _():
         place_copy().wait()
+        table_copy().wait()
+        for k, ask_ref in enumerate(asks):
+            ask_ref[...] = table[PLACE_ROWS + k : PLACE_ROWS + k + 1, :]
 
     def add_chunk(c, carry):
         @pl.when(step == 0)
@@ -162,28 +179,31 @@
             m_ref[r * width : (r + 1) * width, s * width : (s + 1) * width] = total.astype(BF16)
 
 
-def list_operator(tiles, place, peers, blocks_dev):
+def list_operator(tiles, table, peers, blocks_dev):
     per, width = tiles.shape[0], tiles.shape[1]
     slots = peers * CAP
     slots_here = min(slots, GROUP)
     groups = slots // slots_here
-    return call(
+    outs = call(
         functools.partial(operator_kernel, blocks_dev, slots_here, groups),
         "operator",
-        shape((blocks_dev * width, slots * width), BF16),
+        [shape((blocks_dev * width, slots * width), BF16)] + [shape((1, per), jnp.int32)] * peers,
         [hbm(), hbm()],
         [
             pltpu.VMEM((per, width, width), BF16),
             pltpu.VMEM((SIDES, slots_here * blocks_dev + 1, width, width), F32),
             pltpu.SMEM((PLACE_ROWS, per), jnp.int32),
+            pltpu.VMEM((table_rows(peers), per), jnp.int32),
             pltpu.SemaphoreType.DMA((per // CHUNK,)),
+            pltpu.SemaphoreType.DMA,
             pltpu.SemaphoreType.DMA,
         ],
         moved=2 ** 24,
         limit=VMEM_MOST,
         grid=(groups,),
-        out_specs=pl.BlockSpec((blocks_dev * width, slots_here * width), lambda i: (0, i)),
-    )(place, tiles)
+        out_specs=[pl.BlockSpec((blocks_dev * width, slots_here * width), lambda i: (0, i))] + [vmem()] * peers,
+    )(table, tiles)
+    return outs[0], list(outs[1:])
 
 
 def mirrored(near, m_ref, mir, slots, width):
@@ -429,23 +449,21 @@
     return call(add_kernel, "add_up", shape(came.shape, BF16), [vmem(), vmem()])(keep, came)
 
 
-def widen_kernel(feats, *refs):
-    out_ref = refs[feats]
-    _, columns, width = refs[0].shape
+def widen_kernel(feats, in_ref, out_ref):
+    blocks, columns, width = in_ref.shape
     share = out_ref.shape[1] // width
     first = lax.axis_index("rep") * share
-    me = lax.axis_index("feat")
-    for q in range(feats):
-        rows = pl.ds(pl.multiple_of(lax.rem(me + q, feats) * columns, columns), columns)
+    for f in range(feats):
         for b in range(share):
-            out_ref[rows, b * width : (b + 1) * width] = refs[q][first + b]
-
-
-def widen(parts, reps):
-    blocks_dev, columns, width = parts[0].shape
-    out = shape((len(parts) * columns, blocks_dev // reps * width), BF16)
-    kernel = functools.partial(widen_kernel, len(parts))
-    return call(kernel, "widen", out, [vmem()] * len(parts))(*parts)
+            out_ref[f * columns : (f + 1) * columns, b * width : (b + 1) * width] = in_ref[
+                f * (blocks // feats) + first + b
+            ]
+
+
+def widen(parts, feats, reps):
+    blocks, columns, width = parts.shape
+    out = shape((feats * columns, blocks // feats // reps * width), BF16)
+    return call(functools.partial(widen_kernel, feats), "widen", out, [vmem()])(parts)
 
 
 def dense_kernel(feats, *refs):
@@ -617,19 +635,17 @@
     reps = lax.axis_size("rep")
     far_first = sorted(range(1, peers), key=lambda k: (-(k & (peers // 2)), k))
 
-    half, place, asks = prepare(features, tile_row, tile_col, tile_count, peers, reps)
-    operator = list_operator(tiles, place, peers, blocks_dev)
+    half, table = prepare(features, tile_row, tile_col, tile_count, peers, reps)
+    operator, asks = list_operator(tiles, table, peers, blocks_dev)
     sends, own_mirror = first_sends(features, operator, asks[1:], peers)
-    cots = [cotangent] + [ahead(cotangent, "feat", feats, feats - q) for q in range(1, feats)]
+    cots = lax.all_gather(cotangent, "feat", axis=0, tiled=True)
     pieces, held = {0: [half]}, [0]
     bit = peers // 2
     while bit:
         for k in held:
             parts = pieces[k]
             if k:
-                parts, cots, _ = lax.optimization_barrier(
-                    (halves(after(parts, sends[1])), cots, pieces.get(1, half))
-                )
+                parts = after(halves(after(parts, sends[1])), pieces.get(1, half))
             pieces[k ^ bit] = [across(part, peers, bit) for part in parts]
         held = held + [k ^ bit for k in held]
         bit //= 2
@@ -638,7 +654,7 @@
         came[k] = across(sends[k], peers, k)
     arrived = [part for k in range(1, peers) for part in pieces[k]]
     middle = peers // 2
-    came[middle:], arrived = lax.optimization_barrier((came[middle:], arrived))
+    came[middle:], arrived, cots = lax.optimization_barrier((came[middle:], arrived, cots))
     came[1:middle], arrived = lax.optimization_barrier((came[1:middle], arrived))
     stacked = stack(arrived)
     swapped = ahead(stacked, "rep", reps, 1)
@@ -647,7 +663,7 @@
     keep = keep_rows(acc, asked, operator, reps)
 
     mine = add_up(keep, ahead(give, "rep", reps, 1))
-    cot = widen(cots, reps)
+    cot = widen(cots, feats, reps)
     sums = [mine] + [ahead(mine, "feat", feats, feats - q) for q in range(1, feats)]
     act, give, spread, term = dense(sums, cot, weight, feats)
     shared = ahead(give, "rep", reps, 1)

time: 56.3 us -> 58.2 us (1.034)
  blocking collectives: 0 us -> 7.04 us
  starting transfers between devices: 24.1 us -> 19 us
    all_gather x0 -> x1, blocking collectives: none -> 7.04 us  [local(): cots = lax.all_gather(cotangent, 'feat', axis=0, tiled=True)]
    ppermute x12, starting transfers between devices: 19.6 us -> 16.5 us  [across(): return lax.ppermute(value, 'graph', [(i, i ^ k) for i in range(peers)])]
    ppermute x8 -> x7, starting transfers between devices: 4.51 us -> 2.48 us  [ahead(): return lax.ppermute(value, axis, [(i, (i + k) % size) for i in range(size)])]
    ppermute x12, waiting for transfers between devices: 9.47 us -> 10.8 us  [across(): return lax.ppermute(value, 'graph', [(i, i ^ k) for i in range(peers)])]
    ppermute x8 -> x7, waiting for transfers between devices: 9.79 us -> 8.61 us  [ahead(): return lax.ppermute(value, axis, [(i, (i + k) % size) for i in range(size)])]
    pallas_call x1, Pallas kernels: 2.49 us -> 1.84 us  [prepare(): call(functools.partial(prepare_kernel, peers), 'prepare', [shape((blocks_...]
    pallas_call x1, Pallas kernels: 3.07 us -> 3.67 us  [list_operator(): call(functools.partial(operator_kernel, blocks_dev, slots_here, groups),...]
  transfers between devices with their start and end apart: 20 -> 19, of which waited for: 11 -> 8; matrix products, arithmetic and copies ran while one was open for 0% -> 0% of each run, Pallas kernels for 15% -> 11%
where the time goes in v11:
time: 58.2 us; the launch traced here: 58.1 us
  waiting for transfers between devices  19.4 us (33%)
  starting transfers between devices  19 us (33%)
  Pallas kernels  11.2 us (19%)
  blocking collectives  7.04 us (12%)
  between operations  1.48 us (3%)
    ppermute x12, starting transfers between devices, across(): return lax.ppermute(value, 'graph', [(i, i ^ k) for i in range(peers)])  16.5 us
    ppermute x12, waiting for transfers between devices, across(): return lax.ppermute(value, 'graph', [(i, i ^ k) for i in range(peers)])  10.8 us
    ppermute x7, waiting for transfers between devices, ahead(): return lax.ppermute(value, axis, [(i, (i + k) % size) for i in range(size)])  8.61 us
    all_gather x1, blocking collectives, local(): cots = lax.all_gather(cotangent, 'feat', axis=0, tiled=True)  7.04 us
    pallas_call x1, Pallas kernels, list_operator(): call(functools.partial(operator_kernel, blocks_dev, slots_here, groups),...  3.67 us
    ppermute x7, starting transfers between devices, ahead(): return lax.ppermute(value, axis, [(i, (i + k) % size) for i in range(size)])  2.48 us
    pallas_call x1, Pallas kernels, prepare(): call(functools.partial(prepare_kernel, peers), 'prepare', [shape((blocks_...  1.84 us
  transfers between devices with their start and end apart: 19, of which 8 were waited for; matrix products, arithmetic and copies ran while one was open for 0% of the time, Pallas kernels for 11%

profile of v11, /device:TPU:0, one launch (start us, length us, event | category | flops | bytes accessed | tf_op | source)
XLA Modules:
  0.0 58.1 jit_solution(5374296155419272810)
XLA Ops:
  1.3 1.8 %prepare.1 = (bf16[4,128,128]{2,1,0:T(8,128)(2,1)}, s32[8192,128]{1,0:T(8,128)}) custom-call(s32[1]{0:T(128)S(6)} %copy.10.count_ref, s32[1,128]{1,0:T(1,128)} %bitcast.2, s32[1,128]{1,0:T(1,128)} %bitcast.3, bf16[8,128,128]{2,1,0:T(8,128)(2,1)} %refs_4_.1), custom_call_target="tpu_custom_call" | custom-call | bytes 262144 | tf_op jit(solution)/shard_map/prepare/pallas_call | solution.py:104
  3.1 4.1 %collective-permute-start.4 = (bf16[4,128,128]{2,1,0:T(8,128)(2,1)}, bf16[4,128,128]{2,1,0:T(8,128)(2,1)S(1)}, u32[]{:S(2)}, u32[]{:S(2)}) collective-permute-start(bf16[4,128,128]{2,1,0:T(8,128)(2,1)} %get-tuple-element.64), channel_id=1, source_target_pairs={{0,8},{4,12},{8,0},{12,4},{1,9},{5,13},{9,1},{13,5},{2,10},{6,14},... | collective-permute-start | bytes 393224 | tf_op jit(solution)/shard_map/ppermute | solution.py:624
  7.2 1.6 %collective-permute-start.3 = (bf16[4,128,128]{2,1,0:T(8,128)(2,1)}, bf16[4,128,128]{2,1,0:T(8,128)(2,1)S(1)}, u32[]{:S(2)}, u32[]{:S(2)}) collective-permute-start(bf16[4,128,128]{2,1,0:T(8,128)(2,1)} %get-tuple-element.64), channel_id=1, source_target_pairs={{0,4},{4,0},{8,12},{12,8},{1,5},{5,1},{9,13},{13,9},{2,6},{6,2},{1... | collective-permute-start | bytes 393224 | tf_op jit(solution)/shard_map/ppermute | solution.py:624
  8.8 3.7 %operator.1 = (bf16[1024,1024]{1,0:T(8,128)(2,1)S(1)}, s32[1,128]{1,0:T(1,128)S(1)}, s32[1,128]{1,0:T(1,128)S(1)}, s32[1,128]{1,0:T(1,128)S(1)}, s32[1,128]{1,0:T(1,128)S(1)}) custom-call(s32[8192,128]{1,0:T(8,128)} %get-tuple-element.55.table_in, bf16[128,128,128]{2,1,0:T(8,128)(2,1)} %tiles_ref.1), custom_call_target="tpu_custom_call" | custom-call | bytes 16777216 | tf_op jit(solution)/shard_map/operator/pallas_call | solution.py:187
  13.4 2.5 %collective-permute-start.2 = (bf16[144,256]{1,0:T(8,128)(2,1)S(1)}, bf16[144,256]{1,0:T(8,128)(2,1)S(1)}, u32[]{:S(2)}, u32[]{:S(2)}) collective-permute-start(bf16[144,256]{1,0:T(8,128)(2,1)S(1)} %get-tuple-element.63), channel_id=1, source_target_pairs={{0,12},{4,8},{8,4},{12,0},{1,13},{5,9},{9,5},{13,1},{2,14},{6,10},... | collective-permute-start | bytes 221192 | tf_op jit(solution)/shard_map/ppermute | solution.py:624
  15.8 0.7 %collective-permute-start = (bf16[144,256]{1,0:T(8,128)(2,1)S(1)}, bf16[144,256]{1,0:T(8,128)(2,1)S(1)}, u32[]{:S(2)}, u32[]{:S(2)}) collective-permute-start(bf16[144,256]{1,0:T(8,128)(2,1)S(1)} %get-tuple-element.61), channel_id=1, source_target_pairs={{0,4},{4,0},{8,12},{12,8},{1,5},{5,1},{9,13},{13,9},{2,6},{6,2},{1... | collective-permute-start | bytes 221192 | tf_op jit(solution)/shard_map/ppermute | solution.py:624
  16.5 1.4 %collective-permute-start.5 = (bf16[2,128,128]{2,1,0:T(8,128)(2,1)S(1)}, bf16[2,128,128]{2,1,0:T(8,128)(2,1)S(1)}, u32[]{:S(2)}, u32[]{:S(2)}) collective-permute-start(bf16[2,128,128]{2,1,0:T(8,128)(2,1)S(1)} %get-tuple-element.68), channel_id=1, source_target_pairs={{0,4},{4,0},{8,12},{12,8},{1,5},{5,1},{9,13},{13,9},{2,6},{6,2},{1... | collective-permute-start | bytes 196616 | tf_op jit(solution)/shard_map/ppermute | solution.py:624
  17.9 0.7 %collective-permute-start.6 = (bf16[2,128,128]{2,1,0:T(8,128)(2,1)S(1)}, bf16[2,128,128]{2,1,0:T(8,128)(2,1)S(1)}, u32[]{:S(2)}, u32[]{:S(2)}) collective-permute-start(bf16[2,128,128]{2,1,0:T(8,128)(2,1)S(1)} %get-tuple-element.69), channel_id=1, source_target_pairs={{0,4},{4,0},{8,12},{12,8},{1,5},{5,1},{9,13},{13,9},{2,6},{6,2},{1... | collective-permute-start | bytes 196616 | tf_op jit(solution)/shard_map/ppermute | solution.py:624
  18.6 7.0 %all_gather.3.in_ref = bf16[16,128,128]{2,1,0:T(8,128)(2,1)S(1)} all-gather(bf16[8,128,128]{2,1,0:T(8,128)(2,1)S(1)} %copy-done.2), channel_id=1, replica_groups=mesh['parts'=2,'graph'=4,'feat'=2,'rep'=2] {'feat'}, dimensions={0}, use_global_device_ids=true | all-gather | bytes 786432 | tf_op jit(solution)/shard_map/all_gather | solution.py:641
  26.2 1.3 %collective-permute-done.7.refs_5_ = bf16[12,128,128]{2,1,0:T(8,128)(2,1)S(1)} collective-permute-done((bf16[12,128,128]{2,1,0:T(8,128)(2,1)S(1)}, bf16[12,128,128]{2,1,0:T(8,128)(2,1)S(1)}, u32[]{:S(2)}, u32[]{:S(2)}) %collective-permute-start.7) | collective-permute-done | bytes 393248 | tf_op jit(solution)/shard_map/ppermute | solution.py:620
  28.6 0.8 %collective-permute-done.8.came_ref = bf16[4,128,128]{2,1,0:T(8,128)(2,1)S(1)} collective-permute-done((bf16[4,128,128]{2,1,0:T(8,128)(2,1)S(1)}, bf16[4,128,128]{2,1,0:T(8,128)(2,1)S(1)}, u32[]{:S(2)}, u32[]{:S(2)}) %collective-permute-start.8) | collective-permute-done | bytes 131104 | tf_op jit(solution)/shard_map/ppermute | solution.py:620
  29.5 1.6 %collective-permute-start.9 = (bf16[4,128,128]{2,1,0:T(8,128)(2,1)S(1)}, bf16[4,128,128]{2,1,0:T(8,128)(2,1)S(1)}, u32[]{:S(2)}, u32[]{:S(2)}) collective-permute-start(bf16[4,128,128]{2,1,0:T(8,128)(2,1)S(1)} %add_up.1.refs_0_), channel_id=1, source_target_pairs={{0,2},{2,0},{1,3},{3,1},{4,6},{6,4},{5,7},{7,5},{8,10},{10,8},{9,1... | collective-permute-start | bytes 393224 | tf_op jit(solution)/shard_map/ppermute | solution.py:620
  31.1 4.0 %collective-permute-done.9.refs_1_ = bf16[4,128,128]{2,1,0:T(8,128)(2,1)S(1)} collective-permute-done((bf16[4,128,128]{2,1,0:T(8,128)(2,1)S(1)}, bf16[4,128,128]{2,1,0:T(8,128)(2,1)S(1)}, u32[]{:S(2)}, u32[]{:S(2)}) %collective-permute-start.9) | collective-permute-done | bytes 131104 | tf_op jit(solution)/shard_map/ppermute | solution.py:620
  35.1 0.6 %dense.1 = (bf16[4,128,128]{2,1,0:T(8,128)(2,1)S(1)}, bf16[128,1024]{1,0:T(8,128)(2,1)S(1)}, bf16[4,128,128]{2,1,0:T(8,128)(2,1)S(1)}, bf16[128,256]{1,0:T(8,128)(2,1)S(1)}) custom-call(bf16[4,128,128]{2,1,0:T(8,128)(2,1)S(1)} %add_up.1.refs_0_, bf16[4,128,128]{2,1,0:T(8,128)(2,1)S(1)} %collective-permute-done.9.refs_1_, bf16[256,512]{1,0:T(8,128)(2,1)S(1)} %widen.1.refs_2_, ...), custom_call_target="tpu_custom_call" | custom-call | flops 268435456 | bytes 1048576 | tf_op jit(solution)/shard_map/dense/pallas_call | solution.py:499
  35.8 1.3 %collective-permute-start.10 = (bf16[128,256]{1,0:T(8,128)(2,1)S(1)}, bf16[128,256]{1,0:T(8,128)(2,1)S(1)}, u32[]{:S(2)}, u32[]{:S(2)}) collective-permute-start(bf16[128,256]{1,0:T(8,128)(2,1)S(1)} %get-tuple-element.86.mine_ref), channel_id=1, source_target_pairs={{0,8},{4,12},{8,0},{12,4},{1,9},{5,13},{9,1},{13,5},{2,10},{6,14},... | collective-permute-start | bytes 196616 | tf_op jit(solution)/shard_map/ppermute | solution.py:624
  37.8 1.5 %collective-permute-start.12 = (bf16[128,512]{1,0:T(8,128)(2,1)S(1)}, bf16[128,512]{1,0:T(8,128)(2,1)S(1)}, u32[]{:S(2)}, u32[]{:S(2)}) collective-permute-start(bf16[128,512]{1,0:T(8,128)(2,1)S(1)} %get-tuple-element.96), channel_id=1, source_target_pairs={{0,8},{4,12},{8,0},{12,4},{1,9},{5,13},{9,1},{13,5},{2,10},{6,14},... | collective-permute-start | bytes 393224 | tf_op jit(solution)/shard_map/ppermute | solution.py:624
  39.3 2.2 %collective-permute-start.13 = (bf16[128,512]{1,0:T(8,128)(2,1)S(1)}, bf16[128,512]{1,0:T(8,128)(2,1)S(1)}, u32[]{:S(2)}, u32[]{:S(2)}) collective-permute-start(bf16[128,512]{1,0:T(8,128)(2,1)S(1)} %get-tuple-element.97), channel_id=1, source_target_pairs={{0,12},{4,8},{8,4},{12,0},{1,13},{5,9},{9,5},{13,1},{2,14},{6,10},... | collective-permute-start | bytes 393224 | tf_op jit(solution)/shard_map/ppermute | solution.py:624
  41.6 7.2 %collective-permute-done.10.came_ref = bf16[128,256]{1,0:T(8,128)(2,1)S(1)} collective-permute-done((bf16[128,256]{1,0:T(8,128)(2,1)S(1)}, bf16[128,256]{1,0:T(8,128)(2,1)S(1)}, u32[]{:S(2)}, u32[]{:S(2)}) %collective-permute-start.10) | collective-permute-done | bytes 65568 | tf_op jit(solution)/shard_map/ppermute | solution.py:624
  48.8 0.7 %split_sum.1 = (bf16[128,128]{1,0:T(8,128)(2,1)S(1)}, f32[128,128]{1,0:T(8,128)S(1)}, bf16[8,128,128]{2,1,0:T(8,128)(2,1)}) custom-call(bf16[128,256]{1,0:T(8,128)(2,1)S(1)} %get-tuple-element.86.mine_ref, bf16[128,256]{1,0:T(8,128)(2,1)S(1)} %collective-permute-done.10.came_ref, bf16[4,128,128]{2,1,0:T(8,128)(2,1)S(1)} %get-tuple-element.87.act_ref, ...), custom_call_target="tpu_custom_call" | custom-call | bytes 262144 | tf_op jit(solution)/shard_map/split_sum/pallas_call | solution.py:582
  49.5 1.2 %collective-permute-done.15.came_ref = bf16[128,128]{1,0:T(8,128)(2,1)S(1)} collective-permute-done((bf16[128,128]{1,0:T(8,128)(2,1)S(1)}, bf16[128,128]{1,0:T(8,128)(2,1)S(1)}, u32[]{:S(2)}, u32[]{:S(2)}) %collective-permute-start.15) | collective-permute-done | bytes 32800 | tf_op jit(solution)/shard_map/ppermute | solution.py:620
  51.2 3.5 %collective-permute-done.16.came_ref = bf16[128,128]{1,0:T(8,128)(2,1)S(1)} collective-permute-done((bf16[128,128]{1,0:T(8,128)(2,1)S(1)}, bf16[128,128]{1,0:T(8,128)(2,1)S(1)}, u32[]{:S(2)}, u32[]{:S(2)}) %collective-permute-start.16) | collective-permute-done | bytes 32800 | tf_op jit(solution)/shard_map/ppermute | solution.py:624
  54.8 0.7 %late_rows.3.mine_ref = bf16[8,128,128]{2,1,0:T(8,128)(2,1)S(1)} custom-call(f32[8,128,128]{2,1,0:T(8,128)S(1)} %late_rows.2.refs_0_, s32[1,128]{1,0:T(1,128)S(1)} %get-tuple-element.91.refs_1_, s32[1,128]{1,0:T(1,128)S(1)} %get-tuple-element.92.refs_2_, s32[1,128]{1,0:T(1,128)S(1)} %get-tuple-element.90.refs_0_.refs_3_, ...), custom_call_target="tpu_custom_call" | custom-call | flops 134217728 | bytes 1048576 | tf_op jit(solution)/shard_map/late_rows/pallas_call | solution.py:433
  56.1 1.1 %collective-permute-done.18.other_share_ref = f32[128,128]{1,0:T(8,128)S(1)} collective-permute-done((f32[128,128]{1,0:T(8,128)S(1)}, f32[128,128]{1,0:T(8,128)S(1)}, u32[]{:S(2)}, u32[]{:S(2)}) %collective-permute-start.18) | collective-permute-done | bytes 65568 | tf_op jit(solution)/shard_map/ppermute | solution.py:620
  57.2 0.9 %finish.1 = (bf16[8,128,128]{2,1,0:T(8,128)(2,1)}, f32[256,128]{1,0:T(8,128)}) custom-call(bf16[8,128,128]{2,1,0:T(8,128)(2,1)S(1)} %late_rows.3.mine_ref, bf16[8,128,128]{2,1,0:T(8,128)(2,1)S(1)} %collective-permute-done.17.other_ref, f32[128,128]{1,0:T(8,128)S(1)} %pair_sum.3.share_ref, f32[128,128]{1,0:T(8,128)S(1)} %collective-permute-done.18.other_share_ref), custom_call_target="tpu_custom_call" | custom-call | bytes 262144 | tf_op jit(solution)/shard_map/finish/pallas_call | solution.py:611
  (39 shorter events, 4.4 us)
Async XLA Ops:
  3.1 13.4 %collective-permute-start.4 = (bf16[4,128,128]{2,1,0:T(8,128)(2,1)}, bf16[4,128,128]{2,1,0:T(8,128)(2,1)S(1)}, u32[]{:S(2)}, u32[]{:S(2)}) collective-permute-start(bf16[4,128,128]{2,1,0:T(8,128)(2,1)} %get-tuple-element.64), channel_id=1, source_target_pairs={{0,8},{4,12},{8,0},{12,4},{1,9},{5,13},{9,1},{13,5},{2,10},{6,14},... | collective-permute-start | bytes 393224 | tf_op jit(solution)/shard_map/ppermute | solution.py:624
  7.2 9.3 %collective-permute-start.3 = (bf16[4,128,128]{2,1,0:T(8,128)(2,1)}, bf16[4,128,128]{2,1,0:T(8,128)(2,1)S(1)}, u32[]{:S(2)}, u32[]{:S(2)}) collective-permute-start(bf16[4,128,128]{2,1,0:T(8,128)(2,1)} %get-tuple-element.64), channel_id=1, source_target_pairs={{0,4},{4,0},{8,12},{12,8},{1,5},{5,1},{9,13},{13,9},{2,6},{6,2},{1... | collective-permute-start | bytes 393224 | tf_op jit(solution)/shard_map/ppermute | solution.py:624
  8.8 3.7 %copy-start = (bf16[8,128,128]{2,1,0:T(8,128)(2,1)S(1)}, bf16[8,128,128]{2,1,0:T(8,128)(2,1)}, u32[]{:S(2)}) copy-start(bf16[8,128,128]{2,1,0:T(8,128)(2,1)} %refs_4_.1) | copy-start | bytes 786436
  8.8 9.8 %copy-start.2 = (bf16[8,128,128]{2,1,0:T(8,128)(2,1)S(1)}, bf16[8,128,128]{2,1,0:T(8,128)(2,1)}, u32[]{:S(2)}) copy-start(bf16[8,128,128]{2,1,0:T(8,128)(2,1)} %param.9) | copy-start | bytes 786436
  12.9 12.7 %collective-permute-start.1 = (bf16[144,256]{1,0:T(8,128)(2,1)S(1)}, bf16[144,256]{1,0:T(8,128)(2,1)S(1)}, u32[]{:S(2)}, u32[]{:S(2)}) collective-permute-start(bf16[144,256]{1,0:T(8,128)(2,1)S(1)} %get-tuple-element.62), channel_id=1, source_target_pairs={{0,8},{4,12},{8,0},{12,4},{1,9},{5,13},{9,1},{13,5},{2,10},{6,14},... | collective-permute-start | bytes 221192 | tf_op jit(solution)/shard_map/ppermute | solution.py:624
  13.4 12.3 %collective-permute-start.2 = (bf16[144,256]{1,0:T(8,128)(2,1)S(1)}, bf16[144,256]{1,0:T(8,128)(2,1)S(1)}, u32[]{:S(2)}, u32[]{:S(2)}) collective-permute-start(bf16[144,256]{1,0:T(8,128)(2,1)S(1)} %get-tuple-element.63), channel_id=1, source_target_pairs={{0,12},{4,8},{8,4},{12,0},{1,13},{5,9},{9,5},{13,1},{2,14},{6,10},... | collective-permute-start | bytes 221192 | tf_op jit(solution)/shard_map/ppermute | solution.py:624
  15.8 9.9 %collective-permute-start = (bf16[144,256]{1,0:T(8,128)(2,1)S(1)}, bf16[144,256]{1,0:T(8,128)(2,1)S(1)}, u32[]{:S(2)}, u32[]{:S(2)}) collective-permute-start(bf16[144,256]{1,0:T(8,128)(2,1)S(1)} %get-tuple-element.61), channel_id=1, source_target_pairs={{0,4},{4,0},{8,12},{12,8},{1,5},{5,1},{9,13},{13,9},{2,6},{6,2},{1... | collective-permute-start | bytes 221192 | tf_op jit(solution)/shard_map/ppermute | solution.py:624
  16.5 9.1 %collective-permute-start.5 = (bf16[2,128,128]{2,1,0:T(8,128)(2,1)S(1)}, bf16[2,128,128]{2,1,0:T(8,128)(2,1)S(1)}, u32[]{:S(2)}, u32[]{:S(2)}) collective-permute-start(bf16[2,128,128]{2,1,0:T(8,128)(2,1)S(1)} %get-tuple-element.68), channel_id=1, source_target_pairs={{0,4},{4,0},{8,12},{12,8},{1,5},{5,1},{9,13},{13,9},{2,6},{6,2},{1... | collective-permute-start | bytes 196616 | tf_op jit(solution)/shard_map/ppermute | solution.py:624
  17.9 7.7 %collective-permute-start.6 = (bf16[2,128,128]{2,1,0:T(8,128)(2,1)S(1)}, bf16[2,128,128]{2,1,0:T(8,128)(2,1)S(1)}, u32[]{:S(2)}, u32[]{:S(2)}) collective-permute-start(bf16[2,128,128]{2,1,0:T(8,128)(2,1)S(1)} %get-tuple-element.69), channel_id=1, source_target_pairs={{0,4},{4,0},{8,12},{12,8},{1,5},{5,1},{9,13},{13,9},{2,6},{6,2},{1... | collective-permute-start | bytes 196616 | tf_op jit(solution)/shard_map/ppermute | solution.py:624
  25.7 1.8 %collective-permute-start.7 = (bf16[12,128,128]{2,1,0:T(8,128)(2,1)S(1)}, bf16[12,128,128]{2,1,0:T(8,128)(2,1)S(1)}, u32[]{:S(2)}, u32[]{:S(2)}) collective-permute-start(bf16[12,128,128]{2,1,0:T(8,128)(2,1)S(1)} %stack.1.refs_4_), channel_id=1, source_target_pairs={{0,1},{1,0},{2,3},{3,2},{4,5},{5,4},{6,7},{7,6},{8,9},{9,8},{10,11... | collective-permute-start | bytes 1179656 | tf_op jit(solution)/shard_map/ppermute | solution.py:620
  26.2 8.8 %copy-start.1 = (bf16[256,256]{1,0:T(8,128)(2,1)S(1)}, bf16[256,256]{1,0:T(8,128)(2,1)}, u32[]{:S(2)}) copy-start(bf16[256,256]{1,0:T(8,128)(2,1)} %refs_3_.3) | copy-start | bytes 393220
  28.0 1.4 %collective-permute-start.8 = (bf16[4,128,128]{2,1,0:T(8,128)(2,1)S(1)}, bf16[4,128,128]{2,1,0:T(8,128)(2,1)S(1)}, u32[]{:S(2)}, u32[]{:S(2)}) collective-permute-start(bf16[4,128,128]{2,1,0:T(8,128)(2,1)S(1)} %get-tuple-element.84), channel_id=1, source_target_pairs={{0,1},{1,0},{2,3},{3,2},{4,5},{5,4},{6,7},{7,6},{8,9},{9,8},{10,11... | collective-permute-start | bytes 393224 | tf_op jit(solution)/shard_map/ppermute | solution.py:620
  29.5 5.6 %collective-permute-start.9 = (bf16[4,128,128]{2,1,0:T(8,128)(2,1)S(1)}, bf16[4,128,128]{2,1,0:T(8,128)(2,1)S(1)}, u32[]{:S(2)}, u32[]{:S(2)}) collective-permute-start(bf16[4,128,128]{2,1,0:T(8,128)(2,1)S(1)} %add_up.1.refs_0_), channel_id=1, source_target_pairs={{0,2},{2,0},{1,3},{3,1},{4,6},{6,4},{5,7},{7,5},{8,10},{10,8},{9,1... | collective-permute-start | bytes 393224 | tf_op jit(solution)/shard_map/ppermute | solution.py:620
  35.7 1.6 %collective-permute-start.11 = (bf16[128,1024]{1,0:T(8,128)(2,1)S(1)}, bf16[128,1024]{1,0:T(8,128)(2,1)S(1)}, u32[]{:S(2)}, u32[]{:S(2)}) collective-permute-start(bf16[128,1024]{1,0:T(8,128)(2,1)S(1)} %get-tuple-element.88), channel_id=1, source_target_pairs={{0,1},{1,0},{2,3},{3,2},{4,5},{5,4},{6,7},{7,6},{8,9},{9,8},{10,11... | collective-permute-start | bytes 786440 | tf_op jit(solution)/shard_map/ppermute | solution.py:620
  35.8 13.0 %collective-permute-start.10 = (bf16[128,256]{1,0:T(8,128)(2,1)S(1)}, bf16[128,256]{1,0:T(8,128)(2,1)S(1)}, u32[]{:S(2)}, u32[]{:S(2)}) collective-permute-start(bf16[128,256]{1,0:T(8,128)(2,1)S(1)} %get-tuple-element.86.mine_ref), channel_id=1, source_target_pairs={{0,8},{4,12},{8,0},{12,4},{1,9},{5,13},{9,1},{13,5},{2,10},{6,14},... | collective-permute-start | bytes 196616 | tf_op jit(solution)/shard_map/ppermute | solution.py:624
  37.8 16.9 %collective-permute-start.12 = (bf16[128,512]{1,0:T(8,128)(2,1)S(1)}, bf16[128,512]{1,0:T(8,128)(2,1)S(1)}, u32[]{:S(2)}, u32[]{:S(2)}) collective-permute-start(bf16[128,512]{1,0:T(8,128)(2,1)S(1)} %get-tuple-element.96), channel_id=1, source_target_pairs={{0,8},{4,12},{8,0},{12,4},{1,9},{5,13},{9,1},{13,5},{2,10},{6,14},... | collective-permute-start | bytes 393224 | tf_op jit(solution)/shard_map/ppermute | solution.py:624
  39.3 15.4 %collective-permute-start.13 = (bf16[128,512]{1,0:T(8,128)(2,1)S(1)}, bf16[128,512]{1,0:T(8,128)(2,1)S(1)}, u32[]{:S(2)}, u32[]{:S(2)}) collective-permute-start(bf16[128,512]{1,0:T(8,128)(2,1)S(1)} %get-tuple-element.97), channel_id=1, source_target_pairs={{0,12},{4,8},{8,4},{12,0},{1,13},{5,9},{9,5},{13,1},{2,14},{6,10},... | collective-permute-start | bytes 393224 | tf_op jit(solution)/shard_map/ppermute | solution.py:624
  41.6 13.2 %collective-permute-start.14 = (bf16[128,512]{1,0:T(8,128)(2,1)S(1)}, bf16[128,512]{1,0:T(8,128)(2,1)S(1)}, u32[]{:S(2)}, u32[]{:S(2)}) collective-permute-start(bf16[128,512]{1,0:T(8,128)(2,1)S(1)} %get-tuple-element.98), channel_id=1, source_target_pairs={{0,4},{4,0},{8,12},{12,8},{1,5},{5,1},{9,13},{13,9},{2,6},{6,2},{1... | collective-permute-start | bytes 393224 | tf_op jit(solution)/shard_map/ppermute | solution.py:624
  49.5 1.2 %collective-permute-start.15 = (bf16[128,128]{1,0:T(8,128)(2,1)S(1)}, bf16[128,128]{1,0:T(8,128)(2,1)S(1)}, u32[]{:S(2)}, u32[]{:S(2)}) collective-permute-start(bf16[128,128]{1,0:T(8,128)(2,1)S(1)} %get-tuple-element.100), channel_id=1, source_target_pairs={{0,1},{1,0},{2,3},{3,2},{4,5},{5,4},{6,7},{7,6},{8,9},{9,8},{10,11... | collective-permute-start | bytes 98312 | tf_op jit(solution)/shard_map/ppermute | solution.py:620
  50.8 4.0 %collective-permute-start.16 = (bf16[128,128]{1,0:T(8,128)(2,1)S(1)}, bf16[128,128]{1,0:T(8,128)(2,1)S(1)}, u32[]{:S(2)}, u32[]{:S(2)}) collective-permute-start(bf16[128,128]{1,0:T(8,128)(2,1)S(1)} %pair_sum.2.mine_ref), channel_id=1, source_target_pairs={{0,4},{4,0},{8,12},{12,8},{1,5},{5,1},{9,13},{13,9},{2,6},{6,2},{1... | collective-permute-start | bytes 98312 | tf_op jit(solution)/shard_map/ppermute | solution.py:624
  55.5 1.7 %collective-permute-start.17 = (bf16[8,128,128]{2,1,0:T(8,128)(2,1)S(1)}, bf16[8,128,128]{2,1,0:T(8,128)(2,1)S(1)}, u32[]{:S(2)}, u32[]{:S(2)}) collective-permute-start(bf16[8,128,128]{2,1,0:T(8,128)(2,1)S(1)} %late_rows.3.mine_ref), channel_id=1, source_target_pairs={{0,1},{1,0},{2,3},{3,2},{4,5},{5,4},{6,7},{7,6},{8,9},{9,8},{10,11... | collective-permute-start | bytes 786440 | tf_op jit(solution)/shard_map/ppermute | solution.py:620
  55.6 1.6 %collective-permute-start.18 = (f32[128,128]{1,0:T(8,128)S(1)}, f32[128,128]{1,0:T(8,128)S(1)}, u32[]{:S(2)}, u32[]{:S(2)}) collective-permute-start(f32[128,128]{1,0:T(8,128)S(1)} %pair_sum.3.share_ref), channel_id=1, source_target_pairs={{0,1},{1,0},{2,3},{3,2},{4,5},{5,4},{6,7},{7,6},{8,9},{9,8},{10,11... | collective-permute-start | bytes 196616 | tf_op jit(solution)/shard_map/ppermute | solution.py:620

commit v12 on v11

--- a/solution.py
+++ b/solution.py
@@ -151,9 +151,6 @@
     @pl.when(step == 0)
     def _():
         place_copy().wait()
-        table_copy().wait()
-        for k, ask_ref in enumerate(asks):
-            ask_ref[...] = table[PLACE_ROWS + k : PLACE_ROWS + k + 1, :]
 
     def add_chunk(c, carry):
         @pl.when(step == 0)
@@ -177,6 +174,12 @@
             for side in range(1, SIDES):
                 total = total + acc[side, s * blocks_dev + r]
             m_ref[r * width : (r + 1) * width, s * width : (s + 1) * width] = total.astype(BF16)
+
+    @pl.when(step == 0)
+    def _():
+        table_copy().wait()
+        for k, ask_ref in enumerate(asks):
+            ask_ref[...] = table[PLACE_ROWS + k : PLACE_ROWS + k + 1, :]
 
 
 def list_operator(tiles, table, peers, blocks_dev):
@@ -220,9 +223,11 @@
 
 def first_sends_kernel(peers, *refs):
     ask_refs, refs = refs[: peers - 1], refs[peers - 1 :]
-    x3, m_ref, refs = refs[0], refs[1], refs[2:]
-    send_refs, self_ref, mir = refs[: peers - 1], refs[peers - 1], refs[peers]
+    x3, cot, m_ref, refs = refs[0], refs[1], refs[2], refs[3:]
+    send_refs, self_ref, cot_ref, mir = refs[: peers - 1], refs[peers - 1], refs[peers], refs[peers + 1]
     _, columns, width = x3.shape
+    share = cot_ref.shape[0]
+    cot_ref[...] = cot[pl.ds(lax.axis_index("rep") * share, share)]
     both = CAP * width
     mirrored(lanes(x3), m_ref, mir, peers * CAP, width)
     self_ref[...] = mir[:, :both]
@@ -234,19 +239,19 @@
         out[columns:, :] = jnp.where(lane < width, low, high).astype(F32).astype(BF16)
 
 
-def first_sends(values, operator, asks, peers):
-    _, columns, width = values.shape
+def first_sends(values, cotangent, operator, asks, peers, reps):
+    blocks_dev, columns, width = values.shape
     outs = call(
         functools.partial(first_sends_kernel, peers),
         "first_sends",
         [shape((columns + TAIL, CAP * width), BF16)] * (peers - 1)
-        + [shape((columns, CAP * width), F32)],
-        [vmem()] * (peers + 1),
+        + [shape((columns, CAP * width), F32), shape((blocks_dev // reps, columns, width), BF16)],
+        [vmem()] * (peers + 2),
         [pltpu.VMEM((columns, peers * CAP * width), F32)],
         flops=2 ** 28,
         moved=2 ** 21,
-    )(*asks, values, operator)
-    return [None] + list(outs[: peers - 1]), outs[peers - 1]
+    )(*asks, values, cotangent, operator)
+    return [None] + list(outs[: peers - 1]), outs[peers - 1], outs[peers]
 
 
 def add_sums(acc, block, sums):
@@ -450,19 +455,16 @@
 
 
 def widen_kernel(feats, in_ref, out_ref):
-    blocks, columns, width = in_ref.shape
+    _, columns, width = in_ref.shape
     share = out_ref.shape[1] // width
-    first = lax.axis_index("rep") * share
     for f in range(feats):
         for b in range(share):
-            out_ref[f * columns : (f + 1) * columns, b * width : (b + 1) * width] = in_ref[
-                f * (blocks // feats) + first + b
-            ]
-
-
-def widen(parts, feats, reps):
+            out_ref[f * columns : (f + 1) * columns, b * width : (b + 1) * width] = in_ref[f * share + b]
+
+
+def widen(parts, feats):
     blocks, columns, width = parts.shape
-    out = shape((feats * columns, blocks // feats // reps * width), BF16)
+    out = shape((feats * columns, blocks // feats * width), BF16)
     return call(functools.partial(widen_kernel, feats), "widen", out, [vmem()])(parts)
 
 
@@ -589,12 +591,12 @@
 
 
 def total_term(term, act, shared, peers, reps):
-    bit = peers // 2
-    give, total, activated = split_sum(term, across(term, peers, bit), act, shared, reps)
-    total = pair_sum(total, ahead(give, "rep", reps, 1), F32 if bit == 1 else BF16)
-    while bit > 1:
-        bit //= 2
-        total = pair_sum(total, across(total, peers, bit), F32 if bit == 1 else BF16)
+    give, total, activated = split_sum(term, across(term, peers, 1), act, shared, reps)
+    total = pair_sum(total, ahead(give, "rep", reps, 1), F32 if peers == 2 else BF16)
+    bit = 2
+    while bit < peers:
+        total = pair_sum(total, across(total, peers, bit), F32 if 2 * bit == peers else BF16)
+        bit *= 2
     return total, activated
 
 
@@ -637,8 +639,8 @@
 
     half, table = prepare(features, tile_row, tile_col, tile_count, peers, reps)
     operator, asks = list_operator(tiles, table, peers, blocks_dev)
-    sends, own_mirror = first_sends(features, operator, asks[1:], peers)
-    cots = lax.all_gather(cotangent, "feat", axis=0, tiled=True)
+    sends, own_mirror, own_cot = first_sends(features, cotangent, operator, asks[1:], peers, reps)
+    cots = lax.all_gather(own_cot, "feat", axis=0, tiled=True)
     pieces, held = {0: [half]}, [0]
     bit = peers // 2
     while bit:
@@ -663,7 +665,7 @@
     keep = keep_rows(acc, asked, operator, reps)
 
     mine = add_up(keep, ahead(give, "rep", reps, 1))
-    cot = widen(cots, feats, reps)
+    cot = widen(cots, feats)
     sums = [mine] + [ahead(mine, "feat", feats, feats - q) for q in range(1, feats)]
     act, give, spread, term = dense(sums, cot, weight, feats)
     shared = ahead(give, "rep", reps, 1)

time: 58.2 us -> 55.7 us (0.957)
  waiting for transfers between devices: 19.4 us -> 16.7 us
  starting transfers between devices: 19 us -> 21.1 us
  blocking collectives: 7.04 us -> 5.63 us
    ppermute x12, waiting for transfers between devices: 10.8 us -> 8.18 us  [across(): return lax.ppermute(value, 'graph', [(i, i ^ k) for i in range(peers)])]
    ppermute x12, starting transfers between devices: 16.5 us -> 18.6 us  [across(): return lax.ppermute(value, 'graph', [(i, i ^ k) for i in range(peers)])]
    all_gather x1, blocking collectives: 7.04 us -> 5.63 us  [local(): cots = lax.all_gather(own_cot, 'feat', axis=0, tiled=True)]
  transfers between devices with their start and end apart: 19 -> 19, of which waited for: 8 -> 7; matrix products, arithmetic and copies ran while one was open for 0% -> 0% of each run, Pallas kernels for 11% -> 11%
where the time goes in v12:
time: 55.7 us; the launch traced here: 55.6 us
  starting transfers between devices  21.1 us (38%)
  waiting for transfers between devices  16.7 us (30%)
  Pallas kernels  10.7 us (19%)
  blocking collectives  5.63 us (10%)
  between operations  1.48 us (3%)
    ppermute x12, starting transfers between devices, across(): return lax.ppermute(value, 'graph', [(i, i ^ k) for i in range(peers)])  18.6 us
    ppermute x7, waiting for transfers between devices, ahead(): return lax.ppermute(value, axis, [(i, (i + k) % size) for i in range(size)])  8.52 us
    ppermute x12, waiting for transfers between devices, across(): return lax.ppermute(value, 'graph', [(i, i ^ k) for i in range(peers)])  8.18 us
    all_gather x1, blocking collectives, local(): cots = lax.all_gather(own_cot, 'feat', axis=0, tiled=True)  5.63 us
    pallas_call x1, Pallas kernels, list_operator(): call(functools.partial(operator_kernel, blocks_dev, slots_here, groups),...  3.11 us
    ppermute x7, starting transfers between devices, ahead(): return lax.ppermute(value, axis, [(i, (i + k) % size) for i in range(size)])  2.47 us
    pallas_call x1, Pallas kernels, prepare(): call(functools.partial(prepare_kernel, peers), 'prepare', [shape((blocks_...  1.84 us
  transfers between devices with their start and end apart: 19, of which 7 were waited for; matrix products, arithmetic and copies ran while one was open for 0% of the time, Pallas kernels for 11%

profile of v12, /device:TPU:0, one launch (start us, length us, event | category | flops | bytes accessed | tf_op | source)
XLA Modules:
  0.0 55.6 jit_solution(18164844970770486097)
XLA Ops:
  1.3 1.8 %prepare.1 = (bf16[4,128,128]{2,1,0:T(8,128)(2,1)}, s32[8192,128]{1,0:T(8,128)}) custom-call(s32[1]{0:T(128)S(6)} %copy.10.count_ref, s32[1,128]{1,0:T(1,128)} %bitcast.2, s32[1,128]{1,0:T(1,128)} %bitcast.3, bf16[8,128,128]{2,1,0:T(8,128)(2,1)} %refs_4_.3), custom_call_target="tpu_custom_call" | custom-call | bytes 262144 | tf_op jit(solution)/shard_map/prepare/pallas_call | solution.py:104
  3.1 4.1 %collective-permute-start.4 = (bf16[4,128,128]{2,1,0:T(8,128)(2,1)}, bf16[4,128,128]{2,1,0:T(8,128)(2,1)S(1)}, u32[]{:S(2)}, u32[]{:S(2)}) collective-permute-start(bf16[4,128,128]{2,1,0:T(8,128)(2,1)} %get-tuple-element.65), channel_id=1, source_target_pairs={{0,8},{4,12},{8,0},{12,4},{1,9},{5,13},{9,1},{13,5},{2,10},{6,14},... | collective-permute-start | bytes 393224 | tf_op jit(solution)/shard_map/ppermute | solution.py:626
  7.2 1.6 %collective-permute-start.3 = (bf16[4,128,128]{2,1,0:T(8,128)(2,1)}, bf16[4,128,128]{2,1,0:T(8,128)(2,1)S(1)}, u32[]{:S(2)}, u32[]{:S(2)}) collective-permute-start(bf16[4,128,128]{2,1,0:T(8,128)(2,1)} %get-tuple-element.65), channel_id=1, source_target_pairs={{0,4},{4,0},{8,12},{12,8},{1,5},{5,1},{9,13},{13,9},{2,6},{6,2},{1... | collective-permute-start | bytes 393224 | tf_op jit(solution)/shard_map/ppermute | solution.py:626
  8.8 3.1 %operator.1 = (bf16[1024,1024]{1,0:T(8,128)(2,1)S(1)}, s32[1,128]{1,0:T(1,128)S(1)}, s32[1,128]{1,0:T(1,128)S(1)}, s32[1,128]{1,0:T(1,128)S(1)}, s32[1,128]{1,0:T(1,128)S(1)}) custom-call(s32[8192,128]{1,0:T(8,128)} %get-tuple-element.56.table_in, bf16[128,128,128]{2,1,0:T(8,128)(2,1)} %tiles_ref.1), custom_call_target="tpu_custom_call" | custom-call | bytes 16777216 | tf_op jit(solution)/shard_map/operator/pallas_call | solution.py:190
  12.8 2.5 %collective-permute-start.2 = (bf16[144,256]{1,0:T(8,128)(2,1)S(1)}, bf16[144,256]{1,0:T(8,128)(2,1)S(1)}, u32[]{:S(2)}, u32[]{:S(2)}) collective-permute-start(bf16[144,256]{1,0:T(8,128)(2,1)S(1)} %get-tuple-element.64), channel_id=1, source_target_pairs={{0,12},{4,8},{8,4},{12,0},{1,13},{5,9},{9,5},{13,1},{2,14},{6,10},... | collective-permute-start | bytes 221192 | tf_op jit(solution)/shard_map/ppermute | solution.py:626
  15.3 0.7 %collective-permute-start = (bf16[144,256]{1,0:T(8,128)(2,1)S(1)}, bf16[144,256]{1,0:T(8,128)(2,1)S(1)}, u32[]{:S(2)}, u32[]{:S(2)}) collective-permute-start(bf16[144,256]{1,0:T(8,128)(2,1)S(1)} %get-tuple-element.62), channel_id=1, source_target_pairs={{0,4},{4,0},{8,12},{12,8},{1,5},{5,1},{9,13},{13,9},{2,6},{6,2},{1... | collective-permute-start | bytes 221192 | tf_op jit(solution)/shard_map/ppermute | solution.py:626
  16.0 1.4 %collective-permute-start.5 = (bf16[2,128,128]{2,1,0:T(8,128)(2,1)S(1)}, bf16[2,128,128]{2,1,0:T(8,128)(2,1)S(1)}, u32[]{:S(2)}, u32[]{:S(2)}) collective-permute-start(bf16[2,128,128]{2,1,0:T(8,128)(2,1)S(1)} %get-tuple-element.69), channel_id=1, source_target_pairs={{0,4},{4,0},{8,12},{12,8},{1,5},{5,1},{9,13},{13,9},{2,6},{6,2},{1... | collective-permute-start | bytes 196616 | tf_op jit(solution)/shard_map/ppermute | solution.py:626
  17.4 0.7 %collective-permute-start.6 = (bf16[2,128,128]{2,1,0:T(8,128)(2,1)S(1)}, bf16[2,128,128]{2,1,0:T(8,128)(2,1)S(1)}, u32[]{:S(2)}, u32[]{:S(2)}) collective-permute-start(bf16[2,128,128]{2,1,0:T(8,128)(2,1)S(1)} %get-tuple-element.70), channel_id=1, source_target_pairs={{0,4},{4,0},{8,12},{12,8},{1,5},{5,1},{9,13},{13,9},{2,6},{6,2},{1... | collective-permute-start | bytes 196616 | tf_op jit(solution)/shard_map/ppermute | solution.py:626
  18.1 5.6 %all_gather.3.in_ref = bf16[8,128,128]{2,1,0:T(8,128)(2,1)S(1)} all-gather(bf16[4,128,128]{2,1,0:T(8,128)(2,1)S(1)} %get-tuple-element.71), channel_id=1, replica_groups=mesh['parts'=2,'graph'=4,'feat'=2,'rep'=2] {'feat'}, dimensions={0}, use_global_device_ids=true | all-gather | bytes 393216 | tf_op jit(solution)/shard_map/all_gather | solution.py:643
  24.3 1.3 %collective-permute-done.7.refs_5_ = bf16[12,128,128]{2,1,0:T(8,128)(2,1)S(1)} collective-permute-done((bf16[12,128,128]{2,1,0:T(8,128)(2,1)S(1)}, bf16[12,128,128]{2,1,0:T(8,128)(2,1)S(1)}, u32[]{:S(2)}, u32[]{:S(2)}) %collective-permute-start.7) | collective-permute-done | bytes 393248 | tf_op jit(solution)/shard_map/ppermute | solution.py:622
  26.7 0.8 %collective-permute-done.8.came_ref = bf16[4,128,128]{2,1,0:T(8,128)(2,1)S(1)} collective-permute-done((bf16[4,128,128]{2,1,0:T(8,128)(2,1)S(1)}, bf16[4,128,128]{2,1,0:T(8,128)(2,1)S(1)}, u32[]{:S(2)}, u32[]{:S(2)}) %collective-permute-start.8) | collective-permute-done | bytes 131104 | tf_op jit(solution)/shard_map/ppermute | solution.py:622
  27.5 1.6 %collective-permute-start.9 = (bf16[4,128,128]{2,1,0:T(8,128)(2,1)S(1)}, bf16[4,128,128]{2,1,0:T(8,128)(2,1)S(1)}, u32[]{:S(2)}, u32[]{:S(2)}) collective-permute-start(bf16[4,128,128]{2,1,0:T(8,128)(2,1)S(1)} %add_up.1.refs_0_), channel_id=1, source_target_pairs={{0,2},{2,0},{1,3},{3,1},{4,6},{6,4},{5,7},{7,5},{8,10},{10,8},{9,1... | collective-permute-start | bytes 393224 | tf_op jit(solution)/shard_map/ppermute | solution.py:622
  29.1 4.0 %collective-permute-done.9.refs_1_ = bf16[4,128,128]{2,1,0:T(8,128)(2,1)S(1)} collective-permute-done((bf16[4,128,128]{2,1,0:T(8,128)(2,1)S(1)}, bf16[4,128,128]{2,1,0:T(8,128)(2,1)S(1)}, u32[]{:S(2)}, u32[]{:S(2)}) %collective-permute-start.9) | collective-permute-done | bytes 131104 | tf_op jit(solution)/shard_map/ppermute | solution.py:622
  33.1 0.6 %dense.1 = (bf16[4,128,128]{2,1,0:T(8,128)(2,1)S(1)}, bf16[128,1024]{1,0:T(8,128)(2,1)S(1)}, bf16[4,128,128]{2,1,0:T(8,128)(2,1)S(1)}, bf16[128,256]{1,0:T(8,128)(2,1)S(1)}) custom-call(bf16[4,128,128]{2,1,0:T(8,128)(2,1)S(1)} %add_up.1.refs_0_, bf16[4,128,128]{2,1,0:T(8,128)(2,1)S(1)} %collective-permute-done.9.refs_1_, bf16[256,512]{1,0:T(8,128)(2,1)S(1)} %widen.1.refs_2_, ...), custom_call_target="tpu_custom_call" | custom-call | flops 268435456 | bytes 1048576 | tf_op jit(solution)/shard_map/dense/pallas_call | solution.py:501
  33.8 1.4 %collective-permute-start.10 = (bf16[128,256]{1,0:T(8,128)(2,1)S(1)}, bf16[128,256]{1,0:T(8,128)(2,1)S(1)}, u32[]{:S(2)}, u32[]{:S(2)}) collective-permute-start(bf16[128,256]{1,0:T(8,128)(2,1)S(1)} %get-tuple-element.88.mine_ref), channel_id=1, source_target_pairs={{0,4},{4,0},{8,12},{12,8},{1,5},{5,1},{9,13},{13,9},{2,6},{6,2},{1... | collective-permute-start | bytes 196616 | tf_op jit(solution)/shard_map/ppermute | solution.py:626
  35.8 1.4 %collective-permute-start.12 = (bf16[128,512]{1,0:T(8,128)(2,1)S(1)}, bf16[128,512]{1,0:T(8,128)(2,1)S(1)}, u32[]{:S(2)}, u32[]{:S(2)}) collective-permute-start(bf16[128,512]{1,0:T(8,128)(2,1)S(1)} %get-tuple-element.98), channel_id=1, source_target_pairs={{0,8},{4,12},{8,0},{12,4},{1,9},{5,13},{9,1},{13,5},{2,10},{6,14},... | collective-permute-start | bytes 393224 | tf_op jit(solution)/shard_map/ppermute | solution.py:626
  37.3 2.3 %collective-permute-start.13 = (bf16[128,512]{1,0:T(8,128)(2,1)S(1)}, bf16[128,512]{1,0:T(8,128)(2,1)S(1)}, u32[]{:S(2)}, u32[]{:S(2)}) collective-permute-start(bf16[128,512]{1,0:T(8,128)(2,1)S(1)} %get-tuple-element.99), channel_id=1, source_target_pairs={{0,12},{4,8},{8,4},{12,0},{1,13},{5,9},{9,5},{13,1},{2,14},{6,10},... | collective-permute-start | bytes 393224 | tf_op jit(solution)/shard_map/ppermute | solution.py:626
  39.6 0.7 %split_sum.1 = (bf16[128,128]{1,0:T(8,128)(2,1)S(1)}, f32[128,128]{1,0:T(8,128)S(1)}, bf16[8,128,128]{2,1,0:T(8,128)(2,1)}) custom-call(bf16[128,256]{1,0:T(8,128)(2,1)S(1)} %get-tuple-element.88.mine_ref, bf16[128,256]{1,0:T(8,128)(2,1)S(1)} %collective-permute-done.10.came_ref, bf16[4,128,128]{2,1,0:T(8,128)(2,1)S(1)} %get-tuple-element.89.act_ref, ...), custom_call_target="tpu_custom_call" | custom-call | bytes 262144 | tf_op jit(solution)/shard_map/split_sum/pallas_call | solution.py:584
  40.4 1.2 %collective-permute-done.15.came_ref = bf16[128,128]{1,0:T(8,128)(2,1)S(1)} collective-permute-done((bf16[128,128]{1,0:T(8,128)(2,1)S(1)}, bf16[128,128]{1,0:T(8,128)(2,1)S(1)}, u32[]{:S(2)}, u32[]{:S(2)}) %collective-permute-start.15) | collective-permute-done | bytes 32800 | tf_op jit(solution)/shard_map/ppermute | solution.py:622
  41.6 2.1 %collective-permute-start.16 = (bf16[128,128]{1,0:T(8,128)(2,1)S(1)}, bf16[128,128]{1,0:T(8,128)(2,1)S(1)}, u32[]{:S(2)}, u32[]{:S(2)}) collective-permute-start(bf16[128,128]{1,0:T(8,128)(2,1)S(1)} %pair_sum.2.mine_ref), channel_id=1, source_target_pairs={{0,8},{4,12},{8,0},{12,4},{1,9},{5,13},{9,1},{13,5},{2,10},{6,14},... | collective-permute-start | bytes 98312 | tf_op jit(solution)/shard_map/ppermute | solution.py:626
  44.1 8.1 %collective-permute-done.16.came_ref = bf16[128,128]{1,0:T(8,128)(2,1)S(1)} collective-permute-done((bf16[128,128]{1,0:T(8,128)(2,1)S(1)}, bf16[128,128]{1,0:T(8,128)(2,1)S(1)}, u32[]{:S(2)}, u32[]{:S(2)}) %collective-permute-start.16) | collective-permute-done | bytes 32800 | tf_op jit(solution)/shard_map/ppermute | solution.py:626
  52.3 0.7 %late_rows.3.mine_ref = bf16[8,128,128]{2,1,0:T(8,128)(2,1)S(1)} custom-call(f32[8,128,128]{2,1,0:T(8,128)S(1)} %late_rows.2.refs_0_, s32[1,128]{1,0:T(1,128)S(1)} %get-tuple-element.93.refs_1_, s32[1,128]{1,0:T(1,128)S(1)} %get-tuple-element.94.refs_2_, s32[1,128]{1,0:T(1,128)S(1)} %get-tuple-element.92.refs_0_.refs_3_, ...), custom_call_target="tpu_custom_call" | custom-call | flops 134217728 | bytes 1048576 | tf_op jit(solution)/shard_map/late_rows/pallas_call | solution.py:438
  53.6 1.1 %collective-permute-done.18.other_share_ref = f32[128,128]{1,0:T(8,128)S(1)} collective-permute-done((f32[128,128]{1,0:T(8,128)S(1)}, f32[128,128]{1,0:T(8,128)S(1)}, u32[]{:S(2)}, u32[]{:S(2)}) %collective-permute-start.18) | collective-permute-done | bytes 65568 | tf_op jit(solution)/shard_map/ppermute | solution.py:622
  54.7 0.9 %finish.1 = (bf16[8,128,128]{2,1,0:T(8,128)(2,1)}, f32[256,128]{1,0:T(8,128)}) custom-call(bf16[8,128,128]{2,1,0:T(8,128)(2,1)S(1)} %late_rows.3.mine_ref, bf16[8,128,128]{2,1,0:T(8,128)(2,1)S(1)} %collective-permute-done.17.other_ref, f32[128,128]{1,0:T(8,128)S(1)} %pair_sum.3.share_ref, f32[128,128]{1,0:T(8,128)S(1)} %collective-permute-done.18.other_share_ref), custom_call_target="tpu_custom_call" | custom-call | bytes 262144 | tf_op jit(solution)/shard_map/finish/pallas_call | solution.py:613
  (39 shorter events, 4.2 us)
Async XLA Ops:
  3.1 12.8 %collective-permute-start.4 = (bf16[4,128,128]{2,1,0:T(8,128)(2,1)}, bf16[4,128,128]{2,1,0:T(8,128)(2,1)S(1)}, u32[]{:S(2)}, u32[]{:S(2)}) collective-permute-start(bf16[4,128,128]{2,1,0:T(8,128)(2,1)} %get-tuple-element.65), channel_id=1, source_target_pairs={{0,8},{4,12},{8,0},{12,4},{1,9},{5,13},{9,1},{13,5},{2,10},{6,14},... | collective-permute-start | bytes 393224 | tf_op jit(solution)/shard_map/ppermute | solution.py:626
  7.2 8.7 %collective-permute-start.3 = (bf16[4,128,128]{2,1,0:T(8,128)(2,1)}, bf16[4,128,128]{2,1,0:T(8,128)(2,1)S(1)}, u32[]{:S(2)}, u32[]{:S(2)}) collective-permute-start(bf16[4,128,128]{2,1,0:T(8,128)(2,1)} %get-tuple-element.65), channel_id=1, source_target_pairs={{0,4},{4,0},{8,12},{12,8},{1,5},{5,1},{9,13},{13,9},{2,6},{6,2},{1... | collective-permute-start | bytes 393224 | tf_op jit(solution)/shard_map/ppermute | solution.py:626
  8.8 3.1 %copy-start = (bf16[8,128,128]{2,1,0:T(8,128)(2,1)S(1)}, bf16[8,128,128]{2,1,0:T(8,128)(2,1)}, u32[]{:S(2)}) copy-start(bf16[8,128,128]{2,1,0:T(8,128)(2,1)} %refs_4_.3) | copy-start | bytes 786436
  8.8 3.1 %copy-start.1 = (bf16[8,128,128]{2,1,0:T(8,128)(2,1)S(1)}, bf16[8,128,128]{2,1,0:T(8,128)(2,1)}, u32[]{:S(2)}) copy-start(bf16[8,128,128]{2,1,0:T(8,128)(2,1)} %refs_4_.2) | copy-start | bytes 786436
  12.4 11.3 %collective-permute-start.1 = (bf16[144,256]{1,0:T(8,128)(2,1)S(1)}, bf16[144,256]{1,0:T(8,128)(2,1)S(1)}, u32[]{:S(2)}, u32[]{:S(2)}) collective-permute-start(bf16[144,256]{1,0:T(8,128)(2,1)S(1)} %get-tuple-element.63), channel_id=1, source_target_pairs={{0,8},{4,12},{8,0},{12,4},{1,9},{5,13},{9,1},{13,5},{2,10},{6,14},... | collective-permute-start | bytes 221192 | tf_op jit(solution)/shard_map/ppermute | solution.py:626
  12.8 10.9 %collective-permute-start.2 = (bf16[144,256]{1,0:T(8,128)(2,1)S(1)}, bf16[144,256]{1,0:T(8,128)(2,1)S(1)}, u32[]{:S(2)}, u32[]{:S(2)}) collective-permute-start(bf16[144,256]{1,0:T(8,128)(2,1)S(1)} %get-tuple-element.64), channel_id=1, source_target_pairs={{0,12},{4,8},{8,4},{12,0},{1,13},{5,9},{9,5},{13,1},{2,14},{6,10},... | collective-permute-start | bytes 221192 | tf_op jit(solution)/shard_map/ppermute | solution.py:626
  15.3 8.5 %collective-permute-start = (bf16[144,256]{1,0:T(8,128)(2,1)S(1)}, bf16[144,256]{1,0:T(8,128)(2,1)S(1)}, u32[]{:S(2)}, u32[]{:S(2)}) collective-permute-start(bf16[144,256]{1,0:T(8,128)(2,1)S(1)} %get-tuple-element.62), channel_id=1, source_target_pairs={{0,4},{4,0},{8,12},{12,8},{1,5},{5,1},{9,13},{13,9},{2,6},{6,2},{1... | collective-permute-start | bytes 221192 | tf_op jit(solution)/shard_map/ppermute | solution.py:626
  16.0 7.7 %collective-permute-start.5 = (bf16[2,128,128]{2,1,0:T(8,128)(2,1)S(1)}, bf16[2,128,128]{2,1,0:T(8,128)(2,1)S(1)}, u32[]{:S(2)}, u32[]{:S(2)}) collective-permute-start(bf16[2,128,128]{2,1,0:T(8,128)(2,1)S(1)} %get-tuple-element.69), channel_id=1, source_target_pairs={{0,4},{4,0},{8,12},{12,8},{1,5},{5,1},{9,13},{13,9},{2,6},{6,2},{1... | collective-permute-start | bytes 196616 | tf_op jit(solution)/shard_map/ppermute | solution.py:626
  17.4 6.3 %collective-permute-start.6 = (bf16[2,128,128]{2,1,0:T(8,128)(2,1)S(1)}, bf16[2,128,128]{2,1,0:T(8,128)(2,1)S(1)}, u32[]{:S(2)}, u32[]{:S(2)}) collective-permute-start(bf16[2,128,128]{2,1,0:T(8,128)(2,1)S(1)} %get-tuple-element.70), channel_id=1, source_target_pairs={{0,4},{4,0},{8,12},{12,8},{1,5},{5,1},{9,13},{13,9},{2,6},{6,2},{1... | collective-permute-start | bytes 196616 | tf_op jit(solution)/shard_map/ppermute | solution.py:626
  23.8 1.8 %collective-permute-start.7 = (bf16[12,128,128]{2,1,0:T(8,128)(2,1)S(1)}, bf16[12,128,128]{2,1,0:T(8,128)(2,1)S(1)}, u32[]{:S(2)}, u32[]{:S(2)}) collective-permute-start(bf16[12,128,128]{2,1,0:T(8,128)(2,1)S(1)} %stack.1.refs_4_), channel_id=1, source_target_pairs={{0,1},{1,0},{2,3},{3,2},{4,5},{5,4},{6,7},{7,6},{8,9},{9,8},{10,11... | collective-permute-start | bytes 1179656 | tf_op jit(solution)/shard_map/ppermute | solution.py:622
  24.3 8.8 %copy-start.2 = (bf16[256,256]{1,0:T(8,128)(2,1)S(1)}, bf16[256,256]{1,0:T(8,128)(2,1)}, u32[]{:S(2)}) copy-start(bf16[256,256]{1,0:T(8,128)(2,1)} %refs_3_.3) | copy-start | bytes 393220
  26.1 1.4 %collective-permute-start.8 = (bf16[4,128,128]{2,1,0:T(8,128)(2,1)S(1)}, bf16[4,128,128]{2,1,0:T(8,128)(2,1)S(1)}, u32[]{:S(2)}, u32[]{:S(2)}) collective-permute-start(bf16[4,128,128]{2,1,0:T(8,128)(2,1)S(1)} %get-tuple-element.86), channel_id=1, source_target_pairs={{0,1},{1,0},{2,3},{3,2},{4,5},{5,4},{6,7},{7,6},{8,9},{9,8},{10,11... | collective-permute-start | bytes 393224 | tf_op jit(solution)/shard_map/ppermute | solution.py:622
  27.5 5.6 %collective-permute-start.9 = (bf16[4,128,128]{2,1,0:T(8,128)(2,1)S(1)}, bf16[4,128,128]{2,1,0:T(8,128)(2,1)S(1)}, u32[]{:S(2)}, u32[]{:S(2)}) collective-permute-start(bf16[4,128,128]{2,1,0:T(8,128)(2,1)S(1)} %add_up.1.refs_0_), channel_id=1, source_target_pairs={{0,2},{2,0},{1,3},{3,1},{4,6},{6,4},{5,7},{7,5},{8,10},{10,8},{9,1... | collective-permute-start | bytes 393224 | tf_op jit(solution)/shard_map/ppermute | solution.py:622
  33.8 1.6 %collective-permute-start.11 = (bf16[128,1024]{1,0:T(8,128)(2,1)S(1)}, bf16[128,1024]{1,0:T(8,128)(2,1)S(1)}, u32[]{:S(2)}, u32[]{:S(2)}) collective-permute-start(bf16[128,1024]{1,0:T(8,128)(2,1)S(1)} %get-tuple-element.90), channel_id=1, source_target_pairs={{0,1},{1,0},{2,3},{3,2},{4,5},{5,4},{6,7},{7,6},{8,9},{9,8},{10,11... | collective-permute-start | bytes 786440 | tf_op jit(solution)/shard_map/ppermute | solution.py:622
  33.8 5.8 %collective-permute-start.10 = (bf16[128,256]{1,0:T(8,128)(2,1)S(1)}, bf16[128,256]{1,0:T(8,128)(2,1)S(1)}, u32[]{:S(2)}, u32[]{:S(2)}) collective-permute-start(bf16[128,256]{1,0:T(8,128)(2,1)S(1)} %get-tuple-element.88.mine_ref), channel_id=1, source_target_pairs={{0,4},{4,0},{8,12},{12,8},{1,5},{5,1},{9,13},{13,9},{2,6},{6,2},{1... | collective-permute-start | bytes 196616 | tf_op jit(solution)/shard_map/ppermute | solution.py:626
  35.8 16.4 %collective-permute-start.12 = (bf16[128,512]{1,0:T(8,128)(2,1)S(1)}, bf16[128,512]{1,0:T(8,128)(2,1)S(1)}, u32[]{:S(2)}, u32[]{:S(2)}) collective-permute-start(bf16[128,512]{1,0:T(8,128)(2,1)S(1)} %get-tuple-element.98), channel_id=1, source_target_pairs={{0,8},{4,12},{8,0},{12,4},{1,9},{5,13},{9,1},{13,5},{2,10},{6,14},... | collective-permute-start | bytes 393224 | tf_op jit(solution)/shard_map/ppermute | solution.py:626
  37.3 15.0 %collective-permute-start.13 = (bf16[128,512]{1,0:T(8,128)(2,1)S(1)}, bf16[128,512]{1,0:T(8,128)(2,1)S(1)}, u32[]{:S(2)}, u32[]{:S(2)}) collective-permute-start(bf16[128,512]{1,0:T(8,128)(2,1)S(1)} %get-tuple-element.99), channel_id=1, source_target_pairs={{0,12},{4,8},{8,4},{12,0},{1,13},{5,9},{9,5},{13,1},{2,14},{6,10},... | collective-permute-start | bytes 393224 | tf_op jit(solution)/shard_map/ppermute | solution.py:626
  39.6 12.6 %collective-permute-start.14 = (bf16[128,512]{1,0:T(8,128)(2,1)S(1)}, bf16[128,512]{1,0:T(8,128)(2,1)S(1)}, u32[]{:S(2)}, u32[]{:S(2)}) collective-permute-start(bf16[128,512]{1,0:T(8,128)(2,1)S(1)} %get-tuple-element.100), channel_id=1, source_target_pairs={{0,4},{4,0},{8,12},{12,8},{1,5},{5,1},{9,13},{13,9},{2,6},{6,2},{1... | collective-permute-start | bytes 393224 | tf_op jit(solution)/shard_map/ppermute | solution.py:626
  40.4 1.2 %collective-permute-start.15 = (bf16[128,128]{1,0:T(8,128)(2,1)S(1)}, bf16[128,128]{1,0:T(8,128)(2,1)S(1)}, u32[]{:S(2)}, u32[]{:S(2)}) collective-permute-start(bf16[128,128]{1,0:T(8,128)(2,1)S(1)} %get-tuple-element.102), channel_id=1, source_target_pairs={{0,1},{1,0},{2,3},{3,2},{4,5},{5,4},{6,7},{7,6},{8,9},{9,8},{10,11... | collective-permute-start | bytes 98312 | tf_op jit(solution)/shard_map/ppermute | solution.py:622
  41.6 10.6 %collective-permute-start.16 = (bf16[128,128]{1,0:T(8,128)(2,1)S(1)}, bf16[128,128]{1,0:T(8,128)(2,1)S(1)}, u32[]{:S(2)}, u32[]{:S(2)}) collective-permute-start(bf16[128,128]{1,0:T(8,128)(2,1)S(1)} %pair_sum.2.mine_ref), channel_id=1, source_target_pairs={{0,8},{4,12},{8,0},{12,4},{1,9},{5,13},{9,1},{13,5},{2,10},{6,14},... | collective-permute-start | bytes 98312 | tf_op jit(solution)/shard_map/ppermute | solution.py:626
  53.0 1.7 %collective-permute-start.17 = (bf16[8,128,128]{2,1,0:T(8,128)(2,1)S(1)}, bf16[8,128,128]{2,1,0:T(8,128)(2,1)S(1)}, u32[]{:S(2)}, u32[]{:S(2)}) collective-permute-start(bf16[8,128,128]{2,1,0:T(8,128)(2,1)S(1)} %late_rows.3.mine_ref), channel_id=1, source_target_pairs={{0,1},{1,0},{2,3},{3,2},{4,5},{5,4},{6,7},{7,6},{8,9},{9,8},{10,11... | collective-permute-start | bytes 786440 | tf_op jit(solution)/shard_map/ppermute | solution.py:622
  53.1 1.6 %collective-permute-start.18 = (f32[128,128]{1,0:T(8,128)S(1)}, f32[128,128]{1,0:T(8,128)S(1)}, u32[]{:S(2)}, u32[]{:S(2)}) collective-permute-start(f32[128,128]{1,0:T(8,128)S(1)} %pair_sum.3.share_ref), channel_id=1, source_target_pairs={{0,1},{1,0},{2,3},{3,2},{4,5},{5,4},{6,7},{7,6},{8,9},{9,8},{10,11... | collective-permute-start | bytes 196616 | tf_op jit(solution)/shard_map/ppermute | solution.py:622

commit v13 on v12

--- a/solution.py
+++ b/solution.py
@@ -224,10 +224,13 @@
 def first_sends_kernel(peers, *refs):
     ask_refs, refs = refs[: peers - 1], refs[peers - 1 :]
     x3, cot, m_ref, refs = refs[0], refs[1], refs[2], refs[3:]
-    send_refs, self_ref, cot_ref, mir = refs[: peers - 1], refs[peers - 1], refs[peers], refs[peers + 1]
+    send_refs, self_ref, cot_refs, mir = refs[: peers - 1], refs[peers - 1], refs[peers : peers + 2], refs[peers + 2]
     _, columns, width = x3.shape
-    share = cot_ref.shape[0]
-    cot_ref[...] = cot[pl.ds(lax.axis_index("rep") * share, share)]
+    first = lax.axis_index("rep") * (x3.shape[0] // 2)
+    for cot_ref in cot_refs:
+        part = cot_ref.shape[0]
+        cot_ref[...] = cot[pl.ds(first, part)]
+        first = first + part
     both = CAP * width
     mirrored(lanes(x3), m_ref, mir, peers * CAP, width)
     self_ref[...] = mir[:, :both]
@@ -245,13 +248,14 @@
         functools.partial(first_sends_kernel, peers),
         "first_sends",
         [shape((columns + TAIL, CAP * width), BF16)] * (peers - 1)
-        + [shape((columns, CAP * width), F32), shape((blocks_dev // reps, columns, width), BF16)],
+        + [shape((columns, CAP * width), F32)]
+        + [shape((blocks_dev // reps // 2, columns, width), BF16)] * 2,
         [vmem()] * (peers + 2),
         [pltpu.VMEM((columns, peers * CAP * width), F32)],
         flops=2 ** 28,
         moved=2 ** 21,
     )(*asks, values, cotangent, operator)
-    return [None] + list(outs[: peers - 1]), outs[peers - 1], outs[peers]
+    return [None] + list(outs[: peers - 1]), outs[peers - 1], outs[peers], outs[peers + 1]
 
 
 def add_sums(acc, block, sums):
@@ -454,41 +458,44 @@
     return call(add_kernel, "add_up", shape(came.shape, BF16), [vmem(), vmem()])(keep, came)
 
 
-def widen_kernel(feats, in_ref, out_ref):
-    _, columns, width = in_ref.shape
-    share = out_ref.shape[1] // width
+def widen_kernel(feats, gathered, *refs):
+    parts, out_ref = refs[:feats], refs[feats]
+    share, columns, width = parts[0].shape
+    me = lax.axis_index("feat")
     for f in range(feats):
+        rows = pl.ds(pl.multiple_of(lax.rem(me + f, feats) * columns, columns), columns)
         for b in range(share):
-            out_ref[f * columns : (f + 1) * columns, b * width : (b + 1) * width] = in_ref[f * share + b]
-
-
-def widen(parts, feats):
-    blocks, columns, width = parts.shape
-    out = shape((feats * columns, blocks // feats * width), BF16)
-    return call(functools.partial(widen_kernel, feats), "widen", out, [vmem()])(parts)
-
-
-def dense_kernel(feats, *refs):
-    sums, wide_cot, refs = refs[:feats], refs[feats], refs[feats + 1 :]
+            out_ref[f * columns : (f + 1) * columns, b * width : (b + 1) * width] = gathered[f * share + b]
+            out_ref[rows, (share + b) * width : (share + b + 1) * width] = parts[f][b]
+
+
+def widen(gathered, parts):
+    share, columns, width = parts[0].shape
+    feats = len(parts)
+    out = shape((feats * columns, 2 * share * width), BF16)
+    return call(functools.partial(widen_kernel, feats), "widen", out, [vmem()] * (feats + 1))(gathered, *parts)
+
+
+def dense_kernel(feats, sums, wide_cot, *refs):
     w_ref, act_ref, give_ref, spread_ref, term_ref, wide, pre_scr, grad = refs
     share, columns, width = act_ref.shape
     me = lax.axis_index("feat")
-    rows = [pl.ds(pl.multiple_of(lax.rem(me + q, feats) * columns, columns), columns) for q in range(feats)]
-    for q in range(feats):
+    mine = pl.ds(pl.multiple_of(me * columns, columns), columns)
+    for f in range(feats):
         for b in range(share):
-            wide[rows[q], b * width : (b + 1) * width] = sums[q][b]
+            wide[f * columns : (f + 1) * columns, b * width : (b + 1) * width] = sums[f * share + b]
     pre = dot(w_ref[...], wide[...], TN)
     pre_scr[...] = pre
     sig = jax.nn.sigmoid(pre)
     factor = wide_cot[...].astype(F32) * sig * (1.0 + pre * (1.0 - sig))
     grad[...] = factor.astype(BF16)
-    spread = dot(w_ref[rows[0], :], grad[...]).astype(BF16)
-    term_ref[...] = dot(grad[rows[0], :], wide[...], NT).astype(BF16)
+    spread = dot(w_ref[mine, :], grad[...]).astype(BF16)
+    term_ref[...] = dot(grad[mine, :], wide[...], NT).astype(BF16)
     wide_share = share * width
     give_ref[:, :wide_share] = spread
     for b in range(share):
         spread_ref[b] = spread[:, b * width : (b + 1) * width]
-    own = pre_scr[rows[0], :]
+    own = pre_scr[mine, :]
     act = (own * jax.nn.sigmoid(own)).astype(BF16)
     give_ref[:, wide_share:] = act
     for b in range(share):
@@ -496,7 +503,8 @@
 
 
 def dense(sums, cot, weight, feats):
-    share, columns, width = sums[0].shape
+    blocks, columns, width = sums.shape
+    share = blocks // feats
     features = weight.shape[0]
     return call(
         functools.partial(dense_kernel, feats),
@@ -507,7 +515,7 @@
             shape((share, columns, width), BF16),
             shape((columns, features), BF16),
         ],
-        [vmem()] * (feats + 2),
+        [vmem()] * 3,
         [
             pltpu.VMEM((features, share * width), BF16),
             pltpu.VMEM((features, share * width), F32),
@@ -515,7 +523,7 @@
         ],
         flops=2 ** 28,
         moved=2 ** 20,
-    )(*sums, cot, weight)
+    )(sums, cot, weight)
 
 
 def send_kernel(peers, *refs):
@@ -639,8 +647,8 @@
 
     half, table = prepare(features, tile_row, tile_col, tile_count, peers, reps)
     operator, asks = list_operator(tiles, table, peers, blocks_dev)
-    sends, own_mirror, own_cot = first_sends(features, cotangent, operator, asks[1:], peers, reps)
-    cots = lax.all_gather(own_cot, "feat", axis=0, tiled=True)
+    sends, own_mirror, cot_a, cot_b = first_sends(features, cotangent, operator, asks[1:], peers, reps)
+    cots = lax.all_gather(cot_a, "feat", axis=0, tiled=True)
     pieces, held = {0: [half]}, [0]
     bit = peers // 2
     while bit:
@@ -665,8 +673,9 @@
     keep = keep_rows(acc, asked, operator, reps)
 
     mine = add_up(keep, ahead(give, "rep", reps, 1))
-    cot = widen(cots, feats)
-    sums = [mine] + [ahead(mine, "feat", feats, feats - q) for q in range(1, feats)]
+    waited = after(cot_b, stacked)
+    cot = widen(cots, [cot_b] + [ahead(waited, "feat", feats, feats - q) for q in range(1, feats)])
+    sums = lax.all_gather(mine, "feat", axis=0, tiled=True)
     act, give, spread, term = dense(sums, cot, weight, feats)
     shared = ahead(give, "rep", reps, 1)
     total, activated = total_term(term, act, shared, peers, reps)

time: 55.7 us -> 59.1 us (1.061)
  blocking collectives: 5.63 us -> 10.6 us
  waiting for transfers between devices: 16.7 us -> 15.7 us
  starting transfers between devices: 21.1 us -> 20.5 us
    all_gather x1 -> x2, blocking collectives: 5.63 us -> 10.6 us  [the longest x1 5.64 us: local(): sums = lax.all_gather(mine, 'feat', axis=0, tiled=True)]
    ppermute x7, waiting for transfers between devices: 8.52 us -> 7 us  [ahead(): return lax.ppermute(value, axis, [(i, (i + k) % size) for i in range(size)])]
  transfers between devices with their start and end apart: 19 -> 19, of which waited for: 7 -> 7; matrix products, arithmetic and copies ran while one was open for 0% -> 0% of each run, Pallas kernels for 11% -> 10%
where the time goes in v13:
time: 59.1 us; the launch traced here: 58.9 us
  starting transfers between devices  20.5 us (35%)
  waiting for transfers between devices  15.7 us (27%)
  Pallas kernels  10.6 us (18%)
  blocking collectives  10.6 us (18%)
  between operations  1.48 us (3%)
    ppermute x12, starting transfers between devices, across(): return lax.ppermute(value, 'graph', [(i, i ^ k) for i in range(peers)])  18.1 us
    ppermute x12, waiting for transfers between devices, across(): return lax.ppermute(value, 'graph', [(i, i ^ k) for i in range(peers)])  8.72 us
    ppermute x7, waiting for transfers between devices, ahead(): return lax.ppermute(value, axis, [(i, (i + k) % size) for i in range(size)])  7 us
    all_gather x1, blocking collectives, local(): sums = lax.all_gather(mine, 'feat', axis=0, tiled=True)  5.64 us
    all_gather x1, blocking collectives, local(): cots = lax.all_gather(cot_a, 'feat', axis=0, tiled=True)  4.93 us
    pallas_call x1, Pallas kernels, list_operator(): call(functools.partial(operator_kernel, blocks_dev, slots_here, groups),...  3.11 us
    ppermute x7, starting transfers between devices, ahead(): return lax.ppermute(value, axis, [(i, (i + k) % size) for i in range(size)])  2.42 us
    pallas_call x1, Pallas kernels, prepare(): call(functools.partial(prepare_kernel, peers), 'prepare', [shape((blocks_...  1.84 us
  transfers between devices with their start and end apart: 19, of which 7 were waited for; matrix products, arithmetic and copies ran while one was open for 0% of the time, Pallas kernels for 10%

profile of v13, /device:TPU:0, one launch (start us, length us, event | category | flops | bytes accessed | tf_op | source)
XLA Modules:
  0.0 58.9 jit_solution(13938482158412021543)
XLA Ops:
  1.3 1.8 %prepare.1 = (bf16[4,128,128]{2,1,0:T(8,128)(2,1)}, s32[8192,128]{1,0:T(8,128)}) custom-call(s32[1]{0:T(128)S(6)} %copy.10.count_ref, s32[1,128]{1,0:T(1,128)} %bitcast.2, s32[1,128]{1,0:T(1,128)} %bitcast.3, bf16[8,128,128]{2,1,0:T(8,128)(2,1)} %refs_4_.3), custom_call_target="tpu_custom_call" | custom-call | bytes 262144 | tf_op jit(solution)/shard_map/prepare/pallas_call | solution.py:104
  3.1 4.1 %collective-permute-start.4 = (bf16[4,128,128]{2,1,0:T(8,128)(2,1)}, bf16[4,128,128]{2,1,0:T(8,128)(2,1)S(1)}, u32[]{:S(2)}, u32[]{:S(2)}) collective-permute-start(bf16[4,128,128]{2,1,0:T(8,128)(2,1)} %get-tuple-element.67), channel_id=1, source_target_pairs={{0,8},{4,12},{8,0},{12,4},{1,9},{5,13},{9,1},{13,5},{2,10},{6,14},... | collective-permute-start | bytes 393224 | tf_op jit(solution)/shard_map/ppermute | solution.py:634
  7.2 1.6 %collective-permute-start.3 = (bf16[4,128,128]{2,1,0:T(8,128)(2,1)}, bf16[4,128,128]{2,1,0:T(8,128)(2,1)S(1)}, u32[]{:S(2)}, u32[]{:S(2)}) collective-permute-start(bf16[4,128,128]{2,1,0:T(8,128)(2,1)} %get-tuple-element.67), channel_id=1, source_target_pairs={{0,4},{4,0},{8,12},{12,8},{1,5},{5,1},{9,13},{13,9},{2,6},{6,2},{1... | collective-permute-start | bytes 393224 | tf_op jit(solution)/shard_map/ppermute | solution.py:634
  8.8 3.1 %operator.1 = (bf16[1024,1024]{1,0:T(8,128)(2,1)S(1)}, s32[1,128]{1,0:T(1,128)S(1)}, s32[1,128]{1,0:T(1,128)S(1)}, s32[1,128]{1,0:T(1,128)S(1)}, s32[1,128]{1,0:T(1,128)S(1)}) custom-call(s32[8192,128]{1,0:T(8,128)} %get-tuple-element.58.table_in, bf16[128,128,128]{2,1,0:T(8,128)(2,1)} %tiles_ref.1), custom_call_target="tpu_custom_call" | custom-call | bytes 16777216 | tf_op jit(solution)/shard_map/operator/pallas_call | solution.py:190
  12.8 2.5 %collective-permute-start.2 = (bf16[144,256]{1,0:T(8,128)(2,1)S(1)}, bf16[144,256]{1,0:T(8,128)(2,1)S(1)}, u32[]{:S(2)}, u32[]{:S(2)}) collective-permute-start(bf16[144,256]{1,0:T(8,128)(2,1)S(1)} %get-tuple-element.66), channel_id=1, source_target_pairs={{0,12},{4,8},{8,4},{12,0},{1,13},{5,9},{9,5},{13,1},{2,14},{6,10},... | collective-permute-start | bytes 221192 | tf_op jit(solution)/shard_map/ppermute | solution.py:634
  15.3 0.7 %collective-permute-start = (bf16[144,256]{1,0:T(8,128)(2,1)S(1)}, bf16[144,256]{1,0:T(8,128)(2,1)S(1)}, u32[]{:S(2)}, u32[]{:S(2)}) collective-permute-start(bf16[144,256]{1,0:T(8,128)(2,1)S(1)} %get-tuple-element.64), channel_id=1, source_target_pairs={{0,4},{4,0},{8,12},{12,8},{1,5},{5,1},{9,13},{13,9},{2,6},{6,2},{1... | collective-permute-start | bytes 221192 | tf_op jit(solution)/shard_map/ppermute | solution.py:634
  16.0 1.4 %collective-permute-start.5 = (bf16[2,128,128]{2,1,0:T(8,128)(2,1)S(1)}, bf16[2,128,128]{2,1,0:T(8,128)(2,1)S(1)}, u32[]{:S(2)}, u32[]{:S(2)}) collective-permute-start(bf16[2,128,128]{2,1,0:T(8,128)(2,1)S(1)} %get-tuple-element.71), channel_id=1, source_target_pairs={{0,4},{4,0},{8,12},{12,8},{1,5},{5,1},{9,13},{13,9},{2,6},{6,2},{1... | collective-permute-start | bytes 196616 | tf_op jit(solution)/shard_map/ppermute | solution.py:634
  17.4 0.7 %collective-permute-start.6 = (bf16[2,128,128]{2,1,0:T(8,128)(2,1)S(1)}, bf16[2,128,128]{2,1,0:T(8,128)(2,1)S(1)}, u32[]{:S(2)}, u32[]{:S(2)}) collective-permute-start(bf16[2,128,128]{2,1,0:T(8,128)(2,1)S(1)} %get-tuple-element.72), channel_id=1, source_target_pairs={{0,4},{4,0},{8,12},{12,8},{1,5},{5,1},{9,13},{13,9},{2,6},{6,2},{1... | collective-permute-start | bytes 196616 | tf_op jit(solution)/shard_map/ppermute | solution.py:634
  18.1 4.9 %all_gather.6.gathered = bf16[4,128,128]{2,1,0:T(8,128)(2,1)S(1)} all-gather(bf16[2,128,128]{2,1,0:T(8,128)(2,1)S(1)} %get-tuple-element.73), channel_id=1, replica_groups=mesh['parts'=2,'graph'=4,'feat'=2,'rep'=2] {'feat'}, dimensions={0}, use_global_device_ids=true | all-gather | bytes 196608 | tf_op jit(solution)/shard_map/all_gather | solution.py:651
  24.0 1.3 %collective-permute-done.7.refs_5_ = bf16[12,128,128]{2,1,0:T(8,128)(2,1)S(1)} collective-permute-done((bf16[12,128,128]{2,1,0:T(8,128)(2,1)S(1)}, bf16[12,128,128]{2,1,0:T(8,128)(2,1)S(1)}, u32[]{:S(2)}, u32[]{:S(2)}) %collective-permute-start.7) | collective-permute-done | bytes 393248 | tf_op jit(solution)/shard_map/ppermute | solution.py:630
  26.0 1.5 %collective-permute-start.9 = (bf16[2,128,128]{2,1,0:T(8,128)(2,1)S(1)}, bf16[2,128,128]{2,1,0:T(8,128)(2,1)S(1)}, u32[]{:S(2)}, u32[]{:S(2)}) collective-permute-start(bf16[2,128,128]{2,1,0:T(8,128)(2,1)S(1)} %get-tuple-element.91.refs_0_), channel_id=1, source_target_pairs={{0,2},{2,0},{1,3},{3,1},{4,6},{6,4},{5,7},{7,5},{8,10},{10,8},{9,1... | collective-permute-start | bytes 196616 | tf_op jit(solution)/shard_map/ppermute | solution.py:630
  27.5 2.9 %collective-permute-done.9.refs_1_ = bf16[2,128,128]{2,1,0:T(8,128)(2,1)S(1)} collective-permute-done((bf16[2,128,128]{2,1,0:T(8,128)(2,1)S(1)}, bf16[2,128,128]{2,1,0:T(8,128)(2,1)S(1)}, u32[]{:S(2)}, u32[]{:S(2)}) %collective-permute-start.9) | collective-permute-done | bytes 65568 | tf_op jit(solution)/shard_map/ppermute | solution.py:630
  30.9 5.6 %all_gather.7.sums = bf16[8,128,128]{2,1,0:T(8,128)(2,1)S(1)} all-gather(bf16[4,128,128]{2,1,0:T(8,128)(2,1)S(1)} %add_up.1), channel_id=1, replica_groups=mesh['parts'=2,'graph'=4,'feat'=2,'rep'=2] {'feat'}, dimensions={0}, use_global_device_ids=true | all-gather | bytes 393216 | tf_op jit(solution)/shard_map/all_gather | solution.py:678
  36.5 0.6 %dense.1 = (bf16[4,128,128]{2,1,0:T(8,128)(2,1)S(1)}, bf16[128,1024]{1,0:T(8,128)(2,1)S(1)}, bf16[4,128,128]{2,1,0:T(8,128)(2,1)S(1)}, bf16[128,256]{1,0:T(8,128)(2,1)S(1)}) custom-call(bf16[8,128,128]{2,1,0:T(8,128)(2,1)S(1)} %all_gather.7.sums, bf16[256,512]{1,0:T(8,128)(2,1)S(1)} %widen.1.wide_cot, bf16[256,256]{1,0:T(8,128)(2,1)S(1)} %copy-done.2), custom_call_target="tpu_custom_call" | custom-call | flops 268435456 | bytes 1048576 | tf_op jit(solution)/shard_map/dense/pallas_call | solution.py:509
  37.2 1.0 %collective-permute-start.10 = (bf16[128,256]{1,0:T(8,128)(2,1)S(1)}, bf16[128,256]{1,0:T(8,128)(2,1)S(1)}, u32[]{:S(2)}, u32[]{:S(2)}) collective-permute-start(bf16[128,256]{1,0:T(8,128)(2,1)S(1)} %get-tuple-element.92.mine_ref), channel_id=1, source_target_pairs={{0,4},{4,0},{8,12},{12,8},{1,5},{5,1},{9,13},{13,9},{2,6},{6,2},{1... | collective-permute-start | bytes 196616 | tf_op jit(solution)/shard_map/ppermute | solution.py:634
  39.2 1.3 %collective-permute-start.12 = (bf16[128,512]{1,0:T(8,128)(2,1)S(1)}, bf16[128,512]{1,0:T(8,128)(2,1)S(1)}, u32[]{:S(2)}, u32[]{:S(2)}) collective-permute-start(bf16[128,512]{1,0:T(8,128)(2,1)S(1)} %get-tuple-element.102), channel_id=1, source_target_pairs={{0,8},{4,12},{8,0},{12,4},{1,9},{5,13},{9,1},{13,5},{2,10},{6,14},... | collective-permute-start | bytes 393224 | tf_op jit(solution)/shard_map/ppermute | solution.py:634
  40.5 2.0 %collective-permute-start.13 = (bf16[128,512]{1,0:T(8,128)(2,1)S(1)}, bf16[128,512]{1,0:T(8,128)(2,1)S(1)}, u32[]{:S(2)}, u32[]{:S(2)}) collective-permute-start(bf16[128,512]{1,0:T(8,128)(2,1)S(1)} %get-tuple-element.103), channel_id=1, source_target_pairs={{0,12},{4,8},{8,4},{12,0},{1,13},{5,9},{9,5},{13,1},{2,14},{6,10},... | collective-permute-start | bytes 393224 | tf_op jit(solution)/shard_map/ppermute | solution.py:634
  42.7 0.7 %split_sum.1 = (bf16[128,128]{1,0:T(8,128)(2,1)S(1)}, f32[128,128]{1,0:T(8,128)S(1)}, bf16[8,128,128]{2,1,0:T(8,128)(2,1)}) custom-call(bf16[128,256]{1,0:T(8,128)(2,1)S(1)} %get-tuple-element.92.mine_ref, bf16[128,256]{1,0:T(8,128)(2,1)S(1)} %collective-permute-done.10.came_ref, bf16[4,128,128]{2,1,0:T(8,128)(2,1)S(1)} %get-tuple-element.93.act_ref, ...), custom_call_target="tpu_custom_call" | custom-call | bytes 262144 | tf_op jit(solution)/shard_map/split_sum/pallas_call | solution.py:592
  43.5 1.2 %collective-permute-done.15.came_ref = bf16[128,128]{1,0:T(8,128)(2,1)S(1)} collective-permute-done((bf16[128,128]{1,0:T(8,128)(2,1)S(1)}, bf16[128,128]{1,0:T(8,128)(2,1)S(1)}, u32[]{:S(2)}, u32[]{:S(2)}) %collective-permute-start.15) | collective-permute-done | bytes 32800 | tf_op jit(solution)/shard_map/ppermute | solution.py:630
  44.7 2.2 %collective-permute-start.16 = (bf16[128,128]{1,0:T(8,128)(2,1)S(1)}, bf16[128,128]{1,0:T(8,128)(2,1)S(1)}, u32[]{:S(2)}, u32[]{:S(2)}) collective-permute-start(bf16[128,128]{1,0:T(8,128)(2,1)S(1)} %pair_sum.2.mine_ref), channel_id=1, source_target_pairs={{0,8},{4,12},{8,0},{12,4},{1,9},{5,13},{9,1},{13,5},{2,10},{6,14},... | collective-permute-start | bytes 98312 | tf_op jit(solution)/shard_map/ppermute | solution.py:634
  47.3 8.2 %collective-permute-done.16.came_ref = bf16[128,128]{1,0:T(8,128)(2,1)S(1)} collective-permute-done((bf16[128,128]{1,0:T(8,128)(2,1)S(1)}, bf16[128,128]{1,0:T(8,128)(2,1)S(1)}, u32[]{:S(2)}, u32[]{:S(2)}) %collective-permute-start.16) | collective-permute-done | bytes 32800 | tf_op jit(solution)/shard_map/ppermute | solution.py:634
  55.6 0.7 %late_rows.3.mine_ref = bf16[8,128,128]{2,1,0:T(8,128)(2,1)S(1)} custom-call(f32[8,128,128]{2,1,0:T(8,128)S(1)} %late_rows.2.refs_0_, s32[1,128]{1,0:T(1,128)S(1)} %get-tuple-element.97.refs_1_, s32[1,128]{1,0:T(1,128)S(1)} %get-tuple-element.98.refs_2_, s32[1,128]{1,0:T(1,128)S(1)} %get-tuple-element.96.refs_0_.refs_3_, ...), custom_call_target="tpu_custom_call" | custom-call | flops 134217728 | bytes 1048576 | tf_op jit(solution)/shard_map/late_rows/pallas_call | solution.py:442
  56.9 1.1 %collective-permute-done.18.other_share_ref = f32[128,128]{1,0:T(8,128)S(1)} collective-permute-done((f32[128,128]{1,0:T(8,128)S(1)}, f32[128,128]{1,0:T(8,128)S(1)}, u32[]{:S(2)}, u32[]{:S(2)}) %collective-permute-start.18) | collective-permute-done | bytes 65568 | tf_op jit(solution)/shard_map/ppermute | solution.py:630
  58.0 0.9 %finish.1 = (bf16[8,128,128]{2,1,0:T(8,128)(2,1)}, f32[256,128]{1,0:T(8,128)}) custom-call(bf16[8,128,128]{2,1,0:T(8,128)(2,1)S(1)} %late_rows.3.mine_ref, bf16[8,128,128]{2,1,0:T(8,128)(2,1)S(1)} %collective-permute-done.17.other_ref, f32[128,128]{1,0:T(8,128)S(1)} %pair_sum.3.share_ref, f32[128,128]{1,0:T(8,128)S(1)} %collective-permute-done.18.other_share_ref), custom_call_target="tpu_custom_call" | custom-call | bytes 262144 | tf_op jit(solution)/shard_map/finish/pallas_call | solution.py:621
  (40 shorter events, 5.3 us)
Async XLA Ops:
  3.1 12.8 %collective-permute-start.4 = (bf16[4,128,128]{2,1,0:T(8,128)(2,1)}, bf16[4,128,128]{2,1,0:T(8,128)(2,1)S(1)}, u32[]{:S(2)}, u32[]{:S(2)}) collective-permute-start(bf16[4,128,128]{2,1,0:T(8,128)(2,1)} %get-tuple-element.67), channel_id=1, source_target_pairs={{0,8},{4,12},{8,0},{12,4},{1,9},{5,13},{9,1},{13,5},{2,10},{6,14},... | collective-permute-start | bytes 393224 | tf_op jit(solution)/shard_map/ppermute | solution.py:634
  7.2 8.7 %collective-permute-start.3 = (bf16[4,128,128]{2,1,0:T(8,128)(2,1)}, bf16[4,128,128]{2,1,0:T(8,128)(2,1)S(1)}, u32[]{:S(2)}, u32[]{:S(2)}) collective-permute-start(bf16[4,128,128]{2,1,0:T(8,128)(2,1)} %get-tuple-element.67), channel_id=1, source_target_pairs={{0,4},{4,0},{8,12},{12,8},{1,5},{5,1},{9,13},{13,9},{2,6},{6,2},{1... | collective-permute-start | bytes 393224 | tf_op jit(solution)/shard_map/ppermute | solution.py:634
  8.8 3.1 %copy-start = (bf16[8,128,128]{2,1,0:T(8,128)(2,1)S(1)}, bf16[8,128,128]{2,1,0:T(8,128)(2,1)}, u32[]{:S(2)}) copy-start(bf16[8,128,128]{2,1,0:T(8,128)(2,1)} %refs_4_.3) | copy-start | bytes 786436
  8.8 3.1 %copy-start.1 = (bf16[8,128,128]{2,1,0:T(8,128)(2,1)S(1)}, bf16[8,128,128]{2,1,0:T(8,128)(2,1)}, u32[]{:S(2)}) copy-start(bf16[8,128,128]{2,1,0:T(8,128)(2,1)} %refs_4_.2) | copy-start | bytes 786436
  12.4 10.6 %collective-permute-start.1 = (bf16[144,256]{1,0:T(8,128)(2,1)S(1)}, bf16[144,256]{1,0:T(8,128)(2,1)S(1)}, u32[]{:S(2)}, u32[]{:S(2)}) collective-permute-start(bf16[144,256]{1,0:T(8,128)(2,1)S(1)} %get-tuple-element.65), channel_id=1, source_target_pairs={{0,8},{4,12},{8,0},{12,4},{1,9},{5,13},{9,1},{13,5},{2,10},{6,14},... | collective-permute-start | bytes 221192 | tf_op jit(solution)/shard_map/ppermute | solution.py:634
  12.8 10.2 %collective-permute-start.2 = (bf16[144,256]{1,0:T(8,128)(2,1)S(1)}, bf16[144,256]{1,0:T(8,128)(2,1)S(1)}, u32[]{:S(2)}, u32[]{:S(2)}) collective-permute-start(bf16[144,256]{1,0:T(8,128)(2,1)S(1)} %get-tuple-element.66), channel_id=1, source_target_pairs={{0,12},{4,8},{8,4},{12,0},{1,13},{5,9},{9,5},{13,1},{2,14},{6,10},... | collective-permute-start | bytes 221192 | tf_op jit(solution)/shard_map/ppermute | solution.py:634
  15.3 8.2 %collective-permute-start = (bf16[144,256]{1,0:T(8,128)(2,1)S(1)}, bf16[144,256]{1,0:T(8,128)(2,1)S(1)}, u32[]{:S(2)}, u32[]{:S(2)}) collective-permute-start(bf16[144,256]{1,0:T(8,128)(2,1)S(1)} %get-tuple-element.64), channel_id=1, source_target_pairs={{0,4},{4,0},{8,12},{12,8},{1,5},{5,1},{9,13},{13,9},{2,6},{6,2},{1... | collective-permute-start | bytes 221192 | tf_op jit(solution)/shard_map/ppermute | solution.py:634
  16.0 7.0 %collective-permute-start.5 = (bf16[2,128,128]{2,1,0:T(8,128)(2,1)S(1)}, bf16[2,128,128]{2,1,0:T(8,128)(2,1)S(1)}, u32[]{:S(2)}, u32[]{:S(2)}) collective-permute-start(bf16[2,128,128]{2,1,0:T(8,128)(2,1)S(1)} %get-tuple-element.71), channel_id=1, source_target_pairs={{0,4},{4,0},{8,12},{12,8},{1,5},{5,1},{9,13},{13,9},{2,6},{6,2},{1... | collective-permute-start | bytes 196616 | tf_op jit(solution)/shard_map/ppermute | solution.py:634
  17.4 6.1 %collective-permute-start.6 = (bf16[2,128,128]{2,1,0:T(8,128)(2,1)S(1)}, bf16[2,128,128]{2,1,0:T(8,128)(2,1)S(1)}, u32[]{:S(2)}, u32[]{:S(2)}) collective-permute-start(bf16[2,128,128]{2,1,0:T(8,128)(2,1)S(1)} %get-tuple-element.72), channel_id=1, source_target_pairs={{0,4},{4,0},{8,12},{12,8},{1,5},{5,1},{9,13},{13,9},{2,6},{6,2},{1... | collective-permute-start | bytes 196616 | tf_op jit(solution)/shard_map/ppermute | solution.py:634
  23.5 1.8 %collective-permute-start.7 = (bf16[12,128,128]{2,1,0:T(8,128)(2,1)S(1)}, bf16[12,128,128]{2,1,0:T(8,128)(2,1)S(1)}, u32[]{:S(2)}, u32[]{:S(2)}) collective-permute-start(bf16[12,128,128]{2,1,0:T(8,128)(2,1)S(1)} %stack.1.refs_4_), channel_id=1, source_target_pairs={{0,1},{1,0},{2,3},{3,2},{4,5},{5,4},{6,7},{7,6},{8,9},{9,8},{10,11... | collective-permute-start | bytes 1179656 | tf_op jit(solution)/shard_map/ppermute | solution.py:630
  24.0 12.5 %copy-start.2 = (bf16[256,256]{1,0:T(8,128)(2,1)S(1)}, bf16[256,256]{1,0:T(8,128)(2,1)}, u32[]{:S(2)}) copy-start(bf16[256,256]{1,0:T(8,128)(2,1)} %refs_0_.1) | copy-start | bytes 393220
  25.8 5.0 %collective-permute-start.8 = (bf16[4,128,128]{2,1,0:T(8,128)(2,1)S(1)}, bf16[4,128,128]{2,1,0:T(8,128)(2,1)S(1)}, u32[]{:S(2)}, u32[]{:S(2)}) collective-permute-start(bf16[4,128,128]{2,1,0:T(8,128)(2,1)S(1)} %get-tuple-element.88), channel_id=1, source_target_pairs={{0,1},{1,0},{2,3},{3,2},{4,5},{5,4},{6,7},{7,6},{8,9},{9,8},{10,11... | collective-permute-start | bytes 393224 | tf_op jit(solution)/shard_map/ppermute | solution.py:630
  26.0 4.4 %collective-permute-start.9 = (bf16[2,128,128]{2,1,0:T(8,128)(2,1)S(1)}, bf16[2,128,128]{2,1,0:T(8,128)(2,1)S(1)}, u32[]{:S(2)}, u32[]{:S(2)}) collective-permute-start(bf16[2,128,128]{2,1,0:T(8,128)(2,1)S(1)} %get-tuple-element.91.refs_0_), channel_id=1, source_target_pairs={{0,2},{2,0},{1,3},{3,1},{4,6},{6,4},{5,7},{7,5},{8,10},{10,8},{9,1... | collective-permute-start | bytes 196616 | tf_op jit(solution)/shard_map/ppermute | solution.py:630
  37.1 1.6 %collective-permute-start.11 = (bf16[128,1024]{1,0:T(8,128)(2,1)S(1)}, bf16[128,1024]{1,0:T(8,128)(2,1)S(1)}, u32[]{:S(2)}, u32[]{:S(2)}) collective-permute-start(bf16[128,1024]{1,0:T(8,128)(2,1)S(1)} %get-tuple-element.94), channel_id=1, source_target_pairs={{0,1},{1,0},{2,3},{3,2},{4,5},{5,4},{6,7},{7,6},{8,9},{9,8},{10,11... | collective-permute-start | bytes 786440 | tf_op jit(solution)/shard_map/ppermute | solution.py:630
  37.2 5.5 %collective-permute-start.10 = (bf16[128,256]{1,0:T(8,128)(2,1)S(1)}, bf16[128,256]{1,0:T(8,128)(2,1)S(1)}, u32[]{:S(2)}, u32[]{:S(2)}) collective-permute-start(bf16[128,256]{1,0:T(8,128)(2,1)S(1)} %get-tuple-element.92.mine_ref), channel_id=1, source_target_pairs={{0,4},{4,0},{8,12},{12,8},{1,5},{5,1},{9,13},{13,9},{2,6},{6,2},{1... | collective-permute-start | bytes 196616 | tf_op jit(solution)/shard_map/ppermute | solution.py:634
  39.2 16.4 %collective-permute-start.12 = (bf16[128,512]{1,0:T(8,128)(2,1)S(1)}, bf16[128,512]{1,0:T(8,128)(2,1)S(1)}, u32[]{:S(2)}, u32[]{:S(2)}) collective-permute-start(bf16[128,512]{1,0:T(8,128)(2,1)S(1)} %get-tuple-element.102), channel_id=1, source_target_pairs={{0,8},{4,12},{8,0},{12,4},{1,9},{5,13},{9,1},{13,5},{2,10},{6,14},... | collective-permute-start | bytes 393224 | tf_op jit(solution)/shard_map/ppermute | solution.py:634
  40.5 15.1 %collective-permute-start.13 = (bf16[128,512]{1,0:T(8,128)(2,1)S(1)}, bf16[128,512]{1,0:T(8,128)(2,1)S(1)}, u32[]{:S(2)}, u32[]{:S(2)}) collective-permute-start(bf16[128,512]{1,0:T(8,128)(2,1)S(1)} %get-tuple-element.103), channel_id=1, source_target_pairs={{0,12},{4,8},{8,4},{12,0},{1,13},{5,9},{9,5},{13,1},{2,14},{6,10},... | collective-permute-start | bytes 393224 | tf_op jit(solution)/shard_map/ppermute | solution.py:634
  42.5 13.1 %collective-permute-start.14 = (bf16[128,512]{1,0:T(8,128)(2,1)S(1)}, bf16[128,512]{1,0:T(8,128)(2,1)S(1)}, u32[]{:S(2)}, u32[]{:S(2)}) collective-permute-start(bf16[128,512]{1,0:T(8,128)(2,1)S(1)} %get-tuple-element.104), channel_id=1, source_target_pairs={{0,4},{4,0},{8,12},{12,8},{1,5},{5,1},{9,13},{13,9},{2,6},{6,2},{1... | collective-permute-start | bytes 393224 | tf_op jit(solution)/shard_map/ppermute | solution.py:634
  43.5 1.2 %collective-permute-start.15 = (bf16[128,128]{1,0:T(8,128)(2,1)S(1)}, bf16[128,128]{1,0:T(8,128)(2,1)S(1)}, u32[]{:S(2)}, u32[]{:S(2)}) collective-permute-start(bf16[128,128]{1,0:T(8,128)(2,1)S(1)} %get-tuple-element.106), channel_id=1, source_target_pairs={{0,1},{1,0},{2,3},{3,2},{4,5},{5,4},{6,7},{7,6},{8,9},{9,8},{10,11... | collective-permute-start | bytes 98312 | tf_op jit(solution)/shard_map/ppermute | solution.py:630
  44.7 10.9 %collective-permute-start.16 = (bf16[128,128]{1,0:T(8,128)(2,1)S(1)}, bf16[128,128]{1,0:T(8,128)(2,1)S(1)}, u32[]{:S(2)}, u32[]{:S(2)}) collective-permute-start(bf16[128,128]{1,0:T(8,128)(2,1)S(1)} %pair_sum.2.mine_ref), channel_id=1, source_target_pairs={{0,8},{4,12},{8,0},{12,4},{1,9},{5,13},{9,1},{13,5},{2,10},{6,14},... | collective-permute-start | bytes 98312 | tf_op jit(solution)/shard_map/ppermute | solution.py:634
  56.3 1.7 %collective-permute-start.17 = (bf16[8,128,128]{2,1,0:T(8,128)(2,1)S(1)}, bf16[8,128,128]{2,1,0:T(8,128)(2,1)S(1)}, u32[]{:S(2)}, u32[]{:S(2)}) collective-permute-start(bf16[8,128,128]{2,1,0:T(8,128)(2,1)S(1)} %late_rows.3.mine_ref), channel_id=1, source_target_pairs={{0,1},{1,0},{2,3},{3,2},{4,5},{5,4},{6,7},{7,6},{8,9},{9,8},{10,11... | collective-permute-start | bytes 786440 | tf_op jit(solution)/shard_map/ppermute | solution.py:630
  56.4 1.6 %collective-permute-start.18 = (f32[128,128]{1,0:T(8,128)S(1)}, f32[128,128]{1,0:T(8,128)S(1)}, u32[]{:S(2)}, u32[]{:S(2)}) collective-permute-start(f32[128,128]{1,0:T(8,128)S(1)} %pair_sum.3.share_ref), channel_id=1, source_target_pairs={{0,1},{1,0},{2,3},{3,2},{4,5},{5,4},{6,7},{7,6},{8,9},{9,8},{10,11... | collective-permute-start | bytes 196616 | tf_op jit(solution)/shard_map/ppermute | solution.py:630

commit v14 on v12

--- a/solution.py
+++ b/solution.py
@@ -10,7 +10,7 @@
 CAP = 2
 GROUP = 8
 CHUNK = 16
-SIDES = 2
+SIDES = 1
 PLACE_ROWS = 8
 PLACE_BUFFER = 2 ** 22
 TAIL = 16
@@ -63,14 +63,13 @@
     return jnp.concatenate([x3[b] for b in range(x3.shape[0])], axis=1)
 
 
-def places(peers, blocks_dev, count, row, col, table):
+def places(peers, blocks_dev, row, col, table):
     me = lax.axis_index("graph")
     lane = lax.broadcasted_iota(jnp.int32, col.shape, 1)
-    live = lane < count
-    place = jnp.full(col.shape, peers * CAP * blocks_dev, jnp.int32)
+    place = jnp.zeros(col.shape, jnp.int32)
     for k in range(peers):
         local = col - jnp.bitwise_xor(me, k) * blocks_dev
-        inside = live & (local >= 0) & (local < blocks_dev)
+        inside = (local >= 0) & (local < blocks_dev)
         low = jnp.min(jnp.where(inside, local, blocks_dev - 1), axis=1, keepdims=True)
         high = jnp.max(jnp.where(inside, local, 0), axis=1, keepdims=True)
         table[PLACE_ROWS + k : PLACE_ROWS + k + 1, :] = jnp.where(lane == 0, low, high)
@@ -83,29 +82,28 @@
     return PLACE_ROWS + -(-peers // 8) * 8
 
 
-def prepare_kernel(peers, count_ref, row_ref, col_ref, x3, half_out, table_out, table, half_sem, sem):
+def prepare_kernel(peers, row_ref, col_ref, x3, half_out, table_out, table, half_sem, sem):
     share = half_out.shape[0]
     mine = pl.ds(lax.axis_index("rep") * share, share)
     half_copy = pltpu.make_async_copy(x3.at[mine], half_out, half_sem)
     half_copy.start()
-    count = jnp.broadcast_to(count_ref[...], (1, 1))
     if table.shape[0] > PLACE_ROWS + peers:
         table[...] = jnp.zeros(table.shape, jnp.int32)
-    places(peers, x3.shape[0], count, row_ref[...], col_ref[...], table)
+    places(peers, x3.shape[0], row_ref[...], col_ref[...], table)
     copy = pltpu.make_async_copy(table, table_out.at[pl.ds(0, table.shape[0])], sem)
     copy.start()
     half_copy.wait()
     copy.wait()
 
 
-def prepare(features, tile_row, tile_col, tile_count, peers, reps):
+def prepare(features, tile_row, tile_col, peers, reps):
     per = tile_col.shape[0]
     blocks_dev, columns, width = features.shape
     return call(
         functools.partial(prepare_kernel, peers),
         "prepare",
         [shape((blocks_dev // reps, columns, width), BF16), shape((PLACE_BUFFER // (4 * per), per), jnp.int32)],
-        [vmem()] * 4,
+        [vmem()] * 3,
         [
             pltpu.VMEM((table_rows(peers), per), jnp.int32),
             pltpu.SemaphoreType.DMA,
@@ -113,7 +111,7 @@
         ],
         limit=VMEM_ALL,
         out_specs=[hbm(), hbm()],
-    )(tile_count, tile_row.reshape(1, per), tile_col.reshape(1, per), features)
+    )(tile_row.reshape(1, per), tile_col.reshape(1, per), features)
 
 
 def pick(ids_ref, lane):
@@ -122,7 +120,7 @@
     return jnp.max(jnp.where(at == lane, ids, 0.0)).astype(jnp.int32)
 
 
-def operator_kernel(blocks_dev, slots_here, groups, table_in, tiles_ref, m_ref, *refs):
+def operator_kernel(blocks_dev, slots_here, groups, count_ref, table_in, tiles_ref, m_ref, *refs):
     asks, (tiles, acc, place_ref, table, sems, sem, table_sem) = refs[:-7], refs[-7:]
     step = pl.program_id(0)
     per, width = tiles.shape[0], tiles.shape[1]
@@ -152,6 +150,8 @@
     def _():
         place_copy().wait()
 
+    count = count_ref[0]
+
     def add_chunk(c, carry):
         @pl.when(step == 0)
         def _():
@@ -160,9 +160,11 @@
         for u in range(CHUNK):
             t = c * CHUNK + u
             place = place_ref[0, t]
+            here = t < count
             if groups > 1:
                 place = place - step * spare
-                place = jnp.where((place >= 0) & (place < spare), place, spare)
+                here = here & (place >= 0) & (place < spare)
+            place = jnp.where(here, place, spare)
             side = u % SIDES
             acc[side, place] = acc[side, place] + tiles[t].astype(F32)
         return carry
@@ -182,7 +184,7 @@
             ask_ref[...] = table[PLACE_ROWS + k : PLACE_ROWS + k + 1, :]
 
 
-def list_operator(tiles, table, peers, blocks_dev):
+def list_operator(tiles, table, tile_count, peers, blocks_dev):
     per, width = tiles.shape[0], tiles.shape[1]
     slots = peers * CAP
     slots_here = min(slots, GROUP)
@@ -191,7 +193,7 @@
         functools.partial(operator_kernel, blocks_dev, slots_here, groups),
         "operator",
         [shape((blocks_dev * width, slots * width), BF16)] + [shape((1, per), jnp.int32)] * peers,
-        [hbm(), hbm()],
+        [smem(), hbm(), hbm()],
         [
             pltpu.VMEM((per, width, width), BF16),
             pltpu.VMEM((SIDES, slots_here * blocks_dev + 1, width, width), F32),
@@ -205,7 +207,7 @@
         limit=VMEM_MOST,
         grid=(groups,),
         out_specs=[pl.BlockSpec((blocks_dev * width, slots_here * width), lambda i: (0, i))] + [vmem()] * peers,
-    )(table, tiles)
+    )(tile_count, table, tiles)
     return outs[0], list(outs[1:])
 
 
@@ -275,12 +277,16 @@
     return own_rows(far, m_ref, 0)
 
 
-def far_of(block, mine_ref, other_ref, ask_ref, at=0):
-    half = lax.axis_index("rep")
-    share = block.shape[0] // 2
-    block[pl.ds(half * share, share)] = mine_ref[at * share : (at + 1) * share]
-    block[pl.ds((1 - half) * share, share)] = other_ref[at * share : (at + 1) * share]
-    return jnp.concatenate([block[pick(ask_ref, s)] for s in range(CAP)], axis=1)
+def far_of(share, mine_ref, other_ref, ask_ref, at):
+    first = lax.axis_index("rep") * share
+    blocks = []
+    for s in range(CAP):
+        local = pick(ask_ref, s) - first
+        own = (local >= 0) & (local < share)
+        here = at * share + jnp.where(own, local, 0)
+        there = at * share + jnp.where(own, 0, jnp.where(local < 0, local + share, local - share))
+        blocks.append(jnp.where(own, mine_ref[here], other_ref[there]))
+    return jnp.concatenate(blocks, axis=1)
 
 
 def first_rows_kernel(peers, *refs):
@@ -363,12 +369,12 @@
 
 def give_rows_kernel(peers, *refs):
     ask_refs, refs = refs[: peers - 1], refs[peers - 1 :]
-    before, mine_ref, other_ref, m_ref, give_ref, far_ref, block = refs
+    before, mine_ref, other_ref, m_ref, give_ref, far_ref = refs
+    share = give_ref.shape[0]
     both = CAP * before.shape[2]
     for k in range(1, peers):
-        far_ref[:, k * both : (k + 1) * both] = far_of(block, mine_ref, other_ref, ask_refs[k - 1], k - 1)
+        far_ref[:, k * both : (k + 1) * both] = far_of(share, mine_ref, other_ref, ask_refs[k - 1], k - 1)
     far_ref[:, :both] = jnp.zeros((far_ref.shape[0], both), BF16)
-    share = give_ref.shape[0]
     rows = half_rows(before, far_ref, m_ref, (1 - lax.axis_index("rep")) * share, share)
     for b in range(share):
         give_ref[b] = rows[b].astype(BF16)
@@ -381,7 +387,6 @@
         "give_rows",
         [shape((blocks_dev // reps, columns, width), BF16), shape((columns, peers * CAP * width), BF16)],
         [vmem()] * (peers + 3),
-        [pltpu.VMEM(before.shape, BF16)],
         flops=2 ** 27,
         moved=2 ** 20,
     )(*asks[1:], before, mine, other, operator)
@@ -637,8 +642,8 @@
     reps = lax.axis_size("rep")
     far_first = sorted(range(1, peers), key=lambda k: (-(k & (peers // 2)), k))
 
-    half, table = prepare(features, tile_row, tile_col, tile_count, peers, reps)
-    operator, asks = list_operator(tiles, table, peers, blocks_dev)
+    half, table = prepare(features, tile_row, tile_col, peers, reps)
+    operator, asks = list_operator(tiles, table, tile_count, peers, blocks_dev)
     sends, own_mirror, own_cot = first_sends(features, cotangent, operator, asks[1:], peers, reps)
     cots = lax.all_gather(own_cot, "feat", axis=0, tiled=True)
     pieces, held = {0: [half]}, [0]

time: 55.7 us -> 55.6 us (level)
  no operation moved by 1% of the time
where the time goes in v14:
time: 55.6 us; the launch traced here: 55.4 us
  starting transfers between devices  21 us (38%)
  waiting for transfers between devices  16.8 us (30%)
  Pallas kernels  10.5 us (19%)
  blocking collectives  5.63 us (10%)
  between operations  1.5 us (3%)
    ppermute x12, starting transfers between devices, across(): return lax.ppermute(value, 'graph', [(i, i ^ k) for i in range(peers)])  18.5 us
    ppermute x7, waiting for transfers between devices, ahead(): return lax.ppermute(value, axis, [(i, (i + k) % size) for i in range(size)])  8.49 us
    ppermute x12, waiting for transfers between devices, across(): return lax.ppermute(value, 'graph', [(i, i ^ k) for i in range(peers)])  8.31 us
    all_gather x1, blocking collectives, local(): cots = lax.all_gather(own_cot, 'feat', axis=0, tiled=True)  5.63 us
    pallas_call x1, Pallas kernels, list_operator(): call(functools.partial(operator_kernel, blocks_dev, slots_here, groups),...  2.99 us
    ppermute x7, starting transfers between devices, ahead(): return lax.ppermute(value, axis, [(i, (i + k) % size) for i in range(size)])  2.46 us
    pallas_call x1, Pallas kernels, prepare(): call(functools.partial(prepare_kernel, peers), 'prepare', [shape((blocks_...  1.76 us
  transfers between devices with their start and end apart: 19, of which 7 were waited for; matrix products, arithmetic and copies ran while one was open for 0% of the time, Pallas kernels for 11%

profile of v14, /device:TPU:0, one launch (start us, length us, event | category | flops | bytes accessed | tf_op | source)
XLA Modules:
  0.0 55.4 jit_solution(14729234585106493644)
XLA Ops:
  0.6 1.8 %prepare.1 = (bf16[4,128,128]{2,1,0:T(8,128)(2,1)}, s32[8192,128]{1,0:T(8,128)}) custom-call(s32[1,128]{1,0:T(1,128)} %bitcast.2, s32[1,128]{1,0:T(1,128)} %bitcast.3, bf16[8,128,128]{2,1,0:T(8,128)(2,1)} %refs_4_.3), custom_call_target="tpu_custom_call" | custom-call | bytes 262144 | tf_op jit(solution)/shard_map/prepare/pallas_call | solution.py:102
  2.4 4.1 %collective-permute-start.4 = (bf16[4,128,128]{2,1,0:T(8,128)(2,1)}, bf16[4,128,128]{2,1,0:T(8,128)(2,1)S(1)}, u32[]{:S(2)}, u32[]{:S(2)}) collective-permute-start(bf16[4,128,128]{2,1,0:T(8,128)(2,1)} %get-tuple-element.65), channel_id=1, source_target_pairs={{0,8},{4,12},{8,0},{12,4},{1,9},{5,13},{9,1},{13,5},{2,10},{6,14},... | collective-permute-start | bytes 393224 | tf_op jit(solution)/shard_map/ppermute | solution.py:631
  6.5 1.6 %collective-permute-start.3 = (bf16[4,128,128]{2,1,0:T(8,128)(2,1)}, bf16[4,128,128]{2,1,0:T(8,128)(2,1)S(1)}, u32[]{:S(2)}, u32[]{:S(2)}) collective-permute-start(bf16[4,128,128]{2,1,0:T(8,128)(2,1)} %get-tuple-element.65), channel_id=1, source_target_pairs={{0,4},{4,0},{8,12},{12,8},{1,5},{5,1},{9,13},{13,9},{2,6},{6,2},{1... | collective-permute-start | bytes 393224 | tf_op jit(solution)/shard_map/ppermute | solution.py:631
  8.8 3.0 %operator.1 = (bf16[1024,1024]{1,0:T(8,128)(2,1)S(1)}, s32[1,128]{1,0:T(1,128)S(1)}, s32[1,128]{1,0:T(1,128)S(1)}, s32[1,128]{1,0:T(1,128)S(1)}, s32[1,128]{1,0:T(1,128)S(1)}) custom-call(s32[1]{0:T(128)S(6)} %copy.10.count_ref, s32[8192,128]{1,0:T(8,128)} %get-tuple-element.56.table_in, bf16[128,128,128]{2,1,0:T(8,128)(2,1)} %tiles_ref.1), custom_call_target="tpu_custom_call" | custom-call | bytes 16777216 | tf_op jit(solution)/shard_map/operator/pallas_call | solution.py:192
  12.6 2.5 %collective-permute-start.2 = (bf16[144,256]{1,0:T(8,128)(2,1)S(1)}, bf16[144,256]{1,0:T(8,128)(2,1)S(1)}, u32[]{:S(2)}, u32[]{:S(2)}) collective-permute-start(bf16[144,256]{1,0:T(8,128)(2,1)S(1)} %get-tuple-element.64), channel_id=1, source_target_pairs={{0,12},{4,8},{8,4},{12,0},{1,13},{5,9},{9,5},{13,1},{2,14},{6,10},... | collective-permute-start | bytes 221192 | tf_op jit(solution)/shard_map/ppermute | solution.py:631
  15.1 0.6 %collective-permute-start = (bf16[144,256]{1,0:T(8,128)(2,1)S(1)}, bf16[144,256]{1,0:T(8,128)(2,1)S(1)}, u32[]{:S(2)}, u32[]{:S(2)}) collective-permute-start(bf16[144,256]{1,0:T(8,128)(2,1)S(1)} %get-tuple-element.62), channel_id=1, source_target_pairs={{0,4},{4,0},{8,12},{12,8},{1,5},{5,1},{9,13},{13,9},{2,6},{6,2},{1... | collective-permute-start | bytes 221192 | tf_op jit(solution)/shard_map/ppermute | solution.py:631
  15.8 1.4 %collective-permute-start.5 = (bf16[2,128,128]{2,1,0:T(8,128)(2,1)S(1)}, bf16[2,128,128]{2,1,0:T(8,128)(2,1)S(1)}, u32[]{:S(2)}, u32[]{:S(2)}) collective-permute-start(bf16[2,128,128]{2,1,0:T(8,128)(2,1)S(1)} %get-tuple-element.69), channel_id=1, source_target_pairs={{0,4},{4,0},{8,12},{12,8},{1,5},{5,1},{9,13},{13,9},{2,6},{6,2},{1... | collective-permute-start | bytes 196616 | tf_op jit(solution)/shard_map/ppermute | solution.py:631
  17.3 0.6 %collective-permute-start.6 = (bf16[2,128,128]{2,1,0:T(8,128)(2,1)S(1)}, bf16[2,128,128]{2,1,0:T(8,128)(2,1)S(1)}, u32[]{:S(2)}, u32[]{:S(2)}) collective-permute-start(bf16[2,128,128]{2,1,0:T(8,128)(2,1)S(1)} %get-tuple-element.70), channel_id=1, source_target_pairs={{0,4},{4,0},{8,12},{12,8},{1,5},{5,1},{9,13},{13,9},{2,6},{6,2},{1... | collective-permute-start | bytes 196616 | tf_op jit(solution)/shard_map/ppermute | solution.py:631
  17.9 5.6 %all_gather.3.in_ref = bf16[8,128,128]{2,1,0:T(8,128)(2,1)S(1)} all-gather(bf16[4,128,128]{2,1,0:T(8,128)(2,1)S(1)} %get-tuple-element.71), channel_id=1, replica_groups=mesh['parts'=2,'graph'=4,'feat'=2,'rep'=2] {'feat'}, dimensions={0}, use_global_device_ids=true | all-gather | bytes 393216 | tf_op jit(solution)/shard_map/all_gather | solution.py:648
  24.1 1.3 %collective-permute-done.7.refs_5_ = bf16[12,128,128]{2,1,0:T(8,128)(2,1)S(1)} collective-permute-done((bf16[12,128,128]{2,1,0:T(8,128)(2,1)S(1)}, bf16[12,128,128]{2,1,0:T(8,128)(2,1)S(1)}, u32[]{:S(2)}, u32[]{:S(2)}) %collective-permute-start.7) | collective-permute-done | bytes 393248 | tf_op jit(solution)/shard_map/ppermute | solution.py:627
  26.5 0.8 %collective-permute-done.8.came_ref = bf16[4,128,128]{2,1,0:T(8,128)(2,1)S(1)} collective-permute-done((bf16[4,128,128]{2,1,0:T(8,128)(2,1)S(1)}, bf16[4,128,128]{2,1,0:T(8,128)(2,1)S(1)}, u32[]{:S(2)}, u32[]{:S(2)}) %collective-permute-start.8) | collective-permute-done | bytes 131104 | tf_op jit(solution)/shard_map/ppermute | solution.py:627
  27.3 1.6 %collective-permute-start.9 = (bf16[4,128,128]{2,1,0:T(8,128)(2,1)S(1)}, bf16[4,128,128]{2,1,0:T(8,128)(2,1)S(1)}, u32[]{:S(2)}, u32[]{:S(2)}) collective-permute-start(bf16[4,128,128]{2,1,0:T(8,128)(2,1)S(1)} %add_up.1.refs_0_), channel_id=1, source_target_pairs={{0,2},{2,0},{1,3},{3,1},{4,6},{6,4},{5,7},{7,5},{8,10},{10,8},{9,1... | collective-permute-start | bytes 393224 | tf_op jit(solution)/shard_map/ppermute | solution.py:627
  28.9 4.0 %collective-permute-done.9.refs_1_ = bf16[4,128,128]{2,1,0:T(8,128)(2,1)S(1)} collective-permute-done((bf16[4,128,128]{2,1,0:T(8,128)(2,1)S(1)}, bf16[4,128,128]{2,1,0:T(8,128)(2,1)S(1)}, u32[]{:S(2)}, u32[]{:S(2)}) %collective-permute-start.9) | collective-permute-done | bytes 131104 | tf_op jit(solution)/shard_map/ppermute | solution.py:627
  32.9 0.7 %dense.1 = (bf16[4,128,128]{2,1,0:T(8,128)(2,1)S(1)}, bf16[128,1024]{1,0:T(8,128)(2,1)S(1)}, bf16[4,128,128]{2,1,0:T(8,128)(2,1)S(1)}, bf16[128,256]{1,0:T(8,128)(2,1)S(1)}) custom-call(bf16[4,128,128]{2,1,0:T(8,128)(2,1)S(1)} %add_up.1.refs_0_, bf16[4,128,128]{2,1,0:T(8,128)(2,1)S(1)} %collective-permute-done.9.refs_1_, bf16[256,512]{1,0:T(8,128)(2,1)S(1)} %widen.1.refs_2_, ...), custom_call_target="tpu_custom_call" | custom-call | flops 268435456 | bytes 1048576 | tf_op jit(solution)/shard_map/dense/pallas_call | solution.py:506
  33.7 1.4 %collective-permute-start.10 = (bf16[128,256]{1,0:T(8,128)(2,1)S(1)}, bf16[128,256]{1,0:T(8,128)(2,1)S(1)}, u32[]{:S(2)}, u32[]{:S(2)}) collective-permute-start(bf16[128,256]{1,0:T(8,128)(2,1)S(1)} %get-tuple-element.88.mine_ref), channel_id=1, source_target_pairs={{0,4},{4,0},{8,12},{12,8},{1,5},{5,1},{9,13},{13,9},{2,6},{6,2},{1... | collective-permute-start | bytes 196616 | tf_op jit(solution)/shard_map/ppermute | solution.py:631
  35.7 1.3 %collective-permute-start.12 = (bf16[128,512]{1,0:T(8,128)(2,1)S(1)}, bf16[128,512]{1,0:T(8,128)(2,1)S(1)}, u32[]{:S(2)}, u32[]{:S(2)}) collective-permute-start(bf16[128,512]{1,0:T(8,128)(2,1)S(1)} %get-tuple-element.98), channel_id=1, source_target_pairs={{0,8},{4,12},{8,0},{12,4},{1,9},{5,13},{9,1},{13,5},{2,10},{6,14},... | collective-permute-start | bytes 393224 | tf_op jit(solution)/shard_map/ppermute | solution.py:631
  37.0 2.5 %collective-permute-start.13 = (bf16[128,512]{1,0:T(8,128)(2,1)S(1)}, bf16[128,512]{1,0:T(8,128)(2,1)S(1)}, u32[]{:S(2)}, u32[]{:S(2)}) collective-permute-start(bf16[128,512]{1,0:T(8,128)(2,1)S(1)} %get-tuple-element.99), channel_id=1, source_target_pairs={{0,12},{4,8},{8,4},{12,0},{1,13},{5,9},{9,5},{13,1},{2,14},{6,10},... | collective-permute-start | bytes 393224 | tf_op jit(solution)/shard_map/ppermute | solution.py:631
  39.5 0.7 %split_sum.1 = (bf16[128,128]{1,0:T(8,128)(2,1)S(1)}, f32[128,128]{1,0:T(8,128)S(1)}, bf16[8,128,128]{2,1,0:T(8,128)(2,1)}) custom-call(bf16[128,256]{1,0:T(8,128)(2,1)S(1)} %get-tuple-element.88.mine_ref, bf16[128,256]{1,0:T(8,128)(2,1)S(1)} %collective-permute-done.10.came_ref, bf16[4,128,128]{2,1,0:T(8,128)(2,1)S(1)} %get-tuple-element.89.act_ref, ...), custom_call_target="tpu_custom_call" | custom-call | bytes 262144 | tf_op jit(solution)/shard_map/split_sum/pallas_call | solution.py:589
  40.2 1.2 %collective-permute-done.15.came_ref = bf16[128,128]{1,0:T(8,128)(2,1)S(1)} collective-permute-done((bf16[128,128]{1,0:T(8,128)(2,1)S(1)}, bf16[128,128]{1,0:T(8,128)(2,1)S(1)}, u32[]{:S(2)}, u32[]{:S(2)}) %collective-permute-start.15) | collective-permute-done | bytes 32800 | tf_op jit(solution)/shard_map/ppermute | solution.py:627
  41.4 1.9 %collective-permute-start.16 = (bf16[128,128]{1,0:T(8,128)(2,1)S(1)}, bf16[128,128]{1,0:T(8,128)(2,1)S(1)}, u32[]{:S(2)}, u32[]{:S(2)}) collective-permute-start(bf16[128,128]{1,0:T(8,128)(2,1)S(1)} %pair_sum.2.mine_ref), channel_id=1, source_target_pairs={{0,8},{4,12},{8,0},{12,4},{1,9},{5,13},{9,1},{13,5},{2,10},{6,14},... | collective-permute-start | bytes 98312 | tf_op jit(solution)/shard_map/ppermute | solution.py:631
  43.8 8.3 %collective-permute-done.16.came_ref = bf16[128,128]{1,0:T(8,128)(2,1)S(1)} collective-permute-done((bf16[128,128]{1,0:T(8,128)(2,1)S(1)}, bf16[128,128]{1,0:T(8,128)(2,1)S(1)}, u32[]{:S(2)}, u32[]{:S(2)}) %collective-permute-start.16) | collective-permute-done | bytes 32800 | tf_op jit(solution)/shard_map/ppermute | solution.py:631
  52.1 0.7 %late_rows.3.mine_ref = bf16[8,128,128]{2,1,0:T(8,128)(2,1)S(1)} custom-call(f32[8,128,128]{2,1,0:T(8,128)S(1)} %late_rows.2.refs_0_, s32[1,128]{1,0:T(1,128)S(1)} %get-tuple-element.93.refs_1_, s32[1,128]{1,0:T(1,128)S(1)} %get-tuple-element.94.refs_2_, s32[1,128]{1,0:T(1,128)S(1)} %get-tuple-element.92.refs_0_.refs_3_, ...), custom_call_target="tpu_custom_call" | custom-call | flops 134217728 | bytes 1048576 | tf_op jit(solution)/shard_map/late_rows/pallas_call | solution.py:443
  53.4 1.1 %collective-permute-done.18.other_share_ref = f32[128,128]{1,0:T(8,128)S(1)} collective-permute-done((f32[128,128]{1,0:T(8,128)S(1)}, f32[128,128]{1,0:T(8,128)S(1)}, u32[]{:S(2)}, u32[]{:S(2)}) %collective-permute-start.18) | collective-permute-done | bytes 65568 | tf_op jit(solution)/shard_map/ppermute | solution.py:627
  54.5 0.9 %finish.1 = (bf16[8,128,128]{2,1,0:T(8,128)(2,1)}, f32[256,128]{1,0:T(8,128)}) custom-call(bf16[8,128,128]{2,1,0:T(8,128)(2,1)S(1)} %late_rows.3.mine_ref, bf16[8,128,128]{2,1,0:T(8,128)(2,1)S(1)} %collective-permute-done.17.other_ref, f32[128,128]{1,0:T(8,128)S(1)} %pair_sum.3.share_ref, f32[128,128]{1,0:T(8,128)S(1)} %collective-permute-done.18.other_share_ref), custom_call_target="tpu_custom_call" | custom-call | bytes 262144 | tf_op jit(solution)/shard_map/finish/pallas_call | solution.py:618
  (39 shorter events, 4.1 us)
Async XLA Ops:
  2.4 13.4 %collective-permute-start.4 = (bf16[4,128,128]{2,1,0:T(8,128)(2,1)}, bf16[4,128,128]{2,1,0:T(8,128)(2,1)S(1)}, u32[]{:S(2)}, u32[]{:S(2)}) collective-permute-start(bf16[4,128,128]{2,1,0:T(8,128)(2,1)} %get-tuple-element.65), channel_id=1, source_target_pairs={{0,8},{4,12},{8,0},{12,4},{1,9},{5,13},{9,1},{13,5},{2,10},{6,14},... | collective-permute-start | bytes 393224 | tf_op jit(solution)/shard_map/ppermute | solution.py:631
  6.5 9.3 %collective-permute-start.3 = (bf16[4,128,128]{2,1,0:T(8,128)(2,1)}, bf16[4,128,128]{2,1,0:T(8,128)(2,1)S(1)}, u32[]{:S(2)}, u32[]{:S(2)}) collective-permute-start(bf16[4,128,128]{2,1,0:T(8,128)(2,1)} %get-tuple-element.65), channel_id=1, source_target_pairs={{0,4},{4,0},{8,12},{12,8},{1,5},{5,1},{9,13},{13,9},{2,6},{6,2},{1... | collective-permute-start | bytes 393224 | tf_op jit(solution)/shard_map/ppermute | solution.py:631
  8.7 3.0 %copy-start = (bf16[8,128,128]{2,1,0:T(8,128)(2,1)S(1)}, bf16[8,128,128]{2,1,0:T(8,128)(2,1)}, u32[]{:S(2)}) copy-start(bf16[8,128,128]{2,1,0:T(8,128)(2,1)} %refs_4_.3) | copy-start | bytes 786436
  8.7 3.0 %copy-start.1 = (bf16[8,128,128]{2,1,0:T(8,128)(2,1)S(1)}, bf16[8,128,128]{2,1,0:T(8,128)(2,1)}, u32[]{:S(2)}) copy-start(bf16[8,128,128]{2,1,0:T(8,128)(2,1)} %refs_4_.2) | copy-start | bytes 786436
  12.2 11.3 %collective-permute-start.1 = (bf16[144,256]{1,0:T(8,128)(2,1)S(1)}, bf16[144,256]{1,0:T(8,128)(2,1)S(1)}, u32[]{:S(2)}, u32[]{:S(2)}) collective-permute-start(bf16[144,256]{1,0:T(8,128)(2,1)S(1)} %get-tuple-element.63), channel_id=1, source_target_pairs={{0,8},{4,12},{8,0},{12,4},{1,9},{5,13},{9,1},{13,5},{2,10},{6,14},... | collective-permute-start | bytes 221192 | tf_op jit(solution)/shard_map/ppermute | solution.py:631
  12.6 10.9 %collective-permute-start.2 = (bf16[144,256]{1,0:T(8,128)(2,1)S(1)}, bf16[144,256]{1,0:T(8,128)(2,1)S(1)}, u32[]{:S(2)}, u32[]{:S(2)}) collective-permute-start(bf16[144,256]{1,0:T(8,128)(2,1)S(1)} %get-tuple-element.64), channel_id=1, source_target_pairs={{0,12},{4,8},{8,4},{12,0},{1,13},{5,9},{9,5},{13,1},{2,14},{6,10},... | collective-permute-start | bytes 221192 | tf_op jit(solution)/shard_map/ppermute | solution.py:631
  15.1 8.4 %collective-permute-start = (bf16[144,256]{1,0:T(8,128)(2,1)S(1)}, bf16[144,256]{1,0:T(8,128)(2,1)S(1)}, u32[]{:S(2)}, u32[]{:S(2)}) collective-permute-start(bf16[144,256]{1,0:T(8,128)(2,1)S(1)} %get-tuple-element.62), channel_id=1, source_target_pairs={{0,4},{4,0},{8,12},{12,8},{1,5},{5,1},{9,13},{13,9},{2,6},{6,2},{1... | collective-permute-start | bytes 221192 | tf_op jit(solution)/shard_map/ppermute | solution.py:631
  15.8 7.7 %collective-permute-start.5 = (bf16[2,128,128]{2,1,0:T(8,128)(2,1)S(1)}, bf16[2,128,128]{2,1,0:T(8,128)(2,1)S(1)}, u32[]{:S(2)}, u32[]{:S(2)}) collective-permute-start(bf16[2,128,128]{2,1,0:T(8,128)(2,1)S(1)} %get-tuple-element.69), channel_id=1, source_target_pairs={{0,4},{4,0},{8,12},{12,8},{1,5},{5,1},{9,13},{13,9},{2,6},{6,2},{1... | collective-permute-start | bytes 196616 | tf_op jit(solution)/shard_map/ppermute | solution.py:631
  17.3 6.3 %collective-permute-start.6 = (bf16[2,128,128]{2,1,0:T(8,128)(2,1)S(1)}, bf16[2,128,128]{2,1,0:T(8,128)(2,1)S(1)}, u32[]{:S(2)}, u32[]{:S(2)}) collective-permute-start(bf16[2,128,128]{2,1,0:T(8,128)(2,1)S(1)} %get-tuple-element.70), channel_id=1, source_target_pairs={{0,4},{4,0},{8,12},{12,8},{1,5},{5,1},{9,13},{13,9},{2,6},{6,2},{1... | collective-permute-start | bytes 196616 | tf_op jit(solution)/shard_map/ppermute | solution.py:631
  23.6 1.8 %collective-permute-start.7 = (bf16[12,128,128]{2,1,0:T(8,128)(2,1)S(1)}, bf16[12,128,128]{2,1,0:T(8,128)(2,1)S(1)}, u32[]{:S(2)}, u32[]{:S(2)}) collective-permute-start(bf16[12,128,128]{2,1,0:T(8,128)(2,1)S(1)} %stack.1.refs_4_), channel_id=1, source_target_pairs={{0,1},{1,0},{2,3},{3,2},{4,5},{5,4},{6,7},{7,6},{8,9},{9,8},{10,11... | collective-permute-start | bytes 1179656 | tf_op jit(solution)/shard_map/ppermute | solution.py:627
  24.1 8.8 %copy-start.2 = (bf16[256,256]{1,0:T(8,128)(2,1)S(1)}, bf16[256,256]{1,0:T(8,128)(2,1)}, u32[]{:S(2)}) copy-start(bf16[256,256]{1,0:T(8,128)(2,1)} %refs_3_.3) | copy-start | bytes 393220
  25.9 1.4 %collective-permute-start.8 = (bf16[4,128,128]{2,1,0:T(8,128)(2,1)S(1)}, bf16[4,128,128]{2,1,0:T(8,128)(2,1)S(1)}, u32[]{:S(2)}, u32[]{:S(2)}) collective-permute-start(bf16[4,128,128]{2,1,0:T(8,128)(2,1)S(1)} %get-tuple-element.86), channel_id=1, source_target_pairs={{0,1},{1,0},{2,3},{3,2},{4,5},{5,4},{6,7},{7,6},{8,9},{9,8},{10,11... | collective-permute-start | bytes 393224 | tf_op jit(solution)/shard_map/ppermute | solution.py:627
  27.3 5.6 %collective-permute-start.9 = (bf16[4,128,128]{2,1,0:T(8,128)(2,1)S(1)}, bf16[4,128,128]{2,1,0:T(8,128)(2,1)S(1)}, u32[]{:S(2)}, u32[]{:S(2)}) collective-permute-start(bf16[4,128,128]{2,1,0:T(8,128)(2,1)S(1)} %add_up.1.refs_0_), channel_id=1, source_target_pairs={{0,2},{2,0},{1,3},{3,1},{4,6},{6,4},{5,7},{7,5},{8,10},{10,8},{9,1... | collective-permute-start | bytes 393224 | tf_op jit(solution)/shard_map/ppermute | solution.py:627
  33.6 1.6 %collective-permute-start.11 = (bf16[128,1024]{1,0:T(8,128)(2,1)S(1)}, bf16[128,1024]{1,0:T(8,128)(2,1)S(1)}, u32[]{:S(2)}, u32[]{:S(2)}) collective-permute-start(bf16[128,1024]{1,0:T(8,128)(2,1)S(1)} %get-tuple-element.90), channel_id=1, source_target_pairs={{0,1},{1,0},{2,3},{3,2},{4,5},{5,4},{6,7},{7,6},{8,9},{9,8},{10,11... | collective-permute-start | bytes 786440 | tf_op jit(solution)/shard_map/ppermute | solution.py:627
  33.7 5.8 %collective-permute-start.10 = (bf16[128,256]{1,0:T(8,128)(2,1)S(1)}, bf16[128,256]{1,0:T(8,128)(2,1)S(1)}, u32[]{:S(2)}, u32[]{:S(2)}) collective-permute-start(bf16[128,256]{1,0:T(8,128)(2,1)S(1)} %get-tuple-element.88.mine_ref), channel_id=1, source_target_pairs={{0,4},{4,0},{8,12},{12,8},{1,5},{5,1},{9,13},{13,9},{2,6},{6,2},{1... | collective-permute-start | bytes 196616 | tf_op jit(solution)/shard_map/ppermute | solution.py:631
  35.7 16.4 %collective-permute-start.12 = (bf16[128,512]{1,0:T(8,128)(2,1)S(1)}, bf16[128,512]{1,0:T(8,128)(2,1)S(1)}, u32[]{:S(2)}, u32[]{:S(2)}) collective-permute-start(bf16[128,512]{1,0:T(8,128)(2,1)S(1)} %get-tuple-element.98), channel_id=1, source_target_pairs={{0,8},{4,12},{8,0},{12,4},{1,9},{5,13},{9,1},{13,5},{2,10},{6,14},... | collective-permute-start | bytes 393224 | tf_op jit(solution)/shard_map/ppermute | solution.py:631
  37.0 15.1 %collective-permute-start.13 = (bf16[128,512]{1,0:T(8,128)(2,1)S(1)}, bf16[128,512]{1,0:T(8,128)(2,1)S(1)}, u32[]{:S(2)}, u32[]{:S(2)}) collective-permute-start(bf16[128,512]{1,0:T(8,128)(2,1)S(1)} %get-tuple-element.99), channel_id=1, source_target_pairs={{0,12},{4,8},{8,4},{12,0},{1,13},{5,9},{9,5},{13,1},{2,14},{6,10},... | collective-permute-start | bytes 393224 | tf_op jit(solution)/shard_map/ppermute | solution.py:631
  39.5 12.6 %collective-permute-start.14 = (bf16[128,512]{1,0:T(8,128)(2,1)S(1)}, bf16[128,512]{1,0:T(8,128)(2,1)S(1)}, u32[]{:S(2)}, u32[]{:S(2)}) collective-permute-start(bf16[128,512]{1,0:T(8,128)(2,1)S(1)} %get-tuple-element.100), channel_id=1, source_target_pairs={{0,4},{4,0},{8,12},{12,8},{1,5},{5,1},{9,13},{13,9},{2,6},{6,2},{1... | collective-permute-start | bytes 393224 | tf_op jit(solution)/shard_map/ppermute | solution.py:631
  40.2 1.2 %collective-permute-start.15 = (bf16[128,128]{1,0:T(8,128)(2,1)S(1)}, bf16[128,128]{1,0:T(8,128)(2,1)S(1)}, u32[]{:S(2)}, u32[]{:S(2)}) collective-permute-start(bf16[128,128]{1,0:T(8,128)(2,1)S(1)} %get-tuple-element.102), channel_id=1, source_target_pairs={{0,1},{1,0},{2,3},{3,2},{4,5},{5,4},{6,7},{7,6},{8,9},{9,8},{10,11... | collective-permute-start | bytes 98312 | tf_op jit(solution)/shard_map/ppermute | solution.py:627
  41.4 10.6 %collective-permute-start.16 = (bf16[128,128]{1,0:T(8,128)(2,1)S(1)}, bf16[128,128]{1,0:T(8,128)(2,1)S(1)}, u32[]{:S(2)}, u32[]{:S(2)}) collective-permute-start(bf16[128,128]{1,0:T(8,128)(2,1)S(1)} %pair_sum.2.mine_ref), channel_id=1, source_target_pairs={{0,8},{4,12},{8,0},{12,4},{1,9},{5,13},{9,1},{13,5},{2,10},{6,14},... | collective-permute-start | bytes 98312 | tf_op jit(solution)/shard_map/ppermute | solution.py:631
  52.8 1.7 %collective-permute-start.17 = (bf16[8,128,128]{2,1,0:T(8,128)(2,1)S(1)}, bf16[8,128,128]{2,1,0:T(8,128)(2,1)S(1)}, u32[]{:S(2)}, u32[]{:S(2)}) collective-permute-start(bf16[8,128,128]{2,1,0:T(8,128)(2,1)S(1)} %late_rows.3.mine_ref), channel_id=1, source_target_pairs={{0,1},{1,0},{2,3},{3,2},{4,5},{5,4},{6,7},{7,6},{8,9},{9,8},{10,11... | collective-permute-start | bytes 786440 | tf_op jit(solution)/shard_map/ppermute | solution.py:627
  52.9 1.6 %collective-permute-start.18 = (f32[128,128]{1,0:T(8,128)S(1)}, f32[128,128]{1,0:T(8,128)S(1)}, u32[]{:S(2)}, u32[]{:S(2)}) collective-permute-start(f32[128,128]{1,0:T(8,128)S(1)} %pair_sum.3.share_ref), channel_id=1, source_target_pairs={{0,1},{1,0},{2,3},{3,2},{4,5},{5,4},{6,7},{7,6},{8,9},{9,8},{10,11... | collective-permute-start | bytes 196616 | tf_op jit(solution)/shard_map/ppermute | solution.py:627

commit v15 on v14

--- a/solution.py
+++ b/solution.py
@@ -411,44 +411,47 @@
     )(before, far, operator)
 
 
-def late_rows_kernel(ks, first, last, *refs):
-    if first:
-        ask_ref, x3, self_ref = refs[:3]
-    else:
-        before = refs[0]
-    refs = refs[3 if first else 1 :]
-    ids_refs, refs = refs[: len(ks)], refs[len(ks) :]
-    came_refs, refs = refs[: len(ks)], refs[len(ks) :]
-    m_ref, out_ref = refs[:2]
-    acc = refs[2] if last else out_ref
+def late_self_kernel(ask_ref, x3, self_ref, m_ref, act_ref, shared_ref, acc, out_ref):
+    width = x3.shape[2]
+    put_rows(acc, self_rows(x3, m_ref, ask_ref))
+    for s in range(CAP):
+        add_sums(acc, pick(ask_ref, s), self_ref[:, s * width : (s + 1) * width])
+    half = lax.axis_index("rep")
+    blocks = act_ref.shape[0]
+    out_ref[pl.ds(half * blocks, blocks)] = act_ref[...]
+    for b in range(blocks):
+        at = (blocks + b) * width
+        out_ref[(1 - half) * blocks + b] = shared_ref[:, at : at + width]
+
+
+def late_self(ask, values, own_mirror, operator, act, shared):
+    return call(
+        late_self_kernel,
+        "late_self",
+        [shape(values.shape, F32), shape(values.shape, BF16)],
+        [vmem()] * 6,
+        flops=2 ** 26,
+    )(ask, values, own_mirror, operator, act, shared)
+
+
+def late_rows_kernel(k, before, ids_ref, came_ref, m_ref, out_ref, acc):
     width = acc.shape[2]
     both = CAP * width
-    own = self_rows(x3, m_ref, ask_ref) if first else None
-    for i, k in enumerate(ks):
-        add = own_rows(came_refs[i][:, both : 2 * both], m_ref, k)
-        own = add if own is None else own + add
-    put_rows(acc, own, None if first else before)
-    if first:
-        for s in range(CAP):
-            add_sums(acc, pick(ask_ref, s), self_ref[:, s * width : (s + 1) * width])
-    for i in range(len(ks)):
-        for s in range(CAP):
-            add_sums(acc, pick(ids_refs[i], s), came_refs[i][:, s * width : (s + 1) * width])
-    if last:
-        out_ref[...] = acc[...].astype(BF16)
-
-
-def late_rows(head, ids, came, ks, operator, first, last):
-    values = head[1] if first else head[0]
+    put_rows(acc, own_rows(came_ref[:, both : 2 * both], m_ref, k), before)
+    for s in range(CAP):
+        add_sums(acc, pick(ids_ref, s), came_ref[:, s * width : (s + 1) * width])
+    out_ref[...] = acc[...].astype(out_ref.dtype)
+
+
+def late_rows(before, ids, came, operator, k, dtype):
     return call(
-        functools.partial(late_rows_kernel, ks, first, last),
+        functools.partial(late_rows_kernel, k),
         "late_rows",
-        shape(values.shape, BF16 if last else F32),
-        [vmem()] * (len(head) + 2 * len(ks) + 1),
-        [pltpu.VMEM(values.shape, F32)] if last else [],
-        flops=2 ** 27,
-        moved=2 ** 20,
-    )(*head, *[ids[k] for k in ks], *[came[k] for k in ks], operator)
+        shape(before.shape, dtype),
+        [vmem()] * 4,
+        [pltpu.VMEM(before.shape, F32)],
+        flops=2 ** 26,
+    )(before, ids, came, operator)
 
 
 def add_kernel(keep_ref, came_ref, out_ref):
@@ -488,7 +491,7 @@
     factor = wide_cot[...].astype(F32) * sig * (1.0 + pre * (1.0 - sig))
     grad[...] = factor.astype(BF16)
     spread = dot(w_ref[rows[0], :], grad[...]).astype(BF16)
-    term_ref[...] = dot(grad[rows[0], :], wide[...], NT).astype(BF16)
+    term_ref[...] = dot(grad[rows[0], :], wide[...], NT)
     wide_share = share * width
     give_ref[:, :wide_share] = spread
     for b in range(share):
@@ -510,7 +513,7 @@
             shape((share, columns, width), BF16),
             shape((columns, 2 * share * width), BF16),
             shape((share, columns, width), BF16),
-            shape((columns, features), BF16),
+            shape((columns, features), F32),
         ],
         [vmem()] * (feats + 2),
         [
@@ -570,39 +573,30 @@
     return call(pair_kernel, "pair_sum", shape(mine.shape, dtype), [vmem(), vmem()])(mine, came)
 
 
-def split_kernel(mine_ref, came_ref, act_ref, shared_ref, give_ref, keep_ref, out_ref, total):
+def split_kernel(mine_ref, came_ref, give_ref, keep_ref, total):
     half = lax.axis_index("rep")
-    blocks, _, width = act_ref.shape
-    out_ref[pl.ds(half * blocks, blocks)] = act_ref[...]
-    for b in range(blocks):
-        at = (blocks + b) * width
-        out_ref[(1 - half) * blocks + b] = shared_ref[:, at : at + width]
     part = keep_ref.shape[1]
     total[...] = mine_ref[...].astype(F32) + came_ref[...].astype(F32)
     give_ref[...] = total[:, pl.ds(pl.multiple_of((1 - half) * part, part), part)].astype(BF16)
     keep_ref[...] = total[:, pl.ds(pl.multiple_of(half * part, part), part)]
 
 
-def split_sum(mine, came, act, shared, reps):
+def split_sum(mine, came, reps):
     columns, features = mine.shape
     part = (columns, features // reps)
     return call(
         split_kernel,
         "split_sum",
-        [shape(part, BF16), shape(part, F32), shape((reps * act.shape[0],) + act.shape[1:], BF16)],
-        [vmem()] * 4,
+        [shape(part, BF16), shape(part, F32)],
+        [vmem()] * 2,
         [pltpu.VMEM(mine.shape, F32)],
-    )(mine, came, act, shared)
-
-
-def total_term(term, act, shared, peers, reps):
-    give, total, activated = split_sum(term, across(term, peers, 1), act, shared, reps)
+    )(mine, came)
+
+
+def pair_term(term, peers, reps):
+    give, total = split_sum(term, across(term, peers, 1), reps)
     total = pair_sum(total, ahead(give, "rep", reps, 1), F32 if peers == 2 else BF16)
-    bit = 2
-    while bit < peers:
-        total = pair_sum(total, across(total, peers, bit), F32 if 2 * bit == peers else BF16)
-        bit *= 2
-    return total, activated
+    return total
 
 
 def finish_kernel(mine_ref, other_ref, share_ref, other_share_ref, grad_ref, weight_ref):
@@ -674,16 +668,25 @@
     sums = [mine] + [ahead(mine, "feat", feats, feats - q) for q in range(1, feats)]
     act, give, spread, term = dense(sums, cot, weight, feats)
     shared = ahead(give, "rep", reps, 1)
-    total, activated = total_term(term, act, shared, peers, reps)
+    total = pair_term(term, peers, reps)
     values, sends, own_mirror = sends_of(spread, shared, operator, ids, peers, reps)
 
     came = [None] * peers
     for k in far_first:
         came[k] = across(sends[k], peers, k)
-    ordered, total = lax.optimization_barrier(([came[k] for k in far_first], total))
-    came = [None] + [ordered[far_first.index(k)] for k in range(1, peers)]
-    acc = late_rows([asks[0], values, own_mirror], ids, came, [], operator, True, False)
-    part = late_rows([acc], ids, came, far_first, operator, False, True)
+    acc, activated = late_self(asks[0], values, own_mirror, operator, act, shared)
+    *firsts, last = sorted(range(1, peers), key=lambda k: (k == peers - 1, -(k & middle), k))
+    for k in firsts:
+        acc = late_rows(acc, ids[k], came[k], operator, k, F32)
+    bit = 2
+    while bit < peers:
+        other = across(total, peers, bit)
+        if 2 * bit == peers:
+            total, acc = lax.optimization_barrier((total, acc))
+        total = pair_sum(total, other, F32 if 2 * bit == peers else BF16)
+        bit *= 2
+    acc, total = lax.optimization_barrier((acc, total))
+    part = late_rows(acc, ids[last], came[last], operator, last, BF16)
     input_grad, weight_grad = finish(
         part, ahead(part, "rep", reps, 1), total, ahead(total, "rep", reps, 1)
     )

time: 55.6 us -> 55.1 us (level)
  starting transfers between devices: 21 us -> 20 us
    ppermute x12, starting transfers between devices: 18.5 us -> 17.5 us  [across(): return lax.ppermute(value, 'graph', [(i, i ^ k) for i in range(peers)])]
    pallas_call x3 -> x5, Pallas kernels: 1.84 us -> 2.12 us  [the longest x3 1.09 us: late_rows(): call(functools.partial(late_rows_kernel, k), 'late_rows', shape(before.sh...]
  transfers between devices with their start and end apart: 19 -> 19, of which waited for: 7 -> 9; matrix products, arithmetic and copies ran while one was open for 0% -> 0% of each run, Pallas kernels for 11% -> 12%
where the time goes in v15:
time: 55.1 us; the launch traced here: 54.9 us
  starting transfers between devices  20 us (36%)
  waiting for transfers between devices  17.1 us (31%)
  Pallas kernels  10.7 us (19%)
  blocking collectives  5.63 us (10%)
  between operations  1.5 us (3%)
    ppermute x12, starting transfers between devices, across(): return lax.ppermute(value, 'graph', [(i, i ^ k) for i in range(peers)])  17.5 us
    ppermute x12, waiting for transfers between devices, across(): return lax.ppermute(value, 'graph', [(i, i ^ k) for i in range(peers)])  8.59 us
    ppermute x7, waiting for transfers between devices, ahead(): return lax.ppermute(value, axis, [(i, (i + k) % size) for i in range(size)])  8.48 us
    all_gather x1, blocking collectives, local(): cots = lax.all_gather(own_cot, 'feat', axis=0, tiled=True)  5.63 us
    pallas_call x1, Pallas kernels, list_operator(): call(functools.partial(operator_kernel, blocks_dev, slots_here, groups),...  3 us
    ppermute x7, starting transfers between devices, ahead(): return lax.ppermute(value, axis, [(i, (i + k) % size) for i in range(size)])  2.54 us
    pallas_call x1, Pallas kernels, prepare(): call(functools.partial(prepare_kernel, peers), 'prepare', [shape((blocks_...  1.76 us
  transfers between devices with their start and end apart: 19, of which 9 were waited for; matrix products, arithmetic and copies ran while one was open for 0% of the time, Pallas kernels for 12%

profile of v15, /device:TPU:0, one launch (start us, length us, event | category | flops | bytes accessed | tf_op | source)
XLA Modules:
  0.0 54.9 jit_solution(431610842885890363)
XLA Ops:
  0.6 1.8 %prepare.1 = (bf16[4,128,128]{2,1,0:T(8,128)(2,1)}, s32[8192,128]{1,0:T(8,128)}) custom-call(s32[1,128]{1,0:T(1,128)} %bitcast.2, s32[1,128]{1,0:T(1,128)} %bitcast.3, bf16[8,128,128]{2,1,0:T(8,128)(2,1)} %refs_4_.3), custom_call_target="tpu_custom_call" | custom-call | bytes 262144 | tf_op jit(solution)/shard_map/prepare/pallas_call | solution.py:102
  2.4 4.1 %collective-permute-start.4 = (bf16[4,128,128]{2,1,0:T(8,128)(2,1)}, bf16[4,128,128]{2,1,0:T(8,128)(2,1)S(1)}, u32[]{:S(2)}, u32[]{:S(2)}) collective-permute-start(bf16[4,128,128]{2,1,0:T(8,128)(2,1)} %get-tuple-element.66), channel_id=1, source_target_pairs={{0,8},{4,12},{8,0},{12,4},{1,9},{5,13},{9,1},{13,5},{2,10},{6,14},... | collective-permute-start | bytes 393224 | tf_op jit(solution)/shard_map/ppermute | solution.py:625
  6.5 1.6 %collective-permute-start.3 = (bf16[4,128,128]{2,1,0:T(8,128)(2,1)}, bf16[4,128,128]{2,1,0:T(8,128)(2,1)S(1)}, u32[]{:S(2)}, u32[]{:S(2)}) collective-permute-start(bf16[4,128,128]{2,1,0:T(8,128)(2,1)} %get-tuple-element.66), channel_id=1, source_target_pairs={{0,4},{4,0},{8,12},{12,8},{1,5},{5,1},{9,13},{13,9},{2,6},{6,2},{1... | collective-permute-start | bytes 393224 | tf_op jit(solution)/shard_map/ppermute | solution.py:625
  8.8 3.0 %operator.1 = (bf16[1024,1024]{1,0:T(8,128)(2,1)S(1)}, s32[1,128]{1,0:T(1,128)S(1)}, s32[1,128]{1,0:T(1,128)S(1)}, s32[1,128]{1,0:T(1,128)S(1)}, s32[1,128]{1,0:T(1,128)S(1)}) custom-call(s32[1]{0:T(128)S(6)} %copy.10.count_ref, s32[8192,128]{1,0:T(8,128)} %get-tuple-element.57.table_in, bf16[128,128,128]{2,1,0:T(8,128)(2,1)} %tiles_ref.1), custom_call_target="tpu_custom_call" | custom-call | bytes 16777216 | tf_op jit(solution)/shard_map/operator/pallas_call | solution.py:192
  12.7 2.5 %collective-permute-start.2 = (bf16[144,256]{1,0:T(8,128)(2,1)S(1)}, bf16[144,256]{1,0:T(8,128)(2,1)S(1)}, u32[]{:S(2)}, u32[]{:S(2)}) collective-permute-start(bf16[144,256]{1,0:T(8,128)(2,1)S(1)} %get-tuple-element.65), channel_id=1, source_target_pairs={{0,12},{4,8},{8,4},{12,0},{1,13},{5,9},{9,5},{13,1},{2,14},{6,10},... | collective-permute-start | bytes 221192 | tf_op jit(solution)/shard_map/ppermute | solution.py:625
  15.1 0.6 %collective-permute-start = (bf16[144,256]{1,0:T(8,128)(2,1)S(1)}, bf16[144,256]{1,0:T(8,128)(2,1)S(1)}, u32[]{:S(2)}, u32[]{:S(2)}) collective-permute-start(bf16[144,256]{1,0:T(8,128)(2,1)S(1)} %get-tuple-element.63), channel_id=1, source_target_pairs={{0,4},{4,0},{8,12},{12,8},{1,5},{5,1},{9,13},{13,9},{2,6},{6,2},{1... | collective-permute-start | bytes 221192 | tf_op jit(solution)/shard_map/ppermute | solution.py:625
  15.8 1.4 %collective-permute-start.5 = (bf16[2,128,128]{2,1,0:T(8,128)(2,1)S(1)}, bf16[2,128,128]{2,1,0:T(8,128)(2,1)S(1)}, u32[]{:S(2)}, u32[]{:S(2)}) collective-permute-start(bf16[2,128,128]{2,1,0:T(8,128)(2,1)S(1)} %get-tuple-element.70), channel_id=1, source_target_pairs={{0,4},{4,0},{8,12},{12,8},{1,5},{5,1},{9,13},{13,9},{2,6},{6,2},{1... | collective-permute-start | bytes 196616 | tf_op jit(solution)/shard_map/ppermute | solution.py:625
  17.3 0.6 %collective-permute-start.6 = (bf16[2,128,128]{2,1,0:T(8,128)(2,1)S(1)}, bf16[2,128,128]{2,1,0:T(8,128)(2,1)S(1)}, u32[]{:S(2)}, u32[]{:S(2)}) collective-permute-start(bf16[2,128,128]{2,1,0:T(8,128)(2,1)S(1)} %get-tuple-element.71), channel_id=1, source_target_pairs={{0,4},{4,0},{8,12},{12,8},{1,5},{5,1},{9,13},{13,9},{2,6},{6,2},{1... | collective-permute-start | bytes 196616 | tf_op jit(solution)/shard_map/ppermute | solution.py:625
  17.9 5.6 %all_gather.3.in_ref = bf16[8,128,128]{2,1,0:T(8,128)(2,1)S(1)} all-gather(bf16[4,128,128]{2,1,0:T(8,128)(2,1)S(1)} %get-tuple-element.72), channel_id=1, replica_groups=mesh['parts'=2,'graph'=4,'feat'=2,'rep'=2] {'feat'}, dimensions={0}, use_global_device_ids=true | all-gather | bytes 393216 | tf_op jit(solution)/shard_map/all_gather | solution.py:642
  24.1 1.3 %collective-permute-done.7.refs_5_ = bf16[12,128,128]{2,1,0:T(8,128)(2,1)S(1)} collective-permute-done((bf16[12,128,128]{2,1,0:T(8,128)(2,1)S(1)}, bf16[12,128,128]{2,1,0:T(8,128)(2,1)S(1)}, u32[]{:S(2)}, u32[]{:S(2)}) %collective-permute-start.7) | collective-permute-done | bytes 393248 | tf_op jit(solution)/shard_map/ppermute | solution.py:621
  26.5 0.8 %collective-permute-done.8.came_ref = bf16[4,128,128]{2,1,0:T(8,128)(2,1)S(1)} collective-permute-done((bf16[4,128,128]{2,1,0:T(8,128)(2,1)S(1)}, bf16[4,128,128]{2,1,0:T(8,128)(2,1)S(1)}, u32[]{:S(2)}, u32[]{:S(2)}) %collective-permute-start.8) | collective-permute-done | bytes 131104 | tf_op jit(solution)/shard_map/ppermute | solution.py:621
  27.3 1.6 %collective-permute-start.9 = (bf16[4,128,128]{2,1,0:T(8,128)(2,1)S(1)}, bf16[4,128,128]{2,1,0:T(8,128)(2,1)S(1)}, u32[]{:S(2)}, u32[]{:S(2)}) collective-permute-start(bf16[4,128,128]{2,1,0:T(8,128)(2,1)S(1)} %add_up.1.refs_0_), channel_id=1, source_target_pairs={{0,2},{2,0},{1,3},{3,1},{4,6},{6,4},{5,7},{7,5},{8,10},{10,8},{9,1... | collective-permute-start | bytes 393224 | tf_op jit(solution)/shard_map/ppermute | solution.py:621
  28.9 4.0 %collective-permute-done.9.refs_1_ = bf16[4,128,128]{2,1,0:T(8,128)(2,1)S(1)} collective-permute-done((bf16[4,128,128]{2,1,0:T(8,128)(2,1)S(1)}, bf16[4,128,128]{2,1,0:T(8,128)(2,1)S(1)}, u32[]{:S(2)}, u32[]{:S(2)}) %collective-permute-start.9) | collective-permute-done | bytes 131104 | tf_op jit(solution)/shard_map/ppermute | solution.py:621
  32.9 0.7 %dense.1 = (bf16[4,128,128]{2,1,0:T(8,128)(2,1)S(1)}, bf16[128,1024]{1,0:T(8,128)(2,1)S(1)}, bf16[4,128,128]{2,1,0:T(8,128)(2,1)S(1)}, f32[128,256]{1,0:T(8,128)S(1)}) custom-call(bf16[4,128,128]{2,1,0:T(8,128)(2,1)S(1)} %add_up.1.refs_0_, bf16[4,128,128]{2,1,0:T(8,128)(2,1)S(1)} %collective-permute-done.9.refs_1_, bf16[256,512]{1,0:T(8,128)(2,1)S(1)} %widen.1.refs_2_, ...), custom_call_target="tpu_custom_call" | custom-call | flops 268435456 | bytes 1048576 | tf_op jit(solution)/shard_map/dense/pallas_call | solution.py:509
  33.7 1.4 %collective-permute-start.11 = (f32[128,256]{1,0:T(8,128)S(1)}, f32[128,256]{1,0:T(8,128)S(1)}, u32[]{:S(2)}, u32[]{:S(2)}) collective-permute-start(f32[128,256]{1,0:T(8,128)S(1)} %get-tuple-element.98.mine_ref), channel_id=1, source_target_pairs={{0,4},{4,0},{8,12},{12,8},{1,5},{5,1},{9,13},{13,9},{2,6},{6,2},{1... | collective-permute-start | bytes 393224 | tf_op jit(solution)/shard_map/ppermute | solution.py:625
  35.6 1.3 %collective-permute-start.13 = (bf16[128,512]{1,0:T(8,128)(2,1)S(1)}, bf16[128,512]{1,0:T(8,128)(2,1)S(1)}, u32[]{:S(2)}, u32[]{:S(2)}) collective-permute-start(bf16[128,512]{1,0:T(8,128)(2,1)S(1)} %get-tuple-element.102), channel_id=1, source_target_pairs={{0,8},{4,12},{8,0},{12,4},{1,9},{5,13},{9,1},{13,5},{2,10},{6,14},... | collective-permute-start | bytes 393224 | tf_op jit(solution)/shard_map/ppermute | solution.py:625
  37.0 0.6 %collective-permute-start.14 = (bf16[128,512]{1,0:T(8,128)(2,1)S(1)}, bf16[128,512]{1,0:T(8,128)(2,1)S(1)}, u32[]{:S(2)}, u32[]{:S(2)}) collective-permute-start(bf16[128,512]{1,0:T(8,128)(2,1)S(1)} %get-tuple-element.103), channel_id=1, source_target_pairs={{0,4},{4,0},{8,12},{12,8},{1,5},{5,1},{9,13},{13,9},{2,6},{6,2},{1... | collective-permute-start | bytes 393224 | tf_op jit(solution)/shard_map/ppermute | solution.py:625
  37.6 2.5 %collective-permute-start.16 = (bf16[128,512]{1,0:T(8,128)(2,1)S(1)}, bf16[128,512]{1,0:T(8,128)(2,1)S(1)}, u32[]{:S(2)}, u32[]{:S(2)}) collective-permute-start(bf16[128,512]{1,0:T(8,128)(2,1)S(1)} %get-tuple-element.107), channel_id=1, source_target_pairs={{0,12},{4,8},{8,4},{12,0},{1,13},{5,9},{9,5},{13,1},{2,14},{6,10},... | collective-permute-start | bytes 393224 | tf_op jit(solution)/shard_map/ppermute | solution.py:625
  40.8 1.2 %collective-permute-done.12.came_ref = bf16[128,128]{1,0:T(8,128)(2,1)S(1)} collective-permute-done((bf16[128,128]{1,0:T(8,128)(2,1)S(1)}, bf16[128,128]{1,0:T(8,128)(2,1)S(1)}, u32[]{:S(2)}, u32[]{:S(2)}) %collective-permute-start.12) | collective-permute-done | bytes 32800 | tf_op jit(solution)/shard_map/ppermute | solution.py:621
  42.3 1.0 %late_self.1 = (f32[8,128,128]{2,1,0:T(8,128)S(1)}, bf16[8,128,128]{2,1,0:T(8,128)(2,1)}) custom-call(s32[1,128]{1,0:T(1,128)S(1)} %get-tuple-element.58.refs_0_.ask_ref, bf16[8,128,128]{2,1,0:T(8,128)(2,1)S(1)} %get-tuple-element.94.x3, f32[128,256]{1,0:T(8,128)S(1)} %get-tuple-element.95.self_ref, ...), custom_call_target="tpu_custom_call" | custom-call | flops 67108864 | bytes 262144 | tf_op jit(solution)/shard_map/late_self/pallas_call | solution.py:428
  43.3 3.0 %collective-permute-done.13.came_ref = bf16[128,512]{1,0:T(8,128)(2,1)S(1)} collective-permute-done((bf16[128,512]{1,0:T(8,128)(2,1)S(1)}, bf16[128,512]{1,0:T(8,128)(2,1)S(1)}, u32[]{:S(2)}, u32[]{:S(2)}) %collective-permute-start.13) | collective-permute-done | bytes 131104 | tf_op jit(solution)/shard_map/ppermute | solution.py:625
  47.0 5.0 %collective-permute-done.15.came_ref = bf16[128,128]{1,0:T(8,128)(2,1)S(1)} collective-permute-done((bf16[128,128]{1,0:T(8,128)(2,1)S(1)}, bf16[128,128]{1,0:T(8,128)(2,1)S(1)}, u32[]{:S(2)}, u32[]{:S(2)}) %collective-permute-start.15) | collective-permute-done | bytes 32800 | tf_op jit(solution)/shard_map/ppermute | solution.py:625
  52.9 1.1 %collective-permute-done.18.other_share_ref = f32[128,128]{1,0:T(8,128)S(1)} collective-permute-done((f32[128,128]{1,0:T(8,128)S(1)}, f32[128,128]{1,0:T(8,128)S(1)}, u32[]{:S(2)}, u32[]{:S(2)}) %collective-permute-start.18) | collective-permute-done | bytes 65568 | tf_op jit(solution)/shard_map/ppermute | solution.py:621
  54.1 0.9 %finish.1 = (bf16[8,128,128]{2,1,0:T(8,128)(2,1)}, f32[256,128]{1,0:T(8,128)}) custom-call(bf16[8,128,128]{2,1,0:T(8,128)(2,1)S(1)} %late_rows.5.mine_ref, bf16[8,128,128]{2,1,0:T(8,128)(2,1)S(1)} %collective-permute-done.17.other_ref, f32[128,128]{1,0:T(8,128)S(1)} %pair_sum.3.share_ref, f32[128,128]{1,0:T(8,128)S(1)} %collective-permute-done.18.other_share_ref), custom_call_target="tpu_custom_call" | custom-call | bytes 262144 | tf_op jit(solution)/shard_map/finish/pallas_call | solution.py:612
  (41 shorter events, 5.8 us)
Async XLA Ops:
  2.4 13.4 %collective-permute-start.4 = (bf16[4,128,128]{2,1,0:T(8,128)(2,1)}, bf16[4,128,128]{2,1,0:T(8,128)(2,1)S(1)}, u32[]{:S(2)}, u32[]{:S(2)}) collective-permute-start(bf16[4,128,128]{2,1,0:T(8,128)(2,1)} %get-tuple-element.66), channel_id=1, source_target_pairs={{0,8},{4,12},{8,0},{12,4},{1,9},{5,13},{9,1},{13,5},{2,10},{6,14},... | collective-permute-start | bytes 393224 | tf_op jit(solution)/shard_map/ppermute | solution.py:625
  6.5 9.3 %collective-permute-start.3 = (bf16[4,128,128]{2,1,0:T(8,128)(2,1)}, bf16[4,128,128]{2,1,0:T(8,128)(2,1)S(1)}, u32[]{:S(2)}, u32[]{:S(2)}) collective-permute-start(bf16[4,128,128]{2,1,0:T(8,128)(2,1)} %get-tuple-element.66), channel_id=1, source_target_pairs={{0,4},{4,0},{8,12},{12,8},{1,5},{5,1},{9,13},{13,9},{2,6},{6,2},{1... | collective-permute-start | bytes 393224 | tf_op jit(solution)/shard_map/ppermute | solution.py:625
  8.7 3.0 %copy-start = (bf16[8,128,128]{2,1,0:T(8,128)(2,1)S(1)}, bf16[8,128,128]{2,1,0:T(8,128)(2,1)}, u32[]{:S(2)}) copy-start(bf16[8,128,128]{2,1,0:T(8,128)(2,1)} %refs_4_.3) | copy-start | bytes 786436
  8.7 3.0 %copy-start.1 = (bf16[8,128,128]{2,1,0:T(8,128)(2,1)S(1)}, bf16[8,128,128]{2,1,0:T(8,128)(2,1)}, u32[]{:S(2)}) copy-start(bf16[8,128,128]{2,1,0:T(8,128)(2,1)} %refs_4_.2) | copy-start | bytes 786436
  12.2 11.3 %collective-permute-start.1 = (bf16[144,256]{1,0:T(8,128)(2,1)S(1)}, bf16[144,256]{1,0:T(8,128)(2,1)S(1)}, u32[]{:S(2)}, u32[]{:S(2)}) collective-permute-start(bf16[144,256]{1,0:T(8,128)(2,1)S(1)} %get-tuple-element.64), channel_id=1, source_target_pairs={{0,8},{4,12},{8,0},{12,4},{1,9},{5,13},{9,1},{13,5},{2,10},{6,14},... | collective-permute-start | bytes 221192 | tf_op jit(solution)/shard_map/ppermute | solution.py:625
  12.7 10.9 %collective-permute-start.2 = (bf16[144,256]{1,0:T(8,128)(2,1)S(1)}, bf16[144,256]{1,0:T(8,128)(2,1)S(1)}, u32[]{:S(2)}, u32[]{:S(2)}) collective-permute-start(bf16[144,256]{1,0:T(8,128)(2,1)S(1)} %get-tuple-element.65), channel_id=1, source_target_pairs={{0,12},{4,8},{8,4},{12,0},{1,13},{5,9},{9,5},{13,1},{2,14},{6,10},... | collective-permute-start | bytes 221192 | tf_op jit(solution)/shard_map/ppermute | solution.py:625
  15.1 8.4 %collective-permute-start = (bf16[144,256]{1,0:T(8,128)(2,1)S(1)}, bf16[144,256]{1,0:T(8,128)(2,1)S(1)}, u32[]{:S(2)}, u32[]{:S(2)}) collective-permute-start(bf16[144,256]{1,0:T(8,128)(2,1)S(1)} %get-tuple-element.63), channel_id=1, source_target_pairs={{0,4},{4,0},{8,12},{12,8},{1,5},{5,1},{9,13},{13,9},{2,6},{6,2},{1... | collective-permute-start | bytes 221192 | tf_op jit(solution)/shard_map/ppermute | solution.py:625
  15.8 7.7 %collective-permute-start.5 = (bf16[2,128,128]{2,1,0:T(8,128)(2,1)S(1)}, bf16[2,128,128]{2,1,0:T(8,128)(2,1)S(1)}, u32[]{:S(2)}, u32[]{:S(2)}) collective-permute-start(bf16[2,128,128]{2,1,0:T(8,128)(2,1)S(1)} %get-tuple-element.70), channel_id=1, source_target_pairs={{0,4},{4,0},{8,12},{12,8},{1,5},{5,1},{9,13},{13,9},{2,6},{6,2},{1... | collective-permute-start | bytes 196616 | tf_op jit(solution)/shard_map/ppermute | solution.py:625
  17.3 6.3 %collective-permute-start.6 = (bf16[2,128,128]{2,1,0:T(8,128)(2,1)S(1)}, bf16[2,128,128]{2,1,0:T(8,128)(2,1)S(1)}, u32[]{:S(2)}, u32[]{:S(2)}) collective-permute-start(bf16[2,128,128]{2,1,0:T(8,128)(2,1)S(1)} %get-tuple-element.71), channel_id=1, source_target_pairs={{0,4},{4,0},{8,12},{12,8},{1,5},{5,1},{9,13},{13,9},{2,6},{6,2},{1... | collective-permute-start | bytes 196616 | tf_op jit(solution)/shard_map/ppermute | solution.py:625
  23.6 1.8 %collective-permute-start.7 = (bf16[12,128,128]{2,1,0:T(8,128)(2,1)S(1)}, bf16[12,128,128]{2,1,0:T(8,128)(2,1)S(1)}, u32[]{:S(2)}, u32[]{:S(2)}) collective-permute-start(bf16[12,128,128]{2,1,0:T(8,128)(2,1)S(1)} %stack.1.refs_4_), channel_id=1, source_target_pairs={{0,1},{1,0},{2,3},{3,2},{4,5},{5,4},{6,7},{7,6},{8,9},{9,8},{10,11... | collective-permute-start | bytes 1179656 | tf_op jit(solution)/shard_map/ppermute | solution.py:621
  24.1 8.8 %copy-start.2 = (bf16[256,256]{1,0:T(8,128)(2,1)S(1)}, bf16[256,256]{1,0:T(8,128)(2,1)}, u32[]{:S(2)}) copy-start(bf16[256,256]{1,0:T(8,128)(2,1)} %refs_3_.3) | copy-start | bytes 393220
  25.9 1.4 %collective-permute-start.8 = (bf16[4,128,128]{2,1,0:T(8,128)(2,1)S(1)}, bf16[4,128,128]{2,1,0:T(8,128)(2,1)S(1)}, u32[]{:S(2)}, u32[]{:S(2)}) collective-permute-start(bf16[4,128,128]{2,1,0:T(8,128)(2,1)S(1)} %get-tuple-element.90), channel_id=1, source_target_pairs={{0,1},{1,0},{2,3},{3,2},{4,5},{5,4},{6,7},{7,6},{8,9},{9,8},{10,11... | collective-permute-start | bytes 393224 | tf_op jit(solution)/shard_map/ppermute | solution.py:621
  27.3 5.6 %collective-permute-start.9 = (bf16[4,128,128]{2,1,0:T(8,128)(2,1)S(1)}, bf16[4,128,128]{2,1,0:T(8,128)(2,1)S(1)}, u32[]{:S(2)}, u32[]{:S(2)}) collective-permute-start(bf16[4,128,128]{2,1,0:T(8,128)(2,1)S(1)} %add_up.1.refs_0_), channel_id=1, source_target_pairs={{0,2},{2,0},{1,3},{3,1},{4,6},{6,4},{5,7},{7,5},{8,10},{10,8},{9,1... | collective-permute-start | bytes 393224 | tf_op jit(solution)/shard_map/ppermute | solution.py:621
  33.6 1.6 %collective-permute-start.10 = (bf16[128,1024]{1,0:T(8,128)(2,1)S(1)}, bf16[128,1024]{1,0:T(8,128)(2,1)S(1)}, u32[]{:S(2)}, u32[]{:S(2)}) collective-permute-start(bf16[128,1024]{1,0:T(8,128)(2,1)S(1)} %get-tuple-element.93), channel_id=1, source_target_pairs={{0,1},{1,0},{2,3},{3,2},{4,5},{5,4},{6,7},{7,6},{8,9},{9,8},{10,11... | collective-permute-start | bytes 786440 | tf_op jit(solution)/shard_map/ppermute | solution.py:621
  33.7 7.0 %collective-permute-start.11 = (f32[128,256]{1,0:T(8,128)S(1)}, f32[128,256]{1,0:T(8,128)S(1)}, u32[]{:S(2)}, u32[]{:S(2)}) collective-permute-start(f32[128,256]{1,0:T(8,128)S(1)} %get-tuple-element.98.mine_ref), channel_id=1, source_target_pairs={{0,4},{4,0},{8,12},{12,8},{1,5},{5,1},{9,13},{13,9},{2,6},{6,2},{1... | collective-permute-start | bytes 393224 | tf_op jit(solution)/shard_map/ppermute | solution.py:625
  35.6 10.6 %collective-permute-start.13 = (bf16[128,512]{1,0:T(8,128)(2,1)S(1)}, bf16[128,512]{1,0:T(8,128)(2,1)S(1)}, u32[]{:S(2)}, u32[]{:S(2)}) collective-permute-start(bf16[128,512]{1,0:T(8,128)(2,1)S(1)} %get-tuple-element.102), channel_id=1, source_target_pairs={{0,8},{4,12},{8,0},{12,4},{1,9},{5,13},{9,1},{13,5},{2,10},{6,14},... | collective-permute-start | bytes 393224 | tf_op jit(solution)/shard_map/ppermute | solution.py:625
  37.0 9.7 %collective-permute-start.14 = (bf16[128,512]{1,0:T(8,128)(2,1)S(1)}, bf16[128,512]{1,0:T(8,128)(2,1)S(1)}, u32[]{:S(2)}, u32[]{:S(2)}) collective-permute-start(bf16[128,512]{1,0:T(8,128)(2,1)S(1)} %get-tuple-element.103), channel_id=1, source_target_pairs={{0,4},{4,0},{8,12},{12,8},{1,5},{5,1},{9,13},{13,9},{2,6},{6,2},{1... | collective-permute-start | bytes 393224 | tf_op jit(solution)/shard_map/ppermute | solution.py:625
  37.6 14.4 %collective-permute-start.16 = (bf16[128,512]{1,0:T(8,128)(2,1)S(1)}, bf16[128,512]{1,0:T(8,128)(2,1)S(1)}, u32[]{:S(2)}, u32[]{:S(2)}) collective-permute-start(bf16[128,512]{1,0:T(8,128)(2,1)S(1)} %get-tuple-element.107), channel_id=1, source_target_pairs={{0,12},{4,8},{8,4},{12,0},{1,13},{5,9},{9,5},{13,1},{2,14},{6,10},... | collective-permute-start | bytes 393224 | tf_op jit(solution)/shard_map/ppermute | solution.py:625
  40.8 1.3 %collective-permute-start.12 = (bf16[128,128]{1,0:T(8,128)(2,1)S(1)}, bf16[128,128]{1,0:T(8,128)(2,1)S(1)}, u32[]{:S(2)}, u32[]{:S(2)}) collective-permute-start(bf16[128,128]{1,0:T(8,128)(2,1)S(1)} %get-tuple-element.100), channel_id=1, source_target_pairs={{0,1},{1,0},{2,3},{3,2},{4,5},{5,4},{6,7},{7,6},{8,9},{9,8},{10,11... | collective-permute-start | bytes 98312 | tf_op jit(solution)/shard_map/ppermute | solution.py:621
  42.0 9.9 %collective-permute-start.15 = (bf16[128,128]{1,0:T(8,128)(2,1)S(1)}, bf16[128,128]{1,0:T(8,128)(2,1)S(1)}, u32[]{:S(2)}, u32[]{:S(2)}) collective-permute-start(bf16[128,128]{1,0:T(8,128)(2,1)S(1)} %pair_sum.2.mine_ref), channel_id=1, source_target_pairs={{0,8},{4,12},{8,0},{12,4},{1,9},{5,13},{9,1},{13,5},{2,10},{6,14},... | collective-permute-start | bytes 98312 | tf_op jit(solution)/shard_map/ppermute | solution.py:625
  52.4 1.7 %collective-permute-start.17 = (bf16[8,128,128]{2,1,0:T(8,128)(2,1)S(1)}, bf16[8,128,128]{2,1,0:T(8,128)(2,1)S(1)}, u32[]{:S(2)}, u32[]{:S(2)}) collective-permute-start(bf16[8,128,128]{2,1,0:T(8,128)(2,1)S(1)} %late_rows.5.mine_ref), channel_id=1, source_target_pairs={{0,1},{1,0},{2,3},{3,2},{4,5},{5,4},{6,7},{7,6},{8,9},{9,8},{10,11... | collective-permute-start | bytes 786440 | tf_op jit(solution)/shard_map/ppermute | solution.py:621
  52.4 1.6 %collective-permute-start.18 = (f32[128,128]{1,0:T(8,128)S(1)}, f32[128,128]{1,0:T(8,128)S(1)}, u32[]{:S(2)}, u32[]{:S(2)}) collective-permute-start(f32[128,128]{1,0:T(8,128)S(1)} %pair_sum.3.share_ref), channel_id=1, source_target_pairs={{0,1},{1,0},{2,3},{3,2},{4,5},{5,4},{6,7},{7,6},{8,9},{9,8},{10,11... | collective-permute-start | bytes 196616 | tf_op jit(solution)/shard_map/ppermute | solution.py:621

commit v16 on v15

--- a/solution.py
+++ b/solution.py
@@ -9,7 +9,7 @@
 
 CAP = 2
 GROUP = 8
-CHUNK = 16
+CHUNK = 8
 SIDES = 1
 PLACE_ROWS = 8
 PLACE_BUFFER = 2 ** 22
@@ -65,16 +65,20 @@
 
 def places(peers, blocks_dev, row, col, table):
     me = lax.axis_index("graph")
+    both = (2 * peers, col.shape[1])
+    side = lax.broadcasted_iota(jnp.int32, both, 0)
+    k_of = jnp.where(side < peers, side, side - peers)
+    local = jnp.broadcast_to(col, both) - jnp.bitwise_xor(me, k_of) * blocks_dev
+    inside = (local >= 0) & (local < blocks_dev)
+    ends = jnp.where(side < peers, jnp.where(inside, local, blocks_dev - 1), jnp.where(inside, -local, 0))
+    ends = jnp.min(ends, axis=1, keepdims=True)
     lane = lax.broadcasted_iota(jnp.int32, col.shape, 1)
     place = jnp.zeros(col.shape, jnp.int32)
     for k in range(peers):
-        local = col - jnp.bitwise_xor(me, k) * blocks_dev
-        inside = (local >= 0) & (local < blocks_dev)
-        low = jnp.min(jnp.where(inside, local, blocks_dev - 1), axis=1, keepdims=True)
-        high = jnp.max(jnp.where(inside, local, 0), axis=1, keepdims=True)
+        low, high = ends[k : k + 1], -ends[peers + k : peers + k + 1]
         table[PLACE_ROWS + k : PLACE_ROWS + k + 1, :] = jnp.where(lane == 0, low, high)
-        slot = k * CAP + (local != low).astype(jnp.int32)
-        place = jnp.where(inside, slot * blocks_dev + row, place)
+        slot = k * CAP + (local[k : k + 1] != low).astype(jnp.int32)
+        place = jnp.where(inside[k : k + 1], slot * blocks_dev + row, place)
     table[:PLACE_ROWS, :] = jnp.broadcast_to(place, (PLACE_ROWS, place.shape[1]))
 
 
@@ -82,15 +86,24 @@
     return PLACE_ROWS + -(-peers // 8) * 8
 
 
-def prepare_kernel(peers, row_ref, col_ref, x3, half_out, table_out, table, half_sem, sem):
+def prepare_kernel(peers, row_in, col_in, x3, half_out, table_out, half, row, col, table, in_sem, row_sem, col_sem, sems):
     share = half_out.shape[0]
     mine = pl.ds(lax.axis_index("rep") * share, share)
-    half_copy = pltpu.make_async_copy(x3.at[mine], half_out, half_sem)
-    half_copy.start()
+    half_in = pltpu.make_async_copy(x3.at[mine], half, in_sem)
+    row_copy = pltpu.make_async_copy(row_in, row, row_sem)
+    col_copy = pltpu.make_async_copy(col_in, col, col_sem)
+    col_copy.start()
+    row_copy.start()
+    half_in.start()
     if table.shape[0] > PLACE_ROWS + peers:
         table[...] = jnp.zeros(table.shape, jnp.int32)
-    places(peers, x3.shape[0], row_ref[...], col_ref[...], table)
-    copy = pltpu.make_async_copy(table, table_out.at[pl.ds(0, table.shape[0])], sem)
+    half_in.wait()
+    half_copy = pltpu.make_async_copy(half, half_out, sems.at[0])
+    half_copy.start()
+    col_copy.wait()
+    row_copy.wait()
+    places(peers, x3.shape[0], row[...], col[...], table)
+    copy = pltpu.make_async_copy(table, table_out.at[pl.ds(0, table.shape[0])], sems.at[1])
     copy.start()
     half_copy.wait()
     copy.wait()
@@ -99,15 +112,21 @@
 def prepare(features, tile_row, tile_col, peers, reps):
     per = tile_col.shape[0]
     blocks_dev, columns, width = features.shape
+    share = (blocks_dev // reps, columns, width)
     return call(
         functools.partial(prepare_kernel, peers),
         "prepare",
-        [shape((blocks_dev // reps, columns, width), BF16), shape((PLACE_BUFFER // (4 * per), per), jnp.int32)],
-        [vmem()] * 3,
+        [shape(share, BF16), shape((PLACE_BUFFER // (4 * per), per), jnp.int32)],
+        [hbm()] * 3,
         [
+            pltpu.VMEM(share, BF16),
+            pltpu.VMEM((1, per), jnp.int32),
+            pltpu.VMEM((1, per), jnp.int32),
             pltpu.VMEM((table_rows(peers), per), jnp.int32),
             pltpu.SemaphoreType.DMA,
             pltpu.SemaphoreType.DMA,
+            pltpu.SemaphoreType.DMA,
+            pltpu.SemaphoreType.DMA((2,)),
         ],
         limit=VMEM_ALL,
         out_specs=[hbm(), hbm()],

time: 55.1 us -> 55.1 us (level)
  no operation moved by 1% of the time
where the time goes in v16:
time: 55.1 us; the launch traced here: 54.9 us
  starting transfers between devices  20 us (36%)
  waiting for transfers between devices  17.1 us (31%)
  Pallas kernels  10.7 us (19%)
  blocking collectives  5.63 us (10%)
  between operations  1.5 us (3%)
    ppermute x12, starting transfers between devices, across(): return lax.ppermute(value, 'graph', [(i, i ^ k) for i in range(peers)])  17.4 us
    ppermute x12, waiting for transfers between devices, across(): return lax.ppermute(value, 'graph', [(i, i ^ k) for i in range(peers)])  8.59 us
    ppermute x7, waiting for transfers between devices, ahead(): return lax.ppermute(value, axis, [(i, (i + k) % size) for i in range(size)])  8.49 us
    all_gather x1, blocking collectives, local(): cots = lax.all_gather(own_cot, 'feat', axis=0, tiled=True)  5.63 us
    pallas_call x1, Pallas kernels, list_operator(): call(functools.partial(operator_kernel, blocks_dev, slots_here, groups),...  2.99 us
    ppermute x7, starting transfers between devices, ahead(): return lax.ppermute(value, axis, [(i, (i + k) % size) for i in range(size)])  2.54 us
    pallas_call x1, Pallas kernels, prepare(): call(functools.partial(prepare_kernel, peers), 'prepare', [shape(share, B...  1.75 us
  transfers between devices with their start and end apart: 19, of which 9 were waited for; matrix products, arithmetic and copies ran while one was open for 0% of the time, Pallas kernels for 12%

profile of v16, /device:TPU:0, one launch (start us, length us, event | category | flops | bytes accessed | tf_op | source)
XLA Modules:
  0.0 54.9 jit_solution(1600319513981644280)
XLA Ops:
  0.6 1.7 %prepare.1 = (bf16[4,128,128]{2,1,0:T(8,128)(2,1)}, s32[8192,128]{1,0:T(8,128)}) custom-call(s32[1,128]{1,0:T(1,128)} %bitcast.2, s32[1,128]{1,0:T(1,128)} %bitcast.3, bf16[8,128,128]{2,1,0:T(8,128)(2,1)} %refs_4_.3), custom_call_target="tpu_custom_call" | custom-call | bytes 262144 | tf_op jit(solution)/shard_map/prepare/pallas_call | solution.py:116
  2.4 4.1 %collective-permute-start.4 = (bf16[4,128,128]{2,1,0:T(8,128)(2,1)}, bf16[4,128,128]{2,1,0:T(8,128)(2,1)S(1)}, u32[]{:S(2)}, u32[]{:S(2)}) collective-permute-start(bf16[4,128,128]{2,1,0:T(8,128)(2,1)} %get-tuple-element.66), channel_id=1, source_target_pairs={{0,8},{4,12},{8,0},{12,4},{1,9},{5,13},{9,1},{13,5},{2,10},{6,14},... | collective-permute-start | bytes 393224 | tf_op jit(solution)/shard_map/ppermute | solution.py:644
  6.5 1.6 %collective-permute-start.3 = (bf16[4,128,128]{2,1,0:T(8,128)(2,1)}, bf16[4,128,128]{2,1,0:T(8,128)(2,1)S(1)}, u32[]{:S(2)}, u32[]{:S(2)}) collective-permute-start(bf16[4,128,128]{2,1,0:T(8,128)(2,1)} %get-tuple-element.66), channel_id=1, source_target_pairs={{0,4},{4,0},{8,12},{12,8},{1,5},{5,1},{9,13},{13,9},{2,6},{6,2},{1... | collective-permute-start | bytes 393224 | tf_op jit(solution)/shard_map/ppermute | solution.py:644
  8.7 3.0 %operator.1 = (bf16[1024,1024]{1,0:T(8,128)(2,1)S(1)}, s32[1,128]{1,0:T(1,128)S(1)}, s32[1,128]{1,0:T(1,128)S(1)}, s32[1,128]{1,0:T(1,128)S(1)}, s32[1,128]{1,0:T(1,128)S(1)}) custom-call(s32[1]{0:T(128)S(6)} %copy.10.count_ref, s32[8192,128]{1,0:T(8,128)} %get-tuple-element.57.table_in, bf16[128,128,128]{2,1,0:T(8,128)(2,1)} %tiles_ref.1), custom_call_target="tpu_custom_call" | custom-call | bytes 16777216 | tf_op jit(solution)/shard_map/operator/pallas_call | solution.py:211
  12.6 2.5 %collective-permute-start.2 = (bf16[144,256]{1,0:T(8,128)(2,1)S(1)}, bf16[144,256]{1,0:T(8,128)(2,1)S(1)}, u32[]{:S(2)}, u32[]{:S(2)}) collective-permute-start(bf16[144,256]{1,0:T(8,128)(2,1)S(1)} %get-tuple-element.65), channel_id=1, source_target_pairs={{0,12},{4,8},{8,4},{12,0},{1,13},{5,9},{9,5},{13,1},{2,14},{6,10},... | collective-permute-start | bytes 221192 | tf_op jit(solution)/shard_map/ppermute | solution.py:644
  15.1 0.7 %collective-permute-start = (bf16[144,256]{1,0:T(8,128)(2,1)S(1)}, bf16[144,256]{1,0:T(8,128)(2,1)S(1)}, u32[]{:S(2)}, u32[]{:S(2)}) collective-permute-start(bf16[144,256]{1,0:T(8,128)(2,1)S(1)} %get-tuple-element.63), channel_id=1, source_target_pairs={{0,4},{4,0},{8,12},{12,8},{1,5},{5,1},{9,13},{13,9},{2,6},{6,2},{1... | collective-permute-start | bytes 221192 | tf_op jit(solution)/shard_map/ppermute | solution.py:644
  15.8 1.4 %collective-permute-start.5 = (bf16[2,128,128]{2,1,0:T(8,128)(2,1)S(1)}, bf16[2,128,128]{2,1,0:T(8,128)(2,1)S(1)}, u32[]{:S(2)}, u32[]{:S(2)}) collective-permute-start(bf16[2,128,128]{2,1,0:T(8,128)(2,1)S(1)} %get-tuple-element.70), channel_id=1, source_target_pairs={{0,4},{4,0},{8,12},{12,8},{1,5},{5,1},{9,13},{13,9},{2,6},{6,2},{1... | collective-permute-start | bytes 196616 | tf_op jit(solution)/shard_map/ppermute | solution.py:644
  17.2 0.7 %collective-permute-start.6 = (bf16[2,128,128]{2,1,0:T(8,128)(2,1)S(1)}, bf16[2,128,128]{2,1,0:T(8,128)(2,1)S(1)}, u32[]{:S(2)}, u32[]{:S(2)}) collective-permute-start(bf16[2,128,128]{2,1,0:T(8,128)(2,1)S(1)} %get-tuple-element.71), channel_id=1, source_target_pairs={{0,4},{4,0},{8,12},{12,8},{1,5},{5,1},{9,13},{13,9},{2,6},{6,2},{1... | collective-permute-start | bytes 196616 | tf_op jit(solution)/shard_map/ppermute | solution.py:644
  17.9 5.6 %all_gather.3.in_ref = bf16[8,128,128]{2,1,0:T(8,128)(2,1)S(1)} all-gather(bf16[4,128,128]{2,1,0:T(8,128)(2,1)S(1)} %get-tuple-element.72), channel_id=1, replica_groups=mesh['parts'=2,'graph'=4,'feat'=2,'rep'=2] {'feat'}, dimensions={0}, use_global_device_ids=true | all-gather | bytes 393216 | tf_op jit(solution)/shard_map/all_gather | solution.py:661
  24.1 1.3 %collective-permute-done.7.refs_5_ = bf16[12,128,128]{2,1,0:T(8,128)(2,1)S(1)} collective-permute-done((bf16[12,128,128]{2,1,0:T(8,128)(2,1)S(1)}, bf16[12,128,128]{2,1,0:T(8,128)(2,1)S(1)}, u32[]{:S(2)}, u32[]{:S(2)}) %collective-permute-start.7) | collective-permute-done | bytes 393248 | tf_op jit(solution)/shard_map/ppermute | solution.py:640
  26.5 0.8 %collective-permute-done.8.came_ref = bf16[4,128,128]{2,1,0:T(8,128)(2,1)S(1)} collective-permute-done((bf16[4,128,128]{2,1,0:T(8,128)(2,1)S(1)}, bf16[4,128,128]{2,1,0:T(8,128)(2,1)S(1)}, u32[]{:S(2)}, u32[]{:S(2)}) %collective-permute-start.8) | collective-permute-done | bytes 131104 | tf_op jit(solution)/shard_map/ppermute | solution.py:640
  27.3 1.6 %collective-permute-start.9 = (bf16[4,128,128]{2,1,0:T(8,128)(2,1)S(1)}, bf16[4,128,128]{2,1,0:T(8,128)(2,1)S(1)}, u32[]{:S(2)}, u32[]{:S(2)}) collective-permute-start(bf16[4,128,128]{2,1,0:T(8,128)(2,1)S(1)} %add_up.1.refs_0_), channel_id=1, source_target_pairs={{0,2},{2,0},{1,3},{3,1},{4,6},{6,4},{5,7},{7,5},{8,10},{10,8},{9,1... | collective-permute-start | bytes 393224 | tf_op jit(solution)/shard_map/ppermute | solution.py:640
  28.9 4.0 %collective-permute-done.9.refs_1_ = bf16[4,128,128]{2,1,0:T(8,128)(2,1)S(1)} collective-permute-done((bf16[4,128,128]{2,1,0:T(8,128)(2,1)S(1)}, bf16[4,128,128]{2,1,0:T(8,128)(2,1)S(1)}, u32[]{:S(2)}, u32[]{:S(2)}) %collective-permute-start.9) | collective-permute-done | bytes 131104 | tf_op jit(solution)/shard_map/ppermute | solution.py:640
  32.9 0.7 %dense.1 = (bf16[4,128,128]{2,1,0:T(8,128)(2,1)S(1)}, bf16[128,1024]{1,0:T(8,128)(2,1)S(1)}, bf16[4,128,128]{2,1,0:T(8,128)(2,1)S(1)}, f32[128,256]{1,0:T(8,128)S(1)}) custom-call(bf16[4,128,128]{2,1,0:T(8,128)(2,1)S(1)} %add_up.1.refs_0_, bf16[4,128,128]{2,1,0:T(8,128)(2,1)S(1)} %collective-permute-done.9.refs_1_, bf16[256,512]{1,0:T(8,128)(2,1)S(1)} %widen.1.refs_2_, ...), custom_call_target="tpu_custom_call" | custom-call | flops 268435456 | bytes 1048576 | tf_op jit(solution)/shard_map/dense/pallas_call | solution.py:528
  33.7 1.4 %collective-permute-start.11 = (f32[128,256]{1,0:T(8,128)S(1)}, f32[128,256]{1,0:T(8,128)S(1)}, u32[]{:S(2)}, u32[]{:S(2)}) collective-permute-start(f32[128,256]{1,0:T(8,128)S(1)} %get-tuple-element.98.mine_ref), channel_id=1, source_target_pairs={{0,4},{4,0},{8,12},{12,8},{1,5},{5,1},{9,13},{13,9},{2,6},{6,2},{1... | collective-permute-start | bytes 393224 | tf_op jit(solution)/shard_map/ppermute | solution.py:644
  35.6 1.3 %collective-permute-start.13 = (bf16[128,512]{1,0:T(8,128)(2,1)S(1)}, bf16[128,512]{1,0:T(8,128)(2,1)S(1)}, u32[]{:S(2)}, u32[]{:S(2)}) collective-permute-start(bf16[128,512]{1,0:T(8,128)(2,1)S(1)} %get-tuple-element.102), channel_id=1, source_target_pairs={{0,8},{4,12},{8,0},{12,4},{1,9},{5,13},{9,1},{13,5},{2,10},{6,14},... | collective-permute-start | bytes 393224 | tf_op jit(solution)/shard_map/ppermute | solution.py:644
  36.9 0.6 %collective-permute-start.14 = (bf16[128,512]{1,0:T(8,128)(2,1)S(1)}, bf16[128,512]{1,0:T(8,128)(2,1)S(1)}, u32[]{:S(2)}, u32[]{:S(2)}) collective-permute-start(bf16[128,512]{1,0:T(8,128)(2,1)S(1)} %get-tuple-element.103), channel_id=1, source_target_pairs={{0,4},{4,0},{8,12},{12,8},{1,5},{5,1},{9,13},{13,9},{2,6},{6,2},{1... | collective-permute-start | bytes 393224 | tf_op jit(solution)/shard_map/ppermute | solution.py:644
  37.6 2.5 %collective-permute-start.16 = (bf16[128,512]{1,0:T(8,128)(2,1)S(1)}, bf16[128,512]{1,0:T(8,128)(2,1)S(1)}, u32[]{:S(2)}, u32[]{:S(2)}) collective-permute-start(bf16[128,512]{1,0:T(8,128)(2,1)S(1)} %get-tuple-element.107), channel_id=1, source_target_pairs={{0,12},{4,8},{8,4},{12,0},{1,13},{5,9},{9,5},{13,1},{2,14},{6,10},... | collective-permute-start | bytes 393224 | tf_op jit(solution)/shard_map/ppermute | solution.py:644
  40.8 1.2 %collective-permute-done.12.came_ref = bf16[128,128]{1,0:T(8,128)(2,1)S(1)} collective-permute-done((bf16[128,128]{1,0:T(8,128)(2,1)S(1)}, bf16[128,128]{1,0:T(8,128)(2,1)S(1)}, u32[]{:S(2)}, u32[]{:S(2)}) %collective-permute-start.12) | collective-permute-done | bytes 32800 | tf_op jit(solution)/shard_map/ppermute | solution.py:640
  42.3 1.0 %late_self.1 = (f32[8,128,128]{2,1,0:T(8,128)S(1)}, bf16[8,128,128]{2,1,0:T(8,128)(2,1)}) custom-call(s32[1,128]{1,0:T(1,128)S(1)} %get-tuple-element.58.refs_0_.ask_ref, bf16[8,128,128]{2,1,0:T(8,128)(2,1)S(1)} %get-tuple-element.94.x3, f32[128,256]{1,0:T(8,128)S(1)} %get-tuple-element.95.self_ref, ...), custom_call_target="tpu_custom_call" | custom-call | flops 67108864 | bytes 262144 | tf_op jit(solution)/shard_map/late_self/pallas_call | solution.py:447
  43.3 3.0 %collective-permute-done.13.came_ref = bf16[128,512]{1,0:T(8,128)(2,1)S(1)} collective-permute-done((bf16[128,512]{1,0:T(8,128)(2,1)S(1)}, bf16[128,512]{1,0:T(8,128)(2,1)S(1)}, u32[]{:S(2)}, u32[]{:S(2)}) %collective-permute-start.13) | collective-permute-done | bytes 131104 | tf_op jit(solution)/shard_map/ppermute | solution.py:644
  47.0 5.0 %collective-permute-done.15.came_ref = bf16[128,128]{1,0:T(8,128)(2,1)S(1)} collective-permute-done((bf16[128,128]{1,0:T(8,128)(2,1)S(1)}, bf16[128,128]{1,0:T(8,128)(2,1)S(1)}, u32[]{:S(2)}, u32[]{:S(2)}) %collective-permute-start.15) | collective-permute-done | bytes 32800 | tf_op jit(solution)/shard_map/ppermute | solution.py:644
  52.9 1.1 %collective-permute-done.18.other_share_ref = f32[128,128]{1,0:T(8,128)S(1)} collective-permute-done((f32[128,128]{1,0:T(8,128)S(1)}, f32[128,128]{1,0:T(8,128)S(1)}, u32[]{:S(2)}, u32[]{:S(2)}) %collective-permute-start.18) | collective-permute-done | bytes 65568 | tf_op jit(solution)/shard_map/ppermute | solution.py:640
  54.0 0.9 %finish.1 = (bf16[8,128,128]{2,1,0:T(8,128)(2,1)}, f32[256,128]{1,0:T(8,128)}) custom-call(bf16[8,128,128]{2,1,0:T(8,128)(2,1)S(1)} %late_rows.5.mine_ref, bf16[8,128,128]{2,1,0:T(8,128)(2,1)S(1)} %collective-permute-done.17.other_ref, f32[128,128]{1,0:T(8,128)S(1)} %pair_sum.3.share_ref, f32[128,128]{1,0:T(8,128)S(1)} %collective-permute-done.18.other_share_ref), custom_call_target="tpu_custom_call" | custom-call | bytes 262144 | tf_op jit(solution)/shard_map/finish/pallas_call | solution.py:631
  (41 shorter events, 5.8 us)
Async XLA Ops:
  2.4 13.4 %collective-permute-start.4 = (bf16[4,128,128]{2,1,0:T(8,128)(2,1)}, bf16[4,128,128]{2,1,0:T(8,128)(2,1)S(1)}, u32[]{:S(2)}, u32[]{:S(2)}) collective-permute-start(bf16[4,128,128]{2,1,0:T(8,128)(2,1)} %get-tuple-element.66), channel_id=1, source_target_pairs={{0,8},{4,12},{8,0},{12,4},{1,9},{5,13},{9,1},{13,5},{2,10},{6,14},... | collective-permute-start | bytes 393224 | tf_op jit(solution)/shard_map/ppermute | solution.py:644
  6.5 9.3 %collective-permute-start.3 = (bf16[4,128,128]{2,1,0:T(8,128)(2,1)}, bf16[4,128,128]{2,1,0:T(8,128)(2,1)S(1)}, u32[]{:S(2)}, u32[]{:S(2)}) collective-permute-start(bf16[4,128,128]{2,1,0:T(8,128)(2,1)} %get-tuple-element.66), channel_id=1, source_target_pairs={{0,4},{4,0},{8,12},{12,8},{1,5},{5,1},{9,13},{13,9},{2,6},{6,2},{1... | collective-permute-start | bytes 393224 | tf_op jit(solution)/shard_map/ppermute | solution.py:644
  8.7 3.0 %copy-start = (bf16[8,128,128]{2,1,0:T(8,128)(2,1)S(1)}, bf16[8,128,128]{2,1,0:T(8,128)(2,1)}, u32[]{:S(2)}) copy-start(bf16[8,128,128]{2,1,0:T(8,128)(2,1)} %refs_4_.3) | copy-start | bytes 786436
  8.7 3.0 %copy-start.1 = (bf16[8,128,128]{2,1,0:T(8,128)(2,1)S(1)}, bf16[8,128,128]{2,1,0:T(8,128)(2,1)}, u32[]{:S(2)}) copy-start(bf16[8,128,128]{2,1,0:T(8,128)(2,1)} %refs_4_.2) | copy-start | bytes 786436
  12.2 11.3 %collective-permute-start.1 = (bf16[144,256]{1,0:T(8,128)(2,1)S(1)}, bf16[144,256]{1,0:T(8,128)(2,1)S(1)}, u32[]{:S(2)}, u32[]{:S(2)}) collective-permute-start(bf16[144,256]{1,0:T(8,128)(2,1)S(1)} %get-tuple-element.64), channel_id=1, source_target_pairs={{0,8},{4,12},{8,0},{12,4},{1,9},{5,13},{9,1},{13,5},{2,10},{6,14},... | collective-permute-start | bytes 221192 | tf_op jit(solution)/shard_map/ppermute | solution.py:644
  12.6 10.9 %collective-permute-start.2 = (bf16[144,256]{1,0:T(8,128)(2,1)S(1)}, bf16[144,256]{1,0:T(8,128)(2,1)S(1)}, u32[]{:S(2)}, u32[]{:S(2)}) collective-permute-start(bf16[144,256]{1,0:T(8,128)(2,1)S(1)} %get-tuple-element.65), channel_id=1, source_target_pairs={{0,12},{4,8},{8,4},{12,0},{1,13},{5,9},{9,5},{13,1},{2,14},{6,10},... | collective-permute-start | bytes 221192 | tf_op jit(solution)/shard_map/ppermute | solution.py:644
  15.1 8.4 %collective-permute-start = (bf16[144,256]{1,0:T(8,128)(2,1)S(1)}, bf16[144,256]{1,0:T(8,128)(2,1)S(1)}, u32[]{:S(2)}, u32[]{:S(2)}) collective-permute-start(bf16[144,256]{1,0:T(8,128)(2,1)S(1)} %get-tuple-element.63), channel_id=1, source_target_pairs={{0,4},{4,0},{8,12},{12,8},{1,5},{5,1},{9,13},{13,9},{2,6},{6,2},{1... | collective-permute-start | bytes 221192 | tf_op jit(solution)/shard_map/ppermute | solution.py:644
  15.8 7.7 %collective-permute-start.5 = (bf16[2,128,128]{2,1,0:T(8,128)(2,1)S(1)}, bf16[2,128,128]{2,1,0:T(8,128)(2,1)S(1)}, u32[]{:S(2)}, u32[]{:S(2)}) collective-permute-start(bf16[2,128,128]{2,1,0:T(8,128)(2,1)S(1)} %get-tuple-element.70), channel_id=1, source_target_pairs={{0,4},{4,0},{8,12},{12,8},{1,5},{5,1},{9,13},{13,9},{2,6},{6,2},{1... | collective-permute-start | bytes 196616 | tf_op jit(solution)/shard_map/ppermute | solution.py:644
  17.2 6.3 %collective-permute-start.6 = (bf16[2,128,128]{2,1,0:T(8,128)(2,1)S(1)}, bf16[2,128,128]{2,1,0:T(8,128)(2,1)S(1)}, u32[]{:S(2)}, u32[]{:S(2)}) collective-permute-start(bf16[2,128,128]{2,1,0:T(8,128)(2,1)S(1)} %get-tuple-element.71), channel_id=1, source_target_pairs={{0,4},{4,0},{8,12},{12,8},{1,5},{5,1},{9,13},{13,9},{2,6},{6,2},{1... | collective-permute-start | bytes 196616 | tf_op jit(solution)/shard_map/ppermute | solution.py:644
  23.6 1.8 %collective-permute-start.7 = (bf16[12,128,128]{2,1,0:T(8,128)(2,1)S(1)}, bf16[12,128,128]{2,1,0:T(8,128)(2,1)S(1)}, u32[]{:S(2)}, u32[]{:S(2)}) collective-permute-start(bf16[12,128,128]{2,1,0:T(8,128)(2,1)S(1)} %stack.1.refs_4_), channel_id=1, source_target_pairs={{0,1},{1,0},{2,3},{3,2},{4,5},{5,4},{6,7},{7,6},{8,9},{9,8},{10,11... | collective-permute-start | bytes 1179656 | tf_op jit(solution)/shard_map/ppermute | solution.py:640
  24.1 8.8 %copy-start.2 = (bf16[256,256]{1,0:T(8,128)(2,1)S(1)}, bf16[256,256]{1,0:T(8,128)(2,1)}, u32[]{:S(2)}) copy-start(bf16[256,256]{1,0:T(8,128)(2,1)} %refs_3_.3) | copy-start | bytes 393220
  25.9 1.4 %collective-permute-start.8 = (bf16[4,128,128]{2,1,0:T(8,128)(2,1)S(1)}, bf16[4,128,128]{2,1,0:T(8,128)(2,1)S(1)}, u32[]{:S(2)}, u32[]{:S(2)}) collective-permute-start(bf16[4,128,128]{2,1,0:T(8,128)(2,1)S(1)} %get-tuple-element.90), channel_id=1, source_target_pairs={{0,1},{1,0},{2,3},{3,2},{4,5},{5,4},{6,7},{7,6},{8,9},{9,8},{10,11... | collective-permute-start | bytes 393224 | tf_op jit(solution)/shard_map/ppermute | solution.py:640
  27.3 5.6 %collective-permute-start.9 = (bf16[4,128,128]{2,1,0:T(8,128)(2,1)S(1)}, bf16[4,128,128]{2,1,0:T(8,128)(2,1)S(1)}, u32[]{:S(2)}, u32[]{:S(2)}) collective-permute-start(bf16[4,128,128]{2,1,0:T(8,128)(2,1)S(1)} %add_up.1.refs_0_), channel_id=1, source_target_pairs={{0,2},{2,0},{1,3},{3,1},{4,6},{6,4},{5,7},{7,5},{8,10},{10,8},{9,1... | collective-permute-start | bytes 393224 | tf_op jit(solution)/shard_map/ppermute | solution.py:640
  33.6 1.6 %collective-permute-start.10 = (bf16[128,1024]{1,0:T(8,128)(2,1)S(1)}, bf16[128,1024]{1,0:T(8,128)(2,1)S(1)}, u32[]{:S(2)}, u32[]{:S(2)}) collective-permute-start(bf16[128,1024]{1,0:T(8,128)(2,1)S(1)} %get-tuple-element.93), channel_id=1, source_target_pairs={{0,1},{1,0},{2,3},{3,2},{4,5},{5,4},{6,7},{7,6},{8,9},{9,8},{10,11... | collective-permute-start | bytes 786440 | tf_op jit(solution)/shard_map/ppermute | solution.py:640
  33.7 7.1 %collective-permute-start.11 = (f32[128,256]{1,0:T(8,128)S(1)}, f32[128,256]{1,0:T(8,128)S(1)}, u32[]{:S(2)}, u32[]{:S(2)}) collective-permute-start(f32[128,256]{1,0:T(8,128)S(1)} %get-tuple-element.98.mine_ref), channel_id=1, source_target_pairs={{0,4},{4,0},{8,12},{12,8},{1,5},{5,1},{9,13},{13,9},{2,6},{6,2},{1... | collective-permute-start | bytes 393224 | tf_op jit(solution)/shard_map/ppermute | solution.py:644
  35.6 10.6 %collective-permute-start.13 = (bf16[128,512]{1,0:T(8,128)(2,1)S(1)}, bf16[128,512]{1,0:T(8,128)(2,1)S(1)}, u32[]{:S(2)}, u32[]{:S(2)}) collective-permute-start(bf16[128,512]{1,0:T(8,128)(2,1)S(1)} %get-tuple-element.102), channel_id=1, source_target_pairs={{0,8},{4,12},{8,0},{12,4},{1,9},{5,13},{9,1},{13,5},{2,10},{6,14},... | collective-permute-start | bytes 393224 | tf_op jit(solution)/shard_map/ppermute | solution.py:644
  36.9 9.7 %collective-permute-start.14 = (bf16[128,512]{1,0:T(8,128)(2,1)S(1)}, bf16[128,512]{1,0:T(8,128)(2,1)S(1)}, u32[]{:S(2)}, u32[]{:S(2)}) collective-permute-start(bf16[128,512]{1,0:T(8,128)(2,1)S(1)} %get-tuple-element.103), channel_id=1, source_target_pairs={{0,4},{4,0},{8,12},{12,8},{1,5},{5,1},{9,13},{13,9},{2,6},{6,2},{1... | collective-permute-start | bytes 393224 | tf_op jit(solution)/shard_map/ppermute | solution.py:644
  37.6 14.4 %collective-permute-start.16 = (bf16[128,512]{1,0:T(8,128)(2,1)S(1)}, bf16[128,512]{1,0:T(8,128)(2,1)S(1)}, u32[]{:S(2)}, u32[]{:S(2)}) collective-permute-start(bf16[128,512]{1,0:T(8,128)(2,1)S(1)} %get-tuple-element.107), channel_id=1, source_target_pairs={{0,12},{4,8},{8,4},{12,0},{1,13},{5,9},{9,5},{13,1},{2,14},{6,10},... | collective-permute-start | bytes 393224 | tf_op jit(solution)/shard_map/ppermute | solution.py:644
  40.7 1.3 %collective-permute-start.12 = (bf16[128,128]{1,0:T(8,128)(2,1)S(1)}, bf16[128,128]{1,0:T(8,128)(2,1)S(1)}, u32[]{:S(2)}, u32[]{:S(2)}) collective-permute-start(bf16[128,128]{1,0:T(8,128)(2,1)S(1)} %get-tuple-element.100), channel_id=1, source_target_pairs={{0,1},{1,0},{2,3},{3,2},{4,5},{5,4},{6,7},{7,6},{8,9},{9,8},{10,11... | collective-permute-start | bytes 98312 | tf_op jit(solution)/shard_map/ppermute | solution.py:640
  42.0 9.9 %collective-permute-start.15 = (bf16[128,128]{1,0:T(8,128)(2,1)S(1)}, bf16[128,128]{1,0:T(8,128)(2,1)S(1)}, u32[]{:S(2)}, u32[]{:S(2)}) collective-permute-start(bf16[128,128]{1,0:T(8,128)(2,1)S(1)} %pair_sum.2.mine_ref), channel_id=1, source_target_pairs={{0,8},{4,12},{8,0},{12,4},{1,9},{5,13},{9,1},{13,5},{2,10},{6,14},... | collective-permute-start | bytes 98312 | tf_op jit(solution)/shard_map/ppermute | solution.py:644
  52.3 1.7 %collective-permute-start.17 = (bf16[8,128,128]{2,1,0:T(8,128)(2,1)S(1)}, bf16[8,128,128]{2,1,0:T(8,128)(2,1)S(1)}, u32[]{:S(2)}, u32[]{:S(2)}) collective-permute-start(bf16[8,128,128]{2,1,0:T(8,128)(2,1)S(1)} %late_rows.5.mine_ref), channel_id=1, source_target_pairs={{0,1},{1,0},{2,3},{3,2},{4,5},{5,4},{6,7},{7,6},{8,9},{9,8},{10,11... | collective-permute-start | bytes 786440 | tf_op jit(solution)/shard_map/ppermute | solution.py:640
  52.4 1.6 %collective-permute-start.18 = (f32[128,128]{1,0:T(8,128)S(1)}, f32[128,128]{1,0:T(8,128)S(1)}, u32[]{:S(2)}, u32[]{:S(2)}) collective-permute-start(f32[128,128]{1,0:T(8,128)S(1)} %pair_sum.3.share_ref), channel_id=1, source_target_pairs={{0,1},{1,0},{2,3},{3,2},{4,5},{5,4},{6,7},{7,6},{8,9},{9,8},{10,11... | collective-permute-start | bytes 196616 | tf_op jit(solution)/shard_map/ppermute | solution.py:640

commit v17 on v15

--- a/solution.py
+++ b/solution.py
@@ -322,32 +322,51 @@
     return outs[0], [None] + list(outs[1:])
 
 
-def stack_kernel(*refs):
-    at = 0
+def below_kernel(sums_ref, half_ref, out_ref):
+    top = sums_ref.shape[0]
+    share, columns, width = half_ref.shape
+    out_ref[:top, :] = sums_ref[...]
+    for b in range(share):
+        row, left = top + b // CAP * columns, b % CAP * width
+        out_ref[row : row + columns, left : left + width] = half_ref[b]
+
+
+def below(sums, half):
+    share, columns, width = half.shape
+    out = shape((sums.shape[0] + share // CAP * columns, sums.shape[1]), BF16)
+    return call(below_kernel, "below", out, [vmem(), vmem()])(sums, half)
+
+
+def stack_kernel(count, *refs):
+    share = refs[0].shape[0]
+    for k, ref in enumerate(refs[:count]):
+        refs[-1][k * share : (k + 1) * share] = ref[...]
+
+
+def stack(pieces, sums):
+    share, columns, width = pieces[0].shape
+    out = shape((len(pieces) * share, columns, width), BF16)
+    kernel = functools.partial(stack_kernel, len(pieces))
+    return call(kernel, "stack", out, [vmem()] * (len(pieces) + len(sums)), flops=2 ** 31)(*pieces, *sums)
+
+
+def stack_more_kernel(first_ref, *refs):
+    out_ref = refs[-1]
+    at, columns, width = first_ref.shape
+    out_ref[:at] = first_ref[...]
     for ref in refs[:-1]:
-        share = ref.shape[0]
-        refs[-1][at : at + share] = ref[...]
+        share = (ref.shape[0] - TAIL) // columns * CAP - CAP
+        for b in range(share):
+            row, left = columns + TAIL + b // CAP * columns, b % CAP * width
+            out_ref[at + b] = ref[row : row + columns, left : left + width]
         at += share
 
 
-def halves_kernel(in_ref, low_ref, high_ref):
-    share = low_ref.shape[0]
-    low_ref[...] = in_ref[:share]
-    high_ref[...] = in_ref[share:]
-
-
-def halves(parts):
-    if len(parts) > 1:
-        return parts
-    share, columns, width = parts[0].shape
-    part = shape((share // 2, columns, width), BF16)
-    return list(call(halves_kernel, "halves", [part, part], [vmem()])(*parts))
-
-
-def stack(pieces):
-    _, columns, width = pieces[0].shape
-    out = shape((sum(piece.shape[0] for piece in pieces), columns, width), BF16)
-    return call(stack_kernel, "stack", out, [vmem()] * len(pieces))(*pieces)
+def stack_more(first, chunks):
+    at, columns, width = first.shape
+    share = (chunks[0].shape[0] - TAIL) // columns * CAP - CAP
+    out = shape((at + len(chunks) * share, columns, width), BF16)
+    return call(stack_more_kernel, "stack_more", out, [vmem()] * (1 + len(chunks)))(first, *chunks)
 
 
 def half_rows(before, far_ref, m_ref, first, share):
@@ -462,18 +481,20 @@
     return call(add_kernel, "add_up", shape(came.shape, BF16), [vmem(), vmem()])(keep, came)
 
 
-def widen_kernel(feats, in_ref, out_ref):
-    _, columns, width = in_ref.shape
-    share = out_ref.shape[1] // width
-    for f in range(feats):
+def widen_kernel(feats, *refs):
+    out_ref = refs[feats]
+    share, columns, width = refs[0].shape
+    me = lax.axis_index("feat")
+    for q in range(feats):
+        rows = pl.ds(pl.multiple_of(lax.rem(me + q, feats) * columns, columns), columns)
         for b in range(share):
-            out_ref[f * columns : (f + 1) * columns, b * width : (b + 1) * width] = in_ref[f * share + b]
-
-
-def widen(parts, feats):
-    blocks, columns, width = parts.shape
-    out = shape((feats * columns, blocks // feats * width), BF16)
-    return call(functools.partial(widen_kernel, feats), "widen", out, [vmem()])(parts)
+            out_ref[rows, b * width : (b + 1) * width] = refs[q][b]
+
+
+def widen(parts):
+    share, columns, width = parts[0].shape
+    out = shape((len(parts) * columns, share * width), BF16)
+    return call(functools.partial(widen_kernel, len(parts)), "widen", out, [vmem()] * len(parts))(*parts)
 
 
 def dense_kernel(feats, *refs):
@@ -639,32 +660,29 @@
     half, table = prepare(features, tile_row, tile_col, peers, reps)
     operator, asks = list_operator(tiles, table, tile_count, peers, blocks_dev)
     sends, own_mirror, own_cot = first_sends(features, cotangent, operator, asks[1:], peers, reps)
-    cots = lax.all_gather(own_cot, "feat", axis=0, tiled=True)
-    pieces, held = {0: [half]}, [0]
-    bit = peers // 2
-    while bit:
-        for k in held:
-            parts = pieces[k]
-            if k:
-                parts = after(halves(after(parts, sends[1])), pieces.get(1, half))
-            pieces[k ^ bit] = [across(part, peers, bit) for part in parts]
-        held = held + [k ^ bit for k in held]
-        bit //= 2
+    middle = peers // 2
+    pieces = [across(half, peers, j) for j in range(1, middle)]
+    crossed = across(half, peers, middle)
     came = [None] * peers
     for k in far_first:
-        came[k] = across(sends[k], peers, k)
-    arrived = [part for k in range(1, peers) for part in pieces[k]]
-    middle = peers // 2
-    came[middle:], arrived, cots = lax.optimization_barrier((came[middle:], arrived, cots))
-    came[1:middle], arrived = lax.optimization_barrier((came[1:middle], arrived))
-    stacked = stack(arrived)
+        if k >= middle:
+            came[k] = across(sends[k], peers, k)
+    for j in range(1, middle):
+        chunk, pieces[j - 1] = lax.optimization_barrier((below(sends[j], crossed), pieces[j - 1]))
+        came[j] = across(chunk, peers, j)
+    held = after(own_cot, crossed)
+    cots = [own_cot] + [ahead(held, "feat", feats, feats - q) for q in range(1, feats)]
+    stacked = stack(pieces + [crossed], came[middle:])
+    came[1:middle], stacked = lax.optimization_barrier((came[1:middle], stacked))
+    stacked, cots = lax.optimization_barrier((stacked, cots))
+    stacked = stack_more(stacked, came[1:middle])
     swapped = ahead(stacked, "rep", reps, 1)
     acc, ids = first_rows(features, operator, asks[0], came, own_mirror, peers)
     give, asked = give_rows(acc, asks, stacked, swapped, operator, peers, reps)
     keep = keep_rows(acc, asked, operator, reps)
 
     mine = add_up(keep, ahead(give, "rep", reps, 1))
-    cot = widen(cots, feats)
+    cot = widen(cots)
     sums = [mine] + [ahead(mine, "feat", feats, feats - q) for q in range(1, feats)]
     act, give, spread, term = dense(sums, cot, weight, feats)
     shared = ahead(give, "rep", reps, 1)

time: 55.1 us -> 54.9 us (level)
  waiting for transfers between devices: 17.1 us -> 24.1 us
  blocking collectives: 5.63 us -> 0 us
  starting transfers between devices: 20 us -> 18.3 us
    ppermute x12 -> x10, waiting for transfers between devices: 8.59 us -> 14.3 us  [across(): return lax.ppermute(value, 'graph', [(i, i ^ k) for i in range(peers)])]
    all_gather x1 -> x0, blocking collectives: 5.63 us -> none  [local(): cots = lax.all_gather(own_cot, 'feat', axis=0, tiled=True)]
    ppermute x12 -> x10, starting transfers between devices: 17.5 us -> 14.3 us  [across(): return lax.ppermute(value, 'graph', [(i, i ^ k) for i in range(peers)])]
    ppermute x7 -> x8, starting transfers between devices: 2.54 us -> 4.03 us  [ahead(): return lax.ppermute(value, axis, [(i, (i + k) % size) for i in range(size)])]
    ppermute x7 -> x8, waiting for transfers between devices: 8.48 us -> 9.84 us  [ahead(): return lax.ppermute(value, axis, [(i, (i + k) % size) for i in range(size)])]
  transfers between devices with their start and end apart: 19 -> 18, of which waited for: 9 -> 11; matrix products, arithmetic and copies ran while one was open for 0% -> 0% of each run, Pallas kernels for 12% -> 12%
where the time goes in v17:
time: 54.9 us; the launch traced here: 54.8 us
  waiting for transfers between devices  24.1 us (44%)
  starting transfers between devices  18.3 us (33%)
  Pallas kernels  10.8 us (20%)
  between operations  1.49 us (3%)
    ppermute x10, starting transfers between devices, across(): return lax.ppermute(value, 'graph', [(i, i ^ k) for i in range(peers)])  14.3 us
    ppermute x10, waiting for transfers between devices, across(): return lax.ppermute(value, 'graph', [(i, i ^ k) for i in range(peers)])  14.3 us
    ppermute x8, waiting for transfers between devices, ahead(): return lax.ppermute(value, axis, [(i, (i + k) % size) for i in range(size)])  9.84 us
    ppermute x8, starting transfers between devices, ahead(): return lax.ppermute(value, axis, [(i, (i + k) % size) for i in range(size)])  4.03 us
    pallas_call x1, Pallas kernels, list_operator(): call(functools.partial(operator_kernel, blocks_dev, slots_here, groups),...  2.99 us
    pallas_call x1, Pallas kernels, prepare(): call(functools.partial(prepare_kernel, peers), 'prepare', [shape((blocks_...  1.76 us
  transfers between devices with their start and end apart: 18, of which 11 were waited for; matrix products, arithmetic and copies ran while one was open for 0% of the time, Pallas kernels for 12%

profile of v17, /device:TPU:0, one launch (start us, length us, event | category | flops | bytes accessed | tf_op | source)
XLA Modules:
  0.0 54.8 jit_solution(12150943487028253992)
XLA Ops:
  0.6 1.8 %prepare.1 = (bf16[4,128,128]{2,1,0:T(8,128)(2,1)}, s32[8192,128]{1,0:T(8,128)}) custom-call(s32[1,128]{1,0:T(1,128)} %bitcast.2, s32[1,128]{1,0:T(1,128)} %bitcast.3, bf16[8,128,128]{2,1,0:T(8,128)(2,1)} %refs_4_.3), custom_call_target="tpu_custom_call" | custom-call | bytes 262144 | tf_op jit(solution)/shard_map/prepare/pallas_call | solution.py:102
  2.4 4.1 %collective-permute-start = (bf16[4,128,128]{2,1,0:T(8,128)(2,1)}, bf16[4,128,128]{2,1,0:T(8,128)(2,1)S(1)}, u32[]{:S(2)}, u32[]{:S(2)}) collective-permute-start(bf16[4,128,128]{2,1,0:T(8,128)(2,1)} %get-tuple-element.55), channel_id=1, source_target_pairs={{0,8},{4,12},{8,0},{12,4},{1,9},{5,13},{9,1},{13,5},{2,10},{6,14},... | collective-permute-start | bytes 393224 | tf_op jit(solution)/shard_map/ppermute | solution.py:646
  6.5 1.6 %collective-permute-start.1 = (bf16[4,128,128]{2,1,0:T(8,128)(2,1)}, bf16[4,128,128]{2,1,0:T(8,128)(2,1)S(1)}, u32[]{:S(2)}, u32[]{:S(2)}) collective-permute-start(bf16[4,128,128]{2,1,0:T(8,128)(2,1)} %get-tuple-element.55), channel_id=1, source_target_pairs={{0,4},{4,0},{8,12},{12,8},{1,5},{5,1},{9,13},{13,9},{2,6},{6,2},{1... | collective-permute-start | bytes 393224 | tf_op jit(solution)/shard_map/ppermute | solution.py:646
  8.8 3.0 %operator.1 = (bf16[1024,1024]{1,0:T(8,128)(2,1)S(1)}, s32[1,128]{1,0:T(1,128)S(1)}, s32[1,128]{1,0:T(1,128)S(1)}, s32[1,128]{1,0:T(1,128)S(1)}, s32[1,128]{1,0:T(1,128)S(1)}) custom-call(s32[1]{0:T(128)S(6)} %copy.10.count_ref, s32[8192,128]{1,0:T(8,128)} %get-tuple-element.48.table_in, bf16[128,128,128]{2,1,0:T(8,128)(2,1)} %tiles_ref.1), custom_call_target="tpu_custom_call" | custom-call | bytes 16777216 | tf_op jit(solution)/shard_map/operator/pallas_call | solution.py:192
  12.6 2.5 %collective-permute-start.4 = (bf16[144,256]{1,0:T(8,128)(2,1)S(1)}, bf16[144,256]{1,0:T(8,128)(2,1)S(1)}, u32[]{:S(2)}, u32[]{:S(2)}) collective-permute-start(bf16[144,256]{1,0:T(8,128)(2,1)S(1)} %get-tuple-element.59), channel_id=1, source_target_pairs={{0,12},{4,8},{8,4},{12,0},{1,13},{5,9},{9,5},{13,1},{2,14},{6,10},... | collective-permute-start | bytes 221192 | tf_op jit(solution)/shard_map/ppermute | solution.py:646
  15.2 0.7 %collective-permute-start.2 = (bf16[400,256]{1,0:T(8,128)(2,1)S(1)}, bf16[400,256]{1,0:T(8,128)(2,1)S(1)}, u32[]{:S(2)}, u32[]{:S(2)}) collective-permute-start(bf16[400,256]{1,0:T(8,128)(2,1)S(1)} %below.1), channel_id=1, source_target_pairs={{0,4},{4,0},{8,12},{12,8},{1,5},{5,1},{9,13},{13,9},{2,6},{6,2},{1... | collective-permute-start | bytes 614408 | tf_op jit(solution)/shard_map/ppermute | solution.py:646
  15.9 1.5 %collective-permute-start.5 = (bf16[4,128,128]{2,1,0:T(8,128)(2,1)S(1)}, bf16[4,128,128]{2,1,0:T(8,128)(2,1)S(1)}, u32[]{:S(2)}, u32[]{:S(2)}) collective-permute-start(bf16[4,128,128]{2,1,0:T(8,128)(2,1)S(1)} %get-tuple-element.72.refs_0_), channel_id=1, source_target_pairs={{0,2},{2,0},{1,3},{3,1},{4,6},{6,4},{5,7},{7,5},{8,10},{10,8},{9,1... | collective-permute-start | bytes 393224 | tf_op jit(solution)/shard_map/ppermute | solution.py:642
  17.4 2.6 %collective-permute-done.3.refs_2_ = bf16[144,256]{1,0:T(8,128)(2,1)S(1)} collective-permute-done((bf16[144,256]{1,0:T(8,128)(2,1)S(1)}, bf16[144,256]{1,0:T(8,128)(2,1)S(1)}, u32[]{:S(2)}, u32[]{:S(2)}) %collective-permute-start.3) | collective-permute-done | bytes 73760 | tf_op jit(solution)/shard_map/ppermute | solution.py:646
  20.1 3.3 %collective-permute-done.2.refs_1_.refs_0_ = bf16[400,256]{1,0:T(8,128)(2,1)S(1)} collective-permute-done((bf16[400,256]{1,0:T(8,128)(2,1)S(1)}, bf16[400,256]{1,0:T(8,128)(2,1)S(1)}, u32[]{:S(2)}, u32[]{:S(2)}) %collective-permute-start.2) | collective-permute-done | bytes 204832 | tf_op jit(solution)/shard_map/ppermute | solution.py:646
  23.9 1.3 %collective-permute-done.6.refs_5_ = bf16[12,128,128]{2,1,0:T(8,128)(2,1)S(1)} collective-permute-done((bf16[12,128,128]{2,1,0:T(8,128)(2,1)S(1)}, bf16[12,128,128]{2,1,0:T(8,128)(2,1)S(1)}, u32[]{:S(2)}, u32[]{:S(2)}) %collective-permute-start.6) | collective-permute-done | bytes 393248 | tf_op jit(solution)/shard_map/ppermute | solution.py:642
  26.2 0.8 %collective-permute-done.7.came_ref = bf16[4,128,128]{2,1,0:T(8,128)(2,1)S(1)} collective-permute-done((bf16[4,128,128]{2,1,0:T(8,128)(2,1)S(1)}, bf16[4,128,128]{2,1,0:T(8,128)(2,1)S(1)}, u32[]{:S(2)}, u32[]{:S(2)}) %collective-permute-start.7) | collective-permute-done | bytes 131104 | tf_op jit(solution)/shard_map/ppermute | solution.py:642
  27.1 1.6 %collective-permute-start.8 = (bf16[4,128,128]{2,1,0:T(8,128)(2,1)S(1)}, bf16[4,128,128]{2,1,0:T(8,128)(2,1)S(1)}, u32[]{:S(2)}, u32[]{:S(2)}) collective-permute-start(bf16[4,128,128]{2,1,0:T(8,128)(2,1)S(1)} %add_up.1.refs_0_), channel_id=1, source_target_pairs={{0,2},{2,0},{1,3},{3,1},{4,6},{6,4},{5,7},{7,5},{8,10},{10,8},{9,1... | collective-permute-start | bytes 393224 | tf_op jit(solution)/shard_map/ppermute | solution.py:642
  28.7 4.0 %collective-permute-done.8.refs_1_ = bf16[4,128,128]{2,1,0:T(8,128)(2,1)S(1)} collective-permute-done((bf16[4,128,128]{2,1,0:T(8,128)(2,1)S(1)}, bf16[4,128,128]{2,1,0:T(8,128)(2,1)S(1)}, u32[]{:S(2)}, u32[]{:S(2)}) %collective-permute-start.8) | collective-permute-done | bytes 131104 | tf_op jit(solution)/shard_map/ppermute | solution.py:642
  32.7 0.7 %dense.1 = (bf16[4,128,128]{2,1,0:T(8,128)(2,1)S(1)}, bf16[128,1024]{1,0:T(8,128)(2,1)S(1)}, bf16[4,128,128]{2,1,0:T(8,128)(2,1)S(1)}, f32[128,256]{1,0:T(8,128)S(1)}) custom-call(bf16[4,128,128]{2,1,0:T(8,128)(2,1)S(1)} %add_up.1.refs_0_, bf16[4,128,128]{2,1,0:T(8,128)(2,1)S(1)} %collective-permute-done.8.refs_1_, bf16[256,512]{1,0:T(8,128)(2,1)S(1)} %widen.1.refs_2_, ...), custom_call_target="tpu_custom_call" | custom-call | flops 268435456 | bytes 1048576 | tf_op jit(solution)/shard_map/dense/pallas_call | solution.py:530
  33.5 1.4 %collective-permute-done.9.refs_4_.shared_ref = bf16[128,1024]{1,0:T(8,128)(2,1)S(1)} collective-permute-done((bf16[128,1024]{1,0:T(8,128)(2,1)S(1)}, bf16[128,1024]{1,0:T(8,128)(2,1)S(1)}, u32[]{:S(2)}, u32[]{:S(2)}) %collective-permute-start.9) | collective-permute-done | bytes 262176 | tf_op jit(solution)/shard_map/ppermute | solution.py:642
  35.4 1.5 %collective-permute-start.12 = (bf16[128,512]{1,0:T(8,128)(2,1)S(1)}, bf16[128,512]{1,0:T(8,128)(2,1)S(1)}, u32[]{:S(2)}, u32[]{:S(2)}) collective-permute-start(bf16[128,512]{1,0:T(8,128)(2,1)S(1)} %get-tuple-element.84), channel_id=1, source_target_pairs={{0,8},{4,12},{8,0},{12,4},{1,9},{5,13},{9,1},{13,5},{2,10},{6,14},... | collective-permute-start | bytes 393224 | tf_op jit(solution)/shard_map/ppermute | solution.py:646
  36.9 1.5 %collective-permute-start.13 = (bf16[128,512]{1,0:T(8,128)(2,1)S(1)}, bf16[128,512]{1,0:T(8,128)(2,1)S(1)}, u32[]{:S(2)}, u32[]{:S(2)}) collective-permute-start(bf16[128,512]{1,0:T(8,128)(2,1)S(1)} %get-tuple-element.85), channel_id=1, source_target_pairs={{0,4},{4,0},{8,12},{12,8},{1,5},{5,1},{9,13},{13,9},{2,6},{6,2},{1... | collective-permute-start | bytes 393224 | tf_op jit(solution)/shard_map/ppermute | solution.py:646
  38.4 1.5 %collective-permute-start.15 = (bf16[128,512]{1,0:T(8,128)(2,1)S(1)}, bf16[128,512]{1,0:T(8,128)(2,1)S(1)}, u32[]{:S(2)}, u32[]{:S(2)}) collective-permute-start(bf16[128,512]{1,0:T(8,128)(2,1)S(1)} %get-tuple-element.89), channel_id=1, source_target_pairs={{0,12},{4,8},{8,4},{12,0},{1,13},{5,9},{9,5},{13,1},{2,14},{6,10},... | collective-permute-start | bytes 393224 | tf_op jit(solution)/shard_map/ppermute | solution.py:646
  40.5 1.2 %collective-permute-done.11.came_ref = bf16[128,128]{1,0:T(8,128)(2,1)S(1)} collective-permute-done((bf16[128,128]{1,0:T(8,128)(2,1)S(1)}, bf16[128,128]{1,0:T(8,128)(2,1)S(1)}, u32[]{:S(2)}, u32[]{:S(2)}) %collective-permute-start.11) | collective-permute-done | bytes 32800 | tf_op jit(solution)/shard_map/ppermute | solution.py:642
  42.2 1.0 %late_self.1 = (f32[8,128,128]{2,1,0:T(8,128)S(1)}, bf16[8,128,128]{2,1,0:T(8,128)(2,1)}) custom-call(s32[1,128]{1,0:T(1,128)S(1)} %get-tuple-element.49.refs_0_.ask_ref, bf16[8,128,128]{2,1,0:T(8,128)(2,1)S(1)} %get-tuple-element.76.x3, f32[128,256]{1,0:T(8,128)S(1)} %get-tuple-element.77.self_ref, ...), custom_call_target="tpu_custom_call" | custom-call | flops 67108864 | bytes 262144 | tf_op jit(solution)/shard_map/late_self/pallas_call | solution.py:447
  43.2 2.4 %collective-permute-done.12.came_ref = bf16[128,512]{1,0:T(8,128)(2,1)S(1)} collective-permute-done((bf16[128,512]{1,0:T(8,128)(2,1)S(1)}, bf16[128,512]{1,0:T(8,128)(2,1)S(1)}, u32[]{:S(2)}, u32[]{:S(2)}) %collective-permute-start.12) | collective-permute-done | bytes 131104 | tf_op jit(solution)/shard_map/ppermute | solution.py:646
  46.3 5.5 %collective-permute-done.14.came_ref = bf16[128,128]{1,0:T(8,128)(2,1)S(1)} collective-permute-done((bf16[128,128]{1,0:T(8,128)(2,1)S(1)}, bf16[128,128]{1,0:T(8,128)(2,1)S(1)}, u32[]{:S(2)}, u32[]{:S(2)}) %collective-permute-start.14) | collective-permute-done | bytes 32800 | tf_op jit(solution)/shard_map/ppermute | solution.py:646
  52.7 1.1 %collective-permute-done.17.other_share_ref = f32[128,128]{1,0:T(8,128)S(1)} collective-permute-done((f32[128,128]{1,0:T(8,128)S(1)}, f32[128,128]{1,0:T(8,128)S(1)}, u32[]{:S(2)}, u32[]{:S(2)}) %collective-permute-start.17) | collective-permute-done | bytes 65568 | tf_op jit(solution)/shard_map/ppermute | solution.py:642
  53.9 0.9 %finish.1 = (bf16[8,128,128]{2,1,0:T(8,128)(2,1)}, f32[256,128]{1,0:T(8,128)}) custom-call(bf16[8,128,128]{2,1,0:T(8,128)(2,1)S(1)} %late_rows.5.mine_ref, bf16[8,128,128]{2,1,0:T(8,128)(2,1)S(1)} %collective-permute-done.16.other_ref, f32[128,128]{1,0:T(8,128)S(1)} %pair_sum.3.share_ref, f32[128,128]{1,0:T(8,128)S(1)} %collective-permute-done.17.other_share_ref), custom_call_target="tpu_custom_call" | custom-call | bytes 262144 | tf_op jit(solution)/shard_map/finish/pallas_call | solution.py:633
  (39 shorter events, 6.0 us)
Async XLA Ops:
  2.4 12.7 %collective-permute-start = (bf16[4,128,128]{2,1,0:T(8,128)(2,1)}, bf16[4,128,128]{2,1,0:T(8,128)(2,1)S(1)}, u32[]{:S(2)}, u32[]{:S(2)}) collective-permute-start(bf16[4,128,128]{2,1,0:T(8,128)(2,1)} %get-tuple-element.55), channel_id=1, source_target_pairs={{0,8},{4,12},{8,0},{12,4},{1,9},{5,13},{9,1},{13,5},{2,10},{6,14},... | collective-permute-start | bytes 393224 | tf_op jit(solution)/shard_map/ppermute | solution.py:646
  6.5 8.7 %collective-permute-start.1 = (bf16[4,128,128]{2,1,0:T(8,128)(2,1)}, bf16[4,128,128]{2,1,0:T(8,128)(2,1)S(1)}, u32[]{:S(2)}, u32[]{:S(2)}) collective-permute-start(bf16[4,128,128]{2,1,0:T(8,128)(2,1)} %get-tuple-element.55), channel_id=1, source_target_pairs={{0,4},{4,0},{8,12},{12,8},{1,5},{5,1},{9,13},{13,9},{2,6},{6,2},{1... | collective-permute-start | bytes 393224 | tf_op jit(solution)/shard_map/ppermute | solution.py:646
  8.7 3.0 %copy-start = (bf16[8,128,128]{2,1,0:T(8,128)(2,1)S(1)}, bf16[8,128,128]{2,1,0:T(8,128)(2,1)}, u32[]{:S(2)}) copy-start(bf16[8,128,128]{2,1,0:T(8,128)(2,1)} %refs_4_.3) | copy-start | bytes 786436
  8.7 3.0 %copy-start.1 = (bf16[8,128,128]{2,1,0:T(8,128)(2,1)S(1)}, bf16[8,128,128]{2,1,0:T(8,128)(2,1)}, u32[]{:S(2)}) copy-start(bf16[8,128,128]{2,1,0:T(8,128)(2,1)} %refs_4_.2) | copy-start | bytes 786436
  12.2 7.8 %collective-permute-start.3 = (bf16[144,256]{1,0:T(8,128)(2,1)S(1)}, bf16[144,256]{1,0:T(8,128)(2,1)S(1)}, u32[]{:S(2)}, u32[]{:S(2)}) collective-permute-start(bf16[144,256]{1,0:T(8,128)(2,1)S(1)} %get-tuple-element.58), channel_id=1, source_target_pairs={{0,8},{4,12},{8,0},{12,4},{1,9},{5,13},{9,1},{13,5},{2,10},{6,14},... | collective-permute-start | bytes 221192 | tf_op jit(solution)/shard_map/ppermute | solution.py:646
  12.6 7.4 %collective-permute-start.4 = (bf16[144,256]{1,0:T(8,128)(2,1)S(1)}, bf16[144,256]{1,0:T(8,128)(2,1)S(1)}, u32[]{:S(2)}, u32[]{:S(2)}) collective-permute-start(bf16[144,256]{1,0:T(8,128)(2,1)S(1)} %get-tuple-element.59), channel_id=1, source_target_pairs={{0,12},{4,8},{8,4},{12,0},{1,13},{5,9},{9,5},{13,1},{2,14},{6,10},... | collective-permute-start | bytes 221192 | tf_op jit(solution)/shard_map/ppermute | solution.py:646
  15.2 8.1 %collective-permute-start.2 = (bf16[400,256]{1,0:T(8,128)(2,1)S(1)}, bf16[400,256]{1,0:T(8,128)(2,1)S(1)}, u32[]{:S(2)}, u32[]{:S(2)}) collective-permute-start(bf16[400,256]{1,0:T(8,128)(2,1)S(1)} %below.1), channel_id=1, source_target_pairs={{0,4},{4,0},{8,12},{12,8},{1,5},{5,1},{9,13},{13,9},{2,6},{6,2},{1... | collective-permute-start | bytes 614408 | tf_op jit(solution)/shard_map/ppermute | solution.py:646
  15.9 7.4 %collective-permute-start.5 = (bf16[4,128,128]{2,1,0:T(8,128)(2,1)S(1)}, bf16[4,128,128]{2,1,0:T(8,128)(2,1)S(1)}, u32[]{:S(2)}, u32[]{:S(2)}) collective-permute-start(bf16[4,128,128]{2,1,0:T(8,128)(2,1)S(1)} %get-tuple-element.72.refs_0_), channel_id=1, source_target_pairs={{0,2},{2,0},{1,3},{3,1},{4,6},{6,4},{5,7},{7,5},{8,10},{10,8},{9,1... | collective-permute-start | bytes 393224 | tf_op jit(solution)/shard_map/ppermute | solution.py:642
  23.4 1.8 %collective-permute-start.6 = (bf16[12,128,128]{2,1,0:T(8,128)(2,1)S(1)}, bf16[12,128,128]{2,1,0:T(8,128)(2,1)S(1)}, u32[]{:S(2)}, u32[]{:S(2)}) collective-permute-start(bf16[12,128,128]{2,1,0:T(8,128)(2,1)S(1)} %stack_more.1.refs_4_), channel_id=1, source_target_pairs={{0,1},{1,0},{2,3},{3,2},{4,5},{5,4},{6,7},{7,6},{8,9},{9,8},{10,11... | collective-permute-start | bytes 1179656 | tf_op jit(solution)/shard_map/ppermute | solution.py:642
  23.9 8.8 %copy-start.2 = (bf16[256,256]{1,0:T(8,128)(2,1)S(1)}, bf16[256,256]{1,0:T(8,128)(2,1)}, u32[]{:S(2)}) copy-start(bf16[256,256]{1,0:T(8,128)(2,1)} %refs_3_.3) | copy-start | bytes 393220
  25.6 1.4 %collective-permute-start.7 = (bf16[4,128,128]{2,1,0:T(8,128)(2,1)S(1)}, bf16[4,128,128]{2,1,0:T(8,128)(2,1)S(1)}, u32[]{:S(2)}, u32[]{:S(2)}) collective-permute-start(bf16[4,128,128]{2,1,0:T(8,128)(2,1)S(1)} %get-tuple-element.71), channel_id=1, source_target_pairs={{0,1},{1,0},{2,3},{3,2},{4,5},{5,4},{6,7},{7,6},{8,9},{9,8},{10,11... | collective-permute-start | bytes 393224 | tf_op jit(solution)/shard_map/ppermute | solution.py:642
  27.1 5.6 %collective-permute-start.8 = (bf16[4,128,128]{2,1,0:T(8,128)(2,1)S(1)}, bf16[4,128,128]{2,1,0:T(8,128)(2,1)S(1)}, u32[]{:S(2)}, u32[]{:S(2)}) collective-permute-start(bf16[4,128,128]{2,1,0:T(8,128)(2,1)S(1)} %add_up.1.refs_0_), channel_id=1, source_target_pairs={{0,2},{2,0},{1,3},{3,1},{4,6},{6,4},{5,7},{7,5},{8,10},{10,8},{9,1... | collective-permute-start | bytes 393224 | tf_op jit(solution)/shard_map/ppermute | solution.py:642
  33.3 1.6 %collective-permute-start.9 = (bf16[128,1024]{1,0:T(8,128)(2,1)S(1)}, bf16[128,1024]{1,0:T(8,128)(2,1)S(1)}, u32[]{:S(2)}, u32[]{:S(2)}) collective-permute-start(bf16[128,1024]{1,0:T(8,128)(2,1)S(1)} %get-tuple-element.75), channel_id=1, source_target_pairs={{0,1},{1,0},{2,3},{3,2},{4,5},{5,4},{6,7},{7,6},{8,9},{9,8},{10,11... | collective-permute-start | bytes 786440 | tf_op jit(solution)/shard_map/ppermute | solution.py:642
  33.4 6.9 %collective-permute-start.10 = (f32[128,256]{1,0:T(8,128)S(1)}, f32[128,256]{1,0:T(8,128)S(1)}, u32[]{:S(2)}, u32[]{:S(2)}) collective-permute-start(f32[128,256]{1,0:T(8,128)S(1)} %get-tuple-element.80.mine_ref), channel_id=1, source_target_pairs={{0,4},{4,0},{8,12},{12,8},{1,5},{5,1},{9,13},{13,9},{2,6},{6,2},{1... | collective-permute-start | bytes 393224 | tf_op jit(solution)/shard_map/ppermute | solution.py:646
  35.4 10.1 %collective-permute-start.12 = (bf16[128,512]{1,0:T(8,128)(2,1)S(1)}, bf16[128,512]{1,0:T(8,128)(2,1)S(1)}, u32[]{:S(2)}, u32[]{:S(2)}) collective-permute-start(bf16[128,512]{1,0:T(8,128)(2,1)S(1)} %get-tuple-element.84), channel_id=1, source_target_pairs={{0,8},{4,12},{8,0},{12,4},{1,9},{5,13},{9,1},{13,5},{2,10},{6,14},... | collective-permute-start | bytes 393224 | tf_op jit(solution)/shard_map/ppermute | solution.py:646
  36.9 9.0 %collective-permute-start.13 = (bf16[128,512]{1,0:T(8,128)(2,1)S(1)}, bf16[128,512]{1,0:T(8,128)(2,1)S(1)}, u32[]{:S(2)}, u32[]{:S(2)}) collective-permute-start(bf16[128,512]{1,0:T(8,128)(2,1)S(1)} %get-tuple-element.85), channel_id=1, source_target_pairs={{0,4},{4,0},{8,12},{12,8},{1,5},{5,1},{9,13},{13,9},{2,6},{6,2},{1... | collective-permute-start | bytes 393224 | tf_op jit(solution)/shard_map/ppermute | solution.py:646
  38.4 13.4 %collective-permute-start.15 = (bf16[128,512]{1,0:T(8,128)(2,1)S(1)}, bf16[128,512]{1,0:T(8,128)(2,1)S(1)}, u32[]{:S(2)}, u32[]{:S(2)}) collective-permute-start(bf16[128,512]{1,0:T(8,128)(2,1)S(1)} %get-tuple-element.89), channel_id=1, source_target_pairs={{0,12},{4,8},{8,4},{12,0},{1,13},{5,9},{9,5},{13,1},{2,14},{6,10},... | collective-permute-start | bytes 393224 | tf_op jit(solution)/shard_map/ppermute | solution.py:646
  40.4 1.3 %collective-permute-start.11 = (bf16[128,128]{1,0:T(8,128)(2,1)S(1)}, bf16[128,128]{1,0:T(8,128)(2,1)S(1)}, u32[]{:S(2)}, u32[]{:S(2)}) collective-permute-start(bf16[128,128]{1,0:T(8,128)(2,1)S(1)} %get-tuple-element.82), channel_id=1, source_target_pairs={{0,1},{1,0},{2,3},{3,2},{4,5},{5,4},{6,7},{7,6},{8,9},{9,8},{10,11... | collective-permute-start | bytes 98312 | tf_op jit(solution)/shard_map/ppermute | solution.py:642
  41.7 10.1 %collective-permute-start.14 = (bf16[128,128]{1,0:T(8,128)(2,1)S(1)}, bf16[128,128]{1,0:T(8,128)(2,1)S(1)}, u32[]{:S(2)}, u32[]{:S(2)}) collective-permute-start(bf16[128,128]{1,0:T(8,128)(2,1)S(1)} %pair_sum.2.mine_ref), channel_id=1, source_target_pairs={{0,8},{4,12},{8,0},{12,4},{1,9},{5,13},{9,1},{13,5},{2,10},{6,14},... | collective-permute-start | bytes 98312 | tf_op jit(solution)/shard_map/ppermute | solution.py:646
  52.2 1.7 %collective-permute-start.16 = (bf16[8,128,128]{2,1,0:T(8,128)(2,1)S(1)}, bf16[8,128,128]{2,1,0:T(8,128)(2,1)S(1)}, u32[]{:S(2)}, u32[]{:S(2)}) collective-permute-start(bf16[8,128,128]{2,1,0:T(8,128)(2,1)S(1)} %late_rows.5.mine_ref), channel_id=1, source_target_pairs={{0,1},{1,0},{2,3},{3,2},{4,5},{5,4},{6,7},{7,6},{8,9},{9,8},{10,11... | collective-permute-start | bytes 786440 | tf_op jit(solution)/shard_map/ppermute | solution.py:642
  52.2 1.6 %collective-permute-start.17 = (f32[128,128]{1,0:T(8,128)S(1)}, f32[128,128]{1,0:T(8,128)S(1)}, u32[]{:S(2)}, u32[]{:S(2)}) collective-permute-start(f32[128,128]{1,0:T(8,128)S(1)} %pair_sum.3.share_ref), channel_id=1, source_target_pairs={{0,1},{1,0},{2,3},{3,2},{4,5},{5,4},{6,7},{7,6},{8,9},{9,8},{10,11... | collective-permute-start | bytes 196616 | tf_op jit(solution)/shard_map/ppermute | solution.py:642

commit v18 on v17

--- a/solution.py
+++ b/solution.py
@@ -183,6 +183,12 @@
         for k, ask_ref in enumerate(asks):
             ask_ref[...] = table[PLACE_ROWS + k : PLACE_ROWS + k + 1, :]
 
+    rows = blocks_dev * width
+    for s in range(slots_here):
+        row = PLACE_ROWS + (step * slots_here + s) // CAP
+        block = table[pl.ds(row, 1), s % CAP : s % CAP + 1].astype(F32).astype(BF16)
+        m_ref[rows:, s * width : (s + 1) * width] = jnp.broadcast_to(block, (TAIL, width))
+
 
 def list_operator(tiles, table, tile_count, peers, blocks_dev):
     per, width = tiles.shape[0], tiles.shape[1]
@@ -192,7 +198,7 @@
     outs = call(
         functools.partial(operator_kernel, blocks_dev, slots_here, groups),
         "operator",
-        [shape((blocks_dev * width, slots * width), BF16)] + [shape((1, per), jnp.int32)] * peers,
+        [shape((blocks_dev * width + TAIL, slots * width), BF16)] + [shape((1, per), jnp.int32)] * peers,
         [smem(), hbm(), hbm()],
         [
             pltpu.VMEM((per, width, width), BF16),
@@ -206,21 +212,21 @@
         moved=2 ** 24,
         limit=VMEM_MOST,
         grid=(groups,),
-        out_specs=[pl.BlockSpec((blocks_dev * width, slots_here * width), lambda i: (0, i))] + [vmem()] * peers,
+        out_specs=[pl.BlockSpec((blocks_dev * width + TAIL, slots_here * width), lambda i: (0, i))] + [vmem()] * peers,
     )(tile_count, table, tiles)
     return outs[0], list(outs[1:])
 
 
 def mirrored(near, m_ref, mir, slots, width):
     if slots <= GROUP:
-        mir[...] = dot(near, m_ref[...])
+        mir[...] = dot(near, m_ref[: near.shape[1], :])
     else:
         part = GROUP * width
 
         @pl.loop(0, slots // GROUP)
         def _(i):
             where = pl.ds(pl.multiple_of(i * part, part), part)
-            mir[:, where] = dot(near, m_ref[:, where])
+            mir[:, where] = dot(near, m_ref[: near.shape[1], where])
 
 
 def first_sends_kernel(peers, *refs):
@@ -262,7 +268,7 @@
 
 def own_rows(far, m_ref, k):
     both = far.shape[1]
-    return dot(far, m_ref[:, k * both : (k + 1) * both], NT)
+    return dot(far, m_ref[: m_ref.shape[0] - TAIL, k * both : (k + 1) * both], NT)
 
 
 def put_rows(acc, own, before=None):
@@ -277,15 +283,13 @@
     return own_rows(far, m_ref, 0)
 
 
-def far_of(share, mine_ref, other_ref, ask_ref, at):
+def far_of(share, mine_ref, asked, at):
     first = lax.axis_index("rep") * share
     blocks = []
-    for s in range(CAP):
-        local = pick(ask_ref, s) - first
+    for block in asked:
+        local = block - first
         own = (local >= 0) & (local < share)
-        here = at * share + jnp.where(own, local, 0)
-        there = at * share + jnp.where(own, 0, jnp.where(local < 0, local + share, local - share))
-        blocks.append(jnp.where(own, mine_ref[here], other_ref[there]))
+        blocks.append(jnp.where(own, mine_ref[at * share + jnp.where(own, local, 0)], jnp.bfloat16(0)))
     return jnp.concatenate(blocks, axis=1)
 
 
@@ -347,7 +351,7 @@
     share, columns, width = pieces[0].shape
     out = shape((len(pieces) * share, columns, width), BF16)
     kernel = functools.partial(stack_kernel, len(pieces))
-    return call(kernel, "stack", out, [vmem()] * (len(pieces) + len(sums)), flops=2 ** 31)(*pieces, *sums)
+    return call(kernel, "stack", out, [vmem()] * (len(pieces) + len(sums)), flops=2 ** 36)(*pieces, *sums)
 
 
 def stack_more_kernel(first_ref, *refs):
@@ -369,65 +373,77 @@
     return call(stack_more_kernel, "stack_more", out, [vmem()] * (1 + len(chunks)))(first, *chunks)
 
 
-def half_rows(before, far_ref, m_ref, first, share):
+def half_rows(before, far_refs, m_refs, first, share):
     columns, width = before.shape[1:]
     both = CAP * width
     rows = pl.ds(pl.multiple_of(first * width, share * width), share * width)
-    if m_ref.shape[1] <= GROUP * width:
-        own = dot(far_ref[:, both:], m_ref[rows, both:], NT)
-    else:
-
-        def add_peer(k, total):
-            here = pl.ds(pl.multiple_of(k * both, both), both)
-            return total + dot(far_ref[:, here], m_ref[rows, here], NT)
-
-        zeros = jnp.zeros((columns, share * width), F32)
-        own = lax.fori_loop(1, m_ref.shape[1] // both, add_peer, zeros)
+    slots_wide = m_refs[0].shape[1]
+    own = jnp.zeros((columns, share * width), F32)
+    for far_ref, m_ref in zip(far_refs, m_refs):
+        if slots_wide <= GROUP * width:
+            own = own + dot(far_ref[:, both:], m_ref[rows, both:], NT)
+        else:
+
+            def add_peer(k, total):
+                here = pl.ds(pl.multiple_of(k * both, both), both)
+                return total + dot(far_ref[:, here], m_ref[rows, here], NT)
+
+            own = lax.fori_loop(1, slots_wide // both, add_peer, own)
     return [before[first + b] + own[:, b * width : (b + 1) * width] for b in range(share)]
 
 
 def give_rows_kernel(peers, *refs):
     ask_refs, refs = refs[: peers - 1], refs[peers - 1 :]
-    before, mine_ref, other_ref, m_ref, give_ref, far_ref = refs
-    share = give_ref.shape[0]
-    both = CAP * before.shape[2]
+    before, mine_ref, m_ref, other_m_ref, give_ref, far_ref, other_far_ref = refs
+    share, columns, width = give_ref.shape
+    both = CAP * width
+    tail = m_ref.shape[0] - TAIL
     for k in range(1, peers):
-        far_ref[:, k * both : (k + 1) * both] = far_of(share, mine_ref, other_ref, ask_refs[k - 1], k - 1)
-    far_ref[:, :both] = jnp.zeros((far_ref.shape[0], both), BF16)
-    rows = half_rows(before, far_ref, m_ref, (1 - lax.axis_index("rep")) * share, share)
+        here = slice(k * both, (k + 1) * both)
+        asked = [pick(ask_refs[k - 1], s) for s in range(CAP)]
+        far_ref[:, here] = far_of(share, mine_ref, asked, k - 1)
+        marks = [other_m_ref[tail:, k * both + s * width : k * both + (s + 1) * width] for s in range(CAP)]
+        asked = [jnp.max(mark.astype(F32)).astype(jnp.int32) for mark in marks]
+        other_far_ref[:, here] = far_of(share, mine_ref, asked, k - 1)
+    far_ref[:, :both] = jnp.zeros((columns, both), BF16)
+    other_far_ref[:, :both] = jnp.zeros((columns, both), BF16)
+    first = (1 - lax.axis_index("rep")) * share
+    rows = half_rows(before, [far_ref, other_far_ref], [m_ref, other_m_ref], first, share)
     for b in range(share):
         give_ref[b] = rows[b].astype(BF16)
 
 
-def give_rows(before, asks, mine, other, operator, peers, reps):
+def give_rows(before, asks, mine, operator, other_operator, peers, reps):
     blocks_dev, columns, width = before.shape
+    far = shape((columns, peers * CAP * width), BF16)
     return call(
         functools.partial(give_rows_kernel, peers),
         "give_rows",
-        [shape((blocks_dev // reps, columns, width), BF16), shape((columns, peers * CAP * width), BF16)],
+        [shape((blocks_dev // reps, columns, width), BF16), far, far],
         [vmem()] * (peers + 3),
         flops=2 ** 27,
         moved=2 ** 20,
-    )(*asks[1:], before, mine, other, operator)
-
-
-def keep_rows_kernel(before, far_ref, m_ref, keep_ref):
+    )(*asks[1:], before, mine, operator, other_operator)
+
+
+def keep_rows_kernel(before, far_ref, other_far_ref, m_ref, other_m_ref, keep_ref):
     share = keep_ref.shape[0]
-    rows = half_rows(before, far_ref, m_ref, lax.axis_index("rep") * share, share)
+    first = lax.axis_index("rep") * share
+    rows = half_rows(before, [far_ref, other_far_ref], [m_ref, other_m_ref], first, share)
     for b in range(share):
         keep_ref[b] = rows[b]
 
 
-def keep_rows(before, far, operator, reps):
+def keep_rows(before, far, other_far, operator, other_operator, reps):
     blocks_dev, columns, width = before.shape
     return call(
         keep_rows_kernel,
         "keep_rows",
         shape((blocks_dev // reps, columns, width), F32),
-        [vmem()] * 3,
+        [vmem()] * 5,
         flops=2 ** 27,
         moved=2 ** 20,
-    )(before, far, operator)
+    )(before, far, other_far, operator, other_operator)
 
 
 def late_self_kernel(ask_ref, x3, self_ref, m_ref, act_ref, shared_ref, acc, out_ref):
@@ -481,20 +497,18 @@
     return call(add_kernel, "add_up", shape(came.shape, BF16), [vmem(), vmem()])(keep, came)
 
 
-def widen_kernel(feats, *refs):
-    out_ref = refs[feats]
-    share, columns, width = refs[0].shape
-    me = lax.axis_index("feat")
-    for q in range(feats):
-        rows = pl.ds(pl.multiple_of(lax.rem(me + q, feats) * columns, columns), columns)
+def widen_kernel(feats, in_ref, out_ref):
+    _, columns, width = in_ref.shape
+    share = out_ref.shape[1] // width
+    for f in range(feats):
         for b in range(share):
-            out_ref[rows, b * width : (b + 1) * width] = refs[q][b]
-
-
-def widen(parts):
-    share, columns, width = parts[0].shape
-    out = shape((len(parts) * columns, share * width), BF16)
-    return call(functools.partial(widen_kernel, len(parts)), "widen", out, [vmem()] * len(parts))(*parts)
+            out_ref[f * columns : (f + 1) * columns, b * width : (b + 1) * width] = in_ref[f * share + b]
+
+
+def widen(parts, feats):
+    blocks, columns, width = parts.shape
+    out = shape((feats * columns, blocks // feats * width), BF16)
+    return call(functools.partial(widen_kernel, feats), "widen", out, [vmem()])(parts)
 
 
 def dense_kernel(feats, *refs):
@@ -670,19 +684,17 @@
     for j in range(1, middle):
         chunk, pieces[j - 1] = lax.optimization_barrier((below(sends[j], crossed), pieces[j - 1]))
         came[j] = across(chunk, peers, j)
-    held = after(own_cot, crossed)
-    cots = [own_cot] + [ahead(held, "feat", feats, feats - q) for q in range(1, feats)]
+    cots = lax.all_gather(own_cot, "feat", axis=0, tiled=True)
+    pieces, crossed, cots = lax.optimization_barrier((pieces, crossed, cots))
     stacked = stack(pieces + [crossed], came[middle:])
-    came[1:middle], stacked = lax.optimization_barrier((came[1:middle], stacked))
-    stacked, cots = lax.optimization_barrier((stacked, cots))
     stacked = stack_more(stacked, came[1:middle])
-    swapped = ahead(stacked, "rep", reps, 1)
+    other_operator = ahead(operator, "rep", reps, 1)
     acc, ids = first_rows(features, operator, asks[0], came, own_mirror, peers)
-    give, asked = give_rows(acc, asks, stacked, swapped, operator, peers, reps)
-    keep = keep_rows(acc, asked, operator, reps)
+    give, asked, other_asked = give_rows(acc, asks, stacked, operator, other_operator, peers, reps)
+    keep = keep_rows(acc, asked, other_asked, operator, other_operator, reps)
 
     mine = add_up(keep, ahead(give, "rep", reps, 1))
-    cot = widen(cots)
+    cot = widen(cots, feats)
     sums = [mine] + [ahead(mine, "feat", feats, feats - q) for q in range(1, feats)]
     act, give, spread, term = dense(sums, cot, weight, feats)
     shared = ahead(give, "rep", reps, 1)

time: 54.9 us -> 59.2 us (1.078)
  blocking collectives: 0 us -> 6.57 us
  waiting for transfers between devices: 24.1 us -> 22.6 us
  starting transfers between devices: 18.3 us -> 16.9 us
  Pallas kernels: 10.8 us -> 11.4 us
    all_gather x0 -> x1, blocking collectives: none -> 6.57 us  [local(): cots = lax.all_gather(own_cot, 'feat', axis=0, tiled=True)]
    ppermute x8 -> x7, waiting for transfers between devices: 9.84 us -> 7.78 us  [ahead(): return lax.ppermute(value, axis, [(i, (i + k) % size) for i in range(size)])]
    ppermute x8 -> x7, starting transfers between devices: 4.03 us -> 2.34 us  [ahead(): return lax.ppermute(value, axis, [(i, (i + k) % size) for i in range(size)])]
  transfers between devices with their start and end apart: 18 -> 17, of which waited for: 11 -> 9; matrix products, arithmetic and copies ran while one was open for 0% -> 0% of each run, Pallas kernels for 12% -> 12%
where the time goes in v18:
time: 59.2 us; the launch traced here: 59 us
  waiting for transfers between devices  22.6 us (38%)
  starting transfers between devices  16.9 us (29%)
  Pallas kernels  11.4 us (19%)
  blocking collectives  6.57 us (11%)
  between operations  1.5 us (3%)
    ppermute x10, waiting for transfers between devices, across(): return lax.ppermute(value, 'graph', [(i, i ^ k) for i in range(peers)])  14.8 us
    ppermute x10, starting transfers between devices, across(): return lax.ppermute(value, 'graph', [(i, i ^ k) for i in range(peers)])  14.6 us
    ppermute x7, waiting for transfers between devices, ahead(): return lax.ppermute(value, axis, [(i, (i + k) % size) for i in range(size)])  7.78 us
    all_gather x1, blocking collectives, local(): cots = lax.all_gather(own_cot, 'feat', axis=0, tiled=True)  6.57 us
    pallas_call x1, Pallas kernels, list_operator(): call(functools.partial(operator_kernel, blocks_dev, slots_here, groups),...  3.1 us
    ppermute x7, starting transfers between devices, ahead(): return lax.ppermute(value, axis, [(i, (i + k) % size) for i in range(size)])  2.34 us
    pallas_call x1, Pallas kernels, prepare(): call(functools.partial(prepare_kernel, peers), 'prepare', [shape((blocks_...  1.76 us
  transfers between devices with their start and end apart: 17, of which 9 were waited for; matrix products, arithmetic and copies ran while one was open for 0% of the time, Pallas kernels for 12%

profile of v18, /device:TPU:0, one launch (start us, length us, event | category | flops | bytes accessed | tf_op | source)
XLA Modules:
  0.0 59.0 jit_solution(400834193876909006)
XLA Ops:
  0.6 1.8 %prepare.1 = (bf16[4,128,128]{2,1,0:T(8,128)(2,1)}, s32[8192,128]{1,0:T(8,128)}) custom-call(s32[1,128]{1,0:T(1,128)} %bitcast.2, s32[1,128]{1,0:T(1,128)} %bitcast.3, bf16[8,128,128]{2,1,0:T(8,128)(2,1)} %refs_4_.3), custom_call_target="tpu_custom_call" | custom-call | bytes 262144 | tf_op jit(solution)/shard_map/prepare/pallas_call | solution.py:102
  2.4 4.1 %collective-permute-start = (bf16[4,128,128]{2,1,0:T(8,128)(2,1)}, bf16[4,128,128]{2,1,0:T(8,128)(2,1)S(1)}, u32[]{:S(2)}, u32[]{:S(2)}) collective-permute-start(bf16[4,128,128]{2,1,0:T(8,128)(2,1)} %get-tuple-element.53), channel_id=1, source_target_pairs={{0,8},{4,12},{8,0},{12,4},{1,9},{5,13},{9,1},{13,5},{2,10},{6,14},... | collective-permute-start | bytes 393224 | tf_op jit(solution)/shard_map/ppermute | solution.py:660
  6.5 1.6 %collective-permute-start.1 = (bf16[4,128,128]{2,1,0:T(8,128)(2,1)}, bf16[4,128,128]{2,1,0:T(8,128)(2,1)S(1)}, u32[]{:S(2)}, u32[]{:S(2)}) collective-permute-start(bf16[4,128,128]{2,1,0:T(8,128)(2,1)} %get-tuple-element.53), channel_id=1, source_target_pairs={{0,4},{4,0},{8,12},{12,8},{1,5},{5,1},{9,13},{13,9},{2,6},{6,2},{1... | collective-permute-start | bytes 393224 | tf_op jit(solution)/shard_map/ppermute | solution.py:660
  8.8 3.1 %operator.1 = (bf16[1040,1024]{1,0:T(8,128)(2,1)S(1)}, s32[1,128]{1,0:T(1,128)S(1)}, s32[1,128]{1,0:T(1,128)S(1)}, s32[1,128]{1,0:T(1,128)S(1)}, s32[1,128]{1,0:T(1,128)S(1)}) custom-call(s32[1]{0:T(128)S(6)} %copy.10.count_ref, s32[8192,128]{1,0:T(8,128)} %get-tuple-element.46.table_in, bf16[128,128,128]{2,1,0:T(8,128)(2,1)} %tiles_ref.1), custom_call_target="tpu_custom_call" | custom-call | bytes 16777216 | tf_op jit(solution)/shard_map/operator/pallas_call | solution.py:198
  12.8 2.5 %collective-permute-start.4 = (bf16[144,256]{1,0:T(8,128)(2,1)S(1)}, bf16[144,256]{1,0:T(8,128)(2,1)S(1)}, u32[]{:S(2)}, u32[]{:S(2)}) collective-permute-start(bf16[144,256]{1,0:T(8,128)(2,1)S(1)} %get-tuple-element.56), channel_id=1, source_target_pairs={{0,12},{4,8},{8,4},{12,0},{1,13},{5,9},{9,5},{13,1},{2,14},{6,10},... | collective-permute-start | bytes 221192 | tf_op jit(solution)/shard_map/ppermute | solution.py:660
  15.2 6.6 %all_gather.3.in_ref = bf16[8,128,128]{2,1,0:T(8,128)(2,1)S(1)} all-gather(bf16[4,128,128]{2,1,0:T(8,128)(2,1)S(1)} %get-tuple-element.63), channel_id=1, replica_groups=mesh['parts'=2,'graph'=4,'feat'=2,'rep'=2] {'feat'}, dimensions={0}, use_global_device_ids=true | all-gather | bytes 393216 | tf_op jit(solution)/shard_map/all_gather | solution.py:687
  21.9 0.7 %collective-permute-start.2 = (bf16[400,256]{1,0:T(8,128)(2,1)S(1)}, bf16[400,256]{1,0:T(8,128)(2,1)S(1)}, u32[]{:S(2)}, u32[]{:S(2)}) collective-permute-start(bf16[400,256]{1,0:T(8,128)(2,1)S(1)} %below.1), channel_id=1, source_target_pairs={{0,4},{4,0},{8,12},{12,8},{1,5},{5,1},{9,13},{13,9},{2,6},{6,2},{1... | collective-permute-start | bytes 614408 | tf_op jit(solution)/shard_map/ppermute | solution.py:660
  22.6 6.0 %collective-permute-done.2.refs_1_.refs_0_ = bf16[400,256]{1,0:T(8,128)(2,1)S(1)} collective-permute-done((bf16[400,256]{1,0:T(8,128)(2,1)S(1)}, bf16[400,256]{1,0:T(8,128)(2,1)S(1)}, u32[]{:S(2)}, u32[]{:S(2)}) %collective-permute-start.2) | collective-permute-done | bytes 204832 | tf_op jit(solution)/shard_map/ppermute | solution.py:660
  29.1 0.7 %give_rows.1 = (bf16[4,128,128]{2,1,0:T(8,128)(2,1)S(1)}, bf16[128,1024]{1,0:T(8,128)(2,1)S(1)}, bf16[128,1024]{1,0:T(8,128)(2,1)S(1)}) custom-call(s32[1,128]{1,0:T(1,128)S(1)} %get-tuple-element.48.refs_0_, s32[1,128]{1,0:T(1,128)S(1)} %get-tuple-element.49.refs_1_, s32[1,128]{1,0:T(1,128)S(1)} %get-tuple-element.50.refs_2_, ...), custom_call_target="tpu_custom_call" | custom-call | flops 134217728 | bytes 1048576 | tf_op jit(solution)/shard_map/give_rows/pallas_call | solution.py:419
  29.9 0.7 %keep_rows.1.keep_ref = f32[4,128,128]{2,1,0:T(8,128)S(1)} custom-call(f32[8,128,128]{2,1,0:T(8,128)S(1)} %get-tuple-element.61.refs_3_.before, bf16[128,1024]{1,0:T(8,128)(2,1)S(1)} %get-tuple-element.66.far_ref, bf16[128,1024]{1,0:T(8,128)(2,1)S(1)} %get-tuple-element.67.other_far_ref, bf16[1040,1024]{1,0:T(8,128)(2,1)S(1)} %get-tuple-element.51.refs_5_.m_ref, ...), custom_call_target="tpu_custom_call" | custom-call | flops 134217728 | bytes 1048576 | tf_op jit(solution)/shard_map/keep_rows/pallas_call | solution.py:439
  30.6 0.7 %collective-permute-done.6.came_ref = bf16[4,128,128]{2,1,0:T(8,128)(2,1)S(1)} collective-permute-done((bf16[4,128,128]{2,1,0:T(8,128)(2,1)S(1)}, bf16[4,128,128]{2,1,0:T(8,128)(2,1)S(1)}, u32[]{:S(2)}, u32[]{:S(2)}) %collective-permute-start.6) | collective-permute-done | bytes 131104 | tf_op jit(solution)/shard_map/ppermute | solution.py:656
  31.3 1.6 %collective-permute-start.7 = (bf16[4,128,128]{2,1,0:T(8,128)(2,1)S(1)}, bf16[4,128,128]{2,1,0:T(8,128)(2,1)S(1)}, u32[]{:S(2)}, u32[]{:S(2)}) collective-permute-start(bf16[4,128,128]{2,1,0:T(8,128)(2,1)S(1)} %add_up.1.refs_0_), channel_id=1, source_target_pairs={{0,2},{2,0},{1,3},{3,1},{4,6},{6,4},{5,7},{7,5},{8,10},{10,8},{9,1... | collective-permute-start | bytes 393224 | tf_op jit(solution)/shard_map/ppermute | solution.py:656
  32.9 4.0 %collective-permute-done.7.refs_1_ = bf16[4,128,128]{2,1,0:T(8,128)(2,1)S(1)} collective-permute-done((bf16[4,128,128]{2,1,0:T(8,128)(2,1)S(1)}, bf16[4,128,128]{2,1,0:T(8,128)(2,1)S(1)}, u32[]{:S(2)}, u32[]{:S(2)}) %collective-permute-start.7) | collective-permute-done | bytes 131104 | tf_op jit(solution)/shard_map/ppermute | solution.py:656
  36.9 0.7 %dense.1 = (bf16[4,128,128]{2,1,0:T(8,128)(2,1)S(1)}, bf16[128,1024]{1,0:T(8,128)(2,1)S(1)}, bf16[4,128,128]{2,1,0:T(8,128)(2,1)S(1)}, f32[128,256]{1,0:T(8,128)S(1)}) custom-call(bf16[4,128,128]{2,1,0:T(8,128)(2,1)S(1)} %add_up.1.refs_0_, bf16[4,128,128]{2,1,0:T(8,128)(2,1)S(1)} %collective-permute-done.7.refs_1_, bf16[256,512]{1,0:T(8,128)(2,1)S(1)} %widen.1.refs_2_, ...), custom_call_target="tpu_custom_call" | custom-call | flops 268435456 | bytes 1048576 | tf_op jit(solution)/shard_map/dense/pallas_call | solution.py:544
  37.7 0.7 %collective-permute-start.9 = (f32[128,256]{1,0:T(8,128)S(1)}, f32[128,256]{1,0:T(8,128)S(1)}, u32[]{:S(2)}, u32[]{:S(2)}) collective-permute-start(f32[128,256]{1,0:T(8,128)S(1)} %get-tuple-element.76.mine_ref), channel_id=1, source_target_pairs={{0,4},{4,0},{8,12},{12,8},{1,5},{5,1},{9,13},{13,9},{2,6},{6,2},{1... | collective-permute-start | bytes 393224 | tf_op jit(solution)/shard_map/ppermute | solution.py:660
  38.4 0.8 %collective-permute-done.8.refs_4_.shared_ref = bf16[128,1024]{1,0:T(8,128)(2,1)S(1)} collective-permute-done((bf16[128,1024]{1,0:T(8,128)(2,1)S(1)}, bf16[128,1024]{1,0:T(8,128)(2,1)S(1)}, u32[]{:S(2)}, u32[]{:S(2)}) %collective-permute-start.8) | collective-permute-done | bytes 262176 | tf_op jit(solution)/shard_map/ppermute | solution.py:656
  40.2 1.5 %collective-permute-start.12 = (bf16[128,512]{1,0:T(8,128)(2,1)S(1)}, bf16[128,512]{1,0:T(8,128)(2,1)S(1)}, u32[]{:S(2)}, u32[]{:S(2)}) collective-permute-start(bf16[128,512]{1,0:T(8,128)(2,1)S(1)} %get-tuple-element.81), channel_id=1, source_target_pairs={{0,4},{4,0},{8,12},{12,8},{1,5},{5,1},{9,13},{13,9},{2,6},{6,2},{1... | collective-permute-start | bytes 393224 | tf_op jit(solution)/shard_map/ppermute | solution.py:660
  41.6 2.4 %collective-permute-start.14 = (bf16[128,512]{1,0:T(8,128)(2,1)S(1)}, bf16[128,512]{1,0:T(8,128)(2,1)S(1)}, u32[]{:S(2)}, u32[]{:S(2)}) collective-permute-start(bf16[128,512]{1,0:T(8,128)(2,1)S(1)} %get-tuple-element.85), channel_id=1, source_target_pairs={{0,12},{4,8},{8,4},{12,0},{1,13},{5,9},{9,5},{13,1},{2,14},{6,10},... | collective-permute-start | bytes 393224 | tf_op jit(solution)/shard_map/ppermute | solution.py:660
  44.3 1.2 %collective-permute-done.10.came_ref = bf16[128,128]{1,0:T(8,128)(2,1)S(1)} collective-permute-done((bf16[128,128]{1,0:T(8,128)(2,1)S(1)}, bf16[128,128]{1,0:T(8,128)(2,1)S(1)}, u32[]{:S(2)}, u32[]{:S(2)}) %collective-permute-start.10) | collective-permute-done | bytes 32800 | tf_op jit(solution)/shard_map/ppermute | solution.py:656
  45.6 1.0 %late_self.1 = (f32[8,128,128]{2,1,0:T(8,128)S(1)}, bf16[8,128,128]{2,1,0:T(8,128)(2,1)}) custom-call(s32[1,128]{1,0:T(1,128)S(1)} %get-tuple-element.47.refs_0_.ask_ref, bf16[8,128,128]{2,1,0:T(8,128)(2,1)S(1)} %get-tuple-element.72.x3, f32[128,256]{1,0:T(8,128)S(1)} %get-tuple-element.73.self_ref, bf16[1040,1024]{1,0:T(8,128)(2,1)S(1)} %get-tuple-element.51.refs_5_.m_ref, ...), custom_call_target="tpu_custom_call" | custom-call | flops 67108864 | bytes 262144 | tf_op jit(solution)/shard_map/late_self/pallas_call | solution.py:463
  46.6 3.4 %collective-permute-done.11.came_ref = bf16[128,512]{1,0:T(8,128)(2,1)S(1)} collective-permute-done((bf16[128,512]{1,0:T(8,128)(2,1)S(1)}, bf16[128,512]{1,0:T(8,128)(2,1)S(1)}, u32[]{:S(2)}, u32[]{:S(2)}) %collective-permute-start.11) | collective-permute-done | bytes 131104 | tf_op jit(solution)/shard_map/ppermute | solution.py:660
  50.8 5.3 %collective-permute-done.13.came_ref = bf16[128,128]{1,0:T(8,128)(2,1)S(1)} collective-permute-done((bf16[128,128]{1,0:T(8,128)(2,1)S(1)}, bf16[128,128]{1,0:T(8,128)(2,1)S(1)}, u32[]{:S(2)}, u32[]{:S(2)}) %collective-permute-start.13) | collective-permute-done | bytes 32800 | tf_op jit(solution)/shard_map/ppermute | solution.py:660
  57.0 1.1 %collective-permute-done.16.other_share_ref = f32[128,128]{1,0:T(8,128)S(1)} collective-permute-done((f32[128,128]{1,0:T(8,128)S(1)}, f32[128,128]{1,0:T(8,128)S(1)}, u32[]{:S(2)}, u32[]{:S(2)}) %collective-permute-start.16) | collective-permute-done | bytes 65568 | tf_op jit(solution)/shard_map/ppermute | solution.py:656
  58.1 0.9 %finish.1 = (bf16[8,128,128]{2,1,0:T(8,128)(2,1)}, f32[256,128]{1,0:T(8,128)}) custom-call(bf16[8,128,128]{2,1,0:T(8,128)(2,1)S(1)} %late_rows.5.mine_ref, bf16[8,128,128]{2,1,0:T(8,128)(2,1)S(1)} %collective-permute-done.15.other_ref, f32[128,128]{1,0:T(8,128)S(1)} %pair_sum.3.share_ref, f32[128,128]{1,0:T(8,128)S(1)} %collective-permute-done.16.other_share_ref), custom_call_target="tpu_custom_call" | custom-call | bytes 262144 | tf_op jit(solution)/shard_map/finish/pallas_call | solution.py:647
  (38 shorter events, 4.6 us)
Async XLA Ops:
  2.4 19.4 %collective-permute-start = (bf16[4,128,128]{2,1,0:T(8,128)(2,1)}, bf16[4,128,128]{2,1,0:T(8,128)(2,1)S(1)}, u32[]{:S(2)}, u32[]{:S(2)}) collective-permute-start(bf16[4,128,128]{2,1,0:T(8,128)(2,1)} %get-tuple-element.53), channel_id=1, source_target_pairs={{0,8},{4,12},{8,0},{12,4},{1,9},{5,13},{9,1},{13,5},{2,10},{6,14},... | collective-permute-start | bytes 393224 | tf_op jit(solution)/shard_map/ppermute | solution.py:660
  6.5 15.3 %collective-permute-start.1 = (bf16[4,128,128]{2,1,0:T(8,128)(2,1)}, bf16[4,128,128]{2,1,0:T(8,128)(2,1)S(1)}, u32[]{:S(2)}, u32[]{:S(2)}) collective-permute-start(bf16[4,128,128]{2,1,0:T(8,128)(2,1)} %get-tuple-element.53), channel_id=1, source_target_pairs={{0,4},{4,0},{8,12},{12,8},{1,5},{5,1},{9,13},{13,9},{2,6},{6,2},{1... | collective-permute-start | bytes 393224 | tf_op jit(solution)/shard_map/ppermute | solution.py:660
  8.7 3.1 %copy-start = (bf16[8,128,128]{2,1,0:T(8,128)(2,1)S(1)}, bf16[8,128,128]{2,1,0:T(8,128)(2,1)}, u32[]{:S(2)}) copy-start(bf16[8,128,128]{2,1,0:T(8,128)(2,1)} %refs_4_.3) | copy-start | bytes 786436
  8.7 3.1 %copy-start.1 = (bf16[8,128,128]{2,1,0:T(8,128)(2,1)S(1)}, bf16[8,128,128]{2,1,0:T(8,128)(2,1)}, u32[]{:S(2)}) copy-start(bf16[8,128,128]{2,1,0:T(8,128)(2,1)} %refs_4_.2) | copy-start | bytes 786436
  12.3 10.2 %collective-permute-start.3 = (bf16[144,256]{1,0:T(8,128)(2,1)S(1)}, bf16[144,256]{1,0:T(8,128)(2,1)S(1)}, u32[]{:S(2)}, u32[]{:S(2)}) collective-permute-start(bf16[144,256]{1,0:T(8,128)(2,1)S(1)} %get-tuple-element.55), channel_id=1, source_target_pairs={{0,8},{4,12},{8,0},{12,4},{1,9},{5,13},{9,1},{13,5},{2,10},{6,14},... | collective-permute-start | bytes 221192 | tf_op jit(solution)/shard_map/ppermute | solution.py:660
  12.8 9.8 %collective-permute-start.4 = (bf16[144,256]{1,0:T(8,128)(2,1)S(1)}, bf16[144,256]{1,0:T(8,128)(2,1)S(1)}, u32[]{:S(2)}, u32[]{:S(2)}) collective-permute-start(bf16[144,256]{1,0:T(8,128)(2,1)S(1)} %get-tuple-element.56), channel_id=1, source_target_pairs={{0,12},{4,8},{8,4},{12,0},{1,13},{5,9},{9,5},{13,1},{2,14},{6,10},... | collective-permute-start | bytes 221192 | tf_op jit(solution)/shard_map/ppermute | solution.py:660
  15.2 13.9 %collective-permute-start.5 = (bf16[1040,1024]{1,0:T(8,128)(2,1)S(1)}, bf16[1040,1024]{1,0:T(8,128)(2,1)S(1)}, u32[]{:S(2)}, u32[]{:S(2)}) collective-permute-start(bf16[1040,1024]{1,0:T(8,128)(2,1)S(1)} %get-tuple-element.51.refs_5_.m_ref), channel_id=1, source_target_pairs={{0,1},{1,0},{2,3},{3,2},{4,5},{5,4},{6,7},{7,6},{8,9},{9,8},{10,11... | collective-permute-start | bytes 6389768 | tf_op jit(solution)/shard_map/ppermute | solution.py:656
  21.9 6.8 %collective-permute-start.2 = (bf16[400,256]{1,0:T(8,128)(2,1)S(1)}, bf16[400,256]{1,0:T(8,128)(2,1)S(1)}, u32[]{:S(2)}, u32[]{:S(2)}) collective-permute-start(bf16[400,256]{1,0:T(8,128)(2,1)S(1)} %below.1), channel_id=1, source_target_pairs={{0,4},{4,0},{8,12},{12,8},{1,5},{5,1},{9,13},{13,9},{2,6},{6,2},{1... | collective-permute-start | bytes 614408 | tf_op jit(solution)/shard_map/ppermute | solution.py:660
  29.8 7.1 %copy-start.2 = (bf16[256,256]{1,0:T(8,128)(2,1)S(1)}, bf16[256,256]{1,0:T(8,128)(2,1)}, u32[]{:S(2)}) copy-start(bf16[256,256]{1,0:T(8,128)(2,1)} %refs_3_.3) | copy-start | bytes 393220
  29.9 1.4 %collective-permute-start.6 = (bf16[4,128,128]{2,1,0:T(8,128)(2,1)S(1)}, bf16[4,128,128]{2,1,0:T(8,128)(2,1)S(1)}, u32[]{:S(2)}, u32[]{:S(2)}) collective-permute-start(bf16[4,128,128]{2,1,0:T(8,128)(2,1)S(1)} %get-tuple-element.68), channel_id=1, source_target_pairs={{0,1},{1,0},{2,3},{3,2},{4,5},{5,4},{6,7},{7,6},{8,9},{9,8},{10,11... | collective-permute-start | bytes 393224 | tf_op jit(solution)/shard_map/ppermute | solution.py:656
  31.3 5.6 %collective-permute-start.7 = (bf16[4,128,128]{2,1,0:T(8,128)(2,1)S(1)}, bf16[4,128,128]{2,1,0:T(8,128)(2,1)S(1)}, u32[]{:S(2)}, u32[]{:S(2)}) collective-permute-start(bf16[4,128,128]{2,1,0:T(8,128)(2,1)S(1)} %add_up.1.refs_0_), channel_id=1, source_target_pairs={{0,2},{2,0},{1,3},{3,1},{4,6},{6,4},{5,7},{7,5},{8,10},{10,8},{9,1... | collective-permute-start | bytes 393224 | tf_op jit(solution)/shard_map/ppermute | solution.py:656
  37.6 1.6 %collective-permute-start.8 = (bf16[128,1024]{1,0:T(8,128)(2,1)S(1)}, bf16[128,1024]{1,0:T(8,128)(2,1)S(1)}, u32[]{:S(2)}, u32[]{:S(2)}) collective-permute-start(bf16[128,1024]{1,0:T(8,128)(2,1)S(1)} %get-tuple-element.71), channel_id=1, source_target_pairs={{0,1},{1,0},{2,3},{3,2},{4,5},{5,4},{6,7},{7,6},{8,9},{9,8},{10,11... | collective-permute-start | bytes 786440 | tf_op jit(solution)/shard_map/ppermute | solution.py:656
  37.7 6.6 %collective-permute-start.9 = (f32[128,256]{1,0:T(8,128)S(1)}, f32[128,256]{1,0:T(8,128)S(1)}, u32[]{:S(2)}, u32[]{:S(2)}) collective-permute-start(f32[128,256]{1,0:T(8,128)S(1)} %get-tuple-element.76.mine_ref), channel_id=1, source_target_pairs={{0,4},{4,0},{8,12},{12,8},{1,5},{5,1},{9,13},{13,9},{2,6},{6,2},{1... | collective-permute-start | bytes 393224 | tf_op jit(solution)/shard_map/ppermute | solution.py:660
  39.6 10.4 %collective-permute-start.11 = (bf16[128,512]{1,0:T(8,128)(2,1)S(1)}, bf16[128,512]{1,0:T(8,128)(2,1)S(1)}, u32[]{:S(2)}, u32[]{:S(2)}) collective-permute-start(bf16[128,512]{1,0:T(8,128)(2,1)S(1)} %get-tuple-element.80), channel_id=1, source_target_pairs={{0,8},{4,12},{8,0},{12,4},{1,9},{5,13},{9,1},{13,5},{2,10},{6,14},... | collective-permute-start | bytes 393224 | tf_op jit(solution)/shard_map/ppermute | solution.py:660
  40.2 10.2 %collective-permute-start.12 = (bf16[128,512]{1,0:T(8,128)(2,1)S(1)}, bf16[128,512]{1,0:T(8,128)(2,1)S(1)}, u32[]{:S(2)}, u32[]{:S(2)}) collective-permute-start(bf16[128,512]{1,0:T(8,128)(2,1)S(1)} %get-tuple-element.81), channel_id=1, source_target_pairs={{0,4},{4,0},{8,12},{12,8},{1,5},{5,1},{9,13},{13,9},{2,6},{6,2},{1... | collective-permute-start | bytes 393224 | tf_op jit(solution)/shard_map/ppermute | solution.py:660
  41.6 14.4 %collective-permute-start.14 = (bf16[128,512]{1,0:T(8,128)(2,1)S(1)}, bf16[128,512]{1,0:T(8,128)(2,1)S(1)}, u32[]{:S(2)}, u32[]{:S(2)}) collective-permute-start(bf16[128,512]{1,0:T(8,128)(2,1)S(1)} %get-tuple-element.85), channel_id=1, source_target_pairs={{0,12},{4,8},{8,4},{12,0},{1,13},{5,9},{9,5},{13,1},{2,14},{6,10},... | collective-permute-start | bytes 393224 | tf_op jit(solution)/shard_map/ppermute | solution.py:660
  44.3 1.3 %collective-permute-start.10 = (bf16[128,128]{1,0:T(8,128)(2,1)S(1)}, bf16[128,128]{1,0:T(8,128)(2,1)S(1)}, u32[]{:S(2)}, u32[]{:S(2)}) collective-permute-start(bf16[128,128]{1,0:T(8,128)(2,1)S(1)} %get-tuple-element.78), channel_id=1, source_target_pairs={{0,1},{1,0},{2,3},{3,2},{4,5},{5,4},{6,7},{7,6},{8,9},{9,8},{10,11... | collective-permute-start | bytes 98312 | tf_op jit(solution)/shard_map/ppermute | solution.py:656
  45.5 10.5 %collective-permute-start.13 = (bf16[128,128]{1,0:T(8,128)(2,1)S(1)}, bf16[128,128]{1,0:T(8,128)(2,1)S(1)}, u32[]{:S(2)}, u32[]{:S(2)}) collective-permute-start(bf16[128,128]{1,0:T(8,128)(2,1)S(1)} %pair_sum.2.mine_ref), channel_id=1, source_target_pairs={{0,8},{4,12},{8,0},{12,4},{1,9},{5,13},{9,1},{13,5},{2,10},{6,14},... | collective-permute-start | bytes 98312 | tf_op jit(solution)/shard_map/ppermute | solution.py:660
  56.4 1.7 %collective-permute-start.15 = (bf16[8,128,128]{2,1,0:T(8,128)(2,1)S(1)}, bf16[8,128,128]{2,1,0:T(8,128)(2,1)S(1)}, u32[]{:S(2)}, u32[]{:S(2)}) collective-permute-start(bf16[8,128,128]{2,1,0:T(8,128)(2,1)S(1)} %late_rows.5.mine_ref), channel_id=1, source_target_pairs={{0,1},{1,0},{2,3},{3,2},{4,5},{5,4},{6,7},{7,6},{8,9},{9,8},{10,11... | collective-permute-start | bytes 786440 | tf_op jit(solution)/shard_map/ppermute | solution.py:656
  56.5 1.6 %collective-permute-start.16 = (f32[128,128]{1,0:T(8,128)S(1)}, f32[128,128]{1,0:T(8,128)S(1)}, u32[]{:S(2)}, u32[]{:S(2)}) collective-permute-start(f32[128,128]{1,0:T(8,128)S(1)} %pair_sum.3.share_ref), channel_id=1, source_target_pairs={{0,1},{1,0},{2,3},{3,2},{4,5},{5,4},{6,7},{7,6},{8,9},{9,8},{10,11... | collective-permute-start | bytes 196616 | tf_op jit(solution)/shard_map/ppermute | solution.py:656

commit v19 on v17

--- a/solution.py
+++ b/solution.py
@@ -672,8 +672,8 @@
         came[j] = across(chunk, peers, j)
     held = after(own_cot, crossed)
     cots = [own_cot] + [ahead(held, "feat", feats, feats - q) for q in range(1, feats)]
-    stacked = stack(pieces + [crossed], came[middle:])
-    came[1:middle], stacked = lax.optimization_barrier((came[1:middle], stacked))
+    stacked = stack(pieces + [crossed], came[middle:-1])
+    came[1:middle], came[-1], stacked = lax.optimization_barrier((came[1:middle], came[-1], stacked))
     stacked, cots = lax.optimization_barrier((stacked, cots))
     stacked = stack_more(stacked, came[1:middle])
     swapped = ahead(stacked, "rep", reps, 1)

time: 54.9 us -> 55.1 us (level)
  transfers between devices with their start and end apart: 18 -> 18, of which waited for: 11 -> 13; matrix products, arithmetic and copies ran while one was open for 0% -> 0% of each run, Pallas kernels for 12% -> 12%
where the time goes in v19:
time: 55.1 us; the launch traced here: 55 us
  waiting for transfers between devices  23.9 us (43%)
  starting transfers between devices  18.8 us (34%)
  Pallas kernels  10.8 us (20%)
  between operations  1.48 us (3%)
    ppermute x10, starting transfers between devices, across(): return lax.ppermute(value, 'graph', [(i, i ^ k) for i in range(peers)])  14.8 us
    ppermute x10, waiting for transfers between devices, across(): return lax.ppermute(value, 'graph', [(i, i ^ k) for i in range(peers)])  14.1 us
    ppermute x8, waiting for transfers between devices, ahead(): return lax.ppermute(value, axis, [(i, (i + k) % size) for i in range(size)])  9.85 us
    ppermute x8, starting transfers between devices, ahead(): return lax.ppermute(value, axis, [(i, (i + k) % size) for i in range(size)])  4.04 us
    pallas_call x1, Pallas kernels, list_operator(): call(functools.partial(operator_kernel, blocks_dev, slots_here, groups),...  3 us
    pallas_call x1, Pallas kernels, prepare(): call(functools.partial(prepare_kernel, peers), 'prepare', [shape((blocks_...  1.76 us
  transfers between devices with their start and end apart: 18, of which 13 were waited for; matrix products, arithmetic and copies ran while one was open for 0% of the time, Pallas kernels for 12%

profile of v19, /device:TPU:0, one launch (start us, length us, event | category | flops | bytes accessed | tf_op | source)
XLA Modules:
  0.0 55.0 jit_solution(10280603622168703279)
XLA Ops:
  0.6 1.8 %prepare.1 = (bf16[4,128,128]{2,1,0:T(8,128)(2,1)}, s32[8192,128]{1,0:T(8,128)}) custom-call(s32[1,128]{1,0:T(1,128)} %bitcast.2, s32[1,128]{1,0:T(1,128)} %bitcast.3, bf16[8,128,128]{2,1,0:T(8,128)(2,1)} %refs_4_.3), custom_call_target="tpu_custom_call" | custom-call | bytes 262144 | tf_op jit(solution)/shard_map/prepare/pallas_call | solution.py:102
  2.4 4.1 %collective-permute-start = (bf16[4,128,128]{2,1,0:T(8,128)(2,1)}, bf16[4,128,128]{2,1,0:T(8,128)(2,1)S(1)}, u32[]{:S(2)}, u32[]{:S(2)}) collective-permute-start(bf16[4,128,128]{2,1,0:T(8,128)(2,1)} %get-tuple-element.56), channel_id=1, source_target_pairs={{0,8},{4,12},{8,0},{12,4},{1,9},{5,13},{9,1},{13,5},{2,10},{6,14},... | collective-permute-start | bytes 393224 | tf_op jit(solution)/shard_map/ppermute | solution.py:646
  6.5 1.6 %collective-permute-start.1 = (bf16[4,128,128]{2,1,0:T(8,128)(2,1)}, bf16[4,128,128]{2,1,0:T(8,128)(2,1)S(1)}, u32[]{:S(2)}, u32[]{:S(2)}) collective-permute-start(bf16[4,128,128]{2,1,0:T(8,128)(2,1)} %get-tuple-element.56), channel_id=1, source_target_pairs={{0,4},{4,0},{8,12},{12,8},{1,5},{5,1},{9,13},{13,9},{2,6},{6,2},{1... | collective-permute-start | bytes 393224 | tf_op jit(solution)/shard_map/ppermute | solution.py:646
  8.8 3.0 %operator.1 = (bf16[1024,1024]{1,0:T(8,128)(2,1)S(1)}, s32[1,128]{1,0:T(1,128)S(1)}, s32[1,128]{1,0:T(1,128)S(1)}, s32[1,128]{1,0:T(1,128)S(1)}, s32[1,128]{1,0:T(1,128)S(1)}) custom-call(s32[1]{0:T(128)S(6)} %copy.10.count_ref, s32[8192,128]{1,0:T(8,128)} %get-tuple-element.49.table_in, bf16[128,128,128]{2,1,0:T(8,128)(2,1)} %tiles_ref.1), custom_call_target="tpu_custom_call" | custom-call | bytes 16777216 | tf_op jit(solution)/shard_map/operator/pallas_call | solution.py:192
  13.3 1.6 %collective-permute-start.2 = (bf16[400,256]{1,0:T(8,128)(2,1)S(1)}, bf16[400,256]{1,0:T(8,128)(2,1)S(1)}, u32[]{:S(2)}, u32[]{:S(2)}) collective-permute-start(bf16[400,256]{1,0:T(8,128)(2,1)S(1)} %below.1), channel_id=1, source_target_pairs={{0,4},{4,0},{8,12},{12,8},{1,5},{5,1},{9,13},{13,9},{2,6},{6,2},{1... | collective-permute-start | bytes 614408 | tf_op jit(solution)/shard_map/ppermute | solution.py:646
  14.9 2.1 %collective-permute-start.3 = (bf16[144,256]{1,0:T(8,128)(2,1)S(1)}, bf16[144,256]{1,0:T(8,128)(2,1)S(1)}, u32[]{:S(2)}, u32[]{:S(2)}) collective-permute-start(bf16[144,256]{1,0:T(8,128)(2,1)S(1)} %get-tuple-element.58), channel_id=1, source_target_pairs={{0,12},{4,8},{8,4},{12,0},{1,13},{5,9},{9,5},{13,1},{2,14},{6,10},... | collective-permute-start | bytes 221192 | tf_op jit(solution)/shard_map/ppermute | solution.py:646
  17.0 1.5 %collective-permute-start.5 = (bf16[4,128,128]{2,1,0:T(8,128)(2,1)S(1)}, bf16[4,128,128]{2,1,0:T(8,128)(2,1)S(1)}, u32[]{:S(2)}, u32[]{:S(2)}) collective-permute-start(bf16[4,128,128]{2,1,0:T(8,128)(2,1)S(1)} %get-tuple-element.74.refs_0_), channel_id=1, source_target_pairs={{0,2},{2,0},{1,3},{3,1},{4,6},{6,4},{5,7},{7,5},{8,10},{10,8},{9,1... | collective-permute-start | bytes 393224 | tf_op jit(solution)/shard_map/ppermute | solution.py:642
  18.7 4.9 %collective-permute-done.3.refs_3_ = bf16[144,256]{1,0:T(8,128)(2,1)S(1)} collective-permute-done((bf16[144,256]{1,0:T(8,128)(2,1)S(1)}, bf16[144,256]{1,0:T(8,128)(2,1)S(1)}, u32[]{:S(2)}, u32[]{:S(2)}) %collective-permute-start.3) | collective-permute-done | bytes 73760 | tf_op jit(solution)/shard_map/ppermute | solution.py:646
  24.1 1.3 %collective-permute-done.6.refs_5_ = bf16[12,128,128]{2,1,0:T(8,128)(2,1)S(1)} collective-permute-done((bf16[12,128,128]{2,1,0:T(8,128)(2,1)S(1)}, bf16[12,128,128]{2,1,0:T(8,128)(2,1)S(1)}, u32[]{:S(2)}, u32[]{:S(2)}) %collective-permute-start.6) | collective-permute-done | bytes 393248 | tf_op jit(solution)/shard_map/ppermute | solution.py:642
  26.5 0.8 %collective-permute-done.7.came_ref = bf16[4,128,128]{2,1,0:T(8,128)(2,1)S(1)} collective-permute-done((bf16[4,128,128]{2,1,0:T(8,128)(2,1)S(1)}, bf16[4,128,128]{2,1,0:T(8,128)(2,1)S(1)}, u32[]{:S(2)}, u32[]{:S(2)}) %collective-permute-start.7) | collective-permute-done | bytes 131104 | tf_op jit(solution)/shard_map/ppermute | solution.py:642
  27.3 1.6 %collective-permute-start.8 = (bf16[4,128,128]{2,1,0:T(8,128)(2,1)S(1)}, bf16[4,128,128]{2,1,0:T(8,128)(2,1)S(1)}, u32[]{:S(2)}, u32[]{:S(2)}) collective-permute-start(bf16[4,128,128]{2,1,0:T(8,128)(2,1)S(1)} %add_up.1.refs_0_), channel_id=1, source_target_pairs={{0,2},{2,0},{1,3},{3,1},{4,6},{6,4},{5,7},{7,5},{8,10},{10,8},{9,1... | collective-permute-start | bytes 393224 | tf_op jit(solution)/shard_map/ppermute | solution.py:642
  28.9 4.0 %collective-permute-done.8.refs_1_ = bf16[4,128,128]{2,1,0:T(8,128)(2,1)S(1)} collective-permute-done((bf16[4,128,128]{2,1,0:T(8,128)(2,1)S(1)}, bf16[4,128,128]{2,1,0:T(8,128)(2,1)S(1)}, u32[]{:S(2)}, u32[]{:S(2)}) %collective-permute-start.8) | collective-permute-done | bytes 131104 | tf_op jit(solution)/shard_map/ppermute | solution.py:642
  32.9 0.7 %dense.1 = (bf16[4,128,128]{2,1,0:T(8,128)(2,1)S(1)}, bf16[128,1024]{1,0:T(8,128)(2,1)S(1)}, bf16[4,128,128]{2,1,0:T(8,128)(2,1)S(1)}, f32[128,256]{1,0:T(8,128)S(1)}) custom-call(bf16[4,128,128]{2,1,0:T(8,128)(2,1)S(1)} %add_up.1.refs_0_, bf16[4,128,128]{2,1,0:T(8,128)(2,1)S(1)} %collective-permute-done.8.refs_1_, bf16[256,512]{1,0:T(8,128)(2,1)S(1)} %widen.1.refs_2_, ...), custom_call_target="tpu_custom_call" | custom-call | flops 268435456 | bytes 1048576 | tf_op jit(solution)/shard_map/dense/pallas_call | solution.py:530
  33.7 1.4 %collective-permute-done.9.refs_4_.shared_ref = bf16[128,1024]{1,0:T(8,128)(2,1)S(1)} collective-permute-done((bf16[128,1024]{1,0:T(8,128)(2,1)S(1)}, bf16[128,1024]{1,0:T(8,128)(2,1)S(1)}, u32[]{:S(2)}, u32[]{:S(2)}) %collective-permute-start.9) | collective-permute-done | bytes 262176 | tf_op jit(solution)/shard_map/ppermute | solution.py:642
  35.6 1.3 %collective-permute-start.12 = (bf16[128,512]{1,0:T(8,128)(2,1)S(1)}, bf16[128,512]{1,0:T(8,128)(2,1)S(1)}, u32[]{:S(2)}, u32[]{:S(2)}) collective-permute-start(bf16[128,512]{1,0:T(8,128)(2,1)S(1)} %get-tuple-element.86), channel_id=1, source_target_pairs={{0,8},{4,12},{8,0},{12,4},{1,9},{5,13},{9,1},{13,5},{2,10},{6,14},... | collective-permute-start | bytes 393224 | tf_op jit(solution)/shard_map/ppermute | solution.py:646
  36.9 1.5 %collective-permute-start.13 = (bf16[128,512]{1,0:T(8,128)(2,1)S(1)}, bf16[128,512]{1,0:T(8,128)(2,1)S(1)}, u32[]{:S(2)}, u32[]{:S(2)}) collective-permute-start(bf16[128,512]{1,0:T(8,128)(2,1)S(1)} %get-tuple-element.87), channel_id=1, source_target_pairs={{0,4},{4,0},{8,12},{12,8},{1,5},{5,1},{9,13},{13,9},{2,6},{6,2},{1... | collective-permute-start | bytes 393224 | tf_op jit(solution)/shard_map/ppermute | solution.py:646
  38.4 1.7 %collective-permute-start.15 = (bf16[128,512]{1,0:T(8,128)(2,1)S(1)}, bf16[128,512]{1,0:T(8,128)(2,1)S(1)}, u32[]{:S(2)}, u32[]{:S(2)}) collective-permute-start(bf16[128,512]{1,0:T(8,128)(2,1)S(1)} %get-tuple-element.91), channel_id=1, source_target_pairs={{0,12},{4,8},{8,4},{12,0},{1,13},{5,9},{9,5},{13,1},{2,14},{6,10},... | collective-permute-start | bytes 393224 | tf_op jit(solution)/shard_map/ppermute | solution.py:646
  40.5 1.2 %collective-permute-done.11.came_ref = bf16[128,128]{1,0:T(8,128)(2,1)S(1)} collective-permute-done((bf16[128,128]{1,0:T(8,128)(2,1)S(1)}, bf16[128,128]{1,0:T(8,128)(2,1)S(1)}, u32[]{:S(2)}, u32[]{:S(2)}) %collective-permute-start.11) | collective-permute-done | bytes 32800 | tf_op jit(solution)/shard_map/ppermute | solution.py:642
  42.2 1.0 %late_self.1 = (f32[8,128,128]{2,1,0:T(8,128)S(1)}, bf16[8,128,128]{2,1,0:T(8,128)(2,1)}) custom-call(s32[1,128]{1,0:T(1,128)S(1)} %get-tuple-element.50.refs_0_.ask_ref, bf16[8,128,128]{2,1,0:T(8,128)(2,1)S(1)} %get-tuple-element.78.x3, f32[128,256]{1,0:T(8,128)S(1)} %get-tuple-element.79.self_ref, ...), custom_call_target="tpu_custom_call" | custom-call | flops 67108864 | bytes 262144 | tf_op jit(solution)/shard_map/late_self/pallas_call | solution.py:447
  43.2 2.6 %collective-permute-done.12.came_ref = bf16[128,512]{1,0:T(8,128)(2,1)S(1)} collective-permute-done((bf16[128,512]{1,0:T(8,128)(2,1)S(1)}, bf16[128,512]{1,0:T(8,128)(2,1)S(1)}, u32[]{:S(2)}, u32[]{:S(2)}) %collective-permute-start.12) | collective-permute-done | bytes 131104 | tf_op jit(solution)/shard_map/ppermute | solution.py:646
  46.5 5.5 %collective-permute-done.14.came_ref = bf16[128,128]{1,0:T(8,128)(2,1)S(1)} collective-permute-done((bf16[128,128]{1,0:T(8,128)(2,1)S(1)}, bf16[128,128]{1,0:T(8,128)(2,1)S(1)}, u32[]{:S(2)}, u32[]{:S(2)}) %collective-permute-start.14) | collective-permute-done | bytes 32800 | tf_op jit(solution)/shard_map/ppermute | solution.py:646
  52.5 0.5 collective-permute-start.17
  53.0 1.1 %collective-permute-done.17.other_share_ref = f32[128,128]{1,0:T(8,128)S(1)} collective-permute-done((f32[128,128]{1,0:T(8,128)S(1)}, f32[128,128]{1,0:T(8,128)S(1)}, u32[]{:S(2)}, u32[]{:S(2)}) %collective-permute-start.17) | collective-permute-done | bytes 65568 | tf_op jit(solution)/shard_map/ppermute | solution.py:642
  54.1 0.9 %finish.1 = (bf16[8,128,128]{2,1,0:T(8,128)(2,1)}, f32[256,128]{1,0:T(8,128)}) custom-call(bf16[8,128,128]{2,1,0:T(8,128)(2,1)S(1)} %late_rows.5.mine_ref, bf16[8,128,128]{2,1,0:T(8,128)(2,1)S(1)} %collective-permute-done.16.other_ref, f32[128,128]{1,0:T(8,128)S(1)} %pair_sum.3.share_ref, f32[128,128]{1,0:T(8,128)S(1)} %collective-permute-done.17.other_share_ref), custom_call_target="tpu_custom_call" | custom-call | bytes 262144 | tf_op jit(solution)/shard_map/finish/pallas_call | solution.py:633
  (39 shorter events, 6.0 us)
Async XLA Ops:
  2.4 10.7 %collective-permute-start = (bf16[4,128,128]{2,1,0:T(8,128)(2,1)}, bf16[4,128,128]{2,1,0:T(8,128)(2,1)S(1)}, u32[]{:S(2)}, u32[]{:S(2)}) collective-permute-start(bf16[4,128,128]{2,1,0:T(8,128)(2,1)} %get-tuple-element.56), channel_id=1, source_target_pairs={{0,8},{4,12},{8,0},{12,4},{1,9},{5,13},{9,1},{13,5},{2,10},{6,14},... | collective-permute-start | bytes 393224 | tf_op jit(solution)/shard_map/ppermute | solution.py:646
  6.5 6.8 %collective-permute-start.1 = (bf16[4,128,128]{2,1,0:T(8,128)(2,1)}, bf16[4,128,128]{2,1,0:T(8,128)(2,1)S(1)}, u32[]{:S(2)}, u32[]{:S(2)}) collective-permute-start(bf16[4,128,128]{2,1,0:T(8,128)(2,1)} %get-tuple-element.56), channel_id=1, source_target_pairs={{0,4},{4,0},{8,12},{12,8},{1,5},{5,1},{9,13},{13,9},{2,6},{6,2},{1... | collective-permute-start | bytes 393224 | tf_op jit(solution)/shard_map/ppermute | solution.py:646
  8.7 3.0 %copy-start = (bf16[8,128,128]{2,1,0:T(8,128)(2,1)S(1)}, bf16[8,128,128]{2,1,0:T(8,128)(2,1)}, u32[]{:S(2)}) copy-start(bf16[8,128,128]{2,1,0:T(8,128)(2,1)} %refs_4_.3) | copy-start | bytes 786436
  8.7 3.0 %copy-start.1 = (bf16[8,128,128]{2,1,0:T(8,128)(2,1)S(1)}, bf16[8,128,128]{2,1,0:T(8,128)(2,1)}, u32[]{:S(2)}) copy-start(bf16[8,128,128]{2,1,0:T(8,128)(2,1)} %refs_4_.2) | copy-start | bytes 786436
  12.2 6.4 %collective-permute-start.4 = (bf16[144,256]{1,0:T(8,128)(2,1)S(1)}, bf16[144,256]{1,0:T(8,128)(2,1)S(1)}, u32[]{:S(2)}, u32[]{:S(2)}) collective-permute-start(bf16[144,256]{1,0:T(8,128)(2,1)S(1)} %get-tuple-element.60), channel_id=1, source_target_pairs={{0,8},{4,12},{8,0},{12,4},{1,9},{5,13},{9,1},{13,5},{2,10},{6,14},... | collective-permute-start | bytes 221192 | tf_op jit(solution)/shard_map/ppermute | solution.py:646
  13.3 10.2 %collective-permute-start.2 = (bf16[400,256]{1,0:T(8,128)(2,1)S(1)}, bf16[400,256]{1,0:T(8,128)(2,1)S(1)}, u32[]{:S(2)}, u32[]{:S(2)}) collective-permute-start(bf16[400,256]{1,0:T(8,128)(2,1)S(1)} %below.1), channel_id=1, source_target_pairs={{0,4},{4,0},{8,12},{12,8},{1,5},{5,1},{9,13},{13,9},{2,6},{6,2},{1... | collective-permute-start | bytes 614408 | tf_op jit(solution)/shard_map/ppermute | solution.py:646
  14.9 8.6 %collective-permute-start.3 = (bf16[144,256]{1,0:T(8,128)(2,1)S(1)}, bf16[144,256]{1,0:T(8,128)(2,1)S(1)}, u32[]{:S(2)}, u32[]{:S(2)}) collective-permute-start(bf16[144,256]{1,0:T(8,128)(2,1)S(1)} %get-tuple-element.58), channel_id=1, source_target_pairs={{0,12},{4,8},{8,4},{12,0},{1,13},{5,9},{9,5},{13,1},{2,14},{6,10},... | collective-permute-start | bytes 221192 | tf_op jit(solution)/shard_map/ppermute | solution.py:646
  17.0 6.6 %collective-permute-start.5 = (bf16[4,128,128]{2,1,0:T(8,128)(2,1)S(1)}, bf16[4,128,128]{2,1,0:T(8,128)(2,1)S(1)}, u32[]{:S(2)}, u32[]{:S(2)}) collective-permute-start(bf16[4,128,128]{2,1,0:T(8,128)(2,1)S(1)} %get-tuple-element.74.refs_0_), channel_id=1, source_target_pairs={{0,2},{2,0},{1,3},{3,1},{4,6},{6,4},{5,7},{7,5},{8,10},{10,8},{9,1... | collective-permute-start | bytes 393224 | tf_op jit(solution)/shard_map/ppermute | solution.py:642
  23.6 1.8 %collective-permute-start.6 = (bf16[12,128,128]{2,1,0:T(8,128)(2,1)S(1)}, bf16[12,128,128]{2,1,0:T(8,128)(2,1)S(1)}, u32[]{:S(2)}, u32[]{:S(2)}) collective-permute-start(bf16[12,128,128]{2,1,0:T(8,128)(2,1)S(1)} %stack_more.1.refs_4_), channel_id=1, source_target_pairs={{0,1},{1,0},{2,3},{3,2},{4,5},{5,4},{6,7},{7,6},{8,9},{9,8},{10,11... | collective-permute-start | bytes 1179656 | tf_op jit(solution)/shard_map/ppermute | solution.py:642
  24.1 8.8 %copy-start.2 = (bf16[256,256]{1,0:T(8,128)(2,1)S(1)}, bf16[256,256]{1,0:T(8,128)(2,1)}, u32[]{:S(2)}) copy-start(bf16[256,256]{1,0:T(8,128)(2,1)} %refs_3_.3) | copy-start | bytes 393220
  25.9 1.4 %collective-permute-start.7 = (bf16[4,128,128]{2,1,0:T(8,128)(2,1)S(1)}, bf16[4,128,128]{2,1,0:T(8,128)(2,1)S(1)}, u32[]{:S(2)}, u32[]{:S(2)}) collective-permute-start(bf16[4,128,128]{2,1,0:T(8,128)(2,1)S(1)} %get-tuple-element.73), channel_id=1, source_target_pairs={{0,1},{1,0},{2,3},{3,2},{4,5},{5,4},{6,7},{7,6},{8,9},{9,8},{10,11... | collective-permute-start | bytes 393224 | tf_op jit(solution)/shard_map/ppermute | solution.py:642
  27.3 5.6 %collective-permute-start.8 = (bf16[4,128,128]{2,1,0:T(8,128)(2,1)S(1)}, bf16[4,128,128]{2,1,0:T(8,128)(2,1)S(1)}, u32[]{:S(2)}, u32[]{:S(2)}) collective-permute-start(bf16[4,128,128]{2,1,0:T(8,128)(2,1)S(1)} %add_up.1.refs_0_), channel_id=1, source_target_pairs={{0,2},{2,0},{1,3},{3,1},{4,6},{6,4},{5,7},{7,5},{8,10},{10,8},{9,1... | collective-permute-start | bytes 393224 | tf_op jit(solution)/shard_map/ppermute | solution.py:642
  33.6 1.6 %collective-permute-start.9 = (bf16[128,1024]{1,0:T(8,128)(2,1)S(1)}, bf16[128,1024]{1,0:T(8,128)(2,1)S(1)}, u32[]{:S(2)}, u32[]{:S(2)}) collective-permute-start(bf16[128,1024]{1,0:T(8,128)(2,1)S(1)} %get-tuple-element.77), channel_id=1, source_target_pairs={{0,1},{1,0},{2,3},{3,2},{4,5},{5,4},{6,7},{7,6},{8,9},{9,8},{10,11... | collective-permute-start | bytes 786440 | tf_op jit(solution)/shard_map/ppermute | solution.py:642
  33.7 6.7 %collective-permute-start.10 = (f32[128,256]{1,0:T(8,128)S(1)}, f32[128,256]{1,0:T(8,128)S(1)}, u32[]{:S(2)}, u32[]{:S(2)}) collective-permute-start(f32[128,256]{1,0:T(8,128)S(1)} %get-tuple-element.82.mine_ref), channel_id=1, source_target_pairs={{0,4},{4,0},{8,12},{12,8},{1,5},{5,1},{9,13},{13,9},{2,6},{6,2},{1... | collective-permute-start | bytes 393224 | tf_op jit(solution)/shard_map/ppermute | solution.py:646
  35.6 10.1 %collective-permute-start.12 = (bf16[128,512]{1,0:T(8,128)(2,1)S(1)}, bf16[128,512]{1,0:T(8,128)(2,1)S(1)}, u32[]{:S(2)}, u32[]{:S(2)}) collective-permute-start(bf16[128,512]{1,0:T(8,128)(2,1)S(1)} %get-tuple-element.86), channel_id=1, source_target_pairs={{0,8},{4,12},{8,0},{12,4},{1,9},{5,13},{9,1},{13,5},{2,10},{6,14},... | collective-permute-start | bytes 393224 | tf_op jit(solution)/shard_map/ppermute | solution.py:646
  36.9 9.2 %collective-permute-start.13 = (bf16[128,512]{1,0:T(8,128)(2,1)S(1)}, bf16[128,512]{1,0:T(8,128)(2,1)S(1)}, u32[]{:S(2)}, u32[]{:S(2)}) collective-permute-start(bf16[128,512]{1,0:T(8,128)(2,1)S(1)} %get-tuple-element.87), channel_id=1, source_target_pairs={{0,4},{4,0},{8,12},{12,8},{1,5},{5,1},{9,13},{13,9},{2,6},{6,2},{1... | collective-permute-start | bytes 393224 | tf_op jit(solution)/shard_map/ppermute | solution.py:646
  38.4 13.6 %collective-permute-start.15 = (bf16[128,512]{1,0:T(8,128)(2,1)S(1)}, bf16[128,512]{1,0:T(8,128)(2,1)S(1)}, u32[]{:S(2)}, u32[]{:S(2)}) collective-permute-start(bf16[128,512]{1,0:T(8,128)(2,1)S(1)} %get-tuple-element.91), channel_id=1, source_target_pairs={{0,12},{4,8},{8,4},{12,0},{1,13},{5,9},{9,5},{13,1},{2,14},{6,10},... | collective-permute-start | bytes 393224 | tf_op jit(solution)/shard_map/ppermute | solution.py:646
  40.4 1.3 %collective-permute-start.11 = (bf16[128,128]{1,0:T(8,128)(2,1)S(1)}, bf16[128,128]{1,0:T(8,128)(2,1)S(1)}, u32[]{:S(2)}, u32[]{:S(2)}) collective-permute-start(bf16[128,128]{1,0:T(8,128)(2,1)S(1)} %get-tuple-element.84), channel_id=1, source_target_pairs={{0,1},{1,0},{2,3},{3,2},{4,5},{5,4},{6,7},{7,6},{8,9},{9,8},{10,11... | collective-permute-start | bytes 98312 | tf_op jit(solution)/shard_map/ppermute | solution.py:642
  41.7 10.3 %collective-permute-start.14 = (bf16[128,128]{1,0:T(8,128)(2,1)S(1)}, bf16[128,128]{1,0:T(8,128)(2,1)S(1)}, u32[]{:S(2)}, u32[]{:S(2)}) collective-permute-start(bf16[128,128]{1,0:T(8,128)(2,1)S(1)} %pair_sum.2.mine_ref), channel_id=1, source_target_pairs={{0,8},{4,12},{8,0},{12,4},{1,9},{5,13},{9,1},{13,5},{2,10},{6,14},... | collective-permute-start | bytes 98312 | tf_op jit(solution)/shard_map/ppermute | solution.py:646
  52.4 1.7 %collective-permute-start.16 = (bf16[8,128,128]{2,1,0:T(8,128)(2,1)S(1)}, bf16[8,128,128]{2,1,0:T(8,128)(2,1)S(1)}, u32[]{:S(2)}, u32[]{:S(2)}) collective-permute-start(bf16[8,128,128]{2,1,0:T(8,128)(2,1)S(1)} %late_rows.5.mine_ref), channel_id=1, source_target_pairs={{0,1},{1,0},{2,3},{3,2},{4,5},{5,4},{6,7},{7,6},{8,9},{9,8},{10,11... | collective-permute-start | bytes 786440 | tf_op jit(solution)/shard_map/ppermute | solution.py:642
  52.5 1.6 %collective-permute-start.17 = (f32[128,128]{1,0:T(8,128)S(1)}, f32[128,128]{1,0:T(8,128)S(1)}, u32[]{:S(2)}, u32[]{:S(2)}) collective-permute-start(f32[128,128]{1,0:T(8,128)S(1)} %pair_sum.3.share_ref), channel_id=1, source_target_pairs={{0,1},{1,0},{2,3},{3,2},{4,5},{5,4},{6,7},{7,6},{8,9},{9,8},{10,11... | collective-permute-start | bytes 196616 | tf_op jit(solution)/shard_map/ppermute | solution.py:642

commit v20 on v19

--- a/solution.py
+++ b/solution.py
@@ -469,7 +469,7 @@
         shape(before.shape, dtype),
         [vmem()] * 4,
         [pltpu.VMEM(before.shape, F32)],
-        flops=2 ** 26,
+        flops=2 ** 29,
     )(before, ids, came, operator)
 
 
@@ -512,7 +512,7 @@
     factor = wide_cot[...].astype(F32) * sig * (1.0 + pre * (1.0 - sig))
     grad[...] = factor.astype(BF16)
     spread = dot(w_ref[rows[0], :], grad[...]).astype(BF16)
-    term_ref[...] = dot(grad[rows[0], :], wide[...], NT)
+    term_ref[...] = dot(grad[rows[0], :], wide[...], NT).astype(BF16)
     wide_share = share * width
     give_ref[:, :wide_share] = spread
     for b in range(share):
@@ -534,7 +534,7 @@
             shape((share, columns, width), BF16),
             shape((columns, 2 * share * width), BF16),
             shape((share, columns, width), BF16),
-            shape((columns, features), F32),
+            shape((columns, features), BF16),
         ],
         [vmem()] * (feats + 2),
         [
@@ -586,12 +586,24 @@
     return outs[0], [None] + list(outs[1:peers]), outs[peers]
 
 
-def pair_kernel(mine_ref, came_ref, out_ref):
-    out_ref[...] = (mine_ref[...].astype(F32) + came_ref[...].astype(F32)).astype(out_ref.dtype)
-
-
-def pair_sum(mine, came, dtype):
-    return call(pair_kernel, "pair_sum", shape(mine.shape, dtype), [vmem(), vmem()])(mine, came)
+def pair_kernel(at, mine_ref, came_ref, out_ref):
+    out_ref[...] = (mine_ref[...].astype(F32) + came_ref[:, at:].astype(F32)).astype(out_ref.dtype)
+
+
+def pair_sum(mine, came, dtype, at=0):
+    kernel = functools.partial(pair_kernel, at)
+    return call(kernel, "pair_sum", shape(mine.shape, dtype), [vmem(), vmem()])(mine, came)
+
+
+def beside_kernel(chunk_ref, term_ref, out_ref):
+    width = chunk_ref.shape[1]
+    out_ref[:, :width] = chunk_ref[...]
+    out_ref[:, width:] = term_ref[...]
+
+
+def beside(chunk, term):
+    out = shape((chunk.shape[0], chunk.shape[1] + term.shape[1]), BF16)
+    return call(beside_kernel, "beside", out, [vmem(), vmem()])(chunk, term)
 
 
 def split_kernel(mine_ref, came_ref, give_ref, keep_ref, total):
@@ -614,9 +626,13 @@
     )(mine, came)
 
 
-def pair_term(term, peers, reps):
+def half_term(term, peers, reps):
     give, total = split_sum(term, across(term, peers, 1), reps)
-    total = pair_sum(total, ahead(give, "rep", reps, 1), F32 if peers == 2 else BF16)
+    total = pair_sum(total, ahead(give, "rep", reps, 1), BF16)
+    bit = 2
+    while 2 * bit < peers:
+        total = pair_sum(total, across(total, peers, bit), BF16)
+        bit *= 2
     return total
 
 
@@ -686,25 +702,17 @@
     sums = [mine] + [ahead(mine, "feat", feats, feats - q) for q in range(1, feats)]
     act, give, spread, term = dense(sums, cot, weight, feats)
     shared = ahead(give, "rep", reps, 1)
-    total = pair_term(term, peers, reps)
+    term = half_term(term, peers, reps)
     values, sends, own_mirror = sends_of(spread, shared, operator, ids, peers, reps)
 
-    came = [None] * peers
-    for k in far_first:
-        came[k] = across(sends[k], peers, k)
+    *firsts, last = sorted(range(1, peers), key=lambda k: (k == peers - 1, -(k & middle), k))
+    sends[last] = beside(sends[last], term)
+    came = [None] + [across(sends[k], peers, k) for k in range(1, peers)]
     acc, activated = late_self(asks[0], values, own_mirror, operator, act, shared)
-    *firsts, last = sorted(range(1, peers), key=lambda k: (k == peers - 1, -(k & middle), k))
     for k in firsts:
         acc = late_rows(acc, ids[k], came[k], operator, k, F32)
-    bit = 2
-    while bit < peers:
-        other = across(total, peers, bit)
-        if 2 * bit == peers:
-            total, acc = lax.optimization_barrier((total, acc))
-        total = pair_sum(total, other, F32 if 2 * bit == peers else BF16)
-        bit *= 2
-    acc, total = lax.optimization_barrier((acc, total))
     part = late_rows(acc, ids[last], came[last], operator, last, BF16)
+    total = pair_sum(term, came[last], F32, 2 * CAP * width)
     input_grad, weight_grad = finish(
         part, ahead(part, "rep", reps, 1), total, ahead(total, "rep", reps, 1)
     )

time: 55.1 us -> 53.8 us (0.976)
  starting transfers between devices: 18.8 us -> 17.8 us
    ppermute x10 -> x9, starting transfers between devices: 14.8 us -> 13.7 us  [across(): return lax.ppermute(value, 'graph', [(i, i ^ k) for i in range(peers)])]
    ppermute x10 -> x9, waiting for transfers between devices: 14.1 us -> 14.1 us  [across(): return lax.ppermute(value, 'graph', [(i, i ^ k) for i in range(peers)])]
  transfers between devices with their start and end apart: 18 -> 17, of which waited for: 13 -> 13; matrix products, arithmetic and copies ran while one was open for 0% -> 0% of each run, Pallas kernels for 12% -> 12%
where the time goes in v20:
time: 53.8 us; the launch traced here: 53.7 us
  waiting for transfers between devices  23.6 us (44%)
  starting transfers between devices  17.8 us (33%)
  Pallas kernels  10.8 us (20%)
  between operations  1.49 us (3%)
    ppermute x9, waiting for transfers between devices, across(): return lax.ppermute(value, 'graph', [(i, i ^ k) for i in range(peers)])  14.1 us
    ppermute x9, starting transfers between devices, across(): return lax.ppermute(value, 'graph', [(i, i ^ k) for i in range(peers)])  13.7 us
    ppermute x8, waiting for transfers between devices, ahead(): return lax.ppermute(value, axis, [(i, (i + k) % size) for i in range(size)])  9.43 us
    ppermute x8, starting transfers between devices, ahead(): return lax.ppermute(value, axis, [(i, (i + k) % size) for i in range(size)])  4.09 us
    pallas_call x1, Pallas kernels, list_operator(): call(functools.partial(operator_kernel, blocks_dev, slots_here, groups),...  2.99 us
    pallas_call x1, Pallas kernels, prepare(): call(functools.partial(prepare_kernel, peers), 'prepare', [shape((blocks_...  1.76 us
    pallas_call x3, Pallas kernels, late_rows(): call(functools.partial(late_rows_kernel, k), 'late_rows', shape(before.sh...  1.09 us
  transfers between devices with their start and end apart: 17, of which 13 were waited for; matrix products, arithmetic and copies ran while one was open for 0% of the time, Pallas kernels for 12%

profile of v20, /device:TPU:0, one launch (start us, length us, event | category | flops | bytes accessed | tf_op | source)
XLA Modules:
  0.0 53.7 jit_solution(1546702575390852300)
XLA Ops:
  0.6 1.8 %prepare.1 = (bf16[4,128,128]{2,1,0:T(8,128)(2,1)}, s32[8192,128]{1,0:T(8,128)}) custom-call(s32[1,128]{1,0:T(1,128)} %bitcast.2, s32[1,128]{1,0:T(1,128)} %bitcast.3, bf16[8,128,128]{2,1,0:T(8,128)(2,1)} %refs_4_.3), custom_call_target="tpu_custom_call" | custom-call | bytes 262144 | tf_op jit(solution)/shard_map/prepare/pallas_call | solution.py:102
  2.4 4.1 %collective-permute-start = (bf16[4,128,128]{2,1,0:T(8,128)(2,1)}, bf16[4,128,128]{2,1,0:T(8,128)(2,1)S(1)}, u32[]{:S(2)}, u32[]{:S(2)}) collective-permute-start(bf16[4,128,128]{2,1,0:T(8,128)(2,1)} %get-tuple-element.52), channel_id=1, source_target_pairs={{0,8},{4,12},{8,0},{12,4},{1,9},{5,13},{9,1},{13,5},{2,10},{6,14},... | collective-permute-start | bytes 393224 | tf_op jit(solution)/shard_map/ppermute | solution.py:662
  6.5 1.6 %collective-permute-start.1 = (bf16[4,128,128]{2,1,0:T(8,128)(2,1)}, bf16[4,128,128]{2,1,0:T(8,128)(2,1)S(1)}, u32[]{:S(2)}, u32[]{:S(2)}) collective-permute-start(bf16[4,128,128]{2,1,0:T(8,128)(2,1)} %get-tuple-element.52), channel_id=1, source_target_pairs={{0,4},{4,0},{8,12},{12,8},{1,5},{5,1},{9,13},{13,9},{2,6},{6,2},{1... | collective-permute-start | bytes 393224 | tf_op jit(solution)/shard_map/ppermute | solution.py:662
  8.8 3.0 %operator.1 = (bf16[1024,1024]{1,0:T(8,128)(2,1)S(1)}, s32[1,128]{1,0:T(1,128)S(1)}, s32[1,128]{1,0:T(1,128)S(1)}, s32[1,128]{1,0:T(1,128)S(1)}, s32[1,128]{1,0:T(1,128)S(1)}) custom-call(s32[1]{0:T(128)S(6)} %copy.10.count_ref, s32[8192,128]{1,0:T(8,128)} %get-tuple-element.45.table_in, bf16[128,128,128]{2,1,0:T(8,128)(2,1)} %tiles_ref.1), custom_call_target="tpu_custom_call" | custom-call | bytes 16777216 | tf_op jit(solution)/shard_map/operator/pallas_call | solution.py:192
  13.3 1.6 %collective-permute-start.2 = (bf16[400,256]{1,0:T(8,128)(2,1)S(1)}, bf16[400,256]{1,0:T(8,128)(2,1)S(1)}, u32[]{:S(2)}, u32[]{:S(2)}) collective-permute-start(bf16[400,256]{1,0:T(8,128)(2,1)S(1)} %below.1), channel_id=1, source_target_pairs={{0,4},{4,0},{8,12},{12,8},{1,5},{5,1},{9,13},{13,9},{2,6},{6,2},{1... | collective-permute-start | bytes 614408 | tf_op jit(solution)/shard_map/ppermute | solution.py:662
  14.9 2.1 %collective-permute-start.3 = (bf16[144,256]{1,0:T(8,128)(2,1)S(1)}, bf16[144,256]{1,0:T(8,128)(2,1)S(1)}, u32[]{:S(2)}, u32[]{:S(2)}) collective-permute-start(bf16[144,256]{1,0:T(8,128)(2,1)S(1)} %get-tuple-element.54), channel_id=1, source_target_pairs={{0,12},{4,8},{8,4},{12,0},{1,13},{5,9},{9,5},{13,1},{2,14},{6,10},... | collective-permute-start | bytes 221192 | tf_op jit(solution)/shard_map/ppermute | solution.py:662
  17.0 1.5 %collective-permute-start.5 = (bf16[4,128,128]{2,1,0:T(8,128)(2,1)S(1)}, bf16[4,128,128]{2,1,0:T(8,128)(2,1)S(1)}, u32[]{:S(2)}, u32[]{:S(2)}) collective-permute-start(bf16[4,128,128]{2,1,0:T(8,128)(2,1)S(1)} %get-tuple-element.70.refs_0_), channel_id=1, source_target_pairs={{0,2},{2,0},{1,3},{3,1},{4,6},{6,4},{5,7},{7,5},{8,10},{10,8},{9,1... | collective-permute-start | bytes 393224 | tf_op jit(solution)/shard_map/ppermute | solution.py:658
  18.7 4.9 %collective-permute-done.3.refs_3_ = bf16[144,256]{1,0:T(8,128)(2,1)S(1)} collective-permute-done((bf16[144,256]{1,0:T(8,128)(2,1)S(1)}, bf16[144,256]{1,0:T(8,128)(2,1)S(1)}, u32[]{:S(2)}, u32[]{:S(2)}) %collective-permute-start.3) | collective-permute-done | bytes 73760 | tf_op jit(solution)/shard_map/ppermute | solution.py:662
  24.1 1.3 %collective-permute-done.6.refs_5_ = bf16[12,128,128]{2,1,0:T(8,128)(2,1)S(1)} collective-permute-done((bf16[12,128,128]{2,1,0:T(8,128)(2,1)S(1)}, bf16[12,128,128]{2,1,0:T(8,128)(2,1)S(1)}, u32[]{:S(2)}, u32[]{:S(2)}) %collective-permute-start.6) | collective-permute-done | bytes 393248 | tf_op jit(solution)/shard_map/ppermute | solution.py:658
  26.5 0.8 %collective-permute-done.7.came_ref = bf16[4,128,128]{2,1,0:T(8,128)(2,1)S(1)} collective-permute-done((bf16[4,128,128]{2,1,0:T(8,128)(2,1)S(1)}, bf16[4,128,128]{2,1,0:T(8,128)(2,1)S(1)}, u32[]{:S(2)}, u32[]{:S(2)}) %collective-permute-start.7) | collective-permute-done | bytes 131104 | tf_op jit(solution)/shard_map/ppermute | solution.py:658
  27.3 1.6 %collective-permute-start.8 = (bf16[4,128,128]{2,1,0:T(8,128)(2,1)S(1)}, bf16[4,128,128]{2,1,0:T(8,128)(2,1)S(1)}, u32[]{:S(2)}, u32[]{:S(2)}) collective-permute-start(bf16[4,128,128]{2,1,0:T(8,128)(2,1)S(1)} %add_up.1.refs_0_), channel_id=1, source_target_pairs={{0,2},{2,0},{1,3},{3,1},{4,6},{6,4},{5,7},{7,5},{8,10},{10,8},{9,1... | collective-permute-start | bytes 393224 | tf_op jit(solution)/shard_map/ppermute | solution.py:658
  28.9 4.0 %collective-permute-done.8.refs_1_ = bf16[4,128,128]{2,1,0:T(8,128)(2,1)S(1)} collective-permute-done((bf16[4,128,128]{2,1,0:T(8,128)(2,1)S(1)}, bf16[4,128,128]{2,1,0:T(8,128)(2,1)S(1)}, u32[]{:S(2)}, u32[]{:S(2)}) %collective-permute-start.8) | collective-permute-done | bytes 131104 | tf_op jit(solution)/shard_map/ppermute | solution.py:658
  32.9 0.7 %dense.1 = (bf16[4,128,128]{2,1,0:T(8,128)(2,1)S(1)}, bf16[128,1024]{1,0:T(8,128)(2,1)S(1)}, bf16[4,128,128]{2,1,0:T(8,128)(2,1)S(1)}, bf16[128,256]{1,0:T(8,128)(2,1)S(1)}) custom-call(bf16[4,128,128]{2,1,0:T(8,128)(2,1)S(1)} %add_up.1.refs_0_, bf16[4,128,128]{2,1,0:T(8,128)(2,1)S(1)} %collective-permute-done.8.refs_1_, bf16[256,512]{1,0:T(8,128)(2,1)S(1)} %widen.1.refs_2_, ...), custom_call_target="tpu_custom_call" | custom-call | flops 268435456 | bytes 1048576 | tf_op jit(solution)/shard_map/dense/pallas_call | solution.py:530
  33.7 1.4 %collective-permute-done.9.refs_4_.shared_ref = bf16[128,1024]{1,0:T(8,128)(2,1)S(1)} collective-permute-done((bf16[128,1024]{1,0:T(8,128)(2,1)S(1)}, bf16[128,1024]{1,0:T(8,128)(2,1)S(1)}, u32[]{:S(2)}, u32[]{:S(2)}) %collective-permute-start.9) | collective-permute-done | bytes 262176 | tf_op jit(solution)/shard_map/ppermute | solution.py:658
  35.6 1.3 %collective-permute-start.10 = (bf16[128,512]{1,0:T(8,128)(2,1)S(1)}, bf16[128,512]{1,0:T(8,128)(2,1)S(1)}, u32[]{:S(2)}, u32[]{:S(2)}) collective-permute-start(bf16[128,512]{1,0:T(8,128)(2,1)S(1)} %get-tuple-element.79), channel_id=1, source_target_pairs={{0,8},{4,12},{8,0},{12,4},{1,9},{5,13},{9,1},{13,5},{2,10},{6,14},... | collective-permute-start | bytes 393224 | tf_op jit(solution)/shard_map/ppermute | solution.py:662
  36.9 1.2 %collective-permute-done.12.came_ref = bf16[128,256]{1,0:T(8,128)(2,1)S(1)} collective-permute-done((bf16[128,256]{1,0:T(8,128)(2,1)S(1)}, bf16[128,256]{1,0:T(8,128)(2,1)S(1)}, u32[]{:S(2)}, u32[]{:S(2)}) %collective-permute-start.12) | collective-permute-done | bytes 65568 | tf_op jit(solution)/shard_map/ppermute | solution.py:662
  38.6 0.9 %collective-permute-done.13.came_ref = bf16[128,128]{1,0:T(8,128)(2,1)S(1)} collective-permute-done((bf16[128,128]{1,0:T(8,128)(2,1)S(1)}, bf16[128,128]{1,0:T(8,128)(2,1)S(1)}, u32[]{:S(2)}, u32[]{:S(2)}) %collective-permute-start.13) | collective-permute-done | bytes 32800 | tf_op jit(solution)/shard_map/ppermute | solution.py:658
  39.5 2.2 %collective-permute-start.14 = (bf16[128,640]{1,0:T(8,128)(2,1)S(1)}, bf16[128,640]{1,0:T(8,128)(2,1)S(1)}, u32[]{:S(2)}, u32[]{:S(2)}) collective-permute-start(bf16[128,640]{1,0:T(8,128)(2,1)S(1)} %beside.1), channel_id=1, source_target_pairs={{0,12},{4,8},{8,4},{12,0},{1,13},{5,9},{9,5},{13,1},{2,14},{6,10},... | collective-permute-start | bytes 491528 | tf_op jit(solution)/shard_map/ppermute | solution.py:662
  41.7 1.0 %late_self.1 = (f32[8,128,128]{2,1,0:T(8,128)S(1)}, bf16[8,128,128]{2,1,0:T(8,128)(2,1)}) custom-call(s32[1,128]{1,0:T(1,128)S(1)} %get-tuple-element.46.refs_0_.ask_ref, bf16[8,128,128]{2,1,0:T(8,128)(2,1)S(1)} %get-tuple-element.74.x3, f32[128,256]{1,0:T(8,128)S(1)} %get-tuple-element.75.self_ref, ...), custom_call_target="tpu_custom_call" | custom-call | flops 67108864 | bytes 262144 | tf_op jit(solution)/shard_map/late_self/pallas_call | solution.py:447
  42.7 2.8 %collective-permute-done.10.came_ref = bf16[128,512]{1,0:T(8,128)(2,1)S(1)} collective-permute-done((bf16[128,512]{1,0:T(8,128)(2,1)S(1)}, bf16[128,512]{1,0:T(8,128)(2,1)S(1)}, u32[]{:S(2)}, u32[]{:S(2)}) %collective-permute-start.10) | collective-permute-done | bytes 131104 | tf_op jit(solution)/shard_map/ppermute | solution.py:662
  45.9 4.5 %collective-permute-done.11.came_ref = bf16[128,512]{1,0:T(8,128)(2,1)S(1)} collective-permute-done((bf16[128,512]{1,0:T(8,128)(2,1)S(1)}, bf16[128,512]{1,0:T(8,128)(2,1)S(1)}, u32[]{:S(2)}, u32[]{:S(2)}) %collective-permute-start.11) | collective-permute-done | bytes 131104 | tf_op jit(solution)/shard_map/ppermute | solution.py:662
  51.2 0.6 %collective-permute-start.16 = (f32[128,128]{1,0:T(8,128)S(1)}, f32[128,128]{1,0:T(8,128)S(1)}, u32[]{:S(2)}, u32[]{:S(2)}) collective-permute-start(f32[128,128]{1,0:T(8,128)S(1)} %pair_sum.3.share_ref), channel_id=1, source_target_pairs={{0,1},{1,0},{2,3},{3,2},{4,5},{5,4},{6,7},{7,6},{8,9},{9,8},{10,11... | collective-permute-start | bytes 196616 | tf_op jit(solution)/shard_map/ppermute | solution.py:658
  51.8 1.0 %collective-permute-done.16.other_share_ref = f32[128,128]{1,0:T(8,128)S(1)} collective-permute-done((f32[128,128]{1,0:T(8,128)S(1)}, f32[128,128]{1,0:T(8,128)S(1)}, u32[]{:S(2)}, u32[]{:S(2)}) %collective-permute-start.16) | collective-permute-done | bytes 65568 | tf_op jit(solution)/shard_map/ppermute | solution.py:658
  52.8 0.9 %finish.1 = (bf16[8,128,128]{2,1,0:T(8,128)(2,1)}, f32[256,128]{1,0:T(8,128)}) custom-call(bf16[8,128,128]{2,1,0:T(8,128)(2,1)S(1)} %late_rows.5.mine_ref, bf16[8,128,128]{2,1,0:T(8,128)(2,1)S(1)} %collective-permute-done.15.other_ref, f32[128,128]{1,0:T(8,128)S(1)} %pair_sum.3.share_ref, f32[128,128]{1,0:T(8,128)S(1)} %collective-permute-done.16.other_share_ref), custom_call_target="tpu_custom_call" | custom-call | bytes 262144 | tf_op jit(solution)/shard_map/finish/pallas_call | solution.py:649
  (38 shorter events, 5.6 us)
Async XLA Ops:
  2.4 10.7 %collective-permute-start = (bf16[4,128,128]{2,1,0:T(8,128)(2,1)}, bf16[4,128,128]{2,1,0:T(8,128)(2,1)S(1)}, u32[]{:S(2)}, u32[]{:S(2)}) collective-permute-start(bf16[4,128,128]{2,1,0:T(8,128)(2,1)} %get-tuple-element.52), channel_id=1, source_target_pairs={{0,8},{4,12},{8,0},{12,4},{1,9},{5,13},{9,1},{13,5},{2,10},{6,14},... | collective-permute-start | bytes 393224 | tf_op jit(solution)/shard_map/ppermute | solution.py:662
  6.5 6.8 %collective-permute-start.1 = (bf16[4,128,128]{2,1,0:T(8,128)(2,1)}, bf16[4,128,128]{2,1,0:T(8,128)(2,1)S(1)}, u32[]{:S(2)}, u32[]{:S(2)}) collective-permute-start(bf16[4,128,128]{2,1,0:T(8,128)(2,1)} %get-tuple-element.52), channel_id=1, source_target_pairs={{0,4},{4,0},{8,12},{12,8},{1,5},{5,1},{9,13},{13,9},{2,6},{6,2},{1... | collective-permute-start | bytes 393224 | tf_op jit(solution)/shard_map/ppermute | solution.py:662
  8.7 3.0 %copy-start = (bf16[8,128,128]{2,1,0:T(8,128)(2,1)S(1)}, bf16[8,128,128]{2,1,0:T(8,128)(2,1)}, u32[]{:S(2)}) copy-start(bf16[8,128,128]{2,1,0:T(8,128)(2,1)} %refs_4_.3) | copy-start | bytes 786436
  8.7 3.0 %copy-start.1 = (bf16[8,128,128]{2,1,0:T(8,128)(2,1)S(1)}, bf16[8,128,128]{2,1,0:T(8,128)(2,1)}, u32[]{:S(2)}) copy-start(bf16[8,128,128]{2,1,0:T(8,128)(2,1)} %refs_4_.2) | copy-start | bytes 786436
  12.2 6.4 %collective-permute-start.4 = (bf16[144,256]{1,0:T(8,128)(2,1)S(1)}, bf16[144,256]{1,0:T(8,128)(2,1)S(1)}, u32[]{:S(2)}, u32[]{:S(2)}) collective-permute-start(bf16[144,256]{1,0:T(8,128)(2,1)S(1)} %get-tuple-element.56), channel_id=1, source_target_pairs={{0,8},{4,12},{8,0},{12,4},{1,9},{5,13},{9,1},{13,5},{2,10},{6,14},... | collective-permute-start | bytes 221192 | tf_op jit(solution)/shard_map/ppermute | solution.py:662
  13.3 10.2 %collective-permute-start.2 = (bf16[400,256]{1,0:T(8,128)(2,1)S(1)}, bf16[400,256]{1,0:T(8,128)(2,1)S(1)}, u32[]{:S(2)}, u32[]{:S(2)}) collective-permute-start(bf16[400,256]{1,0:T(8,128)(2,1)S(1)} %below.1), channel_id=1, source_target_pairs={{0,4},{4,0},{8,12},{12,8},{1,5},{5,1},{9,13},{13,9},{2,6},{6,2},{1... | collective-permute-start | bytes 614408 | tf_op jit(solution)/shard_map/ppermute | solution.py:662
  14.9 8.6 %collective-permute-start.3 = (bf16[144,256]{1,0:T(8,128)(2,1)S(1)}, bf16[144,256]{1,0:T(8,128)(2,1)S(1)}, u32[]{:S(2)}, u32[]{:S(2)}) collective-permute-start(bf16[144,256]{1,0:T(8,128)(2,1)S(1)} %get-tuple-element.54), channel_id=1, source_target_pairs={{0,12},{4,8},{8,4},{12,0},{1,13},{5,9},{9,5},{13,1},{2,14},{6,10},... | collective-permute-start | bytes 221192 | tf_op jit(solution)/shard_map/ppermute | solution.py:662
  17.0 6.6 %collective-permute-start.5 = (bf16[4,128,128]{2,1,0:T(8,128)(2,1)S(1)}, bf16[4,128,128]{2,1,0:T(8,128)(2,1)S(1)}, u32[]{:S(2)}, u32[]{:S(2)}) collective-permute-start(bf16[4,128,128]{2,1,0:T(8,128)(2,1)S(1)} %get-tuple-element.70.refs_0_), channel_id=1, source_target_pairs={{0,2},{2,0},{1,3},{3,1},{4,6},{6,4},{5,7},{7,5},{8,10},{10,8},{9,1... | collective-permute-start | bytes 393224 | tf_op jit(solution)/shard_map/ppermute | solution.py:658
  23.6 1.8 %collective-permute-start.6 = (bf16[12,128,128]{2,1,0:T(8,128)(2,1)S(1)}, bf16[12,128,128]{2,1,0:T(8,128)(2,1)S(1)}, u32[]{:S(2)}, u32[]{:S(2)}) collective-permute-start(bf16[12,128,128]{2,1,0:T(8,128)(2,1)S(1)} %stack_more.1.refs_4_), channel_id=1, source_target_pairs={{0,1},{1,0},{2,3},{3,2},{4,5},{5,4},{6,7},{7,6},{8,9},{9,8},{10,11... | collective-permute-start | bytes 1179656 | tf_op jit(solution)/shard_map/ppermute | solution.py:658
  24.1 8.8 %copy-start.2 = (bf16[256,256]{1,0:T(8,128)(2,1)S(1)}, bf16[256,256]{1,0:T(8,128)(2,1)}, u32[]{:S(2)}) copy-start(bf16[256,256]{1,0:T(8,128)(2,1)} %refs_3_.3) | copy-start | bytes 393220
  25.8 1.4 %collective-permute-start.7 = (bf16[4,128,128]{2,1,0:T(8,128)(2,1)S(1)}, bf16[4,128,128]{2,1,0:T(8,128)(2,1)S(1)}, u32[]{:S(2)}, u32[]{:S(2)}) collective-permute-start(bf16[4,128,128]{2,1,0:T(8,128)(2,1)S(1)} %get-tuple-element.69), channel_id=1, source_target_pairs={{0,1},{1,0},{2,3},{3,2},{4,5},{5,4},{6,7},{7,6},{8,9},{9,8},{10,11... | collective-permute-start | bytes 393224 | tf_op jit(solution)/shard_map/ppermute | solution.py:658
  27.3 5.6 %collective-permute-start.8 = (bf16[4,128,128]{2,1,0:T(8,128)(2,1)S(1)}, bf16[4,128,128]{2,1,0:T(8,128)(2,1)S(1)}, u32[]{:S(2)}, u32[]{:S(2)}) collective-permute-start(bf16[4,128,128]{2,1,0:T(8,128)(2,1)S(1)} %add_up.1.refs_0_), channel_id=1, source_target_pairs={{0,2},{2,0},{1,3},{3,1},{4,6},{6,4},{5,7},{7,5},{8,10},{10,8},{9,1... | collective-permute-start | bytes 393224 | tf_op jit(solution)/shard_map/ppermute | solution.py:658
  33.6 1.6 %collective-permute-start.9 = (bf16[128,1024]{1,0:T(8,128)(2,1)S(1)}, bf16[128,1024]{1,0:T(8,128)(2,1)S(1)}, u32[]{:S(2)}, u32[]{:S(2)}) collective-permute-start(bf16[128,1024]{1,0:T(8,128)(2,1)S(1)} %get-tuple-element.73), channel_id=1, source_target_pairs={{0,1},{1,0},{2,3},{3,2},{4,5},{5,4},{6,7},{7,6},{8,9},{9,8},{10,11... | collective-permute-start | bytes 786440 | tf_op jit(solution)/shard_map/ppermute | solution.py:658
  33.6 4.5 %collective-permute-start.12 = (bf16[128,256]{1,0:T(8,128)(2,1)S(1)}, bf16[128,256]{1,0:T(8,128)(2,1)S(1)}, u32[]{:S(2)}, u32[]{:S(2)}) collective-permute-start(bf16[128,256]{1,0:T(8,128)(2,1)S(1)} %get-tuple-element.82.mine_ref), channel_id=1, source_target_pairs={{0,4},{4,0},{8,12},{12,8},{1,5},{5,1},{9,13},{13,9},{2,6},{6,2},{1... | collective-permute-start | bytes 196616 | tf_op jit(solution)/shard_map/ppermute | solution.py:662
  35.6 9.9 %collective-permute-start.10 = (bf16[128,512]{1,0:T(8,128)(2,1)S(1)}, bf16[128,512]{1,0:T(8,128)(2,1)S(1)}, u32[]{:S(2)}, u32[]{:S(2)}) collective-permute-start(bf16[128,512]{1,0:T(8,128)(2,1)S(1)} %get-tuple-element.79), channel_id=1, source_target_pairs={{0,8},{4,12},{8,0},{12,4},{1,9},{5,13},{9,1},{13,5},{2,10},{6,14},... | collective-permute-start | bytes 393224 | tf_op jit(solution)/shard_map/ppermute | solution.py:662
  38.2 1.3 %collective-permute-start.13 = (bf16[128,128]{1,0:T(8,128)(2,1)S(1)}, bf16[128,128]{1,0:T(8,128)(2,1)S(1)}, u32[]{:S(2)}, u32[]{:S(2)}) collective-permute-start(bf16[128,128]{1,0:T(8,128)(2,1)S(1)} %get-tuple-element.84), channel_id=1, source_target_pairs={{0,1},{1,0},{2,3},{3,2},{4,5},{5,4},{6,7},{7,6},{8,9},{9,8},{10,11... | collective-permute-start | bytes 98312 | tf_op jit(solution)/shard_map/ppermute | solution.py:658
  38.3 12.1 %collective-permute-start.11 = (bf16[128,512]{1,0:T(8,128)(2,1)S(1)}, bf16[128,512]{1,0:T(8,128)(2,1)S(1)}, u32[]{:S(2)}, u32[]{:S(2)}) collective-permute-start(bf16[128,512]{1,0:T(8,128)(2,1)S(1)} %get-tuple-element.80), channel_id=1, source_target_pairs={{0,4},{4,0},{8,12},{12,8},{1,5},{5,1},{9,13},{13,9},{2,6},{6,2},{1... | collective-permute-start | bytes 393224 | tf_op jit(solution)/shard_map/ppermute | solution.py:662
  39.5 11.2 %collective-permute-start.14 = (bf16[128,640]{1,0:T(8,128)(2,1)S(1)}, bf16[128,640]{1,0:T(8,128)(2,1)S(1)}, u32[]{:S(2)}, u32[]{:S(2)}) collective-permute-start(bf16[128,640]{1,0:T(8,128)(2,1)S(1)} %beside.1), channel_id=1, source_target_pairs={{0,12},{4,8},{8,4},{12,0},{1,13},{5,9},{9,5},{13,1},{2,14},{6,10},... | collective-permute-start | bytes 491528 | tf_op jit(solution)/shard_map/ppermute | solution.py:662
  51.1 1.7 %collective-permute-start.15 = (bf16[8,128,128]{2,1,0:T(8,128)(2,1)S(1)}, bf16[8,128,128]{2,1,0:T(8,128)(2,1)S(1)}, u32[]{:S(2)}, u32[]{:S(2)}) collective-permute-start(bf16[8,128,128]{2,1,0:T(8,128)(2,1)S(1)} %late_rows.5.mine_ref), channel_id=1, source_target_pairs={{0,1},{1,0},{2,3},{3,2},{4,5},{5,4},{6,7},{7,6},{8,9},{9,8},{10,11... | collective-permute-start | bytes 786440 | tf_op jit(solution)/shard_map/ppermute | solution.py:658
  51.2 1.6 %collective-permute-start.16 = (f32[128,128]{1,0:T(8,128)S(1)}, f32[128,128]{1,0:T(8,128)S(1)}, u32[]{:S(2)}, u32[]{:S(2)}) collective-permute-start(f32[128,128]{1,0:T(8,128)S(1)} %pair_sum.3.share_ref), channel_id=1, source_target_pairs={{0,1},{1,0},{2,3},{3,2},{4,5},{5,4},{6,7},{7,6},{8,9},{9,8},{10,11... | collective-permute-start | bytes 196616 | tf_op jit(solution)/shard_map/ppermute | solution.py:658

commit v21 on v20

--- a/solution.py
+++ b/solution.py
@@ -499,7 +499,7 @@
 
 def dense_kernel(feats, *refs):
     sums, wide_cot, refs = refs[:feats], refs[feats], refs[feats + 1 :]
-    w_ref, act_ref, give_ref, spread_ref, term_ref, wide, pre_scr, grad = refs
+    w_ref, act_ref, give_ref, spread_ref, own_grad_ref, wide, pre_scr, grad = refs
     share, columns, width = act_ref.shape
     me = lax.axis_index("feat")
     rows = [pl.ds(pl.multiple_of(lax.rem(me + q, feats) * columns, columns), columns) for q in range(feats)]
@@ -512,7 +512,7 @@
     factor = wide_cot[...].astype(F32) * sig * (1.0 + pre * (1.0 - sig))
     grad[...] = factor.astype(BF16)
     spread = dot(w_ref[rows[0], :], grad[...]).astype(BF16)
-    term_ref[...] = dot(grad[rows[0], :], wide[...], NT).astype(BF16)
+    own_grad_ref[...] = grad[rows[0], :]
     wide_share = share * width
     give_ref[:, :wide_share] = spread
     for b in range(share):
@@ -534,17 +534,26 @@
             shape((share, columns, width), BF16),
             shape((columns, 2 * share * width), BF16),
             shape((share, columns, width), BF16),
-            shape((columns, features), BF16),
+            shape((columns, share * width), BF16),
+            shape((features, share * width), BF16),
         ],
         [vmem()] * (feats + 2),
         [
-            pltpu.VMEM((features, share * width), BF16),
             pltpu.VMEM((features, share * width), F32),
             pltpu.VMEM((features, share * width), BF16),
         ],
         flops=2 ** 28,
         moved=2 ** 20,
     )(*sums, cot, weight)
+
+
+def term_kernel(own_grad_ref, wide, term_ref):
+    term_ref[...] = dot(own_grad_ref[...], wide[...], NT).astype(BF16)
+
+
+def term_of(own_grad, wide):
+    out = shape((own_grad.shape[0], wide.shape[0]), BF16)
+    return call(term_kernel, "term", out, [vmem(), vmem()], flops=2 ** 26)(own_grad, wide)
 
 
 def send_kernel(peers, *refs):
@@ -700,7 +709,8 @@
     mine = add_up(keep, ahead(give, "rep", reps, 1))
     cot = widen(cots)
     sums = [mine] + [ahead(mine, "feat", feats, feats - q) for q in range(1, feats)]
-    act, give, spread, term = dense(sums, cot, weight, feats)
+    act, give, spread, own_grad, wide = dense(sums, cot, weight, feats)
+    term = term_of(own_grad, wide)
     shared = ahead(give, "rep", reps, 1)
     term = half_term(term, peers, reps)
     values, sends, own_mirror = sends_of(spread, shared, operator, ids, peers, reps)

time: 53.8 us -> 53.8 us (level)
  transfers between devices with their start and end apart: 17 -> 17, of which waited for: 13 -> 13; matrix products, arithmetic and copies ran while one was open for 0% -> 0% of each run, Pallas kernels for 12% -> 13%
where the time goes in v21:
time: 53.8 us; the launch traced here: 53.7 us
  waiting for transfers between devices  23.1 us (43%)
  starting transfers between devices  18 us (33%)
  Pallas kernels  11 us (20%)
  between operations  1.5 us (3%)
    ppermute x9, starting transfers between devices, across(): return lax.ppermute(value, 'graph', [(i, i ^ k) for i in range(peers)])  14 us
    ppermute x9, waiting for transfers between devices, across(): return lax.ppermute(value, 'graph', [(i, i ^ k) for i in range(peers)])  13.9 us
    ppermute x8, waiting for transfers between devices, ahead(): return lax.ppermute(value, axis, [(i, (i + k) % size) for i in range(size)])  9.19 us
    ppermute x8, starting transfers between devices, ahead(): return lax.ppermute(value, axis, [(i, (i + k) % size) for i in range(size)])  4.09 us
    pallas_call x1, Pallas kernels, list_operator(): call(functools.partial(operator_kernel, blocks_dev, slots_here, groups),...  2.99 us
    pallas_call x1, Pallas kernels, prepare(): call(functools.partial(prepare_kernel, peers), 'prepare', [shape((blocks_...  1.76 us
    pallas_call x3, Pallas kernels, late_rows(): call(functools.partial(late_rows_kernel, k), 'late_rows', shape(before.sh...  1.09 us
  transfers between devices with their start and end apart: 17, of which 13 were waited for; matrix products, arithmetic and copies ran while one was open for 0% of the time, Pallas kernels for 13%

profile of v21, /device:TPU:0, one launch (start us, length us, event | category | flops | bytes accessed | tf_op | source)
XLA Modules:
  0.0 53.7 jit_solution(5646379025275932737)
XLA Ops:
  0.6 1.8 %prepare.1 = (bf16[4,128,128]{2,1,0:T(8,128)(2,1)}, s32[8192,128]{1,0:T(8,128)}) custom-call(s32[1,128]{1,0:T(1,128)} %bitcast.2, s32[1,128]{1,0:T(1,128)} %bitcast.3, bf16[8,128,128]{2,1,0:T(8,128)(2,1)} %refs_4_.3), custom_call_target="tpu_custom_call" | custom-call | bytes 262144 | tf_op jit(solution)/shard_map/prepare/pallas_call | solution.py:102
  2.4 4.1 %collective-permute-start = (bf16[4,128,128]{2,1,0:T(8,128)(2,1)}, bf16[4,128,128]{2,1,0:T(8,128)(2,1)S(1)}, u32[]{:S(2)}, u32[]{:S(2)}) collective-permute-start(bf16[4,128,128]{2,1,0:T(8,128)(2,1)} %get-tuple-element.53), channel_id=1, source_target_pairs={{0,8},{4,12},{8,0},{12,4},{1,9},{5,13},{9,1},{13,5},{2,10},{6,14},... | collective-permute-start | bytes 393224 | tf_op jit(solution)/shard_map/ppermute | solution.py:671
  6.5 1.6 %collective-permute-start.1 = (bf16[4,128,128]{2,1,0:T(8,128)(2,1)}, bf16[4,128,128]{2,1,0:T(8,128)(2,1)S(1)}, u32[]{:S(2)}, u32[]{:S(2)}) collective-permute-start(bf16[4,128,128]{2,1,0:T(8,128)(2,1)} %get-tuple-element.53), channel_id=1, source_target_pairs={{0,4},{4,0},{8,12},{12,8},{1,5},{5,1},{9,13},{13,9},{2,6},{6,2},{1... | collective-permute-start | bytes 393224 | tf_op jit(solution)/shard_map/ppermute | solution.py:671
  8.8 3.0 %operator.1 = (bf16[1024,1024]{1,0:T(8,128)(2,1)S(1)}, s32[1,128]{1,0:T(1,128)S(1)}, s32[1,128]{1,0:T(1,128)S(1)}, s32[1,128]{1,0:T(1,128)S(1)}, s32[1,128]{1,0:T(1,128)S(1)}) custom-call(s32[1]{0:T(128)S(6)} %copy.10.count_ref, s32[8192,128]{1,0:T(8,128)} %get-tuple-element.46.table_in, bf16[128,128,128]{2,1,0:T(8,128)(2,1)} %tiles_ref.1), custom_call_target="tpu_custom_call" | custom-call | bytes 16777216 | tf_op jit(solution)/shard_map/operator/pallas_call | solution.py:192
  13.3 1.6 %collective-permute-start.2 = (bf16[400,256]{1,0:T(8,128)(2,1)S(1)}, bf16[400,256]{1,0:T(8,128)(2,1)S(1)}, u32[]{:S(2)}, u32[]{:S(2)}) collective-permute-start(bf16[400,256]{1,0:T(8,128)(2,1)S(1)} %below.1), channel_id=1, source_target_pairs={{0,4},{4,0},{8,12},{12,8},{1,5},{5,1},{9,13},{13,9},{2,6},{6,2},{1... | collective-permute-start | bytes 614408 | tf_op jit(solution)/shard_map/ppermute | solution.py:671
  14.9 2.1 %collective-permute-start.3 = (bf16[144,256]{1,0:T(8,128)(2,1)S(1)}, bf16[144,256]{1,0:T(8,128)(2,1)S(1)}, u32[]{:S(2)}, u32[]{:S(2)}) collective-permute-start(bf16[144,256]{1,0:T(8,128)(2,1)S(1)} %get-tuple-element.55), channel_id=1, source_target_pairs={{0,12},{4,8},{8,4},{12,0},{1,13},{5,9},{9,5},{13,1},{2,14},{6,10},... | collective-permute-start | bytes 221192 | tf_op jit(solution)/shard_map/ppermute | solution.py:671
  17.0 1.5 %collective-permute-start.5 = (bf16[4,128,128]{2,1,0:T(8,128)(2,1)S(1)}, bf16[4,128,128]{2,1,0:T(8,128)(2,1)S(1)}, u32[]{:S(2)}, u32[]{:S(2)}) collective-permute-start(bf16[4,128,128]{2,1,0:T(8,128)(2,1)S(1)} %get-tuple-element.71.refs_0_), channel_id=1, source_target_pairs={{0,2},{2,0},{1,3},{3,1},{4,6},{6,4},{5,7},{7,5},{8,10},{10,8},{9,1... | collective-permute-start | bytes 393224 | tf_op jit(solution)/shard_map/ppermute | solution.py:667
  18.7 4.8 %collective-permute-done.3.refs_3_ = bf16[144,256]{1,0:T(8,128)(2,1)S(1)} collective-permute-done((bf16[144,256]{1,0:T(8,128)(2,1)S(1)}, bf16[144,256]{1,0:T(8,128)(2,1)S(1)}, u32[]{:S(2)}, u32[]{:S(2)}) %collective-permute-start.3) | collective-permute-done | bytes 73760 | tf_op jit(solution)/shard_map/ppermute | solution.py:671
  24.1 1.3 %collective-permute-done.6.refs_5_ = bf16[12,128,128]{2,1,0:T(8,128)(2,1)S(1)} collective-permute-done((bf16[12,128,128]{2,1,0:T(8,128)(2,1)S(1)}, bf16[12,128,128]{2,1,0:T(8,128)(2,1)S(1)}, u32[]{:S(2)}, u32[]{:S(2)}) %collective-permute-start.6) | collective-permute-done | bytes 393248 | tf_op jit(solution)/shard_map/ppermute | solution.py:667
  26.5 0.8 %collective-permute-done.7.came_ref = bf16[4,128,128]{2,1,0:T(8,128)(2,1)S(1)} collective-permute-done((bf16[4,128,128]{2,1,0:T(8,128)(2,1)S(1)}, bf16[4,128,128]{2,1,0:T(8,128)(2,1)S(1)}, u32[]{:S(2)}, u32[]{:S(2)}) %collective-permute-start.7) | collective-permute-done | bytes 131104 | tf_op jit(solution)/shard_map/ppermute | solution.py:667
  27.3 1.6 %collective-permute-start.8 = (bf16[4,128,128]{2,1,0:T(8,128)(2,1)S(1)}, bf16[4,128,128]{2,1,0:T(8,128)(2,1)S(1)}, u32[]{:S(2)}, u32[]{:S(2)}) collective-permute-start(bf16[4,128,128]{2,1,0:T(8,128)(2,1)S(1)} %add_up.1.refs_0_), channel_id=1, source_target_pairs={{0,2},{2,0},{1,3},{3,1},{4,6},{6,4},{5,7},{7,5},{8,10},{10,8},{9,1... | collective-permute-start | bytes 393224 | tf_op jit(solution)/shard_map/ppermute | solution.py:667
  28.9 4.0 %collective-permute-done.8.refs_1_ = bf16[4,128,128]{2,1,0:T(8,128)(2,1)S(1)} collective-permute-done((bf16[4,128,128]{2,1,0:T(8,128)(2,1)S(1)}, bf16[4,128,128]{2,1,0:T(8,128)(2,1)S(1)}, u32[]{:S(2)}, u32[]{:S(2)}) %collective-permute-start.8) | collective-permute-done | bytes 131104 | tf_op jit(solution)/shard_map/ppermute | solution.py:667
  32.9 0.6 %dense.1 = (bf16[4,128,128]{2,1,0:T(8,128)(2,1)S(1)}, bf16[128,1024]{1,0:T(8,128)(2,1)S(1)}, bf16[4,128,128]{2,1,0:T(8,128)(2,1)S(1)}, bf16[128,512]{1,0:T(8,128)(2,1)S(1)}, bf16[256,512]{1,0:T(8,128)(2,1)S(1)}) custom-call(bf16[4,128,128]{2,1,0:T(8,128)(2,1)S(1)} %add_up.1.refs_0_, bf16[4,128,128]{2,1,0:T(8,128)(2,1)S(1)} %collective-permute-done.8.refs_1_, ...), custom_call_target="tpu_custom_call" | custom-call | flops 268435456 | bytes 1048576 | tf_op jit(solution)/shard_map/dense/pallas_call | solution.py:530
  33.9 1.2 %collective-permute-done.9.refs_4_.shared_ref = bf16[128,1024]{1,0:T(8,128)(2,1)S(1)} collective-permute-done((bf16[128,1024]{1,0:T(8,128)(2,1)S(1)}, bf16[128,1024]{1,0:T(8,128)(2,1)S(1)}, u32[]{:S(2)}, u32[]{:S(2)}) %collective-permute-start.9) | collective-permute-done | bytes 262176 | tf_op jit(solution)/shard_map/ppermute | solution.py:667
  35.6 1.6 %collective-permute-start.10 = (bf16[128,512]{1,0:T(8,128)(2,1)S(1)}, bf16[128,512]{1,0:T(8,128)(2,1)S(1)}, u32[]{:S(2)}, u32[]{:S(2)}) collective-permute-start(bf16[128,512]{1,0:T(8,128)(2,1)S(1)} %get-tuple-element.80), channel_id=1, source_target_pairs={{0,8},{4,12},{8,0},{12,4},{1,9},{5,13},{9,1},{13,5},{2,10},{6,14},... | collective-permute-start | bytes 393224 | tf_op jit(solution)/shard_map/ppermute | solution.py:671
  37.2 1.3 %collective-permute-done.12.came_ref = bf16[128,256]{1,0:T(8,128)(2,1)S(1)} collective-permute-done((bf16[128,256]{1,0:T(8,128)(2,1)S(1)}, bf16[128,256]{1,0:T(8,128)(2,1)S(1)}, u32[]{:S(2)}, u32[]{:S(2)}) %collective-permute-start.12) | collective-permute-done | bytes 65568 | tf_op jit(solution)/shard_map/ppermute | solution.py:671
  38.9 0.8 %collective-permute-done.13.came_ref = bf16[128,128]{1,0:T(8,128)(2,1)S(1)} collective-permute-done((bf16[128,128]{1,0:T(8,128)(2,1)S(1)}, bf16[128,128]{1,0:T(8,128)(2,1)S(1)}, u32[]{:S(2)}, u32[]{:S(2)}) %collective-permute-start.13) | collective-permute-done | bytes 32800 | tf_op jit(solution)/shard_map/ppermute | solution.py:667
  39.8 2.2 %collective-permute-start.14 = (bf16[128,640]{1,0:T(8,128)(2,1)S(1)}, bf16[128,640]{1,0:T(8,128)(2,1)S(1)}, u32[]{:S(2)}, u32[]{:S(2)}) collective-permute-start(bf16[128,640]{1,0:T(8,128)(2,1)S(1)} %beside.1), channel_id=1, source_target_pairs={{0,12},{4,8},{8,4},{12,0},{1,13},{5,9},{9,5},{13,1},{2,14},{6,10},... | collective-permute-start | bytes 491528 | tf_op jit(solution)/shard_map/ppermute | solution.py:671
  42.0 1.0 %late_self.1 = (f32[8,128,128]{2,1,0:T(8,128)S(1)}, bf16[8,128,128]{2,1,0:T(8,128)(2,1)}) custom-call(s32[1,128]{1,0:T(1,128)S(1)} %get-tuple-element.47.refs_0_.ask_ref, bf16[8,128,128]{2,1,0:T(8,128)(2,1)S(1)} %get-tuple-element.75.x3, f32[128,256]{1,0:T(8,128)S(1)} %get-tuple-element.76.self_ref, ...), custom_call_target="tpu_custom_call" | custom-call | flops 67108864 | bytes 262144 | tf_op jit(solution)/shard_map/late_self/pallas_call | solution.py:447
  43.0 2.7 %collective-permute-done.10.came_ref = bf16[128,512]{1,0:T(8,128)(2,1)S(1)} collective-permute-done((bf16[128,512]{1,0:T(8,128)(2,1)S(1)}, bf16[128,512]{1,0:T(8,128)(2,1)S(1)}, u32[]{:S(2)}, u32[]{:S(2)}) %collective-permute-start.10) | collective-permute-done | bytes 131104 | tf_op jit(solution)/shard_map/ppermute | solution.py:671
  46.1 4.2 %collective-permute-done.11.came_ref = bf16[128,512]{1,0:T(8,128)(2,1)S(1)} collective-permute-done((bf16[128,512]{1,0:T(8,128)(2,1)S(1)}, bf16[128,512]{1,0:T(8,128)(2,1)S(1)}, u32[]{:S(2)}, u32[]{:S(2)}) %collective-permute-start.11) | collective-permute-done | bytes 131104 | tf_op jit(solution)/shard_map/ppermute | solution.py:671
  51.2 0.6 %collective-permute-start.16 = (f32[128,128]{1,0:T(8,128)S(1)}, f32[128,128]{1,0:T(8,128)S(1)}, u32[]{:S(2)}, u32[]{:S(2)}) collective-permute-start(f32[128,128]{1,0:T(8,128)S(1)} %pair_sum.3.share_ref), channel_id=1, source_target_pairs={{0,1},{1,0},{2,3},{3,2},{4,5},{5,4},{6,7},{7,6},{8,9},{9,8},{10,11... | collective-permute-start | bytes 196616 | tf_op jit(solution)/shard_map/ppermute | solution.py:667
  51.7 1.0 %collective-permute-done.16.other_share_ref = f32[128,128]{1,0:T(8,128)S(1)} collective-permute-done((f32[128,128]{1,0:T(8,128)S(1)}, f32[128,128]{1,0:T(8,128)S(1)}, u32[]{:S(2)}, u32[]{:S(2)}) %collective-permute-start.16) | collective-permute-done | bytes 65568 | tf_op jit(solution)/shard_map/ppermute | solution.py:667
  52.8 0.9 %finish.1 = (bf16[8,128,128]{2,1,0:T(8,128)(2,1)}, f32[256,128]{1,0:T(8,128)}) custom-call(bf16[8,128,128]{2,1,0:T(8,128)(2,1)S(1)} %late_rows.5.mine_ref, bf16[8,128,128]{2,1,0:T(8,128)(2,1)S(1)} %collective-permute-done.15.other_ref, f32[128,128]{1,0:T(8,128)S(1)} %pair_sum.3.share_ref, f32[128,128]{1,0:T(8,128)S(1)} %collective-permute-done.16.other_share_ref), custom_call_target="tpu_custom_call" | custom-call | bytes 262144 | tf_op jit(solution)/shard_map/finish/pallas_call | solution.py:658
  (39 shorter events, 5.9 us)
Async XLA Ops:
  2.4 10.7 %collective-permute-start = (bf16[4,128,128]{2,1,0:T(8,128)(2,1)}, bf16[4,128,128]{2,1,0:T(8,128)(2,1)S(1)}, u32[]{:S(2)}, u32[]{:S(2)}) collective-permute-start(bf16[4,128,128]{2,1,0:T(8,128)(2,1)} %get-tuple-element.53), channel_id=1, source_target_pairs={{0,8},{4,12},{8,0},{12,4},{1,9},{5,13},{9,1},{13,5},{2,10},{6,14},... | collective-permute-start | bytes 393224 | tf_op jit(solution)/shard_map/ppermute | solution.py:671
  6.5 6.8 %collective-permute-start.1 = (bf16[4,128,128]{2,1,0:T(8,128)(2,1)}, bf16[4,128,128]{2,1,0:T(8,128)(2,1)S(1)}, u32[]{:S(2)}, u32[]{:S(2)}) collective-permute-start(bf16[4,128,128]{2,1,0:T(8,128)(2,1)} %get-tuple-element.53), channel_id=1, source_target_pairs={{0,4},{4,0},{8,12},{12,8},{1,5},{5,1},{9,13},{13,9},{2,6},{6,2},{1... | collective-permute-start | bytes 393224 | tf_op jit(solution)/shard_map/ppermute | solution.py:671
  8.7 3.0 %copy-start = (bf16[8,128,128]{2,1,0:T(8,128)(2,1)S(1)}, bf16[8,128,128]{2,1,0:T(8,128)(2,1)}, u32[]{:S(2)}) copy-start(bf16[8,128,128]{2,1,0:T(8,128)(2,1)} %refs_4_.3) | copy-start | bytes 786436
  8.7 3.0 %copy-start.1 = (bf16[8,128,128]{2,1,0:T(8,128)(2,1)S(1)}, bf16[8,128,128]{2,1,0:T(8,128)(2,1)}, u32[]{:S(2)}) copy-start(bf16[8,128,128]{2,1,0:T(8,128)(2,1)} %refs_4_.2) | copy-start | bytes 786436
  12.2 6.4 %collective-permute-start.4 = (bf16[144,256]{1,0:T(8,128)(2,1)S(1)}, bf16[144,256]{1,0:T(8,128)(2,1)S(1)}, u32[]{:S(2)}, u32[]{:S(2)}) collective-permute-start(bf16[144,256]{1,0:T(8,128)(2,1)S(1)} %get-tuple-element.57), channel_id=1, source_target_pairs={{0,8},{4,12},{8,0},{12,4},{1,9},{5,13},{9,1},{13,5},{2,10},{6,14},... | collective-permute-start | bytes 221192 | tf_op jit(solution)/shard_map/ppermute | solution.py:671
  13.3 10.2 %collective-permute-start.2 = (bf16[400,256]{1,0:T(8,128)(2,1)S(1)}, bf16[400,256]{1,0:T(8,128)(2,1)S(1)}, u32[]{:S(2)}, u32[]{:S(2)}) collective-permute-start(bf16[400,256]{1,0:T(8,128)(2,1)S(1)} %below.1), channel_id=1, source_target_pairs={{0,4},{4,0},{8,12},{12,8},{1,5},{5,1},{9,13},{13,9},{2,6},{6,2},{1... | collective-permute-start | bytes 614408 | tf_op jit(solution)/shard_map/ppermute | solution.py:671
  14.9 8.6 %collective-permute-start.3 = (bf16[144,256]{1,0:T(8,128)(2,1)S(1)}, bf16[144,256]{1,0:T(8,128)(2,1)S(1)}, u32[]{:S(2)}, u32[]{:S(2)}) collective-permute-start(bf16[144,256]{1,0:T(8,128)(2,1)S(1)} %get-tuple-element.55), channel_id=1, source_target_pairs={{0,12},{4,8},{8,4},{12,0},{1,13},{5,9},{9,5},{13,1},{2,14},{6,10},... | collective-permute-start | bytes 221192 | tf_op jit(solution)/shard_map/ppermute | solution.py:671
  17.0 6.6 %collective-permute-start.5 = (bf16[4,128,128]{2,1,0:T(8,128)(2,1)S(1)}, bf16[4,128,128]{2,1,0:T(8,128)(2,1)S(1)}, u32[]{:S(2)}, u32[]{:S(2)}) collective-permute-start(bf16[4,128,128]{2,1,0:T(8,128)(2,1)S(1)} %get-tuple-element.71.refs_0_), channel_id=1, source_target_pairs={{0,2},{2,0},{1,3},{3,1},{4,6},{6,4},{5,7},{7,5},{8,10},{10,8},{9,1... | collective-permute-start | bytes 393224 | tf_op jit(solution)/shard_map/ppermute | solution.py:667
  23.6 1.8 %collective-permute-start.6 = (bf16[12,128,128]{2,1,0:T(8,128)(2,1)S(1)}, bf16[12,128,128]{2,1,0:T(8,128)(2,1)S(1)}, u32[]{:S(2)}, u32[]{:S(2)}) collective-permute-start(bf16[12,128,128]{2,1,0:T(8,128)(2,1)S(1)} %stack_more.1.refs_4_), channel_id=1, source_target_pairs={{0,1},{1,0},{2,3},{3,2},{4,5},{5,4},{6,7},{7,6},{8,9},{9,8},{10,11... | collective-permute-start | bytes 1179656 | tf_op jit(solution)/shard_map/ppermute | solution.py:667
  24.1 8.8 %copy-start.2 = (bf16[256,256]{1,0:T(8,128)(2,1)S(1)}, bf16[256,256]{1,0:T(8,128)(2,1)}, u32[]{:S(2)}) copy-start(bf16[256,256]{1,0:T(8,128)(2,1)} %refs_3_.3) | copy-start | bytes 393220
  25.8 1.4 %collective-permute-start.7 = (bf16[4,128,128]{2,1,0:T(8,128)(2,1)S(1)}, bf16[4,128,128]{2,1,0:T(8,128)(2,1)S(1)}, u32[]{:S(2)}, u32[]{:S(2)}) collective-permute-start(bf16[4,128,128]{2,1,0:T(8,128)(2,1)S(1)} %get-tuple-element.70), channel_id=1, source_target_pairs={{0,1},{1,0},{2,3},{3,2},{4,5},{5,4},{6,7},{7,6},{8,9},{9,8},{10,11... | collective-permute-start | bytes 393224 | tf_op jit(solution)/shard_map/ppermute | solution.py:667
  27.3 5.6 %collective-permute-start.8 = (bf16[4,128,128]{2,1,0:T(8,128)(2,1)S(1)}, bf16[4,128,128]{2,1,0:T(8,128)(2,1)S(1)}, u32[]{:S(2)}, u32[]{:S(2)}) collective-permute-start(bf16[4,128,128]{2,1,0:T(8,128)(2,1)S(1)} %add_up.1.refs_0_), channel_id=1, source_target_pairs={{0,2},{2,0},{1,3},{3,1},{4,6},{6,4},{5,7},{7,5},{8,10},{10,8},{9,1... | collective-permute-start | bytes 393224 | tf_op jit(solution)/shard_map/ppermute | solution.py:667
  33.6 1.6 %collective-permute-start.9 = (bf16[128,1024]{1,0:T(8,128)(2,1)S(1)}, bf16[128,1024]{1,0:T(8,128)(2,1)S(1)}, u32[]{:S(2)}, u32[]{:S(2)}) collective-permute-start(bf16[128,1024]{1,0:T(8,128)(2,1)S(1)} %get-tuple-element.74), channel_id=1, source_target_pairs={{0,1},{1,0},{2,3},{3,2},{4,5},{5,4},{6,7},{7,6},{8,9},{9,8},{10,11... | collective-permute-start | bytes 786440 | tf_op jit(solution)/shard_map/ppermute | solution.py:667
  33.9 4.6 %collective-permute-start.12 = (bf16[128,256]{1,0:T(8,128)(2,1)S(1)}, bf16[128,256]{1,0:T(8,128)(2,1)S(1)}, u32[]{:S(2)}, u32[]{:S(2)}) collective-permute-start(bf16[128,256]{1,0:T(8,128)(2,1)S(1)} %term.1.mine_ref), channel_id=1, source_target_pairs={{0,4},{4,0},{8,12},{12,8},{1,5},{5,1},{9,13},{13,9},{2,6},{6,2},{1... | collective-permute-start | bytes 196616 | tf_op jit(solution)/shard_map/ppermute | solution.py:671
  35.6 10.1 %collective-permute-start.10 = (bf16[128,512]{1,0:T(8,128)(2,1)S(1)}, bf16[128,512]{1,0:T(8,128)(2,1)S(1)}, u32[]{:S(2)}, u32[]{:S(2)}) collective-permute-start(bf16[128,512]{1,0:T(8,128)(2,1)S(1)} %get-tuple-element.80), channel_id=1, source_target_pairs={{0,8},{4,12},{8,0},{12,4},{1,9},{5,13},{9,1},{13,5},{2,10},{6,14},... | collective-permute-start | bytes 393224 | tf_op jit(solution)/shard_map/ppermute | solution.py:671
  38.5 1.3 %collective-permute-start.13 = (bf16[128,128]{1,0:T(8,128)(2,1)S(1)}, bf16[128,128]{1,0:T(8,128)(2,1)S(1)}, u32[]{:S(2)}, u32[]{:S(2)}) collective-permute-start(bf16[128,128]{1,0:T(8,128)(2,1)S(1)} %get-tuple-element.86), channel_id=1, source_target_pairs={{0,1},{1,0},{2,3},{3,2},{4,5},{5,4},{6,7},{7,6},{8,9},{9,8},{10,11... | collective-permute-start | bytes 98312 | tf_op jit(solution)/shard_map/ppermute | solution.py:667
  38.5 11.8 %collective-permute-start.11 = (bf16[128,512]{1,0:T(8,128)(2,1)S(1)}, bf16[128,512]{1,0:T(8,128)(2,1)S(1)}, u32[]{:S(2)}, u32[]{:S(2)}) collective-permute-start(bf16[128,512]{1,0:T(8,128)(2,1)S(1)} %get-tuple-element.81), channel_id=1, source_target_pairs={{0,4},{4,0},{8,12},{12,8},{1,5},{5,1},{9,13},{13,9},{2,6},{6,2},{1... | collective-permute-start | bytes 393224 | tf_op jit(solution)/shard_map/ppermute | solution.py:671
  39.8 11.0 %collective-permute-start.14 = (bf16[128,640]{1,0:T(8,128)(2,1)S(1)}, bf16[128,640]{1,0:T(8,128)(2,1)S(1)}, u32[]{:S(2)}, u32[]{:S(2)}) collective-permute-start(bf16[128,640]{1,0:T(8,128)(2,1)S(1)} %beside.1), channel_id=1, source_target_pairs={{0,12},{4,8},{8,4},{12,0},{1,13},{5,9},{9,5},{13,1},{2,14},{6,10},... | collective-permute-start | bytes 491528 | tf_op jit(solution)/shard_map/ppermute | solution.py:671
  51.1 1.7 %collective-permute-start.15 = (bf16[8,128,128]{2,1,0:T(8,128)(2,1)S(1)}, bf16[8,128,128]{2,1,0:T(8,128)(2,1)S(1)}, u32[]{:S(2)}, u32[]{:S(2)}) collective-permute-start(bf16[8,128,128]{2,1,0:T(8,128)(2,1)S(1)} %late_rows.5.mine_ref), channel_id=1, source_target_pairs={{0,1},{1,0},{2,3},{3,2},{4,5},{5,4},{6,7},{7,6},{8,9},{9,8},{10,11... | collective-permute-start | bytes 786440 | tf_op jit(solution)/shard_map/ppermute | solution.py:667
  51.2 1.6 %collective-permute-start.16 = (f32[128,128]{1,0:T(8,128)S(1)}, f32[128,128]{1,0:T(8,128)S(1)}, u32[]{:S(2)}, u32[]{:S(2)}) collective-permute-start(f32[128,128]{1,0:T(8,128)S(1)} %pair_sum.3.share_ref), channel_id=1, source_target_pairs={{0,1},{1,0},{2,3},{3,2},{4,5},{5,4},{6,7},{7,6},{8,9},{9,8},{10,11... | collective-permute-start | bytes 196616 | tf_op jit(solution)/shard_map/ppermute | solution.py:667

commit v22 on v20

--- a/solution.py
+++ b/solution.py
@@ -688,8 +688,8 @@
         came[j] = across(chunk, peers, j)
     held = after(own_cot, crossed)
     cots = [own_cot] + [ahead(held, "feat", feats, feats - q) for q in range(1, feats)]
-    stacked = stack(pieces + [crossed], came[middle:-1])
-    came[1:middle], came[-1], stacked = lax.optimization_barrier((came[1:middle], came[-1], stacked))
+    stacked = stack(pieces + [crossed], came[middle:])
+    came[1:middle], stacked = lax.optimization_barrier((came[1:middle], stacked))
     stacked, cots = lax.optimization_barrier((stacked, cots))
     stacked = stack_more(stacked, came[1:middle])
     swapped = ahead(stacked, "rep", reps, 1)

time: 53.8 us -> 53.6 us (level)
  transfers between devices with their start and end apart: 17 -> 17, of which waited for: 13 -> 11; matrix products, arithmetic and copies ran while one was open for 0% -> 0% of each run, Pallas kernels for 12% -> 12%
where the time goes in v22:
time: 53.6 us; the launch traced here: 53.5 us
  waiting for transfers between devices  23.2 us (43%)
  starting transfers between devices  18 us (34%)
  Pallas kernels  10.8 us (20%)
  between operations  1.5 us (3%)
    ppermute x9, waiting for transfers between devices, across(): return lax.ppermute(value, 'graph', [(i, i ^ k) for i in range(peers)])  14 us
    ppermute x9, starting transfers between devices, across(): return lax.ppermute(value, 'graph', [(i, i ^ k) for i in range(peers)])  13.9 us
    ppermute x8, waiting for transfers between devices, ahead(): return lax.ppermute(value, axis, [(i, (i + k) % size) for i in range(size)])  9.23 us
    ppermute x8, starting transfers between devices, ahead(): return lax.ppermute(value, axis, [(i, (i + k) % size) for i in range(size)])  4.09 us
    pallas_call x1, Pallas kernels, list_operator(): call(functools.partial(operator_kernel, blocks_dev, slots_here, groups),...  2.99 us
    pallas_call x1, Pallas kernels, prepare(): call(functools.partial(prepare_kernel, peers), 'prepare', [shape((blocks_...  1.76 us
    pallas_call x3, Pallas kernels, late_rows(): call(functools.partial(late_rows_kernel, k), 'late_rows', shape(before.sh...  1.08 us
  transfers between devices with their start and end apart: 17, of which 11 were waited for; matrix products, arithmetic and copies ran while one was open for 0% of the time, Pallas kernels for 12%

profile of v22, /device:TPU:0, one launch (start us, length us, event | category | flops | bytes accessed | tf_op | source)
XLA Modules:
  0.0 53.5 jit_solution(7326356172375195803)
XLA Ops:
  0.6 1.8 %prepare.1 = (bf16[4,128,128]{2,1,0:T(8,128)(2,1)}, s32[8192,128]{1,0:T(8,128)}) custom-call(s32[1,128]{1,0:T(1,128)} %bitcast.2, s32[1,128]{1,0:T(1,128)} %bitcast.3, bf16[8,128,128]{2,1,0:T(8,128)(2,1)} %refs_4_.3), custom_call_target="tpu_custom_call" | custom-call | bytes 262144 | tf_op jit(solution)/shard_map/prepare/pallas_call | solution.py:102
  2.4 4.1 %collective-permute-start = (bf16[4,128,128]{2,1,0:T(8,128)(2,1)}, bf16[4,128,128]{2,1,0:T(8,128)(2,1)S(1)}, u32[]{:S(2)}, u32[]{:S(2)}) collective-permute-start(bf16[4,128,128]{2,1,0:T(8,128)(2,1)} %get-tuple-element.51), channel_id=1, source_target_pairs={{0,8},{4,12},{8,0},{12,4},{1,9},{5,13},{9,1},{13,5},{2,10},{6,14},... | collective-permute-start | bytes 393224 | tf_op jit(solution)/shard_map/ppermute | solution.py:662
  6.5 1.6 %collective-permute-start.1 = (bf16[4,128,128]{2,1,0:T(8,128)(2,1)}, bf16[4,128,128]{2,1,0:T(8,128)(2,1)S(1)}, u32[]{:S(2)}, u32[]{:S(2)}) collective-permute-start(bf16[4,128,128]{2,1,0:T(8,128)(2,1)} %get-tuple-element.51), channel_id=1, source_target_pairs={{0,4},{4,0},{8,12},{12,8},{1,5},{5,1},{9,13},{13,9},{2,6},{6,2},{1... | collective-permute-start | bytes 393224 | tf_op jit(solution)/shard_map/ppermute | solution.py:662
  8.8 3.0 %operator.1 = (bf16[1024,1024]{1,0:T(8,128)(2,1)S(1)}, s32[1,128]{1,0:T(1,128)S(1)}, s32[1,128]{1,0:T(1,128)S(1)}, s32[1,128]{1,0:T(1,128)S(1)}, s32[1,128]{1,0:T(1,128)S(1)}) custom-call(s32[1]{0:T(128)S(6)} %copy.10.count_ref, s32[8192,128]{1,0:T(8,128)} %get-tuple-element.44.table_in, bf16[128,128,128]{2,1,0:T(8,128)(2,1)} %tiles_ref.1), custom_call_target="tpu_custom_call" | custom-call | bytes 16777216 | tf_op jit(solution)/shard_map/operator/pallas_call | solution.py:192
  12.7 2.5 %collective-permute-start.4 = (bf16[144,256]{1,0:T(8,128)(2,1)S(1)}, bf16[144,256]{1,0:T(8,128)(2,1)S(1)}, u32[]{:S(2)}, u32[]{:S(2)}) collective-permute-start(bf16[144,256]{1,0:T(8,128)(2,1)S(1)} %get-tuple-element.55), channel_id=1, source_target_pairs={{0,12},{4,8},{8,4},{12,0},{1,13},{5,9},{9,5},{13,1},{2,14},{6,10},... | collective-permute-start | bytes 221192 | tf_op jit(solution)/shard_map/ppermute | solution.py:662
  15.2 0.7 %collective-permute-start.2 = (bf16[400,256]{1,0:T(8,128)(2,1)S(1)}, bf16[400,256]{1,0:T(8,128)(2,1)S(1)}, u32[]{:S(2)}, u32[]{:S(2)}) collective-permute-start(bf16[400,256]{1,0:T(8,128)(2,1)S(1)} %below.1), channel_id=1, source_target_pairs={{0,4},{4,0},{8,12},{12,8},{1,5},{5,1},{9,13},{13,9},{2,6},{6,2},{1... | collective-permute-start | bytes 614408 | tf_op jit(solution)/shard_map/ppermute | solution.py:662
  15.9 1.5 %collective-permute-start.5 = (bf16[4,128,128]{2,1,0:T(8,128)(2,1)S(1)}, bf16[4,128,128]{2,1,0:T(8,128)(2,1)S(1)}, u32[]{:S(2)}, u32[]{:S(2)}) collective-permute-start(bf16[4,128,128]{2,1,0:T(8,128)(2,1)S(1)} %get-tuple-element.68.refs_0_), channel_id=1, source_target_pairs={{0,2},{2,0},{1,3},{3,1},{4,6},{6,4},{5,7},{7,5},{8,10},{10,8},{9,1... | collective-permute-start | bytes 393224 | tf_op jit(solution)/shard_map/ppermute | solution.py:658
  17.4 2.6 %collective-permute-done.3.refs_2_ = bf16[144,256]{1,0:T(8,128)(2,1)S(1)} collective-permute-done((bf16[144,256]{1,0:T(8,128)(2,1)S(1)}, bf16[144,256]{1,0:T(8,128)(2,1)S(1)}, u32[]{:S(2)}, u32[]{:S(2)}) %collective-permute-start.3) | collective-permute-done | bytes 73760 | tf_op jit(solution)/shard_map/ppermute | solution.py:662
  20.1 3.3 %collective-permute-done.2.refs_1_.refs_0_ = bf16[400,256]{1,0:T(8,128)(2,1)S(1)} collective-permute-done((bf16[400,256]{1,0:T(8,128)(2,1)S(1)}, bf16[400,256]{1,0:T(8,128)(2,1)S(1)}, u32[]{:S(2)}, u32[]{:S(2)}) %collective-permute-start.2) | collective-permute-done | bytes 204832 | tf_op jit(solution)/shard_map/ppermute | solution.py:662
  23.9 1.3 %collective-permute-done.6.refs_5_ = bf16[12,128,128]{2,1,0:T(8,128)(2,1)S(1)} collective-permute-done((bf16[12,128,128]{2,1,0:T(8,128)(2,1)S(1)}, bf16[12,128,128]{2,1,0:T(8,128)(2,1)S(1)}, u32[]{:S(2)}, u32[]{:S(2)}) %collective-permute-start.6) | collective-permute-done | bytes 393248 | tf_op jit(solution)/shard_map/ppermute | solution.py:658
  26.2 0.8 %collective-permute-done.7.came_ref = bf16[4,128,128]{2,1,0:T(8,128)(2,1)S(1)} collective-permute-done((bf16[4,128,128]{2,1,0:T(8,128)(2,1)S(1)}, bf16[4,128,128]{2,1,0:T(8,128)(2,1)S(1)}, u32[]{:S(2)}, u32[]{:S(2)}) %collective-permute-start.7) | collective-permute-done | bytes 131104 | tf_op jit(solution)/shard_map/ppermute | solution.py:658
  27.1 1.6 %collective-permute-start.8 = (bf16[4,128,128]{2,1,0:T(8,128)(2,1)S(1)}, bf16[4,128,128]{2,1,0:T(8,128)(2,1)S(1)}, u32[]{:S(2)}, u32[]{:S(2)}) collective-permute-start(bf16[4,128,128]{2,1,0:T(8,128)(2,1)S(1)} %add_up.1.refs_0_), channel_id=1, source_target_pairs={{0,2},{2,0},{1,3},{3,1},{4,6},{6,4},{5,7},{7,5},{8,10},{10,8},{9,1... | collective-permute-start | bytes 393224 | tf_op jit(solution)/shard_map/ppermute | solution.py:658
  28.7 4.0 %collective-permute-done.8.refs_1_ = bf16[4,128,128]{2,1,0:T(8,128)(2,1)S(1)} collective-permute-done((bf16[4,128,128]{2,1,0:T(8,128)(2,1)S(1)}, bf16[4,128,128]{2,1,0:T(8,128)(2,1)S(1)}, u32[]{:S(2)}, u32[]{:S(2)}) %collective-permute-start.8) | collective-permute-done | bytes 131104 | tf_op jit(solution)/shard_map/ppermute | solution.py:658
  32.7 0.7 %dense.1 = (bf16[4,128,128]{2,1,0:T(8,128)(2,1)S(1)}, bf16[128,1024]{1,0:T(8,128)(2,1)S(1)}, bf16[4,128,128]{2,1,0:T(8,128)(2,1)S(1)}, bf16[128,256]{1,0:T(8,128)(2,1)S(1)}) custom-call(bf16[4,128,128]{2,1,0:T(8,128)(2,1)S(1)} %add_up.1.refs_0_, bf16[4,128,128]{2,1,0:T(8,128)(2,1)S(1)} %collective-permute-done.8.refs_1_, bf16[256,512]{1,0:T(8,128)(2,1)S(1)} %widen.1.refs_2_, ...), custom_call_target="tpu_custom_call" | custom-call | flops 268435456 | bytes 1048576 | tf_op jit(solution)/shard_map/dense/pallas_call | solution.py:530
  33.5 1.4 %collective-permute-done.9.refs_4_.shared_ref = bf16[128,1024]{1,0:T(8,128)(2,1)S(1)} collective-permute-done((bf16[128,1024]{1,0:T(8,128)(2,1)S(1)}, bf16[128,1024]{1,0:T(8,128)(2,1)S(1)}, u32[]{:S(2)}, u32[]{:S(2)}) %collective-permute-start.9) | collective-permute-done | bytes 262176 | tf_op jit(solution)/shard_map/ppermute | solution.py:658
  35.4 1.5 %collective-permute-start.10 = (bf16[128,512]{1,0:T(8,128)(2,1)S(1)}, bf16[128,512]{1,0:T(8,128)(2,1)S(1)}, u32[]{:S(2)}, u32[]{:S(2)}) collective-permute-start(bf16[128,512]{1,0:T(8,128)(2,1)S(1)} %get-tuple-element.77), channel_id=1, source_target_pairs={{0,8},{4,12},{8,0},{12,4},{1,9},{5,13},{9,1},{13,5},{2,10},{6,14},... | collective-permute-start | bytes 393224 | tf_op jit(solution)/shard_map/ppermute | solution.py:662
  36.9 1.0 %collective-permute-done.12.came_ref = bf16[128,256]{1,0:T(8,128)(2,1)S(1)} collective-permute-done((bf16[128,256]{1,0:T(8,128)(2,1)S(1)}, bf16[128,256]{1,0:T(8,128)(2,1)S(1)}, u32[]{:S(2)}, u32[]{:S(2)}) %collective-permute-start.12) | collective-permute-done | bytes 65568 | tf_op jit(solution)/shard_map/ppermute | solution.py:662
  38.6 0.7 %collective-permute-done.13.came_ref = bf16[128,128]{1,0:T(8,128)(2,1)S(1)} collective-permute-done((bf16[128,128]{1,0:T(8,128)(2,1)S(1)}, bf16[128,128]{1,0:T(8,128)(2,1)S(1)}, u32[]{:S(2)}, u32[]{:S(2)}) %collective-permute-start.13) | collective-permute-done | bytes 32800 | tf_op jit(solution)/shard_map/ppermute | solution.py:658
  39.3 2.4 %collective-permute-start.14 = (bf16[128,640]{1,0:T(8,128)(2,1)S(1)}, bf16[128,640]{1,0:T(8,128)(2,1)S(1)}, u32[]{:S(2)}, u32[]{:S(2)}) collective-permute-start(bf16[128,640]{1,0:T(8,128)(2,1)S(1)} %beside.1), channel_id=1, source_target_pairs={{0,12},{4,8},{8,4},{12,0},{1,13},{5,9},{9,5},{13,1},{2,14},{6,10},... | collective-permute-start | bytes 491528 | tf_op jit(solution)/shard_map/ppermute | solution.py:662
  41.7 1.0 %late_self.1 = (f32[8,128,128]{2,1,0:T(8,128)S(1)}, bf16[8,128,128]{2,1,0:T(8,128)(2,1)}) custom-call(s32[1,128]{1,0:T(1,128)S(1)} %get-tuple-element.45.refs_0_.ask_ref, bf16[8,128,128]{2,1,0:T(8,128)(2,1)S(1)} %get-tuple-element.72.x3, f32[128,256]{1,0:T(8,128)S(1)} %get-tuple-element.73.self_ref, ...), custom_call_target="tpu_custom_call" | custom-call | flops 67108864 | bytes 262144 | tf_op jit(solution)/shard_map/late_self/pallas_call | solution.py:447
  42.7 2.5 %collective-permute-done.10.came_ref = bf16[128,512]{1,0:T(8,128)(2,1)S(1)} collective-permute-done((bf16[128,512]{1,0:T(8,128)(2,1)S(1)}, bf16[128,512]{1,0:T(8,128)(2,1)S(1)}, u32[]{:S(2)}, u32[]{:S(2)}) %collective-permute-start.10) | collective-permute-done | bytes 131104 | tf_op jit(solution)/shard_map/ppermute | solution.py:662
  45.6 4.6 %collective-permute-done.11.came_ref = bf16[128,512]{1,0:T(8,128)(2,1)S(1)} collective-permute-done((bf16[128,512]{1,0:T(8,128)(2,1)S(1)}, bf16[128,512]{1,0:T(8,128)(2,1)S(1)}, u32[]{:S(2)}, u32[]{:S(2)}) %collective-permute-start.11) | collective-permute-done | bytes 131104 | tf_op jit(solution)/shard_map/ppermute | solution.py:662
  51.5 1.0 %collective-permute-done.16.other_share_ref = f32[128,128]{1,0:T(8,128)S(1)} collective-permute-done((f32[128,128]{1,0:T(8,128)S(1)}, f32[128,128]{1,0:T(8,128)S(1)}, u32[]{:S(2)}, u32[]{:S(2)}) %collective-permute-start.16) | collective-permute-done | bytes 65568 | tf_op jit(solution)/shard_map/ppermute | solution.py:658
  52.6 0.9 %finish.1 = (bf16[8,128,128]{2,1,0:T(8,128)(2,1)}, f32[256,128]{1,0:T(8,128)}) custom-call(bf16[8,128,128]{2,1,0:T(8,128)(2,1)S(1)} %late_rows.5.mine_ref, bf16[8,128,128]{2,1,0:T(8,128)(2,1)S(1)} %collective-permute-done.15.other_ref, f32[128,128]{1,0:T(8,128)S(1)} %pair_sum.3.share_ref, f32[128,128]{1,0:T(8,128)S(1)} %collective-permute-done.16.other_share_ref), custom_call_target="tpu_custom_call" | custom-call | bytes 262144 | tf_op jit(solution)/shard_map/finish/pallas_call | solution.py:649
  (38 shorter events, 5.6 us)
Async XLA Ops:
  2.4 12.7 %collective-permute-start = (bf16[4,128,128]{2,1,0:T(8,128)(2,1)}, bf16[4,128,128]{2,1,0:T(8,128)(2,1)S(1)}, u32[]{:S(2)}, u32[]{:S(2)}) collective-permute-start(bf16[4,128,128]{2,1,0:T(8,128)(2,1)} %get-tuple-element.51), channel_id=1, source_target_pairs={{0,8},{4,12},{8,0},{12,4},{1,9},{5,13},{9,1},{13,5},{2,10},{6,14},... | collective-permute-start | bytes 393224 | tf_op jit(solution)/shard_map/ppermute | solution.py:662
  6.5 8.7 %collective-permute-start.1 = (bf16[4,128,128]{2,1,0:T(8,128)(2,1)}, bf16[4,128,128]{2,1,0:T(8,128)(2,1)S(1)}, u32[]{:S(2)}, u32[]{:S(2)}) collective-permute-start(bf16[4,128,128]{2,1,0:T(8,128)(2,1)} %get-tuple-element.51), channel_id=1, source_target_pairs={{0,4},{4,0},{8,12},{12,8},{1,5},{5,1},{9,13},{13,9},{2,6},{6,2},{1... | collective-permute-start | bytes 393224 | tf_op jit(solution)/shard_map/ppermute | solution.py:662
  8.7 3.0 %copy-start = (bf16[8,128,128]{2,1,0:T(8,128)(2,1)S(1)}, bf16[8,128,128]{2,1,0:T(8,128)(2,1)}, u32[]{:S(2)}) copy-start(bf16[8,128,128]{2,1,0:T(8,128)(2,1)} %refs_4_.3) | copy-start | bytes 786436
  8.7 3.0 %copy-start.1 = (bf16[8,128,128]{2,1,0:T(8,128)(2,1)S(1)}, bf16[8,128,128]{2,1,0:T(8,128)(2,1)}, u32[]{:S(2)}) copy-start(bf16[8,128,128]{2,1,0:T(8,128)(2,1)} %refs_4_.2) | copy-start | bytes 786436
  12.2 7.8 %collective-permute-start.3 = (bf16[144,256]{1,0:T(8,128)(2,1)S(1)}, bf16[144,256]{1,0:T(8,128)(2,1)S(1)}, u32[]{:S(2)}, u32[]{:S(2)}) collective-permute-start(bf16[144,256]{1,0:T(8,128)(2,1)S(1)} %get-tuple-element.54), channel_id=1, source_target_pairs={{0,8},{4,12},{8,0},{12,4},{1,9},{5,13},{9,1},{13,5},{2,10},{6,14},... | collective-permute-start | bytes 221192 | tf_op jit(solution)/shard_map/ppermute | solution.py:662
  12.7 7.4 %collective-permute-start.4 = (bf16[144,256]{1,0:T(8,128)(2,1)S(1)}, bf16[144,256]{1,0:T(8,128)(2,1)S(1)}, u32[]{:S(2)}, u32[]{:S(2)}) collective-permute-start(bf16[144,256]{1,0:T(8,128)(2,1)S(1)} %get-tuple-element.55), channel_id=1, source_target_pairs={{0,12},{4,8},{8,4},{12,0},{1,13},{5,9},{9,5},{13,1},{2,14},{6,10},... | collective-permute-start | bytes 221192 | tf_op jit(solution)/shard_map/ppermute | solution.py:662
  15.2 8.1 %collective-permute-start.2 = (bf16[400,256]{1,0:T(8,128)(2,1)S(1)}, bf16[400,256]{1,0:T(8,128)(2,1)S(1)}, u32[]{:S(2)}, u32[]{:S(2)}) collective-permute-start(bf16[400,256]{1,0:T(8,128)(2,1)S(1)} %below.1), channel_id=1, source_target_pairs={{0,4},{4,0},{8,12},{12,8},{1,5},{5,1},{9,13},{13,9},{2,6},{6,2},{1... | collective-permute-start | bytes 614408 | tf_op jit(solution)/shard_map/ppermute | solution.py:662
  15.9 7.4 %collective-permute-start.5 = (bf16[4,128,128]{2,1,0:T(8,128)(2,1)S(1)}, bf16[4,128,128]{2,1,0:T(8,128)(2,1)S(1)}, u32[]{:S(2)}, u32[]{:S(2)}) collective-permute-start(bf16[4,128,128]{2,1,0:T(8,128)(2,1)S(1)} %get-tuple-element.68.refs_0_), channel_id=1, source_target_pairs={{0,2},{2,0},{1,3},{3,1},{4,6},{6,4},{5,7},{7,5},{8,10},{10,8},{9,1... | collective-permute-start | bytes 393224 | tf_op jit(solution)/shard_map/ppermute | solution.py:658
  23.4 1.8 %collective-permute-start.6 = (bf16[12,128,128]{2,1,0:T(8,128)(2,1)S(1)}, bf16[12,128,128]{2,1,0:T(8,128)(2,1)S(1)}, u32[]{:S(2)}, u32[]{:S(2)}) collective-permute-start(bf16[12,128,128]{2,1,0:T(8,128)(2,1)S(1)} %stack_more.1.refs_4_), channel_id=1, source_target_pairs={{0,1},{1,0},{2,3},{3,2},{4,5},{5,4},{6,7},{7,6},{8,9},{9,8},{10,11... | collective-permute-start | bytes 1179656 | tf_op jit(solution)/shard_map/ppermute | solution.py:658
  23.9 8.8 %copy-start.2 = (bf16[256,256]{1,0:T(8,128)(2,1)S(1)}, bf16[256,256]{1,0:T(8,128)(2,1)}, u32[]{:S(2)}) copy-start(bf16[256,256]{1,0:T(8,128)(2,1)} %refs_3_.3) | copy-start | bytes 393220
  25.6 1.4 %collective-permute-start.7 = (bf16[4,128,128]{2,1,0:T(8,128)(2,1)S(1)}, bf16[4,128,128]{2,1,0:T(8,128)(2,1)S(1)}, u32[]{:S(2)}, u32[]{:S(2)}) collective-permute-start(bf16[4,128,128]{2,1,0:T(8,128)(2,1)S(1)} %get-tuple-element.67), channel_id=1, source_target_pairs={{0,1},{1,0},{2,3},{3,2},{4,5},{5,4},{6,7},{7,6},{8,9},{9,8},{10,11... | collective-permute-start | bytes 393224 | tf_op jit(solution)/shard_map/ppermute | solution.py:658
  27.1 5.6 %collective-permute-start.8 = (bf16[4,128,128]{2,1,0:T(8,128)(2,1)S(1)}, bf16[4,128,128]{2,1,0:T(8,128)(2,1)S(1)}, u32[]{:S(2)}, u32[]{:S(2)}) collective-permute-start(bf16[4,128,128]{2,1,0:T(8,128)(2,1)S(1)} %add_up.1.refs_0_), channel_id=1, source_target_pairs={{0,2},{2,0},{1,3},{3,1},{4,6},{6,4},{5,7},{7,5},{8,10},{10,8},{9,1... | collective-permute-start | bytes 393224 | tf_op jit(solution)/shard_map/ppermute | solution.py:658
  33.3 1.6 %collective-permute-start.9 = (bf16[128,1024]{1,0:T(8,128)(2,1)S(1)}, bf16[128,1024]{1,0:T(8,128)(2,1)S(1)}, u32[]{:S(2)}, u32[]{:S(2)}) collective-permute-start(bf16[128,1024]{1,0:T(8,128)(2,1)S(1)} %get-tuple-element.71), channel_id=1, source_target_pairs={{0,1},{1,0},{2,3},{3,2},{4,5},{5,4},{6,7},{7,6},{8,9},{9,8},{10,11... | collective-permute-start | bytes 786440 | tf_op jit(solution)/shard_map/ppermute | solution.py:658
  33.4 4.5 %collective-permute-start.12 = (bf16[128,256]{1,0:T(8,128)(2,1)S(1)}, bf16[128,256]{1,0:T(8,128)(2,1)S(1)}, u32[]{:S(2)}, u32[]{:S(2)}) collective-permute-start(bf16[128,256]{1,0:T(8,128)(2,1)S(1)} %get-tuple-element.80.mine_ref), channel_id=1, source_target_pairs={{0,4},{4,0},{8,12},{12,8},{1,5},{5,1},{9,13},{13,9},{2,6},{6,2},{1... | collective-permute-start | bytes 196616 | tf_op jit(solution)/shard_map/ppermute | solution.py:662
  35.4 9.8 %collective-permute-start.10 = (bf16[128,512]{1,0:T(8,128)(2,1)S(1)}, bf16[128,512]{1,0:T(8,128)(2,1)S(1)}, u32[]{:S(2)}, u32[]{:S(2)}) collective-permute-start(bf16[128,512]{1,0:T(8,128)(2,1)S(1)} %get-tuple-element.77), channel_id=1, source_target_pairs={{0,8},{4,12},{8,0},{12,4},{1,9},{5,13},{9,1},{13,5},{2,10},{6,14},... | collective-permute-start | bytes 393224 | tf_op jit(solution)/shard_map/ppermute | solution.py:662
  38.0 1.3 %collective-permute-start.13 = (bf16[128,128]{1,0:T(8,128)(2,1)S(1)}, bf16[128,128]{1,0:T(8,128)(2,1)S(1)}, u32[]{:S(2)}, u32[]{:S(2)}) collective-permute-start(bf16[128,128]{1,0:T(8,128)(2,1)S(1)} %get-tuple-element.82), channel_id=1, source_target_pairs={{0,1},{1,0},{2,3},{3,2},{4,5},{5,4},{6,7},{7,6},{8,9},{9,8},{10,11... | collective-permute-start | bytes 98312 | tf_op jit(solution)/shard_map/ppermute | solution.py:658
  38.0 12.1 %collective-permute-start.11 = (bf16[128,512]{1,0:T(8,128)(2,1)S(1)}, bf16[128,512]{1,0:T(8,128)(2,1)S(1)}, u32[]{:S(2)}, u32[]{:S(2)}) collective-permute-start(bf16[128,512]{1,0:T(8,128)(2,1)S(1)} %get-tuple-element.78), channel_id=1, source_target_pairs={{0,4},{4,0},{8,12},{12,8},{1,5},{5,1},{9,13},{13,9},{2,6},{6,2},{1... | collective-permute-start | bytes 393224 | tf_op jit(solution)/shard_map/ppermute | solution.py:662
  39.3 11.2 %collective-permute-start.14 = (bf16[128,640]{1,0:T(8,128)(2,1)S(1)}, bf16[128,640]{1,0:T(8,128)(2,1)S(1)}, u32[]{:S(2)}, u32[]{:S(2)}) collective-permute-start(bf16[128,640]{1,0:T(8,128)(2,1)S(1)} %beside.1), channel_id=1, source_target_pairs={{0,12},{4,8},{8,4},{12,0},{1,13},{5,9},{9,5},{13,1},{2,14},{6,10},... | collective-permute-start | bytes 491528 | tf_op jit(solution)/shard_map/ppermute | solution.py:662
  50.9 1.7 %collective-permute-start.15 = (bf16[8,128,128]{2,1,0:T(8,128)(2,1)S(1)}, bf16[8,128,128]{2,1,0:T(8,128)(2,1)S(1)}, u32[]{:S(2)}, u32[]{:S(2)}) collective-permute-start(bf16[8,128,128]{2,1,0:T(8,128)(2,1)S(1)} %late_rows.5.mine_ref), channel_id=1, source_target_pairs={{0,1},{1,0},{2,3},{3,2},{4,5},{5,4},{6,7},{7,6},{8,9},{9,8},{10,11... | collective-permute-start | bytes 786440 | tf_op jit(solution)/shard_map/ppermute | solution.py:658
  51.0 1.6 %collective-permute-start.16 = (f32[128,128]{1,0:T(8,128)S(1)}, f32[128,128]{1,0:T(8,128)S(1)}, u32[]{:S(2)}, u32[]{:S(2)}) collective-permute-start(f32[128,128]{1,0:T(8,128)S(1)} %pair_sum.3.share_ref), channel_id=1, source_target_pairs={{0,1},{1,0},{2,3},{3,2},{4,5},{5,4},{6,7},{7,6},{8,9},{9,8},{10,11... | collective-permute-start | bytes 196616 | tf_op jit(solution)/shard_map/ppermute | solution.py:658
